TPU v7x, 32 devices: a whole 2x2x4 slice. The times are simulated.
32 devices in a mesh: groups: 2 (over y), ex: 8 (over z, x), dim: 2 (over core).
Axes of the slice: x: 2, y: 2, z: 4, core: 2. Of those that a mesh axis runs over, the one named last changes fastest.
Arguments:
- store: bfloat16 [12288, 4096], P(('groups', 'ex'), 'dim'), parts along dimension 0, may hold values from -6 to 6
- queries: bfloat16 [2048, 4096], P(('groups', 'ex'), 'dim'), parts along dimension 0, may hold values from -0.09375 to 0.09375
- precond: float32 [4096], P('dim'), may hold values from 0.25 to 4
- query_rank: int32 [16, 128], P(('groups', 'ex')), parts along dimension 0, may hold values from 0 to 127, each once within a row
- valid_rows: int32 [16], P(('groups', 'ex')), parts along dimension 0, may hold values from 1 to 768, 4608 in all
Outputs:
- scores: float32 [12288, 512], P(('groups', 'ex', 'dim')), parts along dimension 0
There are 2 independent parts, one for each index of `groups`. A program takes and returns all parts, laid end to end along the dimension named above; an argument that names none is the same for every part. Nothing has to cross between parts.
Inputs may be any that keep to these rules, and one draw needn't show every extreme that they name: `query_rank`: each row is a permutation of 0 to 127. `valid_rows`: the counts sum to 8 * 768 * 3 // 4.
All inputs are finite; a program needn't handle non-finite values. No bound on the sum of `valid_rows` on one device may be relied on, other than what follows from the above.
Results may differ from a plain program's by a relative error of at most 0.0029.
Values may be sent and summed in bfloat16 or wider, within the bound.
No kernel may reach another device: no remote copies, remote signals or barrier semaphores. Data moves between devices by JAX's collectives and lax.ppermute only.
A program may use at most 64 MiB of HBM per device.

v0:
```python
import jax
import jax.numpy as jnp
from jax import lax
from jax.sharding import PartitionSpec as P

STEPS = 4


def passed_along(block, axis, distance):
    devices = range(lax.axis_size(axis))
    route = [((i - distance) % len(devices), i) for i in devices]
    return lax.ppermute(block, axis, route)


def shards(store, queries, precond, query_rank, valid_rows):
    block_rows = queries.shape[0]
    pre = (queries.astype(jnp.float32) * precond[None, :]).astype(jnp.bfloat16)
    positions = lax.broadcasted_iota(jnp.int32, (block_rows, block_rows), 0)
    placing = (positions == query_rank[0][None, :]).astype(jnp.bfloat16)
    ordered = jnp.dot(placing, pre, preferred_element_type=jnp.float32).astype(jnp.bfloat16)
    row_ids = lax.broadcasted_iota(jnp.int32, (store.shape[0], 1), 0)
    keep = row_ids < valid_rows[0]
    blocks = [ordered]
    current = ordered
    for step in range(1, STEPS):
        current = passed_along(current, "ex", 1)
        blocks.append(current)
    pieces = []
    for block in blocks:
        result = lax.dot_general(
            store, block, (((1,), (1,)), ((), ())), preferred_element_type=jnp.float32
        )
        pieces.append(
            lax.psum_scatter(
                jnp.where(keep, result, jnp.float32(0.0)), "dim", scatter_dimension=0, tiled=True
            )
        )
    return jnp.concatenate(pieces, axis=1)


def solution(mesh):
    return jax.shard_map(
        shards,
        mesh=mesh,
        in_specs=(
            P(("groups", "ex"), "dim"),
            P(("groups", "ex"), "dim"),
            P("dim"),
            P(("groups", "ex"), None),
            P(("groups", "ex")),
        ),
        out_specs=P(("groups", "ex", "dim"), None),
        check_vma=False,
    )
```

profile of v0, /device:TPU:0, one launch (start us, length us, event | category | flops | bytes accessed | tf_op | source)
XLA Modules:
  0.0 77.5 jit_solution(7443772278969305702)
XLA Ops:
  6.5 2.3 %convolution_convert_fusion = bf16[128,2048]{1,0:T(8,128)(2,1)} fusion(bf16[128,2048]{1,0:T(8,128)(2,1)} %param.6, f32[2048]{0:T(1024)} %param.7, s32[128]{0:T(128)} %bitcast.19), kind=kOutput, calls=%fused_computation | convolution fusion | flops 68173824 | bytes 1057280 | tf_op jit(solution)/shard_map/dot_general | solution.py:20
  8.8 2.9 %collective-permute-start = (bf16[128,2048]{1,0:T(8,128)(2,1)}, bf16[128,2048]{1,0:T(8,128)(2,1)}, u32[]{:S(2)}, u32[]{:S(2)}) collective-permute-start(bf16[128,2048]{1,0:T(8,128)(2,1)} %convolution_convert_fusion), channel_id=1, source_target_pairs={{14,0},{0,2},{2,4},{4,6},{6,8},{8,10},{10,12},{12,14},{15,1},{1,3}... | collective-permute-start | bytes 1572872 | tf_op jit(solution)/shard_map/ppermute | solution.py:12
  12.4 3.0 %fusion.3 = f32[768,128]{0,1:T(8,128)} fusion(bf16[128,2048]{1,0:T(8,128)(2,1)} %convolution_convert_fusion, bf16[768,2048]{1,0:T(8,128)(2,1)S(1)} %copy-done, pred[768]{0:T(1024)(128)(4,1)S(1)} %iota_compare_fusion.2), kind=kOutput, calls=%fused_computation.8 | convolution fusion | flops 402751488 | bytes 4064000 | tf_op jit(solution)/shard_map/dot_general | solution.py:30
  15.4 0.0 reduce-scatter.5.cloned.1.call-update
  15.4 0.0 reduce-scatter.7.cloned.1.call-start
  15.5 11.5 %collective-permute-done = bf16[128,2048]{1,0:T(8,128)(2,1)} collective-permute-done((bf16[128,2048]{1,0:T(8,128)(2,1)}, bf16[128,2048]{1,0:T(8,128)(2,1)}, u32[]{:S(2)}, u32[]{:S(2)}) %collective-permute-start) | collective-permute-done | bytes 524320 | tf_op jit(solution)/shard_map/ppermute | solution.py:12
  27.0 0.0 collective-permute-start.1
  27.0 3.0 %fusion.2 = f32[768,128]{0,1:T(8,128)} fusion(bf16[128,2048]{1,0:T(8,128)(2,1)} %collective-permute-done, bf16[768,2048]{1,0:T(8,128)(2,1)S(1)} %copy-done, pred[768]{0:T(1024)(128)(4,1)S(1)} %iota_compare_fusion.2), kind=kOutput, calls=%fused_computation.6 | convolution fusion | flops 402751488 | bytes 4064000 | tf_op jit(solution)/shard_map/dot_general | solution.py:30
  30.0 0.0 reduce-scatter.7.cloned.1.call-update
  30.1 0.0 reduce-scatter.9.cloned.1.call-start
  30.1 13.1 %collective-permute-done.1 = bf16[128,2048]{1,0:T(8,128)(2,1)} collective-permute-done((bf16[128,2048]{1,0:T(8,128)(2,1)}, bf16[128,2048]{1,0:T(8,128)(2,1)}, u32[]{:S(2)}, u32[]{:S(2)}) %collective-permute-start.1) | collective-permute-done | bytes 524320 | tf_op jit(solution)/shard_map/ppermute | solution.py:12
  43.2 0.0 collective-permute-start.2
  43.2 3.0 %fusion.1 = f32[768,128]{0,1:T(8,128)} fusion(bf16[128,2048]{1,0:T(8,128)(2,1)} %collective-permute-done.1, bf16[768,2048]{1,0:T(8,128)(2,1)S(1)} %copy-done, pred[768]{0:T(1024)(128)(4,1)S(1)} %iota_compare_fusion.2), kind=kOutput, calls=%fused_computation.4 | convolution fusion | flops 402751488 | bytes 4064000 | tf_op jit(solution)/shard_map/dot_general | solution.py:30
  46.2 0.0 reduce-scatter.9.cloned.1.call-update
  46.2 0.0 reduce-scatter.11.cloned.1.call-start
  46.3 12.1 %collective-permute-done.2 = bf16[128,2048]{1,0:T(8,128)(2,1)} collective-permute-done((bf16[128,2048]{1,0:T(8,128)(2,1)}, bf16[128,2048]{1,0:T(8,128)(2,1)}, u32[]{:S(2)}, u32[]{:S(2)}) %collective-permute-start.2) | collective-permute-done | bytes 524320 | tf_op jit(solution)/shard_map/ppermute | solution.py:12
  58.4 3.0 %fusion = f32[768,128]{0,1:T(8,128)} fusion(bf16[128,2048]{1,0:T(8,128)(2,1)} %collective-permute-done.2, bf16[768,2048]{1,0:T(8,128)(2,1)S(1)} %copy-done, pred[768]{0:T(1024)(128)(4,1)S(1)} %iota_compare_fusion.2), kind=kOutput, calls=%fused_computation.2 | convolution fusion | flops 402751488 | bytes 4064000 | tf_op jit(solution)/shard_map/dot_general | solution.py:30
  61.3 0.0 reduce-scatter.11.cloned.1.call-update
  61.4 0.0 reduce-scatter.5.cloned.1.call-done
  61.4 0.0 reduce-scatter.7.cloned.1.call-done
  61.4 0.0 reduce-scatter.9.cloned.1.call-done
  61.4 5.1 %reduce-scatter.11.cloned.1.call-done = f32[384,128]{0,1:T(8,128)} async-done(((f32[768,128]{0,1:T(8,128)}), f32[384,128]{0,1:T(8,128)}) %reduce-scatter.11.cloned.1.call-update) | async-done | bytes 196624 | tf_op jit(solution)/shard_map/reduce_scatter | solution.py:34
  66.5 2.2 %pad_maximum_fusion = f32[384,512]{0,1:T(8,128)} fusion(f32[384,128]{0,1:T(8,128)} %reduce-scatter.11.cloned.1.call-done, f32[384,128]{0,1:T(8,128)} %reduce-scatter.9.cloned.1.call-done, f32[384,128]{0,1:T(8,128)} %reduce-scatter.7.cloned.1.call-done, f32[384,128]{0,1:T(8,128)} %reduce-scatter.5.cloned.1.call-done), kind=kLoop, calls=%fused_computation.10 | loop fusion | flops 589824 | bytes 1572864 | tf_op jit(solution)/shard_map/concatenate | solution.py:38
  68.7 2.3 %copy.6 = f32[384,512]{1,0:T(8,128)} copy(f32[384,512]{0,1:T(8,128)} %pad_maximum_fusion) | data formatting | bytes 1572864 | tf_op jit(solution)/shard_map/concatenate | solution.py:38
  (4 shorter events, 0.0 us)
Async XLA Ops:
  6.5 5.9 %copy-start = (bf16[768,2048]{1,0:T(8,128)(2,1)S(1)}, bf16[768,2048]{1,0:T(8,128)(2,1)}, u32[]{:S(2)}) copy-start(bf16[768,2048]{1,0:T(8,128)(2,1)} %param.5) | copy-start | bytes 9437188
  6.5 54.8 %reduce-scatter.5.cloned.1.call-start = ((), (), s32[]{:S(2)}) async-start(), calls=%async_computation.4 | async-start | bytes 589824 | tf_op jit(solution)/shard_map/reduce_scatter | solution.py:34
  8.8 18.2 %collective-permute-start = (bf16[128,2048]{1,0:T(8,128)(2,1)}, bf16[128,2048]{1,0:T(8,128)(2,1)}, u32[]{:S(2)}, u32[]{:S(2)}) collective-permute-start(bf16[128,2048]{1,0:T(8,128)(2,1)} %convolution_convert_fusion), channel_id=1, source_target_pairs={{14,0},{0,2},{2,4},{4,6},{6,8},{8,10},{10,12},{12,14},{15,1},{1,3}... | collective-permute-start | bytes 1572872 | tf_op jit(solution)/shard_map/ppermute | solution.py:12
  15.4 46.0 %reduce-scatter.7.cloned.1.call-start = ((), (), s32[]{:S(2)}) async-start(), calls=%async_computation.5 | async-start | bytes 589824 | tf_op jit(solution)/shard_map/reduce_scatter | solution.py:34
  27.0 16.1 %collective-permute-start.1 = (bf16[128,2048]{1,0:T(8,128)(2,1)}, bf16[128,2048]{1,0:T(8,128)(2,1)}, u32[]{:S(2)}, u32[]{:S(2)}) collective-permute-start(bf16[128,2048]{1,0:T(8,128)(2,1)} %collective-permute-done), channel_id=1, source_target_pairs={{14,0},{0,2},{2,4},{4,6},{6,8},{8,10},{10,12},{12,14},{15,1},{1,3}... | collective-permute-start | bytes 1572872 | tf_op jit(solution)/shard_map/ppermute | solution.py:12
  30.1 31.4 %reduce-scatter.9.cloned.1.call-start = ((), (), s32[]{:S(2)}) async-start(), calls=%async_computation.6 | async-start | bytes 589824 | tf_op jit(solution)/shard_map/reduce_scatter | solution.py:34
  43.2 15.2 %collective-permute-start.2 = (bf16[128,2048]{1,0:T(8,128)(2,1)}, bf16[128,2048]{1,0:T(8,128)(2,1)}, u32[]{:S(2)}, u32[]{:S(2)}) collective-permute-start(bf16[128,2048]{1,0:T(8,128)(2,1)} %collective-permute-done.1), channel_id=1, source_target_pairs={{14,0},{0,2},{2,4},{4,6},{6,8},{8,10},{10,12},{12,14},{15,1},{1,3}... | collective-permute-start | bytes 1572872 | tf_op jit(solution)/shard_map/ppermute | solution.py:12
  46.2 20.3 %reduce-scatter.11.cloned.1.call-start = ((), (), s32[]{:S(2)}) async-start(), calls=%async_computation.7 | async-start | bytes 589824 | tf_op jit(solution)/shard_map/reduce_scatter | solution.py:34
Sparse Core Ops, SparseCore 0:
  15.6 8.0 reduce-scatter.4
  30.2 9.2 reduce-scatter.6
  46.3 8.9 reduce-scatter.8
  61.5 5.0 reduce-scatter.10
where the time goes:
time: 77.9 us; the launch traced here: 77.5 us
  waiting for transfers between devices  41.9 us (54%)
  matrix products  14.2 us (18%)
  between operations  13.8 us (18%)
  starting transfers between devices  3.07 us (4%)
  local copies, waits for them, and re-layouts  2.28 us (3%)
  other arithmetic  2.16 us (3%)
    ppermute x3, waiting for transfers between devices, passed_along(): return lax.ppermute(block, axis, route)  36.7 us
    dot_general x4, matrix products, shards(): lax.dot_general(store, block, (((1,), (1,)), ((), ())), preferred_element...  12 us
    reduce_scatter x4, waiting for transfers between devices, shards(): lax.psum_scatter(jnp.where(keep, result, jnp.float32(0.0)), 'dim', scatte...  5.16 us
    ppermute x3, starting transfers between devices, passed_along(): return lax.ppermute(block, axis, route)  2.95 us
    concatenate x1, local copies, waits for them, and re-layouts, shards(): return jnp.concatenate(pieces, axis=1)  2.28 us
    dot_general x1, matrix products, shards(): jnp.dot(placing, pre, preferred_element_type=jnp.float32)  2.28 us
    concatenate x1, other arithmetic, shards(): return jnp.concatenate(pieces, axis=1)  2.16 us
  transfers between devices with their start and end apart: 7, of which 4 were waited for; matrix products, arithmetic and copies ran while one was open for 15% of the time, Pallas kernels for 0%

commit v1 on v0

v1 whole, which is shorter than its diff:
```python
import functools

import jax
import jax.numpy as jnp
from jax import lax
from jax.experimental import pallas as pl
from jax.experimental.pallas import tpu as pltpu
from jax.sharding import PartitionSpec as P

STEPS = 4
CHUNKS = 2
VMEM_BYTES = 16 * 1024 * 1024


def params():
    return pltpu.CompilerParams(vmem_limit_bytes=VMEM_BYTES)


def whole_spec():
    return pl.BlockSpec(memory_space=pltpu.VMEM)


def prepare_kernel(queries, precond, rank, *chunks):
    rows = queries.shape[0]
    positions = lax.broadcasted_iota(jnp.int32, (rows, rows), 0)
    placing = (positions == rank[...]).astype(jnp.bfloat16)
    width = chunks[0].shape[1]
    for n, chunk in enumerate(chunks):
        cut = slice(n * width, (n + 1) * width)
        pre = (queries[:, cut].astype(jnp.float32) * precond[:, cut]).astype(jnp.bfloat16)
        chunk[...] = jnp.dot(placing, pre, preferred_element_type=jnp.float32).astype(jnp.bfloat16)


def prepare(queries, precond, rank):
    rows, depth = queries.shape
    shape = jax.ShapeDtypeStruct((rows, depth // CHUNKS), jnp.bfloat16)
    return pl.pallas_call(
        prepare_kernel,
        out_shape=[shape] * CHUNKS,
        in_specs=[whole_spec()] * 3,
        out_specs=[whole_spec()] * CHUNKS,
        compiler_params=params(),
        cost_estimate=pl.CostEstimate(
            flops=2 * rows * rows * depth, bytes_accessed=4 * rows * depth, transcendentals=0
        ),
    )(queries, precond, rank)


def scores_kernel(cuts, carried, *refs):
    store, blocks = refs[0], refs[1:1 + len(cuts)]
    carry = refs[1 + len(cuts):-2]
    send, own = refs[-2:]
    half = send.shape[0]
    me = lax.axis_index("dim")
    for where, out in ((1 - me, send), (me, own)):
        rows = pl.ds(pl.multiple_of(where * half, half), half)
        total = None
        if carried:
            total = (carry[0] if out is send else carry[1])[...]
        for n, block in zip(cuts, blocks):
            width = block.shape[1]
            part = lax.dot_general(
                store[rows, n * width:(n + 1) * width],
                block[...],
                (((1,), (1,)), ((), ())),
                preferred_element_type=jnp.float32,
            )
            total = part if total is None else total + part
        out[...] = total


def partial_scores(store, blocks, carry=()):
    cuts = [n for n, _ in blocks]
    blocks = [block for _, block in blocks]
    rows, columns = store.shape[0], blocks[0].shape[0]
    shape = jax.ShapeDtypeStruct((rows // 2, columns), jnp.float32)
    operands = [store, *blocks, *carry]
    depth = sum(block.shape[1] for block in blocks)
    return pl.pallas_call(
        functools.partial(scores_kernel, cuts, bool(carry)),
        out_shape=[shape] * 2,
        in_specs=[whole_spec()] * len(operands),
        out_specs=[whole_spec()] * 2,
        compiler_params=params(),
        cost_estimate=pl.CostEstimate(
            flops=2 * rows * columns * depth,
            bytes_accessed=2 * (rows + columns) * depth + 4 * rows * columns,
            transcendentals=0,
        ),
    )(*operands)


def finish_kernel(places, valid, *refs):
    out = refs[-1]
    half, columns = refs[0].shape
    me = lax.axis_index("dim")
    odd = lax.rem(lax.axis_index("ex"), 2)
    row_ids = lax.broadcasted_iota(jnp.int32, (half, columns), 0) + me * half
    keep = row_ids < valid[0]
    for n, place in enumerate(places):
        step = place[0] + odd * (place[1] - place[0])
        total = refs[2 * n][...] + refs[2 * n + 1][...]
        out[:, pl.ds(pl.multiple_of(step * columns, columns), columns)] = jnp.where(keep, total, 0.0)


def finish(valid, pairs, places):
    half, columns = pairs[0][0].shape
    operands = [ref for pair in pairs for ref in pair]
    return pl.pallas_call(
        functools.partial(finish_kernel, places),
        out_shape=jax.ShapeDtypeStruct((half, columns * len(pairs)), jnp.float32),
        in_specs=[pl.BlockSpec(memory_space=pltpu.SMEM)] + [whole_spec()] * len(operands),
        out_specs=whole_spec(),
        compiler_params=params(),
        cost_estimate=pl.CostEstimate(
            flops=half * columns * len(pairs),
            bytes_accessed=12 * half * columns * len(pairs),
            transcendentals=0,
        ),
    )(valid, *operands)


def shards(store, queries, precond, query_rank, valid_rows):
    size = lax.axis_size("ex")
    ahead = [(i, (i + 2) % size) for i in range(size)]
    swap = [(i, i ^ 1) for i in range(size)]
    to_odd = [(i, i + 1) for i in range(0, size, 2)]
    even_ahead = [(i, (i + 2) % size) for i in range(0, size, 2)]
    over_dim = [(0, 1), (1, 0)]

    own = prepare(queries, precond[None, :], query_rank)
    chunks = range(CHUNKS)
    two_back = [lax.ppermute(own[n], "ex", ahead) for n in chunks]
    odd_one_back = [lax.ppermute(own[n], "ex", to_odd) for n in chunks]
    swapped = [lax.ppermute(two_back[n], "ex", swap) for n in chunks]
    even_three_back = [lax.ppermute(swapped[n], "ex", even_ahead) for n in chunks]

    pairs = []
    for blocks in (own, two_back, swapped):
        send, kept = partial_scores(store, list(enumerate(blocks)))
        pairs.append((kept, lax.ppermute(send, "dim", over_dim)))
    carry = partial_scores(store, list(enumerate(odd_one_back)))
    for n in chunks:
        carry = partial_scores(store, [(n, even_three_back[n])], (carry[0], carry[1]))
    pairs.append((carry[1], lax.ppermute(carry[0], "dim", over_dim)))
    return finish(valid_rows, pairs, ((0, 0), (2, 2), (1, 3), (3, 1)))


def solution(mesh):
    return jax.shard_map(
        shards,
        mesh=mesh,
        in_specs=(
            P(("groups", "ex"), "dim"),
            P(("groups", "ex"), "dim"),
            P("dim"),
            P(("groups", "ex"), None),
            P(("groups", "ex")),
        ),
        out_specs=P(("groups", "ex", "dim"), None),
        check_vma=False,
    )
```

time: 77.9 us -> 44.7 us (0.57)
  waiting for transfers between devices: 41.9 us -> 16.1 us
  matrix products: 14.2 us -> 0 us
  between operations: 13.8 us -> 0.83 us
  starting transfers between devices: 3.07 us -> 16 us
  Pallas kernels: 0 us -> 6.29 us
  local copies, waits for them, and re-layouts: 2.28 us -> 5.12 us
  other arithmetic: 2.16 us -> 0 us
    ppermute x3 -> x12, waiting for transfers between devices: 36.7 us -> 16.1 us  [the longest x2 10.6 us: shards(): two_back = [lax.ppermute(own[n], 'ex', ahead) for n in chunks]]
    dot_general x5 -> x0, matrix products: 14.2 us -> none  [the longest x4 12 us: shards(): lax.dot_general(store, block, (((1,), (1,)), ((), ())), preferred_element...]
    ppermute x3 -> x12, starting transfers between devices: 2.95 us -> 16 us  [the longest x2 4.65 us: shards(): two_back = [lax.ppermute(own[n], 'ex', ahead) for n in chunks]]
    pallas_call x0 -> x8, Pallas kernels: none -> 6.29 us  [the longest x6 4.99 us: partial_scores(): pl.pallas_call(functools.partial(scores_kernel, cuts, bool(carry)), out_s...]
    reduce_scatter x4 -> x0, waiting for transfers between devices: 5.16 us -> none  [shards(): lax.psum_scatter(jnp.where(keep, result, jnp.float32(0.0)), 'dim', scatte...]
    unnamed x2 -> x10, local copies, waits for them, and re-layouts: 0.01 us -> 5.12 us
    concatenate x1 -> x0, local copies, waits for them, and re-layouts: 2.28 us -> none  [shards(): return jnp.concatenate(pieces, axis=1)]
    concatenate x1 -> x0, other arithmetic: 2.16 us -> none  [shards(): return jnp.concatenate(pieces, axis=1)]
  transfers between devices with their start and end apart: 7 -> 12, of which waited for: 4 -> 6; matrix products, arithmetic and copies ran while one was open for 15% -> 0% of each run, Pallas kernels for 0% -> 11%
where the time goes in v1:
time: 44.7 us; the launch traced here: 44.3 us
  waiting for transfers between devices  16.1 us (36%)
  starting transfers between devices  16 us (36%)
  Pallas kernels  6.29 us (14%)
  local copies, waits for them, and re-layouts  5.12 us (11%)
  between operations  0.83 us (2%)
    ppermute x2, waiting for transfers between devices, shards(): two_back = [lax.ppermute(own[n], 'ex', ahead) for n in chunks]  10.6 us
    unnamed x10, local copies, waits for them, and re-layouts  5.12 us
    pallas_call x6, Pallas kernels, partial_scores(): pl.pallas_call(functools.partial(scores_kernel, cuts, bool(carry)), out_s...  4.99 us
    ppermute x2, starting transfers between devices, shards(): two_back = [lax.ppermute(own[n], 'ex', ahead) for n in chunks]  4.65 us
    ppermute x2, starting transfers between devices, shards(): lax.ppermute(swapped[n], 'ex', even_ahead)  4.05 us
    ppermute x2, starting transfers between devices, shards(): odd_one_back = [lax.ppermute(own[n], 'ex', to_odd) for n in chunks]  3.74 us
    ppermute x2, starting transfers between devices, shards(): swapped = [lax.ppermute(two_back[n], 'ex', swap) for n in chunks]  3.23 us
    ppermute x2, waiting for transfers between devices, shards(): odd_one_back = [lax.ppermute(own[n], 'ex', to_odd) for n in chunks]  2.45 us
  transfers between devices with their start and end apart: 12, of which 6 were waited for; matrix products, arithmetic and copies ran while one was open for 0% of the time, Pallas kernels for 11%

profile of v1, /device:TPU:0, one launch (start us, length us, event | category | flops | bytes accessed | tf_op | source)
XLA Modules:
  0.0 44.3 jit_solution(18265227072184711649)
XLA Ops:
  0.0 1.0 %copy-done.2 = bf16[128,2048]{1,0:T(8,128)(2,1)S(1)} copy-done((bf16[128,2048]{1,0:T(8,128)(2,1)S(1)}, bf16[128,2048]{1,0:T(8,128)(2,1)}, u32[]{:S(2)}) %copy-start.2) | copy-done | bytes 524312
  1.0 0.7 %copy-done.3 = f32[2048]{0:T(1024)S(1)} copy-done((f32[2048]{0:T(1024)S(1)}, f32[2048]{0:T(1024)}, u32[]{:S(2)}) %copy-start.3) | copy-done | bytes 8216
  1.7 0.7 %copy-done.4 = s32[1,128]{1,0:T(1,128)S(1)} copy-done((s32[1,128]{1,0:T(1,128)S(1)}, s32[1,128]{1,0:T(1,128)}, u32[]{:S(2)}) %copy-start.4) | copy-done | bytes 536
  2.7 3.1 %collective-permute-start.1 = (bf16[128,1024]{1,0:T(8,128)(2,1)S(1)}, bf16[128,1024]{1,0:T(8,128)(2,1)S(1)}, u32[]{:S(2)}, u32[]{:S(2)}) collective-permute-start(bf16[128,1024]{1,0:T(8,128)(2,1)S(1)} %get-tuple-element.19.refs_1_), channel_id=1, source_target_pairs={{0,4},{2,6},{4,8},{6,10},{8,12},{10,14},{12,0},{14,2},{1,5},{3,7},... | collective-permute-start | bytes 786440 | tf_op jit(solution)/shard_map/ppermute | solution.py:133
  5.8 1.6 %collective-permute-start.2 = (bf16[128,1024]{1,0:T(8,128)(2,1)S(1)}, bf16[128,1024]{1,0:T(8,128)(2,1)S(1)}, u32[]{:S(2)}, u32[]{:S(2)}) collective-permute-start(bf16[128,1024]{1,0:T(8,128)(2,1)S(1)} %get-tuple-element.20.refs_2_), channel_id=1, source_target_pairs={{0,4},{2,6},{4,8},{6,10},{8,12},{10,14},{12,0},{14,2},{1,5},{3,7},... | collective-permute-start | bytes 786440 | tf_op jit(solution)/shard_map/ppermute | solution.py:133
  7.4 7.6 %collective-permute-done.1.refs_1_ = bf16[128,1024]{1,0:T(8,128)(2,1)S(1)} collective-permute-done((bf16[128,1024]{1,0:T(8,128)(2,1)S(1)}, bf16[128,1024]{1,0:T(8,128)(2,1)S(1)}, u32[]{:S(2)}, u32[]{:S(2)}) %collective-permute-start.1) | collective-permute-done | bytes 262176 | tf_op jit(solution)/shard_map/ppermute | solution.py:133
  14.9 1.7 %collective-permute-start.4 = (bf16[128,1024]{1,0:T(8,128)(2,1)S(1)}, bf16[128,1024]{1,0:T(8,128)(2,1)S(1)}, u32[]{:S(2)}, u32[]{:S(2)}) collective-permute-start(bf16[128,1024]{1,0:T(8,128)(2,1)S(1)} %collective-permute-done.1.refs_1_), channel_id=1, source_target_pairs={{0,2},{2,0},{4,6},{6,4},{8,10},{10,8},{12,14},{14,12},{1,3},{3,1},... | collective-permute-start | bytes 786440 | tf_op jit(solution)/shard_map/ppermute | solution.py:135
  16.7 3.0 %collective-permute-done.2.refs_2_ = bf16[128,1024]{1,0:T(8,128)(2,1)S(1)} collective-permute-done((bf16[128,1024]{1,0:T(8,128)(2,1)S(1)}, bf16[128,1024]{1,0:T(8,128)(2,1)S(1)}, u32[]{:S(2)}, u32[]{:S(2)}) %collective-permute-start.2) | collective-permute-done | bytes 262176 | tf_op jit(solution)/shard_map/ppermute | solution.py:133
  19.7 1.5 %collective-permute-start.5 = (bf16[128,1024]{1,0:T(8,128)(2,1)S(1)}, bf16[128,1024]{1,0:T(8,128)(2,1)S(1)}, u32[]{:S(2)}, u32[]{:S(2)}) collective-permute-start(bf16[128,1024]{1,0:T(8,128)(2,1)S(1)} %collective-permute-done.2.refs_2_), channel_id=1, source_target_pairs={{0,2},{2,0},{4,6},{6,4},{8,10},{10,8},{12,14},{14,12},{1,3},{3,1},... | collective-permute-start | bytes 786440 | tf_op jit(solution)/shard_map/ppermute | solution.py:135
  21.2 2.4 %collective-permute-start.9 = (bf16[128,1024]{1,0:T(8,128)(2,1)S(1)}, bf16[128,1024]{1,0:T(8,128)(2,1)S(1)}, u32[]{:S(2)}, u32[]{:S(2)}) collective-permute-start(bf16[128,1024]{1,0:T(8,128)(2,1)S(1)} %get-tuple-element.19.refs_1_), channel_id=1, source_target_pairs={{0,2},{4,6},{8,10},{12,14},{1,3},{5,7},{9,11},{13,15},{16,18},{20,... | collective-permute-start | bytes 786440 | tf_op jit(solution)/shard_map/ppermute | solution.py:134
  23.7 1.3 %collective-permute-start.10 = (bf16[128,1024]{1,0:T(8,128)(2,1)S(1)}, bf16[128,1024]{1,0:T(8,128)(2,1)S(1)}, u32[]{:S(2)}, u32[]{:S(2)}) collective-permute-start(bf16[128,1024]{1,0:T(8,128)(2,1)S(1)} %get-tuple-element.20.refs_2_), channel_id=1, source_target_pairs={{0,2},{4,6},{8,10},{12,14},{1,3},{5,7},{9,11},{13,15},{16,18},{20,... | collective-permute-start | bytes 786440 | tf_op jit(solution)/shard_map/ppermute | solution.py:134
  25.0 1.9 %collective-permute-start.8 = (bf16[128,1024]{1,0:T(8,128)(2,1)S(1)}, bf16[128,1024]{1,0:T(8,128)(2,1)S(1)}, u32[]{:S(2)}, u32[]{:S(2)}) collective-permute-start(bf16[128,1024]{1,0:T(8,128)(2,1)S(1)} %collective-permute-done.4.refs_1_), channel_id=1, source_target_pairs={{0,4},{4,8},{8,12},{12,0},{1,5},{5,9},{9,13},{13,1},{16,20},{20,24... | collective-permute-start | bytes 786440 | tf_op jit(solution)/shard_map/ppermute | solution.py:136
  26.9 1.1 %collective-permute-done.5.refs_2_ = bf16[128,1024]{1,0:T(8,128)(2,1)S(1)} collective-permute-done((bf16[128,1024]{1,0:T(8,128)(2,1)S(1)}, bf16[128,1024]{1,0:T(8,128)(2,1)S(1)}, u32[]{:S(2)}, u32[]{:S(2)}) %collective-permute-start.5) | collective-permute-done | bytes 262176 | tf_op jit(solution)/shard_map/ppermute | solution.py:135
  28.0 2.1 %collective-permute-start.7 = (bf16[128,1024]{1,0:T(8,128)(2,1)S(1)}, bf16[128,1024]{1,0:T(8,128)(2,1)S(1)}, u32[]{:S(2)}, u32[]{:S(2)}) collective-permute-start(bf16[128,1024]{1,0:T(8,128)(2,1)S(1)} %collective-permute-done.5.refs_2_), channel_id=1, source_target_pairs={{0,4},{4,8},{8,12},{12,0},{1,5},{5,9},{9,13},{13,1},{16,20},{20,24... | collective-permute-start | bytes 786440 | tf_op jit(solution)/shard_map/ppermute | solution.py:136
  30.1 1.9 %copy-done = bf16[768,2048]{1,0:T(8,128)(2,1)S(1)} copy-done((bf16[768,2048]{1,0:T(8,128)(2,1)S(1)}, bf16[768,2048]{1,0:T(8,128)(2,1)}, u32[]{:S(2)}) %copy-start) | copy-done | bytes 3145752
  32.0 1.0 %shard_map.56 = (f32[384,128]{1,0:T(8,128)S(1)}, f32[384,128]{1,0:T(8,128)S(1)}) custom-call(bf16[768,2048]{1,0:T(8,128)(2,1)S(1)} %copy-done, bf16[128,1024]{1,0:T(8,128)(2,1)S(1)} %get-tuple-element.19.refs_1_, bf16[128,1024]{1,0:T(8,128)(2,1)S(1)} %get-tuple-element.20.refs_2_), custom_call_target="tpu_custom_call" | custom-call | flops 402653184 | bytes 4063232 | tf_op jit(solution)/shard_map/pallas_call | solution.py:79
  33.1 0.8 %copy-done.1 = bf16[768,2048]{1,0:T(8,128)(2,1)S(1)} copy-done((bf16[768,2048]{1,0:T(8,128)(2,1)S(1)}, bf16[768,2048]{1,0:T(8,128)(2,1)}, u32[]{:S(2)}) %copy-start.1) | copy-done | bytes 3145752
  33.9 1.0 %shard_map.57 = (f32[384,128]{1,0:T(8,128)S(1)}, f32[384,128]{1,0:T(8,128)S(1)}) custom-call(bf16[768,2048]{1,0:T(8,128)(2,1)S(1)} %copy-done.1, bf16[128,1024]{1,0:T(8,128)(2,1)S(1)} %collective-permute-done.1.refs_1_, bf16[128,1024]{1,0:T(8,128)(2,1)S(1)} %collective-permute-done.2.refs_2_), custom_call_target="tpu_custom_call" | custom-call | flops 402653184 | bytes 4063232 | tf_op jit(solution)/shard_map/pallas_call | solution.py:79
  35.0 2.5 %collective-permute-done.10.refs_2_ = bf16[128,1024]{1,0:T(8,128)(2,1)S(1)} collective-permute-done((bf16[128,1024]{1,0:T(8,128)(2,1)S(1)}, bf16[128,1024]{1,0:T(8,128)(2,1)S(1)}, u32[]{:S(2)}, u32[]{:S(2)}) %collective-permute-start.10) | collective-permute-done | bytes 262176 | tf_op jit(solution)/shard_map/ppermute | solution.py:134
  37.4 1.0 %shard_map.59 = (f32[384,128]{1,0:T(8,128)S(1)}, f32[384,128]{1,0:T(8,128)S(1)}) custom-call(bf16[768,2048]{1,0:T(8,128)(2,1)S(1)} %copy-done.1, bf16[128,1024]{1,0:T(8,128)(2,1)S(1)} %collective-permute-done.9.refs_1_, bf16[128,1024]{1,0:T(8,128)(2,1)S(1)} %collective-permute-done.10.refs_2_), custom_call_target="tpu_custom_call" | custom-call | flops 402653184 | bytes 4063232 | tf_op jit(solution)/shard_map/pallas_call | solution.py:79
  38.4 1.0 %shard_map.58 = (f32[384,128]{1,0:T(8,128)S(1)}, f32[384,128]{1,0:T(8,128)S(1)}) custom-call(bf16[768,2048]{1,0:T(8,128)(2,1)S(1)} %copy-done.1, bf16[128,1024]{1,0:T(8,128)(2,1)S(1)} %collective-permute-done.4.refs_1_, bf16[128,1024]{1,0:T(8,128)(2,1)S(1)} %collective-permute-done.5.refs_2_), custom_call_target="tpu_custom_call" | custom-call | flops 402653184 | bytes 4063232 | tf_op jit(solution)/shard_map/pallas_call | solution.py:79
  40.0 1.2 %collective-permute-done.7.refs_1_ = bf16[128,1024]{1,0:T(8,128)(2,1)S(1)} collective-permute-done((bf16[128,1024]{1,0:T(8,128)(2,1)S(1)}, bf16[128,1024]{1,0:T(8,128)(2,1)S(1)}, u32[]{:S(2)}, u32[]{:S(2)}) %collective-permute-start.7) | collective-permute-done | bytes 262176 | tf_op jit(solution)/shard_map/ppermute | solution.py:136
  42.6 0.8 %collective-permute-done.11.refs_7_ = f32[384,128]{1,0:T(8,128)S(1)} collective-permute-done((f32[384,128]{1,0:T(8,128)S(1)}, f32[384,128]{1,0:T(8,128)S(1)}, u32[]{:S(2)}, u32[]{:S(2)}) %collective-permute-start.11) | collective-permute-done | bytes 196640 | tf_op jit(solution)/shard_map/ppermute | solution.py:145
  43.3 1.0 %shard_map.62 = f32[384,512]{1,0:T(8,128)} custom-call(s32[1]{0:T(128)S(6)} %copy.6.valid, f32[384,128]{1,0:T(8,128)S(1)} %get-tuple-element.21.refs_0_, f32[384,128]{1,0:T(8,128)S(1)} %collective-permute-done.refs_1_, f32[384,128]{1,0:T(8,128)S(1)} %get-tuple-element.23.refs_2_, f32[384,128]{1,0:T(8,128)S(1)} %collective-permute-done.3.refs_3_, ...), custom_call_target="tpu_custom_call" | custom-call | flops 196608 | bytes 2359296 | tf_op jit(solution)/shard_map/pallas_call | solution.py:109
  (18 shorter events, 1.8 us)
Async XLA Ops:
  0.0 1.0 %copy-start.2 = (bf16[128,2048]{1,0:T(8,128)(2,1)S(1)}, bf16[128,2048]{1,0:T(8,128)(2,1)}, u32[]{:S(2)}) copy-start(bf16[128,2048]{1,0:T(8,128)(2,1)} %queries.1) | copy-start | bytes 1572868
  1.0 0.7 %copy-start.3 = (f32[2048]{0:T(1024)S(1)}, f32[2048]{0:T(1024)}, u32[]{:S(2)}) copy-start(f32[2048]{0:T(1024)} %param.7) | copy-start | bytes 24580
  1.7 0.7 %copy-start.4 = (s32[1,128]{1,0:T(1,128)S(1)}, s32[1,128]{1,0:T(1,128)}, u32[]{:S(2)}) copy-start(s32[1,128]{1,0:T(1,128)} %rank.1) | copy-start | bytes 1540
  2.7 12.2 %collective-permute-start.1 = (bf16[128,1024]{1,0:T(8,128)(2,1)S(1)}, bf16[128,1024]{1,0:T(8,128)(2,1)S(1)}, u32[]{:S(2)}, u32[]{:S(2)}) collective-permute-start(bf16[128,1024]{1,0:T(8,128)(2,1)S(1)} %get-tuple-element.19.refs_1_), channel_id=1, source_target_pairs={{0,4},{2,6},{4,8},{6,10},{8,12},{10,14},{12,0},{14,2},{1,5},{3,7},... | collective-permute-start | bytes 786440 | tf_op jit(solution)/shard_map/ppermute | solution.py:133
  5.8 13.9 %collective-permute-start.2 = (bf16[128,1024]{1,0:T(8,128)(2,1)S(1)}, bf16[128,1024]{1,0:T(8,128)(2,1)S(1)}, u32[]{:S(2)}, u32[]{:S(2)}) collective-permute-start(bf16[128,1024]{1,0:T(8,128)(2,1)S(1)} %get-tuple-element.20.refs_2_), channel_id=1, source_target_pairs={{0,4},{2,6},{4,8},{6,10},{8,12},{10,14},{12,0},{14,2},{1,5},{3,7},... | collective-permute-start | bytes 786440 | tf_op jit(solution)/shard_map/ppermute | solution.py:133
  14.9 10.0 %collective-permute-start.4 = (bf16[128,1024]{1,0:T(8,128)(2,1)S(1)}, bf16[128,1024]{1,0:T(8,128)(2,1)S(1)}, u32[]{:S(2)}, u32[]{:S(2)}) collective-permute-start(bf16[128,1024]{1,0:T(8,128)(2,1)S(1)} %collective-permute-done.1.refs_1_), channel_id=1, source_target_pairs={{0,2},{2,0},{4,6},{6,4},{8,10},{10,8},{12,14},{14,12},{1,3},{3,1},... | collective-permute-start | bytes 786440 | tf_op jit(solution)/shard_map/ppermute | solution.py:135
  19.7 8.3 %collective-permute-start.5 = (bf16[128,1024]{1,0:T(8,128)(2,1)S(1)}, bf16[128,1024]{1,0:T(8,128)(2,1)S(1)}, u32[]{:S(2)}, u32[]{:S(2)}) collective-permute-start(bf16[128,1024]{1,0:T(8,128)(2,1)S(1)} %collective-permute-done.2.refs_2_), channel_id=1, source_target_pairs={{0,2},{2,0},{4,6},{6,4},{8,10},{10,8},{12,14},{14,12},{1,3},{3,1},... | collective-permute-start | bytes 786440 | tf_op jit(solution)/shard_map/ppermute | solution.py:135
  21.2 13.7 %collective-permute-start.9 = (bf16[128,1024]{1,0:T(8,128)(2,1)S(1)}, bf16[128,1024]{1,0:T(8,128)(2,1)S(1)}, u32[]{:S(2)}, u32[]{:S(2)}) collective-permute-start(bf16[128,1024]{1,0:T(8,128)(2,1)S(1)} %get-tuple-element.19.refs_1_), channel_id=1, source_target_pairs={{0,2},{4,6},{8,10},{12,14},{1,3},{5,7},{9,11},{13,15},{16,18},{20,... | collective-permute-start | bytes 786440 | tf_op jit(solution)/shard_map/ppermute | solution.py:134
  23.7 13.8 %collective-permute-start.10 = (bf16[128,1024]{1,0:T(8,128)(2,1)S(1)}, bf16[128,1024]{1,0:T(8,128)(2,1)S(1)}, u32[]{:S(2)}, u32[]{:S(2)}) collective-permute-start(bf16[128,1024]{1,0:T(8,128)(2,1)S(1)} %get-tuple-element.20.refs_2_), channel_id=1, source_target_pairs={{0,2},{4,6},{8,10},{12,14},{1,3},{5,7},{9,11},{13,15},{16,18},{20,... | collective-permute-start | bytes 786440 | tf_op jit(solution)/shard_map/ppermute | solution.py:134
  25.0 14.5 %collective-permute-start.8 = (bf16[128,1024]{1,0:T(8,128)(2,1)S(1)}, bf16[128,1024]{1,0:T(8,128)(2,1)S(1)}, u32[]{:S(2)}, u32[]{:S(2)}) collective-permute-start(bf16[128,1024]{1,0:T(8,128)(2,1)S(1)} %collective-permute-done.4.refs_1_), channel_id=1, source_target_pairs={{0,4},{4,8},{8,12},{12,0},{1,5},{5,9},{9,13},{13,1},{16,20},{20,24... | collective-permute-start | bytes 786440 | tf_op jit(solution)/shard_map/ppermute | solution.py:136
  28.0 13.2 %collective-permute-start.7 = (bf16[128,1024]{1,0:T(8,128)(2,1)S(1)}, bf16[128,1024]{1,0:T(8,128)(2,1)S(1)}, u32[]{:S(2)}, u32[]{:S(2)}) collective-permute-start(bf16[128,1024]{1,0:T(8,128)(2,1)S(1)} %collective-permute-done.5.refs_2_), channel_id=1, source_target_pairs={{0,4},{4,8},{8,12},{12,0},{1,5},{5,9},{9,13},{13,1},{16,20},{20,24... | collective-permute-start | bytes 786440 | tf_op jit(solution)/shard_map/ppermute | solution.py:136
  30.1 1.9 %copy-start = (bf16[768,2048]{1,0:T(8,128)(2,1)S(1)}, bf16[768,2048]{1,0:T(8,128)(2,1)}, u32[]{:S(2)}) copy-start(bf16[768,2048]{1,0:T(8,128)(2,1)} %refs_0_.11) | copy-start | bytes 9437188
  32.0 1.9 %copy-start.1 = (bf16[768,2048]{1,0:T(8,128)(2,1)S(1)}, bf16[768,2048]{1,0:T(8,128)(2,1)}, u32[]{:S(2)}) copy-start(bf16[768,2048]{1,0:T(8,128)(2,1)} %refs_0_.11) | copy-start | bytes 9437188
  33.0 9.5 %collective-permute-start = (f32[384,128]{1,0:T(8,128)S(1)}, f32[384,128]{1,0:T(8,128)S(1)}, u32[]{:S(2)}, u32[]{:S(2)}) collective-permute-start(f32[384,128]{1,0:T(8,128)S(1)} %get-tuple-element.22), channel_id=1, source_target_pairs={{0,1},{1,0},{2,3},{3,2},{4,5},{5,4},{6,7},{7,6},{8,9},{9,8},{10,11... | collective-permute-start | bytes 589832 | tf_op jit(solution)/shard_map/ppermute | solution.py:141
  34.9 7.7 %collective-permute-start.3 = (f32[384,128]{1,0:T(8,128)S(1)}, f32[384,128]{1,0:T(8,128)S(1)}, u32[]{:S(2)}, u32[]{:S(2)}) collective-permute-start(f32[384,128]{1,0:T(8,128)S(1)} %get-tuple-element.24), channel_id=1, source_target_pairs={{0,1},{1,0},{2,3},{3,2},{4,5},{5,4},{6,7},{7,6},{8,9},{9,8},{10,11... | collective-permute-start | bytes 589832 | tf_op jit(solution)/shard_map/ppermute | solution.py:141
  39.4 3.2 %collective-permute-start.6 = (f32[384,128]{1,0:T(8,128)S(1)}, f32[384,128]{1,0:T(8,128)S(1)}, u32[]{:S(2)}, u32[]{:S(2)}) collective-permute-start(f32[384,128]{1,0:T(8,128)S(1)} %get-tuple-element.26), channel_id=1, source_target_pairs={{0,1},{1,0},{2,3},{3,2},{4,5},{5,4},{6,7},{7,6},{8,9},{9,8},{10,11... | collective-permute-start | bytes 589832 | tf_op jit(solution)/shard_map/ppermute | solution.py:141
  41.8 1.5 %collective-permute-start.11 = (f32[384,128]{1,0:T(8,128)S(1)}, f32[384,128]{1,0:T(8,128)S(1)}, u32[]{:S(2)}, u32[]{:S(2)}) collective-permute-start(f32[384,128]{1,0:T(8,128)S(1)} %get-tuple-element.32), channel_id=1, source_target_pairs={{0,1},{1,0},{2,3},{3,2},{4,5},{5,4},{6,7},{7,6},{8,9},{9,8},{10,11... | collective-permute-start | bytes 589832 | tf_op jit(solution)/shard_map/ppermute | solution.py:145

commit v2 on v1

--- a/solution.py
+++ b/solution.py
@@ -20,15 +20,33 @@
     return pl.BlockSpec(memory_space=pltpu.VMEM)
 
 
-def prepare_kernel(queries, precond, rank, *chunks):
-    rows = queries.shape[0]
+def far_spec():
+    return pl.BlockSpec(memory_space=pltpu.HBM)
+
+
+def prepare_kernel(queries, precond, rank, *refs):
+    chunks, (held, scale, places, ready, arrived, left) = refs[:CHUNKS], refs[CHUNKS:]
+    rows, width = chunks[0].shape
+    cuts = [slice(n * width, (n + 1) * width) for n in range(CHUNKS)]
+    loads = [pltpu.make_async_copy(rank, places, arrived.at[CHUNKS])]
+    loads.append(pltpu.make_async_copy(precond, scale, arrived.at[CHUNKS + 1]))
+    for n, cut in enumerate(cuts):
+        loads.append(pltpu.make_async_copy(queries.at[:, cut], held.at[:, cut], arrived.at[n]))
+    for load in loads:
+        load.start()
+    loads[0].wait()
+    loads[1].wait()
     positions = lax.broadcasted_iota(jnp.int32, (rows, rows), 0)
-    placing = (positions == rank[...]).astype(jnp.bfloat16)
-    width = chunks[0].shape[1]
-    for n, chunk in enumerate(chunks):
-        cut = slice(n * width, (n + 1) * width)
-        pre = (queries[:, cut].astype(jnp.float32) * precond[:, cut]).astype(jnp.bfloat16)
-        chunk[...] = jnp.dot(placing, pre, preferred_element_type=jnp.float32).astype(jnp.bfloat16)
+    placing = (positions == places[...]).astype(jnp.bfloat16)
+    stores = []
+    for n, cut in enumerate(cuts):
+        loads[2 + n].wait()
+        pre = (held[:, cut].astype(jnp.float32) * scale[:, cut]).astype(jnp.bfloat16)
+        ready[:, cut] = jnp.dot(placing, pre, preferred_element_type=jnp.float32).astype(jnp.bfloat16)
+        stores.append(pltpu.make_async_copy(ready.at[:, cut], chunks[n], left.at[n]))
+        stores[n].start()
+    for store in stores:
+        store.wait()
 
 
 def prepare(queries, precond, rank):
@@ -37,8 +55,16 @@
     return pl.pallas_call(
         prepare_kernel,
         out_shape=[shape] * CHUNKS,
-        in_specs=[whole_spec()] * 3,
-        out_specs=[whole_spec()] * CHUNKS,
+        in_specs=[far_spec()] * 3,
+        out_specs=[far_spec()] * CHUNKS,
+        scratch_shapes=[
+            pltpu.VMEM((rows, depth), jnp.bfloat16),
+            pltpu.VMEM((1, depth), jnp.float32),
+            pltpu.VMEM((1, rows), jnp.int32),
+            pltpu.VMEM((rows, depth), jnp.bfloat16),
+            pltpu.SemaphoreType.DMA((CHUNKS + 2,)),
+            pltpu.SemaphoreType.DMA((CHUNKS,)),
+        ],
         compiler_params=params(),
         cost_estimate=pl.CostEstimate(
             flops=2 * rows * rows * depth, bytes_accessed=4 * rows * depth, transcendentals=0
@@ -48,20 +74,27 @@
 
 def scores_kernel(cuts, carried, *refs):
     store, blocks = refs[0], refs[1:1 + len(cuts)]
-    carry = refs[1 + len(cuts):-2]
-    send, own = refs[-2:]
+    carry = refs[1 + len(cuts):-4]
+    send, own, held, arrived = refs[-4:]
     half = send.shape[0]
     me = lax.axis_index("dim")
+    loads = [
+        pltpu.make_async_copy(block, held.at[n], arrived.at[n]) for n, block in enumerate(blocks)
+    ]
+    for load in loads:
+        load.start()
+    for load in loads:
+        load.wait()
     for where, out in ((1 - me, send), (me, own)):
         rows = pl.ds(pl.multiple_of(where * half, half), half)
         total = None
         if carried:
             total = (carry[0] if out is send else carry[1])[...]
-        for n, block in zip(cuts, blocks):
-            width = block.shape[1]
+        for slot, n in enumerate(cuts):
+            width = held.shape[2]
             part = lax.dot_general(
                 store[rows, n * width:(n + 1) * width],
-                block[...],
+                held[slot],
                 (((1,), (1,)), ((), ())),
                 preferred_element_type=jnp.float32,
             )
@@ -72,22 +105,25 @@
 def partial_scores(store, blocks, carry=()):
     cuts = [n for n, _ in blocks]
     blocks = [block for _, block in blocks]
-    rows, columns = store.shape[0], blocks[0].shape[0]
+    rows, (columns, width) = store.shape[0], blocks[0].shape
     shape = jax.ShapeDtypeStruct((rows // 2, columns), jnp.float32)
-    operands = [store, *blocks, *carry]
-    depth = sum(block.shape[1] for block in blocks)
+    depth = len(blocks) * width
     return pl.pallas_call(
         functools.partial(scores_kernel, cuts, bool(carry)),
         out_shape=[shape] * 2,
-        in_specs=[whole_spec()] * len(operands),
+        in_specs=[whole_spec()] + [far_spec()] * len(blocks) + [whole_spec()] * len(carry),
         out_specs=[whole_spec()] * 2,
+        scratch_shapes=[
+            pltpu.VMEM((len(blocks), columns, width), jnp.bfloat16),
+            pltpu.SemaphoreType.DMA((len(blocks),)),
+        ],
         compiler_params=params(),
         cost_estimate=pl.CostEstimate(
             flops=2 * rows * columns * depth,
             bytes_accessed=2 * (rows + columns) * depth + 4 * rows * columns,
             transcendentals=0,
         ),
-    )(*operands)
+    )(store, *blocks, *carry)
 
 
 def finish_kernel(places, valid, *refs):

time: 44.7 us -> 45 us (level)
  Pallas kernels: 6.29 us -> 6.93 us
  transfers between devices with their start and end apart: 12 -> 12, of which waited for: 6 -> 6; matrix products, arithmetic and copies ran while one was open for 0% -> 0% of each run, Pallas kernels for 11% -> 12%
where the time goes in v2:
time: 45 us; the launch traced here: 44.6 us
  starting transfers between devices  16 us (36%)
  waiting for transfers between devices  15.9 us (35%)
  Pallas kernels  6.93 us (15%)
  local copies, waits for them, and re-layouts  5.05 us (11%)
  between operations  0.83 us (2%)
    ppermute x2, waiting for transfers between devices, shards(): two_back = [lax.ppermute(own[n], 'ex', ahead) for n in chunks]  10.6 us
    pallas_call x6, Pallas kernels, partial_scores(): pl.pallas_call(functools.partial(scores_kernel, cuts, bool(carry)), out_s...  5.34 us
    unnamed x10, local copies, waits for them, and re-layouts  5.05 us
    ppermute x2, starting transfers between devices, shards(): two_back = [lax.ppermute(own[n], 'ex', ahead) for n in chunks]  4.66 us
    ppermute x2, starting transfers between devices, shards(): lax.ppermute(swapped[n], 'ex', even_ahead)  4.06 us
    ppermute x2, starting transfers between devices, shards(): odd_one_back = [lax.ppermute(own[n], 'ex', to_odd) for n in chunks]  3.74 us
    ppermute x2, starting transfers between devices, shards(): swapped = [lax.ppermute(two_back[n], 'ex', swap) for n in chunks]  3.23 us
    ppermute x2, waiting for transfers between devices, shards(): odd_one_back = [lax.ppermute(own[n], 'ex', to_odd) for n in chunks]  2.39 us
  transfers between devices with their start and end apart: 12, of which 6 were waited for; matrix products, arithmetic and copies ran while one was open for 0% of the time, Pallas kernels for 12%

profile of v2, /device:TPU:0, one launch (start us, length us, event | category | flops | bytes accessed | tf_op | source)
XLA Modules:
  0.0 44.6 jit_solution(14652965152664500999)
XLA Ops:
  0.0 1.0 %copy-done.2 = bf16[128,2048]{1,0:T(8,128)(2,1)S(1)} copy-done((bf16[128,2048]{1,0:T(8,128)(2,1)S(1)}, bf16[128,2048]{1,0:T(8,128)(2,1)}, u32[]{:S(2)}) %copy-start.2) | copy-done | bytes 524312
  1.0 0.7 %copy-done.3 = f32[2048]{0:T(1024)S(1)} copy-done((f32[2048]{0:T(1024)S(1)}, f32[2048]{0:T(1024)}, u32[]{:S(2)}) %copy-start.3) | copy-done | bytes 8216
  1.7 0.7 %copy-done.4 = s32[1,128]{1,0:T(1,128)S(1)} copy-done((s32[1,128]{1,0:T(1,128)S(1)}, s32[1,128]{1,0:T(1,128)}, u32[]{:S(2)}) %copy-start.4) | copy-done | bytes 536
  3.0 3.1 %collective-permute-start.1 = (bf16[128,1024]{1,0:T(8,128)(2,1)S(1)}, bf16[128,1024]{1,0:T(8,128)(2,1)S(1)}, u32[]{:S(2)}, u32[]{:S(2)}) collective-permute-start(bf16[128,1024]{1,0:T(8,128)(2,1)S(1)} %get-tuple-element.19.refs_1_), channel_id=1, source_target_pairs={{0,4},{2,6},{4,8},{6,10},{8,12},{10,14},{12,0},{14,2},{1,5},{3,7},... | collective-permute-start | bytes 786440 | tf_op jit(solution)/shard_map/ppermute | solution.py:169
  6.1 1.6 %collective-permute-start.2 = (bf16[128,1024]{1,0:T(8,128)(2,1)S(1)}, bf16[128,1024]{1,0:T(8,128)(2,1)S(1)}, u32[]{:S(2)}, u32[]{:S(2)}) collective-permute-start(bf16[128,1024]{1,0:T(8,128)(2,1)S(1)} %get-tuple-element.20.refs_2_), channel_id=1, source_target_pairs={{0,4},{2,6},{4,8},{6,10},{8,12},{10,14},{12,0},{14,2},{1,5},{3,7},... | collective-permute-start | bytes 786440 | tf_op jit(solution)/shard_map/ppermute | solution.py:169
  7.7 7.6 %collective-permute-done.1.refs_1_ = bf16[128,1024]{1,0:T(8,128)(2,1)S(1)} collective-permute-done((bf16[128,1024]{1,0:T(8,128)(2,1)S(1)}, bf16[128,1024]{1,0:T(8,128)(2,1)S(1)}, u32[]{:S(2)}, u32[]{:S(2)}) %collective-permute-start.1) | collective-permute-done | bytes 262176 | tf_op jit(solution)/shard_map/ppermute | solution.py:169
  15.2 1.7 %collective-permute-start.4 = (bf16[128,1024]{1,0:T(8,128)(2,1)S(1)}, bf16[128,1024]{1,0:T(8,128)(2,1)S(1)}, u32[]{:S(2)}, u32[]{:S(2)}) collective-permute-start(bf16[128,1024]{1,0:T(8,128)(2,1)S(1)} %collective-permute-done.1.refs_1_), channel_id=1, source_target_pairs={{0,2},{2,0},{4,6},{6,4},{8,10},{10,8},{12,14},{14,12},{1,3},{3,1},... | collective-permute-start | bytes 786440 | tf_op jit(solution)/shard_map/ppermute | solution.py:171
  17.0 3.1 %collective-permute-done.2.refs_2_ = bf16[128,1024]{1,0:T(8,128)(2,1)S(1)} collective-permute-done((bf16[128,1024]{1,0:T(8,128)(2,1)S(1)}, bf16[128,1024]{1,0:T(8,128)(2,1)S(1)}, u32[]{:S(2)}, u32[]{:S(2)}) %collective-permute-start.2) | collective-permute-done | bytes 262176 | tf_op jit(solution)/shard_map/ppermute | solution.py:169
  20.0 1.5 %collective-permute-start.5 = (bf16[128,1024]{1,0:T(8,128)(2,1)S(1)}, bf16[128,1024]{1,0:T(8,128)(2,1)S(1)}, u32[]{:S(2)}, u32[]{:S(2)}) collective-permute-start(bf16[128,1024]{1,0:T(8,128)(2,1)S(1)} %collective-permute-done.2.refs_2_), channel_id=1, source_target_pairs={{0,2},{2,0},{4,6},{6,4},{8,10},{10,8},{12,14},{14,12},{1,3},{3,1},... | collective-permute-start | bytes 786440 | tf_op jit(solution)/shard_map/ppermute | solution.py:171
  21.5 2.4 %collective-permute-start.9 = (bf16[128,1024]{1,0:T(8,128)(2,1)S(1)}, bf16[128,1024]{1,0:T(8,128)(2,1)S(1)}, u32[]{:S(2)}, u32[]{:S(2)}) collective-permute-start(bf16[128,1024]{1,0:T(8,128)(2,1)S(1)} %get-tuple-element.19.refs_1_), channel_id=1, source_target_pairs={{0,2},{4,6},{8,10},{12,14},{1,3},{5,7},{9,11},{13,15},{16,18},{20,... | collective-permute-start | bytes 786440 | tf_op jit(solution)/shard_map/ppermute | solution.py:170
  24.0 1.3 %collective-permute-start.10 = (bf16[128,1024]{1,0:T(8,128)(2,1)S(1)}, bf16[128,1024]{1,0:T(8,128)(2,1)S(1)}, u32[]{:S(2)}, u32[]{:S(2)}) collective-permute-start(bf16[128,1024]{1,0:T(8,128)(2,1)S(1)} %get-tuple-element.20.refs_2_), channel_id=1, source_target_pairs={{0,2},{4,6},{8,10},{12,14},{1,3},{5,7},{9,11},{13,15},{16,18},{20,... | collective-permute-start | bytes 786440 | tf_op jit(solution)/shard_map/ppermute | solution.py:170
  25.3 1.9 %collective-permute-start.8 = (bf16[128,1024]{1,0:T(8,128)(2,1)S(1)}, bf16[128,1024]{1,0:T(8,128)(2,1)S(1)}, u32[]{:S(2)}, u32[]{:S(2)}) collective-permute-start(bf16[128,1024]{1,0:T(8,128)(2,1)S(1)} %collective-permute-done.4.refs_1_), channel_id=1, source_target_pairs={{0,4},{4,8},{8,12},{12,0},{1,5},{5,9},{9,13},{13,1},{16,20},{20,24... | collective-permute-start | bytes 786440 | tf_op jit(solution)/shard_map/ppermute | solution.py:172
  27.2 1.1 %collective-permute-done.5.refs_2_ = bf16[128,1024]{1,0:T(8,128)(2,1)S(1)} collective-permute-done((bf16[128,1024]{1,0:T(8,128)(2,1)S(1)}, bf16[128,1024]{1,0:T(8,128)(2,1)S(1)}, u32[]{:S(2)}, u32[]{:S(2)}) %collective-permute-start.5) | collective-permute-done | bytes 262176 | tf_op jit(solution)/shard_map/ppermute | solution.py:171
  28.3 2.1 %collective-permute-start.7 = (bf16[128,1024]{1,0:T(8,128)(2,1)S(1)}, bf16[128,1024]{1,0:T(8,128)(2,1)S(1)}, u32[]{:S(2)}, u32[]{:S(2)}) collective-permute-start(bf16[128,1024]{1,0:T(8,128)(2,1)S(1)} %collective-permute-done.5.refs_2_), channel_id=1, source_target_pairs={{0,4},{4,8},{8,12},{12,0},{1,5},{5,9},{9,13},{13,1},{16,20},{20,24... | collective-permute-start | bytes 786440 | tf_op jit(solution)/shard_map/ppermute | solution.py:172
  30.4 1.9 %copy-done = bf16[768,2048]{1,0:T(8,128)(2,1)S(1)} copy-done((bf16[768,2048]{1,0:T(8,128)(2,1)S(1)}, bf16[768,2048]{1,0:T(8,128)(2,1)}, u32[]{:S(2)}) %copy-start) | copy-done | bytes 3145752
  32.3 1.0 %shard_map.56 = (f32[384,128]{1,0:T(8,128)S(1)}, f32[384,128]{1,0:T(8,128)S(1)}) custom-call(bf16[768,2048]{1,0:T(8,128)(2,1)S(1)} %copy-done, bf16[128,1024]{1,0:T(8,128)(2,1)S(1)} %get-tuple-element.19.refs_1_, bf16[128,1024]{1,0:T(8,128)(2,1)S(1)} %get-tuple-element.20.refs_2_), custom_call_target="tpu_custom_call" | custom-call | flops 402653184 | bytes 4063232 | tf_op jit(solution)/shard_map/pallas_call | solution.py:111
  33.4 0.8 %copy-done.1 = bf16[768,2048]{1,0:T(8,128)(2,1)S(1)} copy-done((bf16[768,2048]{1,0:T(8,128)(2,1)S(1)}, bf16[768,2048]{1,0:T(8,128)(2,1)}, u32[]{:S(2)}) %copy-start.1) | copy-done | bytes 3145752
  34.2 1.0 %shard_map.57 = (f32[384,128]{1,0:T(8,128)S(1)}, f32[384,128]{1,0:T(8,128)S(1)}) custom-call(bf16[768,2048]{1,0:T(8,128)(2,1)S(1)} %copy-done.1, bf16[128,1024]{1,0:T(8,128)(2,1)S(1)} %collective-permute-done.1.refs_1_, bf16[128,1024]{1,0:T(8,128)(2,1)S(1)} %collective-permute-done.2.refs_2_), custom_call_target="tpu_custom_call" | custom-call | flops 402653184 | bytes 4063232 | tf_op jit(solution)/shard_map/pallas_call | solution.py:111
  35.3 2.4 %collective-permute-done.10.refs_2_ = bf16[128,1024]{1,0:T(8,128)(2,1)S(1)} collective-permute-done((bf16[128,1024]{1,0:T(8,128)(2,1)S(1)}, bf16[128,1024]{1,0:T(8,128)(2,1)S(1)}, u32[]{:S(2)}, u32[]{:S(2)}) %collective-permute-start.10) | collective-permute-done | bytes 262176 | tf_op jit(solution)/shard_map/ppermute | solution.py:170
  37.7 1.0 %shard_map.59 = (f32[384,128]{1,0:T(8,128)S(1)}, f32[384,128]{1,0:T(8,128)S(1)}) custom-call(bf16[768,2048]{1,0:T(8,128)(2,1)S(1)} %copy-done.1, bf16[128,1024]{1,0:T(8,128)(2,1)S(1)} %collective-permute-done.9.refs_1_, bf16[128,1024]{1,0:T(8,128)(2,1)S(1)} %collective-permute-done.10.refs_2_), custom_call_target="tpu_custom_call" | custom-call | flops 402653184 | bytes 4063232 | tf_op jit(solution)/shard_map/pallas_call | solution.py:111
  38.7 1.0 %shard_map.58 = (f32[384,128]{1,0:T(8,128)S(1)}, f32[384,128]{1,0:T(8,128)S(1)}) custom-call(bf16[768,2048]{1,0:T(8,128)(2,1)S(1)} %copy-done.1, bf16[128,1024]{1,0:T(8,128)(2,1)S(1)} %collective-permute-done.4.refs_1_, bf16[128,1024]{1,0:T(8,128)(2,1)S(1)} %collective-permute-done.5.refs_2_), custom_call_target="tpu_custom_call" | custom-call | flops 402653184 | bytes 4063232 | tf_op jit(solution)/shard_map/pallas_call | solution.py:111
  40.5 1.0 %collective-permute-done.7.refs_1_ = bf16[128,1024]{1,0:T(8,128)(2,1)S(1)} collective-permute-done((bf16[128,1024]{1,0:T(8,128)(2,1)S(1)}, bf16[128,1024]{1,0:T(8,128)(2,1)S(1)}, u32[]{:S(2)}, u32[]{:S(2)}) %collective-permute-start.7) | collective-permute-done | bytes 262176 | tf_op jit(solution)/shard_map/ppermute | solution.py:172
  42.9 0.8 %collective-permute-done.11.refs_7_ = f32[384,128]{1,0:T(8,128)S(1)} collective-permute-done((f32[384,128]{1,0:T(8,128)S(1)}, f32[384,128]{1,0:T(8,128)S(1)}, u32[]{:S(2)}, u32[]{:S(2)}) %collective-permute-start.11) | collective-permute-done | bytes 196640 | tf_op jit(solution)/shard_map/ppermute | solution.py:181
  43.6 1.0 %shard_map.62 = f32[384,512]{1,0:T(8,128)} custom-call(s32[1]{0:T(128)S(6)} %copy.6.valid, f32[384,128]{1,0:T(8,128)S(1)} %get-tuple-element.21.refs_0_, f32[384,128]{1,0:T(8,128)S(1)} %collective-permute-done.refs_1_, f32[384,128]{1,0:T(8,128)S(1)} %get-tuple-element.23.refs_2_, f32[384,128]{1,0:T(8,128)S(1)} %collective-permute-done.3.refs_3_, ...), custom_call_target="tpu_custom_call" | custom-call | flops 196608 | bytes 2359296 | tf_op jit(solution)/shard_map/pallas_call | solution.py:145
  (18 shorter events, 2.1 us)
Async XLA Ops:
  0.0 1.0 %copy-start.2 = (bf16[128,2048]{1,0:T(8,128)(2,1)S(1)}, bf16[128,2048]{1,0:T(8,128)(2,1)}, u32[]{:S(2)}) copy-start(bf16[128,2048]{1,0:T(8,128)(2,1)} %queries.1) | copy-start | bytes 1572868
  1.0 0.7 %copy-start.3 = (f32[2048]{0:T(1024)S(1)}, f32[2048]{0:T(1024)}, u32[]{:S(2)}) copy-start(f32[2048]{0:T(1024)} %param.7) | copy-start | bytes 24580
  1.7 0.7 %copy-start.4 = (s32[1,128]{1,0:T(1,128)S(1)}, s32[1,128]{1,0:T(1,128)}, u32[]{:S(2)}) copy-start(s32[1,128]{1,0:T(1,128)} %rank.1) | copy-start | bytes 1540
  3.0 12.2 %collective-permute-start.1 = (bf16[128,1024]{1,0:T(8,128)(2,1)S(1)}, bf16[128,1024]{1,0:T(8,128)(2,1)S(1)}, u32[]{:S(2)}, u32[]{:S(2)}) collective-permute-start(bf16[128,1024]{1,0:T(8,128)(2,1)S(1)} %get-tuple-element.19.refs_1_), channel_id=1, source_target_pairs={{0,4},{2,6},{4,8},{6,10},{8,12},{10,14},{12,0},{14,2},{1,5},{3,7},... | collective-permute-start | bytes 786440 | tf_op jit(solution)/shard_map/ppermute | solution.py:169
  6.1 13.9 %collective-permute-start.2 = (bf16[128,1024]{1,0:T(8,128)(2,1)S(1)}, bf16[128,1024]{1,0:T(8,128)(2,1)S(1)}, u32[]{:S(2)}, u32[]{:S(2)}) collective-permute-start(bf16[128,1024]{1,0:T(8,128)(2,1)S(1)} %get-tuple-element.20.refs_2_), channel_id=1, source_target_pairs={{0,4},{2,6},{4,8},{6,10},{8,12},{10,14},{12,0},{14,2},{1,5},{3,7},... | collective-permute-start | bytes 786440 | tf_op jit(solution)/shard_map/ppermute | solution.py:169
  15.2 10.0 %collective-permute-start.4 = (bf16[128,1024]{1,0:T(8,128)(2,1)S(1)}, bf16[128,1024]{1,0:T(8,128)(2,1)S(1)}, u32[]{:S(2)}, u32[]{:S(2)}) collective-permute-start(bf16[128,1024]{1,0:T(8,128)(2,1)S(1)} %collective-permute-done.1.refs_1_), channel_id=1, source_target_pairs={{0,2},{2,0},{4,6},{6,4},{8,10},{10,8},{12,14},{14,12},{1,3},{3,1},... | collective-permute-start | bytes 786440 | tf_op jit(solution)/shard_map/ppermute | solution.py:171
  20.0 8.3 %collective-permute-start.5 = (bf16[128,1024]{1,0:T(8,128)(2,1)S(1)}, bf16[128,1024]{1,0:T(8,128)(2,1)S(1)}, u32[]{:S(2)}, u32[]{:S(2)}) collective-permute-start(bf16[128,1024]{1,0:T(8,128)(2,1)S(1)} %collective-permute-done.2.refs_2_), channel_id=1, source_target_pairs={{0,2},{2,0},{4,6},{6,4},{8,10},{10,8},{12,14},{14,12},{1,3},{3,1},... | collective-permute-start | bytes 786440 | tf_op jit(solution)/shard_map/ppermute | solution.py:171
  21.5 13.7 %collective-permute-start.9 = (bf16[128,1024]{1,0:T(8,128)(2,1)S(1)}, bf16[128,1024]{1,0:T(8,128)(2,1)S(1)}, u32[]{:S(2)}, u32[]{:S(2)}) collective-permute-start(bf16[128,1024]{1,0:T(8,128)(2,1)S(1)} %get-tuple-element.19.refs_1_), channel_id=1, source_target_pairs={{0,2},{4,6},{8,10},{12,14},{1,3},{5,7},{9,11},{13,15},{16,18},{20,... | collective-permute-start | bytes 786440 | tf_op jit(solution)/shard_map/ppermute | solution.py:170
  24.0 13.8 %collective-permute-start.10 = (bf16[128,1024]{1,0:T(8,128)(2,1)S(1)}, bf16[128,1024]{1,0:T(8,128)(2,1)S(1)}, u32[]{:S(2)}, u32[]{:S(2)}) collective-permute-start(bf16[128,1024]{1,0:T(8,128)(2,1)S(1)} %get-tuple-element.20.refs_2_), channel_id=1, source_target_pairs={{0,2},{4,6},{8,10},{12,14},{1,3},{5,7},{9,11},{13,15},{16,18},{20,... | collective-permute-start | bytes 786440 | tf_op jit(solution)/shard_map/ppermute | solution.py:170
  25.3 14.6 %collective-permute-start.8 = (bf16[128,1024]{1,0:T(8,128)(2,1)S(1)}, bf16[128,1024]{1,0:T(8,128)(2,1)S(1)}, u32[]{:S(2)}, u32[]{:S(2)}) collective-permute-start(bf16[128,1024]{1,0:T(8,128)(2,1)S(1)} %collective-permute-done.4.refs_1_), channel_id=1, source_target_pairs={{0,4},{4,8},{8,12},{12,0},{1,5},{5,9},{9,13},{13,1},{16,20},{20,24... | collective-permute-start | bytes 786440 | tf_op jit(solution)/shard_map/ppermute | solution.py:172
  28.3 13.2 %collective-permute-start.7 = (bf16[128,1024]{1,0:T(8,128)(2,1)S(1)}, bf16[128,1024]{1,0:T(8,128)(2,1)S(1)}, u32[]{:S(2)}, u32[]{:S(2)}) collective-permute-start(bf16[128,1024]{1,0:T(8,128)(2,1)S(1)} %collective-permute-done.5.refs_2_), channel_id=1, source_target_pairs={{0,4},{4,8},{8,12},{12,0},{1,5},{5,9},{9,13},{13,1},{16,20},{20,24... | collective-permute-start | bytes 786440 | tf_op jit(solution)/shard_map/ppermute | solution.py:172
  30.4 1.9 %copy-start = (bf16[768,2048]{1,0:T(8,128)(2,1)S(1)}, bf16[768,2048]{1,0:T(8,128)(2,1)}, u32[]{:S(2)}) copy-start(bf16[768,2048]{1,0:T(8,128)(2,1)} %refs_0_.11) | copy-start | bytes 9437188
  32.3 1.9 %copy-start.1 = (bf16[768,2048]{1,0:T(8,128)(2,1)S(1)}, bf16[768,2048]{1,0:T(8,128)(2,1)}, u32[]{:S(2)}) copy-start(bf16[768,2048]{1,0:T(8,128)(2,1)} %refs_0_.11) | copy-start | bytes 9437188
  33.4 9.5 %collective-permute-start = (f32[384,128]{1,0:T(8,128)S(1)}, f32[384,128]{1,0:T(8,128)S(1)}, u32[]{:S(2)}, u32[]{:S(2)}) collective-permute-start(f32[384,128]{1,0:T(8,128)S(1)} %get-tuple-element.22), channel_id=1, source_target_pairs={{0,1},{1,0},{2,3},{3,2},{4,5},{5,4},{6,7},{7,6},{8,9},{9,8},{10,11... | collective-permute-start | bytes 589832 | tf_op jit(solution)/shard_map/ppermute | solution.py:177
  35.3 7.6 %collective-permute-start.3 = (f32[384,128]{1,0:T(8,128)S(1)}, f32[384,128]{1,0:T(8,128)S(1)}, u32[]{:S(2)}, u32[]{:S(2)}) collective-permute-start(f32[384,128]{1,0:T(8,128)S(1)} %get-tuple-element.24), channel_id=1, source_target_pairs={{0,1},{1,0},{2,3},{3,2},{4,5},{5,4},{6,7},{7,6},{8,9},{9,8},{10,11... | collective-permute-start | bytes 589832 | tf_op jit(solution)/shard_map/ppermute | solution.py:177
  39.8 3.1 %collective-permute-start.6 = (f32[384,128]{1,0:T(8,128)S(1)}, f32[384,128]{1,0:T(8,128)S(1)}, u32[]{:S(2)}, u32[]{:S(2)}) collective-permute-start(f32[384,128]{1,0:T(8,128)S(1)} %get-tuple-element.26), channel_id=1, source_target_pairs={{0,1},{1,0},{2,3},{3,2},{4,5},{5,4},{6,7},{7,6},{8,9},{9,8},{10,11... | collective-permute-start | bytes 589832 | tf_op jit(solution)/shard_map/ppermute | solution.py:177
  42.1 1.5 %collective-permute-start.11 = (f32[384,128]{1,0:T(8,128)S(1)}, f32[384,128]{1,0:T(8,128)S(1)}, u32[]{:S(2)}, u32[]{:S(2)}) collective-permute-start(f32[384,128]{1,0:T(8,128)S(1)} %get-tuple-element.32), channel_id=1, source_target_pairs={{0,1},{1,0},{2,3},{3,2},{4,5},{5,4},{6,7},{7,6},{8,9},{9,8},{10,11... | collective-permute-start | bytes 589832 | tf_op jit(solution)/shard_map/ppermute | solution.py:181

commit v3 on v1

--- a/solution.py
+++ b/solution.py
@@ -20,25 +20,47 @@
     return pl.BlockSpec(memory_space=pltpu.VMEM)
 
 
-def prepare_kernel(queries, precond, rank, *chunks):
-    rows = queries.shape[0]
+def in_hbm(x):
+    return pltpu.with_memory_space_constraint(x, pltpu.HBM)
+
+
+def prepare_kernel(queries, precond, rank, *refs):
+    chunks, (held, scale, places, arrived) = refs[:CHUNKS], refs[CHUNKS:]
+    rows, width = chunks[0].shape
+    cuts = [slice(n * width, (n + 1) * width) for n in range(CHUNKS)]
+    loads = [pltpu.make_async_copy(rank, places, arrived.at[CHUNKS])]
+    loads.append(pltpu.make_async_copy(precond, scale, arrived.at[CHUNKS + 1]))
+    for n, cut in enumerate(cuts):
+        loads.append(pltpu.make_async_copy(queries.at[:, cut], held.at[:, cut], arrived.at[n]))
+    for load in loads:
+        load.start()
+    loads[0].wait()
+    loads[1].wait()
     positions = lax.broadcasted_iota(jnp.int32, (rows, rows), 0)
-    placing = (positions == rank[...]).astype(jnp.bfloat16)
-    width = chunks[0].shape[1]
-    for n, chunk in enumerate(chunks):
-        cut = slice(n * width, (n + 1) * width)
-        pre = (queries[:, cut].astype(jnp.float32) * precond[:, cut]).astype(jnp.bfloat16)
-        chunk[...] = jnp.dot(placing, pre, preferred_element_type=jnp.float32).astype(jnp.bfloat16)
+    placing = (positions == places[...]).astype(jnp.bfloat16)
+    for n, cut in enumerate(cuts):
+        loads[2 + n].wait()
+        pre = (held[:, cut].astype(jnp.float32) * scale[:, cut]).astype(jnp.bfloat16)
+        chunks[n][...] = jnp.dot(placing, pre, preferred_element_type=jnp.float32).astype(
+            jnp.bfloat16
+        )
 
 
 def prepare(queries, precond, rank):
     rows, depth = queries.shape
     shape = jax.ShapeDtypeStruct((rows, depth // CHUNKS), jnp.bfloat16)
+    queries, precond, rank = [in_hbm(x) for x in (queries, precond, rank)]
     return pl.pallas_call(
         prepare_kernel,
         out_shape=[shape] * CHUNKS,
-        in_specs=[whole_spec()] * 3,
+        in_specs=[pl.BlockSpec(memory_space=pltpu.HBM)] * 3,
         out_specs=[whole_spec()] * CHUNKS,
+        scratch_shapes=[
+            pltpu.VMEM((rows, depth), jnp.bfloat16),
+            pltpu.VMEM((1, depth), jnp.float32),
+            pltpu.VMEM((1, rows), jnp.int32),
+            pltpu.SemaphoreType.DMA((CHUNKS + 2,)),
+        ],
         compiler_params=params(),
         cost_estimate=pl.CostEstimate(
             flops=2 * rows * rows * depth, bytes_accessed=4 * rows * depth, transcendentals=0
@@ -90,24 +112,21 @@
     )(*operands)
 
 
-def finish_kernel(places, valid, *refs):
+def finish_kernel(valid, *refs):
     out = refs[-1]
     half, columns = refs[0].shape
-    me = lax.axis_index("dim")
-    odd = lax.rem(lax.axis_index("ex"), 2)
-    row_ids = lax.broadcasted_iota(jnp.int32, (half, columns), 0) + me * half
+    row_ids = lax.broadcasted_iota(jnp.int32, (half, columns), 0) + lax.axis_index("dim") * half
     keep = row_ids < valid[0]
-    for n, place in enumerate(places):
-        step = place[0] + odd * (place[1] - place[0])
+    for n in range(len(refs) // 2):
         total = refs[2 * n][...] + refs[2 * n + 1][...]
-        out[:, pl.ds(pl.multiple_of(step * columns, columns), columns)] = jnp.where(keep, total, 0.0)
+        out[:, n * columns:(n + 1) * columns] = jnp.where(keep, total, 0.0)
 
 
-def finish(valid, pairs, places):
+def finish(valid, pairs):
     half, columns = pairs[0][0].shape
     operands = [ref for pair in pairs for ref in pair]
     return pl.pallas_call(
-        functools.partial(finish_kernel, places),
+        finish_kernel,
         out_shape=jax.ShapeDtypeStruct((half, columns * len(pairs)), jnp.float32),
         in_specs=[pl.BlockSpec(memory_space=pltpu.SMEM)] + [whole_spec()] * len(operands),
         out_specs=whole_spec(),
@@ -120,30 +139,37 @@
     )(valid, *operands)
 
 
+def after(x, *earlier):
+    return lax.optimization_barrier((x, *earlier))[0]
+
+
 def shards(store, queries, precond, query_rank, valid_rows):
     size = lax.axis_size("ex")
+    odd = lax.rem(lax.axis_index("ex"), 2) == 1
     ahead = [(i, (i + 2) % size) for i in range(size)]
     swap = [(i, i ^ 1) for i in range(size)]
-    to_odd = [(i, i + 1) for i in range(0, size, 2)]
-    even_ahead = [(i, (i + 2) % size) for i in range(0, size, 2)]
     over_dim = [(0, 1), (1, 0)]
 
     own = prepare(queries, precond[None, :], query_rank)
-    chunks = range(CHUNKS)
-    two_back = [lax.ppermute(own[n], "ex", ahead) for n in chunks]
-    odd_one_back = [lax.ppermute(own[n], "ex", to_odd) for n in chunks]
-    swapped = [lax.ppermute(two_back[n], "ex", swap) for n in chunks]
-    even_three_back = [lax.ppermute(swapped[n], "ex", even_ahead) for n in chunks]
+    two_back, one_back, three_back = [], [], []
+    for n in range(CHUNKS):
+        block = after(own[n], *two_back)
+        two_back.append(lax.ppermute(block, "ex", ahead))
+    for n in range(CHUNKS):
+        one_back.append(lax.ppermute(jnp.where(odd, two_back[n], own[n]), "ex", swap))
+    for n in range(CHUNKS):
+        block = after(one_back[n], *two_back, *three_back)
+        three_back.append(lax.ppermute(block, "ex", ahead))
 
     pairs = []
-    for blocks in (own, two_back, swapped):
+    for blocks in (own, one_back, two_back):
         send, kept = partial_scores(store, list(enumerate(blocks)))
         pairs.append((kept, lax.ppermute(send, "dim", over_dim)))
-    carry = partial_scores(store, list(enumerate(odd_one_back)))
-    for n in chunks:
-        carry = partial_scores(store, [(n, even_three_back[n])], (carry[0], carry[1]))
+    carry = ()
+    for n in range(CHUNKS):
+        carry = partial_scores(store, [(n, three_back[n])], carry)
     pairs.append((carry[1], lax.ppermute(carry[0], "dim", over_dim)))
-    return finish(valid_rows, pairs, ((0, 0), (2, 2), (1, 3), (3, 1)))
+    return finish(valid_rows, pairs)
 
 
 def solution(mesh):

time: 44.7 us -> 42.9 us (0.960)
  waiting for transfers between devices: 16.1 us -> 26.4 us
  starting transfers between devices: 16 us -> 6.26 us
  local copies, waits for them, and re-layouts: 5.12 us -> 2.73 us
    ppermute x8 -> x6, waiting for transfers between devices: 15.3 us -> 25.6 us  [the longest x2 11.1 us: shards(): two_back.append(lax.ppermute(block, 'ex', ahead))]
    ppermute x8 -> x6, starting transfers between devices: 15.7 us -> 5.48 us  [the longest x2 3.08 us: shards(): two_back.append(lax.ppermute(block, 'ex', ahead))]
    unnamed x10 -> x4, local copies, waits for them, and re-layouts: 5.12 us -> 2.73 us
    pallas_call x2, Pallas kernels: 1.3 us -> 2.48 us  [the longest x1 1.47 us: prepare(): pl.pallas_call(prepare_kernel, out_shape=[shape] * CHUNKS, in_specs=[pl.B...]
    pallas_call x6 -> x5, Pallas kernels: 4.99 us -> 4.01 us  [partial_scores(): pl.pallas_call(functools.partial(scores_kernel, cuts, bool(carry)), out_s...]
    ppermute x3, starting transfers between devices: 0.21 us -> 0.7 us  [shards(): pairs.append((kept, lax.ppermute(send, 'dim', over_dim)))]
  transfers between devices with their start and end apart: 12 -> 10, of which waited for: 6 -> 6; matrix products, arithmetic and copies ran while one was open for 0% -> 0% of each run, Pallas kernels for 11% -> 9%
where the time goes in v3:
time: 42.9 us; the launch traced here: 42.7 us
  waiting for transfers between devices  26.4 us (62%)
  Pallas kernels  6.48 us (15%)
  starting transfers between devices  6.26 us (15%)
  local copies, waits for them, and re-layouts  2.73 us (6%)
  between operations  0.76 us (2%)
    ppermute x2, waiting for transfers between devices, shards(): two_back.append(lax.ppermute(block, 'ex', ahead))  11.1 us
    ppermute x2, waiting for transfers between devices, shards(): three_back.append(lax.ppermute(block, 'ex', ahead))  8.55 us
    ppermute x2, waiting for transfers between devices, shards(): lax.ppermute(jnp.where(odd, two_back[n], own[n]), 'ex', swap)  5.99 us
    pallas_call x5, Pallas kernels, partial_scores(): pl.pallas_call(functools.partial(scores_kernel, cuts, bool(carry)), out_s...  4.01 us
    ppermute x2, starting transfers between devices, shards(): two_back.append(lax.ppermute(block, 'ex', ahead))  3.08 us
    unnamed x4, local copies, waits for them, and re-layouts  2.73 us
    ppermute x2, starting transfers between devices, shards(): lax.ppermute(jnp.where(odd, two_back[n], own[n]), 'ex', swap)  2.4 us
    pallas_call x1, Pallas kernels, prepare(): pl.pallas_call(prepare_kernel, out_shape=[shape] * CHUNKS, in_specs=[pl.B...  1.47 us
  transfers between devices with their start and end apart: 10, of which 6 were waited for; matrix products, arithmetic and copies ran while one was open for 0% of the time, Pallas kernels for 9%

profile of v3, /device:TPU:0, one launch (start us, length us, event | category | flops | bytes accessed | tf_op | source)
XLA Modules:
  0.0 42.7 jit_solution(8866082426666879999)
XLA Ops:
  0.0 1.5 %shard_map.55 = (bf16[128,1024]{1,0:T(8,128)(2,1)S(1)}, bf16[128,1024]{1,0:T(8,128)(2,1)S(1)}) custom-call(bf16[128,2048]{1,0:T(8,128)(2,1)} %queries.1, f32[1,2048]{1,0:T(1,128)} %bitcast.1, s32[1,128]{1,0:T(1,128)} %rank.1), custom_call_target="tpu_custom_call" | custom-call | flops 67108864 | bytes 1048576 | tf_op jit(solution)/shard_map/pallas_call | solution.py:53
  1.5 3.1 %collective-permute-start.1 = (bf16[128,1024]{1,0:T(8,128)(2,1)S(1)}, bf16[128,1024]{1,0:T(8,128)(2,1)S(1)}, u32[]{:S(2)}, u32[]{:S(2)}) collective-permute-start(bf16[128,1024]{1,0:T(8,128)(2,1)S(1)} %get-tuple-element.20.refs_1_), channel_id=1, source_target_pairs={{0,4},{2,6},{4,8},{6,10},{8,12},{10,14},{12,0},{14,2},{1,5},{3,7},... | collective-permute-start | bytes 786440 | tf_op jit(solution)/shard_map/ppermute | solution.py:157
  4.6 8.3 %collective-permute-done.1.refs_1_ = bf16[128,1024]{1,0:T(8,128)(2,1)S(1)} collective-permute-done((bf16[128,1024]{1,0:T(8,128)(2,1)S(1)}, bf16[128,1024]{1,0:T(8,128)(2,1)S(1)}, u32[]{:S(2)}, u32[]{:S(2)}) %collective-permute-start.1) | collective-permute-done | bytes 262176 | tf_op jit(solution)/shard_map/ppermute | solution.py:157
  12.9 1.6 %collective-permute-start.2 = (bf16[128,1024]{1,0:T(8,128)(2,1)S(1)}, bf16[128,1024]{1,0:T(8,128)(2,1)S(1)}, u32[]{:S(2)}, u32[]{:S(2)}) collective-permute-start(bf16[128,1024]{1,0:T(8,128)(2,1)S(1)} %broadcast_select_fusion.1), channel_id=1, source_target_pairs={{0,2},{2,0},{4,6},{6,4},{8,10},{10,8},{12,14},{14,12},{1,3},{3,1},... | collective-permute-start | bytes 786440 | tf_op jit(solution)/shard_map/ppermute | solution.py:159
  14.5 0.0 collective-permute-start.3
  14.5 6.0 %collective-permute-done.2.refs_1_ = bf16[128,1024]{1,0:T(8,128)(2,1)S(1)} collective-permute-done((bf16[128,1024]{1,0:T(8,128)(2,1)S(1)}, bf16[128,1024]{1,0:T(8,128)(2,1)S(1)}, u32[]{:S(2)}, u32[]{:S(2)}) %collective-permute-start.2) | collective-permute-done | bytes 262176 | tf_op jit(solution)/shard_map/ppermute | solution.py:159
  20.5 2.8 %collective-permute-done.3.refs_2_ = bf16[128,1024]{1,0:T(8,128)(2,1)S(1)} collective-permute-done((bf16[128,1024]{1,0:T(8,128)(2,1)S(1)}, bf16[128,1024]{1,0:T(8,128)(2,1)S(1)}, u32[]{:S(2)}, u32[]{:S(2)}) %collective-permute-start.3) | collective-permute-done | bytes 262176 | tf_op jit(solution)/shard_map/ppermute | solution.py:157
  23.2 0.0 collective-permute-start.7
  23.3 0.8 %collective-permute-start.4 = (bf16[128,1024]{1,0:T(8,128)(2,1)S(1)}, bf16[128,1024]{1,0:T(8,128)(2,1)S(1)}, u32[]{:S(2)}, u32[]{:S(2)}) collective-permute-start(bf16[128,1024]{1,0:T(8,128)(2,1)S(1)} %broadcast_select_fusion), channel_id=1, source_target_pairs={{0,2},{2,0},{4,6},{6,4},{8,10},{10,8},{12,14},{14,12},{1,3},{3,1},... | collective-permute-start | bytes 786440 | tf_op jit(solution)/shard_map/ppermute | solution.py:159
  24.1 7.3 %collective-permute-done.7.refs_1_ = bf16[128,1024]{1,0:T(8,128)(2,1)S(1)} collective-permute-done((bf16[128,1024]{1,0:T(8,128)(2,1)S(1)}, bf16[128,1024]{1,0:T(8,128)(2,1)S(1)}, u32[]{:S(2)}, u32[]{:S(2)}) %collective-permute-start.7) | collective-permute-done | bytes 262176 | tf_op jit(solution)/shard_map/ppermute | solution.py:162
  31.4 1.9 %copy-done = bf16[768,2048]{1,0:T(8,128)(2,1)S(1)} copy-done((bf16[768,2048]{1,0:T(8,128)(2,1)S(1)}, bf16[768,2048]{1,0:T(8,128)(2,1)}, u32[]{:S(2)}) %copy-start) | copy-done | bytes 3145752
  33.3 1.0 %shard_map.56 = (f32[384,128]{1,0:T(8,128)S(1)}, f32[384,128]{1,0:T(8,128)S(1)}) custom-call(bf16[768,2048]{1,0:T(8,128)(2,1)S(1)} %copy-done, bf16[128,1024]{1,0:T(8,128)(2,1)S(1)} %get-tuple-element.20.refs_1_, bf16[128,1024]{1,0:T(8,128)(2,1)S(1)} %get-tuple-element.24.refs_2_), custom_call_target="tpu_custom_call" | custom-call | flops 402653184 | bytes 4063232 | tf_op jit(solution)/shard_map/pallas_call | solution.py:101
  34.3 0.1 collective-permute-start
  34.4 0.8 %copy-done.1 = bf16[768,2048]{1,0:T(8,128)(2,1)S(1)} copy-done((bf16[768,2048]{1,0:T(8,128)(2,1)S(1)}, bf16[768,2048]{1,0:T(8,128)(2,1)}, u32[]{:S(2)}) %copy-start.1) | copy-done | bytes 3145752
  35.2 1.0 %shard_map.58 = (f32[384,128]{1,0:T(8,128)S(1)}, f32[384,128]{1,0:T(8,128)S(1)}) custom-call(bf16[768,2048]{1,0:T(8,128)(2,1)S(1)} %copy-done.1, bf16[128,1024]{1,0:T(8,128)(2,1)S(1)} %collective-permute-done.1.refs_1_, bf16[128,1024]{1,0:T(8,128)(2,1)S(1)} %collective-permute-done.3.refs_2_), custom_call_target="tpu_custom_call" | custom-call | flops 402653184 | bytes 4063232 | tf_op jit(solution)/shard_map/pallas_call | solution.py:101
  36.2 0.1 collective-permute-start.6
  36.3 1.0 %shard_map.57 = (f32[384,128]{1,0:T(8,128)S(1)}, f32[384,128]{1,0:T(8,128)S(1)}) custom-call(bf16[768,2048]{1,0:T(8,128)(2,1)S(1)} %copy-done.1, bf16[128,1024]{1,0:T(8,128)(2,1)S(1)} %collective-permute-done.2.refs_1_, bf16[128,1024]{1,0:T(8,128)(2,1)S(1)} %collective-permute-done.4.refs_2_), custom_call_target="tpu_custom_call" | custom-call | flops 402653184 | bytes 4063232 | tf_op jit(solution)/shard_map/pallas_call | solution.py:101
  37.2 0.6 %collective-permute-start.5 = (f32[384,128]{1,0:T(8,128)S(1)}, f32[384,128]{1,0:T(8,128)S(1)}, u32[]{:S(2)}, u32[]{:S(2)}) collective-permute-start(f32[384,128]{1,0:T(8,128)S(1)} %get-tuple-element.26), channel_id=1, source_target_pairs={{0,1},{1,0},{2,3},{3,2},{4,5},{5,4},{6,7},{7,6},{8,9},{9,8},{10,11... | collective-permute-start | bytes 589832 | tf_op jit(solution)/shard_map/ppermute | solution.py:167
  37.8 0.6 %shard_map.59 = (f32[384,128]{1,0:T(8,128)S(1)}, f32[384,128]{1,0:T(8,128)S(1)}) custom-call(bf16[768,2048]{1,0:T(8,128)(2,1)S(1)} %copy-done.1, bf16[128,1024]{1,0:T(8,128)(2,1)S(1)} %collective-permute-done.7.refs_1_), custom_call_target="tpu_custom_call" | custom-call | flops 201326592 | bytes 2228224 | tf_op jit(solution)/shard_map/pallas_call | solution.py:101
  38.3 1.3 %collective-permute-done.8.refs_1_ = bf16[128,1024]{1,0:T(8,128)(2,1)S(1)} collective-permute-done((bf16[128,1024]{1,0:T(8,128)(2,1)S(1)}, bf16[128,1024]{1,0:T(8,128)(2,1)S(1)}, u32[]{:S(2)}, u32[]{:S(2)}) %collective-permute-start.8) | collective-permute-done | bytes 262176 | tf_op jit(solution)/shard_map/ppermute | solution.py:162
  39.6 0.6 %shard_map.60 = (f32[384,128]{1,0:T(8,128)S(1)}, f32[384,128]{1,0:T(8,128)S(1)}) custom-call(bf16[768,2048]{1,0:T(8,128)(2,1)S(1)} %copy-done.1, bf16[128,1024]{1,0:T(8,128)(2,1)S(1)} %collective-permute-done.8.refs_1_, f32[384,128]{1,0:T(8,128)S(1)} %get-tuple-element.31.refs_2_, f32[384,128]{1,0:T(8,128)S(1)} %get-tuple-element.32.refs_3_), custom_call_target="tpu_custom_call" | custom-call | flops 201326592 | bytes 2228224 | tf_op jit(solution)/shard_map/pallas_call | solution.py:101
  40.2 0.1 collective-permute-start.9
  40.9 0.8 %collective-permute-done.9.refs_7_ = f32[384,128]{1,0:T(8,128)S(1)} collective-permute-done((f32[384,128]{1,0:T(8,128)S(1)}, f32[384,128]{1,0:T(8,128)S(1)}, u32[]{:S(2)}, u32[]{:S(2)}) %collective-permute-start.9) | collective-permute-done | bytes 196640 | tf_op jit(solution)/shard_map/ppermute | solution.py:171
  41.7 1.0 %shard_map.61 = f32[384,512]{1,0:T(8,128)} custom-call(s32[1]{0:T(128)S(6)} %copy.6.valid, f32[384,128]{1,0:T(8,128)S(1)} %get-tuple-element.22.refs_0_, f32[384,128]{1,0:T(8,128)S(1)} %collective-permute-done.refs_1_, f32[384,128]{1,0:T(8,128)S(1)} %get-tuple-element.25.refs_2_, f32[384,128]{1,0:T(8,128)S(1)} %collective-permute-done.5.refs_3_, ...), custom_call_target="tpu_custom_call" | custom-call | flops 196608 | bytes 2359296 | tf_op jit(solution)/shard_map/pallas_call | solution.py:128
  (9 shorter events, 0.1 us)
Async XLA Ops:
  1.5 11.4 %collective-permute-start.1 = (bf16[128,1024]{1,0:T(8,128)(2,1)S(1)}, bf16[128,1024]{1,0:T(8,128)(2,1)S(1)}, u32[]{:S(2)}, u32[]{:S(2)}) collective-permute-start(bf16[128,1024]{1,0:T(8,128)(2,1)S(1)} %get-tuple-element.20.refs_1_), channel_id=1, source_target_pairs={{0,4},{2,6},{4,8},{6,10},{8,12},{10,14},{12,0},{14,2},{1,5},{3,7},... | collective-permute-start | bytes 786440 | tf_op jit(solution)/shard_map/ppermute | solution.py:157
  12.9 7.6 %collective-permute-start.2 = (bf16[128,1024]{1,0:T(8,128)(2,1)S(1)}, bf16[128,1024]{1,0:T(8,128)(2,1)S(1)}, u32[]{:S(2)}, u32[]{:S(2)}) collective-permute-start(bf16[128,1024]{1,0:T(8,128)(2,1)S(1)} %broadcast_select_fusion.1), channel_id=1, source_target_pairs={{0,2},{2,0},{4,6},{6,4},{8,10},{10,8},{12,14},{14,12},{1,3},{3,1},... | collective-permute-start | bytes 786440 | tf_op jit(solution)/shard_map/ppermute | solution.py:159
  14.5 8.8 %collective-permute-start.3 = (bf16[128,1024]{1,0:T(8,128)(2,1)S(1)}, bf16[128,1024]{1,0:T(8,128)(2,1)S(1)}, u32[]{:S(2)}, u32[]{:S(2)}) collective-permute-start(bf16[128,1024]{1,0:T(8,128)(2,1)S(1)} %get-tuple-element.24.refs_2_), channel_id=1, source_target_pairs={{0,4},{2,6},{4,8},{6,10},{8,12},{10,14},{12,0},{14,2},{1,5},{3,7},... | collective-permute-start | bytes 786440 | tf_op jit(solution)/shard_map/ppermute | solution.py:157
  23.2 8.2 %collective-permute-start.7 = (bf16[128,1024]{1,0:T(8,128)(2,1)S(1)}, bf16[128,1024]{1,0:T(8,128)(2,1)S(1)}, u32[]{:S(2)}, u32[]{:S(2)}) collective-permute-start(bf16[128,1024]{1,0:T(8,128)(2,1)S(1)} %collective-permute-done.2.refs_1_), channel_id=1, source_target_pairs={{0,4},{2,6},{4,8},{6,10},{8,12},{10,14},{12,0},{14,2},{1,5},{3,7},... | collective-permute-start | bytes 786440 | tf_op jit(solution)/shard_map/ppermute | solution.py:162
  23.3 8.1 %collective-permute-start.4 = (bf16[128,1024]{1,0:T(8,128)(2,1)S(1)}, bf16[128,1024]{1,0:T(8,128)(2,1)S(1)}, u32[]{:S(2)}, u32[]{:S(2)}) collective-permute-start(bf16[128,1024]{1,0:T(8,128)(2,1)S(1)} %broadcast_select_fusion), channel_id=1, source_target_pairs={{0,2},{2,0},{4,6},{6,4},{8,10},{10,8},{12,14},{14,12},{1,3},{3,1},... | collective-permute-start | bytes 786440 | tf_op jit(solution)/shard_map/ppermute | solution.py:159
  31.4 8.2 %collective-permute-start.8 = (bf16[128,1024]{1,0:T(8,128)(2,1)S(1)}, bf16[128,1024]{1,0:T(8,128)(2,1)S(1)}, u32[]{:S(2)}, u32[]{:S(2)}) collective-permute-start(bf16[128,1024]{1,0:T(8,128)(2,1)S(1)} %collective-permute-done.4.refs_2_), channel_id=1, source_target_pairs={{0,4},{2,6},{4,8},{6,10},{8,12},{10,14},{12,0},{14,2},{1,5},{3,7},... | collective-permute-start | bytes 786440 | tf_op jit(solution)/shard_map/ppermute | solution.py:162
  31.4 1.9 %copy-start = (bf16[768,2048]{1,0:T(8,128)(2,1)S(1)}, bf16[768,2048]{1,0:T(8,128)(2,1)}, u32[]{:S(2)}) copy-start(bf16[768,2048]{1,0:T(8,128)(2,1)} %refs_0_.9) | copy-start | bytes 9437188
  33.3 1.9 %copy-start.1 = (bf16[768,2048]{1,0:T(8,128)(2,1)S(1)}, bf16[768,2048]{1,0:T(8,128)(2,1)}, u32[]{:S(2)}) copy-start(bf16[768,2048]{1,0:T(8,128)(2,1)} %refs_0_.9) | copy-start | bytes 9437188
  34.3 6.6 %collective-permute-start = (f32[384,128]{1,0:T(8,128)S(1)}, f32[384,128]{1,0:T(8,128)S(1)}, u32[]{:S(2)}, u32[]{:S(2)}) collective-permute-start(f32[384,128]{1,0:T(8,128)S(1)} %get-tuple-element.23), channel_id=1, source_target_pairs={{0,1},{1,0},{2,3},{3,2},{4,5},{5,4},{6,7},{7,6},{8,9},{9,8},{10,11... | collective-permute-start | bytes 589832 | tf_op jit(solution)/shard_map/ppermute | solution.py:167
  36.2 4.7 %collective-permute-start.6 = (f32[384,128]{1,0:T(8,128)S(1)}, f32[384,128]{1,0:T(8,128)S(1)}, u32[]{:S(2)}, u32[]{:S(2)}) collective-permute-start(f32[384,128]{1,0:T(8,128)S(1)} %get-tuple-element.28), channel_id=1, source_target_pairs={{0,1},{1,0},{2,3},{3,2},{4,5},{5,4},{6,7},{7,6},{8,9},{9,8},{10,11... | collective-permute-start | bytes 589832 | tf_op jit(solution)/shard_map/ppermute | solution.py:167
  37.2 3.7 %collective-permute-start.5 = (f32[384,128]{1,0:T(8,128)S(1)}, f32[384,128]{1,0:T(8,128)S(1)}, u32[]{:S(2)}, u32[]{:S(2)}) collective-permute-start(f32[384,128]{1,0:T(8,128)S(1)} %get-tuple-element.26), channel_id=1, source_target_pairs={{0,1},{1,0},{2,3},{3,2},{4,5},{5,4},{6,7},{7,6},{8,9},{9,8},{10,11... | collective-permute-start | bytes 589832 | tf_op jit(solution)/shard_map/ppermute | solution.py:167
  40.2 1.5 %collective-permute-start.9 = (f32[384,128]{1,0:T(8,128)S(1)}, f32[384,128]{1,0:T(8,128)S(1)}, u32[]{:S(2)}, u32[]{:S(2)}) collective-permute-start(f32[384,128]{1,0:T(8,128)S(1)} %get-tuple-element.34), channel_id=1, source_target_pairs={{0,1},{1,0},{2,3},{3,2},{4,5},{5,4},{6,7},{7,6},{8,9},{9,8},{10,11... | collective-permute-start | bytes 589832 | tf_op jit(solution)/shard_map/ppermute | solution.py:171

commit v4 on v3

--- a/solution.py
+++ b/solution.py
@@ -8,7 +8,8 @@
 from jax.sharding import PartitionSpec as P
 
 STEPS = 4
-CHUNKS = 2
+PARTS = (4, 4, 4, 4)
+CHUNKS = len(PARTS)
 VMEM_BYTES = 16 * 1024 * 1024
 
 
@@ -24,10 +25,15 @@
     return pltpu.with_memory_space_constraint(x, pltpu.HBM)
 
 
+def cuts_of(depth):
+    ends = [depth * sum(PARTS[:n + 1]) // sum(PARTS) for n in range(CHUNKS)]
+    return [slice(start, end) for start, end in zip([0] + ends, ends)]
+
+
 def prepare_kernel(queries, precond, rank, *refs):
     chunks, (held, scale, places, arrived) = refs[:CHUNKS], refs[CHUNKS:]
-    rows, width = chunks[0].shape
-    cuts = [slice(n * width, (n + 1) * width) for n in range(CHUNKS)]
+    rows, depth = queries.shape
+    cuts = cuts_of(depth)
     loads = [pltpu.make_async_copy(rank, places, arrived.at[CHUNKS])]
     loads.append(pltpu.make_async_copy(precond, scale, arrived.at[CHUNKS + 1]))
     for n, cut in enumerate(cuts):
@@ -48,11 +54,13 @@
 
 def prepare(queries, precond, rank):
     rows, depth = queries.shape
-    shape = jax.ShapeDtypeStruct((rows, depth // CHUNKS), jnp.bfloat16)
+    shapes = [
+        jax.ShapeDtypeStruct((rows, cut.stop - cut.start), jnp.bfloat16) for cut in cuts_of(depth)
+    ]
     queries, precond, rank = [in_hbm(x) for x in (queries, precond, rank)]
     return pl.pallas_call(
         prepare_kernel,
-        out_shape=[shape] * CHUNKS,
+        out_shape=shapes,
         in_specs=[pl.BlockSpec(memory_space=pltpu.HBM)] * 3,
         out_specs=[whole_spec()] * CHUNKS,
         scratch_shapes=[
@@ -80,9 +88,8 @@
         if carried:
             total = (carry[0] if out is send else carry[1])[...]
         for n, block in zip(cuts, blocks):
-            width = block.shape[1]
             part = lax.dot_general(
-                store[rows, n * width:(n + 1) * width],
+                store[rows, cuts_of(store.shape[1])[n]],
                 block[...],
                 (((1,), (1,)), ((), ())),
                 preferred_element_type=jnp.float32,
@@ -153,13 +160,14 @@
     own = prepare(queries, precond[None, :], query_rank)
     two_back, one_back, three_back = [], [], []
     for n in range(CHUNKS):
-        block = after(own[n], *two_back)
-        two_back.append(lax.ppermute(block, "ex", ahead))
+        two_back.append(lax.ppermute(own[n], "ex", ahead))
     for n in range(CHUNKS):
-        one_back.append(lax.ppermute(jnp.where(odd, two_back[n], own[n]), "ex", swap))
+        block = two_back[n]
+        if n == CHUNKS - 1:
+            block = after(block, one_back[0])
+        one_back.append(lax.ppermute(jnp.where(odd, block, own[n]), "ex", swap))
     for n in range(CHUNKS):
-        block = after(one_back[n], *two_back, *three_back)
-        three_back.append(lax.ppermute(block, "ex", ahead))
+        three_back.append(lax.ppermute(one_back[n], "ex", ahead))
 
     pairs = []
     for blocks in (own, one_back, two_back):

time: 42.9 us -> 37.8 us (0.88)
  waiting for transfers between devices: 26.4 us -> 10.7 us
  starting transfers between devices: 6.26 us -> 16.3 us
  Pallas kernels: 6.48 us -> 7.07 us
    ppermute x6 -> x12, waiting for transfers between devices: 25.6 us -> 9.93 us  [the longest x4 5.27 us: shards(): two_back.append(lax.ppermute(own[n], 'ex', ahead))]
    ppermute x6 -> x12, starting transfers between devices: 5.48 us -> 15.5 us  [the longest x4 6.96 us: shards(): one_back.append(lax.ppermute(jnp.where(odd, block, own[n]), 'ex', swap))]
    pallas_call x5 -> x7, Pallas kernels: 4.01 us -> 4.34 us  [partial_scores(): pl.pallas_call(functools.partial(scores_kernel, cuts, bool(carry)), out_s...]
  transfers between devices with their start and end apart: 10 -> 16, of which waited for: 6 -> 9; matrix products, arithmetic and copies ran while one was open for 0% -> 0% of each run, Pallas kernels for 9% -> 12%
where the time goes in v4:
time: 37.8 us; the launch traced here: 37.6 us
  starting transfers between devices  16.3 us (43%)
  waiting for transfers between devices  10.7 us (28%)
  Pallas kernels  7.07 us (19%)
  local copies, waits for them, and re-layouts  2.73 us (7%)
  between operations  0.8 us (2%)
    ppermute x4, starting transfers between devices, shards(): one_back.append(lax.ppermute(jnp.where(odd, block, own[n]), 'ex', swap))  6.96 us
    ppermute x4, starting transfers between devices, shards(): two_back.append(lax.ppermute(own[n], 'ex', ahead))  6.29 us
    ppermute x4, waiting for transfers between devices, shards(): two_back.append(lax.ppermute(own[n], 'ex', ahead))  5.27 us
    pallas_call x7, Pallas kernels, partial_scores(): pl.pallas_call(functools.partial(scores_kernel, cuts, bool(carry)), out_s...  4.34 us
    ppermute x4, waiting for transfers between devices, shards(): one_back.append(lax.ppermute(jnp.where(odd, block, own[n]), 'ex', swap))  2.73 us
    unnamed x4, local copies, waits for them, and re-layouts  2.73 us
    ppermute x4, starting transfers between devices, shards(): three_back.append(lax.ppermute(one_back[n], 'ex', ahead))  2.23 us
    ppermute x4, waiting for transfers between devices, shards(): three_back.append(lax.ppermute(one_back[n], 'ex', ahead))  1.93 us
  transfers between devices with their start and end apart: 16, of which 9 were waited for; matrix products, arithmetic and copies ran while one was open for 0% of the time, Pallas kernels for 12%

profile of v4, /device:TPU:0, one launch (start us, length us, event | category | flops | bytes accessed | tf_op | source)
XLA Modules:
  0.0 37.6 jit_solution(4507623811078893178)
XLA Ops:
  0.0 1.7 %shard_map.55 = (bf16[128,512]{1,0:T(8,128)(2,1)S(1)}, bf16[128,512]{1,0:T(8,128)(2,1)S(1)}, bf16[128,512]{1,0:T(8,128)(2,1)S(1)}, bf16[128,512]{1,0:T(8,128)(2,1)S(1)}) custom-call(bf16[128,2048]{1,0:T(8,128)(2,1)} %queries.1, f32[1,2048]{1,0:T(1,128)} %bitcast.1, s32[1,128]{1,0:T(1,128)} %rank.1), custom_call_target="tpu_custom_call" | custom-call | flops 67108864 | bytes 1048576 | tf_op jit(solution)/shard_map/pallas_call | solution.py:61
  1.7 3.1 %collective-permute-start.1 = (bf16[128,512]{1,0:T(8,128)(2,1)S(1)}, bf16[128,512]{1,0:T(8,128)(2,1)S(1)}, u32[]{:S(2)}, u32[]{:S(2)}) collective-permute-start(bf16[128,512]{1,0:T(8,128)(2,1)S(1)} %get-tuple-element.24.refs_1_), channel_id=1, source_target_pairs={{0,4},{2,6},{4,8},{6,10},{8,12},{10,14},{12,0},{14,2},{1,5},{3,7},... | collective-permute-start | bytes 393224 | tf_op jit(solution)/shard_map/ppermute | solution.py:163
  4.8 1.6 %collective-permute-start.3 = (bf16[128,512]{1,0:T(8,128)(2,1)S(1)}, bf16[128,512]{1,0:T(8,128)(2,1)S(1)}, u32[]{:S(2)}, u32[]{:S(2)}) collective-permute-start(bf16[128,512]{1,0:T(8,128)(2,1)S(1)} %get-tuple-element.25.refs_2_), channel_id=1, source_target_pairs={{0,4},{2,6},{4,8},{6,10},{8,12},{10,14},{12,0},{14,2},{1,5},{3,7},... | collective-permute-start | bytes 393224 | tf_op jit(solution)/shard_map/ppermute | solution.py:163
  6.4 1.6 %collective-permute-start.5 = (bf16[128,512]{1,0:T(8,128)(2,1)S(1)}, bf16[128,512]{1,0:T(8,128)(2,1)S(1)}, u32[]{:S(2)}, u32[]{:S(2)}) collective-permute-start(bf16[128,512]{1,0:T(8,128)(2,1)S(1)} %get-tuple-element.26.refs_3_), channel_id=1, source_target_pairs={{0,4},{2,6},{4,8},{6,10},{8,12},{10,14},{12,0},{14,2},{1,5},{3,7},... | collective-permute-start | bytes 393224 | tf_op jit(solution)/shard_map/ppermute | solution.py:163
  8.0 3.1 %collective-permute-done.1.refs_1_ = bf16[128,512]{1,0:T(8,128)(2,1)S(1)} collective-permute-done((bf16[128,512]{1,0:T(8,128)(2,1)S(1)}, bf16[128,512]{1,0:T(8,128)(2,1)S(1)}, u32[]{:S(2)}, u32[]{:S(2)}) %collective-permute-start.1) | collective-permute-done | bytes 131104 | tf_op jit(solution)/shard_map/ppermute | solution.py:163
  11.2 1.8 %collective-permute-start.2 = (bf16[128,512]{1,0:T(8,128)(2,1)S(1)}, bf16[128,512]{1,0:T(8,128)(2,1)S(1)}, u32[]{:S(2)}, u32[]{:S(2)}) collective-permute-start(bf16[128,512]{1,0:T(8,128)(2,1)S(1)} %broadcast_select_fusion.3), channel_id=1, source_target_pairs={{0,2},{2,0},{4,6},{6,4},{8,10},{10,8},{12,14},{14,12},{1,3},{3,1},... | collective-permute-start | bytes 393224 | tf_op jit(solution)/shard_map/ppermute | solution.py:168
  13.0 1.0 %collective-permute-done.3.refs_2_ = bf16[128,512]{1,0:T(8,128)(2,1)S(1)} collective-permute-done((bf16[128,512]{1,0:T(8,128)(2,1)S(1)}, bf16[128,512]{1,0:T(8,128)(2,1)S(1)}, u32[]{:S(2)}, u32[]{:S(2)}) %collective-permute-start.3) | collective-permute-done | bytes 131104 | tf_op jit(solution)/shard_map/ppermute | solution.py:163
  14.0 1.8 %collective-permute-start.4 = (bf16[128,512]{1,0:T(8,128)(2,1)S(1)}, bf16[128,512]{1,0:T(8,128)(2,1)S(1)}, u32[]{:S(2)}, u32[]{:S(2)}) collective-permute-start(bf16[128,512]{1,0:T(8,128)(2,1)S(1)} %broadcast_select_fusion.2), channel_id=1, source_target_pairs={{0,2},{2,0},{4,6},{6,4},{8,10},{10,8},{12,14},{14,12},{1,3},{3,1},... | collective-permute-start | bytes 393224 | tf_op jit(solution)/shard_map/ppermute | solution.py:168
  15.8 1.0 %collective-permute-done.5.refs_3_ = bf16[128,512]{1,0:T(8,128)(2,1)S(1)} collective-permute-done((bf16[128,512]{1,0:T(8,128)(2,1)S(1)}, bf16[128,512]{1,0:T(8,128)(2,1)S(1)}, u32[]{:S(2)}, u32[]{:S(2)}) %collective-permute-start.5) | collective-permute-done | bytes 131104 | tf_op jit(solution)/shard_map/ppermute | solution.py:163
  16.8 1.8 %collective-permute-start.6 = (bf16[128,512]{1,0:T(8,128)(2,1)S(1)}, bf16[128,512]{1,0:T(8,128)(2,1)S(1)}, u32[]{:S(2)}, u32[]{:S(2)}) collective-permute-start(bf16[128,512]{1,0:T(8,128)(2,1)S(1)} %broadcast_select_fusion.1), channel_id=1, source_target_pairs={{0,2},{2,0},{4,6},{6,4},{8,10},{10,8},{12,14},{14,12},{1,3},{3,1},... | collective-permute-start | bytes 393224 | tf_op jit(solution)/shard_map/ppermute | solution.py:168
  18.8 1.6 %collective-permute-start.8 = (bf16[128,512]{1,0:T(8,128)(2,1)S(1)}, bf16[128,512]{1,0:T(8,128)(2,1)S(1)}, u32[]{:S(2)}, u32[]{:S(2)}) collective-permute-start(bf16[128,512]{1,0:T(8,128)(2,1)S(1)} %broadcast_select_fusion), channel_id=1, source_target_pairs={{0,2},{2,0},{4,6},{6,4},{8,10},{10,8},{12,14},{14,12},{1,3},{3,1},... | collective-permute-start | bytes 393224 | tf_op jit(solution)/shard_map/ppermute | solution.py:168
  20.3 1.3 %collective-permute-start.13 = (bf16[128,512]{1,0:T(8,128)(2,1)S(1)}, bf16[128,512]{1,0:T(8,128)(2,1)S(1)}, u32[]{:S(2)}, u32[]{:S(2)}) collective-permute-start(bf16[128,512]{1,0:T(8,128)(2,1)S(1)} %collective-permute-done.4.refs_2_), channel_id=1, source_target_pairs={{0,4},{2,6},{4,8},{6,10},{8,12},{10,14},{12,0},{14,2},{1,5},{3,7},... | collective-permute-start | bytes 393224 | tf_op jit(solution)/shard_map/ppermute | solution.py:170
  21.6 1.3 %collective-permute-done.6.refs_3_ = bf16[128,512]{1,0:T(8,128)(2,1)S(1)} collective-permute-done((bf16[128,512]{1,0:T(8,128)(2,1)S(1)}, bf16[128,512]{1,0:T(8,128)(2,1)S(1)}, u32[]{:S(2)}, u32[]{:S(2)}) %collective-permute-start.6) | collective-permute-done | bytes 131104 | tf_op jit(solution)/shard_map/ppermute | solution.py:168
  23.2 1.4 %collective-permute-done.8.refs_4_ = bf16[128,512]{1,0:T(8,128)(2,1)S(1)} collective-permute-done((bf16[128,512]{1,0:T(8,128)(2,1)S(1)}, bf16[128,512]{1,0:T(8,128)(2,1)S(1)}, u32[]{:S(2)}, u32[]{:S(2)}) %collective-permute-start.8) | collective-permute-done | bytes 131104 | tf_op jit(solution)/shard_map/ppermute | solution.py:168
  24.6 0.7 %collective-permute-start.11 = (bf16[128,512]{1,0:T(8,128)(2,1)S(1)}, bf16[128,512]{1,0:T(8,128)(2,1)S(1)}, u32[]{:S(2)}, u32[]{:S(2)}) collective-permute-start(bf16[128,512]{1,0:T(8,128)(2,1)S(1)} %collective-permute-done.8.refs_4_), channel_id=1, source_target_pairs={{0,4},{2,6},{4,8},{6,10},{8,12},{10,14},{12,0},{14,2},{1,5},{3,7},... | collective-permute-start | bytes 393224 | tf_op jit(solution)/shard_map/ppermute | solution.py:170
  25.3 1.9 %copy-done = bf16[768,2048]{1,0:T(8,128)(2,1)S(1)} copy-done((bf16[768,2048]{1,0:T(8,128)(2,1)S(1)}, bf16[768,2048]{1,0:T(8,128)(2,1)}, u32[]{:S(2)}) %copy-start) | copy-done | bytes 3145752
  27.2 1.0 %shard_map.56 = (f32[384,128]{1,0:T(8,128)S(1)}, f32[384,128]{1,0:T(8,128)S(1)}) custom-call(bf16[768,2048]{1,0:T(8,128)(2,1)S(1)} %copy-done, bf16[128,512]{1,0:T(8,128)(2,1)S(1)} %get-tuple-element.24.refs_1_, bf16[128,512]{1,0:T(8,128)(2,1)S(1)} %get-tuple-element.25.refs_2_, bf16[128,512]{1,0:T(8,128)(2,1)S(1)} %get-tuple-element.26.refs_3_, ...), custom_call_target="tpu_custom_call" | custom-call | flops 402653184 | bytes 4063232 | tf_op jit(solution)/shard_map/pallas_call | solution.py:108
  28.2 0.8 %copy-done.1 = bf16[768,2048]{1,0:T(8,128)(2,1)S(1)} copy-done((bf16[768,2048]{1,0:T(8,128)(2,1)S(1)}, bf16[768,2048]{1,0:T(8,128)(2,1)}, u32[]{:S(2)}) %copy-start.1) | copy-done | bytes 3145752
  29.1 1.0 %shard_map.58 = (f32[384,128]{1,0:T(8,128)S(1)}, f32[384,128]{1,0:T(8,128)S(1)}) custom-call(bf16[768,2048]{1,0:T(8,128)(2,1)S(1)} %copy-done.1, bf16[128,512]{1,0:T(8,128)(2,1)S(1)} %collective-permute-done.1.refs_1_, bf16[128,512]{1,0:T(8,128)(2,1)S(1)} %collective-permute-done.3.refs_2_, bf16[128,512]{1,0:T(8,128)(2,1)S(1)} %collective-permute-done.5.refs_3_, ...), custom_call_target="tpu_custom_call" | custom-call | flops 402653184 | bytes 4063232 | tf_op jit(solution)/shard_map/pallas_call | solution.py:108
  30.5 1.0 %shard_map.57 = (f32[384,128]{1,0:T(8,128)S(1)}, f32[384,128]{1,0:T(8,128)S(1)}) custom-call(bf16[768,2048]{1,0:T(8,128)(2,1)S(1)} %copy-done.1, bf16[128,512]{1,0:T(8,128)(2,1)S(1)} %collective-permute-done.2.refs_1_, bf16[128,512]{1,0:T(8,128)(2,1)S(1)} %collective-permute-done.4.refs_2_, bf16[128,512]{1,0:T(8,128)(2,1)S(1)} %collective-permute-done.6.refs_3_, ...), custom_call_target="tpu_custom_call" | custom-call | flops 402653184 | bytes 4063232 | tf_op jit(solution)/shard_map/pallas_call | solution.py:108
  32.4 0.9 %collective-permute-done.12.refs_1_ = bf16[128,512]{1,0:T(8,128)(2,1)S(1)} collective-permute-done((bf16[128,512]{1,0:T(8,128)(2,1)S(1)}, bf16[128,512]{1,0:T(8,128)(2,1)S(1)}, u32[]{:S(2)}, u32[]{:S(2)}) %collective-permute-start.12) | collective-permute-done | bytes 131104 | tf_op jit(solution)/shard_map/ppermute | solution.py:170
  33.7 1.0 %collective-permute-done.11.refs_1_ = bf16[128,512]{1,0:T(8,128)(2,1)S(1)} collective-permute-done((bf16[128,512]{1,0:T(8,128)(2,1)S(1)}, bf16[128,512]{1,0:T(8,128)(2,1)S(1)}, u32[]{:S(2)}, u32[]{:S(2)}) %collective-permute-start.11) | collective-permute-done | bytes 131104 | tf_op jit(solution)/shard_map/ppermute | solution.py:170
  35.8 0.8 %collective-permute-done.15.refs_7_ = f32[384,128]{1,0:T(8,128)S(1)} collective-permute-done((f32[384,128]{1,0:T(8,128)S(1)}, f32[384,128]{1,0:T(8,128)S(1)}, u32[]{:S(2)}, u32[]{:S(2)}) %collective-permute-start.15) | collective-permute-done | bytes 196640 | tf_op jit(solution)/shard_map/ppermute | solution.py:179
  36.6 1.0 %shard_map.63 = f32[384,512]{1,0:T(8,128)} custom-call(s32[1]{0:T(128)S(6)} %copy.6.valid, f32[384,128]{1,0:T(8,128)S(1)} %get-tuple-element.28.refs_0_, f32[384,128]{1,0:T(8,128)S(1)} %collective-permute-done.refs_1_, f32[384,128]{1,0:T(8,128)S(1)} %get-tuple-element.31.refs_2_, f32[384,128]{1,0:T(8,128)S(1)} %collective-permute-done.9.refs_3_, ...), custom_call_target="tpu_custom_call" | custom-call | flops 196608 | bytes 2359296 | tf_op jit(solution)/shard_map/pallas_call | solution.py:135
  (25 shorter events, 2.8 us)
Async XLA Ops:
  1.7 9.4 %collective-permute-start.1 = (bf16[128,512]{1,0:T(8,128)(2,1)S(1)}, bf16[128,512]{1,0:T(8,128)(2,1)S(1)}, u32[]{:S(2)}, u32[]{:S(2)}) collective-permute-start(bf16[128,512]{1,0:T(8,128)(2,1)S(1)} %get-tuple-element.24.refs_1_), channel_id=1, source_target_pairs={{0,4},{2,6},{4,8},{6,10},{8,12},{10,14},{12,0},{14,2},{1,5},{3,7},... | collective-permute-start | bytes 393224 | tf_op jit(solution)/shard_map/ppermute | solution.py:163
  4.8 9.2 %collective-permute-start.3 = (bf16[128,512]{1,0:T(8,128)(2,1)S(1)}, bf16[128,512]{1,0:T(8,128)(2,1)S(1)}, u32[]{:S(2)}, u32[]{:S(2)}) collective-permute-start(bf16[128,512]{1,0:T(8,128)(2,1)S(1)} %get-tuple-element.25.refs_2_), channel_id=1, source_target_pairs={{0,4},{2,6},{4,8},{6,10},{8,12},{10,14},{12,0},{14,2},{1,5},{3,7},... | collective-permute-start | bytes 393224 | tf_op jit(solution)/shard_map/ppermute | solution.py:163
  6.4 10.4 %collective-permute-start.5 = (bf16[128,512]{1,0:T(8,128)(2,1)S(1)}, bf16[128,512]{1,0:T(8,128)(2,1)S(1)}, u32[]{:S(2)}, u32[]{:S(2)}) collective-permute-start(bf16[128,512]{1,0:T(8,128)(2,1)S(1)} %get-tuple-element.26.refs_3_), channel_id=1, source_target_pairs={{0,4},{2,6},{4,8},{6,10},{8,12},{10,14},{12,0},{14,2},{1,5},{3,7},... | collective-permute-start | bytes 393224 | tf_op jit(solution)/shard_map/ppermute | solution.py:163
  8.0 10.8 %collective-permute-start.7 = (bf16[128,512]{1,0:T(8,128)(2,1)S(1)}, bf16[128,512]{1,0:T(8,128)(2,1)S(1)}, u32[]{:S(2)}, u32[]{:S(2)}) collective-permute-start(bf16[128,512]{1,0:T(8,128)(2,1)S(1)} %get-tuple-element.27.refs_4_), channel_id=1, source_target_pairs={{0,4},{2,6},{4,8},{6,10},{8,12},{10,14},{12,0},{14,2},{1,5},{3,7},... | collective-permute-start | bytes 393224 | tf_op jit(solution)/shard_map/ppermute | solution.py:163
  11.2 7.6 %collective-permute-start.2 = (bf16[128,512]{1,0:T(8,128)(2,1)S(1)}, bf16[128,512]{1,0:T(8,128)(2,1)S(1)}, u32[]{:S(2)}, u32[]{:S(2)}) collective-permute-start(bf16[128,512]{1,0:T(8,128)(2,1)S(1)} %broadcast_select_fusion.3), channel_id=1, source_target_pairs={{0,2},{2,0},{4,6},{6,4},{8,10},{10,8},{12,14},{14,12},{1,3},{3,1},... | collective-permute-start | bytes 393224 | tf_op jit(solution)/shard_map/ppermute | solution.py:168
  14.0 6.4 %collective-permute-start.4 = (bf16[128,512]{1,0:T(8,128)(2,1)S(1)}, bf16[128,512]{1,0:T(8,128)(2,1)S(1)}, u32[]{:S(2)}, u32[]{:S(2)}) collective-permute-start(bf16[128,512]{1,0:T(8,128)(2,1)S(1)} %broadcast_select_fusion.2), channel_id=1, source_target_pairs={{0,2},{2,0},{4,6},{6,4},{8,10},{10,8},{12,14},{14,12},{1,3},{3,1},... | collective-permute-start | bytes 393224 | tf_op jit(solution)/shard_map/ppermute | solution.py:168
  16.8 6.1 %collective-permute-start.6 = (bf16[128,512]{1,0:T(8,128)(2,1)S(1)}, bf16[128,512]{1,0:T(8,128)(2,1)S(1)}, u32[]{:S(2)}, u32[]{:S(2)}) collective-permute-start(bf16[128,512]{1,0:T(8,128)(2,1)S(1)} %broadcast_select_fusion.1), channel_id=1, source_target_pairs={{0,2},{2,0},{4,6},{6,4},{8,10},{10,8},{12,14},{14,12},{1,3},{3,1},... | collective-permute-start | bytes 393224 | tf_op jit(solution)/shard_map/ppermute | solution.py:168
  18.8 5.9 %collective-permute-start.8 = (bf16[128,512]{1,0:T(8,128)(2,1)S(1)}, bf16[128,512]{1,0:T(8,128)(2,1)S(1)}, u32[]{:S(2)}, u32[]{:S(2)}) collective-permute-start(bf16[128,512]{1,0:T(8,128)(2,1)S(1)} %broadcast_select_fusion), channel_id=1, source_target_pairs={{0,2},{2,0},{4,6},{6,4},{8,10},{10,8},{12,14},{14,12},{1,3},{3,1},... | collective-permute-start | bytes 393224 | tf_op jit(solution)/shard_map/ppermute | solution.py:168
  20.3 9.7 %collective-permute-start.14 = (bf16[128,512]{1,0:T(8,128)(2,1)S(1)}, bf16[128,512]{1,0:T(8,128)(2,1)S(1)}, u32[]{:S(2)}, u32[]{:S(2)}) collective-permute-start(bf16[128,512]{1,0:T(8,128)(2,1)S(1)} %collective-permute-done.2.refs_1_), channel_id=1, source_target_pairs={{0,4},{2,6},{4,8},{6,10},{8,12},{10,14},{12,0},{14,2},{1,5},{3,7},... | collective-permute-start | bytes 393224 | tf_op jit(solution)/shard_map/ppermute | solution.py:170
  20.3 11.1 %collective-permute-start.13 = (bf16[128,512]{1,0:T(8,128)(2,1)S(1)}, bf16[128,512]{1,0:T(8,128)(2,1)S(1)}, u32[]{:S(2)}, u32[]{:S(2)}) collective-permute-start(bf16[128,512]{1,0:T(8,128)(2,1)S(1)} %collective-permute-done.4.refs_2_), channel_id=1, source_target_pairs={{0,4},{2,6},{4,8},{6,10},{8,12},{10,14},{12,0},{14,2},{1,5},{3,7},... | collective-permute-start | bytes 393224 | tf_op jit(solution)/shard_map/ppermute | solution.py:170
  22.9 10.4 %collective-permute-start.12 = (bf16[128,512]{1,0:T(8,128)(2,1)S(1)}, bf16[128,512]{1,0:T(8,128)(2,1)S(1)}, u32[]{:S(2)}, u32[]{:S(2)}) collective-permute-start(bf16[128,512]{1,0:T(8,128)(2,1)S(1)} %collective-permute-done.6.refs_3_), channel_id=1, source_target_pairs={{0,4},{2,6},{4,8},{6,10},{8,12},{10,14},{12,0},{14,2},{1,5},{3,7},... | collective-permute-start | bytes 393224 | tf_op jit(solution)/shard_map/ppermute | solution.py:170
  24.6 10.1 %collective-permute-start.11 = (bf16[128,512]{1,0:T(8,128)(2,1)S(1)}, bf16[128,512]{1,0:T(8,128)(2,1)S(1)}, u32[]{:S(2)}, u32[]{:S(2)}) collective-permute-start(bf16[128,512]{1,0:T(8,128)(2,1)S(1)} %collective-permute-done.8.refs_4_), channel_id=1, source_target_pairs={{0,4},{2,6},{4,8},{6,10},{8,12},{10,14},{12,0},{14,2},{1,5},{3,7},... | collective-permute-start | bytes 393224 | tf_op jit(solution)/shard_map/ppermute | solution.py:170
  25.3 1.9 %copy-start = (bf16[768,2048]{1,0:T(8,128)(2,1)S(1)}, bf16[768,2048]{1,0:T(8,128)(2,1)}, u32[]{:S(2)}) copy-start(bf16[768,2048]{1,0:T(8,128)(2,1)} %refs_0_.13) | copy-start | bytes 9437188
  27.2 1.9 %copy-start.1 = (bf16[768,2048]{1,0:T(8,128)(2,1)S(1)}, bf16[768,2048]{1,0:T(8,128)(2,1)}, u32[]{:S(2)}) copy-start(bf16[768,2048]{1,0:T(8,128)(2,1)} %refs_0_.13) | copy-start | bytes 9437188
  28.2 7.7 %collective-permute-start = (f32[384,128]{1,0:T(8,128)S(1)}, f32[384,128]{1,0:T(8,128)S(1)}, u32[]{:S(2)}, u32[]{:S(2)}) collective-permute-start(f32[384,128]{1,0:T(8,128)S(1)} %get-tuple-element.29), channel_id=1, source_target_pairs={{0,1},{1,0},{2,3},{3,2},{4,5},{5,4},{6,7},{7,6},{8,9},{9,8},{10,11... | collective-permute-start | bytes 589832 | tf_op jit(solution)/shard_map/ppermute | solution.py:175
  30.1 5.8 %collective-permute-start.10 = (f32[384,128]{1,0:T(8,128)S(1)}, f32[384,128]{1,0:T(8,128)S(1)}, u32[]{:S(2)}, u32[]{:S(2)}) collective-permute-start(f32[384,128]{1,0:T(8,128)S(1)} %get-tuple-element.34), channel_id=1, source_target_pairs={{0,1},{1,0},{2,3},{3,2},{4,5},{5,4},{6,7},{7,6},{8,9},{9,8},{10,11... | collective-permute-start | bytes 589832 | tf_op jit(solution)/shard_map/ppermute | solution.py:175
  31.5 4.4 %collective-permute-start.9 = (f32[384,128]{1,0:T(8,128)S(1)}, f32[384,128]{1,0:T(8,128)S(1)}, u32[]{:S(2)}, u32[]{:S(2)}) collective-permute-start(f32[384,128]{1,0:T(8,128)S(1)} %get-tuple-element.32), channel_id=1, source_target_pairs={{0,1},{1,0},{2,3},{3,2},{4,5},{5,4},{6,7},{7,6},{8,9},{9,8},{10,11... | collective-permute-start | bytes 589832 | tf_op jit(solution)/shard_map/ppermute | solution.py:175
  35.1 1.5 %collective-permute-start.15 = (f32[384,128]{1,0:T(8,128)S(1)}, f32[384,128]{1,0:T(8,128)S(1)}, u32[]{:S(2)}, u32[]{:S(2)}) collective-permute-start(f32[384,128]{1,0:T(8,128)S(1)} %get-tuple-element.42), channel_id=1, source_target_pairs={{0,1},{1,0},{2,3},{3,2},{4,5},{5,4},{6,7},{7,6},{8,9},{9,8},{10,11... | collective-permute-start | bytes 589832 | tf_op jit(solution)/shard_map/ppermute | solution.py:179

commit v5 on v4

--- a/solution.py
+++ b/solution.py
@@ -8,7 +8,7 @@
 from jax.sharding import PartitionSpec as P
 
 STEPS = 4
-PARTS = (4, 4, 4, 4)
+PARTS = (5, 5, 6)
 CHUNKS = len(PARTS)
 VMEM_BYTES = 16 * 1024 * 1024
 
@@ -31,7 +31,7 @@
 
 
 def prepare_kernel(queries, precond, rank, *refs):
-    chunks, (held, scale, places, arrived) = refs[:CHUNKS], refs[CHUNKS:]
+    own, chunks, (held, scale, places, arrived) = refs[0], refs[1:1 + CHUNKS], refs[1 + CHUNKS:]
     rows, depth = queries.shape
     cuts = cuts_of(depth)
     loads = [pltpu.make_async_copy(rank, places, arrived.at[CHUNKS])]
@@ -47,14 +47,15 @@
     for n, cut in enumerate(cuts):
         loads[2 + n].wait()
         pre = (held[:, cut].astype(jnp.float32) * scale[:, cut]).astype(jnp.bfloat16)
-        chunks[n][...] = jnp.dot(placing, pre, preferred_element_type=jnp.float32).astype(
-            jnp.bfloat16
-        )
+        ordered = jnp.dot(placing, pre, preferred_element_type=jnp.float32).astype(jnp.bfloat16)
+        own[:, cut] = ordered
+        chunks[n][...] = ordered
 
 
 def prepare(queries, precond, rank):
     rows, depth = queries.shape
-    shapes = [
+    shapes = [jax.ShapeDtypeStruct((rows, depth), jnp.bfloat16)]
+    shapes += [
         jax.ShapeDtypeStruct((rows, cut.stop - cut.start), jnp.bfloat16) for cut in cuts_of(depth)
     ]
     queries, precond, rank = [in_hbm(x) for x in (queries, precond, rank)]
@@ -62,7 +63,7 @@
         prepare_kernel,
         out_shape=shapes,
         in_specs=[pl.BlockSpec(memory_space=pltpu.HBM)] * 3,
-        out_specs=[whole_spec()] * CHUNKS,
+        out_specs=[whole_spec()] * (1 + CHUNKS),
         scratch_shapes=[
             pltpu.VMEM((rows, depth), jnp.bfloat16),
             pltpu.VMEM((1, depth), jnp.float32),
@@ -76,21 +77,31 @@
     )(queries, precond, rank)
 
 
-def scores_kernel(cuts, carried, *refs):
-    store, blocks = refs[0], refs[1:1 + len(cuts)]
-    carry = refs[1 + len(cuts):-2]
-    send, own = refs[-2:]
-    half = send.shape[0]
+def scores_kernel(pieces, carried, *refs):
+    store, (send, own) = refs[0], refs[-2:]
+    carry = refs[-4:-2] if carried else (None, None)
+    half, depth = send.shape[0], store.shape[1]
+    cuts = cuts_of(depth)
     me = lax.axis_index("dim")
-    for where, out in ((1 - me, send), (me, own)):
+    odd = lax.rem(lax.axis_index("ex"), 2) == 1
+
+    def block(place, n):
+        ref = refs[1 + place]
+        return ref[:, cuts[n]] if ref.shape[1] == depth else ref[...]
+
+    blocks = []
+    for n, even_place, odd_place in pieces:
+        value = block(even_place, n)
+        if odd_place != even_place:
+            value = jnp.where(odd, block(odd_place, n), value)
+        blocks.append((n, value))
+    for where, out, start in ((1 - me, send, carry[0]), (me, own, carry[1])):
         rows = pl.ds(pl.multiple_of(where * half, half), half)
-        total = None
-        if carried:
-            total = (carry[0] if out is send else carry[1])[...]
-        for n, block in zip(cuts, blocks):
+        total = start[...] if carried else None
+        for n, value in blocks:
             part = lax.dot_general(
-                store[rows, cuts_of(store.shape[1])[n]],
-                block[...],
+                store[rows, cuts[n]],
+                value,
                 (((1,), (1,)), ((), ())),
                 preferred_element_type=jnp.float32,
             )
@@ -98,15 +109,21 @@
         out[...] = total
 
 
-def partial_scores(store, blocks, carry=()):
-    cuts = [n for n, _ in blocks]
-    blocks = [block for _, block in blocks]
-    rows, columns = store.shape[0], blocks[0].shape[0]
+def partial_scores(store, pieces, carry=()):
+    operands, placed = [], []
+    for n, *blocks in pieces:
+        places = []
+        for block in blocks:
+            known = [i for i, operand in enumerate(operands) if operand is block]
+            places.append(known[0] if known else len(operands))
+            operands += [] if known else [block]
+        placed.append((n, places[0], places[-1]))
+    (rows, depth), columns = store.shape, operands[0].shape[0]
+    depth = sum(cuts_of(depth)[n].stop - cuts_of(depth)[n].start for n, *_ in pieces)
+    operands = [store, *operands, *carry]
     shape = jax.ShapeDtypeStruct((rows // 2, columns), jnp.float32)
-    operands = [store, *blocks, *carry]
-    depth = sum(block.shape[1] for block in blocks)
     return pl.pallas_call(
-        functools.partial(scores_kernel, cuts, bool(carry)),
+        functools.partial(scores_kernel, tuple(placed), bool(carry)),
         out_shape=[shape] * 2,
         in_specs=[whole_spec()] * len(operands),
         out_specs=[whole_spec()] * 2,
@@ -155,28 +172,36 @@
     odd = lax.rem(lax.axis_index("ex"), 2) == 1
     ahead = [(i, (i + 2) % size) for i in range(size)]
     swap = [(i, i ^ 1) for i in range(size)]
+    to_odd = [(i, i + 1) for i in range(0, size, 2)]
+    to_even = [(i + 1, i) for i in range(0, size, 2)]
     over_dim = [(0, 1), (1, 0)]
 
-    own = prepare(queries, precond[None, :], query_rank)
-    two_back, one_back, three_back = [], [], []
-    for n in range(CHUNKS):
-        two_back.append(lax.ppermute(own[n], "ex", ahead))
-    for n in range(CHUNKS):
-        block = two_back[n]
-        if n == CHUNKS - 1:
-            block = after(block, one_back[0])
-        one_back.append(lax.ppermute(jnp.where(odd, block, own[n]), "ex", swap))
-    for n in range(CHUNKS):
-        three_back.append(lax.ppermute(one_back[n], "ex", ahead))
-
+    def send(block, route, axis="ex"):
+        return lax.ppermute(block, axis, route)
+
+    own, *chunks = prepare(queries, precond[None, :], query_rank)
+    cuts = cuts_of(own.shape[1])
+    two_back = [send(chunk, ahead) for chunk in chunks]
+    odd_one_back = send(own, to_odd)
+    even_one_back = [send(block, to_even) for block in two_back]
+    up = send(jnp.where(odd, two_back[1], even_one_back[0]), ahead)
+    last_up = send(jnp.where(odd, odd_one_back[:, cuts[2]], even_one_back[2]), ahead)
+    odd_three_back = send(two_back[0], to_odd)
+    across = send(jnp.where(odd, up, two_back[1]), swap)
+
+    every = range(CHUNKS)
     pairs = []
-    for blocks in (own, one_back, two_back):
-        send, kept = partial_scores(store, list(enumerate(blocks)))
-        pairs.append((kept, lax.ppermute(send, "dim", over_dim)))
-    carry = ()
-    for n in range(CHUNKS):
-        carry = partial_scores(store, [(n, three_back[n])], carry)
-    pairs.append((carry[1], lax.ppermute(carry[0], "dim", over_dim)))
+    for pieces in (
+        [(n, own) for n in every],
+        [(n, even_one_back[n], odd_one_back) for n in every],
+        [(n, two_back[n]) for n in every],
+    ):
+        theirs, ours = partial_scores(store, pieces)
+        pairs.append((ours, send(theirs, over_dim, "dim")))
+    carry = partial_scores(store, [(0, up, odd_three_back)])
+    carry = partial_scores(store, [(1, across)], carry)
+    carry = partial_scores(store, [(2, last_up)], carry)
+    pairs.append((carry[1], send(carry[0], over_dim, "dim")))
     return finish(valid_rows, pairs)
 
 

time: 37.8 us -> 43.2 us (1.14)
  starting transfers between devices: 16.3 us -> 21.3 us
    ppermute x16 -> x15, starting transfers between devices: 16.3 us -> 21.3 us  [send(): return lax.ppermute(block, axis, route)]
    ppermute x16 -> x15, waiting for transfers between devices: 10.7 us -> 11 us  [send(): return lax.ppermute(block, axis, route)]
    pallas_call x7 -> x6, Pallas kernels: 4.34 us -> 4.29 us  [partial_scores(): pl.pallas_call(functools.partial(scores_kernel, tuple(placed), bool(carry...]
  transfers between devices with their start and end apart: 16 -> 15, of which waited for: 9 -> 3; matrix products, arithmetic and copies ran while one was open for 0% -> 0% of each run, Pallas kernels for 12% -> 10%
where the time goes in v5:
time: 43.2 us; the launch traced here: 42.9 us
  starting transfers between devices  21.3 us (49%)
  waiting for transfers between devices  11 us (25%)
  Pallas kernels  6.9 us (16%)
  local copies, waits for them, and re-layouts  2.71 us (6%)
  between operations  0.87 us (2%)
    ppermute x15, starting transfers between devices, send(): return lax.ppermute(block, axis, route)  21.3 us
    ppermute x15, waiting for transfers between devices, send(): return lax.ppermute(block, axis, route)  11 us
    pallas_call x6, Pallas kernels, partial_scores(): pl.pallas_call(functools.partial(scores_kernel, tuple(placed), bool(carry...  4.29 us
    unnamed x4, local copies, waits for them, and re-layouts  2.71 us
    pallas_call x1, Pallas kernels, prepare(): pl.pallas_call(prepare_kernel, out_shape=shapes, in_specs=[pl.BlockSpec(m...  1.6 us
    pallas_call x1, Pallas kernels, finish(): pl.pallas_call(finish_kernel, out_shape=jax.ShapeDtypeStruct((half, colum...  1.01 us
  transfers between devices with their start and end apart: 15, of which 3 were waited for; matrix products, arithmetic and copies ran while one was open for 0% of the time, Pallas kernels for 10%

profile of v5, /device:TPU:0, one launch (start us, length us, event | category | flops | bytes accessed | tf_op | source)
XLA Modules:
  0.0 42.9 jit_solution(4280623430914731663)
XLA Ops:
  0.0 1.6 %shard_map.55 = (bf16[128,2048]{1,0:T(8,128)(2,1)S(1)}, bf16[128,640]{1,0:T(8,128)(2,1)S(1)}, bf16[128,640]{1,0:T(8,128)(2,1)S(1)}, bf16[128,768]{1,0:T(8,128)(2,1)S(1)}) custom-call(bf16[128,2048]{1,0:T(8,128)(2,1)} %queries.1, f32[1,2048]{1,0:T(1,128)} %bitcast.1, s32[1,128]{1,0:T(1,128)} %rank.1), custom_call_target="tpu_custom_call" | custom-call | flops 67108864 | bytes 1048576 | tf_op jit(solution)/shard_map/pallas_call | solution.py:62
  1.6 3.1 %collective-permute-start.1 = (bf16[128,640]{1,0:T(8,128)(2,1)S(1)}, bf16[128,640]{1,0:T(8,128)(2,1)S(1)}, u32[]{:S(2)}, u32[]{:S(2)}) collective-permute-start(bf16[128,640]{1,0:T(8,128)(2,1)S(1)} %get-tuple-element.24), channel_id=1, source_target_pairs={{0,4},{2,6},{4,8},{6,10},{8,12},{10,14},{12,0},{14,2},{1,5},{3,7},... | collective-permute-start | bytes 491528 | tf_op jit(solution)/shard_map/ppermute | solution.py:180
  4.7 3.4 %collective-permute-start.3 = (bf16[128,2048]{1,0:T(8,128)(2,1)S(1)}, bf16[128,2048]{1,0:T(8,128)(2,1)S(1)}, u32[]{:S(2)}, u32[]{:S(2)}) collective-permute-start(bf16[128,2048]{1,0:T(8,128)(2,1)S(1)} %get-tuple-element.21.refs_1_), channel_id=1, source_target_pairs={{0,2},{4,6},{8,10},{12,14},{1,3},{5,7},{9,11},{13,15},{16,18},{20,... | collective-permute-start | bytes 1572872 | tf_op jit(solution)/shard_map/ppermute | solution.py:180
  8.1 1.6 %collective-permute-start.6 = (bf16[128,768]{1,0:T(8,128)(2,1)S(1)}, bf16[128,768]{1,0:T(8,128)(2,1)S(1)}, u32[]{:S(2)}, u32[]{:S(2)}) collective-permute-start(bf16[128,768]{1,0:T(8,128)(2,1)S(1)} %get-tuple-element.26), channel_id=1, source_target_pairs={{0,4},{2,6},{4,8},{6,10},{8,12},{10,14},{12,0},{14,2},{1,5},{3,7},... | collective-permute-start | bytes 589832 | tf_op jit(solution)/shard_map/ppermute | solution.py:180
  9.7 1.6 %collective-permute-start.4 = (bf16[128,640]{1,0:T(8,128)(2,1)S(1)}, bf16[128,640]{1,0:T(8,128)(2,1)S(1)}, u32[]{:S(2)}, u32[]{:S(2)}) collective-permute-start(bf16[128,640]{1,0:T(8,128)(2,1)S(1)} %get-tuple-element.25), channel_id=1, source_target_pairs={{0,4},{2,6},{4,8},{6,10},{8,12},{10,14},{12,0},{14,2},{1,5},{3,7},... | collective-permute-start | bytes 491528 | tf_op jit(solution)/shard_map/ppermute | solution.py:180
  11.3 1.3 %collective-permute-start.2 = (bf16[128,640]{1,0:T(8,128)(2,1)S(1)}, bf16[128,640]{1,0:T(8,128)(2,1)S(1)}, u32[]{:S(2)}, u32[]{:S(2)}) collective-permute-start(bf16[128,640]{1,0:T(8,128)(2,1)S(1)} %collective-permute-done.1.refs_1_), channel_id=1, source_target_pairs={{2,0},{6,4},{10,8},{14,12},{3,1},{7,5},{11,9},{15,13},{18,16},{22,... | collective-permute-start | bytes 491528 | tf_op jit(solution)/shard_map/ppermute | solution.py:180
  12.6 4.6 %collective-permute-start.13 = (bf16[128,640]{1,0:T(8,128)(2,1)S(1)}, bf16[128,640]{1,0:T(8,128)(2,1)S(1)}, u32[]{:S(2)}, u32[]{:S(2)}) collective-permute-start(bf16[128,640]{1,0:T(8,128)(2,1)S(1)} %collective-permute-done.1.refs_1_), channel_id=1, source_target_pairs={{0,2},{4,6},{8,10},{12,14},{1,3},{5,7},{9,11},{13,15},{16,18},{20,... | collective-permute-start | bytes 491528 | tf_op jit(solution)/shard_map/ppermute | solution.py:180
  17.2 2.4 %collective-permute-done.4.refs_2_ = bf16[128,640]{1,0:T(8,128)(2,1)S(1)} collective-permute-done((bf16[128,640]{1,0:T(8,128)(2,1)S(1)}, bf16[128,640]{1,0:T(8,128)(2,1)S(1)}, u32[]{:S(2)}, u32[]{:S(2)}) %collective-permute-start.4) | collective-permute-done | bytes 163872 | tf_op jit(solution)/shard_map/ppermute | solution.py:180
  19.6 1.3 %collective-permute-start.5 = (bf16[128,640]{1,0:T(8,128)(2,1)S(1)}, bf16[128,640]{1,0:T(8,128)(2,1)S(1)}, u32[]{:S(2)}, u32[]{:S(2)}) collective-permute-start(bf16[128,640]{1,0:T(8,128)(2,1)S(1)} %collective-permute-done.4.refs_2_), channel_id=1, source_target_pairs={{2,0},{6,4},{10,8},{14,12},{3,1},{7,5},{11,9},{15,13},{18,16},{22,... | collective-permute-start | bytes 491528 | tf_op jit(solution)/shard_map/ppermute | solution.py:180
  20.9 1.3 %collective-permute-start.7 = (bf16[128,768]{1,0:T(8,128)(2,1)S(1)}, bf16[128,768]{1,0:T(8,128)(2,1)S(1)}, u32[]{:S(2)}, u32[]{:S(2)}) collective-permute-start(bf16[128,768]{1,0:T(8,128)(2,1)S(1)} %collective-permute-done.6.refs_3_), channel_id=1, source_target_pairs={{2,0},{6,4},{10,8},{14,12},{3,1},{7,5},{11,9},{15,13},{18,16},{22,... | collective-permute-start | bytes 589832 | tf_op jit(solution)/shard_map/ppermute | solution.py:180
  22.3 7.8 %collective-permute-done.7.refs_4_ = bf16[128,768]{1,0:T(8,128)(2,1)S(1)} collective-permute-done((bf16[128,768]{1,0:T(8,128)(2,1)S(1)}, bf16[128,768]{1,0:T(8,128)(2,1)S(1)}, u32[]{:S(2)}, u32[]{:S(2)}) %collective-permute-start.7) | collective-permute-done | bytes 196640 | tf_op jit(solution)/shard_map/ppermute | solution.py:180
  30.2 2.3 %collective-permute-start.12 = (bf16[128,640]{1,0:T(8,128)(2,1)S(1)}, bf16[128,640]{1,0:T(8,128)(2,1)S(1)}, u32[]{:S(2)}, u32[]{:S(2)}) collective-permute-start(bf16[128,640]{1,0:T(8,128)(2,1)S(1)} %broadcast_select_fusion), channel_id=1, source_target_pairs={{0,2},{2,0},{4,6},{6,4},{8,10},{10,8},{12,14},{14,12},{1,3},{3,1},... | collective-permute-start | bytes 491528 | tf_op jit(solution)/shard_map/ppermute | solution.py:180
  32.5 1.9 %copy-done = bf16[768,2048]{1,0:T(8,128)(2,1)S(1)} copy-done((bf16[768,2048]{1,0:T(8,128)(2,1)S(1)}, bf16[768,2048]{1,0:T(8,128)(2,1)}, u32[]{:S(2)}) %copy-start) | copy-done | bytes 3145752
  34.4 1.0 %shard_map.56 = (f32[384,128]{1,0:T(8,128)S(1)}, f32[384,128]{1,0:T(8,128)S(1)}) custom-call(bf16[768,2048]{1,0:T(8,128)(2,1)S(1)} %copy-done, bf16[128,2048]{1,0:T(8,128)(2,1)S(1)} %get-tuple-element.21.refs_1_), custom_call_target="tpu_custom_call" | custom-call | flops 402653184 | bytes 4063232 | tf_op jit(solution)/shard_map/pallas_call | solution.py:125
  35.5 0.8 %copy-done.1 = bf16[768,2048]{1,0:T(8,128)(2,1)S(1)} copy-done((bf16[768,2048]{1,0:T(8,128)(2,1)S(1)}, bf16[768,2048]{1,0:T(8,128)(2,1)}, u32[]{:S(2)}) %copy-start.1) | copy-done | bytes 3145752
  36.3 1.0 %shard_map.58 = (f32[384,128]{1,0:T(8,128)S(1)}, f32[384,128]{1,0:T(8,128)S(1)}) custom-call(bf16[768,2048]{1,0:T(8,128)(2,1)S(1)} %copy-done.1, bf16[128,640]{1,0:T(8,128)(2,1)S(1)} %collective-permute-done.1.refs_1_, bf16[128,640]{1,0:T(8,128)(2,1)S(1)} %collective-permute-done.4.refs_2_, bf16[128,768]{1,0:T(8,128)(2,1)S(1)} %collective-permute-done.6.refs_3_), custom_call_target="tpu_custom_call" | custom-call | flops 402653184 | bytes 4063232 | tf_op jit(solution)/shard_map/pallas_call | solution.py:125
  37.4 0.4 %shard_map.59 = (f32[384,128]{1,0:T(8,128)S(1)}, f32[384,128]{1,0:T(8,128)S(1)}) custom-call(bf16[768,2048]{1,0:T(8,128)(2,1)S(1)} %copy-done.1, bf16[128,640]{1,0:T(8,128)(2,1)S(1)} %collective-permute-done.11.refs_1_, bf16[128,640]{1,0:T(8,128)(2,1)S(1)} %collective-permute-done.13.refs_2_), custom_call_target="tpu_custom_call" | custom-call | flops 125829120 | bytes 1540096 | tf_op jit(solution)/shard_map/pallas_call | solution.py:125
  37.9 1.0 %shard_map.57 = (f32[384,128]{1,0:T(8,128)S(1)}, f32[384,128]{1,0:T(8,128)S(1)}) custom-call(bf16[768,2048]{1,0:T(8,128)(2,1)S(1)} %copy-done.1, bf16[128,640]{1,0:T(8,128)(2,1)S(1)} %collective-permute-done.2.refs_1_, bf16[128,2048]{1,0:T(8,128)(2,1)S(1)} %collective-permute-done.3.refs_2_, bf16[128,640]{1,0:T(8,128)(2,1)S(1)} %collective-permute-done.5.refs_3_, ...), custom_call_target="tpu_custom_call" | custom-call | flops 402653184 | bytes 4063232 | tf_op jit(solution)/shard_map/pallas_call | solution.py:125
  38.9 0.6 %collective-permute-start.8 = (f32[384,128]{1,0:T(8,128)S(1)}, f32[384,128]{1,0:T(8,128)S(1)}, u32[]{:S(2)}, u32[]{:S(2)}) collective-permute-start(f32[384,128]{1,0:T(8,128)S(1)} %get-tuple-element.28), channel_id=1, source_target_pairs={{0,1},{1,0},{2,3},{3,2},{4,5},{5,4},{6,7},{7,6},{8,9},{9,8},{10,11... | collective-permute-start | bytes 589832 | tf_op jit(solution)/shard_map/ppermute | solution.py:180
  39.4 0.4 shard_map.60
  39.9 0.5 %shard_map.61 = (f32[384,128]{1,0:T(8,128)S(1)}, f32[384,128]{1,0:T(8,128)S(1)}) custom-call(bf16[768,2048]{1,0:T(8,128)(2,1)S(1)} %copy-done.1, bf16[128,768]{1,0:T(8,128)(2,1)S(1)} %collective-permute-done.10.refs_1_, f32[384,128]{1,0:T(8,128)S(1)} %get-tuple-element.33.refs_2_, f32[384,128]{1,0:T(8,128)S(1)} %get-tuple-element.34.refs_3_), custom_call_target="tpu_custom_call" | custom-call | flops 150994944 | bytes 1769472 | tf_op jit(solution)/shard_map/pallas_call | solution.py:125
  40.3 0.1 collective-permute-start.14
  41.1 0.7 %collective-permute-done.14.refs_7_ = f32[384,128]{1,0:T(8,128)S(1)} collective-permute-done((f32[384,128]{1,0:T(8,128)S(1)}, f32[384,128]{1,0:T(8,128)S(1)}, u32[]{:S(2)}, u32[]{:S(2)}) %collective-permute-start.14) | collective-permute-done | bytes 196640 | tf_op jit(solution)/shard_map/ppermute | solution.py:180
  41.8 1.0 %shard_map.62 = f32[384,512]{1,0:T(8,128)} custom-call(s32[1]{0:T(128)S(6)} %copy.6.valid, f32[384,128]{1,0:T(8,128)S(1)} %get-tuple-element.22.refs_0_, f32[384,128]{1,0:T(8,128)S(1)} %collective-permute-done.refs_1_, f32[384,128]{1,0:T(8,128)S(1)} %get-tuple-element.27.refs_2_, f32[384,128]{1,0:T(8,128)S(1)} %collective-permute-done.8.refs_3_, ...), custom_call_target="tpu_custom_call" | custom-call | flops 196608 | bytes 2359296 | tf_op jit(solution)/shard_map/pallas_call | solution.py:152
  (21 shorter events, 0.4 us)
Async XLA Ops:
  1.6 9.7 %collective-permute-start.1 = (bf16[128,640]{1,0:T(8,128)(2,1)S(1)}, bf16[128,640]{1,0:T(8,128)(2,1)S(1)}, u32[]{:S(2)}, u32[]{:S(2)}) collective-permute-start(bf16[128,640]{1,0:T(8,128)(2,1)S(1)} %get-tuple-element.24), channel_id=1, source_target_pairs={{0,4},{2,6},{4,8},{6,10},{8,12},{10,14},{12,0},{14,2},{1,5},{3,7},... | collective-permute-start | bytes 491528 | tf_op jit(solution)/shard_map/ppermute | solution.py:180
  4.7 25.4 %collective-permute-start.3 = (bf16[128,2048]{1,0:T(8,128)(2,1)S(1)}, bf16[128,2048]{1,0:T(8,128)(2,1)S(1)}, u32[]{:S(2)}, u32[]{:S(2)}) collective-permute-start(bf16[128,2048]{1,0:T(8,128)(2,1)S(1)} %get-tuple-element.21.refs_1_), channel_id=1, source_target_pairs={{0,2},{4,6},{8,10},{12,14},{1,3},{5,7},{9,11},{13,15},{16,18},{20,... | collective-permute-start | bytes 1572872 | tf_op jit(solution)/shard_map/ppermute | solution.py:180
  8.1 12.7 %collective-permute-start.6 = (bf16[128,768]{1,0:T(8,128)(2,1)S(1)}, bf16[128,768]{1,0:T(8,128)(2,1)S(1)}, u32[]{:S(2)}, u32[]{:S(2)}) collective-permute-start(bf16[128,768]{1,0:T(8,128)(2,1)S(1)} %get-tuple-element.26), channel_id=1, source_target_pairs={{0,4},{2,6},{4,8},{6,10},{8,12},{10,14},{12,0},{14,2},{1,5},{3,7},... | collective-permute-start | bytes 589832 | tf_op jit(solution)/shard_map/ppermute | solution.py:180
  9.7 9.8 %collective-permute-start.4 = (bf16[128,640]{1,0:T(8,128)(2,1)S(1)}, bf16[128,640]{1,0:T(8,128)(2,1)S(1)}, u32[]{:S(2)}, u32[]{:S(2)}) collective-permute-start(bf16[128,640]{1,0:T(8,128)(2,1)S(1)} %get-tuple-element.25), channel_id=1, source_target_pairs={{0,4},{2,6},{4,8},{6,10},{8,12},{10,14},{12,0},{14,2},{1,5},{3,7},... | collective-permute-start | bytes 491528 | tf_op jit(solution)/shard_map/ppermute | solution.py:180
  11.3 10.8 %collective-permute-start.2 = (bf16[128,640]{1,0:T(8,128)(2,1)S(1)}, bf16[128,640]{1,0:T(8,128)(2,1)S(1)}, u32[]{:S(2)}, u32[]{:S(2)}) collective-permute-start(bf16[128,640]{1,0:T(8,128)(2,1)S(1)} %collective-permute-done.1.refs_1_), channel_id=1, source_target_pairs={{2,0},{6,4},{10,8},{14,12},{3,1},{7,5},{11,9},{15,13},{18,16},{22,... | collective-permute-start | bytes 491528 | tf_op jit(solution)/shard_map/ppermute | solution.py:180
  12.6 24.7 %collective-permute-start.13 = (bf16[128,640]{1,0:T(8,128)(2,1)S(1)}, bf16[128,640]{1,0:T(8,128)(2,1)S(1)}, u32[]{:S(2)}, u32[]{:S(2)}) collective-permute-start(bf16[128,640]{1,0:T(8,128)(2,1)S(1)} %collective-permute-done.1.refs_1_), channel_id=1, source_target_pairs={{0,2},{4,6},{8,10},{12,14},{1,3},{5,7},{9,11},{13,15},{16,18},{20,... | collective-permute-start | bytes 491528 | tf_op jit(solution)/shard_map/ppermute | solution.py:180
  19.6 18.3 %collective-permute-start.5 = (bf16[128,640]{1,0:T(8,128)(2,1)S(1)}, bf16[128,640]{1,0:T(8,128)(2,1)S(1)}, u32[]{:S(2)}, u32[]{:S(2)}) collective-permute-start(bf16[128,640]{1,0:T(8,128)(2,1)S(1)} %collective-permute-done.4.refs_2_), channel_id=1, source_target_pairs={{2,0},{6,4},{10,8},{14,12},{3,1},{7,5},{11,9},{15,13},{18,16},{22,... | collective-permute-start | bytes 491528 | tf_op jit(solution)/shard_map/ppermute | solution.py:180
  20.9 9.2 %collective-permute-start.7 = (bf16[128,768]{1,0:T(8,128)(2,1)S(1)}, bf16[128,768]{1,0:T(8,128)(2,1)S(1)}, u32[]{:S(2)}, u32[]{:S(2)}) collective-permute-start(bf16[128,768]{1,0:T(8,128)(2,1)S(1)} %collective-permute-done.6.refs_3_), channel_id=1, source_target_pairs={{2,0},{6,4},{10,8},{14,12},{3,1},{7,5},{11,9},{15,13},{18,16},{22,... | collective-permute-start | bytes 589832 | tf_op jit(solution)/shard_map/ppermute | solution.py:180
  22.2 8.0 %collective-permute-start.11 = (bf16[128,640]{1,0:T(8,128)(2,1)S(1)}, bf16[128,640]{1,0:T(8,128)(2,1)S(1)}, u32[]{:S(2)}, u32[]{:S(2)}) collective-permute-start(bf16[128,640]{1,0:T(8,128)(2,1)S(1)} %broadcast_select_fusion.1), channel_id=1, source_target_pairs={{0,4},{2,6},{4,8},{6,10},{8,12},{10,14},{12,0},{14,2},{1,5},{3,7},... | collective-permute-start | bytes 491528 | tf_op jit(solution)/shard_map/ppermute | solution.py:180
  30.1 9.7 %collective-permute-start.10 = (bf16[128,768]{1,0:T(8,128)(2,1)S(1)}, bf16[128,768]{1,0:T(8,128)(2,1)S(1)}, u32[]{:S(2)}, u32[]{:S(2)}) collective-permute-start(bf16[128,768]{1,0:T(8,128)(2,1)S(1)} %slice_select_fusion), channel_id=1, source_target_pairs={{0,4},{2,6},{4,8},{6,10},{8,12},{10,14},{12,0},{14,2},{1,5},{3,7},... | collective-permute-start | bytes 589832 | tf_op jit(solution)/shard_map/ppermute | solution.py:180
  30.2 9.2 %collective-permute-start.12 = (bf16[128,640]{1,0:T(8,128)(2,1)S(1)}, bf16[128,640]{1,0:T(8,128)(2,1)S(1)}, u32[]{:S(2)}, u32[]{:S(2)}) collective-permute-start(bf16[128,640]{1,0:T(8,128)(2,1)S(1)} %broadcast_select_fusion), channel_id=1, source_target_pairs={{0,2},{2,0},{4,6},{6,4},{8,10},{10,8},{12,14},{14,12},{1,3},{3,1},... | collective-permute-start | bytes 491528 | tf_op jit(solution)/shard_map/ppermute | solution.py:180
  32.5 1.9 %copy-start = (bf16[768,2048]{1,0:T(8,128)(2,1)S(1)}, bf16[768,2048]{1,0:T(8,128)(2,1)}, u32[]{:S(2)}) copy-start(bf16[768,2048]{1,0:T(8,128)(2,1)} %refs_0_.11) | copy-start | bytes 9437188
  34.4 1.9 %copy-start.1 = (bf16[768,2048]{1,0:T(8,128)(2,1)S(1)}, bf16[768,2048]{1,0:T(8,128)(2,1)}, u32[]{:S(2)}) copy-start(bf16[768,2048]{1,0:T(8,128)(2,1)} %refs_0_.11) | copy-start | bytes 9437188
  35.4 5.7 %collective-permute-start = (f32[384,128]{1,0:T(8,128)S(1)}, f32[384,128]{1,0:T(8,128)S(1)}, u32[]{:S(2)}, u32[]{:S(2)}) collective-permute-start(f32[384,128]{1,0:T(8,128)S(1)} %get-tuple-element.23), channel_id=1, source_target_pairs={{0,1},{1,0},{2,3},{3,2},{4,5},{5,4},{6,7},{7,6},{8,9},{9,8},{10,11... | collective-permute-start | bytes 589832 | tf_op jit(solution)/shard_map/ppermute | solution.py:180
  37.3 3.8 %collective-permute-start.9 = (f32[384,128]{1,0:T(8,128)S(1)}, f32[384,128]{1,0:T(8,128)S(1)}, u32[]{:S(2)}, u32[]{:S(2)}) collective-permute-start(f32[384,128]{1,0:T(8,128)S(1)} %get-tuple-element.30), channel_id=1, source_target_pairs={{0,1},{1,0},{2,3},{3,2},{4,5},{5,4},{6,7},{7,6},{8,9},{9,8},{10,11... | collective-permute-start | bytes 589832 | tf_op jit(solution)/shard_map/ppermute | solution.py:180
  38.9 2.2 %collective-permute-start.8 = (f32[384,128]{1,0:T(8,128)S(1)}, f32[384,128]{1,0:T(8,128)S(1)}, u32[]{:S(2)}, u32[]{:S(2)}) collective-permute-start(f32[384,128]{1,0:T(8,128)S(1)} %get-tuple-element.28), channel_id=1, source_target_pairs={{0,1},{1,0},{2,3},{3,2},{4,5},{5,4},{6,7},{7,6},{8,9},{9,8},{10,11... | collective-permute-start | bytes 589832 | tf_op jit(solution)/shard_map/ppermute | solution.py:180
  40.3 1.5 %collective-permute-start.14 = (f32[384,128]{1,0:T(8,128)S(1)}, f32[384,128]{1,0:T(8,128)S(1)}, u32[]{:S(2)}, u32[]{:S(2)}) collective-permute-start(f32[384,128]{1,0:T(8,128)S(1)} %get-tuple-element.36), channel_id=1, source_target_pairs={{0,1},{1,0},{2,3},{3,2},{4,5},{5,4},{6,7},{7,6},{8,9},{9,8},{10,11... | collective-permute-start | bytes 589832 | tf_op jit(solution)/shard_map/ppermute | solution.py:180

commit v6 on v5

--- a/solution.py
+++ b/solution.py
@@ -8,7 +8,7 @@
 from jax.sharding import PartitionSpec as P
 
 STEPS = 4
-PARTS = (5, 5, 6)
+PARTS = (3, 4, 4, 5)
 CHUNKS = len(PARTS)
 VMEM_BYTES = 16 * 1024 * 1024
 
@@ -31,7 +31,7 @@
 
 
 def prepare_kernel(queries, precond, rank, *refs):
-    own, chunks, (held, scale, places, arrived) = refs[0], refs[1:1 + CHUNKS], refs[1 + CHUNKS:]
+    chunks, (held, scale, places, arrived) = refs[:CHUNKS], refs[CHUNKS:]
     rows, depth = queries.shape
     cuts = cuts_of(depth)
     loads = [pltpu.make_async_copy(rank, places, arrived.at[CHUNKS])]
@@ -47,15 +47,14 @@
     for n, cut in enumerate(cuts):
         loads[2 + n].wait()
         pre = (held[:, cut].astype(jnp.float32) * scale[:, cut]).astype(jnp.bfloat16)
-        ordered = jnp.dot(placing, pre, preferred_element_type=jnp.float32).astype(jnp.bfloat16)
-        own[:, cut] = ordered
-        chunks[n][...] = ordered
+        chunks[n][...] = jnp.dot(placing, pre, preferred_element_type=jnp.float32).astype(
+            jnp.bfloat16
+        )
 
 
 def prepare(queries, precond, rank):
     rows, depth = queries.shape
-    shapes = [jax.ShapeDtypeStruct((rows, depth), jnp.bfloat16)]
-    shapes += [
+    shapes = [
         jax.ShapeDtypeStruct((rows, cut.stop - cut.start), jnp.bfloat16) for cut in cuts_of(depth)
     ]
     queries, precond, rank = [in_hbm(x) for x in (queries, precond, rank)]
@@ -63,7 +62,7 @@
         prepare_kernel,
         out_shape=shapes,
         in_specs=[pl.BlockSpec(memory_space=pltpu.HBM)] * 3,
-        out_specs=[whole_spec()] * (1 + CHUNKS),
+        out_specs=[whole_spec()] * CHUNKS,
         scratch_shapes=[
             pltpu.VMEM((rows, depth), jnp.bfloat16),
             pltpu.VMEM((1, depth), jnp.float32),
@@ -163,46 +162,40 @@
     )(valid, *operands)
 
 
-def after(x, *earlier):
-    return lax.optimization_barrier((x, *earlier))[0]
-
-
 def shards(store, queries, precond, query_rank, valid_rows):
     size = lax.axis_size("ex")
     odd = lax.rem(lax.axis_index("ex"), 2) == 1
+    one_ahead = [(i, (i + 1) % size) for i in range(size)]
     ahead = [(i, (i + 2) % size) for i in range(size)]
     swap = [(i, i ^ 1) for i in range(size)]
-    to_odd = [(i, i + 1) for i in range(0, size, 2)]
-    to_even = [(i + 1, i) for i in range(0, size, 2)]
     over_dim = [(0, 1), (1, 0)]
 
     def send(block, route, axis="ex"):
         return lax.ppermute(block, axis, route)
 
-    own, *chunks = prepare(queries, precond[None, :], query_rank)
-    cuts = cuts_of(own.shape[1])
-    two_back = [send(chunk, ahead) for chunk in chunks]
-    odd_one_back = send(own, to_odd)
-    even_one_back = [send(block, to_even) for block in two_back]
-    up = send(jnp.where(odd, two_back[1], even_one_back[0]), ahead)
-    last_up = send(jnp.where(odd, odd_one_back[:, cuts[2]], even_one_back[2]), ahead)
-    odd_three_back = send(two_back[0], to_odd)
-    across = send(jnp.where(odd, up, two_back[1]), swap)
-
-    every = range(CHUNKS)
+    own = prepare(queries, precond[None, :], query_rank)
+    every, last = range(CHUNKS), CHUNKS - 1
+    two_back = [send(own[n], ahead) for n in every]
+    one_back = [send(jnp.where(odd, two_back[n], own[n]), swap) for n in every[:last]]
+    three_back = [send(one_back[n], ahead) for n in every[:last]]
+    direct = send(jnp.where(odd, two_back[last], own[last]), one_ahead)
+    swapped = send(two_back[last], swap)
+    one_back.append((swapped, direct))
+    three_back.append((direct, swapped))
+
     pairs = []
-    for pieces in (
-        [(n, own) for n in every],
-        [(n, even_one_back[n], odd_one_back) for n in every],
-        [(n, two_back[n]) for n in every],
-    ):
-        theirs, ours = partial_scores(store, pieces)
+    for blocks in (own, one_back, two_back):
+        theirs, ours = partial_scores(store, pieces_of(blocks))
         pairs.append((ours, send(theirs, over_dim, "dim")))
-    carry = partial_scores(store, [(0, up, odd_three_back)])
-    carry = partial_scores(store, [(1, across)], carry)
-    carry = partial_scores(store, [(2, last_up)], carry)
+    carry = ()
+    for piece in pieces_of(three_back):
+        carry = partial_scores(store, [piece], carry)
     pairs.append((carry[1], send(carry[0], over_dim, "dim")))
     return finish(valid_rows, pairs)
+
+
+def pieces_of(blocks):
+    return [(n, *block) if isinstance(block, tuple) else (n, block) for n, block in enumerate(blocks)]
 
 
 def solution(mesh):

time: 43.2 us -> 36.1 us (0.84)
  waiting for transfers between devices: 11 us -> 6.2 us
  starting transfers between devices: 21.3 us -> 18.9 us
    ppermute x15 -> x16, waiting for transfers between devices: 11 us -> 6.2 us  [send(): return lax.ppermute(block, axis, route)]
    ppermute x15 -> x16, starting transfers between devices: 21.3 us -> 18.9 us  [send(): return lax.ppermute(block, axis, route)]
    pallas_call x6 -> x7, Pallas kernels: 4.29 us -> 4.42 us  [partial_scores(): pl.pallas_call(functools.partial(scores_kernel, tuple(placed), bool(carry...]
  transfers between devices with their start and end apart: 15 -> 16, of which waited for: 3 -> 5; matrix products, arithmetic and copies ran while one was open for 0% -> 0% of each run, Pallas kernels for 10% -> 12%
where the time goes in v6:
time: 36.1 us; the launch traced here: 35.9 us
  starting transfers between devices  18.9 us (52%)
  Pallas kernels  7.13 us (20%)
  waiting for transfers between devices  6.2 us (17%)
  local copies, waits for them, and re-layouts  2.79 us (8%)
  between operations  0.79 us (2%)
    ppermute x16, starting transfers between devices, send(): return lax.ppermute(block, axis, route)  18.9 us
    ppermute x16, waiting for transfers between devices, send(): return lax.ppermute(block, axis, route)  6.2 us
    pallas_call x7, Pallas kernels, partial_scores(): pl.pallas_call(functools.partial(scores_kernel, tuple(placed), bool(carry...  4.42 us
    unnamed x4, local copies, waits for them, and re-layouts  2.79 us
    pallas_call x1, Pallas kernels, prepare(): pl.pallas_call(prepare_kernel, out_shape=shapes, in_specs=[pl.BlockSpec(m...  1.71 us
    pallas_call x1, Pallas kernels, finish(): pl.pallas_call(finish_kernel, out_shape=jax.ShapeDtypeStruct((half, colum...  1.01 us
  transfers between devices with their start and end apart: 16, of which 5 were waited for; matrix products, arithmetic and copies ran while one was open for 0% of the time, Pallas kernels for 12%

profile of v6, /device:TPU:0, one launch (start us, length us, event | category | flops | bytes accessed | tf_op | source)
XLA Modules:
  0.0 35.9 jit_solution(6011923882201465058)
XLA Ops:
  0.0 1.7 %shard_map.55 = (bf16[128,384]{1,0:T(8,128)(2,1)S(1)}, bf16[128,512]{1,0:T(8,128)(2,1)S(1)}, bf16[128,512]{1,0:T(8,128)(2,1)S(1)}, bf16[128,640]{1,0:T(8,128)(2,1)S(1)}) custom-call(bf16[128,2048]{1,0:T(8,128)(2,1)} %queries.1, f32[1,2048]{1,0:T(1,128)} %bitcast.1, s32[1,128]{1,0:T(1,128)} %rank.1), custom_call_target="tpu_custom_call" | custom-call | flops 67108864 | bytes 1048576 | tf_op jit(solution)/shard_map/pallas_call | solution.py:61
  1.7 3.1 %collective-permute-start.1 = (bf16[128,384]{1,0:T(8,128)(2,1)S(1)}, bf16[128,384]{1,0:T(8,128)(2,1)S(1)}, u32[]{:S(2)}, u32[]{:S(2)}) collective-permute-start(bf16[128,384]{1,0:T(8,128)(2,1)S(1)} %get-tuple-element.23.refs_1_), channel_id=1, source_target_pairs={{0,4},{2,6},{4,8},{6,10},{8,12},{10,14},{12,0},{14,2},{1,5},{3,7},... | collective-permute-start | bytes 294920 | tf_op jit(solution)/shard_map/ppermute | solution.py:174
  4.8 1.6 %collective-permute-start.3 = (bf16[128,512]{1,0:T(8,128)(2,1)S(1)}, bf16[128,512]{1,0:T(8,128)(2,1)S(1)}, u32[]{:S(2)}, u32[]{:S(2)}) collective-permute-start(bf16[128,512]{1,0:T(8,128)(2,1)S(1)} %get-tuple-element.24.refs_2_), channel_id=1, source_target_pairs={{0,4},{2,6},{4,8},{6,10},{8,12},{10,14},{12,0},{14,2},{1,5},{3,7},... | collective-permute-start | bytes 393224 | tf_op jit(solution)/shard_map/ppermute | solution.py:174
  6.4 1.6 %collective-permute-start.5 = (bf16[128,512]{1,0:T(8,128)(2,1)S(1)}, bf16[128,512]{1,0:T(8,128)(2,1)S(1)}, u32[]{:S(2)}, u32[]{:S(2)}) collective-permute-start(bf16[128,512]{1,0:T(8,128)(2,1)S(1)} %get-tuple-element.25.refs_3_), channel_id=1, source_target_pairs={{0,4},{2,6},{4,8},{6,10},{8,12},{10,14},{12,0},{14,2},{1,5},{3,7},... | collective-permute-start | bytes 393224 | tf_op jit(solution)/shard_map/ppermute | solution.py:174
  8.0 2.4 %collective-permute-done.1.refs_1_ = bf16[128,384]{1,0:T(8,128)(2,1)S(1)} collective-permute-done((bf16[128,384]{1,0:T(8,128)(2,1)S(1)}, bf16[128,384]{1,0:T(8,128)(2,1)S(1)}, u32[]{:S(2)}, u32[]{:S(2)}) %collective-permute-start.1) | collective-permute-done | bytes 98336 | tf_op jit(solution)/shard_map/ppermute | solution.py:174
  10.5 1.6 %collective-permute-start.2 = (bf16[128,384]{1,0:T(8,128)(2,1)S(1)}, bf16[128,384]{1,0:T(8,128)(2,1)S(1)}, u32[]{:S(2)}, u32[]{:S(2)}) collective-permute-start(bf16[128,384]{1,0:T(8,128)(2,1)S(1)} %broadcast_select_fusion.3), channel_id=1, source_target_pairs={{0,2},{2,0},{4,6},{6,4},{8,10},{10,8},{12,14},{14,12},{1,3},{3,1},... | collective-permute-start | bytes 294920 | tf_op jit(solution)/shard_map/ppermute | solution.py:174
  12.1 1.2 %collective-permute-done.3.refs_2_ = bf16[128,512]{1,0:T(8,128)(2,1)S(1)} collective-permute-done((bf16[128,512]{1,0:T(8,128)(2,1)S(1)}, bf16[128,512]{1,0:T(8,128)(2,1)S(1)}, u32[]{:S(2)}, u32[]{:S(2)}) %collective-permute-start.3) | collective-permute-done | bytes 131104 | tf_op jit(solution)/shard_map/ppermute | solution.py:174
  13.3 1.6 %collective-permute-start.4 = (bf16[128,512]{1,0:T(8,128)(2,1)S(1)}, bf16[128,512]{1,0:T(8,128)(2,1)S(1)}, u32[]{:S(2)}, u32[]{:S(2)}) collective-permute-start(bf16[128,512]{1,0:T(8,128)(2,1)S(1)} %broadcast_select_fusion.2), channel_id=1, source_target_pairs={{0,2},{2,0},{4,6},{6,4},{8,10},{10,8},{12,14},{14,12},{1,3},{3,1},... | collective-permute-start | bytes 393224 | tf_op jit(solution)/shard_map/ppermute | solution.py:174
  14.9 1.2 %collective-permute-done.5.refs_3_ = bf16[128,512]{1,0:T(8,128)(2,1)S(1)} collective-permute-done((bf16[128,512]{1,0:T(8,128)(2,1)S(1)}, bf16[128,512]{1,0:T(8,128)(2,1)S(1)}, u32[]{:S(2)}, u32[]{:S(2)}) %collective-permute-start.5) | collective-permute-done | bytes 131104 | tf_op jit(solution)/shard_map/ppermute | solution.py:174
  16.1 1.6 %collective-permute-start.6 = (bf16[128,512]{1,0:T(8,128)(2,1)S(1)}, bf16[128,512]{1,0:T(8,128)(2,1)S(1)}, u32[]{:S(2)}, u32[]{:S(2)}) collective-permute-start(bf16[128,512]{1,0:T(8,128)(2,1)S(1)} %broadcast_select_fusion.1), channel_id=1, source_target_pairs={{0,2},{2,0},{4,6},{6,4},{8,10},{10,8},{12,14},{14,12},{1,3},{3,1},... | collective-permute-start | bytes 393224 | tf_op jit(solution)/shard_map/ppermute | solution.py:174
  17.7 1.0 %collective-permute-done.7.refs_4_ = bf16[128,640]{1,0:T(8,128)(2,1)S(1)} collective-permute-done((bf16[128,640]{1,0:T(8,128)(2,1)S(1)}, bf16[128,640]{1,0:T(8,128)(2,1)S(1)}, u32[]{:S(2)}, u32[]{:S(2)}) %collective-permute-start.7) | collective-permute-done | bytes 163872 | tf_op jit(solution)/shard_map/ppermute | solution.py:174
  18.8 1.6 %collective-permute-start.9 = (bf16[128,640]{1,0:T(8,128)(2,1)S(1)}, bf16[128,640]{1,0:T(8,128)(2,1)S(1)}, u32[]{:S(2)}, u32[]{:S(2)}) collective-permute-start(bf16[128,640]{1,0:T(8,128)(2,1)S(1)} %broadcast_select_fusion), channel_id=1, source_target_pairs={{0,2},{2,4},{4,6},{6,8},{8,10},{10,12},{12,14},{14,0},{1,3},{3,5},... | collective-permute-start | bytes 491528 | tf_op jit(solution)/shard_map/ppermute | solution.py:174
  20.4 1.3 %collective-permute-start.14 = (bf16[128,384]{1,0:T(8,128)(2,1)S(1)}, bf16[128,384]{1,0:T(8,128)(2,1)S(1)}, u32[]{:S(2)}, u32[]{:S(2)}) collective-permute-start(bf16[128,384]{1,0:T(8,128)(2,1)S(1)} %collective-permute-done.2.refs_1_), channel_id=1, source_target_pairs={{0,4},{2,6},{4,8},{6,10},{8,12},{10,14},{12,0},{14,2},{1,5},{3,7},... | collective-permute-start | bytes 294920 | tf_op jit(solution)/shard_map/ppermute | solution.py:174
  21.7 1.5 %collective-permute-start.13 = (bf16[128,512]{1,0:T(8,128)(2,1)S(1)}, bf16[128,512]{1,0:T(8,128)(2,1)S(1)}, u32[]{:S(2)}, u32[]{:S(2)}) collective-permute-start(bf16[128,512]{1,0:T(8,128)(2,1)S(1)} %collective-permute-done.4.refs_2_), channel_id=1, source_target_pairs={{0,4},{2,6},{4,8},{6,10},{8,12},{10,14},{12,0},{14,2},{1,5},{3,7},... | collective-permute-start | bytes 393224 | tf_op jit(solution)/shard_map/ppermute | solution.py:174
  23.2 2.1 %collective-permute-start.12 = (bf16[128,512]{1,0:T(8,128)(2,1)S(1)}, bf16[128,512]{1,0:T(8,128)(2,1)S(1)}, u32[]{:S(2)}, u32[]{:S(2)}) collective-permute-start(bf16[128,512]{1,0:T(8,128)(2,1)S(1)} %collective-permute-done.6.refs_3_), channel_id=1, source_target_pairs={{0,4},{2,6},{4,8},{6,10},{8,12},{10,14},{12,0},{14,2},{1,5},{3,7},... | collective-permute-start | bytes 393224 | tf_op jit(solution)/shard_map/ppermute | solution.py:174
  25.3 1.9 %copy-done = bf16[768,2048]{1,0:T(8,128)(2,1)S(1)} copy-done((bf16[768,2048]{1,0:T(8,128)(2,1)S(1)}, bf16[768,2048]{1,0:T(8,128)(2,1)}, u32[]{:S(2)}) %copy-start) | copy-done | bytes 3145752
  27.1 1.0 %shard_map.56 = (f32[384,128]{1,0:T(8,128)S(1)}, f32[384,128]{1,0:T(8,128)S(1)}) custom-call(bf16[768,2048]{1,0:T(8,128)(2,1)S(1)} %copy-done, bf16[128,384]{1,0:T(8,128)(2,1)S(1)} %get-tuple-element.23.refs_1_, bf16[128,512]{1,0:T(8,128)(2,1)S(1)} %get-tuple-element.24.refs_2_, bf16[128,512]{1,0:T(8,128)(2,1)S(1)} %get-tuple-element.25.refs_3_, ...), custom_call_target="tpu_custom_call" | custom-call | flops 402653184 | bytes 4063232 | tf_op jit(solution)/shard_map/pallas_call | solution.py:124
  28.1 0.9 %copy-done.1 = bf16[768,2048]{1,0:T(8,128)(2,1)S(1)} copy-done((bf16[768,2048]{1,0:T(8,128)(2,1)S(1)}, bf16[768,2048]{1,0:T(8,128)(2,1)}, u32[]{:S(2)}) %copy-start.1) | copy-done | bytes 3145752
  29.0 1.0 %shard_map.58 = (f32[384,128]{1,0:T(8,128)S(1)}, f32[384,128]{1,0:T(8,128)S(1)}) custom-call(bf16[768,2048]{1,0:T(8,128)(2,1)S(1)} %copy-done.1, bf16[128,384]{1,0:T(8,128)(2,1)S(1)} %collective-permute-done.1.refs_1_, bf16[128,512]{1,0:T(8,128)(2,1)S(1)} %collective-permute-done.3.refs_2_, bf16[128,512]{1,0:T(8,128)(2,1)S(1)} %collective-permute-done.5.refs_3_, ...), custom_call_target="tpu_custom_call" | custom-call | flops 402653184 | bytes 4063232 | tf_op jit(solution)/shard_map/pallas_call | solution.py:124
  30.4 0.6 %collective-permute-start.11 = (f32[384,128]{1,0:T(8,128)S(1)}, f32[384,128]{1,0:T(8,128)S(1)}, u32[]{:S(2)}, u32[]{:S(2)}) collective-permute-start(f32[384,128]{1,0:T(8,128)S(1)} %get-tuple-element.32), channel_id=1, source_target_pairs={{0,1},{1,0},{2,3},{3,2},{4,5},{5,4},{6,7},{7,6},{8,9},{9,8},{10,11... | collective-permute-start | bytes 589832 | tf_op jit(solution)/shard_map/ppermute | solution.py:174
  31.0 1.0 %shard_map.57 = (f32[384,128]{1,0:T(8,128)S(1)}, f32[384,128]{1,0:T(8,128)S(1)}) custom-call(bf16[768,2048]{1,0:T(8,128)(2,1)S(1)} %copy-done.1, bf16[128,384]{1,0:T(8,128)(2,1)S(1)} %collective-permute-done.2.refs_1_, bf16[128,512]{1,0:T(8,128)(2,1)S(1)} %collective-permute-done.4.refs_2_, bf16[128,512]{1,0:T(8,128)(2,1)S(1)} %collective-permute-done.6.refs_3_, ...), custom_call_target="tpu_custom_call" | custom-call | flops 402653184 | bytes 4063232 | tf_op jit(solution)/shard_map/pallas_call | solution.py:124
  32.8 0.4 %shard_map.62 = (f32[384,128]{1,0:T(8,128)S(1)}, f32[384,128]{1,0:T(8,128)S(1)}) custom-call(bf16[768,2048]{1,0:T(8,128)(2,1)S(1)} %copy-done.1, bf16[128,640]{1,0:T(8,128)(2,1)S(1)} %collective-permute-done.9.refs_5_.refs_1_, bf16[128,640]{1,0:T(8,128)(2,1)S(1)} %collective-permute-done.8.refs_4_.refs_2_, f32[384,128]{1,0:T(8,128)S(1)} %get-tuple-element.37.refs_3_, ...), custom_call_target="tpu_custom_call" | custom-call | flops 125829120 | bytes 1540096 | tf_op jit(solution)/shard_map/pallas_call | solution.py:124
  33.3 0.6 %collective-permute-start.15 = (f32[384,128]{1,0:T(8,128)S(1)}, f32[384,128]{1,0:T(8,128)S(1)}, u32[]{:S(2)}, u32[]{:S(2)}) collective-permute-start(f32[384,128]{1,0:T(8,128)S(1)} %get-tuple-element.40), channel_id=1, source_target_pairs={{0,1},{1,0},{2,3},{3,2},{4,5},{5,4},{6,7},{7,6},{8,9},{9,8},{10,11... | collective-permute-start | bytes 589832 | tf_op jit(solution)/shard_map/ppermute | solution.py:174
  34.9 1.0 %shard_map.63 = f32[384,512]{1,0:T(8,128)} custom-call(s32[1]{0:T(128)S(6)} %copy.6.valid, f32[384,128]{1,0:T(8,128)S(1)} %get-tuple-element.27.refs_0_, f32[384,128]{1,0:T(8,128)S(1)} %collective-permute-done.refs_1_, f32[384,128]{1,0:T(8,128)S(1)} %get-tuple-element.29.refs_2_, f32[384,128]{1,0:T(8,128)S(1)} %collective-permute-done.10.refs_3_, ...), custom_call_target="tpu_custom_call" | custom-call | flops 196608 | bytes 2359296 | tf_op jit(solution)/shard_map/pallas_call | solution.py:151
  (25 shorter events, 1.8 us)
Async XLA Ops:
  1.7 8.7 %collective-permute-start.1 = (bf16[128,384]{1,0:T(8,128)(2,1)S(1)}, bf16[128,384]{1,0:T(8,128)(2,1)S(1)}, u32[]{:S(2)}, u32[]{:S(2)}) collective-permute-start(bf16[128,384]{1,0:T(8,128)(2,1)S(1)} %get-tuple-element.23.refs_1_), channel_id=1, source_target_pairs={{0,4},{2,6},{4,8},{6,10},{8,12},{10,14},{12,0},{14,2},{1,5},{3,7},... | collective-permute-start | bytes 294920 | tf_op jit(solution)/shard_map/ppermute | solution.py:174
  4.8 8.5 %collective-permute-start.3 = (bf16[128,512]{1,0:T(8,128)(2,1)S(1)}, bf16[128,512]{1,0:T(8,128)(2,1)S(1)}, u32[]{:S(2)}, u32[]{:S(2)}) collective-permute-start(bf16[128,512]{1,0:T(8,128)(2,1)S(1)} %get-tuple-element.24.refs_2_), channel_id=1, source_target_pairs={{0,4},{2,6},{4,8},{6,10},{8,12},{10,14},{12,0},{14,2},{1,5},{3,7},... | collective-permute-start | bytes 393224 | tf_op jit(solution)/shard_map/ppermute | solution.py:174
  6.4 9.7 %collective-permute-start.5 = (bf16[128,512]{1,0:T(8,128)(2,1)S(1)}, bf16[128,512]{1,0:T(8,128)(2,1)S(1)}, u32[]{:S(2)}, u32[]{:S(2)}) collective-permute-start(bf16[128,512]{1,0:T(8,128)(2,1)S(1)} %get-tuple-element.25.refs_3_), channel_id=1, source_target_pairs={{0,4},{2,6},{4,8},{6,10},{8,12},{10,14},{12,0},{14,2},{1,5},{3,7},... | collective-permute-start | bytes 393224 | tf_op jit(solution)/shard_map/ppermute | solution.py:174
  8.0 10.8 %collective-permute-start.7 = (bf16[128,640]{1,0:T(8,128)(2,1)S(1)}, bf16[128,640]{1,0:T(8,128)(2,1)S(1)}, u32[]{:S(2)}, u32[]{:S(2)}) collective-permute-start(bf16[128,640]{1,0:T(8,128)(2,1)S(1)} %get-tuple-element.26.refs_4_), channel_id=1, source_target_pairs={{0,4},{2,6},{4,8},{6,10},{8,12},{10,14},{12,0},{14,2},{1,5},{3,7},... | collective-permute-start | bytes 491528 | tf_op jit(solution)/shard_map/ppermute | solution.py:174
  10.5 9.9 %collective-permute-start.2 = (bf16[128,384]{1,0:T(8,128)(2,1)S(1)}, bf16[128,384]{1,0:T(8,128)(2,1)S(1)}, u32[]{:S(2)}, u32[]{:S(2)}) collective-permute-start(bf16[128,384]{1,0:T(8,128)(2,1)S(1)} %broadcast_select_fusion.3), channel_id=1, source_target_pairs={{0,2},{2,0},{4,6},{6,4},{8,10},{10,8},{12,14},{14,12},{1,3},{3,1},... | collective-permute-start | bytes 294920 | tf_op jit(solution)/shard_map/ppermute | solution.py:174
  13.3 8.4 %collective-permute-start.4 = (bf16[128,512]{1,0:T(8,128)(2,1)S(1)}, bf16[128,512]{1,0:T(8,128)(2,1)S(1)}, u32[]{:S(2)}, u32[]{:S(2)}) collective-permute-start(bf16[128,512]{1,0:T(8,128)(2,1)S(1)} %broadcast_select_fusion.2), channel_id=1, source_target_pairs={{0,2},{2,0},{4,6},{6,4},{8,10},{10,8},{12,14},{14,12},{1,3},{3,1},... | collective-permute-start | bytes 393224 | tf_op jit(solution)/shard_map/ppermute | solution.py:174
  16.1 7.1 %collective-permute-start.6 = (bf16[128,512]{1,0:T(8,128)(2,1)S(1)}, bf16[128,512]{1,0:T(8,128)(2,1)S(1)}, u32[]{:S(2)}, u32[]{:S(2)}) collective-permute-start(bf16[128,512]{1,0:T(8,128)(2,1)S(1)} %broadcast_select_fusion.1), channel_id=1, source_target_pairs={{0,2},{2,0},{4,6},{6,4},{8,10},{10,8},{12,14},{14,12},{1,3},{3,1},... | collective-permute-start | bytes 393224 | tf_op jit(solution)/shard_map/ppermute | solution.py:174
  18.8 11.7 %collective-permute-start.9 = (bf16[128,640]{1,0:T(8,128)(2,1)S(1)}, bf16[128,640]{1,0:T(8,128)(2,1)S(1)}, u32[]{:S(2)}, u32[]{:S(2)}) collective-permute-start(bf16[128,640]{1,0:T(8,128)(2,1)S(1)} %broadcast_select_fusion), channel_id=1, source_target_pairs={{0,2},{2,4},{4,6},{6,8},{8,10},{10,12},{12,14},{14,0},{1,3},{3,5},... | collective-permute-start | bytes 491528 | tf_op jit(solution)/shard_map/ppermute | solution.py:174
  20.3 10.7 %collective-permute-start.8 = (bf16[128,640]{1,0:T(8,128)(2,1)S(1)}, bf16[128,640]{1,0:T(8,128)(2,1)S(1)}, u32[]{:S(2)}, u32[]{:S(2)}) collective-permute-start(bf16[128,640]{1,0:T(8,128)(2,1)S(1)} %collective-permute-done.7.refs_4_), channel_id=1, source_target_pairs={{0,2},{2,0},{4,6},{6,4},{8,10},{10,8},{12,14},{14,12},{1,3},{3,1},... | collective-permute-start | bytes 491528 | tf_op jit(solution)/shard_map/ppermute | solution.py:174
  20.4 9.6 %collective-permute-start.14 = (bf16[128,384]{1,0:T(8,128)(2,1)S(1)}, bf16[128,384]{1,0:T(8,128)(2,1)S(1)}, u32[]{:S(2)}, u32[]{:S(2)}) collective-permute-start(bf16[128,384]{1,0:T(8,128)(2,1)S(1)} %collective-permute-done.2.refs_1_), channel_id=1, source_target_pairs={{0,4},{2,6},{4,8},{6,10},{8,12},{10,14},{12,0},{14,2},{1,5},{3,7},... | collective-permute-start | bytes 294920 | tf_op jit(solution)/shard_map/ppermute | solution.py:174
  21.7 10.4 %collective-permute-start.13 = (bf16[128,512]{1,0:T(8,128)(2,1)S(1)}, bf16[128,512]{1,0:T(8,128)(2,1)S(1)}, u32[]{:S(2)}, u32[]{:S(2)}) collective-permute-start(bf16[128,512]{1,0:T(8,128)(2,1)S(1)} %collective-permute-done.4.refs_2_), channel_id=1, source_target_pairs={{0,4},{2,6},{4,8},{6,10},{8,12},{10,14},{12,0},{14,2},{1,5},{3,7},... | collective-permute-start | bytes 393224 | tf_op jit(solution)/shard_map/ppermute | solution.py:174
  23.2 9.3 %collective-permute-start.12 = (bf16[128,512]{1,0:T(8,128)(2,1)S(1)}, bf16[128,512]{1,0:T(8,128)(2,1)S(1)}, u32[]{:S(2)}, u32[]{:S(2)}) collective-permute-start(bf16[128,512]{1,0:T(8,128)(2,1)S(1)} %collective-permute-done.6.refs_3_), channel_id=1, source_target_pairs={{0,4},{2,6},{4,8},{6,10},{8,12},{10,14},{12,0},{14,2},{1,5},{3,7},... | collective-permute-start | bytes 393224 | tf_op jit(solution)/shard_map/ppermute | solution.py:174
  25.2 1.9 %copy-start = (bf16[768,2048]{1,0:T(8,128)(2,1)S(1)}, bf16[768,2048]{1,0:T(8,128)(2,1)}, u32[]{:S(2)}) copy-start(bf16[768,2048]{1,0:T(8,128)(2,1)} %refs_0_.13) | copy-start | bytes 9437188
  27.1 1.9 %copy-start.1 = (bf16[768,2048]{1,0:T(8,128)(2,1)S(1)}, bf16[768,2048]{1,0:T(8,128)(2,1)}, u32[]{:S(2)}) copy-start(bf16[768,2048]{1,0:T(8,128)(2,1)} %refs_0_.13) | copy-start | bytes 9437188
  30.0 4.5 %collective-permute-start = (f32[384,128]{1,0:T(8,128)S(1)}, f32[384,128]{1,0:T(8,128)S(1)}, u32[]{:S(2)}, u32[]{:S(2)}) collective-permute-start(f32[384,128]{1,0:T(8,128)S(1)} %get-tuple-element.28), channel_id=1, source_target_pairs={{0,1},{1,0},{2,3},{3,2},{4,5},{5,4},{6,7},{7,6},{8,9},{9,8},{10,11... | collective-permute-start | bytes 589832 | tf_op jit(solution)/shard_map/ppermute | solution.py:174
  30.4 4.1 %collective-permute-start.11 = (f32[384,128]{1,0:T(8,128)S(1)}, f32[384,128]{1,0:T(8,128)S(1)}, u32[]{:S(2)}, u32[]{:S(2)}) collective-permute-start(f32[384,128]{1,0:T(8,128)S(1)} %get-tuple-element.32), channel_id=1, source_target_pairs={{0,1},{1,0},{2,3},{3,2},{4,5},{5,4},{6,7},{7,6},{8,9},{9,8},{10,11... | collective-permute-start | bytes 589832 | tf_op jit(solution)/shard_map/ppermute | solution.py:174
  32.0 2.5 %collective-permute-start.10 = (f32[384,128]{1,0:T(8,128)S(1)}, f32[384,128]{1,0:T(8,128)S(1)}, u32[]{:S(2)}, u32[]{:S(2)}) collective-permute-start(f32[384,128]{1,0:T(8,128)S(1)} %get-tuple-element.30), channel_id=1, source_target_pairs={{0,1},{1,0},{2,3},{3,2},{4,5},{5,4},{6,7},{7,6},{8,9},{9,8},{10,11... | collective-permute-start | bytes 589832 | tf_op jit(solution)/shard_map/ppermute | solution.py:174
  33.3 1.6 %collective-permute-start.15 = (f32[384,128]{1,0:T(8,128)S(1)}, f32[384,128]{1,0:T(8,128)S(1)}, u32[]{:S(2)}, u32[]{:S(2)}) collective-permute-start(f32[384,128]{1,0:T(8,128)S(1)} %get-tuple-element.40), channel_id=1, source_target_pairs={{0,1},{1,0},{2,3},{3,2},{4,5},{5,4},{6,7},{7,6},{8,9},{9,8},{10,11... | collective-permute-start | bytes 589832 | tf_op jit(solution)/shard_map/ppermute | solution.py:174

commit v7 on v4

v7 whole, which is shorter than its diff:
```python
import functools

import jax
import jax.numpy as jnp
from jax import lax
from jax.experimental import pallas as pl
from jax.experimental.pallas import tpu as pltpu
from jax.sharding import PartitionSpec as P

STEPS = 4
PARTS = (3, 4, 4, 5)
CHUNKS = len(PARTS)
TILES = 6
VMEM_BYTES = 16 * 1024 * 1024


def params():
    return pltpu.CompilerParams(vmem_limit_bytes=VMEM_BYTES)


def whole_spec():
    return pl.BlockSpec(memory_space=pltpu.VMEM)


def far_spec():
    return pl.BlockSpec(memory_space=pltpu.HBM)


def in_hbm(x):
    return pltpu.with_memory_space_constraint(x, pltpu.HBM)


def cost(flops, traffic):
    return pl.CostEstimate(flops=flops, bytes_accessed=traffic, transcendentals=0)


def cuts_of(depth):
    ends = [depth * sum(PARTS[:n + 1]) // sum(PARTS) for n in range(CHUNKS)]
    return [slice(start, end) for start, end in zip([0] + ends, ends)]


def product(rows, block):
    return lax.dot_general(
        rows, block, (((1,), (1,)), ((), ())), preferred_element_type=jnp.float32
    )


def prepare_kernel(queries, precond, rank, *refs):
    chunks, (held, scale, places, arrived) = refs[:CHUNKS], refs[CHUNKS:]
    rows, depth = queries.shape
    cuts = cuts_of(depth)
    loads = [pltpu.make_async_copy(rank, places, arrived.at[CHUNKS])]
    loads.append(pltpu.make_async_copy(precond, scale, arrived.at[CHUNKS + 1]))
    for n, cut in enumerate(cuts):
        loads.append(pltpu.make_async_copy(queries.at[:, cut], held.at[:, cut], arrived.at[n]))
    for load in loads:
        load.start()
    loads[0].wait()
    loads[1].wait()
    positions = lax.broadcasted_iota(jnp.int32, (rows, rows), 0)
    placing = (positions == places[...]).astype(jnp.bfloat16)
    for n, cut in enumerate(cuts):
        loads[2 + n].wait()
        pre = (held[:, cut].astype(jnp.float32) * scale[:, cut]).astype(jnp.bfloat16)
        chunks[n][...] = jnp.dot(placing, pre, preferred_element_type=jnp.float32).astype(
            jnp.bfloat16
        )


def prepare(queries, precond, rank):
    rows, depth = queries.shape
    shapes = [
        jax.ShapeDtypeStruct((rows, cut.stop - cut.start), jnp.bfloat16) for cut in cuts_of(depth)
    ]
    return pl.pallas_call(
        prepare_kernel,
        out_shape=shapes,
        in_specs=[far_spec()] * 3,
        out_specs=[whole_spec()] * CHUNKS,
        scratch_shapes=[
            pltpu.VMEM((rows, depth), jnp.bfloat16),
            pltpu.VMEM((1, depth), jnp.float32),
            pltpu.VMEM((1, rows), jnp.int32),
            pltpu.SemaphoreType.DMA((CHUNKS + 2,)),
        ],
        compiler_params=params(),
        cost_estimate=cost(2 * rows * rows * depth, 4 * rows * depth),
    )(in_hbm(queries), in_hbm(precond), in_hbm(rank))


def first_kernel(*refs):
    store, blocks, (held, send, own, arrived) = refs[0], refs[1:-4], refs[-4:]
    rows, depth = store.shape
    half, tile = rows // 2, rows // TILES
    cuts = cuts_of(depth)
    me = lax.axis_index("dim")
    loads, outs = [], []
    for n in range(TILES):
        out, where = (send, 1 - me) if n < TILES // 2 else (own, me)
        within = pl.ds(n % (TILES // 2) * tile, tile)
        place = pl.ds(pl.multiple_of(where * half + n % (TILES // 2) * tile, tile), tile)
        loads.append(pltpu.make_async_copy(store.at[place], held.at[place], arrived.at[n]))
        loads[n].start()
        outs.append((out, within, place))
    for n, (out, within, place) in enumerate(outs):
        loads[n].wait()
        total = None
        for cut, block in zip(cuts, blocks):
            part = product(held[place, cut], block[...])
            total = part if total is None else total + part
        out[within] = total


def first_scores(store, blocks):
    (rows, depth), columns = store.shape, blocks[0].shape[0]
    shape = jax.ShapeDtypeStruct((rows // 2, columns), jnp.float32)
    return pl.pallas_call(
        first_kernel,
        out_shape=[jax.ShapeDtypeStruct(store.shape, store.dtype), shape, shape],
        in_specs=[far_spec()] + [whole_spec()] * len(blocks),
        out_specs=[whole_spec()] * 3,
        scratch_shapes=[pltpu.SemaphoreType.DMA((TILES,))],
        compiler_params=params(),
        cost_estimate=cost(2 * rows * columns * depth, 2 * (rows + columns) * depth),
    )(in_hbm(store), *blocks)


def scores_kernel(pieces, fresh, *refs):
    count = len(fresh)
    store, outs = refs[0], refs[-2 * count:]
    carried = refs[-2 * count - 2 * (count - sum(fresh)):-2 * count]
    half = outs[0].shape[0]
    cuts = cuts_of(store.shape[1])
    me = lax.axis_index("dim")
    odd = lax.rem(lax.axis_index("ex"), 2) == 1
    sums = {}
    for side, where in enumerate((1 - me, me)):
        rows = pl.ds(pl.multiple_of(where * half, half), half)
        at = 0
        for i, new in enumerate(fresh):
            if not new:
                sums[i] = carried[at + side][...]
                at += 2
            else:
                sums[i] = None
        for n, targets in pieces:
            values = []
            for _, even_place, odd_place in targets:
                value = refs[1 + even_place][...]
                if odd_place != even_place:
                    value = jnp.where(odd, refs[1 + odd_place][...], value)
                values.append(value)
            columns = values[0].shape[0]
            stacked = values[0] if len(values) == 1 else jnp.concatenate(values, axis=0)
            part = product(store[rows, cuts[n]], stacked)
            for k, (i, _, _) in enumerate(targets):
                mine = part[:, k * columns:(k + 1) * columns]
                sums[i] = mine if sums[i] is None else sums[i] + mine
        for i in range(count):
            outs[2 * i + side][...] = sums[i]


def more_scores(store, pieces, carries):
    operands, placed = [], []

    def place(block):
        known = [i for i, operand in enumerate(operands) if operand is block]
        if not known:
            operands.append(block)
        return known[0] if known else len(operands) - 1

    (rows, depth), flops, traffic = store.shape, 0, 0
    for n, targets in pieces:
        kept = []
        for which, *blocks in targets:
            places = [place(block) for block in blocks]
            kept.append((which, places[0], places[-1]))
            flops += 2 * rows * blocks[0].size
        placed.append((n, tuple(kept)))
        traffic += 2 * rows * blocks[0].shape[1]
    columns = operands[0].shape[0]
    fresh = tuple(carry is None for carry in carries)
    operands = [store, *operands, *(half for carry in carries if carry for half in carry)]
    shape = jax.ShapeDtypeStruct((rows // 2, columns), jnp.float32)
    outs = pl.pallas_call(
        functools.partial(scores_kernel, tuple(placed), fresh),
        out_shape=[shape] * (2 * len(carries)),
        in_specs=[whole_spec()] * len(operands),
        out_specs=[whole_spec()] * (2 * len(carries)),
        compiler_params=params(),
        cost_estimate=cost(flops, traffic + 4 * rows * columns * len(carries)),
    )(*operands)
    return [(outs[2 * i], outs[2 * i + 1]) for i in range(len(carries))]


def finish_kernel(places, valid, *refs):
    out, summed, left = refs[-3:]
    half, columns = refs[0].shape
    row_ids = lax.broadcasted_iota(jnp.int32, (half, columns), 0) + lax.axis_index("dim") * half
    keep = row_ids < valid[0]
    stores = []
    for n, place in enumerate(places):
        cut = slice(n * columns, (n + 1) * columns)
        summed[:, cut] = jnp.where(keep, refs[2 * n][...] + refs[2 * n + 1][...], 0.0)
        to = out.at[:, place * columns:(place + 1) * columns]
        stores.append(pltpu.make_async_copy(summed.at[:, cut], to, left.at[n]))
        stores[n].start()
    for store in stores:
        store.wait()


def finish(valid, pairs, places, steps, out=None):
    half, columns = pairs[0][0].shape
    operands = [ref for pair in pairs for ref in pair]
    given = [] if out is None else [in_hbm(out)]
    return pl.pallas_call(
        functools.partial(finish_kernel, places),
        out_shape=pltpu.HBM((half, columns * steps), jnp.float32),
        in_specs=[pl.BlockSpec(memory_space=pltpu.SMEM)]
        + [whole_spec()] * len(operands)
        + [far_spec()] * len(given),
        out_specs=far_spec(),
        scratch_shapes=[
            pltpu.VMEM((half, columns * len(places)), jnp.float32),
            pltpu.SemaphoreType.DMA((len(places),)),
        ],
        input_output_aliases={1 + len(operands): 0} if given else {},
        compiler_params=params(),
        cost_estimate=cost(half * columns * len(pairs), 12 * half * columns * len(pairs)),
    )(valid, *operands, *given)


def after(x, *earlier):
    return lax.optimization_barrier((x, *earlier))[0]


def shards(store, queries, precond, query_rank, valid_rows):
    size = lax.axis_size("ex")
    odd = lax.rem(lax.axis_index("ex"), 2) == 1
    one_ahead = [(i, (i + 1) % size) for i in range(size)]
    ahead = [(i, (i + 2) % size) for i in range(size)]
    swap = [(i, i ^ 1) for i in range(size)]
    over_dim = [(0, 1), (1, 0)]

    def send(block, route, axis="ex"):
        return lax.ppermute(block, axis, route)

    def exchanged(total):
        theirs, ours = total
        return ours, send(theirs, over_dim, "dim")

    own = prepare(queries, precond[None, :], query_rank)
    every, last = range(CHUNKS), CHUNKS - 1
    two_back = [send(own[n], ahead) for n in every]
    store, *own_total = first_scores(store, own)
    own_pair = exchanged(own_total)

    blocks = [after(two_back[0], own_total[0]), *two_back[1:]]
    one_back = [send(jnp.where(odd, blocks[n], own[n]), swap) for n in every[:last]]
    three_back = [send(one_back[n], ahead) for n in every[:last]]
    direct = send(jnp.where(odd, two_back[last], own[last]), one_ahead)
    swapped = send(two_back[last], swap)

    two, one = more_scores(
        store,
        [(n, [(0, two_back[n]), (1, one_back[n])]) for n in every[:last]]
        + [(last, [(0, two_back[last])])],
        [None, None],
    )
    two_pair = exchanged(two)
    one, three = more_scores(
        store, [(last, [(0, swapped, direct), (1, direct, swapped)])], [one, None]
    )
    one_pair = exchanged(one)
    out = finish(valid_rows, [own_pair, one_pair, two_pair], (0, 1, 2), STEPS)
    [three] = more_scores(store, [(n, [(0, three_back[n])]) for n in every[:last - 1]], [three])
    [three] = more_scores(store, [(last - 1, [(0, three_back[last - 1])])], [three])
    return finish(valid_rows, [exchanged(three)], (3,), STEPS, out)


def solution(mesh):
    return jax.shard_map(
        shards,
        mesh=mesh,
        in_specs=(
            P(("groups", "ex"), "dim"),
            P(("groups", "ex"), "dim"),
            P("dim"),
            P(("groups", "ex"), None),
            P(("groups", "ex")),
        ),
        out_specs=P(("groups", "ex", "dim"), None),
        check_vma=False,
    )
```

time: 37.8 us -> 36.8 us (0.974)
  waiting for transfers between devices: 10.7 us -> 5.48 us
  starting transfers between devices: 16.3 us -> 21.4 us
  local copies, waits for them, and re-layouts: 2.73 us -> 0 us
  Pallas kernels: 7.07 us -> 8.81 us
    ppermute x16, waiting for transfers between devices: 10.7 us -> 5.48 us  [send(): return lax.ppermute(block, axis, route)]
    ppermute x16, starting transfers between devices: 16.3 us -> 21.4 us  [send(): return lax.ppermute(block, axis, route)]
    unnamed x4 -> x0, local copies, waits for them, and re-layouts: 2.73 us -> none
    pallas_call x9 -> x8, Pallas kernels: 7.07 us -> 8.81 us  [the longest x1 3.07 us: first_scores(): pl.pallas_call(first_kernel, out_shape=[jax.ShapeDtypeStruct(store.shape,...]
  transfers between devices with their start and end apart: 16 -> 16, of which waited for: 9 -> 4; matrix products, arithmetic and copies ran while one was open for 0% -> 0% of each run, Pallas kernels for 12% -> 17%
where the time goes in v7:
time: 36.8 us; the launch traced here: 36.6 us
  starting transfers between devices  21.4 us (58%)
  Pallas kernels  8.81 us (24%)
  waiting for transfers between devices  5.48 us (15%)
  between operations  0.8 us (2%)
    ppermute x16, starting transfers between devices, send(): return lax.ppermute(block, axis, route)  21.4 us
    ppermute x16, waiting for transfers between devices, send(): return lax.ppermute(block, axis, route)  5.48 us
    pallas_call x1, Pallas kernels, first_scores(): pl.pallas_call(first_kernel, out_shape=[jax.ShapeDtypeStruct(store.shape,...  3.07 us
    pallas_call x4, Pallas kernels, more_scores(): pl.pallas_call(functools.partial(scores_kernel, tuple(placed), fresh), ou...  2.44 us
    pallas_call x1, Pallas kernels, prepare(): pl.pallas_call(prepare_kernel, out_shape=shapes, in_specs=[far_spec()] *...  1.71 us
    pallas_call x2, Pallas kernels, finish(): pl.pallas_call(functools.partial(finish_kernel, places), out_shape=pltpu....  1.59 us
  transfers between devices with their start and end apart: 16, of which 4 were waited for; matrix products, arithmetic and copies ran while one was open for 0% of the time, Pallas kernels for 17%

profile of v7, /device:TPU:0, one launch (start us, length us, event | category | flops | bytes accessed | tf_op | source)
XLA Modules:
  0.0 36.6 jit_solution(5766129825874006973)
XLA Ops:
  0.0 1.7 %shard_map.55 = (bf16[128,384]{1,0:T(8,128)(2,1)S(1)}, bf16[128,512]{1,0:T(8,128)(2,1)S(1)}, bf16[128,512]{1,0:T(8,128)(2,1)S(1)}, bf16[128,640]{1,0:T(8,128)(2,1)S(1)}) custom-call(bf16[128,2048]{1,0:T(8,128)(2,1)} %queries.1, f32[1,2048]{1,0:T(1,128)} %bitcast.1, s32[1,128]{1,0:T(1,128)} %rank.1), custom_call_target="tpu_custom_call" | custom-call | flops 67108864 | bytes 1048576 | tf_op jit(solution)/shard_map/pallas_call | solution.py:75
  1.7 3.1 %collective-permute-start.3 = (bf16[128,384]{1,0:T(8,128)(2,1)S(1)}, bf16[128,384]{1,0:T(8,128)(2,1)S(1)}, u32[]{:S(2)}, u32[]{:S(2)}) collective-permute-start(bf16[128,384]{1,0:T(8,128)(2,1)S(1)} %get-tuple-element.25.refs_1_), channel_id=1, source_target_pairs={{0,4},{2,6},{4,8},{6,10},{8,12},{10,14},{12,0},{14,2},{1,5},{3,7},... | collective-permute-start | bytes 294920 | tf_op jit(solution)/shard_map/ppermute | solution.py:246
  4.8 1.6 %collective-permute-start.6 = (bf16[128,512]{1,0:T(8,128)(2,1)S(1)}, bf16[128,512]{1,0:T(8,128)(2,1)S(1)}, u32[]{:S(2)}, u32[]{:S(2)}) collective-permute-start(bf16[128,512]{1,0:T(8,128)(2,1)S(1)} %get-tuple-element.26.refs_2_), channel_id=1, source_target_pairs={{0,4},{2,6},{4,8},{6,10},{8,12},{10,14},{12,0},{14,2},{1,5},{3,7},... | collective-permute-start | bytes 393224 | tf_op jit(solution)/shard_map/ppermute | solution.py:246
  6.4 1.6 %collective-permute-start = (bf16[128,512]{1,0:T(8,128)(2,1)S(1)}, bf16[128,512]{1,0:T(8,128)(2,1)S(1)}, u32[]{:S(2)}, u32[]{:S(2)}) collective-permute-start(bf16[128,512]{1,0:T(8,128)(2,1)S(1)} %get-tuple-element.27.refs_3_), channel_id=1, source_target_pairs={{0,4},{2,6},{4,8},{6,10},{8,12},{10,14},{12,0},{14,2},{1,5},{3,7},... | collective-permute-start | bytes 393224 | tf_op jit(solution)/shard_map/ppermute | solution.py:246
  8.0 3.1 %shard_map.56 = (bf16[768,2048]{1,0:T(8,128)(2,1)S(1)}, f32[384,128]{1,0:T(8,128)S(1)}, f32[384,128]{1,0:T(8,128)S(1)}) custom-call(bf16[768,2048]{1,0:T(8,128)(2,1)} %refs_0_.1, bf16[128,384]{1,0:T(8,128)(2,1)S(1)} %get-tuple-element.25.refs_1_, bf16[128,512]{1,0:T(8,128)(2,1)S(1)} %get-tuple-element.26.refs_2_, ...), custom_call_target="tpu_custom_call" | custom-call | flops 402653184 | bytes 3670016 | tf_op jit(solution)/shard_map/pallas_call | solution.py:117
  11.1 1.7 %collective-permute-start.4 = (bf16[128,384]{1,0:T(8,128)(2,1)S(1)}, bf16[128,384]{1,0:T(8,128)(2,1)S(1)}, u32[]{:S(2)}, u32[]{:S(2)}) collective-permute-start(bf16[128,384]{1,0:T(8,128)(2,1)S(1)} %broadcast_select_fusion.3), channel_id=1, source_target_pairs={{0,2},{2,0},{4,6},{6,4},{8,10},{10,8},{12,14},{14,12},{1,3},{3,1},... | collective-permute-start | bytes 294920 | tf_op jit(solution)/shard_map/ppermute | solution.py:246
  12.9 0.4 %collective-permute-done.6.refs_3_ = bf16[128,512]{1,0:T(8,128)(2,1)S(1)} collective-permute-done((bf16[128,512]{1,0:T(8,128)(2,1)S(1)}, bf16[128,512]{1,0:T(8,128)(2,1)S(1)}, u32[]{:S(2)}, u32[]{:S(2)}) %collective-permute-start.6) | collective-permute-done | bytes 131104 | tf_op jit(solution)/shard_map/ppermute | solution.py:246
  13.3 1.6 %collective-permute-start.7 = (bf16[128,512]{1,0:T(8,128)(2,1)S(1)}, bf16[128,512]{1,0:T(8,128)(2,1)S(1)}, u32[]{:S(2)}, u32[]{:S(2)}) collective-permute-start(bf16[128,512]{1,0:T(8,128)(2,1)S(1)} %broadcast_select_fusion.1), channel_id=1, source_target_pairs={{0,2},{2,0},{4,6},{6,4},{8,10},{10,8},{12,14},{14,12},{1,3},{3,1},... | collective-permute-start | bytes 393224 | tf_op jit(solution)/shard_map/ppermute | solution.py:246
  14.9 1.2 %collective-permute-done.refs_5_ = bf16[128,512]{1,0:T(8,128)(2,1)S(1)} collective-permute-done((bf16[128,512]{1,0:T(8,128)(2,1)S(1)}, bf16[128,512]{1,0:T(8,128)(2,1)S(1)}, u32[]{:S(2)}, u32[]{:S(2)}) %collective-permute-start) | collective-permute-done | bytes 131104 | tf_op jit(solution)/shard_map/ppermute | solution.py:246
  16.1 1.6 %collective-permute-start.1 = (bf16[128,512]{1,0:T(8,128)(2,1)S(1)}, bf16[128,512]{1,0:T(8,128)(2,1)S(1)}, u32[]{:S(2)}, u32[]{:S(2)}) collective-permute-start(bf16[128,512]{1,0:T(8,128)(2,1)S(1)} %broadcast_select_fusion.2), channel_id=1, source_target_pairs={{0,2},{2,0},{4,6},{6,4},{8,10},{10,8},{12,14},{14,12},{1,3},{3,1},... | collective-permute-start | bytes 393224 | tf_op jit(solution)/shard_map/ppermute | solution.py:246
  17.7 1.0 %collective-permute-done.9.refs_7_ = bf16[128,640]{1,0:T(8,128)(2,1)S(1)} collective-permute-done((bf16[128,640]{1,0:T(8,128)(2,1)S(1)}, bf16[128,640]{1,0:T(8,128)(2,1)S(1)}, u32[]{:S(2)}, u32[]{:S(2)}) %collective-permute-start.9) | collective-permute-done | bytes 163872 | tf_op jit(solution)/shard_map/ppermute | solution.py:246
  18.8 1.6 %collective-permute-start.11 = (bf16[128,640]{1,0:T(8,128)(2,1)S(1)}, bf16[128,640]{1,0:T(8,128)(2,1)S(1)}, u32[]{:S(2)}, u32[]{:S(2)}) collective-permute-start(bf16[128,640]{1,0:T(8,128)(2,1)S(1)} %broadcast_select_fusion), channel_id=1, source_target_pairs={{0,2},{2,4},{4,6},{6,8},{8,10},{10,12},{12,14},{14,0},{1,3},{3,5},... | collective-permute-start | bytes 491528 | tf_op jit(solution)/shard_map/ppermute | solution.py:246
  20.4 1.3 %collective-permute-start.8 = (bf16[128,512]{1,0:T(8,128)(2,1)S(1)}, bf16[128,512]{1,0:T(8,128)(2,1)S(1)}, u32[]{:S(2)}, u32[]{:S(2)}) collective-permute-start(bf16[128,512]{1,0:T(8,128)(2,1)S(1)} %collective-permute-done.7.refs_4_), channel_id=1, source_target_pairs={{0,4},{2,6},{4,8},{6,10},{8,12},{10,14},{12,0},{14,2},{1,5},{3,7},... | collective-permute-start | bytes 393224 | tf_op jit(solution)/shard_map/ppermute | solution.py:246
  21.7 3.9 %collective-permute-start.2 = (bf16[128,512]{1,0:T(8,128)(2,1)S(1)}, bf16[128,512]{1,0:T(8,128)(2,1)S(1)}, u32[]{:S(2)}, u32[]{:S(2)}) collective-permute-start(bf16[128,512]{1,0:T(8,128)(2,1)S(1)} %collective-permute-done.1.refs_6_), channel_id=1, source_target_pairs={{0,4},{2,6},{4,8},{6,10},{8,12},{10,14},{12,0},{14,2},{1,5},{3,7},... | collective-permute-start | bytes 393224 | tf_op jit(solution)/shard_map/ppermute | solution.py:246
  25.5 2.2 %collective-permute-start.5 = (bf16[128,384]{1,0:T(8,128)(2,1)S(1)}, bf16[128,384]{1,0:T(8,128)(2,1)S(1)}, u32[]{:S(2)}, u32[]{:S(2)}) collective-permute-start(bf16[128,384]{1,0:T(8,128)(2,1)S(1)} %collective-permute-done.4.refs_2_), channel_id=1, source_target_pairs={{0,4},{2,6},{4,8},{6,10},{8,12},{10,14},{12,0},{14,2},{1,5},{3,7},... | collective-permute-start | bytes 294920 | tf_op jit(solution)/shard_map/ppermute | solution.py:246
  27.8 1.0 %shard_map.57 = (f32[384,128]{1,0:T(8,128)S(1)}, f32[384,128]{1,0:T(8,128)S(1)}, f32[384,128]{1,0:T(8,128)S(1)}, f32[384,128]{1,0:T(8,128)S(1)}) custom-call(bf16[768,2048]{1,0:T(8,128)(2,1)S(1)} %get-tuple-element.29.refs_0_, bf16[128,384]{1,0:T(8,128)(2,1)S(1)} %collective-permute-done.3.refs_1_, bf16[128,384]{1,0:T(8,128)(2,1)S(1)} %collective-permute-done.4.refs_2_, ...), custom_call_target="tpu_custom_call" | custom-call | flops 679477248 | bytes 3932160 | tf_op jit(solution)/shard_map/pallas_call | solution.py:185
  28.9 0.5 %collective-permute-start.15 = (f32[384,128]{1,0:T(8,128)S(1)}, f32[384,128]{1,0:T(8,128)S(1)}, u32[]{:S(2)}, u32[]{:S(2)}) collective-permute-start(f32[384,128]{1,0:T(8,128)S(1)} %get-tuple-element.44), channel_id=1, source_target_pairs={{0,1},{1,0},{2,3},{3,2},{4,5},{5,4},{6,7},{7,6},{8,9},{9,8},{10,11... | collective-permute-start | bytes 589832 | tf_op jit(solution)/shard_map/ppermute | solution.py:246
  29.4 0.5 %shard_map.58 = (f32[384,128]{1,0:T(8,128)S(1)}, f32[384,128]{1,0:T(8,128)S(1)}, f32[384,128]{1,0:T(8,128)S(1)}, f32[384,128]{1,0:T(8,128)S(1)}) custom-call(bf16[768,2048]{1,0:T(8,128)(2,1)S(1)} %get-tuple-element.29.refs_0_, bf16[128,640]{1,0:T(8,128)(2,1)S(1)} %collective-permute-done.10.refs_1_, bf16[128,640]{1,0:T(8,128)(2,1)S(1)} %collective-permute-done.11.refs_2_, ...), custom_call_target="tpu_custom_call" | custom-call | flops 251658240 | bytes 1769472 | tf_op jit(solution)/shard_map/pallas_call | solution.py:185
  29.9 2.9 %collective-permute-done.5.refs_1_ = bf16[128,384]{1,0:T(8,128)(2,1)S(1)} collective-permute-done((bf16[128,384]{1,0:T(8,128)(2,1)S(1)}, bf16[128,384]{1,0:T(8,128)(2,1)S(1)}, u32[]{:S(2)}, u32[]{:S(2)}) %collective-permute-start.5) | collective-permute-done | bytes 98336 | tf_op jit(solution)/shard_map/ppermute | solution.py:246
  32.8 0.5 %shard_map.59 = (f32[384,128]{1,0:T(8,128)S(1)}, f32[384,128]{1,0:T(8,128)S(1)}) custom-call(bf16[768,2048]{1,0:T(8,128)(2,1)S(1)} %get-tuple-element.29.refs_0_, bf16[128,384]{1,0:T(8,128)(2,1)S(1)} %collective-permute-done.5.refs_1_, bf16[128,512]{1,0:T(8,128)(2,1)S(1)} %collective-permute-done.8.refs_2_, f32[384,128]{1,0:T(8,128)S(1)} %get-tuple-element.34.refs_3_, ...), custom_call_target="tpu_custom_call" | custom-call | flops 176160768 | bytes 1769472 | tf_op jit(solution)/shard_map/pallas_call | solution.py:185
  33.3 0.4 %shard_map.60 = (f32[384,128]{1,0:T(8,128)S(1)}, f32[384,128]{1,0:T(8,128)S(1)}) custom-call(bf16[768,2048]{1,0:T(8,128)(2,1)S(1)} %get-tuple-element.29.refs_0_, bf16[128,512]{1,0:T(8,128)(2,1)S(1)} %collective-permute-done.2.refs_1_, f32[384,128]{1,0:T(8,128)S(1)} %get-tuple-element.36.refs_2_, f32[384,128]{1,0:T(8,128)S(1)} %get-tuple-element.37.refs_3_), custom_call_target="tpu_custom_call" | custom-call | flops 100663296 | bytes 1179648 | tf_op jit(solution)/shard_map/pallas_call | solution.py:185
  33.7 0.6 %collective-permute-start.12 = (f32[384,128]{1,0:T(8,128)S(1)}, f32[384,128]{1,0:T(8,128)S(1)}, u32[]{:S(2)}, u32[]{:S(2)}) collective-permute-start(f32[384,128]{1,0:T(8,128)S(1)} %get-tuple-element.39), channel_id=1, source_target_pairs={{0,1},{1,0},{2,3},{3,2},{4,5},{5,4},{6,7},{7,6},{8,9},{9,8},{10,11... | collective-permute-start | bytes 589832 | tf_op jit(solution)/shard_map/ppermute | solution.py:246
  35.0 0.9 %shard_map.61.refs_2_ = f32[384,512]{1,0:T(8,128)} custom-call(s32[1]{0:T(128)S(6)} %copy.8.valid, f32[384,128]{1,0:T(8,128)S(1)} %get-tuple-element.40.refs_0_, f32[384,128]{1,0:T(8,128)S(1)} %collective-permute-done.13.refs_1_, f32[384,128]{1,0:T(8,128)S(1)} %get-tuple-element.41.refs_2_, f32[384,128]{1,0:T(8,128)S(1)} %collective-permute-done.14.refs_3_, ...), custom_call_target="tpu_custom_call" | custom-call | flops 147456 | bytes 1769472 | tf_op jit(solution)/shard_map/pallas_call | solution.py:216
  35.9 0.7 %shard_map.62 = f32[384,512]{1,0:T(8,128)} custom-call(s32[1]{0:T(128)S(6)} %copy.8.valid, f32[384,128]{1,0:T(8,128)S(1)} %get-tuple-element.38.refs_0_, f32[384,128]{1,0:T(8,128)S(1)} %collective-permute-done.12.refs_1_, f32[384,512]{1,0:T(8,128)} %shard_map.61.refs_2_), custom_call_target="tpu_custom_call", output_to_operand_aliasing={{}: (3, {})} | custom-call | flops 49152 | bytes 589824 | tf_op jit(solution)/shard_map/pallas_call | solution.py:216
  (20 shorter events, 0.3 us)
Async XLA Ops:
  1.7 9.4 %collective-permute-start.3 = (bf16[128,384]{1,0:T(8,128)(2,1)S(1)}, bf16[128,384]{1,0:T(8,128)(2,1)S(1)}, u32[]{:S(2)}, u32[]{:S(2)}) collective-permute-start(bf16[128,384]{1,0:T(8,128)(2,1)S(1)} %get-tuple-element.25.refs_1_), channel_id=1, source_target_pairs={{0,4},{2,6},{4,8},{6,10},{8,12},{10,14},{12,0},{14,2},{1,5},{3,7},... | collective-permute-start | bytes 294920 | tf_op jit(solution)/shard_map/ppermute | solution.py:246
  4.8 8.5 %collective-permute-start.6 = (bf16[128,512]{1,0:T(8,128)(2,1)S(1)}, bf16[128,512]{1,0:T(8,128)(2,1)S(1)}, u32[]{:S(2)}, u32[]{:S(2)}) collective-permute-start(bf16[128,512]{1,0:T(8,128)(2,1)S(1)} %get-tuple-element.26.refs_2_), channel_id=1, source_target_pairs={{0,4},{2,6},{4,8},{6,10},{8,12},{10,14},{12,0},{14,2},{1,5},{3,7},... | collective-permute-start | bytes 393224 | tf_op jit(solution)/shard_map/ppermute | solution.py:246
  6.4 9.7 %collective-permute-start = (bf16[128,512]{1,0:T(8,128)(2,1)S(1)}, bf16[128,512]{1,0:T(8,128)(2,1)S(1)}, u32[]{:S(2)}, u32[]{:S(2)}) collective-permute-start(bf16[128,512]{1,0:T(8,128)(2,1)S(1)} %get-tuple-element.27.refs_3_), channel_id=1, source_target_pairs={{0,4},{2,6},{4,8},{6,10},{8,12},{10,14},{12,0},{14,2},{1,5},{3,7},... | collective-permute-start | bytes 393224 | tf_op jit(solution)/shard_map/ppermute | solution.py:246
  8.0 10.8 %collective-permute-start.9 = (bf16[128,640]{1,0:T(8,128)(2,1)S(1)}, bf16[128,640]{1,0:T(8,128)(2,1)S(1)}, u32[]{:S(2)}, u32[]{:S(2)}) collective-permute-start(bf16[128,640]{1,0:T(8,128)(2,1)S(1)} %get-tuple-element.28.refs_4_), channel_id=1, source_target_pairs={{0,4},{2,6},{4,8},{6,10},{8,12},{10,14},{12,0},{14,2},{1,5},{3,7},... | collective-permute-start | bytes 491528 | tf_op jit(solution)/shard_map/ppermute | solution.py:246
  11.1 14.4 %collective-permute-start.4 = (bf16[128,384]{1,0:T(8,128)(2,1)S(1)}, bf16[128,384]{1,0:T(8,128)(2,1)S(1)}, u32[]{:S(2)}, u32[]{:S(2)}) collective-permute-start(bf16[128,384]{1,0:T(8,128)(2,1)S(1)} %broadcast_select_fusion.3), channel_id=1, source_target_pairs={{0,2},{2,0},{4,6},{6,4},{8,10},{10,8},{12,14},{14,12},{1,3},{3,1},... | collective-permute-start | bytes 294920 | tf_op jit(solution)/shard_map/ppermute | solution.py:246
  13.3 7.1 %collective-permute-start.7 = (bf16[128,512]{1,0:T(8,128)(2,1)S(1)}, bf16[128,512]{1,0:T(8,128)(2,1)S(1)}, u32[]{:S(2)}, u32[]{:S(2)}) collective-permute-start(bf16[128,512]{1,0:T(8,128)(2,1)S(1)} %broadcast_select_fusion.1), channel_id=1, source_target_pairs={{0,2},{2,0},{4,6},{6,4},{8,10},{10,8},{12,14},{14,12},{1,3},{3,1},... | collective-permute-start | bytes 393224 | tf_op jit(solution)/shard_map/ppermute | solution.py:246
  16.1 5.6 %collective-permute-start.1 = (bf16[128,512]{1,0:T(8,128)(2,1)S(1)}, bf16[128,512]{1,0:T(8,128)(2,1)S(1)}, u32[]{:S(2)}, u32[]{:S(2)}) collective-permute-start(bf16[128,512]{1,0:T(8,128)(2,1)S(1)} %broadcast_select_fusion.2), channel_id=1, source_target_pairs={{0,2},{2,0},{4,6},{6,4},{8,10},{10,8},{12,14},{14,12},{1,3},{3,1},... | collective-permute-start | bytes 393224 | tf_op jit(solution)/shard_map/ppermute | solution.py:246
  18.8 10.1 %collective-permute-start.11 = (bf16[128,640]{1,0:T(8,128)(2,1)S(1)}, bf16[128,640]{1,0:T(8,128)(2,1)S(1)}, u32[]{:S(2)}, u32[]{:S(2)}) collective-permute-start(bf16[128,640]{1,0:T(8,128)(2,1)S(1)} %broadcast_select_fusion), channel_id=1, source_target_pairs={{0,2},{2,4},{4,6},{6,8},{8,10},{10,12},{12,14},{14,0},{1,3},{3,5},... | collective-permute-start | bytes 491528 | tf_op jit(solution)/shard_map/ppermute | solution.py:246
  20.3 8.6 %collective-permute-start.10 = (bf16[128,640]{1,0:T(8,128)(2,1)S(1)}, bf16[128,640]{1,0:T(8,128)(2,1)S(1)}, u32[]{:S(2)}, u32[]{:S(2)}) collective-permute-start(bf16[128,640]{1,0:T(8,128)(2,1)S(1)} %collective-permute-done.9.refs_7_), channel_id=1, source_target_pairs={{0,2},{2,0},{4,6},{6,4},{8,10},{10,8},{12,14},{14,12},{1,3},{3,1},... | collective-permute-start | bytes 491528 | tf_op jit(solution)/shard_map/ppermute | solution.py:246
  20.4 12.4 %collective-permute-start.8 = (bf16[128,512]{1,0:T(8,128)(2,1)S(1)}, bf16[128,512]{1,0:T(8,128)(2,1)S(1)}, u32[]{:S(2)}, u32[]{:S(2)}) collective-permute-start(bf16[128,512]{1,0:T(8,128)(2,1)S(1)} %collective-permute-done.7.refs_4_), channel_id=1, source_target_pairs={{0,4},{2,6},{4,8},{6,10},{8,12},{10,14},{12,0},{14,2},{1,5},{3,7},... | collective-permute-start | bytes 393224 | tf_op jit(solution)/shard_map/ppermute | solution.py:246
  21.7 11.7 %collective-permute-start.2 = (bf16[128,512]{1,0:T(8,128)(2,1)S(1)}, bf16[128,512]{1,0:T(8,128)(2,1)S(1)}, u32[]{:S(2)}, u32[]{:S(2)}) collective-permute-start(bf16[128,512]{1,0:T(8,128)(2,1)S(1)} %collective-permute-done.1.refs_6_), channel_id=1, source_target_pairs={{0,4},{2,6},{4,8},{6,10},{8,12},{10,14},{12,0},{14,2},{1,5},{3,7},... | collective-permute-start | bytes 393224 | tf_op jit(solution)/shard_map/ppermute | solution.py:246
  25.5 7.3 %collective-permute-start.5 = (bf16[128,384]{1,0:T(8,128)(2,1)S(1)}, bf16[128,384]{1,0:T(8,128)(2,1)S(1)}, u32[]{:S(2)}, u32[]{:S(2)}) collective-permute-start(bf16[128,384]{1,0:T(8,128)(2,1)S(1)} %collective-permute-done.4.refs_2_), channel_id=1, source_target_pairs={{0,4},{2,6},{4,8},{6,10},{8,12},{10,14},{12,0},{14,2},{1,5},{3,7},... | collective-permute-start | bytes 294920 | tf_op jit(solution)/shard_map/ppermute | solution.py:246
  28.8 6.1 %collective-permute-start.13 = (f32[384,128]{1,0:T(8,128)S(1)}, f32[384,128]{1,0:T(8,128)S(1)}, u32[]{:S(2)}, u32[]{:S(2)}) collective-permute-start(f32[384,128]{1,0:T(8,128)S(1)} %get-tuple-element.30), channel_id=1, source_target_pairs={{0,1},{1,0},{2,3},{3,2},{4,5},{5,4},{6,7},{7,6},{8,9},{9,8},{10,11... | collective-permute-start | bytes 589832 | tf_op jit(solution)/shard_map/ppermute | solution.py:246
  28.9 6.0 %collective-permute-start.15 = (f32[384,128]{1,0:T(8,128)S(1)}, f32[384,128]{1,0:T(8,128)S(1)}, u32[]{:S(2)}, u32[]{:S(2)}) collective-permute-start(f32[384,128]{1,0:T(8,128)S(1)} %get-tuple-element.44), channel_id=1, source_target_pairs={{0,1},{1,0},{2,3},{3,2},{4,5},{5,4},{6,7},{7,6},{8,9},{9,8},{10,11... | collective-permute-start | bytes 589832 | tf_op jit(solution)/shard_map/ppermute | solution.py:246
  32.8 2.2 %collective-permute-start.14 = (f32[384,128]{1,0:T(8,128)S(1)}, f32[384,128]{1,0:T(8,128)S(1)}, u32[]{:S(2)}, u32[]{:S(2)}) collective-permute-start(f32[384,128]{1,0:T(8,128)S(1)} %get-tuple-element.42), channel_id=1, source_target_pairs={{0,1},{1,0},{2,3},{3,2},{4,5},{5,4},{6,7},{7,6},{8,9},{9,8},{10,11... | collective-permute-start | bytes 589832 | tf_op jit(solution)/shard_map/ppermute | solution.py:246
  33.7 2.1 %collective-permute-start.12 = (f32[384,128]{1,0:T(8,128)S(1)}, f32[384,128]{1,0:T(8,128)S(1)}, u32[]{:S(2)}, u32[]{:S(2)}) collective-permute-start(f32[384,128]{1,0:T(8,128)S(1)} %get-tuple-element.39), channel_id=1, source_target_pairs={{0,1},{1,0},{2,3},{3,2},{4,5},{5,4},{6,7},{7,6},{8,9},{9,8},{10,11... | collective-permute-start | bytes 589832 | tf_op jit(solution)/shard_map/ppermute | solution.py:246

commit v8 on v7

--- a/solution.py
+++ b/solution.py
@@ -10,7 +10,7 @@
 STEPS = 4
 PARTS = (3, 4, 4, 5)
 CHUNKS = len(PARTS)
-TILES = 6
+TILES = 2
 VMEM_BYTES = 16 * 1024 * 1024
 
 
@@ -89,11 +89,13 @@
 
 
 def first_kernel(*refs):
-    store, blocks, (held, send, own, arrived) = refs[0], refs[1:-4], refs[-4:]
+    store, valid, blocks, (held, keep, send, own, count, arrived) = refs[0], refs[1], refs[2:-6], refs[-6:]
     rows, depth = store.shape
     half, tile = rows // 2, rows // TILES
     cuts = cuts_of(depth)
     me = lax.axis_index("dim")
+    counted = pltpu.make_async_copy(valid, count, arrived.at[TILES])
+    counted.start()
     loads, outs = [], []
     for n in range(TILES):
         out, where = (send, 1 - me) if n < TILES // 2 else (own, me)
@@ -102,6 +104,9 @@
         loads.append(pltpu.make_async_copy(store.at[place], held.at[place], arrived.at[n]))
         loads[n].start()
         outs.append((out, within, place))
+    counted.wait()
+    row_ids = lax.broadcasted_iota(jnp.int32, keep.shape, 0) + me * half
+    keep[...] = (row_ids < count[0]).astype(jnp.float32)
     for n, (out, within, place) in enumerate(outs):
         loads[n].wait()
         total = None
@@ -111,18 +116,21 @@
         out[within] = total
 
 
-def first_scores(store, blocks):
+def first_scores(store, valid, blocks):
     (rows, depth), columns = store.shape, blocks[0].shape[0]
     shape = jax.ShapeDtypeStruct((rows // 2, columns), jnp.float32)
     return pl.pallas_call(
         first_kernel,
-        out_shape=[jax.ShapeDtypeStruct(store.shape, store.dtype), shape, shape],
-        in_specs=[far_spec()] + [whole_spec()] * len(blocks),
-        out_specs=[whole_spec()] * 3,
-        scratch_shapes=[pltpu.SemaphoreType.DMA((TILES,))],
+        out_shape=[jax.ShapeDtypeStruct(store.shape, store.dtype), shape, shape, shape],
+        in_specs=[far_spec()] * 2 + [whole_spec()] * len(blocks),
+        out_specs=[whole_spec()] * 4,
+        scratch_shapes=[
+            pltpu.SMEM((1,), jnp.int32),
+            pltpu.SemaphoreType.DMA((TILES + 1,)),
+        ],
         compiler_params=params(),
         cost_estimate=cost(2 * rows * columns * depth, 2 * (rows + columns) * depth),
-    )(in_hbm(store), *blocks)
+    )(in_hbm(store), valid, *blocks)
 
 
 def scores_kernel(pieces, fresh, *refs):
@@ -193,15 +201,14 @@
     return [(outs[2 * i], outs[2 * i + 1]) for i in range(len(carries))]
 
 
-def finish_kernel(places, valid, *refs):
+def finish_kernel(places, keep, *refs):
     out, summed, left = refs[-3:]
     half, columns = refs[0].shape
-    row_ids = lax.broadcasted_iota(jnp.int32, (half, columns), 0) + lax.axis_index("dim") * half
-    keep = row_ids < valid[0]
+    inside = keep[...] > 0.5
     stores = []
     for n, place in enumerate(places):
         cut = slice(n * columns, (n + 1) * columns)
-        summed[:, cut] = jnp.where(keep, refs[2 * n][...] + refs[2 * n + 1][...], 0.0)
+        summed[:, cut] = jnp.where(inside, refs[2 * n][...] + refs[2 * n + 1][...], 0.0)
         to = out.at[:, place * columns:(place + 1) * columns]
         stores.append(pltpu.make_async_copy(summed.at[:, cut], to, left.at[n]))
         stores[n].start()
@@ -209,15 +216,14 @@
         store.wait()
 
 
-def finish(valid, pairs, places, steps, out=None):
+def finish(keep, pairs, places, steps, out=None):
     half, columns = pairs[0][0].shape
     operands = [ref for pair in pairs for ref in pair]
     given = [] if out is None else [in_hbm(out)]
     return pl.pallas_call(
         functools.partial(finish_kernel, places),
         out_shape=pltpu.HBM((half, columns * steps), jnp.float32),
-        in_specs=[pl.BlockSpec(memory_space=pltpu.SMEM)]
-        + [whole_spec()] * len(operands)
+        in_specs=[whole_spec()] * (1 + len(operands))
         + [far_spec()] * len(given),
         out_specs=far_spec(),
         scratch_shapes=[
@@ -227,7 +233,7 @@
         input_output_aliases={1 + len(operands): 0} if given else {},
         compiler_params=params(),
         cost_estimate=cost(half * columns * len(pairs), 12 * half * columns * len(pairs)),
-    )(valid, *operands, *given)
+    )(keep, *operands, *given)
 
 
 def after(x, *earlier):
@@ -239,6 +245,7 @@
     odd = lax.rem(lax.axis_index("ex"), 2) == 1
     one_ahead = [(i, (i + 1) % size) for i in range(size)]
     ahead = [(i, (i + 2) % size) for i in range(size)]
+    even_ahead = ahead[::2]
     swap = [(i, i ^ 1) for i in range(size)]
     over_dim = [(0, 1), (1, 0)]
 
@@ -250,32 +257,39 @@
         return ours, send(theirs, over_dim, "dim")
 
     own = prepare(queries, precond[None, :], query_rank)
-    every, last = range(CHUNKS), CHUNKS - 1
-    two_back = [send(own[n], ahead) for n in every]
-    store, *own_total = first_scores(store, own)
+    two_back = [send(block, ahead) for block in own]
+    early = send(own[0], swap)
+    store, keep, *own_total = first_scores(store, valid_rows, own)
     own_pair = exchanged(own_total)
 
-    blocks = [after(two_back[0], own_total[0]), *two_back[1:]]
-    one_back = [send(jnp.where(odd, blocks[n], own[n]), swap) for n in every[:last]]
-    three_back = [send(one_back[n], ahead) for n in every[:last]]
-    direct = send(jnp.where(odd, two_back[last], own[last]), one_ahead)
-    swapped = send(two_back[last], swap)
+    scored = own_total[0]
+    swapped = [send(after(two_back[0], scored), swap)]
+    swapped += [send(jnp.where(odd, after(two_back[n], scored), own[n]), swap) for n in (1, 2)]
+    shifted = [send(swapped[0], even_ahead)] + [send(swapped[n], ahead) for n in (1, 2)]
+    direct = send(jnp.where(odd, two_back[3], own[3]), one_ahead)
+    swapped.append(send(two_back[3], swap))
 
     two, one = more_scores(
         store,
-        [(n, [(0, two_back[n]), (1, one_back[n])]) for n in every[:last]]
-        + [(last, [(0, two_back[last])])],
+        [
+            (0, [(0, two_back[0]), (1, swapped[0], early)]),
+            (1, [(0, two_back[1]), (1, swapped[1])]),
+            (2, [(0, two_back[2]), (1, swapped[2])]),
+            (3, [(0, two_back[3])]),
+        ],
         [None, None],
     )
     two_pair = exchanged(two)
     one, three = more_scores(
-        store, [(last, [(0, swapped, direct), (1, direct, swapped)])], [one, None]
+        store, [(3, [(0, swapped[3], direct), (1, direct, swapped[3])])], [one, None]
     )
     one_pair = exchanged(one)
-    out = finish(valid_rows, [own_pair, one_pair, two_pair], (0, 1, 2), STEPS)
-    [three] = more_scores(store, [(n, [(0, three_back[n])]) for n in every[:last - 1]], [three])
-    [three] = more_scores(store, [(last - 1, [(0, three_back[last - 1])])], [three])
-    return finish(valid_rows, [exchanged(three)], (3,), STEPS, out)
+    [three] = more_scores(
+        store, [(0, [(0, shifted[0], swapped[0])]), (1, [(0, shifted[1])])], [three]
+    )
+    out = finish(keep, [own_pair, one_pair, two_pair], (0, 1, 2), STEPS)
+    [three] = more_scores(store, [(2, [(0, shifted[2])])], [three])
+    return finish(keep, [exchanged(three)], (3,), STEPS, out)
 
 
 def solution(mesh):

time: 36.8 us -> 40.6 us (1.10)
  starting transfers between devices: 21.4 us -> 26.2 us
  waiting for transfers between devices: 5.48 us -> 4.84 us
    ppermute x16 -> x17, starting transfers between devices: 21.4 us -> 26.2 us  [send(): return lax.ppermute(block, axis, route)]
    ppermute x16 -> x17, waiting for transfers between devices: 5.48 us -> 4.84 us  [send(): return lax.ppermute(block, axis, route)]
  transfers between devices with their start and end apart: 16 -> 17, of which waited for: 4 -> 6; matrix products, arithmetic and copies ran while one was open for 0% -> 0% of each run, Pallas kernels for 17% -> 15%
where the time goes in v8:
time: 40.6 us; the launch traced here: 40.4 us
  starting transfers between devices  26.2 us (65%)
  Pallas kernels  8.55 us (21%)
  waiting for transfers between devices  4.84 us (12%)
  between operations  0.77 us (2%)
    ppermute x17, starting transfers between devices, send(): return lax.ppermute(block, axis, route)  26.2 us
    ppermute x17, waiting for transfers between devices, send(): return lax.ppermute(block, axis, route)  4.84 us
    pallas_call x1, Pallas kernels, first_scores(): pl.pallas_call(first_kernel, out_shape=[jax.ShapeDtypeStruct(store.shape,...  2.81 us
    pallas_call x4, Pallas kernels, more_scores(): pl.pallas_call(functools.partial(scores_kernel, tuple(placed), fresh), ou...  2.46 us
    pallas_call x1, Pallas kernels, prepare(): pl.pallas_call(prepare_kernel, out_shape=shapes, in_specs=[far_spec()] *...  1.71 us
    pallas_call x2, Pallas kernels, finish(): pl.pallas_call(functools.partial(finish_kernel, places), out_shape=pltpu....  1.58 us
  transfers between devices with their start and end apart: 17, of which 6 were waited for; matrix products, arithmetic and copies ran while one was open for 0% of the time, Pallas kernels for 15%

profile of v8, /device:TPU:0, one launch (start us, length us, event | category | flops | bytes accessed | tf_op | source)
XLA Modules:
  0.0 40.4 jit_solution(1567765380602843740)
XLA Ops:
  0.0 1.7 %shard_map.55 = (bf16[128,384]{1,0:T(8,128)(2,1)S(1)}, bf16[128,512]{1,0:T(8,128)(2,1)S(1)}, bf16[128,512]{1,0:T(8,128)(2,1)S(1)}, bf16[128,640]{1,0:T(8,128)(2,1)S(1)}) custom-call(bf16[128,2048]{1,0:T(8,128)(2,1)} %queries.1, f32[1,2048]{1,0:T(1,128)} %bitcast.1, s32[1,128]{1,0:T(1,128)} %rank.1), custom_call_target="tpu_custom_call" | custom-call | flops 67108864 | bytes 1048576 | tf_op jit(solution)/shard_map/pallas_call | solution.py:75
  1.7 3.1 %collective-permute-start.6 = (bf16[128,512]{1,0:T(8,128)(2,1)S(1)}, bf16[128,512]{1,0:T(8,128)(2,1)S(1)}, u32[]{:S(2)}, u32[]{:S(2)}) collective-permute-start(bf16[128,512]{1,0:T(8,128)(2,1)S(1)} %get-tuple-element.29.refs_3_), channel_id=1, source_target_pairs={{0,4},{2,6},{4,8},{6,10},{8,12},{10,14},{12,0},{14,2},{1,5},{3,7},... | collective-permute-start | bytes 393224 | tf_op jit(solution)/shard_map/ppermute | solution.py:253
  4.8 1.6 %collective-permute-start.3 = (bf16[128,384]{1,0:T(8,128)(2,1)S(1)}, bf16[128,384]{1,0:T(8,128)(2,1)S(1)}, u32[]{:S(2)}, u32[]{:S(2)}) collective-permute-start(bf16[128,384]{1,0:T(8,128)(2,1)S(1)} %get-tuple-element.28.refs_2_), channel_id=1, source_target_pairs={{0,4},{2,6},{4,8},{6,10},{8,12},{10,14},{12,0},{14,2},{1,5},{3,7},... | collective-permute-start | bytes 294920 | tf_op jit(solution)/shard_map/ppermute | solution.py:253
  6.4 1.5 %collective-permute-start.12 = (bf16[128,384]{1,0:T(8,128)(2,1)S(1)}, bf16[128,384]{1,0:T(8,128)(2,1)S(1)}, u32[]{:S(2)}, u32[]{:S(2)}) collective-permute-start(bf16[128,384]{1,0:T(8,128)(2,1)S(1)} %get-tuple-element.28.refs_2_), channel_id=1, source_target_pairs={{0,2},{2,0},{4,6},{6,4},{8,10},{10,8},{12,14},{14,12},{1,3},{3,1},... | collective-permute-start | bytes 294920 | tf_op jit(solution)/shard_map/ppermute | solution.py:253
  7.9 1.6 %collective-permute-start = (bf16[128,512]{1,0:T(8,128)(2,1)S(1)}, bf16[128,512]{1,0:T(8,128)(2,1)S(1)}, u32[]{:S(2)}, u32[]{:S(2)}) collective-permute-start(bf16[128,512]{1,0:T(8,128)(2,1)S(1)} %get-tuple-element.30.refs_4_), channel_id=1, source_target_pairs={{0,4},{2,6},{4,8},{6,10},{8,12},{10,14},{12,0},{14,2},{1,5},{3,7},... | collective-permute-start | bytes 393224 | tf_op jit(solution)/shard_map/ppermute | solution.py:253
  10.3 2.8 %shard_map.56 = (bf16[768,2048]{1,0:T(8,128)(2,1)S(1)}, f32[384,128]{1,0:T(8,128)S(1)}, f32[384,128]{1,0:T(8,128)S(1)}, f32[384,128]{1,0:T(8,128)S(1)}) custom-call(bf16[768,2048]{1,0:T(8,128)(2,1)} %refs_0_.1, s32[1]{0:T(128)S(6)} %copy.8.refs_1_, bf16[128,384]{1,0:T(8,128)(2,1)S(1)} %get-tuple-element.28.refs_2_, ...), custom_call_target="tpu_custom_call" | custom-call | flops 402653184 | bytes 3670016 | tf_op jit(solution)/shard_map/pallas_call | solution.py:122
  13.3 1.7 %collective-permute-start.4 = (bf16[128,384]{1,0:T(8,128)(2,1)S(1)}, bf16[128,384]{1,0:T(8,128)(2,1)S(1)}, u32[]{:S(2)}, u32[]{:S(2)}) collective-permute-start(bf16[128,384]{1,0:T(8,128)(2,1)S(1)} %collective-permute-done.3.refs_1_), channel_id=1, source_target_pairs={{0,2},{2,0},{4,6},{6,4},{8,10},{10,8},{12,14},{14,12},{1,3},{3,1},... | collective-permute-start | bytes 294920 | tf_op jit(solution)/shard_map/ppermute | solution.py:253
  15.0 0.4 collective-permute-start.7
  15.4 0.7 %collective-permute-done.refs_6_ = bf16[128,512]{1,0:T(8,128)(2,1)S(1)} collective-permute-done((bf16[128,512]{1,0:T(8,128)(2,1)S(1)}, bf16[128,512]{1,0:T(8,128)(2,1)S(1)}, u32[]{:S(2)}, u32[]{:S(2)}) %collective-permute-start) | collective-permute-done | bytes 131104 | tf_op jit(solution)/shard_map/ppermute | solution.py:253
  16.1 1.8 %collective-permute-start.1 = (bf16[128,512]{1,0:T(8,128)(2,1)S(1)}, bf16[128,512]{1,0:T(8,128)(2,1)S(1)}, u32[]{:S(2)}, u32[]{:S(2)}) collective-permute-start(bf16[128,512]{1,0:T(8,128)(2,1)S(1)} %broadcast_select_fusion.2), channel_id=1, source_target_pairs={{0,2},{2,0},{4,6},{6,4},{8,10},{10,8},{12,14},{14,12},{1,3},{3,1},... | collective-permute-start | bytes 393224 | tf_op jit(solution)/shard_map/ppermute | solution.py:253
  17.9 0.9 %collective-permute-done.9.refs_8_ = bf16[128,640]{1,0:T(8,128)(2,1)S(1)} collective-permute-done((bf16[128,640]{1,0:T(8,128)(2,1)S(1)}, bf16[128,640]{1,0:T(8,128)(2,1)S(1)}, u32[]{:S(2)}, u32[]{:S(2)}) %collective-permute-start.9) | collective-permute-done | bytes 163872 | tf_op jit(solution)/shard_map/ppermute | solution.py:253
  18.8 1.5 %collective-permute-start.11 = (bf16[128,640]{1,0:T(8,128)(2,1)S(1)}, bf16[128,640]{1,0:T(8,128)(2,1)S(1)}, u32[]{:S(2)}, u32[]{:S(2)}) collective-permute-start(bf16[128,640]{1,0:T(8,128)(2,1)S(1)} %broadcast_select_fusion), channel_id=1, source_target_pairs={{0,2},{2,4},{4,6},{6,8},{8,10},{10,12},{12,14},{14,0},{1,3},{3,5},... | collective-permute-start | bytes 491528 | tf_op jit(solution)/shard_map/ppermute | solution.py:253
  20.7 5.2 %collective-permute-start.8 = (bf16[128,512]{1,0:T(8,128)(2,1)S(1)}, bf16[128,512]{1,0:T(8,128)(2,1)S(1)}, u32[]{:S(2)}, u32[]{:S(2)}) collective-permute-start(bf16[128,512]{1,0:T(8,128)(2,1)S(1)} %collective-permute-done.7.refs_5_), channel_id=1, source_target_pairs={{0,4},{2,6},{4,8},{6,10},{8,12},{10,14},{12,0},{14,2},{1,5},{3,7},... | collective-permute-start | bytes 393224 | tf_op jit(solution)/shard_map/ppermute | solution.py:253
  25.9 2.9 %collective-permute-start.2 = (bf16[128,512]{1,0:T(8,128)(2,1)S(1)}, bf16[128,512]{1,0:T(8,128)(2,1)S(1)}, u32[]{:S(2)}, u32[]{:S(2)}) collective-permute-start(bf16[128,512]{1,0:T(8,128)(2,1)S(1)} %collective-permute-done.1.refs_7_), channel_id=1, source_target_pairs={{0,4},{2,6},{4,8},{6,10},{8,12},{10,14},{12,0},{14,2},{1,5},{3,7},... | collective-permute-start | bytes 393224 | tf_op jit(solution)/shard_map/ppermute | solution.py:253
  28.8 3.5 %collective-permute-start.5 = (bf16[128,384]{1,0:T(8,128)(2,1)S(1)}, bf16[128,384]{1,0:T(8,128)(2,1)S(1)}, u32[]{:S(2)}, u32[]{:S(2)}) collective-permute-start(bf16[128,384]{1,0:T(8,128)(2,1)S(1)} %collective-permute-done.4.refs_2_), channel_id=1, source_target_pairs={{0,4},{4,8},{8,12},{12,0},{1,5},{5,9},{9,13},{13,1},{16,20},{20,24... | collective-permute-start | bytes 294920 | tf_op jit(solution)/shard_map/ppermute | solution.py:253
  32.3 1.0 %shard_map.57 = (f32[384,128]{1,0:T(8,128)S(1)}, f32[384,128]{1,0:T(8,128)S(1)}, f32[384,128]{1,0:T(8,128)S(1)}, f32[384,128]{1,0:T(8,128)S(1)}) custom-call(bf16[768,2048]{1,0:T(8,128)(2,1)S(1)} %get-tuple-element.33.refs_0_, bf16[128,384]{1,0:T(8,128)(2,1)S(1)} %collective-permute-done.3.refs_1_, bf16[128,384]{1,0:T(8,128)(2,1)S(1)} %collective-permute-done.4.refs_2_, ...), custom_call_target="tpu_custom_call" | custom-call | flops 679477248 | bytes 3932160 | tf_op jit(solution)/shard_map/pallas_call | solution.py:193
  33.4 0.5 %collective-permute-start.16 = (f32[384,128]{1,0:T(8,128)S(1)}, f32[384,128]{1,0:T(8,128)S(1)}, u32[]{:S(2)}, u32[]{:S(2)}) collective-permute-start(f32[384,128]{1,0:T(8,128)S(1)} %get-tuple-element.50), channel_id=1, source_target_pairs={{0,1},{1,0},{2,3},{3,2},{4,5},{5,4},{6,7},{7,6},{8,9},{9,8},{10,11... | collective-permute-start | bytes 589832 | tf_op jit(solution)/shard_map/ppermute | solution.py:253
  33.9 0.5 %shard_map.58 = (f32[384,128]{1,0:T(8,128)S(1)}, f32[384,128]{1,0:T(8,128)S(1)}, f32[384,128]{1,0:T(8,128)S(1)}, f32[384,128]{1,0:T(8,128)S(1)}) custom-call(bf16[768,2048]{1,0:T(8,128)(2,1)S(1)} %get-tuple-element.33.refs_0_, bf16[128,640]{1,0:T(8,128)(2,1)S(1)} %collective-permute-done.10.refs_1_, bf16[128,640]{1,0:T(8,128)(2,1)S(1)} %collective-permute-done.11.refs_2_, ...), custom_call_target="tpu_custom_call" | custom-call | flops 251658240 | bytes 1769472 | tf_op jit(solution)/shard_map/pallas_call | solution.py:193
  34.4 2.7 %collective-permute-done.5.refs_1_ = bf16[128,384]{1,0:T(8,128)(2,1)S(1)} collective-permute-done((bf16[128,384]{1,0:T(8,128)(2,1)S(1)}, bf16[128,384]{1,0:T(8,128)(2,1)S(1)}, u32[]{:S(2)}, u32[]{:S(2)}) %collective-permute-start.5) | collective-permute-done | bytes 98336 | tf_op jit(solution)/shard_map/ppermute | solution.py:253
  37.1 0.5 %shard_map.59 = (f32[384,128]{1,0:T(8,128)S(1)}, f32[384,128]{1,0:T(8,128)S(1)}) custom-call(bf16[768,2048]{1,0:T(8,128)(2,1)S(1)} %get-tuple-element.33.refs_0_, bf16[128,384]{1,0:T(8,128)(2,1)S(1)} %collective-permute-done.5.refs_1_, bf16[128,384]{1,0:T(8,128)(2,1)S(1)} %collective-permute-done.4.refs_2_, ...), custom_call_target="tpu_custom_call" | custom-call | flops 176160768 | bytes 1769472 | tf_op jit(solution)/shard_map/pallas_call | solution.py:193
  37.7 0.4 shard_map.60
  38.0 0.6 %collective-permute-start.13 = (f32[384,128]{1,0:T(8,128)S(1)}, f32[384,128]{1,0:T(8,128)S(1)}, u32[]{:S(2)}, u32[]{:S(2)}) collective-permute-start(f32[384,128]{1,0:T(8,128)S(1)} %get-tuple-element.45), channel_id=1, source_target_pairs={{0,1},{1,0},{2,3},{3,2},{4,5},{5,4},{6,7},{7,6},{8,9},{9,8},{10,11... | collective-permute-start | bytes 589832 | tf_op jit(solution)/shard_map/ppermute | solution.py:253
  38.6 0.9 %shard_map.61.refs_2_ = f32[384,512]{1,0:T(8,128)} custom-call(f32[384,128]{1,0:T(8,128)S(1)} %get-tuple-element.32.keep, f32[384,128]{1,0:T(8,128)S(1)} %get-tuple-element.46.refs_0_, f32[384,128]{1,0:T(8,128)S(1)} %collective-permute-done.14.refs_1_, f32[384,128]{1,0:T(8,128)S(1)} %get-tuple-element.47.refs_2_, ...), custom_call_target="tpu_custom_call" | custom-call | flops 147456 | bytes 1769472 | tf_op jit(solution)/shard_map/pallas_call | solution.py:223
  39.7 0.7 %shard_map.62 = f32[384,512]{1,0:T(8,128)} custom-call(f32[384,128]{1,0:T(8,128)S(1)} %get-tuple-element.32.keep, f32[384,128]{1,0:T(8,128)S(1)} %get-tuple-element.44.refs_0_, f32[384,128]{1,0:T(8,128)S(1)} %collective-permute-done.13.refs_1_, f32[384,512]{1,0:T(8,128)} %shard_map.61.refs_2_), custom_call_target="tpu_custom_call", output_to_operand_aliasing={{}: (3, {})} | custom-call | flops 49152 | bytes 589824 | tf_op jit(solution)/shard_map/pallas_call | solution.py:223
  (21 shorter events, 1.1 us)
Async XLA Ops:
  1.7 13.3 %collective-permute-start.6 = (bf16[128,512]{1,0:T(8,128)(2,1)S(1)}, bf16[128,512]{1,0:T(8,128)(2,1)S(1)}, u32[]{:S(2)}, u32[]{:S(2)}) collective-permute-start(bf16[128,512]{1,0:T(8,128)(2,1)S(1)} %get-tuple-element.29.refs_3_), channel_id=1, source_target_pairs={{0,4},{2,6},{4,8},{6,10},{8,12},{10,14},{12,0},{14,2},{1,5},{3,7},... | collective-permute-start | bytes 393224 | tf_op jit(solution)/shard_map/ppermute | solution.py:253
  4.8 8.5 %collective-permute-start.3 = (bf16[128,384]{1,0:T(8,128)(2,1)S(1)}, bf16[128,384]{1,0:T(8,128)(2,1)S(1)}, u32[]{:S(2)}, u32[]{:S(2)}) collective-permute-start(bf16[128,384]{1,0:T(8,128)(2,1)S(1)} %get-tuple-element.28.refs_2_), channel_id=1, source_target_pairs={{0,4},{2,6},{4,8},{6,10},{8,12},{10,14},{12,0},{14,2},{1,5},{3,7},... | collective-permute-start | bytes 294920 | tf_op jit(solution)/shard_map/ppermute | solution.py:253
  6.4 13.9 %collective-permute-start.12 = (bf16[128,384]{1,0:T(8,128)(2,1)S(1)}, bf16[128,384]{1,0:T(8,128)(2,1)S(1)}, u32[]{:S(2)}, u32[]{:S(2)}) collective-permute-start(bf16[128,384]{1,0:T(8,128)(2,1)S(1)} %get-tuple-element.28.refs_2_), channel_id=1, source_target_pairs={{0,2},{2,0},{4,6},{6,4},{8,10},{10,8},{12,14},{14,12},{1,3},{3,1},... | collective-permute-start | bytes 294920 | tf_op jit(solution)/shard_map/ppermute | solution.py:253
  7.9 8.2 %collective-permute-start = (bf16[128,512]{1,0:T(8,128)(2,1)S(1)}, bf16[128,512]{1,0:T(8,128)(2,1)S(1)}, u32[]{:S(2)}, u32[]{:S(2)}) collective-permute-start(bf16[128,512]{1,0:T(8,128)(2,1)S(1)} %get-tuple-element.30.refs_4_), channel_id=1, source_target_pairs={{0,4},{2,6},{4,8},{6,10},{8,12},{10,14},{12,0},{14,2},{1,5},{3,7},... | collective-permute-start | bytes 393224 | tf_op jit(solution)/shard_map/ppermute | solution.py:253
  9.4 9.3 %collective-permute-start.9 = (bf16[128,640]{1,0:T(8,128)(2,1)S(1)}, bf16[128,640]{1,0:T(8,128)(2,1)S(1)}, u32[]{:S(2)}, u32[]{:S(2)}) collective-permute-start(bf16[128,640]{1,0:T(8,128)(2,1)S(1)} %get-tuple-element.31.refs_5_), channel_id=1, source_target_pairs={{0,4},{2,6},{4,8},{6,10},{8,12},{10,14},{12,0},{14,2},{1,5},{3,7},... | collective-permute-start | bytes 491528 | tf_op jit(solution)/shard_map/ppermute | solution.py:253
  13.3 15.5 %collective-permute-start.4 = (bf16[128,384]{1,0:T(8,128)(2,1)S(1)}, bf16[128,384]{1,0:T(8,128)(2,1)S(1)}, u32[]{:S(2)}, u32[]{:S(2)}) collective-permute-start(bf16[128,384]{1,0:T(8,128)(2,1)S(1)} %collective-permute-done.3.refs_1_), channel_id=1, source_target_pairs={{0,2},{2,0},{4,6},{6,4},{8,10},{10,8},{12,14},{14,12},{1,3},{3,1},... | collective-permute-start | bytes 294920 | tf_op jit(solution)/shard_map/ppermute | solution.py:253
  15.0 5.7 %collective-permute-start.7 = (bf16[128,512]{1,0:T(8,128)(2,1)S(1)}, bf16[128,512]{1,0:T(8,128)(2,1)S(1)}, u32[]{:S(2)}, u32[]{:S(2)}) collective-permute-start(bf16[128,512]{1,0:T(8,128)(2,1)S(1)} %broadcast_select_fusion.1), channel_id=1, source_target_pairs={{0,2},{2,0},{4,6},{6,4},{8,10},{10,8},{12,14},{14,12},{1,3},{3,1},... | collective-permute-start | bytes 393224 | tf_op jit(solution)/shard_map/ppermute | solution.py:253
  16.1 9.8 %collective-permute-start.1 = (bf16[128,512]{1,0:T(8,128)(2,1)S(1)}, bf16[128,512]{1,0:T(8,128)(2,1)S(1)}, u32[]{:S(2)}, u32[]{:S(2)}) collective-permute-start(bf16[128,512]{1,0:T(8,128)(2,1)S(1)} %broadcast_select_fusion.2), channel_id=1, source_target_pairs={{0,2},{2,0},{4,6},{6,4},{8,10},{10,8},{12,14},{14,12},{1,3},{3,1},... | collective-permute-start | bytes 393224 | tf_op jit(solution)/shard_map/ppermute | solution.py:253
  18.8 14.6 %collective-permute-start.11 = (bf16[128,640]{1,0:T(8,128)(2,1)S(1)}, bf16[128,640]{1,0:T(8,128)(2,1)S(1)}, u32[]{:S(2)}, u32[]{:S(2)}) collective-permute-start(bf16[128,640]{1,0:T(8,128)(2,1)S(1)} %broadcast_select_fusion), channel_id=1, source_target_pairs={{0,2},{2,4},{4,6},{6,8},{8,10},{10,12},{12,14},{14,0},{1,3},{3,5},... | collective-permute-start | bytes 491528 | tf_op jit(solution)/shard_map/ppermute | solution.py:253
  20.3 13.1 %collective-permute-start.10 = (bf16[128,640]{1,0:T(8,128)(2,1)S(1)}, bf16[128,640]{1,0:T(8,128)(2,1)S(1)}, u32[]{:S(2)}, u32[]{:S(2)}) collective-permute-start(bf16[128,640]{1,0:T(8,128)(2,1)S(1)} %collective-permute-done.9.refs_8_), channel_id=1, source_target_pairs={{0,2},{2,0},{4,6},{6,4},{8,10},{10,8},{12,14},{14,12},{1,3},{3,1},... | collective-permute-start | bytes 491528 | tf_op jit(solution)/shard_map/ppermute | solution.py:253
  20.7 16.4 %collective-permute-start.8 = (bf16[128,512]{1,0:T(8,128)(2,1)S(1)}, bf16[128,512]{1,0:T(8,128)(2,1)S(1)}, u32[]{:S(2)}, u32[]{:S(2)}) collective-permute-start(bf16[128,512]{1,0:T(8,128)(2,1)S(1)} %collective-permute-done.7.refs_5_), channel_id=1, source_target_pairs={{0,4},{2,6},{4,8},{6,10},{8,12},{10,14},{12,0},{14,2},{1,5},{3,7},... | collective-permute-start | bytes 393224 | tf_op jit(solution)/shard_map/ppermute | solution.py:253
  25.9 11.8 %collective-permute-start.2 = (bf16[128,512]{1,0:T(8,128)(2,1)S(1)}, bf16[128,512]{1,0:T(8,128)(2,1)S(1)}, u32[]{:S(2)}, u32[]{:S(2)}) collective-permute-start(bf16[128,512]{1,0:T(8,128)(2,1)S(1)} %collective-permute-done.1.refs_7_), channel_id=1, source_target_pairs={{0,4},{2,6},{4,8},{6,10},{8,12},{10,14},{12,0},{14,2},{1,5},{3,7},... | collective-permute-start | bytes 393224 | tf_op jit(solution)/shard_map/ppermute | solution.py:253
  28.8 8.3 %collective-permute-start.5 = (bf16[128,384]{1,0:T(8,128)(2,1)S(1)}, bf16[128,384]{1,0:T(8,128)(2,1)S(1)}, u32[]{:S(2)}, u32[]{:S(2)}) collective-permute-start(bf16[128,384]{1,0:T(8,128)(2,1)S(1)} %collective-permute-done.4.refs_2_), channel_id=1, source_target_pairs={{0,4},{4,8},{8,12},{12,0},{1,5},{5,9},{9,13},{13,1},{16,20},{20,24... | collective-permute-start | bytes 294920 | tf_op jit(solution)/shard_map/ppermute | solution.py:253
  33.4 5.3 %collective-permute-start.14 = (f32[384,128]{1,0:T(8,128)S(1)}, f32[384,128]{1,0:T(8,128)S(1)}, u32[]{:S(2)}, u32[]{:S(2)}) collective-permute-start(f32[384,128]{1,0:T(8,128)S(1)} %get-tuple-element.34), channel_id=1, source_target_pairs={{0,1},{1,0},{2,3},{3,2},{4,5},{5,4},{6,7},{7,6},{8,9},{9,8},{10,11... | collective-permute-start | bytes 589832 | tf_op jit(solution)/shard_map/ppermute | solution.py:253
  33.4 5.2 %collective-permute-start.16 = (f32[384,128]{1,0:T(8,128)S(1)}, f32[384,128]{1,0:T(8,128)S(1)}, u32[]{:S(2)}, u32[]{:S(2)}) collective-permute-start(f32[384,128]{1,0:T(8,128)S(1)} %get-tuple-element.50), channel_id=1, source_target_pairs={{0,1},{1,0},{2,3},{3,2},{4,5},{5,4},{6,7},{7,6},{8,9},{9,8},{10,11... | collective-permute-start | bytes 589832 | tf_op jit(solution)/shard_map/ppermute | solution.py:253
  37.1 1.5 %collective-permute-start.15 = (f32[384,128]{1,0:T(8,128)S(1)}, f32[384,128]{1,0:T(8,128)S(1)}, u32[]{:S(2)}, u32[]{:S(2)}) collective-permute-start(f32[384,128]{1,0:T(8,128)S(1)} %get-tuple-element.48), channel_id=1, source_target_pairs={{0,1},{1,0},{2,3},{3,2},{4,5},{5,4},{6,7},{7,6},{8,9},{9,8},{10,11... | collective-permute-start | bytes 589832 | tf_op jit(solution)/shard_map/ppermute | solution.py:253
  38.0 1.6 %collective-permute-start.13 = (f32[384,128]{1,0:T(8,128)S(1)}, f32[384,128]{1,0:T(8,128)S(1)}, u32[]{:S(2)}, u32[]{:S(2)}) collective-permute-start(f32[384,128]{1,0:T(8,128)S(1)} %get-tuple-element.45), channel_id=1, source_target_pairs={{0,1},{1,0},{2,3},{3,2},{4,5},{5,4},{6,7},{7,6},{8,9},{9,8},{10,11... | collective-permute-start | bytes 589832 | tf_op jit(solution)/shard_map/ppermute | solution.py:253

commit v9 on v8

--- a/solution.py
+++ b/solution.py
@@ -266,8 +266,8 @@
     swapped = [send(after(two_back[0], scored), swap)]
     swapped += [send(jnp.where(odd, after(two_back[n], scored), own[n]), swap) for n in (1, 2)]
     shifted = [send(swapped[0], even_ahead)] + [send(swapped[n], ahead) for n in (1, 2)]
-    direct = send(jnp.where(odd, two_back[3], own[3]), one_ahead)
-    swapped.append(send(two_back[3], swap))
+    direct = send(after(jnp.where(odd, two_back[3], own[3]), shifted[0]), one_ahead)
+    swapped.append(send(after(two_back[3], shifted[0]), swap))
 
     two, one = more_scores(
         store,
@@ -280,13 +280,12 @@
         [None, None],
     )
     two_pair = exchanged(two)
+    [three] = more_scores(store, [(1, [(0, shifted[1])])], [None])
+    [three] = more_scores(store, [(0, [(0, shifted[0], swapped[0])])], [three])
     one, three = more_scores(
-        store, [(3, [(0, swapped[3], direct), (1, direct, swapped[3])])], [one, None]
+        store, [(3, [(0, swapped[3], direct), (1, direct, swapped[3])])], [one, three]
     )
     one_pair = exchanged(one)
-    [three] = more_scores(
-        store, [(0, [(0, shifted[0], swapped[0])]), (1, [(0, shifted[1])])], [three]
-    )
     out = finish(keep, [own_pair, one_pair, two_pair], (0, 1, 2), STEPS)
     [three] = more_scores(store, [(2, [(0, shifted[2])])], [three])
     return finish(keep, [exchanged(three)], (3,), STEPS, out)

time: 40.6 us -> 42.1 us (1.037)
  waiting for transfers between devices: 4.84 us -> 16 us
  starting transfers between devices: 26.2 us -> 16.3 us
    ppermute x17, waiting for transfers between devices: 4.84 us -> 16 us  [send(): return lax.ppermute(block, axis, route)]
    ppermute x17, starting transfers between devices: 26.2 us -> 16.3 us  [send(): return lax.ppermute(block, axis, route)]
    pallas_call x4 -> x5, Pallas kernels: 2.46 us -> 2.62 us  [more_scores(): pl.pallas_call(functools.partial(scores_kernel, tuple(placed), fresh), ou...]
  transfers between devices with their start and end apart: 17 -> 17, of which waited for: 6 -> 5; matrix products, arithmetic and copies ran while one was open for 0% -> 0% of each run, Pallas kernels for 15% -> 15%
where the time goes in v9:
time: 42.1 us; the launch traced here: 41.9 us
  starting transfers between devices  16.3 us (39%)
  waiting for transfers between devices  16 us (38%)
  Pallas kernels  8.72 us (21%)
  between operations  0.81 us (2%)
    ppermute x17, starting transfers between devices, send(): return lax.ppermute(block, axis, route)  16.3 us
    ppermute x17, waiting for transfers between devices, send(): return lax.ppermute(block, axis, route)  16 us
    pallas_call x1, Pallas kernels, first_scores(): pl.pallas_call(first_kernel, out_shape=[jax.ShapeDtypeStruct(store.shape,...  2.81 us
    pallas_call x5, Pallas kernels, more_scores(): pl.pallas_call(functools.partial(scores_kernel, tuple(placed), fresh), ou...  2.62 us
    pallas_call x1, Pallas kernels, prepare(): pl.pallas_call(prepare_kernel, out_shape=shapes, in_specs=[far_spec()] *...  1.71 us
    pallas_call x2, Pallas kernels, finish(): pl.pallas_call(functools.partial(finish_kernel, places), out_shape=pltpu....  1.58 us
  transfers between devices with their start and end apart: 17, of which 5 were waited for; matrix products, arithmetic and copies ran while one was open for 0% of the time, Pallas kernels for 15%

profile of v9, /device:TPU:0, one launch (start us, length us, event | category | flops | bytes accessed | tf_op | source)
XLA Modules:
  0.0 41.9 jit_solution(1952226643069239230)
XLA Ops:
  0.0 1.7 %shard_map.55 = (bf16[128,384]{1,0:T(8,128)(2,1)S(1)}, bf16[128,512]{1,0:T(8,128)(2,1)S(1)}, bf16[128,512]{1,0:T(8,128)(2,1)S(1)}, bf16[128,640]{1,0:T(8,128)(2,1)S(1)}) custom-call(bf16[128,2048]{1,0:T(8,128)(2,1)} %queries.1, f32[1,2048]{1,0:T(1,128)} %bitcast.1, s32[1,128]{1,0:T(1,128)} %rank.1), custom_call_target="tpu_custom_call" | custom-call | flops 67108864 | bytes 1048576 | tf_op jit(solution)/shard_map/pallas_call | solution.py:75
  1.7 3.1 %collective-permute-start = (bf16[128,512]{1,0:T(8,128)(2,1)S(1)}, bf16[128,512]{1,0:T(8,128)(2,1)S(1)}, u32[]{:S(2)}, u32[]{:S(2)}) collective-permute-start(bf16[128,512]{1,0:T(8,128)(2,1)S(1)} %get-tuple-element.34.refs_4_), channel_id=1, source_target_pairs={{0,4},{2,6},{4,8},{6,10},{8,12},{10,14},{12,0},{14,2},{1,5},{3,7},... | collective-permute-start | bytes 393224 | tf_op jit(solution)/shard_map/ppermute | solution.py:253
  4.8 1.6 %collective-permute-start.4 = (bf16[128,384]{1,0:T(8,128)(2,1)S(1)}, bf16[128,384]{1,0:T(8,128)(2,1)S(1)}, u32[]{:S(2)}, u32[]{:S(2)}) collective-permute-start(bf16[128,384]{1,0:T(8,128)(2,1)S(1)} %get-tuple-element.32.refs_2_), channel_id=1, source_target_pairs={{0,4},{2,6},{4,8},{6,10},{8,12},{10,14},{12,0},{14,2},{1,5},{3,7},... | collective-permute-start | bytes 294920 | tf_op jit(solution)/shard_map/ppermute | solution.py:253
  6.4 1.5 %collective-permute-start.9 = (bf16[128,384]{1,0:T(8,128)(2,1)S(1)}, bf16[128,384]{1,0:T(8,128)(2,1)S(1)}, u32[]{:S(2)}, u32[]{:S(2)}) collective-permute-start(bf16[128,384]{1,0:T(8,128)(2,1)S(1)} %get-tuple-element.32.refs_2_), channel_id=1, source_target_pairs={{0,2},{2,0},{4,6},{6,4},{8,10},{10,8},{12,14},{14,12},{1,3},{3,1},... | collective-permute-start | bytes 294920 | tf_op jit(solution)/shard_map/ppermute | solution.py:253
  7.9 1.6 %collective-permute-start.3 = (bf16[128,640]{1,0:T(8,128)(2,1)S(1)}, bf16[128,640]{1,0:T(8,128)(2,1)S(1)}, u32[]{:S(2)}, u32[]{:S(2)}) collective-permute-start(bf16[128,640]{1,0:T(8,128)(2,1)S(1)} %get-tuple-element.35.refs_5_), channel_id=1, source_target_pairs={{0,4},{2,6},{4,8},{6,10},{8,12},{10,14},{12,0},{14,2},{1,5},{3,7},... | collective-permute-start | bytes 491528 | tf_op jit(solution)/shard_map/ppermute | solution.py:253
  9.4 0.2 collective-permute-start.10
  10.3 2.8 %shard_map.56 = (bf16[768,2048]{1,0:T(8,128)(2,1)S(1)}, f32[384,128]{1,0:T(8,128)S(1)}, f32[384,128]{1,0:T(8,128)S(1)}, f32[384,128]{1,0:T(8,128)S(1)}) custom-call(bf16[768,2048]{1,0:T(8,128)(2,1)} %refs_0_.1, s32[1]{0:T(128)S(6)} %copy.8.refs_1_, bf16[128,384]{1,0:T(8,128)(2,1)S(1)} %get-tuple-element.32.refs_2_, ...), custom_call_target="tpu_custom_call" | custom-call | flops 402653184 | bytes 3670016 | tf_op jit(solution)/shard_map/pallas_call | solution.py:122
  13.3 1.7 %collective-permute-start.5 = (bf16[128,384]{1,0:T(8,128)(2,1)S(1)}, bf16[128,384]{1,0:T(8,128)(2,1)S(1)}, u32[]{:S(2)}, u32[]{:S(2)}) collective-permute-start(bf16[128,384]{1,0:T(8,128)(2,1)S(1)} %collective-permute-done.4.refs_1_), channel_id=1, source_target_pairs={{0,2},{2,0},{4,6},{6,4},{8,10},{10,8},{12,14},{14,12},{1,3},{3,1},... | collective-permute-start | bytes 294920 | tf_op jit(solution)/shard_map/ppermute | solution.py:253
  15.0 0.4 collective-permute-start.1
  15.4 3.4 %collective-permute-done.10.refs_4_ = bf16[128,512]{1,0:T(8,128)(2,1)S(1)} collective-permute-done((bf16[128,512]{1,0:T(8,128)(2,1)S(1)}, bf16[128,512]{1,0:T(8,128)(2,1)S(1)}, u32[]{:S(2)}, u32[]{:S(2)}) %collective-permute-start.10) | collective-permute-done | bytes 131104 | tf_op jit(solution)/shard_map/ppermute | solution.py:253
  18.8 1.6 %collective-permute-start.11 = (bf16[128,512]{1,0:T(8,128)(2,1)S(1)}, bf16[128,512]{1,0:T(8,128)(2,1)S(1)}, u32[]{:S(2)}, u32[]{:S(2)}) collective-permute-start(bf16[128,512]{1,0:T(8,128)(2,1)S(1)} %broadcast_select_fusion.1), channel_id=1, source_target_pairs={{0,2},{2,0},{4,6},{6,4},{8,10},{10,8},{12,14},{14,12},{1,3},{3,1},... | collective-permute-start | bytes 393224 | tf_op jit(solution)/shard_map/ppermute | solution.py:253
  20.3 1.9 %collective-permute-start.6 = (bf16[128,384]{1,0:T(8,128)(2,1)S(1)}, bf16[128,384]{1,0:T(8,128)(2,1)S(1)}, u32[]{:S(2)}, u32[]{:S(2)}) collective-permute-start(bf16[128,384]{1,0:T(8,128)(2,1)S(1)} %collective-permute-done.5.refs_2_), channel_id=1, source_target_pairs={{0,4},{4,8},{8,12},{12,0},{1,5},{5,9},{9,13},{13,1},{16,20},{20,24... | collective-permute-start | bytes 294920 | tf_op jit(solution)/shard_map/ppermute | solution.py:253
  22.3 6.3 %collective-permute-done.6.refs_1_ = bf16[128,384]{1,0:T(8,128)(2,1)S(1)} collective-permute-done((bf16[128,384]{1,0:T(8,128)(2,1)S(1)}, bf16[128,384]{1,0:T(8,128)(2,1)S(1)}, u32[]{:S(2)}, u32[]{:S(2)}) %collective-permute-start.6) | collective-permute-done | bytes 98336 | tf_op jit(solution)/shard_map/ppermute | solution.py:253
  28.6 2.0 %collective-permute-start.8 = (bf16[128,640]{1,0:T(8,128)(2,1)S(1)}, bf16[128,640]{1,0:T(8,128)(2,1)S(1)}, u32[]{:S(2)}, u32[]{:S(2)}) collective-permute-start(bf16[128,640]{1,0:T(8,128)(2,1)S(1)} %broadcast_select_fusion), channel_id=1, source_target_pairs={{0,2},{2,4},{4,6},{6,8},{8,10},{10,12},{12,14},{14,0},{1,3},{3,5},... | collective-permute-start | bytes 491528 | tf_op jit(solution)/shard_map/ppermute | solution.py:253
  30.8 1.1 %shard_map.57 = (f32[384,128]{1,0:T(8,128)S(1)}, f32[384,128]{1,0:T(8,128)S(1)}, f32[384,128]{1,0:T(8,128)S(1)}, f32[384,128]{1,0:T(8,128)S(1)}) custom-call(bf16[768,2048]{1,0:T(8,128)(2,1)S(1)} %get-tuple-element.37.refs_0_, bf16[128,384]{1,0:T(8,128)(2,1)S(1)} %collective-permute-done.4.refs_1_, bf16[128,384]{1,0:T(8,128)(2,1)S(1)} %collective-permute-done.5.refs_2_, ...), custom_call_target="tpu_custom_call" | custom-call | flops 679477248 | bytes 3932160 | tf_op jit(solution)/shard_map/pallas_call | solution.py:193
  31.9 5.5 %collective-permute-done.12.refs_1_ = bf16[128,512]{1,0:T(8,128)(2,1)S(1)} collective-permute-done((bf16[128,512]{1,0:T(8,128)(2,1)S(1)}, bf16[128,512]{1,0:T(8,128)(2,1)S(1)}, u32[]{:S(2)}, u32[]{:S(2)}) %collective-permute-start.12) | collective-permute-done | bytes 131104 | tf_op jit(solution)/shard_map/ppermute | solution.py:253
  37.4 0.4 shard_map.58
  37.8 0.3 shard_map.59
  38.1 0.5 %shard_map.60 = (f32[384,128]{1,0:T(8,128)S(1)}, f32[384,128]{1,0:T(8,128)S(1)}, f32[384,128]{1,0:T(8,128)S(1)}, f32[384,128]{1,0:T(8,128)S(1)}) custom-call(bf16[768,2048]{1,0:T(8,128)(2,1)S(1)} %get-tuple-element.37.refs_0_, bf16[128,640]{1,0:T(8,128)(2,1)S(1)} %collective-permute-done.7.refs_1_, bf16[128,640]{1,0:T(8,128)(2,1)S(1)} %collective-permute-done.8.refs_2_, ...), custom_call_target="tpu_custom_call" | custom-call | flops 251658240 | bytes 1769472 | tf_op jit(solution)/shard_map/pallas_call | solution.py:193
  38.7 0.6 %collective-permute-start.15 = (f32[384,128]{1,0:T(8,128)S(1)}, f32[384,128]{1,0:T(8,128)S(1)}, u32[]{:S(2)}, u32[]{:S(2)}) collective-permute-start(f32[384,128]{1,0:T(8,128)S(1)} %get-tuple-element.56), channel_id=1, source_target_pairs={{0,1},{1,0},{2,3},{3,2},{4,5},{5,4},{6,7},{7,6},{8,9},{9,8},{10,11... | collective-permute-start | bytes 589832 | tf_op jit(solution)/shard_map/ppermute | solution.py:253
  39.3 0.4 shard_map.61
  39.7 0.6 %collective-permute-done.15.refs_3_ = f32[384,128]{1,0:T(8,128)S(1)} collective-permute-done((f32[384,128]{1,0:T(8,128)S(1)}, f32[384,128]{1,0:T(8,128)S(1)}, u32[]{:S(2)}, u32[]{:S(2)}) %collective-permute-start.15) | collective-permute-done | bytes 196640 | tf_op jit(solution)/shard_map/ppermute | solution.py:253
  40.3 0.9 %shard_map.62.refs_2_ = f32[384,512]{1,0:T(8,128)} custom-call(f32[384,128]{1,0:T(8,128)S(1)} %get-tuple-element.36.keep, f32[384,128]{1,0:T(8,128)S(1)} %get-tuple-element.54.refs_0_, f32[384,128]{1,0:T(8,128)S(1)} %collective-permute-done.14.refs_1_, f32[384,128]{1,0:T(8,128)S(1)} %get-tuple-element.55.refs_2_, ...), custom_call_target="tpu_custom_call" | custom-call | flops 147456 | bytes 1769472 | tf_op jit(solution)/shard_map/pallas_call | solution.py:223
  41.2 0.7 %shard_map.63 = f32[384,512]{1,0:T(8,128)} custom-call(f32[384,128]{1,0:T(8,128)S(1)} %get-tuple-element.36.keep, f32[384,128]{1,0:T(8,128)S(1)} %get-tuple-element.52.refs_0_, f32[384,128]{1,0:T(8,128)S(1)} %collective-permute-done.13.refs_1_, f32[384,512]{1,0:T(8,128)} %shard_map.62.refs_2_), custom_call_target="tpu_custom_call", output_to_operand_aliasing={{}: (3, {})} | custom-call | flops 49152 | bytes 589824 | tf_op jit(solution)/shard_map/pallas_call | solution.py:223
  (22 shorter events, 0.4 us)
Async XLA Ops:
  1.7 13.3 %collective-permute-start = (bf16[128,512]{1,0:T(8,128)(2,1)S(1)}, bf16[128,512]{1,0:T(8,128)(2,1)S(1)}, u32[]{:S(2)}, u32[]{:S(2)}) collective-permute-start(bf16[128,512]{1,0:T(8,128)(2,1)S(1)} %get-tuple-element.34.refs_4_), channel_id=1, source_target_pairs={{0,4},{2,6},{4,8},{6,10},{8,12},{10,14},{12,0},{14,2},{1,5},{3,7},... | collective-permute-start | bytes 393224 | tf_op jit(solution)/shard_map/ppermute | solution.py:253
  4.8 8.5 %collective-permute-start.4 = (bf16[128,384]{1,0:T(8,128)(2,1)S(1)}, bf16[128,384]{1,0:T(8,128)(2,1)S(1)}, u32[]{:S(2)}, u32[]{:S(2)}) collective-permute-start(bf16[128,384]{1,0:T(8,128)(2,1)S(1)} %get-tuple-element.32.refs_2_), channel_id=1, source_target_pairs={{0,4},{2,6},{4,8},{6,10},{8,12},{10,14},{12,0},{14,2},{1,5},{3,7},... | collective-permute-start | bytes 294920 | tf_op jit(solution)/shard_map/ppermute | solution.py:253
  6.4 24.4 %collective-permute-start.9 = (bf16[128,384]{1,0:T(8,128)(2,1)S(1)}, bf16[128,384]{1,0:T(8,128)(2,1)S(1)}, u32[]{:S(2)}, u32[]{:S(2)}) collective-permute-start(bf16[128,384]{1,0:T(8,128)(2,1)S(1)} %get-tuple-element.32.refs_2_), channel_id=1, source_target_pairs={{0,2},{2,0},{4,6},{6,4},{8,10},{10,8},{12,14},{14,12},{1,3},{3,1},... | collective-permute-start | bytes 294920 | tf_op jit(solution)/shard_map/ppermute | solution.py:253
  7.9 14.4 %collective-permute-start.3 = (bf16[128,640]{1,0:T(8,128)(2,1)S(1)}, bf16[128,640]{1,0:T(8,128)(2,1)S(1)}, u32[]{:S(2)}, u32[]{:S(2)}) collective-permute-start(bf16[128,640]{1,0:T(8,128)(2,1)S(1)} %get-tuple-element.35.refs_5_), channel_id=1, source_target_pairs={{0,4},{2,6},{4,8},{6,10},{8,12},{10,14},{12,0},{14,2},{1,5},{3,7},... | collective-permute-start | bytes 491528 | tf_op jit(solution)/shard_map/ppermute | solution.py:253
  9.4 9.3 %collective-permute-start.10 = (bf16[128,512]{1,0:T(8,128)(2,1)S(1)}, bf16[128,512]{1,0:T(8,128)(2,1)S(1)}, u32[]{:S(2)}, u32[]{:S(2)}) collective-permute-start(bf16[128,512]{1,0:T(8,128)(2,1)S(1)} %get-tuple-element.33.refs_3_), channel_id=1, source_target_pairs={{0,4},{2,6},{4,8},{6,10},{8,12},{10,14},{12,0},{14,2},{1,5},{3,7},... | collective-permute-start | bytes 393224 | tf_op jit(solution)/shard_map/ppermute | solution.py:253
  13.3 7.1 %collective-permute-start.5 = (bf16[128,384]{1,0:T(8,128)(2,1)S(1)}, bf16[128,384]{1,0:T(8,128)(2,1)S(1)}, u32[]{:S(2)}, u32[]{:S(2)}) collective-permute-start(bf16[128,384]{1,0:T(8,128)(2,1)S(1)} %collective-permute-done.4.refs_1_), channel_id=1, source_target_pairs={{0,2},{2,0},{4,6},{6,4},{8,10},{10,8},{12,14},{14,12},{1,3},{3,1},... | collective-permute-start | bytes 294920 | tf_op jit(solution)/shard_map/ppermute | solution.py:253
  15.0 15.6 %collective-permute-start.1 = (bf16[128,512]{1,0:T(8,128)(2,1)S(1)}, bf16[128,512]{1,0:T(8,128)(2,1)S(1)}, u32[]{:S(2)}, u32[]{:S(2)}) collective-permute-start(bf16[128,512]{1,0:T(8,128)(2,1)S(1)} %broadcast_select_fusion.2), channel_id=1, source_target_pairs={{0,2},{2,0},{4,6},{6,4},{8,10},{10,8},{12,14},{14,12},{1,3},{3,1},... | collective-permute-start | bytes 393224 | tf_op jit(solution)/shard_map/ppermute | solution.py:253
  18.8 11.9 %collective-permute-start.11 = (bf16[128,512]{1,0:T(8,128)(2,1)S(1)}, bf16[128,512]{1,0:T(8,128)(2,1)S(1)}, u32[]{:S(2)}, u32[]{:S(2)}) collective-permute-start(bf16[128,512]{1,0:T(8,128)(2,1)S(1)} %broadcast_select_fusion.1), channel_id=1, source_target_pairs={{0,2},{2,0},{4,6},{6,4},{8,10},{10,8},{12,14},{14,12},{1,3},{3,1},... | collective-permute-start | bytes 393224 | tf_op jit(solution)/shard_map/ppermute | solution.py:253
  20.3 8.3 %collective-permute-start.6 = (bf16[128,384]{1,0:T(8,128)(2,1)S(1)}, bf16[128,384]{1,0:T(8,128)(2,1)S(1)}, u32[]{:S(2)}, u32[]{:S(2)}) collective-permute-start(bf16[128,384]{1,0:T(8,128)(2,1)S(1)} %collective-permute-done.5.refs_2_), channel_id=1, source_target_pairs={{0,4},{4,8},{8,12},{12,0},{1,5},{5,9},{9,13},{13,1},{16,20},{20,24... | collective-permute-start | bytes 294920 | tf_op jit(solution)/shard_map/ppermute | solution.py:253
  28.6 9.5 %collective-permute-start.7 = (bf16[128,640]{1,0:T(8,128)(2,1)S(1)}, bf16[128,640]{1,0:T(8,128)(2,1)S(1)}, u32[]{:S(2)}, u32[]{:S(2)}) collective-permute-start(bf16[128,640]{1,0:T(8,128)(2,1)S(1)} %collective-permute-done.3.refs_8_), channel_id=1, source_target_pairs={{0,2},{2,0},{4,6},{6,4},{8,10},{10,8},{12,14},{14,12},{1,3},{3,1},... | collective-permute-start | bytes 491528 | tf_op jit(solution)/shard_map/ppermute | solution.py:253
  28.6 9.5 %collective-permute-start.8 = (bf16[128,640]{1,0:T(8,128)(2,1)S(1)}, bf16[128,640]{1,0:T(8,128)(2,1)S(1)}, u32[]{:S(2)}, u32[]{:S(2)}) collective-permute-start(bf16[128,640]{1,0:T(8,128)(2,1)S(1)} %broadcast_select_fusion), channel_id=1, source_target_pairs={{0,2},{2,4},{4,6},{6,8},{8,10},{10,12},{12,14},{14,0},{1,3},{3,5},... | collective-permute-start | bytes 491528 | tf_op jit(solution)/shard_map/ppermute | solution.py:253
  30.7 6.8 %collective-permute-start.12 = (bf16[128,512]{1,0:T(8,128)(2,1)S(1)}, bf16[128,512]{1,0:T(8,128)(2,1)S(1)}, u32[]{:S(2)}, u32[]{:S(2)}) collective-permute-start(bf16[128,512]{1,0:T(8,128)(2,1)S(1)} %collective-permute-done.11.refs_5_), channel_id=1, source_target_pairs={{0,4},{2,6},{4,8},{6,10},{8,12},{10,14},{12,0},{14,2},{1,5},{3,7},... | collective-permute-start | bytes 393224 | tf_op jit(solution)/shard_map/ppermute | solution.py:253
  30.7 8.6 %collective-permute-start.2 = (bf16[128,512]{1,0:T(8,128)(2,1)S(1)}, bf16[128,512]{1,0:T(8,128)(2,1)S(1)}, u32[]{:S(2)}, u32[]{:S(2)}) collective-permute-start(bf16[128,512]{1,0:T(8,128)(2,1)S(1)} %collective-permute-done.1.refs_7_), channel_id=1, source_target_pairs={{0,4},{2,6},{4,8},{6,10},{8,12},{10,14},{12,0},{14,2},{1,5},{3,7},... | collective-permute-start | bytes 393224 | tf_op jit(solution)/shard_map/ppermute | solution.py:253
  30.7 9.0 %collective-permute-start.14 = (f32[384,128]{1,0:T(8,128)S(1)}, f32[384,128]{1,0:T(8,128)S(1)}, u32[]{:S(2)}, u32[]{:S(2)}) collective-permute-start(f32[384,128]{1,0:T(8,128)S(1)} %get-tuple-element.38), channel_id=1, source_target_pairs={{0,1},{1,0},{2,3},{3,2},{4,5},{5,4},{6,7},{7,6},{8,9},{9,8},{10,11... | collective-permute-start | bytes 589832 | tf_op jit(solution)/shard_map/ppermute | solution.py:253
  37.4 2.3 %collective-permute-start.16 = (f32[384,128]{1,0:T(8,128)S(1)}, f32[384,128]{1,0:T(8,128)S(1)}, u32[]{:S(2)}, u32[]{:S(2)}) collective-permute-start(f32[384,128]{1,0:T(8,128)S(1)} %get-tuple-element.58), channel_id=1, source_target_pairs={{0,1},{1,0},{2,3},{3,2},{4,5},{5,4},{6,7},{7,6},{8,9},{9,8},{10,11... | collective-permute-start | bytes 589832 | tf_op jit(solution)/shard_map/ppermute | solution.py:253
  38.7 1.6 %collective-permute-start.15 = (f32[384,128]{1,0:T(8,128)S(1)}, f32[384,128]{1,0:T(8,128)S(1)}, u32[]{:S(2)}, u32[]{:S(2)}) collective-permute-start(f32[384,128]{1,0:T(8,128)S(1)} %get-tuple-element.56), channel_id=1, source_target_pairs={{0,1},{1,0},{2,3},{3,2},{4,5},{5,4},{6,7},{7,6},{8,9},{9,8},{10,11... | collective-permute-start | bytes 589832 | tf_op jit(solution)/shard_map/ppermute | solution.py:253
  39.6 1.6 %collective-permute-start.13 = (f32[384,128]{1,0:T(8,128)S(1)}, f32[384,128]{1,0:T(8,128)S(1)}, u32[]{:S(2)}, u32[]{:S(2)}) collective-permute-start(f32[384,128]{1,0:T(8,128)S(1)} %get-tuple-element.53), channel_id=1, source_target_pairs={{0,1},{1,0},{2,3},{3,2},{4,5},{5,4},{6,7},{7,6},{8,9},{9,8},{10,11... | collective-permute-start | bytes 589832 | tf_op jit(solution)/shard_map/ppermute | solution.py:253

commit v10 on v7

v10 whole, which is shorter than its diff:
```python
import functools

import jax
import jax.numpy as jnp
from jax import lax
from jax.experimental import pallas as pl
from jax.experimental.pallas import tpu as pltpu
from jax.sharding import PartitionSpec as P

STEPS = 4
KINDS = "UUUT"
PARTS = (4, 4, 4, 4)
CHAIN = ((0,), (1,), (3,), (2,))
CHUNKS = len(PARTS)
VMEM_BYTES = 16 * 1024 * 1024


def params():
    return pltpu.CompilerParams(vmem_limit_bytes=VMEM_BYTES)


def whole_spec():
    return pl.BlockSpec(memory_space=pltpu.VMEM)


def far_spec():
    return pl.BlockSpec(memory_space=pltpu.HBM)


def in_hbm(x):
    return pltpu.with_memory_space_constraint(x, pltpu.HBM)


def cost(flops, traffic):
    return pl.CostEstimate(flops=flops, bytes_accessed=traffic, transcendentals=0)


def cuts_of(depth):
    ends = [depth * sum(PARTS[:n + 1]) // sum(PARTS) for n in range(CHUNKS)]
    return [slice(start, end) for start, end in zip([0] + ends, ends)]


def product(rows, block):
    return lax.dot_general(
        rows, block, (((1,), (1,)), ((), ())), preferred_element_type=jnp.float32
    )


def prepare_kernel(queries, precond, rank, *refs):
    chunks, (held, scale, places, arrived) = refs[:CHUNKS], refs[CHUNKS:]
    rows, depth = queries.shape
    cuts = cuts_of(depth)
    loads = [pltpu.make_async_copy(rank, places, arrived.at[CHUNKS])]
    loads.append(pltpu.make_async_copy(precond, scale, arrived.at[CHUNKS + 1]))
    for n, cut in enumerate(cuts):
        loads.append(pltpu.make_async_copy(queries.at[:, cut], held.at[:, cut], arrived.at[n]))
    for load in loads:
        load.start()
    loads[0].wait()
    loads[1].wait()
    positions = lax.broadcasted_iota(jnp.int32, (rows, rows), 0)
    placing = (positions == places[...]).astype(jnp.bfloat16)
    for n, cut in enumerate(cuts):
        loads[2 + n].wait()
        pre = (held[:, cut].astype(jnp.float32) * scale[:, cut]).astype(jnp.bfloat16)
        chunks[n][...] = jnp.dot(placing, pre, preferred_element_type=jnp.float32).astype(
            jnp.bfloat16
        )


def prepare(queries, precond, rank):
    rows, depth = queries.shape
    shapes = [
        jax.ShapeDtypeStruct((rows, cut.stop - cut.start), jnp.bfloat16) for cut in cuts_of(depth)
    ]
    return pl.pallas_call(
        prepare_kernel,
        out_shape=shapes,
        in_specs=[far_spec()] * 3,
        out_specs=[whole_spec()] * CHUNKS,
        scratch_shapes=[
            pltpu.VMEM((rows, depth), jnp.bfloat16),
            pltpu.VMEM((1, depth), jnp.float32),
            pltpu.VMEM((1, rows), jnp.int32),
            pltpu.SemaphoreType.DMA((CHUNKS + 2,)),
        ],
        compiler_params=params(),
        cost_estimate=cost(2 * rows * rows * depth, 4 * rows * depth),
    )(in_hbm(queries), in_hbm(precond), in_hbm(rank))


def scores_kernel(pieces, fresh, loading, *refs):
    count = len(fresh)
    odd = lax.rem(lax.axis_index("ex"), 2) == 1
    loads = []
    if loading:
        store, valid, *refs = refs
        *refs, limit, other, mine, arrived = refs
        stores = other, mine
        half = other.shape[0]
        me = lax.axis_index("dim")
        for side, where in enumerate((1 - me, me)):
            place = pl.ds(pl.multiple_of(where * half, half), half)
            loads.append(pltpu.make_async_copy(store.at[place], stores[side], arrived.at[side]))
            loads[side].start()
        limit[...] = jnp.full(limit.shape, valid[0], jnp.int32)
    else:
        other, mine, *refs = refs
        stores = other, mine
    outs = refs[-2 * count:]
    carried = refs[-2 * count - 2 * (count - sum(fresh)):-2 * count]
    cuts = cuts_of(other.shape[1])
    stacks = []
    for n, targets in pieces:
        values = []
        for _, even_place, odd_place in targets:
            value = refs[even_place][...]
            if odd_place != even_place:
                value = jnp.where(odd, refs[odd_place][...], value)
            values.append(value)
        stacked = values[0] if len(values) == 1 else jnp.concatenate(values, axis=0)
        stacks.append((n, [which for which, _, _ in targets], stacked))
    for side, store in enumerate(stores):
        if loading:
            loads[side].wait()
        sums, at = {}, 0
        for i, new in enumerate(fresh):
            sums[i] = None if new else carried[at + side][...]
            at += 0 if new else 2
        for n, whiches, stacked in stacks:
            part = product(store[:, cuts[n]], stacked)
            columns = stacked.shape[0] // len(whiches)
            for k, i in enumerate(whiches):
                here = part[:, k * columns:(k + 1) * columns]
                sums[i] = here if sums[i] is None else sums[i] + here
        for i in range(count):
            outs[2 * i + side][...] = sums[i]


def more_scores(stores, pieces, carries, valid=None):
    operands, placed = [], []

    def place(block):
        known = [i for i, operand in enumerate(operands) if operand is block]
        if not known:
            operands.append(block)
        return known[0] if known else len(operands) - 1

    loading = valid is not None
    half, depth = stores.shape[0] // 2 if loading else stores[0].shape[0], 0
    flops = 0
    for n, targets in pieces:
        kept = []
        for which, *blocks in targets:
            places = [place(block) for block in blocks]
            kept.append((which, places[0], places[-1]))
            flops += 4 * half * blocks[0].size
        placed.append((n, tuple(kept)))
    columns = operands[0].shape[0]
    fresh = tuple(carry is None for carry in carries)
    first = [in_hbm(stores), valid] if loading else list(stores)
    operands += [side for carry in carries if carry for side in carry]
    specs = [far_spec(), pl.BlockSpec(memory_space=pltpu.SMEM)] if loading else [whole_spec()] * 2
    total = jax.ShapeDtypeStruct((half, columns), jnp.float32)
    more = []
    if loading:
        held = jax.ShapeDtypeStruct((half, stores.shape[1]), stores.dtype)
        more = [jax.ShapeDtypeStruct((8, columns), jnp.int32), held, held]
    count = 2 * len(carries)
    outs = pl.pallas_call(
        functools.partial(scores_kernel, tuple(placed), fresh, loading),
        out_shape=[total] * count + more,
        in_specs=specs + [whole_spec()] * len(operands),
        out_specs=[whole_spec()] * (count + len(more)),
        scratch_shapes=[pltpu.SemaphoreType.DMA((2,))] if loading else [],
        compiler_params=params(),
        cost_estimate=cost(flops, 4 * half * columns * count),
    )(*first, *operands)
    totals = [(outs[2 * i], outs[2 * i + 1]) for i in range(len(carries))]
    return totals + ([outs[count], outs[count + 1:]] if loading else [])


def finish_kernel(places, limit, *refs):
    out, summed, left = refs[-3:]
    half, columns = refs[0].shape
    row_ids = lax.broadcasted_iota(jnp.int32, (half, columns), 0) + lax.axis_index("dim") * half
    inside = row_ids < limit[:1, :]
    stores = []
    for n, place in enumerate(places):
        cut = slice(n * columns, (n + 1) * columns)
        summed[:, cut] = jnp.where(inside, refs[2 * n][...] + refs[2 * n + 1][...], 0.0)
        to = out.at[:, place * columns:(place + 1) * columns]
        stores.append(pltpu.make_async_copy(summed.at[:, cut], to, left.at[n]))
        stores[n].start()
    for store in stores:
        store.wait()


def finish(limit, pairs, places, steps, out=None):
    half, columns = pairs[0][0].shape
    operands = [ref for pair in pairs for ref in pair]
    given = [] if out is None else [in_hbm(out)]
    return pl.pallas_call(
        functools.partial(finish_kernel, places),
        out_shape=pltpu.HBM((half, columns * steps), jnp.float32),
        in_specs=[whole_spec()] * (1 + len(operands))
        + [far_spec()] * len(given),
        out_specs=far_spec(),
        scratch_shapes=[
            pltpu.VMEM((half, columns * len(places)), jnp.float32),
            pltpu.SemaphoreType.DMA((len(places),)),
        ],
        input_output_aliases={1 + len(operands): 0} if given else {},
        compiler_params=params(),
        cost_estimate=cost(half * columns * len(pairs), 12 * half * columns * len(pairs)),
    )(limit, *operands, *given)


def after(x, *earlier):
    return lax.optimization_barrier((x, *earlier))[0]


def shards(store, queries, precond, query_rank, valid_rows):
    size = lax.axis_size("ex")
    odd = lax.rem(lax.axis_index("ex"), 2) == 1
    one_ahead = [(i, (i + 1) % size) for i in range(size)]
    ahead = [(i, (i + 2) % size) for i in range(size)]
    even_ahead = ahead[::2]
    swap = [(i, i ^ 1) for i in range(size)]
    over_dim = [(0, 1), (1, 0)]

    def send(block, route, axis="ex"):
        return lax.ppermute(block, axis, route)

    def exchanged(total):
        theirs, ours = total
        return ours, send(theirs, over_dim, "dim")

    def by_parity(at_even, at_odd):
        return jnp.where(odd, at_odd, at_even)

    own = prepare(queries, precond[None, :], query_rank)
    two_back = [send(block, ahead) for block in own]
    one_back, three_back = [], []
    for n, kind in enumerate(KINDS):
        arrived = two_back[n]
        if kind == "U":
            swapped = send(by_parity(own[n], arrived), swap)
            one_back.append((swapped,))
            three_back.append((send(swapped, ahead),))
        elif kind == "I":
            early, swapped = send(own[n], swap), send(arrived, swap)
            one_back.append((swapped, early))
            three_back.append((send(swapped, even_ahead), swapped))
        else:
            direct = send(by_parity(own[n], two_back[n]), one_ahead)
            swapped = send(two_back[n], swap)
            one_back.append((swapped, direct))
            three_back.append((direct, swapped))

    first, two, one, limit, stores = more_scores(
        store,
        [
            (n, [(0, own[n]), (1, two_back[n])] + ([] if kind == "T" else [(2, *one_back[n])]))
            for n, kind in enumerate(KINDS)
        ],
        [None, None, None],
        valid_rows,
    )
    own_pair = exchanged(first)
    two_pair = exchanged(two)
    three, left = None, KINDS.count("T")
    for group in CHAIN:
        if KINDS[group[0]] == "T":
            pieces = [(n, [(0, *one_back[n]), (1, *three_back[n])]) for n in group]
            one, three = more_scores(stores, pieces, [one, three])
            left -= len(group)
        else:
            [three] = more_scores(stores, [(n, [(0, *three_back[n])]) for n in group], [three])
        if left == 0:
            left, one_pair = -1, exchanged(one)
    out = finish(limit, [own_pair, one_pair, two_pair], (0, 1, 2), STEPS)
    return finish(limit, [exchanged(three)], (3,), STEPS, out)


def solution(mesh):
    return jax.shard_map(
        shards,
        mesh=mesh,
        in_specs=(
            P(("groups", "ex"), "dim"),
            P(("groups", "ex"), "dim"),
            P("dim"),
            P(("groups", "ex"), None),
            P(("groups", "ex")),
        ),
        out_specs=P(("groups", "ex", "dim"), None),
        check_vma=False,
    )
```

time: 36.8 us -> 38.9 us (1.057)
  waiting for transfers between devices: 5.48 us -> 10.6 us
  starting transfers between devices: 21.4 us -> 18 us
  Pallas kernels: 8.81 us -> 9.3 us
    ppermute x16, waiting for transfers between devices: 5.48 us -> 10.6 us  [send(): return lax.ppermute(block, axis, route)]
    ppermute x16, starting transfers between devices: 21.4 us -> 18 us  [send(): return lax.ppermute(block, axis, route)]
    pallas_call x5, Pallas kernels: 5.51 us -> 5.98 us  [more_scores(): pl.pallas_call(functools.partial(scores_kernel, tuple(placed), fresh, loa...]
  transfers between devices with their start and end apart: 16 -> 16, of which waited for: 4 -> 4; matrix products, arithmetic and copies ran while one was open for 0% -> 0% of each run, Pallas kernels for 17% -> 18%
where the time goes in v10:
time: 38.9 us; the launch traced here: 38.8 us
  starting transfers between devices  18 us (46%)
  waiting for transfers between devices  10.6 us (27%)
  Pallas kernels  9.3 us (24%)
  between operations  0.8 us (2%)
    ppermute x16, starting transfers between devices, send(): return lax.ppermute(block, axis, route)  18 us
    ppermute x16, waiting for transfers between devices, send(): return lax.ppermute(block, axis, route)  10.6 us
    pallas_call x5, Pallas kernels, more_scores(): pl.pallas_call(functools.partial(scores_kernel, tuple(placed), fresh, loa...  5.98 us
    pallas_call x1, Pallas kernels, prepare(): pl.pallas_call(prepare_kernel, out_shape=shapes, in_specs=[far_spec()] *...  1.72 us
    pallas_call x2, Pallas kernels, finish(): pl.pallas_call(functools.partial(finish_kernel, places), out_shape=pltpu....  1.61 us
  transfers between devices with their start and end apart: 16, of which 4 were waited for; matrix products, arithmetic and copies ran while one was open for 0% of the time, Pallas kernels for 18%

profile of v10, /device:TPU:0, one launch (start us, length us, event | category | flops | bytes accessed | tf_op | source)
XLA Modules:
  0.0 38.8 jit_solution(2538878710016288643)
XLA Ops:
  0.0 1.7 %shard_map.55 = (bf16[128,512]{1,0:T(8,128)(2,1)S(1)}, bf16[128,512]{1,0:T(8,128)(2,1)S(1)}, bf16[128,512]{1,0:T(8,128)(2,1)S(1)}, bf16[128,512]{1,0:T(8,128)(2,1)S(1)}) custom-call(bf16[128,2048]{1,0:T(8,128)(2,1)} %queries.1, f32[1,2048]{1,0:T(1,128)} %bitcast.1, s32[1,128]{1,0:T(1,128)} %rank.1), custom_call_target="tpu_custom_call" | custom-call | flops 67108864 | bytes 1048576 | tf_op jit(solution)/shard_map/pallas_call | solution.py:76
  1.7 3.1 %collective-permute-start.2 = (bf16[128,512]{1,0:T(8,128)(2,1)S(1)}, bf16[128,512]{1,0:T(8,128)(2,1)S(1)}, u32[]{:S(2)}, u32[]{:S(2)}) collective-permute-start(bf16[128,512]{1,0:T(8,128)(2,1)S(1)} %get-tuple-element.29.refs_5_), channel_id=1, source_target_pairs={{0,4},{2,6},{4,8},{6,10},{8,12},{10,14},{12,0},{14,2},{1,5},{3,7},... | collective-permute-start | bytes 393224 | tf_op jit(solution)/shard_map/ppermute | solution.py:233
  4.8 1.6 %collective-permute-start.4 = (bf16[128,512]{1,0:T(8,128)(2,1)S(1)}, bf16[128,512]{1,0:T(8,128)(2,1)S(1)}, u32[]{:S(2)}, u32[]{:S(2)}) collective-permute-start(bf16[128,512]{1,0:T(8,128)(2,1)S(1)} %get-tuple-element.30.refs_8_), channel_id=1, source_target_pairs={{0,4},{2,6},{4,8},{6,10},{8,12},{10,14},{12,0},{14,2},{1,5},{3,7},... | collective-permute-start | bytes 393224 | tf_op jit(solution)/shard_map/ppermute | solution.py:233
  6.4 1.6 %collective-permute-start = (bf16[128,512]{1,0:T(8,128)(2,1)S(1)}, bf16[128,512]{1,0:T(8,128)(2,1)S(1)}, u32[]{:S(2)}, u32[]{:S(2)}) collective-permute-start(bf16[128,512]{1,0:T(8,128)(2,1)S(1)} %get-tuple-element.28.refs_2_), channel_id=1, source_target_pairs={{0,4},{2,6},{4,8},{6,10},{8,12},{10,14},{12,0},{14,2},{1,5},{3,7},... | collective-permute-start | bytes 393224 | tf_op jit(solution)/shard_map/ppermute | solution.py:233
  8.0 3.1 %collective-permute-done.2.refs_6_ = bf16[128,512]{1,0:T(8,128)(2,1)S(1)} collective-permute-done((bf16[128,512]{1,0:T(8,128)(2,1)S(1)}, bf16[128,512]{1,0:T(8,128)(2,1)S(1)}, u32[]{:S(2)}, u32[]{:S(2)}) %collective-permute-start.2) | collective-permute-done | bytes 131104 | tf_op jit(solution)/shard_map/ppermute | solution.py:233
  11.2 1.8 %collective-permute-start.3 = (bf16[128,512]{1,0:T(8,128)(2,1)S(1)}, bf16[128,512]{1,0:T(8,128)(2,1)S(1)}, u32[]{:S(2)}, u32[]{:S(2)}) collective-permute-start(bf16[128,512]{1,0:T(8,128)(2,1)S(1)} %broadcast_select_fusion.2), channel_id=1, source_target_pairs={{0,2},{2,0},{4,6},{6,4},{8,10},{10,8},{12,14},{14,12},{1,3},{3,1},... | collective-permute-start | bytes 393224 | tf_op jit(solution)/shard_map/ppermute | solution.py:233
  13.0 3.8 %collective-permute-done.refs_3_ = bf16[128,512]{1,0:T(8,128)(2,1)S(1)} collective-permute-done((bf16[128,512]{1,0:T(8,128)(2,1)S(1)}, bf16[128,512]{1,0:T(8,128)(2,1)S(1)}, u32[]{:S(2)}, u32[]{:S(2)}) %collective-permute-start) | collective-permute-done | bytes 131104 | tf_op jit(solution)/shard_map/ppermute | solution.py:233
  16.8 1.8 %collective-permute-start.1 = (bf16[128,512]{1,0:T(8,128)(2,1)S(1)}, bf16[128,512]{1,0:T(8,128)(2,1)S(1)}, u32[]{:S(2)}, u32[]{:S(2)}) collective-permute-start(bf16[128,512]{1,0:T(8,128)(2,1)S(1)} %broadcast_select_fusion.3), channel_id=1, source_target_pairs={{0,2},{2,0},{4,6},{6,4},{8,10},{10,8},{12,14},{14,12},{1,3},{3,1},... | collective-permute-start | bytes 393224 | tf_op jit(solution)/shard_map/ppermute | solution.py:233
  18.6 0.4 collective-permute-start.5
  19.0 3.1 %collective-permute-done.1.refs_4_ = bf16[128,512]{1,0:T(8,128)(2,1)S(1)} collective-permute-done((bf16[128,512]{1,0:T(8,128)(2,1)S(1)}, bf16[128,512]{1,0:T(8,128)(2,1)S(1)}, u32[]{:S(2)}, u32[]{:S(2)}) %collective-permute-start.1) | collective-permute-done | bytes 131104 | tf_op jit(solution)/shard_map/ppermute | solution.py:233
  22.1 1.3 %collective-permute-start.10 = (bf16[128,512]{1,0:T(8,128)(2,1)S(1)}, bf16[128,512]{1,0:T(8,128)(2,1)S(1)}, u32[]{:S(2)}, u32[]{:S(2)}) collective-permute-start(bf16[128,512]{1,0:T(8,128)(2,1)S(1)} %collective-permute-done.3.refs_7_), channel_id=1, source_target_pairs={{0,4},{2,6},{4,8},{6,10},{8,12},{10,14},{12,0},{14,2},{1,5},{3,7},... | collective-permute-start | bytes 393224 | tf_op jit(solution)/shard_map/ppermute | solution.py:233
  23.5 1.5 %collective-permute-start.9 = (bf16[128,512]{1,0:T(8,128)(2,1)S(1)}, bf16[128,512]{1,0:T(8,128)(2,1)S(1)}, u32[]{:S(2)}, u32[]{:S(2)}) collective-permute-start(bf16[128,512]{1,0:T(8,128)(2,1)S(1)} %broadcast_select_fusion), channel_id=1, source_target_pairs={{0,2},{2,4},{4,6},{6,8},{8,10},{10,12},{12,14},{14,0},{1,3},{3,5},... | collective-permute-start | bytes 393224 | tf_op jit(solution)/shard_map/ppermute | solution.py:233
  25.0 1.5 %collective-permute-start.8 = (bf16[128,512]{1,0:T(8,128)(2,1)S(1)}, bf16[128,512]{1,0:T(8,128)(2,1)S(1)}, u32[]{:S(2)}, u32[]{:S(2)}) collective-permute-start(bf16[128,512]{1,0:T(8,128)(2,1)S(1)} %collective-permute-done.6.refs_12_), channel_id=1, source_target_pairs={{0,2},{2,0},{4,6},{6,4},{8,10},{10,8},{12,14},{14,12},{1,3},{3,1},... | collective-permute-start | bytes 393224 | tf_op jit(solution)/shard_map/ppermute | solution.py:233
  27.2 2.1 %collective-permute-start.7 = (bf16[128,512]{1,0:T(8,128)(2,1)S(1)}, bf16[128,512]{1,0:T(8,128)(2,1)S(1)}, u32[]{:S(2)}, u32[]{:S(2)}) collective-permute-start(bf16[128,512]{1,0:T(8,128)(2,1)S(1)} %collective-permute-done.5.refs_10_), channel_id=1, source_target_pairs={{0,4},{2,6},{4,8},{6,10},{8,12},{10,14},{12,0},{14,2},{1,5},{3,7},... | collective-permute-start | bytes 393224 | tf_op jit(solution)/shard_map/ppermute | solution.py:233
  29.3 4.5 %shard_map.56 = (f32[384,128]{1,0:T(8,128)S(1)}, f32[384,128]{1,0:T(8,128)S(1)}, f32[384,128]{1,0:T(8,128)S(1)}, f32[384,128]{1,0:T(8,128)S(1)}, f32[384,128]{1,...) custom-call(bf16[768,2048]{1,0:T(8,128)(2,1)} %refs_0_.1, ...), custom_call_target="tpu_custom_call" | custom-call | flops 1107296256 | bytes 1179648 | tf_op jit(solution)/shard_map/pallas_call | solution.py:170
  33.9 0.4 shard_map.57
  34.2 0.6 %collective-permute-start.15 = (f32[384,128]{1,0:T(8,128)S(1)}, f32[384,128]{1,0:T(8,128)S(1)}, u32[]{:S(2)}, u32[]{:S(2)}) collective-permute-start(f32[384,128]{1,0:T(8,128)S(1)} %get-tuple-element.50), channel_id=1, source_target_pairs={{0,1},{1,0},{2,3},{3,2},{4,5},{5,4},{6,7},{7,6},{8,9},{9,8},{10,11... | collective-permute-start | bytes 589832 | tf_op jit(solution)/shard_map/ppermute | solution.py:233
  34.8 0.4 shard_map.58
  35.2 0.4 %shard_map.59 = (f32[384,128]{1,0:T(8,128)S(1)}, f32[384,128]{1,0:T(8,128)S(1)}, f32[384,128]{1,0:T(8,128)S(1)}, f32[384,128]{1,0:T(8,128)S(1)}) custom-call(bf16[384,2048]{1,0:T(8,128)(2,1)S(1)} %get-tuple-element.33.refs_0_, bf16[384,2048]{1,0:T(8,128)(2,1)S(1)} %get-tuple-element.34.refs_1_, bf16[128,512]{1,0:T(8,128)(2,1)S(1)} %collective-permute-done.8.refs_2_, ...), custom_call_target="tpu_custom_call" | custom-call | flops 201326592 | bytes 786432 | tf_op jit(solution)/shard_map/pallas_call | solution.py:170
  35.7 0.4 shard_map.60
  36.1 0.5 %collective-permute-start.12 = (f32[384,128]{1,0:T(8,128)S(1)}, f32[384,128]{1,0:T(8,128)S(1)}, u32[]{:S(2)}, u32[]{:S(2)}) collective-permute-start(f32[384,128]{1,0:T(8,128)S(1)} %get-tuple-element.44), channel_id=1, source_target_pairs={{0,1},{1,0},{2,3},{3,2},{4,5},{5,4},{6,7},{7,6},{8,9},{9,8},{10,11... | collective-permute-start | bytes 589832 | tf_op jit(solution)/shard_map/ppermute | solution.py:233
  36.7 0.5 %collective-permute-done.14.refs_3_ = f32[384,128]{1,0:T(8,128)S(1)} collective-permute-done((f32[384,128]{1,0:T(8,128)S(1)}, f32[384,128]{1,0:T(8,128)S(1)}, u32[]{:S(2)}, u32[]{:S(2)}) %collective-permute-start.14) | collective-permute-done | bytes 196640 | tf_op jit(solution)/shard_map/ppermute | solution.py:233
  37.1 0.9 %shard_map.61.refs_2_ = f32[384,512]{1,0:T(8,128)} custom-call(s32[8,128]{1,0:T(8,128)S(1)} %get-tuple-element.32.limit, f32[384,128]{1,0:T(8,128)S(1)} %get-tuple-element.45.refs_0_, f32[384,128]{1,0:T(8,128)S(1)} %collective-permute-done.13.refs_1_, f32[384,128]{1,0:T(8,128)S(1)} %get-tuple-element.47.refs_2_, ...), custom_call_target="tpu_custom_call" | custom-call | flops 147456 | bytes 1769472 | tf_op jit(solution)/shard_map/pallas_call | solution.py:203
  38.0 0.7 %shard_map.62 = f32[384,512]{1,0:T(8,128)} custom-call(s32[8,128]{1,0:T(8,128)S(1)} %get-tuple-element.32.limit, f32[384,128]{1,0:T(8,128)S(1)} %get-tuple-element.43.refs_0_, f32[384,128]{1,0:T(8,128)S(1)} %collective-permute-done.12.refs_1_, f32[384,512]{1,0:T(8,128)} %shard_map.61.refs_2_), custom_call_target="tpu_custom_call", output_to_operand_aliasing={{}: (3, {})} | custom-call | flops 49152 | bytes 589824 | tf_op jit(solution)/shard_map/pallas_call | solution.py:203
  (20 shorter events, 0.3 us)
Async XLA Ops:
  1.7 9.4 %collective-permute-start.2 = (bf16[128,512]{1,0:T(8,128)(2,1)S(1)}, bf16[128,512]{1,0:T(8,128)(2,1)S(1)}, u32[]{:S(2)}, u32[]{:S(2)}) collective-permute-start(bf16[128,512]{1,0:T(8,128)(2,1)S(1)} %get-tuple-element.29.refs_5_), channel_id=1, source_target_pairs={{0,4},{2,6},{4,8},{6,10},{8,12},{10,14},{12,0},{14,2},{1,5},{3,7},... | collective-permute-start | bytes 393224 | tf_op jit(solution)/shard_map/ppermute | solution.py:233
  4.8 13.8 %collective-permute-start.4 = (bf16[128,512]{1,0:T(8,128)(2,1)S(1)}, bf16[128,512]{1,0:T(8,128)(2,1)S(1)}, u32[]{:S(2)}, u32[]{:S(2)}) collective-permute-start(bf16[128,512]{1,0:T(8,128)(2,1)S(1)} %get-tuple-element.30.refs_8_), channel_id=1, source_target_pairs={{0,4},{2,6},{4,8},{6,10},{8,12},{10,14},{12,0},{14,2},{1,5},{3,7},... | collective-permute-start | bytes 393224 | tf_op jit(solution)/shard_map/ppermute | solution.py:233
  6.4 10.4 %collective-permute-start = (bf16[128,512]{1,0:T(8,128)(2,1)S(1)}, bf16[128,512]{1,0:T(8,128)(2,1)S(1)}, u32[]{:S(2)}, u32[]{:S(2)}) collective-permute-start(bf16[128,512]{1,0:T(8,128)(2,1)S(1)} %get-tuple-element.28.refs_2_), channel_id=1, source_target_pairs={{0,4},{2,6},{4,8},{6,10},{8,12},{10,14},{12,0},{14,2},{1,5},{3,7},... | collective-permute-start | bytes 393224 | tf_op jit(solution)/shard_map/ppermute | solution.py:233
  8.0 15.5 %collective-permute-start.6 = (bf16[128,512]{1,0:T(8,128)(2,1)S(1)}, bf16[128,512]{1,0:T(8,128)(2,1)S(1)}, u32[]{:S(2)}, u32[]{:S(2)}) collective-permute-start(bf16[128,512]{1,0:T(8,128)(2,1)S(1)} %get-tuple-element.31.refs_11_), channel_id=1, source_target_pairs={{0,4},{2,6},{4,8},{6,10},{8,12},{10,14},{12,0},{14,2},{1,5},{3,7},... | collective-permute-start | bytes 393224 | tf_op jit(solution)/shard_map/ppermute | solution.py:233
  11.2 10.9 %collective-permute-start.3 = (bf16[128,512]{1,0:T(8,128)(2,1)S(1)}, bf16[128,512]{1,0:T(8,128)(2,1)S(1)}, u32[]{:S(2)}, u32[]{:S(2)}) collective-permute-start(bf16[128,512]{1,0:T(8,128)(2,1)S(1)} %broadcast_select_fusion.2), channel_id=1, source_target_pairs={{0,2},{2,0},{4,6},{6,4},{8,10},{10,8},{12,14},{14,12},{1,3},{3,1},... | collective-permute-start | bytes 393224 | tf_op jit(solution)/shard_map/ppermute | solution.py:233
  16.8 5.3 %collective-permute-start.1 = (bf16[128,512]{1,0:T(8,128)(2,1)S(1)}, bf16[128,512]{1,0:T(8,128)(2,1)S(1)}, u32[]{:S(2)}, u32[]{:S(2)}) collective-permute-start(bf16[128,512]{1,0:T(8,128)(2,1)S(1)} %broadcast_select_fusion.3), channel_id=1, source_target_pairs={{0,2},{2,0},{4,6},{6,4},{8,10},{10,8},{12,14},{14,12},{1,3},{3,1},... | collective-permute-start | bytes 393224 | tf_op jit(solution)/shard_map/ppermute | solution.py:233
  18.6 8.6 %collective-permute-start.5 = (bf16[128,512]{1,0:T(8,128)(2,1)S(1)}, bf16[128,512]{1,0:T(8,128)(2,1)S(1)}, u32[]{:S(2)}, u32[]{:S(2)}) collective-permute-start(bf16[128,512]{1,0:T(8,128)(2,1)S(1)} %broadcast_select_fusion.1), channel_id=1, source_target_pairs={{0,2},{2,0},{4,6},{6,4},{8,10},{10,8},{12,14},{14,12},{1,3},{3,1},... | collective-permute-start | bytes 393224 | tf_op jit(solution)/shard_map/ppermute | solution.py:233
  22.1 11.7 %collective-permute-start.11 = (bf16[128,512]{1,0:T(8,128)(2,1)S(1)}, bf16[128,512]{1,0:T(8,128)(2,1)S(1)}, u32[]{:S(2)}, u32[]{:S(2)}) collective-permute-start(bf16[128,512]{1,0:T(8,128)(2,1)S(1)} %collective-permute-done.1.refs_4_), channel_id=1, source_target_pairs={{0,4},{2,6},{4,8},{6,10},{8,12},{10,14},{12,0},{14,2},{1,5},{3,7},... | collective-permute-start | bytes 393224 | tf_op jit(solution)/shard_map/ppermute | solution.py:233
  22.1 12.1 %collective-permute-start.10 = (bf16[128,512]{1,0:T(8,128)(2,1)S(1)}, bf16[128,512]{1,0:T(8,128)(2,1)S(1)}, u32[]{:S(2)}, u32[]{:S(2)}) collective-permute-start(bf16[128,512]{1,0:T(8,128)(2,1)S(1)} %collective-permute-done.3.refs_7_), channel_id=1, source_target_pairs={{0,4},{2,6},{4,8},{6,10},{8,12},{10,14},{12,0},{14,2},{1,5},{3,7},... | collective-permute-start | bytes 393224 | tf_op jit(solution)/shard_map/ppermute | solution.py:233
  23.5 11.7 %collective-permute-start.9 = (bf16[128,512]{1,0:T(8,128)(2,1)S(1)}, bf16[128,512]{1,0:T(8,128)(2,1)S(1)}, u32[]{:S(2)}, u32[]{:S(2)}) collective-permute-start(bf16[128,512]{1,0:T(8,128)(2,1)S(1)} %broadcast_select_fusion), channel_id=1, source_target_pairs={{0,2},{2,4},{4,6},{6,8},{8,10},{10,12},{12,14},{14,0},{1,3},{3,5},... | collective-permute-start | bytes 393224 | tf_op jit(solution)/shard_map/ppermute | solution.py:233
  25.0 10.2 %collective-permute-start.8 = (bf16[128,512]{1,0:T(8,128)(2,1)S(1)}, bf16[128,512]{1,0:T(8,128)(2,1)S(1)}, u32[]{:S(2)}, u32[]{:S(2)}) collective-permute-start(bf16[128,512]{1,0:T(8,128)(2,1)S(1)} %collective-permute-done.6.refs_12_), channel_id=1, source_target_pairs={{0,2},{2,0},{4,6},{6,4},{8,10},{10,8},{12,14},{14,12},{1,3},{3,1},... | collective-permute-start | bytes 393224 | tf_op jit(solution)/shard_map/ppermute | solution.py:233
  27.2 8.5 %collective-permute-start.7 = (bf16[128,512]{1,0:T(8,128)(2,1)S(1)}, bf16[128,512]{1,0:T(8,128)(2,1)S(1)}, u32[]{:S(2)}, u32[]{:S(2)}) collective-permute-start(bf16[128,512]{1,0:T(8,128)(2,1)S(1)} %collective-permute-done.5.refs_10_), channel_id=1, source_target_pairs={{0,4},{2,6},{4,8},{6,10},{8,12},{10,14},{12,0},{14,2},{1,5},{3,7},... | collective-permute-start | bytes 393224 | tf_op jit(solution)/shard_map/ppermute | solution.py:233
  33.8 2.9 %collective-permute-start.13 = (f32[384,128]{1,0:T(8,128)S(1)}, f32[384,128]{1,0:T(8,128)S(1)}, u32[]{:S(2)}, u32[]{:S(2)}) collective-permute-start(f32[384,128]{1,0:T(8,128)S(1)} %get-tuple-element.46), channel_id=1, source_target_pairs={{0,1},{1,0},{2,3},{3,2},{4,5},{5,4},{6,7},{7,6},{8,9},{9,8},{10,11... | collective-permute-start | bytes 589832 | tf_op jit(solution)/shard_map/ppermute | solution.py:233
  34.2 2.4 %collective-permute-start.15 = (f32[384,128]{1,0:T(8,128)S(1)}, f32[384,128]{1,0:T(8,128)S(1)}, u32[]{:S(2)}, u32[]{:S(2)}) collective-permute-start(f32[384,128]{1,0:T(8,128)S(1)} %get-tuple-element.50), channel_id=1, source_target_pairs={{0,1},{1,0},{2,3},{3,2},{4,5},{5,4},{6,7},{7,6},{8,9},{9,8},{10,11... | collective-permute-start | bytes 589832 | tf_op jit(solution)/shard_map/ppermute | solution.py:233
  35.6 1.5 %collective-permute-start.14 = (f32[384,128]{1,0:T(8,128)S(1)}, f32[384,128]{1,0:T(8,128)S(1)}, u32[]{:S(2)}, u32[]{:S(2)}) collective-permute-start(f32[384,128]{1,0:T(8,128)S(1)} %get-tuple-element.48), channel_id=1, source_target_pairs={{0,1},{1,0},{2,3},{3,2},{4,5},{5,4},{6,7},{7,6},{8,9},{9,8},{10,11... | collective-permute-start | bytes 589832 | tf_op jit(solution)/shard_map/ppermute | solution.py:233
  36.1 1.9 %collective-permute-start.12 = (f32[384,128]{1,0:T(8,128)S(1)}, f32[384,128]{1,0:T(8,128)S(1)}, u32[]{:S(2)}, u32[]{:S(2)}) collective-permute-start(f32[384,128]{1,0:T(8,128)S(1)} %get-tuple-element.44), channel_id=1, source_target_pairs={{0,1},{1,0},{2,3},{3,2},{4,5},{5,4},{6,7},{7,6},{8,9},{9,8},{10,11... | collective-permute-start | bytes 589832 | tf_op jit(solution)/shard_map/ppermute | solution.py:233

commit v11 on v10

--- a/solution.py
+++ b/solution.py
@@ -10,7 +10,9 @@
 STEPS = 4
 KINDS = "UUUT"
 PARTS = (4, 4, 4, 4)
-CHAIN = ((0,), (1,), (3,), (2,))
+CHAIN = ("b2", "b1", "b3 o0", "t0")
+ORDER = ("B0", "B1", "B2", "B3", "C2", "C1", "C0", "E2", "E1", "E0", "R3", "C3")
+TIES = {"B3": "B2", "C3": "C0", "R3": "C2"}
 CHUNKS = len(PARTS)
 VMEM_BYTES = 16 * 1024 * 1024
 
@@ -89,13 +91,16 @@
     )(in_hbm(queries), in_hbm(precond), in_hbm(rank))
 
 
-def scores_kernel(pieces, fresh, loading, *refs):
+def scores_kernel(pieces, fresh, loading, counted, *refs):
     count = len(fresh)
+    if counted:
+        valid, *refs, limit = refs
+        limit[...] = jnp.full(limit.shape, valid[0], jnp.int32)
     odd = lax.rem(lax.axis_index("ex"), 2) == 1
     loads = []
     if loading:
-        store, valid, *refs = refs
-        *refs, limit, other, mine, arrived = refs
+        store, *refs = refs
+        *refs, other, mine, arrived = refs
         stores = other, mine
         half = other.shape[0]
         me = lax.axis_index("dim")
@@ -103,7 +108,6 @@
             place = pl.ds(pl.multiple_of(where * half, half), half)
             loads.append(pltpu.make_async_copy(store.at[place], stores[side], arrived.at[side]))
             loads[side].start()
-        limit[...] = jnp.full(limit.shape, valid[0], jnp.int32)
     else:
         other, mine, *refs = refs
         stores = other, mine
@@ -146,7 +150,7 @@
             operands.append(block)
         return known[0] if known else len(operands) - 1
 
-    loading = valid is not None
+    loading = not isinstance(stores, tuple)
     half, depth = stores.shape[0] // 2 if loading else stores[0].shape[0], 0
     flops = 0
     for n, targets in pieces:
@@ -158,17 +162,20 @@
         placed.append((n, tuple(kept)))
     columns = operands[0].shape[0]
     fresh = tuple(carry is None for carry in carries)
-    first = [in_hbm(stores), valid] if loading else list(stores)
+    first = [in_hbm(stores)] if loading else list(stores)
     operands += [side for carry in carries if carry for side in carry]
-    specs = [far_spec(), pl.BlockSpec(memory_space=pltpu.SMEM)] if loading else [whole_spec()] * 2
+    specs = [far_spec()] if loading else [whole_spec()] * 2
     total = jax.ShapeDtypeStruct((half, columns), jnp.float32)
     more = []
     if loading:
         held = jax.ShapeDtypeStruct((half, stores.shape[1]), stores.dtype)
-        more = [jax.ShapeDtypeStruct((8, columns), jnp.int32), held, held]
+        more = [held, held]
+    if valid is not None:
+        first, more = [valid] + first, more + [jax.ShapeDtypeStruct((8, columns), jnp.int32)]
+        specs = [pl.BlockSpec(memory_space=pltpu.SMEM)] + specs
     count = 2 * len(carries)
     outs = pl.pallas_call(
-        functools.partial(scores_kernel, tuple(placed), fresh, loading),
+        functools.partial(scores_kernel, tuple(placed), fresh, loading, valid is not None),
         out_shape=[total] * count + more,
         in_specs=specs + [whole_spec()] * len(operands),
         out_specs=[whole_spec()] * (count + len(more)),
@@ -177,7 +184,9 @@
         cost_estimate=cost(flops, 4 * half * columns * count),
     )(*first, *operands)
     totals = [(outs[2 * i], outs[2 * i + 1]) for i in range(len(carries))]
-    return totals + ([outs[count], outs[count + 1:]] if loading else [])
+    if valid is not None:
+        return totals + [outs[-1]]
+    return totals + ([tuple(outs[count:])] if loading else [])
 
 
 def finish_kernel(places, limit, *refs):
@@ -240,45 +249,63 @@
         return jnp.where(odd, at_odd, at_even)
 
     own = prepare(queries, precond[None, :], query_rank)
-    two_back = [send(block, ahead) for block in own]
-    one_back, three_back = [], []
+    moved = {}
+
+    def tied(name, block):
+        return after(block, *(moved[key] for key in TIES.get(name, "").split()))
+
+    def move(name, block, route):
+        moved[name] = send(tied(name, block), route)
+        return moved[name]
+
+    one_back, three_back, two_back = {}, {}, {}
+    for step in ORDER:
+        kind, n = step[0], int(step[1:])
+        if kind == "B":
+            two_back[n] = move(step, own[n], ahead)
+        elif kind == "A":
+            move(step, own[n], swap)
+        elif kind == "C":
+            block = two_back[n] if KINDS[n] != "U" else by_parity(own[n], two_back[n])
+            move(step, block, swap)
+        elif kind == "E":
+            move(step, moved[f"C{n}"], even_ahead if KINDS[n] == "I" else ahead)
+        else:
+            move(step, by_parity(own[n], two_back[n]), one_ahead)
     for n, kind in enumerate(KINDS):
-        arrived = two_back[n]
+        swapped = moved[f"C{n}"]
         if kind == "U":
-            swapped = send(by_parity(own[n], arrived), swap)
-            one_back.append((swapped,))
-            three_back.append((send(swapped, ahead),))
+            one_back[n], three_back[n] = (swapped,), (moved[f"E{n}"],)
         elif kind == "I":
-            early, swapped = send(own[n], swap), send(arrived, swap)
-            one_back.append((swapped, early))
-            three_back.append((send(swapped, even_ahead), swapped))
+            one_back[n], three_back[n] = (swapped, moved[f"A{n}"]), (moved[f"E{n}"], swapped)
         else:
-            direct = send(by_parity(own[n], two_back[n]), one_ahead)
-            swapped = send(two_back[n], swap)
-            one_back.append((swapped, direct))
-            three_back.append((direct, swapped))
-
-    first, two, one, limit, stores = more_scores(
+            direct = moved[f"R{n}"]
+            one_back[n], three_back[n] = (swapped, direct), (direct, swapped)
+
+    first, two, stores = more_scores(
         store,
-        [
-            (n, [(0, own[n]), (1, two_back[n])] + ([] if kind == "T" else [(2, *one_back[n])]))
-            for n, kind in enumerate(KINDS)
-        ],
-        [None, None, None],
-        valid_rows,
+        [(n, [(0, own[n]), (1, two_back[n])]) for n in range(CHUNKS)],
+        [None, None],
     )
-    own_pair = exchanged(first)
-    two_pair = exchanged(two)
-    three, left = None, KINDS.count("T")
+    own_pair, two_pair = exchanged(first), exchanged(two)
+    one = three = one_pair = None
+    todo = set(range(CHUNKS))
     for group in CHAIN:
-        if KINDS[group[0]] == "T":
-            pieces = [(n, [(0, *one_back[n]), (1, *three_back[n])]) for n in group]
-            one, three = more_scores(stores, pieces, [one, three])
-            left -= len(group)
+        pieces = []
+        for item in group.split():
+            n, parts = int(item[1:]), {"b": (0, 1), "o": (0,), "t": (1,)}[item[0]]
+            blocks = one_back[n], three_back[n]
+            pieces.append((n, [(part, *blocks[part]) for part in parts]))
+            todo -= {n} if 0 in parts else set()
+        if one_pair is None:
+            if one is None:
+                one, three, limit = more_scores(stores, pieces, [one, three], valid_rows)
+            else:
+                one, three = more_scores(stores, pieces, [one, three])
+            one_pair = None if todo else exchanged(one)
         else:
-            [three] = more_scores(stores, [(n, [(0, *three_back[n])]) for n in group], [three])
-        if left == 0:
-            left, one_pair = -1, exchanged(one)
+            pieces = [(n, [(0, *blocks) for _, *blocks in targets]) for n, targets in pieces]
+            [three] = more_scores(stores, pieces, [three])
     out = finish(limit, [own_pair, one_pair, two_pair], (0, 1, 2), STEPS)
     return finish(limit, [exchanged(three)], (3,), STEPS, out)
 

time: 38.9 us -> 35.2 us (0.905)
  waiting for transfers between devices: 10.6 us -> 8.55 us
  Pallas kernels: 9.3 us -> 8.47 us
  starting transfers between devices: 18 us -> 17.2 us
    ppermute x16, waiting for transfers between devices: 10.6 us -> 8.55 us  [send(): return lax.ppermute(block, axis, route)]
    ppermute x16, starting transfers between devices: 18 us -> 17.2 us  [send(): return lax.ppermute(block, axis, route)]
    pallas_call x5, Pallas kernels: 5.98 us -> 5.16 us  [more_scores(): pl.pallas_call(functools.partial(scores_kernel, tuple(placed), fresh, loa...]
  transfers between devices with their start and end apart: 16 -> 16, of which waited for: 4 -> 8; matrix products, arithmetic and copies ran while one was open for 0% -> 0% of each run, Pallas kernels for 18% -> 17%
where the time goes in v11:
time: 35.2 us; the launch traced here: 35 us
  starting transfers between devices  17.2 us (49%)
  waiting for transfers between devices  8.55 us (24%)
  Pallas kernels  8.47 us (24%)
  between operations  0.76 us (2%)
    ppermute x16, starting transfers between devices, send(): return lax.ppermute(block, axis, route)  17.2 us
    ppermute x16, waiting for transfers between devices, send(): return lax.ppermute(block, axis, route)  8.55 us
    pallas_call x5, Pallas kernels, more_scores(): pl.pallas_call(functools.partial(scores_kernel, tuple(placed), fresh, loa...  5.16 us
    pallas_call x1, Pallas kernels, prepare(): pl.pallas_call(prepare_kernel, out_shape=shapes, in_specs=[far_spec()] *...  1.72 us
    pallas_call x2, Pallas kernels, finish(): pl.pallas_call(functools.partial(finish_kernel, places), out_shape=pltpu....  1.59 us
  transfers between devices with their start and end apart: 16, of which 8 were waited for; matrix products, arithmetic and copies ran while one was open for 0% of the time, Pallas kernels for 17%

profile of v11, /device:TPU:0, one launch (start us, length us, event | category | flops | bytes accessed | tf_op | source)
XLA Modules:
  0.0 35.0 jit_solution(11477180389899036139)
XLA Ops:
  0.0 1.7 %shard_map.55 = (bf16[128,512]{1,0:T(8,128)(2,1)S(1)}, bf16[128,512]{1,0:T(8,128)(2,1)S(1)}, bf16[128,512]{1,0:T(8,128)(2,1)S(1)}, bf16[128,512]{1,0:T(8,128)(2,1)S(1)}) custom-call(bf16[128,2048]{1,0:T(8,128)(2,1)} %queries.1, f32[1,2048]{1,0:T(1,128)} %bitcast.1, s32[1,128]{1,0:T(1,128)} %rank.1), custom_call_target="tpu_custom_call" | custom-call | flops 67108864 | bytes 1048576 | tf_op jit(solution)/shard_map/pallas_call | solution.py:78
  1.7 3.1 %collective-permute-start.2 = (bf16[128,512]{1,0:T(8,128)(2,1)S(1)}, bf16[128,512]{1,0:T(8,128)(2,1)S(1)}, u32[]{:S(2)}, u32[]{:S(2)}) collective-permute-start(bf16[128,512]{1,0:T(8,128)(2,1)S(1)} %get-tuple-element.35.refs_5_), channel_id=1, source_target_pairs={{0,4},{2,6},{4,8},{6,10},{8,12},{10,14},{12,0},{14,2},{1,5},{3,7},... | collective-permute-start | bytes 393224 | tf_op jit(solution)/shard_map/ppermute | solution.py:242
  4.8 1.6 %collective-permute-start.1 = (bf16[128,512]{1,0:T(8,128)(2,1)S(1)}, bf16[128,512]{1,0:T(8,128)(2,1)S(1)}, u32[]{:S(2)}, u32[]{:S(2)}) collective-permute-start(bf16[128,512]{1,0:T(8,128)(2,1)S(1)} %get-tuple-element.34.refs_3_), channel_id=1, source_target_pairs={{0,4},{2,6},{4,8},{6,10},{8,12},{10,14},{12,0},{14,2},{1,5},{3,7},... | collective-permute-start | bytes 393224 | tf_op jit(solution)/shard_map/ppermute | solution.py:242
  6.4 1.6 %collective-permute-start = (bf16[128,512]{1,0:T(8,128)(2,1)S(1)}, bf16[128,512]{1,0:T(8,128)(2,1)S(1)}, u32[]{:S(2)}, u32[]{:S(2)}) collective-permute-start(bf16[128,512]{1,0:T(8,128)(2,1)S(1)} %get-tuple-element.33.refs_1_), channel_id=1, source_target_pairs={{0,4},{2,6},{4,8},{6,10},{8,12},{10,14},{12,0},{14,2},{1,5},{3,7},... | collective-permute-start | bytes 393224 | tf_op jit(solution)/shard_map/ppermute | solution.py:242
  8.0 3.2 %collective-permute-done.2.refs_6_ = bf16[128,512]{1,0:T(8,128)(2,1)S(1)} collective-permute-done((bf16[128,512]{1,0:T(8,128)(2,1)S(1)}, bf16[128,512]{1,0:T(8,128)(2,1)S(1)}, u32[]{:S(2)}, u32[]{:S(2)}) %collective-permute-start.2) | collective-permute-done | bytes 131104 | tf_op jit(solution)/shard_map/ppermute | solution.py:242
  11.2 1.8 %collective-permute-start.4 = (bf16[128,512]{1,0:T(8,128)(2,1)S(1)}, bf16[128,512]{1,0:T(8,128)(2,1)S(1)}, u32[]{:S(2)}, u32[]{:S(2)}) collective-permute-start(bf16[128,512]{1,0:T(8,128)(2,1)S(1)} %broadcast_select_fusion.3), channel_id=1, source_target_pairs={{0,2},{2,0},{4,6},{6,4},{8,10},{10,8},{12,14},{14,12},{1,3},{3,1},... | collective-permute-start | bytes 393224 | tf_op jit(solution)/shard_map/ppermute | solution.py:242
  13.0 1.0 %collective-permute-done.1.refs_4_ = bf16[128,512]{1,0:T(8,128)(2,1)S(1)} collective-permute-done((bf16[128,512]{1,0:T(8,128)(2,1)S(1)}, bf16[128,512]{1,0:T(8,128)(2,1)S(1)}, u32[]{:S(2)}, u32[]{:S(2)}) %collective-permute-start.1) | collective-permute-done | bytes 131104 | tf_op jit(solution)/shard_map/ppermute | solution.py:242
  14.0 1.8 %collective-permute-start.10 = (bf16[128,512]{1,0:T(8,128)(2,1)S(1)}, bf16[128,512]{1,0:T(8,128)(2,1)S(1)}, u32[]{:S(2)}, u32[]{:S(2)}) collective-permute-start(bf16[128,512]{1,0:T(8,128)(2,1)S(1)} %broadcast_select_fusion), channel_id=1, source_target_pairs={{0,2},{2,0},{4,6},{6,4},{8,10},{10,8},{12,14},{14,12},{1,3},{3,1},... | collective-permute-start | bytes 393224 | tf_op jit(solution)/shard_map/ppermute | solution.py:242
  15.8 1.0 %collective-permute-done.refs_2_ = bf16[128,512]{1,0:T(8,128)(2,1)S(1)} collective-permute-done((bf16[128,512]{1,0:T(8,128)(2,1)S(1)}, bf16[128,512]{1,0:T(8,128)(2,1)S(1)}, u32[]{:S(2)}, u32[]{:S(2)}) %collective-permute-start) | collective-permute-done | bytes 131104 | tf_op jit(solution)/shard_map/ppermute | solution.py:242
  16.8 1.8 %collective-permute-start.6 = (bf16[128,512]{1,0:T(8,128)(2,1)S(1)}, bf16[128,512]{1,0:T(8,128)(2,1)S(1)}, u32[]{:S(2)}, u32[]{:S(2)}) collective-permute-start(bf16[128,512]{1,0:T(8,128)(2,1)S(1)} %broadcast_select_fusion.2), channel_id=1, source_target_pairs={{0,2},{2,0},{4,6},{6,4},{8,10},{10,8},{12,14},{14,12},{1,3},{3,1},... | collective-permute-start | bytes 393224 | tf_op jit(solution)/shard_map/ppermute | solution.py:242
  18.6 1.5 %collective-permute-done.10.refs_2_ = bf16[128,512]{1,0:T(8,128)(2,1)S(1)} collective-permute-done((bf16[128,512]{1,0:T(8,128)(2,1)S(1)}, bf16[128,512]{1,0:T(8,128)(2,1)S(1)}, u32[]{:S(2)}, u32[]{:S(2)}) %collective-permute-start.10) | collective-permute-done | bytes 131104 | tf_op jit(solution)/shard_map/ppermute | solution.py:242
  20.2 2.0 %collective-permute-start.9 = (bf16[128,512]{1,0:T(8,128)(2,1)S(1)}, bf16[128,512]{1,0:T(8,128)(2,1)S(1)}, u32[]{:S(2)}, u32[]{:S(2)}) collective-permute-start(bf16[128,512]{1,0:T(8,128)(2,1)S(1)} %broadcast_select_fusion.1), channel_id=1, source_target_pairs={{0,2},{2,4},{4,6},{6,8},{8,10},{10,12},{12,14},{14,0},{1,3},{3,5},... | collective-permute-start | bytes 393224 | tf_op jit(solution)/shard_map/ppermute | solution.py:242
  22.5 2.5 %collective-permute-start.8 = (bf16[128,512]{1,0:T(8,128)(2,1)S(1)}, bf16[128,512]{1,0:T(8,128)(2,1)S(1)}, u32[]{:S(2)}, u32[]{:S(2)}) collective-permute-start(bf16[128,512]{1,0:T(8,128)(2,1)S(1)} %collective-permute-done.3.refs_8_), channel_id=1, source_target_pairs={{0,2},{2,0},{4,6},{6,4},{8,10},{10,8},{12,14},{14,12},{1,3},{3,1},... | collective-permute-start | bytes 393224 | tf_op jit(solution)/shard_map/ppermute | solution.py:242
  25.9 3.4 %shard_map.56 = (f32[384,128]{1,0:T(8,128)S(1)}, f32[384,128]{1,0:T(8,128)S(1)}, f32[384,128]{1,0:T(8,128)S(1)}, f32[384,128]{1,0:T(8,128)S(1)}, bf16[384,2048]{...) custom-call(bf16[768,2048]{1,0:T(8,128)(2,1)} %refs_0_.2, bf16[128,512]{1,0:T(8,128)(2,1)S(1)} %get-tuple-element.33.refs_1_, ...), custom_call_target="tpu_custom_call" | custom-call | flops 805306368 | bytes 786432 | tf_op jit(solution)/shard_map/pallas_call | solution.py:177
  29.4 0.4 %shard_map.57 = (f32[384,128]{1,0:T(8,128)S(1)}, f32[384,128]{1,0:T(8,128)S(1)}, f32[384,128]{1,0:T(8,128)S(1)}, f32[384,128]{1,0:T(8,128)S(1)}, s32[8,128]{1,0:T(8,128)S(1)}) custom-call(s32[1]{0:T(128)S(6)} %copy.8.refs_0_, bf16[384,2048]{1,0:T(8,128)(2,1)S(1)} %get-tuple-element.38.refs_1_.refs_0_, ...), custom_call_target="tpu_custom_call" | custom-call | flops 201326592 | bytes 786432 | tf_op jit(solution)/shard_map/pallas_call | solution.py:177
  29.8 0.6 %collective-permute-start.15 = (f32[384,128]{1,0:T(8,128)S(1)}, f32[384,128]{1,0:T(8,128)S(1)}, u32[]{:S(2)}, u32[]{:S(2)}) collective-permute-start(f32[384,128]{1,0:T(8,128)S(1)} %get-tuple-element.60), channel_id=1, source_target_pairs={{0,1},{1,0},{2,3},{3,2},{4,5},{5,4},{6,7},{7,6},{8,9},{9,8},{10,11... | collective-permute-start | bytes 589832 | tf_op jit(solution)/shard_map/ppermute | solution.py:242
  30.3 0.4 %shard_map.58 = (f32[384,128]{1,0:T(8,128)S(1)}, f32[384,128]{1,0:T(8,128)S(1)}, f32[384,128]{1,0:T(8,128)S(1)}, f32[384,128]{1,0:T(8,128)S(1)}) custom-call(bf16[384,2048]{1,0:T(8,128)(2,1)S(1)} %get-tuple-element.38.refs_1_.refs_0_, bf16[384,2048]{1,0:T(8,128)(2,1)S(1)} %get-tuple-element.39.refs_2_.refs_1_, ...), custom_call_target="tpu_custom_call" | custom-call | flops 201326592 | bytes 786432 | tf_op jit(solution)/shard_map/pallas_call | solution.py:177
  30.7 0.6 %collective-permute-done.9.refs_3_ = bf16[128,512]{1,0:T(8,128)(2,1)S(1)} collective-permute-done((bf16[128,512]{1,0:T(8,128)(2,1)S(1)}, bf16[128,512]{1,0:T(8,128)(2,1)S(1)}, u32[]{:S(2)}, u32[]{:S(2)}) %collective-permute-start.9) | collective-permute-done | bytes 131104 | tf_op jit(solution)/shard_map/ppermute | solution.py:242
  31.3 0.6 %shard_map.59 = (f32[384,128]{1,0:T(8,128)S(1)}, f32[384,128]{1,0:T(8,128)S(1)}, f32[384,128]{1,0:T(8,128)S(1)}, f32[384,128]{1,0:T(8,128)S(1)}) custom-call(bf16[384,2048]{1,0:T(8,128)(2,1)S(1)} %get-tuple-element.38.refs_1_.refs_0_, bf16[384,2048]{1,0:T(8,128)(2,1)S(1)} %get-tuple-element.39.refs_2_.refs_1_, ...), custom_call_target="tpu_custom_call" | custom-call | flops 301989888 | bytes 786432 | tf_op jit(solution)/shard_map/pallas_call | solution.py:177
  32.0 0.4 %collective-permute-done.7.refs_2_ = bf16[128,512]{1,0:T(8,128)(2,1)S(1)} collective-permute-done((bf16[128,512]{1,0:T(8,128)(2,1)S(1)}, bf16[128,512]{1,0:T(8,128)(2,1)S(1)}, u32[]{:S(2)}, u32[]{:S(2)}) %collective-permute-start.7) | collective-permute-done | bytes 131104 | tf_op jit(solution)/shard_map/ppermute | solution.py:242
  32.4 0.4 %shard_map.60 = (f32[384,128]{1,0:T(8,128)S(1)}, f32[384,128]{1,0:T(8,128)S(1)}) custom-call(bf16[384,2048]{1,0:T(8,128)(2,1)S(1)} %get-tuple-element.38.refs_1_.refs_0_, bf16[384,2048]{1,0:T(8,128)(2,1)S(1)} %get-tuple-element.39.refs_2_.refs_1_, bf16[128,512]{1,0:T(8,128)(2,1)S(1)} %collective-permute-done.7.refs_2_, ...), custom_call_target="tpu_custom_call" | custom-call | flops 100663296 | bytes 393216 | tf_op jit(solution)/shard_map/pallas_call | solution.py:177
  32.9 0.5 %collective-permute-done.14.refs_3_ = f32[384,128]{1,0:T(8,128)S(1)} collective-permute-done((f32[384,128]{1,0:T(8,128)S(1)}, f32[384,128]{1,0:T(8,128)S(1)}, u32[]{:S(2)}, u32[]{:S(2)}) %collective-permute-start.14) | collective-permute-done | bytes 196640 | tf_op jit(solution)/shard_map/ppermute | solution.py:242
  33.4 0.9 %shard_map.61.refs_2_ = f32[384,512]{1,0:T(8,128)} custom-call(s32[8,128]{1,0:T(8,128)S(1)} %get-tuple-element.40.limit, f32[384,128]{1,0:T(8,128)S(1)} %get-tuple-element.55.refs_0_, f32[384,128]{1,0:T(8,128)S(1)} %collective-permute-done.13.refs_1_, f32[384,128]{1,0:T(8,128)S(1)} %get-tuple-element.57.refs_2_, ...), custom_call_target="tpu_custom_call" | custom-call | flops 147456 | bytes 1769472 | tf_op jit(solution)/shard_map/pallas_call | solution.py:212
  34.3 0.7 %shard_map.62 = f32[384,512]{1,0:T(8,128)} custom-call(s32[8,128]{1,0:T(8,128)S(1)} %get-tuple-element.40.limit, f32[384,128]{1,0:T(8,128)S(1)} %get-tuple-element.53.refs_0_, f32[384,128]{1,0:T(8,128)S(1)} %collective-permute-done.12.refs_1_, f32[384,512]{1,0:T(8,128)} %shard_map.61.refs_2_), custom_call_target="tpu_custom_call", output_to_operand_aliasing={{}: (3, {})} | custom-call | flops 49152 | bytes 589824 | tf_op jit(solution)/shard_map/pallas_call | solution.py:212
  (20 shorter events, 0.9 us)
Async XLA Ops:
  1.7 9.4 %collective-permute-start.2 = (bf16[128,512]{1,0:T(8,128)(2,1)S(1)}, bf16[128,512]{1,0:T(8,128)(2,1)S(1)}, u32[]{:S(2)}, u32[]{:S(2)}) collective-permute-start(bf16[128,512]{1,0:T(8,128)(2,1)S(1)} %get-tuple-element.35.refs_5_), channel_id=1, source_target_pairs={{0,4},{2,6},{4,8},{6,10},{8,12},{10,14},{12,0},{14,2},{1,5},{3,7},... | collective-permute-start | bytes 393224 | tf_op jit(solution)/shard_map/ppermute | solution.py:242
  4.8 9.2 %collective-permute-start.1 = (bf16[128,512]{1,0:T(8,128)(2,1)S(1)}, bf16[128,512]{1,0:T(8,128)(2,1)S(1)}, u32[]{:S(2)}, u32[]{:S(2)}) collective-permute-start(bf16[128,512]{1,0:T(8,128)(2,1)S(1)} %get-tuple-element.34.refs_3_), channel_id=1, source_target_pairs={{0,4},{2,6},{4,8},{6,10},{8,12},{10,14},{12,0},{14,2},{1,5},{3,7},... | collective-permute-start | bytes 393224 | tf_op jit(solution)/shard_map/ppermute | solution.py:242
  6.4 10.4 %collective-permute-start = (bf16[128,512]{1,0:T(8,128)(2,1)S(1)}, bf16[128,512]{1,0:T(8,128)(2,1)S(1)}, u32[]{:S(2)}, u32[]{:S(2)}) collective-permute-start(bf16[128,512]{1,0:T(8,128)(2,1)S(1)} %get-tuple-element.33.refs_1_), channel_id=1, source_target_pairs={{0,4},{2,6},{4,8},{6,10},{8,12},{10,14},{12,0},{14,2},{1,5},{3,7},... | collective-permute-start | bytes 393224 | tf_op jit(solution)/shard_map/ppermute | solution.py:242
  11.2 7.4 %collective-permute-start.4 = (bf16[128,512]{1,0:T(8,128)(2,1)S(1)}, bf16[128,512]{1,0:T(8,128)(2,1)S(1)}, u32[]{:S(2)}, u32[]{:S(2)}) collective-permute-start(bf16[128,512]{1,0:T(8,128)(2,1)S(1)} %broadcast_select_fusion.3), channel_id=1, source_target_pairs={{0,2},{2,0},{4,6},{6,4},{8,10},{10,8},{12,14},{14,12},{1,3},{3,1},... | collective-permute-start | bytes 393224 | tf_op jit(solution)/shard_map/ppermute | solution.py:242
  13.0 7.2 %collective-permute-start.3 = (bf16[128,512]{1,0:T(8,128)(2,1)S(1)}, bf16[128,512]{1,0:T(8,128)(2,1)S(1)}, u32[]{:S(2)}, u32[]{:S(2)}) collective-permute-start(bf16[128,512]{1,0:T(8,128)(2,1)S(1)} %get-tuple-element.37.refs_7_), channel_id=1, source_target_pairs={{0,4},{2,6},{4,8},{6,10},{8,12},{10,14},{12,0},{14,2},{1,5},{3,7},... | collective-permute-start | bytes 393224 | tf_op jit(solution)/shard_map/ppermute | solution.py:242
  14.0 6.1 %collective-permute-start.10 = (bf16[128,512]{1,0:T(8,128)(2,1)S(1)}, bf16[128,512]{1,0:T(8,128)(2,1)S(1)}, u32[]{:S(2)}, u32[]{:S(2)}) collective-permute-start(bf16[128,512]{1,0:T(8,128)(2,1)S(1)} %broadcast_select_fusion), channel_id=1, source_target_pairs={{0,2},{2,0},{4,6},{6,4},{8,10},{10,8},{12,14},{14,12},{1,3},{3,1},... | collective-permute-start | bytes 393224 | tf_op jit(solution)/shard_map/ppermute | solution.py:242
  16.8 5.7 %collective-permute-start.6 = (bf16[128,512]{1,0:T(8,128)(2,1)S(1)}, bf16[128,512]{1,0:T(8,128)(2,1)S(1)}, u32[]{:S(2)}, u32[]{:S(2)}) collective-permute-start(bf16[128,512]{1,0:T(8,128)(2,1)S(1)} %broadcast_select_fusion.2), channel_id=1, source_target_pairs={{0,2},{2,0},{4,6},{6,4},{8,10},{10,8},{12,14},{14,12},{1,3},{3,1},... | collective-permute-start | bytes 393224 | tf_op jit(solution)/shard_map/ppermute | solution.py:242
  18.6 10.7 %collective-permute-start.5 = (bf16[128,512]{1,0:T(8,128)(2,1)S(1)}, bf16[128,512]{1,0:T(8,128)(2,1)S(1)}, u32[]{:S(2)}, u32[]{:S(2)}) collective-permute-start(bf16[128,512]{1,0:T(8,128)(2,1)S(1)} %collective-permute-done.4.refs_3_), channel_id=1, source_target_pairs={{0,4},{2,6},{4,8},{6,10},{8,12},{10,14},{12,0},{14,2},{1,5},{3,7},... | collective-permute-start | bytes 393224 | tf_op jit(solution)/shard_map/ppermute | solution.py:242
  20.1 9.6 %collective-permute-start.11 = (bf16[128,512]{1,0:T(8,128)(2,1)S(1)}, bf16[128,512]{1,0:T(8,128)(2,1)S(1)}, u32[]{:S(2)}, u32[]{:S(2)}) collective-permute-start(bf16[128,512]{1,0:T(8,128)(2,1)S(1)} %collective-permute-done.10.refs_2_), channel_id=1, source_target_pairs={{0,4},{2,6},{4,8},{6,10},{8,12},{10,14},{12,0},{14,2},{1,5},{3,7},... | collective-permute-start | bytes 393224 | tf_op jit(solution)/shard_map/ppermute | solution.py:242
  20.2 11.2 %collective-permute-start.9 = (bf16[128,512]{1,0:T(8,128)(2,1)S(1)}, bf16[128,512]{1,0:T(8,128)(2,1)S(1)}, u32[]{:S(2)}, u32[]{:S(2)}) collective-permute-start(bf16[128,512]{1,0:T(8,128)(2,1)S(1)} %broadcast_select_fusion.1), channel_id=1, source_target_pairs={{0,2},{2,4},{4,6},{6,8},{8,10},{10,12},{12,14},{14,0},{1,3},{3,5},... | collective-permute-start | bytes 393224 | tf_op jit(solution)/shard_map/ppermute | solution.py:242
  22.5 8.8 %collective-permute-start.8 = (bf16[128,512]{1,0:T(8,128)(2,1)S(1)}, bf16[128,512]{1,0:T(8,128)(2,1)S(1)}, u32[]{:S(2)}, u32[]{:S(2)}) collective-permute-start(bf16[128,512]{1,0:T(8,128)(2,1)S(1)} %collective-permute-done.3.refs_8_), channel_id=1, source_target_pairs={{0,2},{2,0},{4,6},{6,4},{8,10},{10,8},{12,14},{14,12},{1,3},{3,1},... | collective-permute-start | bytes 393224 | tf_op jit(solution)/shard_map/ppermute | solution.py:242
  25.6 6.8 %collective-permute-start.7 = (bf16[128,512]{1,0:T(8,128)(2,1)S(1)}, bf16[128,512]{1,0:T(8,128)(2,1)S(1)}, u32[]{:S(2)}, u32[]{:S(2)}) collective-permute-start(bf16[128,512]{1,0:T(8,128)(2,1)S(1)} %collective-permute-done.6.refs_4_), channel_id=1, source_target_pairs={{0,4},{2,6},{4,8},{6,10},{8,12},{10,14},{12,0},{14,2},{1,5},{3,7},... | collective-permute-start | bytes 393224 | tf_op jit(solution)/shard_map/ppermute | solution.py:242
  29.3 3.6 %collective-permute-start.13 = (f32[384,128]{1,0:T(8,128)S(1)}, f32[384,128]{1,0:T(8,128)S(1)}, u32[]{:S(2)}, u32[]{:S(2)}) collective-permute-start(f32[384,128]{1,0:T(8,128)S(1)} %get-tuple-element.56), channel_id=1, source_target_pairs={{0,1},{1,0},{2,3},{3,2},{4,5},{5,4},{6,7},{7,6},{8,9},{9,8},{10,11... | collective-permute-start | bytes 589832 | tf_op jit(solution)/shard_map/ppermute | solution.py:242
  29.8 3.2 %collective-permute-start.15 = (f32[384,128]{1,0:T(8,128)S(1)}, f32[384,128]{1,0:T(8,128)S(1)}, u32[]{:S(2)}, u32[]{:S(2)}) collective-permute-start(f32[384,128]{1,0:T(8,128)S(1)} %get-tuple-element.60), channel_id=1, source_target_pairs={{0,1},{1,0},{2,3},{3,2},{4,5},{5,4},{6,7},{7,6},{8,9},{9,8},{10,11... | collective-permute-start | bytes 589832 | tf_op jit(solution)/shard_map/ppermute | solution.py:242
  31.9 1.5 %collective-permute-start.14 = (f32[384,128]{1,0:T(8,128)S(1)}, f32[384,128]{1,0:T(8,128)S(1)}, u32[]{:S(2)}, u32[]{:S(2)}) collective-permute-start(f32[384,128]{1,0:T(8,128)S(1)} %get-tuple-element.58), channel_id=1, source_target_pairs={{0,1},{1,0},{2,3},{3,2},{4,5},{5,4},{6,7},{7,6},{8,9},{9,8},{10,11... | collective-permute-start | bytes 589832 | tf_op jit(solution)/shard_map/ppermute | solution.py:242
  32.8 1.5 %collective-permute-start.12 = (f32[384,128]{1,0:T(8,128)S(1)}, f32[384,128]{1,0:T(8,128)S(1)}, u32[]{:S(2)}, u32[]{:S(2)}) collective-permute-start(f32[384,128]{1,0:T(8,128)S(1)} %get-tuple-element.54), channel_id=1, source_target_pairs={{0,1},{1,0},{2,3},{3,2},{4,5},{5,4},{6,7},{7,6},{8,9},{9,8},{10,11... | collective-permute-start | bytes 589832 | tf_op jit(solution)/shard_map/ppermute | solution.py:242

commit v12 on v11

--- a/solution.py
+++ b/solution.py
@@ -8,11 +8,12 @@
 from jax.sharding import PartitionSpec as P
 
 STEPS = 4
-KINDS = "UUUT"
-PARTS = (4, 4, 4, 4)
-CHAIN = ("b2", "b1", "b3 o0", "t0")
-ORDER = ("B0", "B1", "B2", "B3", "C2", "C1", "C0", "E2", "E1", "E0", "R3", "C3")
-TIES = {"B3": "B2", "C3": "C0", "R3": "C2"}
+KINDS = "UUT"
+PARTS = (4, 5, 7)
+CHAIN = ("b0", "b2 o1", "t1")
+ORDER = ("B0", "B1", "B2", "C0", "C1", "E0", "E1", "R2", "C2")
+TIES = {"B2": "B0", "C2": "E0"}
+EARLY = "C0"
 CHUNKS = len(PARTS)
 VMEM_BYTES = 16 * 1024 * 1024
 
@@ -91,7 +92,7 @@
     )(in_hbm(queries), in_hbm(precond), in_hbm(rank))
 
 
-def scores_kernel(pieces, fresh, loading, counted, *refs):
+def scores_kernel(pieces, fresh, loading, counted, sides, *refs):
     count = len(fresh)
     if counted:
         valid, *refs, limit = refs
@@ -111,8 +112,9 @@
     else:
         other, mine, *refs = refs
         stores = other, mine
-    outs = refs[-2 * count:]
-    carried = refs[-2 * count - 2 * (count - sum(fresh)):-2 * count]
+    count_out = len(sides) * count
+    outs = refs[-count_out:]
+    carried = refs[-count_out - len(sides) * (count - sum(fresh)):-count_out]
     cuts = cuts_of(other.shape[1])
     stacks = []
     for n, targets in pieces:
@@ -124,13 +126,14 @@
             values.append(value)
         stacked = values[0] if len(values) == 1 else jnp.concatenate(values, axis=0)
         stacks.append((n, [which for which, _, _ in targets], stacked))
-    for side, store in enumerate(stores):
+    for at_side, side in enumerate(sides):
+        store = stores[side]
         if loading:
             loads[side].wait()
         sums, at = {}, 0
         for i, new in enumerate(fresh):
-            sums[i] = None if new else carried[at + side][...]
-            at += 0 if new else 2
+            sums[i] = None if new else carried[at + at_side][...]
+            at += 0 if new else len(sides)
         for n, whiches, stacked in stacks:
             part = product(store[:, cuts[n]], stacked)
             columns = stacked.shape[0] // len(whiches)
@@ -138,10 +141,10 @@
                 here = part[:, k * columns:(k + 1) * columns]
                 sums[i] = here if sums[i] is None else sums[i] + here
         for i in range(count):
-            outs[2 * i + side][...] = sums[i]
-
-
-def more_scores(stores, pieces, carries, valid=None):
+            outs[len(sides) * i + at_side][...] = sums[i]
+
+
+def more_scores(stores, pieces, carries, valid=None, sides=(0, 1)):
     operands, placed = [], []
 
     def place(block):
@@ -163,7 +166,7 @@
     columns = operands[0].shape[0]
     fresh = tuple(carry is None for carry in carries)
     first = [in_hbm(stores)] if loading else list(stores)
-    operands += [side for carry in carries if carry for side in carry]
+    operands += [carry[side] for carry in carries if carry for side in sides]
     specs = [far_spec()] if loading else [whole_spec()] * 2
     total = jax.ShapeDtypeStruct((half, columns), jnp.float32)
     more = []
@@ -173,9 +176,9 @@
     if valid is not None:
         first, more = [valid] + first, more + [jax.ShapeDtypeStruct((8, columns), jnp.int32)]
         specs = [pl.BlockSpec(memory_space=pltpu.SMEM)] + specs
-    count = 2 * len(carries)
+    count = len(sides) * len(carries)
     outs = pl.pallas_call(
-        functools.partial(scores_kernel, tuple(placed), fresh, loading, valid is not None),
+        functools.partial(scores_kernel, tuple(placed), fresh, loading, valid is not None, sides),
         out_shape=[total] * count + more,
         in_specs=specs + [whole_spec()] * len(operands),
         out_specs=[whole_spec()] * (count + len(more)),
@@ -183,7 +186,7 @@
         compiler_params=params(),
         cost_estimate=cost(flops, 4 * half * columns * count),
     )(*first, *operands)
-    totals = [(outs[2 * i], outs[2 * i + 1]) for i in range(len(carries))]
+    totals = [tuple(outs[i:i + len(sides)]) for i in range(0, count, len(sides))]
     if valid is not None:
         return totals + [outs[-1]]
     return totals + ([tuple(outs[count:])] if loading else [])
@@ -249,6 +252,8 @@
         return jnp.where(odd, at_odd, at_even)
 
     own = prepare(queries, precond[None, :], query_rank)
+    first, stores = more_scores(store, [(n, [(0, own[n])]) for n in range(CHUNKS)], [None])
+    own_pair = exchanged(first)
     moved = {}
 
     def tied(name, block):
@@ -267,6 +272,8 @@
             move(step, own[n], swap)
         elif kind == "C":
             block = two_back[n] if KINDS[n] != "U" else by_parity(own[n], two_back[n])
+            if step == EARLY:
+                block = after(block, first[1])
             move(step, block, swap)
         elif kind == "E":
             move(step, moved[f"C{n}"], even_ahead if KINDS[n] == "I" else ahead)
@@ -282,12 +289,9 @@
             direct = moved[f"R{n}"]
             one_back[n], three_back[n] = (swapped, direct), (direct, swapped)
 
-    first, two, stores = more_scores(
-        store,
-        [(n, [(0, own[n]), (1, two_back[n])]) for n in range(CHUNKS)],
-        [None, None],
-    )
-    own_pair, two_pair = exchanged(first), exchanged(two)
+    [two] = more_scores(stores, [(n, [(0, two_back[n])]) for n in range(CHUNKS)], [None])
+    two_pair = exchanged(two)
+    limited = after(valid_rows, two[1])
     one = three = one_pair = None
     todo = set(range(CHUNKS))
     for group in CHAIN:
@@ -297,17 +301,19 @@
             blocks = one_back[n], three_back[n]
             pieces.append((n, [(part, *blocks[part]) for part in parts]))
             todo -= {n} if 0 in parts else set()
-        if one_pair is None:
-            if one is None:
-                one, three, limit = more_scores(stores, pieces, [one, three], valid_rows)
-            else:
-                one, three = more_scores(stores, pieces, [one, three])
-            one_pair = None if todo else exchanged(one)
+        if one is None:
+            one, three, limit = more_scores(stores, pieces, [one, three], limited)
+        elif one_pair is None:
+            one, three = more_scores(stores, pieces, [one, three])
         else:
             pieces = [(n, [(0, *blocks) for _, *blocks in targets]) for n, targets in pieces]
-            [three] = more_scores(stores, pieces, [three])
-    out = finish(limit, [own_pair, one_pair, two_pair], (0, 1, 2), STEPS)
-    return finish(limit, [exchanged(three)], (3,), STEPS, out)
+            [[theirs]] = more_scores(stores, pieces, [three], sides=(0,))
+            [[ours]] = more_scores(stores, pieces, [three], sides=(1,))
+            three = theirs, ours
+        if one_pair is None and not todo:
+            one_pair = exchanged(one)
+    out = finish(limit, [own_pair, two_pair], (0, 2), STEPS)
+    return finish(limit, [one_pair, exchanged(three)], (1, 3), STEPS, out)
 
 
 def solution(mesh):

time: 35.2 us -> 35.8 us (1.017)
  waiting for transfers between devices: 8.55 us -> 10.6 us
  starting transfers between devices: 17.2 us -> 15.3 us
  Pallas kernels: 8.47 us -> 8.97 us
    ppermute x16 -> x13, waiting for transfers between devices: 8.55 us -> 10.6 us  [send(): return lax.ppermute(block, axis, route)]
    ppermute x16 -> x13, starting transfers between devices: 17.2 us -> 15.3 us  [send(): return lax.ppermute(block, axis, route)]
    pallas_call x5 -> x6, Pallas kernels: 5.16 us -> 5.79 us  [more_scores(): pl.pallas_call(functools.partial(scores_kernel, tuple(placed), fresh, loa...]
  transfers between devices with their start and end apart: 16 -> 13, of which waited for: 8 -> 9; matrix products, arithmetic and copies ran while one was open for 0% -> 0% of each run, Pallas kernels for 17% -> 18%
where the time goes in v12:
time: 35.8 us; the launch traced here: 35.7 us
  starting transfers between devices  15.3 us (43%)
  waiting for transfers between devices  10.6 us (30%)
  Pallas kernels  8.97 us (25%)
  between operations  0.78 us (2%)
    ppermute x13, starting transfers between devices, send(): return lax.ppermute(block, axis, route)  15.3 us
    ppermute x13, waiting for transfers between devices, send(): return lax.ppermute(block, axis, route)  10.6 us
    pallas_call x6, Pallas kernels, more_scores(): pl.pallas_call(functools.partial(scores_kernel, tuple(placed), fresh, loa...  5.79 us
    pallas_call x2, Pallas kernels, finish(): pl.pallas_call(functools.partial(finish_kernel, places), out_shape=pltpu....  1.61 us
    pallas_call x1, Pallas kernels, prepare(): pl.pallas_call(prepare_kernel, out_shape=shapes, in_specs=[far_spec()] *...  1.58 us
  transfers between devices with their start and end apart: 13, of which 9 were waited for; matrix products, arithmetic and copies ran while one was open for 0% of the time, Pallas kernels for 18%

profile of v12, /device:TPU:0, one launch (start us, length us, event | category | flops | bytes accessed | tf_op | source)
XLA Modules:
  0.0 35.7 jit_solution(13278545443699327829)
XLA Ops:
  0.0 1.6 %shard_map.55 = (bf16[128,512]{1,0:T(8,128)(2,1)S(1)}, bf16[128,640]{1,0:T(8,128)(2,1)S(1)}, bf16[128,896]{1,0:T(8,128)(2,1)S(1)}) custom-call(bf16[128,2048]{1,0:T(8,128)(2,1)} %queries.1, f32[1,2048]{1,0:T(1,128)} %bitcast.1, s32[1,128]{1,0:T(1,128)} %rank.1), custom_call_target="tpu_custom_call" | custom-call | flops 67108864 | bytes 1048576 | tf_op jit(solution)/shard_map/pallas_call | solution.py:79
  1.6 3.1 %collective-permute-start = (bf16[128,512]{1,0:T(8,128)(2,1)S(1)}, bf16[128,512]{1,0:T(8,128)(2,1)S(1)}, u32[]{:S(2)}, u32[]{:S(2)}) collective-permute-start(bf16[128,512]{1,0:T(8,128)(2,1)S(1)} %get-tuple-element.27.refs_1_), channel_id=1, source_target_pairs={{0,4},{2,6},{4,8},{6,10},{8,12},{10,14},{12,0},{14,2},{1,5},{3,7},... | collective-permute-start | bytes 393224 | tf_op jit(solution)/shard_map/ppermute | solution.py:245
  4.7 1.6 %collective-permute-start.1 = (bf16[128,640]{1,0:T(8,128)(2,1)S(1)}, bf16[128,640]{1,0:T(8,128)(2,1)S(1)}, u32[]{:S(2)}, u32[]{:S(2)}) collective-permute-start(bf16[128,640]{1,0:T(8,128)(2,1)S(1)} %get-tuple-element.28.refs_2_), channel_id=1, source_target_pairs={{0,4},{2,6},{4,8},{6,10},{8,12},{10,14},{12,0},{14,2},{1,5},{3,7},... | collective-permute-start | bytes 491528 | tf_op jit(solution)/shard_map/ppermute | solution.py:245
  6.2 3.0 %shard_map.56 = (f32[384,128]{1,0:T(8,128)S(1)}, f32[384,128]{1,0:T(8,128)S(1)}, bf16[384,2048]{1,0:T(8,128)(2,1)S(1)}, bf16[384,2048]{1,0:T(8,128)(2,1)S(1)}) custom-call(bf16[768,2048]{1,0:T(8,128)(2,1)} %refs_0_.1, bf16[128,512]{1,0:T(8,128)(2,1)S(1)} %get-tuple-element.27.refs_1_, bf16[128,640]{1,0:T(8,128)(2,1)S(1)} %get-tuple-element.28.refs_2_, ...), custom_call_target="tpu_custom_call" | custom-call | flops 402653184 | bytes 393216 | tf_op jit(solution)/shard_map/pallas_call | solution.py:180
  9.2 1.8 %collective-permute-done.refs_2_ = bf16[128,512]{1,0:T(8,128)(2,1)S(1)} collective-permute-done((bf16[128,512]{1,0:T(8,128)(2,1)S(1)}, bf16[128,512]{1,0:T(8,128)(2,1)S(1)}, u32[]{:S(2)}, u32[]{:S(2)}) %collective-permute-start) | collective-permute-done | bytes 131104 | tf_op jit(solution)/shard_map/ppermute | solution.py:245
  11.1 1.8 %collective-permute-start.3 = (bf16[128,512]{1,0:T(8,128)(2,1)S(1)}, bf16[128,512]{1,0:T(8,128)(2,1)S(1)}, u32[]{:S(2)}, u32[]{:S(2)}) collective-permute-start(bf16[128,512]{1,0:T(8,128)(2,1)S(1)} %broadcast_select_fusion.2), channel_id=1, source_target_pairs={{0,2},{2,0},{4,6},{6,4},{8,10},{10,8},{12,14},{14,12},{1,3},{3,1},... | collective-permute-start | bytes 393224 | tf_op jit(solution)/shard_map/ppermute | solution.py:245
  12.8 0.9 %collective-permute-done.1.refs_3_ = bf16[128,640]{1,0:T(8,128)(2,1)S(1)} collective-permute-done((bf16[128,640]{1,0:T(8,128)(2,1)S(1)}, bf16[128,640]{1,0:T(8,128)(2,1)S(1)}, u32[]{:S(2)}, u32[]{:S(2)}) %collective-permute-start.1) | collective-permute-done | bytes 163872 | tf_op jit(solution)/shard_map/ppermute | solution.py:245
  13.7 1.6 %collective-permute-start.7 = (bf16[128,640]{1,0:T(8,128)(2,1)S(1)}, bf16[128,640]{1,0:T(8,128)(2,1)S(1)}, u32[]{:S(2)}, u32[]{:S(2)}) collective-permute-start(bf16[128,640]{1,0:T(8,128)(2,1)S(1)} %broadcast_select_fusion.1), channel_id=1, source_target_pairs={{0,2},{2,0},{4,6},{6,4},{8,10},{10,8},{12,14},{14,12},{1,3},{3,1},... | collective-permute-start | bytes 491528 | tf_op jit(solution)/shard_map/ppermute | solution.py:245
  15.3 1.3 %collective-permute-done.3.refs_3_ = bf16[128,512]{1,0:T(8,128)(2,1)S(1)} collective-permute-done((bf16[128,512]{1,0:T(8,128)(2,1)S(1)}, bf16[128,512]{1,0:T(8,128)(2,1)S(1)}, u32[]{:S(2)}, u32[]{:S(2)}) %collective-permute-start.3) | collective-permute-done | bytes 131104 | tf_op jit(solution)/shard_map/ppermute | solution.py:245
  16.5 1.7 %collective-permute-start.4 = (bf16[128,512]{1,0:T(8,128)(2,1)S(1)}, bf16[128,512]{1,0:T(8,128)(2,1)S(1)}, u32[]{:S(2)}, u32[]{:S(2)}) collective-permute-start(bf16[128,512]{1,0:T(8,128)(2,1)S(1)} %collective-permute-done.3.refs_3_), channel_id=1, source_target_pairs={{0,4},{2,6},{4,8},{6,10},{8,12},{10,14},{12,0},{14,2},{1,5},{3,7},... | collective-permute-start | bytes 393224 | tf_op jit(solution)/shard_map/ppermute | solution.py:245
  18.2 1.0 %collective-permute-done.2.refs_4_ = bf16[128,896]{1,0:T(8,128)(2,1)S(1)} collective-permute-done((bf16[128,896]{1,0:T(8,128)(2,1)S(1)}, bf16[128,896]{1,0:T(8,128)(2,1)S(1)}, u32[]{:S(2)}, u32[]{:S(2)}) %collective-permute-start.2) | collective-permute-done | bytes 229408 | tf_op jit(solution)/shard_map/ppermute | solution.py:245
  19.2 2.2 %collective-permute-start.6 = (bf16[128,896]{1,0:T(8,128)(2,1)S(1)}, bf16[128,896]{1,0:T(8,128)(2,1)S(1)}, u32[]{:S(2)}, u32[]{:S(2)}) collective-permute-start(bf16[128,896]{1,0:T(8,128)(2,1)S(1)} %broadcast_select_fusion), channel_id=1, source_target_pairs={{0,2},{2,4},{4,6},{6,8},{8,10},{10,12},{12,14},{14,0},{1,3},{3,5},... | collective-permute-start | bytes 688136 | tf_op jit(solution)/shard_map/ppermute | solution.py:245
  21.4 1.9 %collective-permute-done.4.refs_4_ = bf16[128,512]{1,0:T(8,128)(2,1)S(1)} collective-permute-done((bf16[128,512]{1,0:T(8,128)(2,1)S(1)}, bf16[128,512]{1,0:T(8,128)(2,1)S(1)}, u32[]{:S(2)}, u32[]{:S(2)}) %collective-permute-start.4) | collective-permute-done | bytes 131104 | tf_op jit(solution)/shard_map/ppermute | solution.py:245
  23.3 2.6 %collective-permute-start.5 = (bf16[128,896]{1,0:T(8,128)(2,1)S(1)}, bf16[128,896]{1,0:T(8,128)(2,1)S(1)}, u32[]{:S(2)}, u32[]{:S(2)}) collective-permute-start(bf16[128,896]{1,0:T(8,128)(2,1)S(1)} %collective-permute-done.2.refs_4_), channel_id=1, source_target_pairs={{0,2},{2,0},{4,6},{6,4},{8,10},{10,8},{12,14},{14,12},{1,3},{3,1},... | collective-permute-start | bytes 688136 | tf_op jit(solution)/shard_map/ppermute | solution.py:245
  26.6 1.0 %shard_map.57 = (f32[384,128]{1,0:T(8,128)S(1)}, f32[384,128]{1,0:T(8,128)S(1)}) custom-call(bf16[384,2048]{1,0:T(8,128)(2,1)S(1)} %get-tuple-element.30.refs_0_.refs_1_, bf16[384,2048]{1,0:T(8,128)(2,1)S(1)} %get-tuple-element.31.refs_1_.refs_2_, bf16[128,512]{1,0:T(8,128)(2,1)S(1)} %collective-permute-done.refs_2_, ...), custom_call_target="tpu_custom_call" | custom-call | flops 402653184 | bytes 393216 | tf_op jit(solution)/shard_map/pallas_call | solution.py:180
  27.6 0.6 %collective-permute-start.12 = (f32[384,128]{1,0:T(8,128)S(1)}, f32[384,128]{1,0:T(8,128)S(1)}, u32[]{:S(2)}, u32[]{:S(2)}) collective-permute-start(f32[384,128]{1,0:T(8,128)S(1)} %get-tuple-element.48), channel_id=1, source_target_pairs={{0,1},{1,0},{2,3},{3,2},{4,5},{5,4},{6,7},{7,6},{8,9},{9,8},{10,11... | collective-permute-start | bytes 589832 | tf_op jit(solution)/shard_map/ppermute | solution.py:245
  28.2 0.4 %shard_map.58 = (f32[384,128]{1,0:T(8,128)S(1)}, f32[384,128]{1,0:T(8,128)S(1)}, f32[384,128]{1,0:T(8,128)S(1)}, f32[384,128]{1,0:T(8,128)S(1)}, s32[8,128]{1,0:T(8,128)S(1)}) custom-call(s32[1]{0:T(128)S(6)} %copy.8.refs_0_, bf16[384,2048]{1,0:T(8,128)(2,1)S(1)} %get-tuple-element.30.refs_0_.refs_1_, ...), custom_call_target="tpu_custom_call" | custom-call | flops 201326592 | bytes 786432 | tf_op jit(solution)/shard_map/pallas_call | solution.py:180
  28.6 1.2 %collective-permute-done.6.refs_3_ = bf16[128,896]{1,0:T(8,128)(2,1)S(1)} collective-permute-done((bf16[128,896]{1,0:T(8,128)(2,1)S(1)}, bf16[128,896]{1,0:T(8,128)(2,1)S(1)}, u32[]{:S(2)}, u32[]{:S(2)}) %collective-permute-start.6) | collective-permute-done | bytes 229408 | tf_op jit(solution)/shard_map/ppermute | solution.py:245
  29.8 1.6 %collective-permute-done.5.refs_2_ = bf16[128,896]{1,0:T(8,128)(2,1)S(1)} collective-permute-done((bf16[128,896]{1,0:T(8,128)(2,1)S(1)}, bf16[128,896]{1,0:T(8,128)(2,1)S(1)}, u32[]{:S(2)}, u32[]{:S(2)}) %collective-permute-start.5) | collective-permute-done | bytes 229408 | tf_op jit(solution)/shard_map/ppermute | solution.py:245
  31.4 0.9 %shard_map.59 = (f32[384,128]{1,0:T(8,128)S(1)}, f32[384,128]{1,0:T(8,128)S(1)}, f32[384,128]{1,0:T(8,128)S(1)}, f32[384,128]{1,0:T(8,128)S(1)}) custom-call(bf16[384,2048]{1,0:T(8,128)(2,1)S(1)} %get-tuple-element.30.refs_0_.refs_1_, bf16[384,2048]{1,0:T(8,128)(2,1)S(1)} %get-tuple-element.31.refs_1_.refs_2_, ...), custom_call_target="tpu_custom_call" | custom-call | flops 478150656 | bytes 786432 | tf_op jit(solution)/shard_map/pallas_call | solution.py:180
  32.3 0.8 %collective-permute-done.9.refs_2_ = bf16[128,640]{1,0:T(8,128)(2,1)S(1)} collective-permute-done((bf16[128,640]{1,0:T(8,128)(2,1)S(1)}, bf16[128,640]{1,0:T(8,128)(2,1)S(1)}, u32[]{:S(2)}, u32[]{:S(2)}) %collective-permute-start.9) | collective-permute-done | bytes 163872 | tf_op jit(solution)/shard_map/ppermute | solution.py:245
  33.5 0.8 %shard_map.62.refs_4_ = f32[384,512]{1,0:T(8,128)} custom-call(s32[8,128]{1,0:T(8,128)S(1)} %get-tuple-element.37.limit, f32[384,128]{1,0:T(8,128)S(1)} %get-tuple-element.35.refs_0_, f32[384,128]{1,0:T(8,128)S(1)} %collective-permute-done.11.refs_1_, f32[384,128]{1,0:T(8,128)S(1)} %get-tuple-element.33.refs_2_, f32[384,128]{1,0:T(8,128)S(1)} %collective-permute-done.12.refs_3_), custom_call_target="tpu_custom_call" | custom-call | flops 98304 | bytes 1179648 | tf_op jit(solution)/shard_map/pallas_call | solution.py:215
  34.3 0.3 shard_map.60.refs_2_
  34.9 0.8 %shard_map.63 = f32[384,512]{1,0:T(8,128)} custom-call(s32[8,128]{1,0:T(8,128)S(1)} %get-tuple-element.37.limit, f32[384,128]{1,0:T(8,128)S(1)} %get-tuple-element.43.refs_0_, f32[384,128]{1,0:T(8,128)S(1)} %collective-permute-done.8.refs_1_, f32[384,128]{1,0:T(8,128)S(1)} %shard_map.60.refs_2_, ...), custom_call_target="tpu_custom_call", output_to_operand_aliasing={{}: (5, {})} | custom-call | flops 98304 | bytes 1179648 | tf_op jit(solution)/shard_map/pallas_call | solution.py:215
  (14 shorter events, 0.8 us)
Async XLA Ops:
  1.6 9.4 %collective-permute-start = (bf16[128,512]{1,0:T(8,128)(2,1)S(1)}, bf16[128,512]{1,0:T(8,128)(2,1)S(1)}, u32[]{:S(2)}, u32[]{:S(2)}) collective-permute-start(bf16[128,512]{1,0:T(8,128)(2,1)S(1)} %get-tuple-element.27.refs_1_), channel_id=1, source_target_pairs={{0,4},{2,6},{4,8},{6,10},{8,12},{10,14},{12,0},{14,2},{1,5},{3,7},... | collective-permute-start | bytes 393224 | tf_op jit(solution)/shard_map/ppermute | solution.py:245
  4.7 9.0 %collective-permute-start.1 = (bf16[128,640]{1,0:T(8,128)(2,1)S(1)}, bf16[128,640]{1,0:T(8,128)(2,1)S(1)}, u32[]{:S(2)}, u32[]{:S(2)}) collective-permute-start(bf16[128,640]{1,0:T(8,128)(2,1)S(1)} %get-tuple-element.28.refs_2_), channel_id=1, source_target_pairs={{0,4},{2,6},{4,8},{6,10},{8,12},{10,14},{12,0},{14,2},{1,5},{3,7},... | collective-permute-start | bytes 491528 | tf_op jit(solution)/shard_map/ppermute | solution.py:245
  11.0 8.2 %collective-permute-start.2 = (bf16[128,896]{1,0:T(8,128)(2,1)S(1)}, bf16[128,896]{1,0:T(8,128)(2,1)S(1)}, u32[]{:S(2)}, u32[]{:S(2)}) collective-permute-start(bf16[128,896]{1,0:T(8,128)(2,1)S(1)} %get-tuple-element.32.refs_3_), channel_id=1, source_target_pairs={{0,4},{2,6},{4,8},{6,10},{8,12},{10,14},{12,0},{14,2},{1,5},{3,7},... | collective-permute-start | bytes 688136 | tf_op jit(solution)/shard_map/ppermute | solution.py:245
  11.1 5.5 %collective-permute-start.3 = (bf16[128,512]{1,0:T(8,128)(2,1)S(1)}, bf16[128,512]{1,0:T(8,128)(2,1)S(1)}, u32[]{:S(2)}, u32[]{:S(2)}) collective-permute-start(bf16[128,512]{1,0:T(8,128)(2,1)S(1)} %broadcast_select_fusion.2), channel_id=1, source_target_pairs={{0,2},{2,0},{4,6},{6,4},{8,10},{10,8},{12,14},{14,12},{1,3},{3,1},... | collective-permute-start | bytes 393224 | tf_op jit(solution)/shard_map/ppermute | solution.py:245
  13.7 12.2 %collective-permute-start.7 = (bf16[128,640]{1,0:T(8,128)(2,1)S(1)}, bf16[128,640]{1,0:T(8,128)(2,1)S(1)}, u32[]{:S(2)}, u32[]{:S(2)}) collective-permute-start(bf16[128,640]{1,0:T(8,128)(2,1)S(1)} %broadcast_select_fusion.1), channel_id=1, source_target_pairs={{0,2},{2,0},{4,6},{6,4},{8,10},{10,8},{12,14},{14,12},{1,3},{3,1},... | collective-permute-start | bytes 491528 | tf_op jit(solution)/shard_map/ppermute | solution.py:245
  16.5 6.8 %collective-permute-start.4 = (bf16[128,512]{1,0:T(8,128)(2,1)S(1)}, bf16[128,512]{1,0:T(8,128)(2,1)S(1)}, u32[]{:S(2)}, u32[]{:S(2)}) collective-permute-start(bf16[128,512]{1,0:T(8,128)(2,1)S(1)} %collective-permute-done.3.refs_3_), channel_id=1, source_target_pairs={{0,4},{2,6},{4,8},{6,10},{8,12},{10,14},{12,0},{14,2},{1,5},{3,7},... | collective-permute-start | bytes 393224 | tf_op jit(solution)/shard_map/ppermute | solution.py:245
  19.2 10.6 %collective-permute-start.6 = (bf16[128,896]{1,0:T(8,128)(2,1)S(1)}, bf16[128,896]{1,0:T(8,128)(2,1)S(1)}, u32[]{:S(2)}, u32[]{:S(2)}) collective-permute-start(bf16[128,896]{1,0:T(8,128)(2,1)S(1)} %broadcast_select_fusion), channel_id=1, source_target_pairs={{0,2},{2,4},{4,6},{6,8},{8,10},{10,12},{12,14},{14,0},{1,3},{3,5},... | collective-permute-start | bytes 688136 | tf_op jit(solution)/shard_map/ppermute | solution.py:245
  23.3 8.0 %collective-permute-start.5 = (bf16[128,896]{1,0:T(8,128)(2,1)S(1)}, bf16[128,896]{1,0:T(8,128)(2,1)S(1)}, u32[]{:S(2)}, u32[]{:S(2)}) collective-permute-start(bf16[128,896]{1,0:T(8,128)(2,1)S(1)} %collective-permute-done.2.refs_4_), channel_id=1, source_target_pairs={{0,2},{2,0},{4,6},{6,4},{8,10},{10,8},{12,14},{14,12},{1,3},{3,1},... | collective-permute-start | bytes 688136 | tf_op jit(solution)/shard_map/ppermute | solution.py:245
  25.9 7.1 %collective-permute-start.9 = (bf16[128,640]{1,0:T(8,128)(2,1)S(1)}, bf16[128,640]{1,0:T(8,128)(2,1)S(1)}, u32[]{:S(2)}, u32[]{:S(2)}) collective-permute-start(bf16[128,640]{1,0:T(8,128)(2,1)S(1)} %collective-permute-done.7.refs_4_), channel_id=1, source_target_pairs={{0,4},{2,6},{4,8},{6,10},{8,12},{10,14},{12,0},{14,2},{1,5},{3,7},... | collective-permute-start | bytes 491528 | tf_op jit(solution)/shard_map/ppermute | solution.py:245
  25.9 7.5 %collective-permute-start.11 = (f32[384,128]{1,0:T(8,128)S(1)}, f32[384,128]{1,0:T(8,128)S(1)}, u32[]{:S(2)}, u32[]{:S(2)}) collective-permute-start(f32[384,128]{1,0:T(8,128)S(1)} %get-tuple-element.47), channel_id=1, source_target_pairs={{0,1},{1,0},{2,3},{3,2},{4,5},{5,4},{6,7},{7,6},{8,9},{9,8},{10,11... | collective-permute-start | bytes 589832 | tf_op jit(solution)/shard_map/ppermute | solution.py:245
  27.6 5.9 %collective-permute-start.12 = (f32[384,128]{1,0:T(8,128)S(1)}, f32[384,128]{1,0:T(8,128)S(1)}, u32[]{:S(2)}, u32[]{:S(2)}) collective-permute-start(f32[384,128]{1,0:T(8,128)S(1)} %get-tuple-element.48), channel_id=1, source_target_pairs={{0,1},{1,0},{2,3},{3,2},{4,5},{5,4},{6,7},{7,6},{8,9},{9,8},{10,11... | collective-permute-start | bytes 589832 | tf_op jit(solution)/shard_map/ppermute | solution.py:245
  32.2 2.4 %collective-permute-start.8 = (f32[384,128]{1,0:T(8,128)S(1)}, f32[384,128]{1,0:T(8,128)S(1)}, u32[]{:S(2)}, u32[]{:S(2)}) collective-permute-start(f32[384,128]{1,0:T(8,128)S(1)} %get-tuple-element.44), channel_id=1, source_target_pairs={{0,1},{1,0},{2,3},{3,2},{4,5},{5,4},{6,7},{7,6},{8,9},{9,8},{10,11... | collective-permute-start | bytes 589832 | tf_op jit(solution)/shard_map/ppermute | solution.py:245
  33.4 1.5 %collective-permute-start.10 = (f32[384,128]{1,0:T(8,128)S(1)}, f32[384,128]{1,0:T(8,128)S(1)}, u32[]{:S(2)}, u32[]{:S(2)}) collective-permute-start(f32[384,128]{1,0:T(8,128)S(1)} %shard_map.61), channel_id=1, source_target_pairs={{0,1},{1,0},{2,3},{3,2},{4,5},{5,4},{6,7},{7,6},{8,9},{9,8},{10,11... | collective-permute-start | bytes 589832 | tf_op jit(solution)/shard_map/ppermute | solution.py:245

commit v13 on v12

--- a/solution.py
+++ b/solution.py
@@ -8,12 +8,12 @@
 from jax.sharding import PartitionSpec as P
 
 STEPS = 4
-KINDS = "UUT"
-PARTS = (4, 5, 7)
-CHAIN = ("b0", "b2 o1", "t1")
-ORDER = ("B0", "B1", "B2", "C0", "C1", "E0", "E1", "R2", "C2")
-TIES = {"B2": "B0", "C2": "E0"}
-EARLY = "C0"
+KINDS = "VV"
+PARTS = (9, 7)
+CHAIN = ("b0", "o1", "t1")
+ORDER = ("B0", "A0", "B1", "A1", "Z0", "R0", "Z1", "R1")
+TIES = {}
+EARLY = "R0"
 CHUNKS = len(PARTS)
 VMEM_BYTES = 16 * 1024 * 1024
 
@@ -257,7 +257,8 @@
     moved = {}
 
     def tied(name, block):
-        return after(block, *(moved[key] for key in TIES.get(name, "").split()))
+        earlier = [first[1]] if name == EARLY else []
+        return after(block, *earlier, *(moved[key] for key in TIES.get(name, "").split()))
 
     def move(name, block, route):
         moved[name] = send(tied(name, block), route)
@@ -272,14 +273,18 @@
             move(step, own[n], swap)
         elif kind == "C":
             block = two_back[n] if KINDS[n] != "U" else by_parity(own[n], two_back[n])
-            if step == EARLY:
-                block = after(block, first[1])
             move(step, block, swap)
+        elif kind == "Z":
+            move(step, moved[f"A{n}"], even_ahead)
         elif kind == "E":
             move(step, moved[f"C{n}"], even_ahead if KINDS[n] == "I" else ahead)
         else:
-            move(step, by_parity(own[n], two_back[n]), one_ahead)
+            block = two_back[n] if KINDS[n] == "V" else by_parity(own[n], two_back[n])
+            move(step, block, one_ahead)
     for n, kind in enumerate(KINDS):
+        if kind == "V":
+            one_back[n], three_back[n] = (moved[f"Z{n}"], moved[f"A{n}"]), (moved[f"R{n}"],)
+            continue
         swapped = moved[f"C{n}"]
         if kind == "U":
             one_back[n], three_back[n] = (swapped,), (moved[f"E{n}"],)

time: 35.8 us -> 42.2 us (1.18)
  starting transfers between devices: 15.3 us -> 23.4 us
  waiting for transfers between devices: 10.6 us -> 9.06 us
    ppermute x13 -> x12, starting transfers between devices: 15.3 us -> 23.4 us  [send(): return lax.ppermute(block, axis, route)]
    ppermute x13 -> x12, waiting for transfers between devices: 10.6 us -> 9.06 us  [send(): return lax.ppermute(block, axis, route)]
  transfers between devices with their start and end apart: 13 -> 12, of which waited for: 9 -> 4; matrix products, arithmetic and copies ran while one was open for 0% -> 0% of each run, Pallas kernels for 18% -> 15%
where the time goes in v13:
time: 42.2 us; the launch traced here: 42 us
  starting transfers between devices  23.4 us (55%)
  waiting for transfers between devices  9.06 us (21%)
  Pallas kernels  8.75 us (21%)
  between operations  0.78 us (2%)
    ppermute x12, starting transfers between devices, send(): return lax.ppermute(block, axis, route)  23.4 us
    ppermute x12, waiting for transfers between devices, send(): return lax.ppermute(block, axis, route)  9.06 us
    pallas_call x6, Pallas kernels, more_scores(): pl.pallas_call(functools.partial(scores_kernel, tuple(placed), fresh, loa...  5.67 us
    pallas_call x2, Pallas kernels, finish(): pl.pallas_call(functools.partial(finish_kernel, places), out_shape=pltpu....  1.6 us
    pallas_call x1, Pallas kernels, prepare(): pl.pallas_call(prepare_kernel, out_shape=shapes, in_specs=[far_spec()] *...  1.48 us
  transfers between devices with their start and end apart: 12, of which 4 were waited for; matrix products, arithmetic and copies ran while one was open for 0% of the time, Pallas kernels for 15%

profile of v13, /device:TPU:0, one launch (start us, length us, event | category | flops | bytes accessed | tf_op | source)
XLA Modules:
  0.0 42.0 jit_solution(2650551858353123280)
XLA Ops:
  0.0 1.5 %shard_map.55 = (bf16[128,1152]{1,0:T(8,128)(2,1)S(1)}, bf16[128,896]{1,0:T(8,128)(2,1)S(1)}) custom-call(bf16[128,2048]{1,0:T(8,128)(2,1)} %queries.1, f32[1,2048]{1,0:T(1,128)} %bitcast.1, s32[1,128]{1,0:T(1,128)} %rank.1), custom_call_target="tpu_custom_call" | custom-call | flops 67108864 | bytes 1048576 | tf_op jit(solution)/shard_map/pallas_call | solution.py:79
  1.5 3.1 %collective-permute-start = (bf16[128,1152]{1,0:T(8,128)(2,1)S(1)}, bf16[128,1152]{1,0:T(8,128)(2,1)S(1)}, u32[]{:S(2)}, u32[]{:S(2)}) collective-permute-start(bf16[128,1152]{1,0:T(8,128)(2,1)S(1)} %get-tuple-element.24.refs_1_), channel_id=1, source_target_pairs={{0,4},{2,6},{4,8},{6,10},{8,12},{10,14},{12,0},{14,2},{1,5},{3,7},... | collective-permute-start | bytes 884744 | tf_op jit(solution)/shard_map/ppermute | solution.py:245
  4.6 1.5 %collective-permute-start.2 = (bf16[128,1152]{1,0:T(8,128)(2,1)S(1)}, bf16[128,1152]{1,0:T(8,128)(2,1)S(1)}, u32[]{:S(2)}, u32[]{:S(2)}) collective-permute-start(bf16[128,1152]{1,0:T(8,128)(2,1)S(1)} %get-tuple-element.24.refs_1_), channel_id=1, source_target_pairs={{0,2},{2,0},{4,6},{6,4},{8,10},{10,8},{12,14},{14,12},{1,3},{3,1},... | collective-permute-start | bytes 884744 | tf_op jit(solution)/shard_map/ppermute | solution.py:245
  6.1 0.5 %collective-permute-start.5 = (bf16[128,896]{1,0:T(8,128)(2,1)S(1)}, bf16[128,896]{1,0:T(8,128)(2,1)S(1)}, u32[]{:S(2)}, u32[]{:S(2)}) collective-permute-start(bf16[128,896]{1,0:T(8,128)(2,1)S(1)} %get-tuple-element.25.refs_2_), channel_id=1, source_target_pairs={{0,2},{2,0},{4,6},{6,4},{8,10},{10,8},{12,14},{14,12},{1,3},{3,1},... | collective-permute-start | bytes 688136 | tf_op jit(solution)/shard_map/ppermute | solution.py:245
  6.6 1.6 %collective-permute-start.1 = (bf16[128,896]{1,0:T(8,128)(2,1)S(1)}, bf16[128,896]{1,0:T(8,128)(2,1)S(1)}, u32[]{:S(2)}, u32[]{:S(2)}) collective-permute-start(bf16[128,896]{1,0:T(8,128)(2,1)S(1)} %get-tuple-element.25.refs_2_), channel_id=1, source_target_pairs={{0,4},{2,6},{4,8},{6,10},{8,12},{10,14},{12,0},{14,2},{1,5},{3,7},... | collective-permute-start | bytes 688136 | tf_op jit(solution)/shard_map/ppermute | solution.py:245
  8.2 2.7 %shard_map.56 = (f32[384,128]{1,0:T(8,128)S(1)}, f32[384,128]{1,0:T(8,128)S(1)}, bf16[384,2048]{1,0:T(8,128)(2,1)S(1)}, bf16[384,2048]{1,0:T(8,128)(2,1)S(1)}) custom-call(bf16[768,2048]{1,0:T(8,128)(2,1)} %refs_0_.1, bf16[128,1152]{1,0:T(8,128)(2,1)S(1)} %get-tuple-element.24.refs_1_, bf16[128,896]{1,0:T(8,128)(2,1)S(1)} %get-tuple-element.25.refs_2_), custom_call_target="tpu_custom_call" | custom-call | flops 402653184 | bytes 393216 | tf_op jit(solution)/shard_map/pallas_call | solution.py:180
  10.9 3.6 %collective-permute-done.refs_2_ = bf16[128,1152]{1,0:T(8,128)(2,1)S(1)} collective-permute-done((bf16[128,1152]{1,0:T(8,128)(2,1)S(1)}, bf16[128,1152]{1,0:T(8,128)(2,1)S(1)}, u32[]{:S(2)}, u32[]{:S(2)}) %collective-permute-start) | collective-permute-done | bytes 294944 | tf_op jit(solution)/shard_map/ppermute | solution.py:245
  14.4 1.7 %collective-permute-start.4 = (bf16[128,1152]{1,0:T(8,128)(2,1)S(1)}, bf16[128,1152]{1,0:T(8,128)(2,1)S(1)}, u32[]{:S(2)}, u32[]{:S(2)}) collective-permute-start(bf16[128,1152]{1,0:T(8,128)(2,1)S(1)} %collective-permute-done.refs_2_), channel_id=1, source_target_pairs={{0,2},{2,4},{4,6},{6,8},{8,10},{10,12},{12,14},{14,0},{1,3},{3,5},... | collective-permute-start | bytes 884744 | tf_op jit(solution)/shard_map/ppermute | solution.py:245
  16.2 1.9 %collective-permute-start.3 = (bf16[128,1152]{1,0:T(8,128)(2,1)S(1)}, bf16[128,1152]{1,0:T(8,128)(2,1)S(1)}, u32[]{:S(2)}, u32[]{:S(2)}) collective-permute-start(bf16[128,1152]{1,0:T(8,128)(2,1)S(1)} %collective-permute-done.2.refs_4_), channel_id=1, source_target_pairs={{0,4},{4,8},{8,12},{12,0},{1,5},{5,9},{9,13},{13,1},{16,20},{20,24... | collective-permute-start | bytes 884744 | tf_op jit(solution)/shard_map/ppermute | solution.py:245
  18.1 0.3 collective-permute-done.5.refs_3_
  18.4 11.8 %collective-permute-start.6 = (bf16[128,896]{1,0:T(8,128)(2,1)S(1)}, bf16[128,896]{1,0:T(8,128)(2,1)S(1)}, u32[]{:S(2)}, u32[]{:S(2)}) collective-permute-start(bf16[128,896]{1,0:T(8,128)(2,1)S(1)} %collective-permute-done.5.refs_3_), channel_id=1, source_target_pairs={{0,4},{4,8},{8,12},{12,0},{1,5},{5,9},{9,13},{13,1},{16,20},{20,24... | collective-permute-start | bytes 688136 | tf_op jit(solution)/shard_map/ppermute | solution.py:245
  30.3 0.1 collective-permute-start.10
  31.0 1.0 %shard_map.57 = (f32[384,128]{1,0:T(8,128)S(1)}, f32[384,128]{1,0:T(8,128)S(1)}) custom-call(bf16[384,2048]{1,0:T(8,128)(2,1)S(1)} %get-tuple-element.26.refs_0_.refs_1_, bf16[384,2048]{1,0:T(8,128)(2,1)S(1)} %get-tuple-element.27.refs_1_.refs_2_, bf16[128,1152]{1,0:T(8,128)(2,1)S(1)} %collective-permute-done.refs_2_, ...), custom_call_target="tpu_custom_call" | custom-call | flops 402653184 | bytes 393216 | tf_op jit(solution)/shard_map/pallas_call | solution.py:180
  32.0 0.6 %collective-permute-start.11 = (f32[384,128]{1,0:T(8,128)S(1)}, f32[384,128]{1,0:T(8,128)S(1)}, u32[]{:S(2)}, u32[]{:S(2)}) collective-permute-start(f32[384,128]{1,0:T(8,128)S(1)} %get-tuple-element.42), channel_id=1, source_target_pairs={{0,1},{1,0},{2,3},{3,2},{4,5},{5,4},{6,7},{7,6},{8,9},{9,8},{10,11... | collective-permute-start | bytes 589832 | tf_op jit(solution)/shard_map/ppermute | solution.py:245
  32.6 0.7 %shard_map.58 = (f32[384,128]{1,0:T(8,128)S(1)}, f32[384,128]{1,0:T(8,128)S(1)}, f32[384,128]{1,0:T(8,128)S(1)}, f32[384,128]{1,0:T(8,128)S(1)}, s32[8,128]{1,0:T(8,128)S(1)}) custom-call(s32[1]{0:T(128)S(6)} %copy.8.refs_0_, bf16[384,2048]{1,0:T(8,128)(2,1)S(1)} %get-tuple-element.26.refs_0_.refs_1_, ...), custom_call_target="tpu_custom_call" | custom-call | flops 452984832 | bytes 786432 | tf_op jit(solution)/shard_map/pallas_call | solution.py:180
  33.3 0.4 collective-permute-done.6.refs_2_
  33.7 0.6 %shard_map.59 = (f32[384,128]{1,0:T(8,128)S(1)}, f32[384,128]{1,0:T(8,128)S(1)}, f32[384,128]{1,0:T(8,128)S(1)}, f32[384,128]{1,0:T(8,128)S(1)}) custom-call(bf16[384,2048]{1,0:T(8,128)(2,1)S(1)} %get-tuple-element.26.refs_0_.refs_1_, bf16[384,2048]{1,0:T(8,128)(2,1)S(1)} %get-tuple-element.27.refs_1_.refs_2_, ...), custom_call_target="tpu_custom_call" | custom-call | flops 176160768 | bytes 786432 | tf_op jit(solution)/shard_map/pallas_call | solution.py:180
  34.3 4.7 %collective-permute-done.8.refs_2_ = bf16[128,896]{1,0:T(8,128)(2,1)S(1)} collective-permute-done((bf16[128,896]{1,0:T(8,128)(2,1)S(1)}, bf16[128,896]{1,0:T(8,128)(2,1)S(1)}, u32[]{:S(2)}, u32[]{:S(2)}) %collective-permute-start.8) | collective-permute-done | bytes 229408 | tf_op jit(solution)/shard_map/ppermute | solution.py:245
  39.0 0.4 shard_map.61
  39.4 0.1 collective-permute-start.9
  39.4 0.5 %collective-permute-start.7 = (f32[384,128]{1,0:T(8,128)S(1)}, f32[384,128]{1,0:T(8,128)S(1)}, u32[]{:S(2)}, u32[]{:S(2)}) collective-permute-start(f32[384,128]{1,0:T(8,128)S(1)} %get-tuple-element.38), channel_id=1, source_target_pairs={{0,1},{1,0},{2,3},{3,2},{4,5},{5,4},{6,7},{7,6},{8,9},{9,8},{10,11... | collective-permute-start | bytes 589832 | tf_op jit(solution)/shard_map/ppermute | solution.py:245
  39.9 0.8 %shard_map.62.refs_4_ = f32[384,512]{1,0:T(8,128)} custom-call(s32[8,128]{1,0:T(8,128)S(1)} %get-tuple-element.32.limit, f32[384,128]{1,0:T(8,128)S(1)} %get-tuple-element.30.refs_0_, f32[384,128]{1,0:T(8,128)S(1)} %collective-permute-done.10.refs_1_, f32[384,128]{1,0:T(8,128)S(1)} %get-tuple-element.28.refs_2_, f32[384,128]{1,0:T(8,128)S(1)} %collective-permute-done.11.refs_3_), custom_call_target="tpu_custom_call" | custom-call | flops 98304 | bytes 1179648 | tf_op jit(solution)/shard_map/pallas_call | solution.py:215
  40.7 0.4 shard_map.60.refs_2_
  41.1 0.8 %shard_map.63 = f32[384,512]{1,0:T(8,128)} custom-call(s32[8,128]{1,0:T(8,128)S(1)} %get-tuple-element.32.limit, f32[384,128]{1,0:T(8,128)S(1)} %get-tuple-element.37.refs_0_, f32[384,128]{1,0:T(8,128)S(1)} %collective-permute-done.7.refs_1_, f32[384,128]{1,0:T(8,128)S(1)} %shard_map.60.refs_2_, ...), custom_call_target="tpu_custom_call", output_to_operand_aliasing={{}: (5, {})} | custom-call | flops 98304 | bytes 1179648 | tf_op jit(solution)/shard_map/pallas_call | solution.py:215
  (9 shorter events, 0.1 us)
Async XLA Ops:
  1.5 12.9 %collective-permute-start = (bf16[128,1152]{1,0:T(8,128)(2,1)S(1)}, bf16[128,1152]{1,0:T(8,128)(2,1)S(1)}, u32[]{:S(2)}, u32[]{:S(2)}) collective-permute-start(bf16[128,1152]{1,0:T(8,128)(2,1)S(1)} %get-tuple-element.24.refs_1_), channel_id=1, source_target_pairs={{0,4},{2,6},{4,8},{6,10},{8,12},{10,14},{12,0},{14,2},{1,5},{3,7},... | collective-permute-start | bytes 884744 | tf_op jit(solution)/shard_map/ppermute | solution.py:245
  4.6 11.6 %collective-permute-start.2 = (bf16[128,1152]{1,0:T(8,128)(2,1)S(1)}, bf16[128,1152]{1,0:T(8,128)(2,1)S(1)}, u32[]{:S(2)}, u32[]{:S(2)}) collective-permute-start(bf16[128,1152]{1,0:T(8,128)(2,1)S(1)} %get-tuple-element.24.refs_1_), channel_id=1, source_target_pairs={{0,2},{2,0},{4,6},{6,4},{8,10},{10,8},{12,14},{14,12},{1,3},{3,1},... | collective-permute-start | bytes 884744 | tf_op jit(solution)/shard_map/ppermute | solution.py:245
  6.1 12.4 %collective-permute-start.5 = (bf16[128,896]{1,0:T(8,128)(2,1)S(1)}, bf16[128,896]{1,0:T(8,128)(2,1)S(1)}, u32[]{:S(2)}, u32[]{:S(2)}) collective-permute-start(bf16[128,896]{1,0:T(8,128)(2,1)S(1)} %get-tuple-element.25.refs_2_), channel_id=1, source_target_pairs={{0,2},{2,0},{4,6},{6,4},{8,10},{10,8},{12,14},{14,12},{1,3},{3,1},... | collective-permute-start | bytes 688136 | tf_op jit(solution)/shard_map/ppermute | solution.py:245
  6.6 23.6 %collective-permute-start.1 = (bf16[128,896]{1,0:T(8,128)(2,1)S(1)}, bf16[128,896]{1,0:T(8,128)(2,1)S(1)}, u32[]{:S(2)}, u32[]{:S(2)}) collective-permute-start(bf16[128,896]{1,0:T(8,128)(2,1)S(1)} %get-tuple-element.25.refs_2_), channel_id=1, source_target_pairs={{0,4},{2,6},{4,8},{6,10},{8,12},{10,14},{12,0},{14,2},{1,5},{3,7},... | collective-permute-start | bytes 688136 | tf_op jit(solution)/shard_map/ppermute | solution.py:245
  14.4 17.6 %collective-permute-start.4 = (bf16[128,1152]{1,0:T(8,128)(2,1)S(1)}, bf16[128,1152]{1,0:T(8,128)(2,1)S(1)}, u32[]{:S(2)}, u32[]{:S(2)}) collective-permute-start(bf16[128,1152]{1,0:T(8,128)(2,1)S(1)} %collective-permute-done.refs_2_), channel_id=1, source_target_pairs={{0,2},{2,4},{4,6},{6,8},{8,10},{10,12},{12,14},{14,0},{1,3},{3,5},... | collective-permute-start | bytes 884744 | tf_op jit(solution)/shard_map/ppermute | solution.py:245
  16.2 16.4 %collective-permute-start.3 = (bf16[128,1152]{1,0:T(8,128)(2,1)S(1)}, bf16[128,1152]{1,0:T(8,128)(2,1)S(1)}, u32[]{:S(2)}, u32[]{:S(2)}) collective-permute-start(bf16[128,1152]{1,0:T(8,128)(2,1)S(1)} %collective-permute-done.2.refs_4_), channel_id=1, source_target_pairs={{0,4},{4,8},{8,12},{12,0},{1,5},{5,9},{9,13},{13,1},{16,20},{20,24... | collective-permute-start | bytes 884744 | tf_op jit(solution)/shard_map/ppermute | solution.py:245
  18.4 15.3 %collective-permute-start.6 = (bf16[128,896]{1,0:T(8,128)(2,1)S(1)}, bf16[128,896]{1,0:T(8,128)(2,1)S(1)}, u32[]{:S(2)}, u32[]{:S(2)}) collective-permute-start(bf16[128,896]{1,0:T(8,128)(2,1)S(1)} %collective-permute-done.5.refs_3_), channel_id=1, source_target_pairs={{0,4},{4,8},{8,12},{12,0},{1,5},{5,9},{9,13},{13,1},{16,20},{20,24... | collective-permute-start | bytes 688136 | tf_op jit(solution)/shard_map/ppermute | solution.py:245
  30.2 8.8 %collective-permute-start.8 = (bf16[128,896]{1,0:T(8,128)(2,1)S(1)}, bf16[128,896]{1,0:T(8,128)(2,1)S(1)}, u32[]{:S(2)}, u32[]{:S(2)}) collective-permute-start(bf16[128,896]{1,0:T(8,128)(2,1)S(1)} %collective-permute-done.1.refs_3_), channel_id=1, source_target_pairs={{0,2},{2,4},{4,6},{6,8},{8,10},{10,12},{12,14},{14,0},{1,3},{3,5},... | collective-permute-start | bytes 688136 | tf_op jit(solution)/shard_map/ppermute | solution.py:245
  30.3 9.7 %collective-permute-start.10 = (f32[384,128]{1,0:T(8,128)S(1)}, f32[384,128]{1,0:T(8,128)S(1)}, u32[]{:S(2)}, u32[]{:S(2)}) collective-permute-start(f32[384,128]{1,0:T(8,128)S(1)} %get-tuple-element.41), channel_id=1, source_target_pairs={{0,1},{1,0},{2,3},{3,2},{4,5},{5,4},{6,7},{7,6},{8,9},{9,8},{10,11... | collective-permute-start | bytes 589832 | tf_op jit(solution)/shard_map/ppermute | solution.py:245
  32.0 7.9 %collective-permute-start.11 = (f32[384,128]{1,0:T(8,128)S(1)}, f32[384,128]{1,0:T(8,128)S(1)}, u32[]{:S(2)}, u32[]{:S(2)}) collective-permute-start(f32[384,128]{1,0:T(8,128)S(1)} %get-tuple-element.42), channel_id=1, source_target_pairs={{0,1},{1,0},{2,3},{3,2},{4,5},{5,4},{6,7},{7,6},{8,9},{9,8},{10,11... | collective-permute-start | bytes 589832 | tf_op jit(solution)/shard_map/ppermute | solution.py:245
  39.4 1.8 %collective-permute-start.9 = (f32[384,128]{1,0:T(8,128)S(1)}, f32[384,128]{1,0:T(8,128)S(1)}, u32[]{:S(2)}, u32[]{:S(2)}) collective-permute-start(f32[384,128]{1,0:T(8,128)S(1)} %shard_map.61), channel_id=1, source_target_pairs={{0,1},{1,0},{2,3},{3,2},{4,5},{5,4},{6,7},{7,6},{8,9},{9,8},{10,11... | collective-permute-start | bytes 589832 | tf_op jit(solution)/shard_map/ppermute | solution.py:245
  39.4 1.7 %collective-permute-start.7 = (f32[384,128]{1,0:T(8,128)S(1)}, f32[384,128]{1,0:T(8,128)S(1)}, u32[]{:S(2)}, u32[]{:S(2)}) collective-permute-start(f32[384,128]{1,0:T(8,128)S(1)} %get-tuple-element.38), channel_id=1, source_target_pairs={{0,1},{1,0},{2,3},{3,2},{4,5},{5,4},{6,7},{7,6},{8,9},{9,8},{10,11... | collective-permute-start | bytes 589832 | tf_op jit(solution)/shard_map/ppermute | solution.py:245

commit v14 on v13

--- a/solution.py
+++ b/solution.py
@@ -8,12 +8,12 @@
 from jax.sharding import PartitionSpec as P
 
 STEPS = 4
-KINDS = "VV"
-PARTS = (9, 7)
-CHAIN = ("b0", "o1", "t1")
-ORDER = ("B0", "A0", "B1", "A1", "Z0", "R0", "Z1", "R1")
-TIES = {}
-EARLY = "R0"
+KINDS = "UUT"
+PARTS = (4, 6, 6)
+CHAIN = ("b0", "b2 o1", "t1")
+ORDER = ("B0", "B1", "B2", "C0", "C1", "E0", "E1", "R2", "C2")
+TIES = {"C2": "C1", "E1": "E0"}
+EARLY = "none"
 CHUNKS = len(PARTS)
 VMEM_BYTES = 16 * 1024 * 1024
 

time: 42.2 us -> 34.4 us (0.82)
  starting transfers between devices: 23.4 us -> 15.3 us
  Pallas kernels: 8.75 us -> 9.29 us
    ppermute x12 -> x13, starting transfers between devices: 23.4 us -> 15.3 us  [send(): return lax.ppermute(block, axis, route)]
    pallas_call x6, Pallas kernels: 5.67 us -> 6.11 us  [more_scores(): pl.pallas_call(functools.partial(scores_kernel, tuple(placed), fresh, loa...]
    ppermute x12 -> x13, waiting for transfers between devices: 9.06 us -> 8.82 us  [send(): return lax.ppermute(block, axis, route)]
  transfers between devices with their start and end apart: 12 -> 13, of which waited for: 4 -> 6; matrix products, arithmetic and copies ran while one was open for 0% -> 0% of each run, Pallas kernels for 15% -> 20%
where the time goes in v14:
time: 34.4 us; the launch traced here: 34.2 us
  starting transfers between devices  15.3 us (44%)
  Pallas kernels  9.29 us (27%)
  waiting for transfers between devices  8.82 us (26%)
  between operations  0.78 us (2%)
    ppermute x13, starting transfers between devices, send(): return lax.ppermute(block, axis, route)  15.3 us
    ppermute x13, waiting for transfers between devices, send(): return lax.ppermute(block, axis, route)  8.82 us
    pallas_call x6, Pallas kernels, more_scores(): pl.pallas_call(functools.partial(scores_kernel, tuple(placed), fresh, loa...  6.11 us
    pallas_call x2, Pallas kernels, finish(): pl.pallas_call(functools.partial(finish_kernel, places), out_shape=pltpu....  1.6 us
    pallas_call x1, Pallas kernels, prepare(): pl.pallas_call(prepare_kernel, out_shape=shapes, in_specs=[far_spec()] *...  1.58 us
  transfers between devices with their start and end apart: 13, of which 6 were waited for; matrix products, arithmetic and copies ran while one was open for 0% of the time, Pallas kernels for 20%

profile of v14, /device:TPU:0, one launch (start us, length us, event | category | flops | bytes accessed | tf_op | source)
XLA Modules:
  0.0 34.2 jit_solution(10711961596291901214)
XLA Ops:
  0.0 1.6 %shard_map.55 = (bf16[128,512]{1,0:T(8,128)(2,1)S(1)}, bf16[128,768]{1,0:T(8,128)(2,1)S(1)}, bf16[128,768]{1,0:T(8,128)(2,1)S(1)}) custom-call(bf16[128,2048]{1,0:T(8,128)(2,1)} %queries.1, f32[1,2048]{1,0:T(1,128)} %bitcast.1, s32[1,128]{1,0:T(1,128)} %rank.1), custom_call_target="tpu_custom_call" | custom-call | flops 67108864 | bytes 1048576 | tf_op jit(solution)/shard_map/pallas_call | solution.py:79
  1.6 3.1 %collective-permute-start = (bf16[128,512]{1,0:T(8,128)(2,1)S(1)}, bf16[128,512]{1,0:T(8,128)(2,1)S(1)}, u32[]{:S(2)}, u32[]{:S(2)}) collective-permute-start(bf16[128,512]{1,0:T(8,128)(2,1)S(1)} %get-tuple-element.26.refs_1_), channel_id=1, source_target_pairs={{0,4},{2,6},{4,8},{6,10},{8,12},{10,14},{12,0},{14,2},{1,5},{3,7},... | collective-permute-start | bytes 393224 | tf_op jit(solution)/shard_map/ppermute | solution.py:245
  4.7 1.6 %collective-permute-start.1 = (bf16[128,768]{1,0:T(8,128)(2,1)S(1)}, bf16[128,768]{1,0:T(8,128)(2,1)S(1)}, u32[]{:S(2)}, u32[]{:S(2)}) collective-permute-start(bf16[128,768]{1,0:T(8,128)(2,1)S(1)} %get-tuple-element.27.refs_2_), channel_id=1, source_target_pairs={{0,4},{2,6},{4,8},{6,10},{8,12},{10,14},{12,0},{14,2},{1,5},{3,7},... | collective-permute-start | bytes 589832 | tf_op jit(solution)/shard_map/ppermute | solution.py:245
  6.2 1.6 %collective-permute-start.2 = (bf16[128,768]{1,0:T(8,128)(2,1)S(1)}, bf16[128,768]{1,0:T(8,128)(2,1)S(1)}, u32[]{:S(2)}, u32[]{:S(2)}) collective-permute-start(bf16[128,768]{1,0:T(8,128)(2,1)S(1)} %get-tuple-element.28.refs_3_), channel_id=1, source_target_pairs={{0,4},{2,6},{4,8},{6,10},{8,12},{10,14},{12,0},{14,2},{1,5},{3,7},... | collective-permute-start | bytes 589832 | tf_op jit(solution)/shard_map/ppermute | solution.py:245
  7.8 3.2 %collective-permute-done.refs_2_ = bf16[128,512]{1,0:T(8,128)(2,1)S(1)} collective-permute-done((bf16[128,512]{1,0:T(8,128)(2,1)S(1)}, bf16[128,512]{1,0:T(8,128)(2,1)S(1)}, u32[]{:S(2)}, u32[]{:S(2)}) %collective-permute-start) | collective-permute-done | bytes 131104 | tf_op jit(solution)/shard_map/ppermute | solution.py:245
  11.0 1.8 %collective-permute-start.3 = (bf16[128,512]{1,0:T(8,128)(2,1)S(1)}, bf16[128,512]{1,0:T(8,128)(2,1)S(1)}, u32[]{:S(2)}, u32[]{:S(2)}) collective-permute-start(bf16[128,512]{1,0:T(8,128)(2,1)S(1)} %broadcast_select_fusion.2), channel_id=1, source_target_pairs={{0,2},{2,0},{4,6},{6,4},{8,10},{10,8},{12,14},{14,12},{1,3},{3,1},... | collective-permute-start | bytes 393224 | tf_op jit(solution)/shard_map/ppermute | solution.py:245
  12.8 2.4 %collective-permute-done.1.refs_3_ = bf16[128,768]{1,0:T(8,128)(2,1)S(1)} collective-permute-done((bf16[128,768]{1,0:T(8,128)(2,1)S(1)}, bf16[128,768]{1,0:T(8,128)(2,1)S(1)}, u32[]{:S(2)}, u32[]{:S(2)}) %collective-permute-start.1) | collective-permute-done | bytes 196640 | tf_op jit(solution)/shard_map/ppermute | solution.py:245
  15.3 1.8 %collective-permute-start.5 = (bf16[128,768]{1,0:T(8,128)(2,1)S(1)}, bf16[128,768]{1,0:T(8,128)(2,1)S(1)}, u32[]{:S(2)}, u32[]{:S(2)}) collective-permute-start(bf16[128,768]{1,0:T(8,128)(2,1)S(1)} %broadcast_select_fusion.1), channel_id=1, source_target_pairs={{0,2},{2,0},{4,6},{6,4},{8,10},{10,8},{12,14},{14,12},{1,3},{3,1},... | collective-permute-start | bytes 589832 | tf_op jit(solution)/shard_map/ppermute | solution.py:245
  17.1 1.6 %collective-permute-done.2.refs_4_ = bf16[128,768]{1,0:T(8,128)(2,1)S(1)} collective-permute-done((bf16[128,768]{1,0:T(8,128)(2,1)S(1)}, bf16[128,768]{1,0:T(8,128)(2,1)S(1)}, u32[]{:S(2)}, u32[]{:S(2)}) %collective-permute-start.2) | collective-permute-done | bytes 196640 | tf_op jit(solution)/shard_map/ppermute | solution.py:245
  18.6 1.7 %collective-permute-start.7 = (bf16[128,768]{1,0:T(8,128)(2,1)S(1)}, bf16[128,768]{1,0:T(8,128)(2,1)S(1)}, u32[]{:S(2)}, u32[]{:S(2)}) collective-permute-start(bf16[128,768]{1,0:T(8,128)(2,1)S(1)} %broadcast_select_fusion), channel_id=1, source_target_pairs={{0,2},{2,4},{4,6},{6,8},{8,10},{10,12},{12,14},{14,0},{1,3},{3,5},... | collective-permute-start | bytes 589832 | tf_op jit(solution)/shard_map/ppermute | solution.py:245
  20.3 0.8 %collective-permute-done.5.refs_4_ = bf16[128,768]{1,0:T(8,128)(2,1)S(1)} collective-permute-done((bf16[128,768]{1,0:T(8,128)(2,1)S(1)}, bf16[128,768]{1,0:T(8,128)(2,1)S(1)}, u32[]{:S(2)}, u32[]{:S(2)}) %collective-permute-start.5) | collective-permute-done | bytes 196640 | tf_op jit(solution)/shard_map/ppermute | solution.py:245
  21.1 2.5 %collective-permute-start.6 = (bf16[128,768]{1,0:T(8,128)(2,1)S(1)}, bf16[128,768]{1,0:T(8,128)(2,1)S(1)}, u32[]{:S(2)}, u32[]{:S(2)}) collective-permute-start(bf16[128,768]{1,0:T(8,128)(2,1)S(1)} %collective-permute-done.2.refs_4_), channel_id=1, source_target_pairs={{0,2},{2,0},{4,6},{6,4},{8,10},{10,8},{12,14},{14,12},{1,3},{3,1},... | collective-permute-start | bytes 589832 | tf_op jit(solution)/shard_map/ppermute | solution.py:245
  23.6 0.2 collective-permute-done.4.refs_4_
  23.8 3.3 %shard_map.56 = (f32[384,128]{1,0:T(8,128)S(1)}, f32[384,128]{1,0:T(8,128)S(1)}, bf16[384,2048]{1,0:T(8,128)(2,1)S(1)}, bf16[384,2048]{1,0:T(8,128)(2,1)S(1)}) custom-call(bf16[768,2048]{1,0:T(8,128)(2,1)} %refs_0_.1, bf16[128,512]{1,0:T(8,128)(2,1)S(1)} %get-tuple-element.26.refs_1_, bf16[128,768]{1,0:T(8,128)(2,1)S(1)} %get-tuple-element.27.refs_2_, ...), custom_call_target="tpu_custom_call" | custom-call | flops 402653184 | bytes 393216 | tf_op jit(solution)/shard_map/pallas_call | solution.py:180
  27.9 1.0 %shard_map.57 = (f32[384,128]{1,0:T(8,128)S(1)}, f32[384,128]{1,0:T(8,128)S(1)}) custom-call(bf16[384,2048]{1,0:T(8,128)(2,1)S(1)} %get-tuple-element.29.refs_0_.refs_1_, bf16[384,2048]{1,0:T(8,128)(2,1)S(1)} %get-tuple-element.30.refs_1_.refs_2_, bf16[128,512]{1,0:T(8,128)(2,1)S(1)} %collective-permute-done.refs_2_, ...), custom_call_target="tpu_custom_call" | custom-call | flops 402653184 | bytes 393216 | tf_op jit(solution)/shard_map/pallas_call | solution.py:180
  28.9 0.6 %collective-permute-start.12 = (f32[384,128]{1,0:T(8,128)S(1)}, f32[384,128]{1,0:T(8,128)S(1)}, u32[]{:S(2)}, u32[]{:S(2)}) collective-permute-start(f32[384,128]{1,0:T(8,128)S(1)} %get-tuple-element.46), channel_id=1, source_target_pairs={{0,1},{1,0},{2,3},{3,2},{4,5},{5,4},{6,7},{7,6},{8,9},{9,8},{10,11... | collective-permute-start | bytes 589832 | tf_op jit(solution)/shard_map/ppermute | solution.py:245
  29.5 0.4 %shard_map.58 = (f32[384,128]{1,0:T(8,128)S(1)}, f32[384,128]{1,0:T(8,128)S(1)}, f32[384,128]{1,0:T(8,128)S(1)}, f32[384,128]{1,0:T(8,128)S(1)}, s32[8,128]{1,0:T(8,128)S(1)}) custom-call(s32[1]{0:T(128)S(6)} %copy.8.refs_0_, bf16[384,2048]{1,0:T(8,128)(2,1)S(1)} %get-tuple-element.29.refs_0_.refs_1_, ...), custom_call_target="tpu_custom_call" | custom-call | flops 201326592 | bytes 786432 | tf_op jit(solution)/shard_map/pallas_call | solution.py:180
  29.9 0.6 %collective-permute-done.6.refs_2_ = bf16[128,768]{1,0:T(8,128)(2,1)S(1)} collective-permute-done((bf16[128,768]{1,0:T(8,128)(2,1)S(1)}, bf16[128,768]{1,0:T(8,128)(2,1)S(1)}, u32[]{:S(2)}, u32[]{:S(2)}) %collective-permute-start.6) | collective-permute-done | bytes 196640 | tf_op jit(solution)/shard_map/ppermute | solution.py:245
  30.5 0.8 %shard_map.59 = (f32[384,128]{1,0:T(8,128)S(1)}, f32[384,128]{1,0:T(8,128)S(1)}, f32[384,128]{1,0:T(8,128)S(1)}, f32[384,128]{1,0:T(8,128)S(1)}) custom-call(bf16[384,2048]{1,0:T(8,128)(2,1)S(1)} %get-tuple-element.29.refs_0_.refs_1_, bf16[384,2048]{1,0:T(8,128)(2,1)S(1)} %get-tuple-element.30.refs_1_.refs_2_, ...), custom_call_target="tpu_custom_call" | custom-call | flops 452984832 | bytes 786432 | tf_op jit(solution)/shard_map/pallas_call | solution.py:180
  31.4 0.3 shard_map.61
  31.7 0.6 %collective-permute-start.10 = (f32[384,128]{1,0:T(8,128)S(1)}, f32[384,128]{1,0:T(8,128)S(1)}, u32[]{:S(2)}, u32[]{:S(2)}) collective-permute-start(f32[384,128]{1,0:T(8,128)S(1)} %shard_map.61), channel_id=1, source_target_pairs={{0,1},{1,0},{2,3},{3,2},{4,5},{5,4},{6,7},{7,6},{8,9},{9,8},{10,11... | collective-permute-start | bytes 589832 | tf_op jit(solution)/shard_map/ppermute | solution.py:245
  32.3 0.8 %shard_map.62.refs_4_ = f32[384,512]{1,0:T(8,128)} custom-call(s32[8,128]{1,0:T(8,128)S(1)} %get-tuple-element.33.limit, f32[384,128]{1,0:T(8,128)S(1)} %get-tuple-element.44.refs_0_, f32[384,128]{1,0:T(8,128)S(1)} %collective-permute-done.11.refs_1_, f32[384,128]{1,0:T(8,128)S(1)} %get-tuple-element.31.refs_2_, f32[384,128]{1,0:T(8,128)S(1)} %collective-permute-done.12.refs_3_), custom_call_target="tpu_custom_call" | custom-call | flops 98304 | bytes 1179648 | tf_op jit(solution)/shard_map/pallas_call | solution.py:215
  33.1 0.3 shard_map.60.refs_2_
  33.4 0.8 %shard_map.63 = f32[384,512]{1,0:T(8,128)} custom-call(s32[8,128]{1,0:T(8,128)S(1)} %get-tuple-element.33.limit, f32[384,128]{1,0:T(8,128)S(1)} %get-tuple-element.39.refs_0_, f32[384,128]{1,0:T(8,128)S(1)} %collective-permute-done.8.refs_1_, f32[384,128]{1,0:T(8,128)S(1)} %shard_map.60.refs_2_, ...), custom_call_target="tpu_custom_call", output_to_operand_aliasing={{}: (5, {})} | custom-call | flops 98304 | bytes 1179648 | tf_op jit(solution)/shard_map/pallas_call | solution.py:215
  (14 shorter events, 0.2 us)
Async XLA Ops:
  1.6 9.4 %collective-permute-start = (bf16[128,512]{1,0:T(8,128)(2,1)S(1)}, bf16[128,512]{1,0:T(8,128)(2,1)S(1)}, u32[]{:S(2)}, u32[]{:S(2)}) collective-permute-start(bf16[128,512]{1,0:T(8,128)(2,1)S(1)} %get-tuple-element.26.refs_1_), channel_id=1, source_target_pairs={{0,4},{2,6},{4,8},{6,10},{8,12},{10,14},{12,0},{14,2},{1,5},{3,7},... | collective-permute-start | bytes 393224 | tf_op jit(solution)/shard_map/ppermute | solution.py:245
  4.7 10.6 %collective-permute-start.1 = (bf16[128,768]{1,0:T(8,128)(2,1)S(1)}, bf16[128,768]{1,0:T(8,128)(2,1)S(1)}, u32[]{:S(2)}, u32[]{:S(2)}) collective-permute-start(bf16[128,768]{1,0:T(8,128)(2,1)S(1)} %get-tuple-element.27.refs_2_), channel_id=1, source_target_pairs={{0,4},{2,6},{4,8},{6,10},{8,12},{10,14},{12,0},{14,2},{1,5},{3,7},... | collective-permute-start | bytes 589832 | tf_op jit(solution)/shard_map/ppermute | solution.py:245
  6.2 12.4 %collective-permute-start.2 = (bf16[128,768]{1,0:T(8,128)(2,1)S(1)}, bf16[128,768]{1,0:T(8,128)(2,1)S(1)}, u32[]{:S(2)}, u32[]{:S(2)}) collective-permute-start(bf16[128,768]{1,0:T(8,128)(2,1)S(1)} %get-tuple-element.28.refs_3_), channel_id=1, source_target_pairs={{0,4},{2,6},{4,8},{6,10},{8,12},{10,14},{12,0},{14,2},{1,5},{3,7},... | collective-permute-start | bytes 589832 | tf_op jit(solution)/shard_map/ppermute | solution.py:245
  11.0 6.0 %collective-permute-start.3 = (bf16[128,512]{1,0:T(8,128)(2,1)S(1)}, bf16[128,512]{1,0:T(8,128)(2,1)S(1)}, u32[]{:S(2)}, u32[]{:S(2)}) collective-permute-start(bf16[128,512]{1,0:T(8,128)(2,1)S(1)} %broadcast_select_fusion.2), channel_id=1, source_target_pairs={{0,2},{2,0},{4,6},{6,4},{8,10},{10,8},{12,14},{14,12},{1,3},{3,1},... | collective-permute-start | bytes 393224 | tf_op jit(solution)/shard_map/ppermute | solution.py:245
  15.3 5.9 %collective-permute-start.5 = (bf16[128,768]{1,0:T(8,128)(2,1)S(1)}, bf16[128,768]{1,0:T(8,128)(2,1)S(1)}, u32[]{:S(2)}, u32[]{:S(2)}) collective-permute-start(bf16[128,768]{1,0:T(8,128)(2,1)S(1)} %broadcast_select_fusion.1), channel_id=1, source_target_pairs={{0,2},{2,0},{4,6},{6,4},{8,10},{10,8},{12,14},{14,12},{1,3},{3,1},... | collective-permute-start | bytes 589832 | tf_op jit(solution)/shard_map/ppermute | solution.py:245
  17.1 6.8 %collective-permute-start.4 = (bf16[128,512]{1,0:T(8,128)(2,1)S(1)}, bf16[128,512]{1,0:T(8,128)(2,1)S(1)}, u32[]{:S(2)}, u32[]{:S(2)}) collective-permute-start(bf16[128,512]{1,0:T(8,128)(2,1)S(1)} %collective-permute-done.3.refs_3_), channel_id=1, source_target_pairs={{0,4},{2,6},{4,8},{6,10},{8,12},{10,14},{12,0},{14,2},{1,5},{3,7},... | collective-permute-start | bytes 393224 | tf_op jit(solution)/shard_map/ppermute | solution.py:245
  18.6 11.2 %collective-permute-start.7 = (bf16[128,768]{1,0:T(8,128)(2,1)S(1)}, bf16[128,768]{1,0:T(8,128)(2,1)S(1)}, u32[]{:S(2)}, u32[]{:S(2)}) collective-permute-start(bf16[128,768]{1,0:T(8,128)(2,1)S(1)} %broadcast_select_fusion), channel_id=1, source_target_pairs={{0,2},{2,4},{4,6},{6,8},{8,10},{10,12},{12,14},{14,0},{1,3},{3,5},... | collective-permute-start | bytes 589832 | tf_op jit(solution)/shard_map/ppermute | solution.py:245
  21.1 9.4 %collective-permute-start.6 = (bf16[128,768]{1,0:T(8,128)(2,1)S(1)}, bf16[128,768]{1,0:T(8,128)(2,1)S(1)}, u32[]{:S(2)}, u32[]{:S(2)}) collective-permute-start(bf16[128,768]{1,0:T(8,128)(2,1)S(1)} %collective-permute-done.2.refs_4_), channel_id=1, source_target_pairs={{0,2},{2,0},{4,6},{6,4},{8,10},{10,8},{12,14},{14,12},{1,3},{3,1},... | collective-permute-start | bytes 589832 | tf_op jit(solution)/shard_map/ppermute | solution.py:245
  23.8 7.5 %collective-permute-start.9 = (bf16[128,768]{1,0:T(8,128)(2,1)S(1)}, bf16[128,768]{1,0:T(8,128)(2,1)S(1)}, u32[]{:S(2)}, u32[]{:S(2)}) collective-permute-start(bf16[128,768]{1,0:T(8,128)(2,1)S(1)} %collective-permute-done.5.refs_4_), channel_id=1, source_target_pairs={{0,4},{2,6},{4,8},{6,10},{8,12},{10,14},{12,0},{14,2},{1,5},{3,7},... | collective-permute-start | bytes 589832 | tf_op jit(solution)/shard_map/ppermute | solution.py:245
  27.2 5.1 %collective-permute-start.11 = (f32[384,128]{1,0:T(8,128)S(1)}, f32[384,128]{1,0:T(8,128)S(1)}, u32[]{:S(2)}, u32[]{:S(2)}) collective-permute-start(f32[384,128]{1,0:T(8,128)S(1)} %get-tuple-element.45), channel_id=1, source_target_pairs={{0,1},{1,0},{2,3},{3,2},{4,5},{5,4},{6,7},{7,6},{8,9},{9,8},{10,11... | collective-permute-start | bytes 589832 | tf_op jit(solution)/shard_map/ppermute | solution.py:245
  28.9 3.4 %collective-permute-start.12 = (f32[384,128]{1,0:T(8,128)S(1)}, f32[384,128]{1,0:T(8,128)S(1)}, u32[]{:S(2)}, u32[]{:S(2)}) collective-permute-start(f32[384,128]{1,0:T(8,128)S(1)} %get-tuple-element.46), channel_id=1, source_target_pairs={{0,1},{1,0},{2,3},{3,2},{4,5},{5,4},{6,7},{7,6},{8,9},{9,8},{10,11... | collective-permute-start | bytes 589832 | tf_op jit(solution)/shard_map/ppermute | solution.py:245
  31.3 2.1 %collective-permute-start.8 = (f32[384,128]{1,0:T(8,128)S(1)}, f32[384,128]{1,0:T(8,128)S(1)}, u32[]{:S(2)}, u32[]{:S(2)}) collective-permute-start(f32[384,128]{1,0:T(8,128)S(1)} %get-tuple-element.40), channel_id=1, source_target_pairs={{0,1},{1,0},{2,3},{3,2},{4,5},{5,4},{6,7},{7,6},{8,9},{9,8},{10,11... | collective-permute-start | bytes 589832 | tf_op jit(solution)/shard_map/ppermute | solution.py:245
  31.7 1.7 %collective-permute-start.10 = (f32[384,128]{1,0:T(8,128)S(1)}, f32[384,128]{1,0:T(8,128)S(1)}, u32[]{:S(2)}, u32[]{:S(2)}) collective-permute-start(f32[384,128]{1,0:T(8,128)S(1)} %shard_map.61), channel_id=1, source_target_pairs={{0,1},{1,0},{2,3},{3,2},{4,5},{5,4},{6,7},{7,6},{8,9},{9,8},{10,11... | collective-permute-start | bytes 589832 | tf_op jit(solution)/shard_map/ppermute | solution.py:245

commit v15 on v14

--- a/solution.py
+++ b/solution.py
@@ -13,7 +13,7 @@
 CHAIN = ("b0", "b2 o1", "t1")
 ORDER = ("B0", "B1", "B2", "C0", "C1", "E0", "E1", "R2", "C2")
 TIES = {"C2": "C1", "E1": "E0"}
-EARLY = "none"
+EARLY = "C0"
 CHUNKS = len(PARTS)
 VMEM_BYTES = 16 * 1024 * 1024
 

time: 34.4 us -> 34.4 us (level)
  starting transfers between devices: 15.3 us -> 14.9 us
  waiting for transfers between devices: 8.82 us -> 9.17 us
    ppermute x13, starting transfers between devices: 15.3 us -> 14.9 us  [send(): return lax.ppermute(block, axis, route)]
    ppermute x13, waiting for transfers between devices: 8.82 us -> 9.17 us  [send(): return lax.ppermute(block, axis, route)]
where the time goes in v15:
time: 34.4 us; the launch traced here: 34.2 us
  starting transfers between devices  14.9 us (43%)
  Pallas kernels  9.3 us (27%)
  waiting for transfers between devices  9.17 us (27%)
  between operations  0.78 us (2%)
    ppermute x13, starting transfers between devices, send(): return lax.ppermute(block, axis, route)  14.9 us
    ppermute x13, waiting for transfers between devices, send(): return lax.ppermute(block, axis, route)  9.17 us
    pallas_call x6, Pallas kernels, more_scores(): pl.pallas_call(functools.partial(scores_kernel, tuple(placed), fresh, loa...  6.11 us
    pallas_call x2, Pallas kernels, finish(): pl.pallas_call(functools.partial(finish_kernel, places), out_shape=pltpu....  1.6 us
    pallas_call x1, Pallas kernels, prepare(): pl.pallas_call(prepare_kernel, out_shape=shapes, in_specs=[far_spec()] *...  1.58 us
  transfers between devices with their start and end apart: 13, of which 6 were waited for; matrix products, arithmetic and copies ran while one was open for 0% of the time, Pallas kernels for 20%

profile of v15, /device:TPU:0, one launch (start us, length us, event | category | flops | bytes accessed | tf_op | source)
XLA Modules:
  0.0 34.2 jit_solution(4576526328658610481)
XLA Ops:
  0.0 1.6 %shard_map.55 = (bf16[128,512]{1,0:T(8,128)(2,1)S(1)}, bf16[128,768]{1,0:T(8,128)(2,1)S(1)}, bf16[128,768]{1,0:T(8,128)(2,1)S(1)}) custom-call(bf16[128,2048]{1,0:T(8,128)(2,1)} %queries.1, f32[1,2048]{1,0:T(1,128)} %bitcast.1, s32[1,128]{1,0:T(1,128)} %rank.1), custom_call_target="tpu_custom_call" | custom-call | flops 67108864 | bytes 1048576 | tf_op jit(solution)/shard_map/pallas_call | solution.py:79
  1.6 3.1 %collective-permute-start = (bf16[128,512]{1,0:T(8,128)(2,1)S(1)}, bf16[128,512]{1,0:T(8,128)(2,1)S(1)}, u32[]{:S(2)}, u32[]{:S(2)}) collective-permute-start(bf16[128,512]{1,0:T(8,128)(2,1)S(1)} %get-tuple-element.27.refs_1_), channel_id=1, source_target_pairs={{0,4},{2,6},{4,8},{6,10},{8,12},{10,14},{12,0},{14,2},{1,5},{3,7},... | collective-permute-start | bytes 393224 | tf_op jit(solution)/shard_map/ppermute | solution.py:245
  4.7 1.6 %collective-permute-start.1 = (bf16[128,768]{1,0:T(8,128)(2,1)S(1)}, bf16[128,768]{1,0:T(8,128)(2,1)S(1)}, u32[]{:S(2)}, u32[]{:S(2)}) collective-permute-start(bf16[128,768]{1,0:T(8,128)(2,1)S(1)} %get-tuple-element.28.refs_2_), channel_id=1, source_target_pairs={{0,4},{2,6},{4,8},{6,10},{8,12},{10,14},{12,0},{14,2},{1,5},{3,7},... | collective-permute-start | bytes 589832 | tf_op jit(solution)/shard_map/ppermute | solution.py:245
  6.2 1.6 %collective-permute-start.2 = (bf16[128,768]{1,0:T(8,128)(2,1)S(1)}, bf16[128,768]{1,0:T(8,128)(2,1)S(1)}, u32[]{:S(2)}, u32[]{:S(2)}) collective-permute-start(bf16[128,768]{1,0:T(8,128)(2,1)S(1)} %get-tuple-element.29.refs_3_), channel_id=1, source_target_pairs={{0,4},{2,6},{4,8},{6,10},{8,12},{10,14},{12,0},{14,2},{1,5},{3,7},... | collective-permute-start | bytes 589832 | tf_op jit(solution)/shard_map/ppermute | solution.py:245
  7.8 3.3 %shard_map.56 = (f32[384,128]{1,0:T(8,128)S(1)}, f32[384,128]{1,0:T(8,128)S(1)}, bf16[384,2048]{1,0:T(8,128)(2,1)S(1)}, bf16[384,2048]{1,0:T(8,128)(2,1)S(1)}) custom-call(bf16[768,2048]{1,0:T(8,128)(2,1)} %refs_0_.1, bf16[128,512]{1,0:T(8,128)(2,1)S(1)} %get-tuple-element.27.refs_1_, bf16[128,768]{1,0:T(8,128)(2,1)S(1)} %get-tuple-element.28.refs_2_, ...), custom_call_target="tpu_custom_call" | custom-call | flops 402653184 | bytes 393216 | tf_op jit(solution)/shard_map/pallas_call | solution.py:180
  11.2 1.6 %collective-permute-start.3 = (bf16[128,512]{1,0:T(8,128)(2,1)S(1)}, bf16[128,512]{1,0:T(8,128)(2,1)S(1)}, u32[]{:S(2)}, u32[]{:S(2)}) collective-permute-start(bf16[128,512]{1,0:T(8,128)(2,1)S(1)} %broadcast_select_fusion.2), channel_id=1, source_target_pairs={{0,2},{2,0},{4,6},{6,4},{8,10},{10,8},{12,14},{14,12},{1,3},{3,1},... | collective-permute-start | bytes 393224 | tf_op jit(solution)/shard_map/ppermute | solution.py:245
  12.8 2.4 %collective-permute-done.1.refs_3_ = bf16[128,768]{1,0:T(8,128)(2,1)S(1)} collective-permute-done((bf16[128,768]{1,0:T(8,128)(2,1)S(1)}, bf16[128,768]{1,0:T(8,128)(2,1)S(1)}, u32[]{:S(2)}, u32[]{:S(2)}) %collective-permute-start.1) | collective-permute-done | bytes 196640 | tf_op jit(solution)/shard_map/ppermute | solution.py:245
  15.3 1.8 %collective-permute-start.5 = (bf16[128,768]{1,0:T(8,128)(2,1)S(1)}, bf16[128,768]{1,0:T(8,128)(2,1)S(1)}, u32[]{:S(2)}, u32[]{:S(2)}) collective-permute-start(bf16[128,768]{1,0:T(8,128)(2,1)S(1)} %broadcast_select_fusion.1), channel_id=1, source_target_pairs={{0,2},{2,0},{4,6},{6,4},{8,10},{10,8},{12,14},{14,12},{1,3},{3,1},... | collective-permute-start | bytes 589832 | tf_op jit(solution)/shard_map/ppermute | solution.py:245
  17.1 1.6 %collective-permute-done.2.refs_4_ = bf16[128,768]{1,0:T(8,128)(2,1)S(1)} collective-permute-done((bf16[128,768]{1,0:T(8,128)(2,1)S(1)}, bf16[128,768]{1,0:T(8,128)(2,1)S(1)}, u32[]{:S(2)}, u32[]{:S(2)}) %collective-permute-start.2) | collective-permute-done | bytes 196640 | tf_op jit(solution)/shard_map/ppermute | solution.py:245
  18.6 1.5 %collective-permute-start.7 = (bf16[128,768]{1,0:T(8,128)(2,1)S(1)}, bf16[128,768]{1,0:T(8,128)(2,1)S(1)}, u32[]{:S(2)}, u32[]{:S(2)}) collective-permute-start(bf16[128,768]{1,0:T(8,128)(2,1)S(1)} %broadcast_select_fusion), channel_id=1, source_target_pairs={{0,2},{2,4},{4,6},{6,8},{8,10},{10,12},{12,14},{14,0},{1,3},{3,5},... | collective-permute-start | bytes 589832 | tf_op jit(solution)/shard_map/ppermute | solution.py:245
  20.2 0.9 %collective-permute-done.5.refs_4_ = bf16[128,768]{1,0:T(8,128)(2,1)S(1)} collective-permute-done((bf16[128,768]{1,0:T(8,128)(2,1)S(1)}, bf16[128,768]{1,0:T(8,128)(2,1)S(1)}, u32[]{:S(2)}, u32[]{:S(2)}) %collective-permute-start.5) | collective-permute-done | bytes 196640 | tf_op jit(solution)/shard_map/ppermute | solution.py:245
  21.1 2.5 %collective-permute-start.6 = (bf16[128,768]{1,0:T(8,128)(2,1)S(1)}, bf16[128,768]{1,0:T(8,128)(2,1)S(1)}, u32[]{:S(2)}, u32[]{:S(2)}) collective-permute-start(bf16[128,768]{1,0:T(8,128)(2,1)S(1)} %collective-permute-done.2.refs_4_), channel_id=1, source_target_pairs={{0,2},{2,0},{4,6},{6,4},{8,10},{10,8},{12,14},{14,12},{1,3},{3,1},... | collective-permute-start | bytes 589832 | tf_op jit(solution)/shard_map/ppermute | solution.py:245
  23.6 0.2 collective-permute-done.4.refs_4_
  24.5 1.0 %shard_map.57 = (f32[384,128]{1,0:T(8,128)S(1)}, f32[384,128]{1,0:T(8,128)S(1)}) custom-call(bf16[384,2048]{1,0:T(8,128)(2,1)S(1)} %get-tuple-element.30.refs_0_.refs_1_, bf16[384,2048]{1,0:T(8,128)(2,1)S(1)} %get-tuple-element.31.refs_1_.refs_2_, bf16[128,512]{1,0:T(8,128)(2,1)S(1)} %collective-permute-done.refs_2_, ...), custom_call_target="tpu_custom_call" | custom-call | flops 402653184 | bytes 393216 | tf_op jit(solution)/shard_map/pallas_call | solution.py:180
  25.5 0.6 %collective-permute-start.12 = (f32[384,128]{1,0:T(8,128)S(1)}, f32[384,128]{1,0:T(8,128)S(1)}, u32[]{:S(2)}, u32[]{:S(2)}) collective-permute-start(f32[384,128]{1,0:T(8,128)S(1)} %get-tuple-element.48), channel_id=1, source_target_pairs={{0,1},{1,0},{2,3},{3,2},{4,5},{5,4},{6,7},{7,6},{8,9},{9,8},{10,11... | collective-permute-start | bytes 589832 | tf_op jit(solution)/shard_map/ppermute | solution.py:245
  26.0 0.4 %shard_map.58 = (f32[384,128]{1,0:T(8,128)S(1)}, f32[384,128]{1,0:T(8,128)S(1)}, f32[384,128]{1,0:T(8,128)S(1)}, f32[384,128]{1,0:T(8,128)S(1)}, s32[8,128]{1,0:T(8,128)S(1)}) custom-call(s32[1]{0:T(128)S(6)} %copy.8.refs_0_, bf16[384,2048]{1,0:T(8,128)(2,1)S(1)} %get-tuple-element.30.refs_0_.refs_1_, ...), custom_call_target="tpu_custom_call" | custom-call | flops 201326592 | bytes 786432 | tf_op jit(solution)/shard_map/pallas_call | solution.py:180
  26.4 2.9 %collective-permute-done.7.refs_3_ = bf16[128,768]{1,0:T(8,128)(2,1)S(1)} collective-permute-done((bf16[128,768]{1,0:T(8,128)(2,1)S(1)}, bf16[128,768]{1,0:T(8,128)(2,1)S(1)}, u32[]{:S(2)}, u32[]{:S(2)}) %collective-permute-start.7) | collective-permute-done | bytes 196640 | tf_op jit(solution)/shard_map/ppermute | solution.py:245
  29.3 1.1 %collective-permute-done.6.refs_2_ = bf16[128,768]{1,0:T(8,128)(2,1)S(1)} collective-permute-done((bf16[128,768]{1,0:T(8,128)(2,1)S(1)}, bf16[128,768]{1,0:T(8,128)(2,1)S(1)}, u32[]{:S(2)}, u32[]{:S(2)}) %collective-permute-start.6) | collective-permute-done | bytes 196640 | tf_op jit(solution)/shard_map/ppermute | solution.py:245
  30.5 0.8 %shard_map.59 = (f32[384,128]{1,0:T(8,128)S(1)}, f32[384,128]{1,0:T(8,128)S(1)}, f32[384,128]{1,0:T(8,128)S(1)}, f32[384,128]{1,0:T(8,128)S(1)}) custom-call(bf16[384,2048]{1,0:T(8,128)(2,1)S(1)} %get-tuple-element.30.refs_0_.refs_1_, bf16[384,2048]{1,0:T(8,128)(2,1)S(1)} %get-tuple-element.31.refs_1_.refs_2_, ...), custom_call_target="tpu_custom_call" | custom-call | flops 452984832 | bytes 786432 | tf_op jit(solution)/shard_map/pallas_call | solution.py:180
  31.4 0.3 shard_map.61
  31.7 0.6 %collective-permute-start.10 = (f32[384,128]{1,0:T(8,128)S(1)}, f32[384,128]{1,0:T(8,128)S(1)}, u32[]{:S(2)}, u32[]{:S(2)}) collective-permute-start(f32[384,128]{1,0:T(8,128)S(1)} %shard_map.61), channel_id=1, source_target_pairs={{0,1},{1,0},{2,3},{3,2},{4,5},{5,4},{6,7},{7,6},{8,9},{9,8},{10,11... | collective-permute-start | bytes 589832 | tf_op jit(solution)/shard_map/ppermute | solution.py:245
  32.3 0.8 %shard_map.62.refs_4_ = f32[384,512]{1,0:T(8,128)} custom-call(s32[8,128]{1,0:T(8,128)S(1)} %get-tuple-element.36.limit, f32[384,128]{1,0:T(8,128)S(1)} %get-tuple-element.34.refs_0_, f32[384,128]{1,0:T(8,128)S(1)} %collective-permute-done.11.refs_1_, f32[384,128]{1,0:T(8,128)S(1)} %get-tuple-element.32.refs_2_, f32[384,128]{1,0:T(8,128)S(1)} %collective-permute-done.12.refs_3_), custom_call_target="tpu_custom_call" | custom-call | flops 98304 | bytes 1179648 | tf_op jit(solution)/shard_map/pallas_call | solution.py:215
  33.1 0.3 shard_map.60.refs_2_
  33.4 0.8 %shard_map.63 = f32[384,512]{1,0:T(8,128)} custom-call(s32[8,128]{1,0:T(8,128)S(1)} %get-tuple-element.36.limit, f32[384,128]{1,0:T(8,128)S(1)} %get-tuple-element.42.refs_0_, f32[384,128]{1,0:T(8,128)S(1)} %collective-permute-done.8.refs_1_, f32[384,128]{1,0:T(8,128)S(1)} %shard_map.60.refs_2_, ...), custom_call_target="tpu_custom_call", output_to_operand_aliasing={{}: (5, {})} | custom-call | flops 98304 | bytes 1179648 | tf_op jit(solution)/shard_map/pallas_call | solution.py:215
  (14 shorter events, 0.2 us)
Async XLA Ops:
  1.6 9.6 %collective-permute-start = (bf16[128,512]{1,0:T(8,128)(2,1)S(1)}, bf16[128,512]{1,0:T(8,128)(2,1)S(1)}, u32[]{:S(2)}, u32[]{:S(2)}) collective-permute-start(bf16[128,512]{1,0:T(8,128)(2,1)S(1)} %get-tuple-element.27.refs_1_), channel_id=1, source_target_pairs={{0,4},{2,6},{4,8},{6,10},{8,12},{10,14},{12,0},{14,2},{1,5},{3,7},... | collective-permute-start | bytes 393224 | tf_op jit(solution)/shard_map/ppermute | solution.py:245
  4.7 10.6 %collective-permute-start.1 = (bf16[128,768]{1,0:T(8,128)(2,1)S(1)}, bf16[128,768]{1,0:T(8,128)(2,1)S(1)}, u32[]{:S(2)}, u32[]{:S(2)}) collective-permute-start(bf16[128,768]{1,0:T(8,128)(2,1)S(1)} %get-tuple-element.28.refs_2_), channel_id=1, source_target_pairs={{0,4},{2,6},{4,8},{6,10},{8,12},{10,14},{12,0},{14,2},{1,5},{3,7},... | collective-permute-start | bytes 589832 | tf_op jit(solution)/shard_map/ppermute | solution.py:245
  6.2 12.4 %collective-permute-start.2 = (bf16[128,768]{1,0:T(8,128)(2,1)S(1)}, bf16[128,768]{1,0:T(8,128)(2,1)S(1)}, u32[]{:S(2)}, u32[]{:S(2)}) collective-permute-start(bf16[128,768]{1,0:T(8,128)(2,1)S(1)} %get-tuple-element.29.refs_3_), channel_id=1, source_target_pairs={{0,4},{2,6},{4,8},{6,10},{8,12},{10,14},{12,0},{14,2},{1,5},{3,7},... | collective-permute-start | bytes 589832 | tf_op jit(solution)/shard_map/ppermute | solution.py:245
  11.2 5.9 %collective-permute-start.3 = (bf16[128,512]{1,0:T(8,128)(2,1)S(1)}, bf16[128,512]{1,0:T(8,128)(2,1)S(1)}, u32[]{:S(2)}, u32[]{:S(2)}) collective-permute-start(bf16[128,512]{1,0:T(8,128)(2,1)S(1)} %broadcast_select_fusion.2), channel_id=1, source_target_pairs={{0,2},{2,0},{4,6},{6,4},{8,10},{10,8},{12,14},{14,12},{1,3},{3,1},... | collective-permute-start | bytes 393224 | tf_op jit(solution)/shard_map/ppermute | solution.py:245
  15.3 5.9 %collective-permute-start.5 = (bf16[128,768]{1,0:T(8,128)(2,1)S(1)}, bf16[128,768]{1,0:T(8,128)(2,1)S(1)}, u32[]{:S(2)}, u32[]{:S(2)}) collective-permute-start(bf16[128,768]{1,0:T(8,128)(2,1)S(1)} %broadcast_select_fusion.1), channel_id=1, source_target_pairs={{0,2},{2,0},{4,6},{6,4},{8,10},{10,8},{12,14},{14,12},{1,3},{3,1},... | collective-permute-start | bytes 589832 | tf_op jit(solution)/shard_map/ppermute | solution.py:245
  17.1 6.8 %collective-permute-start.4 = (bf16[128,512]{1,0:T(8,128)(2,1)S(1)}, bf16[128,512]{1,0:T(8,128)(2,1)S(1)}, u32[]{:S(2)}, u32[]{:S(2)}) collective-permute-start(bf16[128,512]{1,0:T(8,128)(2,1)S(1)} %collective-permute-done.3.refs_3_), channel_id=1, source_target_pairs={{0,4},{2,6},{4,8},{6,10},{8,12},{10,14},{12,0},{14,2},{1,5},{3,7},... | collective-permute-start | bytes 393224 | tf_op jit(solution)/shard_map/ppermute | solution.py:245
  18.6 10.7 %collective-permute-start.7 = (bf16[128,768]{1,0:T(8,128)(2,1)S(1)}, bf16[128,768]{1,0:T(8,128)(2,1)S(1)}, u32[]{:S(2)}, u32[]{:S(2)}) collective-permute-start(bf16[128,768]{1,0:T(8,128)(2,1)S(1)} %broadcast_select_fusion), channel_id=1, source_target_pairs={{0,2},{2,4},{4,6},{6,8},{8,10},{10,12},{12,14},{14,0},{1,3},{3,5},... | collective-permute-start | bytes 589832 | tf_op jit(solution)/shard_map/ppermute | solution.py:245
  21.1 9.4 %collective-permute-start.6 = (bf16[128,768]{1,0:T(8,128)(2,1)S(1)}, bf16[128,768]{1,0:T(8,128)(2,1)S(1)}, u32[]{:S(2)}, u32[]{:S(2)}) collective-permute-start(bf16[128,768]{1,0:T(8,128)(2,1)S(1)} %collective-permute-done.2.refs_4_), channel_id=1, source_target_pairs={{0,2},{2,0},{4,6},{6,4},{8,10},{10,8},{12,14},{14,12},{1,3},{3,1},... | collective-permute-start | bytes 589832 | tf_op jit(solution)/shard_map/ppermute | solution.py:245
  23.8 7.5 %collective-permute-start.9 = (bf16[128,768]{1,0:T(8,128)(2,1)S(1)}, bf16[128,768]{1,0:T(8,128)(2,1)S(1)}, u32[]{:S(2)}, u32[]{:S(2)}) collective-permute-start(bf16[128,768]{1,0:T(8,128)(2,1)S(1)} %collective-permute-done.5.refs_4_), channel_id=1, source_target_pairs={{0,4},{2,6},{4,8},{6,10},{8,12},{10,14},{12,0},{14,2},{1,5},{3,7},... | collective-permute-start | bytes 589832 | tf_op jit(solution)/shard_map/ppermute | solution.py:245
  23.8 8.4 %collective-permute-start.11 = (f32[384,128]{1,0:T(8,128)S(1)}, f32[384,128]{1,0:T(8,128)S(1)}, u32[]{:S(2)}, u32[]{:S(2)}) collective-permute-start(f32[384,128]{1,0:T(8,128)S(1)} %get-tuple-element.47), channel_id=1, source_target_pairs={{0,1},{1,0},{2,3},{3,2},{4,5},{5,4},{6,7},{7,6},{8,9},{9,8},{10,11... | collective-permute-start | bytes 589832 | tf_op jit(solution)/shard_map/ppermute | solution.py:245
  25.5 6.8 %collective-permute-start.12 = (f32[384,128]{1,0:T(8,128)S(1)}, f32[384,128]{1,0:T(8,128)S(1)}, u32[]{:S(2)}, u32[]{:S(2)}) collective-permute-start(f32[384,128]{1,0:T(8,128)S(1)} %get-tuple-element.48), channel_id=1, source_target_pairs={{0,1},{1,0},{2,3},{3,2},{4,5},{5,4},{6,7},{7,6},{8,9},{9,8},{10,11... | collective-permute-start | bytes 589832 | tf_op jit(solution)/shard_map/ppermute | solution.py:245
  31.3 2.1 %collective-permute-start.8 = (f32[384,128]{1,0:T(8,128)S(1)}, f32[384,128]{1,0:T(8,128)S(1)}, u32[]{:S(2)}, u32[]{:S(2)}) collective-permute-start(f32[384,128]{1,0:T(8,128)S(1)} %get-tuple-element.43), channel_id=1, source_target_pairs={{0,1},{1,0},{2,3},{3,2},{4,5},{5,4},{6,7},{7,6},{8,9},{9,8},{10,11... | collective-permute-start | bytes 589832 | tf_op jit(solution)/shard_map/ppermute | solution.py:245
  31.7 1.7 %collective-permute-start.10 = (f32[384,128]{1,0:T(8,128)S(1)}, f32[384,128]{1,0:T(8,128)S(1)}, u32[]{:S(2)}, u32[]{:S(2)}) collective-permute-start(f32[384,128]{1,0:T(8,128)S(1)} %shard_map.61), channel_id=1, source_target_pairs={{0,1},{1,0},{2,3},{3,2},{4,5},{5,4},{6,7},{7,6},{8,9},{9,8},{10,11... | collective-permute-start | bytes 589832 | tf_op jit(solution)/shard_map/ppermute | solution.py:245

commit v16 on v15

--- a/solution.py
+++ b/solution.py
@@ -10,10 +10,11 @@
 STEPS = 4
 KINDS = "UUT"
 PARTS = (4, 6, 6)
-CHAIN = ("b0", "b2 o1", "t1")
+CHAIN = ("b0", "o1", "b2", "t1")
 ORDER = ("B0", "B1", "B2", "C0", "C1", "E0", "E1", "R2", "C2")
-TIES = {"C2": "C1", "E1": "E0"}
+TIES = {"C2": "C0", "E1": "E0"}
 EARLY = "C0"
+OUT = "none"
 CHUNKS = len(PARTS)
 VMEM_BYTES = 16 * 1024 * 1024
 
@@ -298,9 +299,12 @@
     two_pair = exchanged(two)
     limited = after(valid_rows, two[1])
     one = three = one_pair = None
-    todo = set(range(CHUNKS))
+    todo, out = set(range(CHUNKS)), None
     for group in CHAIN:
         pieces = []
+        if group == OUT:
+            out = finish(limit, [own_pair, two_pair], (0, 2), STEPS)
+            one = after(one[0], out), one[1]
         for item in group.split():
             n, parts = int(item[1:]), {"b": (0, 1), "o": (0,), "t": (1,)}[item[0]]
             blocks = one_back[n], three_back[n]
@@ -317,7 +321,8 @@
             three = theirs, ours
         if one_pair is None and not todo:
             one_pair = exchanged(one)
-    out = finish(limit, [own_pair, two_pair], (0, 2), STEPS)
+    if out is None:
+        out = finish(limit, [own_pair, two_pair], (0, 2), STEPS)
     return finish(limit, [one_pair, exchanged(three)], (1, 3), STEPS, out)
 
 

time: 34.4 us -> 34.1 us (level)
  starting transfers between devices: 14.9 us -> 12.3 us
  waiting for transfers between devices: 9.17 us -> 11.3 us
    ppermute x13, starting transfers between devices: 14.9 us -> 12.3 us  [send(): return lax.ppermute(block, axis, route)]
    ppermute x13, waiting for transfers between devices: 9.17 us -> 11.3 us  [send(): return lax.ppermute(block, axis, route)]
    pallas_call x6 -> x7, Pallas kernels: 6.11 us -> 6.33 us  [more_scores(): pl.pallas_call(functools.partial(scores_kernel, tuple(placed), fresh, loa...]
  transfers between devices with their start and end apart: 13 -> 13, of which waited for: 6 -> 7; matrix products, arithmetic and copies ran while one was open for 0% -> 0% of each run, Pallas kernels for 20% -> 21%
where the time goes in v16:
time: 34.1 us; the launch traced here: 33.9 us
  starting transfers between devices  12.3 us (36%)
  waiting for transfers between devices  11.3 us (33%)
  Pallas kernels  9.5 us (28%)
  between operations  0.79 us (2%)
    ppermute x13, starting transfers between devices, send(): return lax.ppermute(block, axis, route)  12.3 us
    ppermute x13, waiting for transfers between devices, send(): return lax.ppermute(block, axis, route)  11.3 us
    pallas_call x7, Pallas kernels, more_scores(): pl.pallas_call(functools.partial(scores_kernel, tuple(placed), fresh, loa...  6.33 us
    pallas_call x2, Pallas kernels, finish(): pl.pallas_call(functools.partial(finish_kernel, places), out_shape=pltpu....  1.59 us
    pallas_call x1, Pallas kernels, prepare(): pl.pallas_call(prepare_kernel, out_shape=shapes, in_specs=[far_spec()] *...  1.58 us
  transfers between devices with their start and end apart: 13, of which 7 were waited for; matrix products, arithmetic and copies ran while one was open for 0% of the time, Pallas kernels for 21%

profile of v16, /device:TPU:0, one launch (start us, length us, event | category | flops | bytes accessed | tf_op | source)
XLA Modules:
  0.0 33.9 jit_solution(2878967415772850924)
XLA Ops:
  0.0 1.6 %shard_map.55 = (bf16[128,512]{1,0:T(8,128)(2,1)S(1)}, bf16[128,768]{1,0:T(8,128)(2,1)S(1)}, bf16[128,768]{1,0:T(8,128)(2,1)S(1)}) custom-call(bf16[128,2048]{1,0:T(8,128)(2,1)} %queries.1, f32[1,2048]{1,0:T(1,128)} %bitcast.1, s32[1,128]{1,0:T(1,128)} %rank.1), custom_call_target="tpu_custom_call" | custom-call | flops 67108864 | bytes 1048576 | tf_op jit(solution)/shard_map/pallas_call | solution.py:80
  1.6 3.1 %collective-permute-start = (bf16[128,512]{1,0:T(8,128)(2,1)S(1)}, bf16[128,512]{1,0:T(8,128)(2,1)S(1)}, u32[]{:S(2)}, u32[]{:S(2)}) collective-permute-start(bf16[128,512]{1,0:T(8,128)(2,1)S(1)} %get-tuple-element.31.refs_1_), channel_id=1, source_target_pairs={{0,4},{2,6},{4,8},{6,10},{8,12},{10,14},{12,0},{14,2},{1,5},{3,7},... | collective-permute-start | bytes 393224 | tf_op jit(solution)/shard_map/ppermute | solution.py:246
  4.7 1.6 %collective-permute-start.1 = (bf16[128,768]{1,0:T(8,128)(2,1)S(1)}, bf16[128,768]{1,0:T(8,128)(2,1)S(1)}, u32[]{:S(2)}, u32[]{:S(2)}) collective-permute-start(bf16[128,768]{1,0:T(8,128)(2,1)S(1)} %get-tuple-element.32.refs_2_), channel_id=1, source_target_pairs={{0,4},{2,6},{4,8},{6,10},{8,12},{10,14},{12,0},{14,2},{1,5},{3,7},... | collective-permute-start | bytes 589832 | tf_op jit(solution)/shard_map/ppermute | solution.py:246
  6.2 1.6 %collective-permute-start.2 = (bf16[128,768]{1,0:T(8,128)(2,1)S(1)}, bf16[128,768]{1,0:T(8,128)(2,1)S(1)}, u32[]{:S(2)}, u32[]{:S(2)}) collective-permute-start(bf16[128,768]{1,0:T(8,128)(2,1)S(1)} %get-tuple-element.33.refs_3_), channel_id=1, source_target_pairs={{0,4},{2,6},{4,8},{6,10},{8,12},{10,14},{12,0},{14,2},{1,5},{3,7},... | collective-permute-start | bytes 589832 | tf_op jit(solution)/shard_map/ppermute | solution.py:246
  7.8 3.3 %shard_map.56 = (f32[384,128]{1,0:T(8,128)S(1)}, f32[384,128]{1,0:T(8,128)S(1)}, bf16[384,2048]{1,0:T(8,128)(2,1)S(1)}, bf16[384,2048]{1,0:T(8,128)(2,1)S(1)}) custom-call(bf16[768,2048]{1,0:T(8,128)(2,1)} %refs_0_.1, bf16[128,512]{1,0:T(8,128)(2,1)S(1)} %get-tuple-element.31.refs_1_, bf16[128,768]{1,0:T(8,128)(2,1)S(1)} %get-tuple-element.32.refs_2_, ...), custom_call_target="tpu_custom_call" | custom-call | flops 402653184 | bytes 393216 | tf_op jit(solution)/shard_map/pallas_call | solution.py:181
  11.2 1.6 %collective-permute-start.3 = (bf16[128,512]{1,0:T(8,128)(2,1)S(1)}, bf16[128,512]{1,0:T(8,128)(2,1)S(1)}, u32[]{:S(2)}, u32[]{:S(2)}) collective-permute-start(bf16[128,512]{1,0:T(8,128)(2,1)S(1)} %broadcast_select_fusion.2), channel_id=1, source_target_pairs={{0,2},{2,0},{4,6},{6,4},{8,10},{10,8},{12,14},{14,12},{1,3},{3,1},... | collective-permute-start | bytes 393224 | tf_op jit(solution)/shard_map/ppermute | solution.py:246
  12.8 2.4 %collective-permute-done.1.refs_3_ = bf16[128,768]{1,0:T(8,128)(2,1)S(1)} collective-permute-done((bf16[128,768]{1,0:T(8,128)(2,1)S(1)}, bf16[128,768]{1,0:T(8,128)(2,1)S(1)}, u32[]{:S(2)}, u32[]{:S(2)}) %collective-permute-start.1) | collective-permute-done | bytes 196640 | tf_op jit(solution)/shard_map/ppermute | solution.py:246
  15.3 1.8 %collective-permute-start.7 = (bf16[128,768]{1,0:T(8,128)(2,1)S(1)}, bf16[128,768]{1,0:T(8,128)(2,1)S(1)}, u32[]{:S(2)}, u32[]{:S(2)}) collective-permute-start(bf16[128,768]{1,0:T(8,128)(2,1)S(1)} %broadcast_select_fusion), channel_id=1, source_target_pairs={{0,2},{2,0},{4,6},{6,4},{8,10},{10,8},{12,14},{14,12},{1,3},{3,1},... | collective-permute-start | bytes 589832 | tf_op jit(solution)/shard_map/ppermute | solution.py:246
  17.1 1.6 %collective-permute-done.2.refs_4_ = bf16[128,768]{1,0:T(8,128)(2,1)S(1)} collective-permute-done((bf16[128,768]{1,0:T(8,128)(2,1)S(1)}, bf16[128,768]{1,0:T(8,128)(2,1)S(1)}, u32[]{:S(2)}, u32[]{:S(2)}) %collective-permute-start.2) | collective-permute-done | bytes 196640 | tf_op jit(solution)/shard_map/ppermute | solution.py:246
  18.6 1.5 %collective-permute-start.6 = (bf16[128,768]{1,0:T(8,128)(2,1)S(1)}, bf16[128,768]{1,0:T(8,128)(2,1)S(1)}, u32[]{:S(2)}, u32[]{:S(2)}) collective-permute-start(bf16[128,768]{1,0:T(8,128)(2,1)S(1)} %broadcast_select_fusion.1), channel_id=1, source_target_pairs={{0,2},{2,4},{4,6},{6,8},{8,10},{10,12},{12,14},{14,0},{1,3},{3,5},... | collective-permute-start | bytes 589832 | tf_op jit(solution)/shard_map/ppermute | solution.py:246
  20.2 0.3 collective-permute-start.5
  20.5 3.3 %collective-permute-done.4.refs_4_ = bf16[128,512]{1,0:T(8,128)(2,1)S(1)} collective-permute-done((bf16[128,512]{1,0:T(8,128)(2,1)S(1)}, bf16[128,512]{1,0:T(8,128)(2,1)S(1)}, u32[]{:S(2)}, u32[]{:S(2)}) %collective-permute-start.4) | collective-permute-done | bytes 131104 | tf_op jit(solution)/shard_map/ppermute | solution.py:246
  24.5 1.0 %shard_map.57 = (f32[384,128]{1,0:T(8,128)S(1)}, f32[384,128]{1,0:T(8,128)S(1)}) custom-call(bf16[384,2048]{1,0:T(8,128)(2,1)S(1)} %get-tuple-element.34.refs_0_.refs_1_, bf16[384,2048]{1,0:T(8,128)(2,1)S(1)} %get-tuple-element.35.refs_1_.refs_2_, bf16[128,512]{1,0:T(8,128)(2,1)S(1)} %collective-permute-done.refs_2_, ...), custom_call_target="tpu_custom_call" | custom-call | flops 402653184 | bytes 393216 | tf_op jit(solution)/shard_map/pallas_call | solution.py:181
  25.5 0.6 %collective-permute-start.12 = (f32[384,128]{1,0:T(8,128)S(1)}, f32[384,128]{1,0:T(8,128)S(1)}, u32[]{:S(2)}, u32[]{:S(2)}) collective-permute-start(f32[384,128]{1,0:T(8,128)S(1)} %get-tuple-element.56), channel_id=1, source_target_pairs={{0,1},{1,0},{2,3},{3,2},{4,5},{5,4},{6,7},{7,6},{8,9},{9,8},{10,11... | collective-permute-start | bytes 589832 | tf_op jit(solution)/shard_map/ppermute | solution.py:246
  26.0 0.4 %shard_map.58 = (f32[384,128]{1,0:T(8,128)S(1)}, f32[384,128]{1,0:T(8,128)S(1)}, f32[384,128]{1,0:T(8,128)S(1)}, f32[384,128]{1,0:T(8,128)S(1)}, s32[8,128]{1,0:T(8,128)S(1)}) custom-call(s32[1]{0:T(128)S(6)} %copy.8.refs_0_, bf16[384,2048]{1,0:T(8,128)(2,1)S(1)} %get-tuple-element.34.refs_0_.refs_1_, ...), custom_call_target="tpu_custom_call" | custom-call | flops 201326592 | bytes 786432 | tf_op jit(solution)/shard_map/pallas_call | solution.py:181
  26.4 0.5 %shard_map.59 = (f32[384,128]{1,0:T(8,128)S(1)}, f32[384,128]{1,0:T(8,128)S(1)}, f32[384,128]{1,0:T(8,128)S(1)}, f32[384,128]{1,0:T(8,128)S(1)}) custom-call(bf16[384,2048]{1,0:T(8,128)(2,1)S(1)} %get-tuple-element.34.refs_0_.refs_1_, bf16[384,2048]{1,0:T(8,128)(2,1)S(1)} %get-tuple-element.35.refs_1_.refs_2_, ...), custom_call_target="tpu_custom_call" | custom-call | flops 150994944 | bytes 786432 | tf_op jit(solution)/shard_map/pallas_call | solution.py:181
  26.9 2.4 %collective-permute-done.6.refs_3_ = bf16[128,768]{1,0:T(8,128)(2,1)S(1)} collective-permute-done((bf16[128,768]{1,0:T(8,128)(2,1)S(1)}, bf16[128,768]{1,0:T(8,128)(2,1)S(1)}, u32[]{:S(2)}, u32[]{:S(2)}) %collective-permute-start.6) | collective-permute-done | bytes 196640 | tf_op jit(solution)/shard_map/ppermute | solution.py:246
  29.3 0.6 %collective-permute-done.5.refs_2_ = bf16[128,768]{1,0:T(8,128)(2,1)S(1)} collective-permute-done((bf16[128,768]{1,0:T(8,128)(2,1)S(1)}, bf16[128,768]{1,0:T(8,128)(2,1)S(1)}, u32[]{:S(2)}, u32[]{:S(2)}) %collective-permute-start.5) | collective-permute-done | bytes 196640 | tf_op jit(solution)/shard_map/ppermute | solution.py:246
  30.0 0.5 %shard_map.60 = (f32[384,128]{1,0:T(8,128)S(1)}, f32[384,128]{1,0:T(8,128)S(1)}, f32[384,128]{1,0:T(8,128)S(1)}, f32[384,128]{1,0:T(8,128)S(1)}) custom-call(bf16[384,2048]{1,0:T(8,128)(2,1)S(1)} %get-tuple-element.34.refs_0_.refs_1_, bf16[384,2048]{1,0:T(8,128)(2,1)S(1)} %get-tuple-element.35.refs_1_.refs_2_, ...), custom_call_target="tpu_custom_call" | custom-call | flops 301989888 | bytes 786432 | tf_op jit(solution)/shard_map/pallas_call | solution.py:181
  30.6 0.7 %collective-permute-done.9.refs_2_ = bf16[128,768]{1,0:T(8,128)(2,1)S(1)} collective-permute-done((bf16[128,768]{1,0:T(8,128)(2,1)S(1)}, bf16[128,768]{1,0:T(8,128)(2,1)S(1)}, u32[]{:S(2)}, u32[]{:S(2)}) %collective-permute-start.9) | collective-permute-done | bytes 196640 | tf_op jit(solution)/shard_map/ppermute | solution.py:246
  31.3 0.3 shard_map.62
  31.7 0.8 %shard_map.63.refs_4_ = f32[384,512]{1,0:T(8,128)} custom-call(s32[8,128]{1,0:T(8,128)S(1)} %get-tuple-element.40.limit, f32[384,128]{1,0:T(8,128)S(1)} %get-tuple-element.38.refs_0_, f32[384,128]{1,0:T(8,128)S(1)} %collective-permute-done.11.refs_1_, f32[384,128]{1,0:T(8,128)S(1)} %get-tuple-element.36.refs_2_, f32[384,128]{1,0:T(8,128)S(1)} %collective-permute-done.12.refs_3_), custom_call_target="tpu_custom_call" | custom-call | flops 98304 | bytes 1179648 | tf_op jit(solution)/shard_map/pallas_call | solution.py:216
  32.5 0.3 shard_map.61.refs_2_
  33.1 0.8 %shard_map.64 = f32[384,512]{1,0:T(8,128)} custom-call(s32[8,128]{1,0:T(8,128)S(1)} %get-tuple-element.40.limit, f32[384,128]{1,0:T(8,128)S(1)} %get-tuple-element.50.refs_0_, f32[384,128]{1,0:T(8,128)S(1)} %collective-permute-done.8.refs_1_, f32[384,128]{1,0:T(8,128)S(1)} %shard_map.61.refs_2_, ...), custom_call_target="tpu_custom_call", output_to_operand_aliasing={{}: (5, {})} | custom-call | flops 98304 | bytes 1179648 | tf_op jit(solution)/shard_map/pallas_call | solution.py:216
  (15 shorter events, 0.5 us)
Async XLA Ops:
  1.6 9.6 %collective-permute-start = (bf16[128,512]{1,0:T(8,128)(2,1)S(1)}, bf16[128,512]{1,0:T(8,128)(2,1)S(1)}, u32[]{:S(2)}, u32[]{:S(2)}) collective-permute-start(bf16[128,512]{1,0:T(8,128)(2,1)S(1)} %get-tuple-element.31.refs_1_), channel_id=1, source_target_pairs={{0,4},{2,6},{4,8},{6,10},{8,12},{10,14},{12,0},{14,2},{1,5},{3,7},... | collective-permute-start | bytes 393224 | tf_op jit(solution)/shard_map/ppermute | solution.py:246
  4.7 10.6 %collective-permute-start.1 = (bf16[128,768]{1,0:T(8,128)(2,1)S(1)}, bf16[128,768]{1,0:T(8,128)(2,1)S(1)}, u32[]{:S(2)}, u32[]{:S(2)}) collective-permute-start(bf16[128,768]{1,0:T(8,128)(2,1)S(1)} %get-tuple-element.32.refs_2_), channel_id=1, source_target_pairs={{0,4},{2,6},{4,8},{6,10},{8,12},{10,14},{12,0},{14,2},{1,5},{3,7},... | collective-permute-start | bytes 589832 | tf_op jit(solution)/shard_map/ppermute | solution.py:246
  6.2 12.4 %collective-permute-start.2 = (bf16[128,768]{1,0:T(8,128)(2,1)S(1)}, bf16[128,768]{1,0:T(8,128)(2,1)S(1)}, u32[]{:S(2)}, u32[]{:S(2)}) collective-permute-start(bf16[128,768]{1,0:T(8,128)(2,1)S(1)} %get-tuple-element.33.refs_3_), channel_id=1, source_target_pairs={{0,4},{2,6},{4,8},{6,10},{8,12},{10,14},{12,0},{14,2},{1,5},{3,7},... | collective-permute-start | bytes 589832 | tf_op jit(solution)/shard_map/ppermute | solution.py:246
  11.2 5.9 %collective-permute-start.3 = (bf16[128,512]{1,0:T(8,128)(2,1)S(1)}, bf16[128,512]{1,0:T(8,128)(2,1)S(1)}, u32[]{:S(2)}, u32[]{:S(2)}) collective-permute-start(bf16[128,512]{1,0:T(8,128)(2,1)S(1)} %broadcast_select_fusion.2), channel_id=1, source_target_pairs={{0,2},{2,0},{4,6},{6,4},{8,10},{10,8},{12,14},{14,12},{1,3},{3,1},... | collective-permute-start | bytes 393224 | tf_op jit(solution)/shard_map/ppermute | solution.py:246
  15.3 8.6 %collective-permute-start.7 = (bf16[128,768]{1,0:T(8,128)(2,1)S(1)}, bf16[128,768]{1,0:T(8,128)(2,1)S(1)}, u32[]{:S(2)}, u32[]{:S(2)}) collective-permute-start(bf16[128,768]{1,0:T(8,128)(2,1)S(1)} %broadcast_select_fusion), channel_id=1, source_target_pairs={{0,2},{2,0},{4,6},{6,4},{8,10},{10,8},{12,14},{14,12},{1,3},{3,1},... | collective-permute-start | bytes 589832 | tf_op jit(solution)/shard_map/ppermute | solution.py:246
  17.1 6.8 %collective-permute-start.4 = (bf16[128,512]{1,0:T(8,128)(2,1)S(1)}, bf16[128,512]{1,0:T(8,128)(2,1)S(1)}, u32[]{:S(2)}, u32[]{:S(2)}) collective-permute-start(bf16[128,512]{1,0:T(8,128)(2,1)S(1)} %collective-permute-done.3.refs_3_), channel_id=1, source_target_pairs={{0,4},{2,6},{4,8},{6,10},{8,12},{10,14},{12,0},{14,2},{1,5},{3,7},... | collective-permute-start | bytes 393224 | tf_op jit(solution)/shard_map/ppermute | solution.py:246
  18.6 10.7 %collective-permute-start.6 = (bf16[128,768]{1,0:T(8,128)(2,1)S(1)}, bf16[128,768]{1,0:T(8,128)(2,1)S(1)}, u32[]{:S(2)}, u32[]{:S(2)}) collective-permute-start(bf16[128,768]{1,0:T(8,128)(2,1)S(1)} %broadcast_select_fusion.1), channel_id=1, source_target_pairs={{0,2},{2,4},{4,6},{6,8},{8,10},{10,12},{12,14},{14,0},{1,3},{3,5},... | collective-permute-start | bytes 589832 | tf_op jit(solution)/shard_map/ppermute | solution.py:246
  20.2 9.8 %collective-permute-start.5 = (bf16[128,768]{1,0:T(8,128)(2,1)S(1)}, bf16[128,768]{1,0:T(8,128)(2,1)S(1)}, u32[]{:S(2)}, u32[]{:S(2)}) collective-permute-start(bf16[128,768]{1,0:T(8,128)(2,1)S(1)} %collective-permute-done.2.refs_4_), channel_id=1, source_target_pairs={{0,2},{2,0},{4,6},{6,4},{8,10},{10,8},{12,14},{14,12},{1,3},{3,1},... | collective-permute-start | bytes 589832 | tf_op jit(solution)/shard_map/ppermute | solution.py:246
  23.8 7.5 %collective-permute-start.9 = (bf16[128,768]{1,0:T(8,128)(2,1)S(1)}, bf16[128,768]{1,0:T(8,128)(2,1)S(1)}, u32[]{:S(2)}, u32[]{:S(2)}) collective-permute-start(bf16[128,768]{1,0:T(8,128)(2,1)S(1)} %collective-permute-done.7.refs_2_), channel_id=1, source_target_pairs={{0,4},{2,6},{4,8},{6,10},{8,12},{10,14},{12,0},{14,2},{1,5},{3,7},... | collective-permute-start | bytes 589832 | tf_op jit(solution)/shard_map/ppermute | solution.py:246
  23.8 7.9 %collective-permute-start.11 = (f32[384,128]{1,0:T(8,128)S(1)}, f32[384,128]{1,0:T(8,128)S(1)}, u32[]{:S(2)}, u32[]{:S(2)}) collective-permute-start(f32[384,128]{1,0:T(8,128)S(1)} %get-tuple-element.55), channel_id=1, source_target_pairs={{0,1},{1,0},{2,3},{3,2},{4,5},{5,4},{6,7},{7,6},{8,9},{9,8},{10,11... | collective-permute-start | bytes 589832 | tf_op jit(solution)/shard_map/ppermute | solution.py:246
  25.5 6.2 %collective-permute-start.12 = (f32[384,128]{1,0:T(8,128)S(1)}, f32[384,128]{1,0:T(8,128)S(1)}, u32[]{:S(2)}, u32[]{:S(2)}) collective-permute-start(f32[384,128]{1,0:T(8,128)S(1)} %get-tuple-element.56), channel_id=1, source_target_pairs={{0,1},{1,0},{2,3},{3,2},{4,5},{5,4},{6,7},{7,6},{8,9},{9,8},{10,11... | collective-permute-start | bytes 589832 | tf_op jit(solution)/shard_map/ppermute | solution.py:246
  30.5 2.3 %collective-permute-start.8 = (f32[384,128]{1,0:T(8,128)S(1)}, f32[384,128]{1,0:T(8,128)S(1)}, u32[]{:S(2)}, u32[]{:S(2)}) collective-permute-start(f32[384,128]{1,0:T(8,128)S(1)} %get-tuple-element.51), channel_id=1, source_target_pairs={{0,1},{1,0},{2,3},{3,2},{4,5},{5,4},{6,7},{7,6},{8,9},{9,8},{10,11... | collective-permute-start | bytes 589832 | tf_op jit(solution)/shard_map/ppermute | solution.py:246
  31.6 1.5 %collective-permute-start.10 = (f32[384,128]{1,0:T(8,128)S(1)}, f32[384,128]{1,0:T(8,128)S(1)}, u32[]{:S(2)}, u32[]{:S(2)}) collective-permute-start(f32[384,128]{1,0:T(8,128)S(1)} %shard_map.62), channel_id=1, source_target_pairs={{0,1},{1,0},{2,3},{3,2},{4,5},{5,4},{6,7},{7,6},{8,9},{9,8},{10,11... | collective-permute-start | bytes 589832 | tf_op jit(solution)/shard_map/ppermute | solution.py:246

commit v17 on v16

--- a/solution.py
+++ b/solution.py
@@ -9,10 +9,10 @@
 
 STEPS = 4
 KINDS = "UUT"
-PARTS = (4, 6, 6)
+PARTS = (5, 5, 6)
 CHAIN = ("b0", "o1", "b2", "t1")
 ORDER = ("B0", "B1", "B2", "C0", "C1", "E0", "E1", "R2", "C2")
-TIES = {"C2": "C0", "E1": "E0"}
+TIES = {"C2": "C0"}
 EARLY = "C0"
 OUT = "none"
 CHUNKS = len(PARTS)

time: 34.1 us -> 34.6 us (1.015)
  starting transfers between devices: 12.3 us -> 15.9 us
  waiting for transfers between devices: 11.3 us -> 8.83 us
  Pallas kernels: 9.5 us -> 8.89 us
    ppermute x13, starting transfers between devices: 12.3 us -> 15.9 us  [send(): return lax.ppermute(block, axis, route)]
    ppermute x13, waiting for transfers between devices: 11.3 us -> 8.83 us  [send(): return lax.ppermute(block, axis, route)]
    pallas_call x7, Pallas kernels: 6.33 us -> 5.69 us  [more_scores(): pl.pallas_call(functools.partial(scores_kernel, tuple(placed), fresh, loa...]
  transfers between devices with their start and end apart: 13 -> 13, of which waited for: 7 -> 5; matrix products, arithmetic and copies ran while one was open for 0% -> 0% of each run, Pallas kernels for 21% -> 19%
where the time goes in v17:
time: 34.6 us; the launch traced here: 34.5 us
  starting transfers between devices  15.9 us (46%)
  Pallas kernels  8.89 us (26%)
  waiting for transfers between devices  8.83 us (26%)
  between operations  0.77 us (2%)
    ppermute x13, starting transfers between devices, send(): return lax.ppermute(block, axis, route)  15.9 us
    ppermute x13, waiting for transfers between devices, send(): return lax.ppermute(block, axis, route)  8.83 us
    pallas_call x7, Pallas kernels, more_scores(): pl.pallas_call(functools.partial(scores_kernel, tuple(placed), fresh, loa...  5.69 us
    pallas_call x1, Pallas kernels, prepare(): pl.pallas_call(prepare_kernel, out_shape=shapes, in_specs=[far_spec()] *...  1.6 us
    pallas_call x2, Pallas kernels, finish(): pl.pallas_call(functools.partial(finish_kernel, places), out_shape=pltpu....  1.6 us
  transfers between devices with their start and end apart: 13, of which 5 were waited for; matrix products, arithmetic and copies ran while one was open for 0% of the time, Pallas kernels for 19%

profile of v17, /device:TPU:0, one launch (start us, length us, event | category | flops | bytes accessed | tf_op | source)
XLA Modules:
  0.0 34.5 jit_solution(13632804259741492215)
XLA Ops:
  0.0 1.6 %shard_map.55 = (bf16[128,640]{1,0:T(8,128)(2,1)S(1)}, bf16[128,640]{1,0:T(8,128)(2,1)S(1)}, bf16[128,768]{1,0:T(8,128)(2,1)S(1)}) custom-call(bf16[128,2048]{1,0:T(8,128)(2,1)} %queries.1, f32[1,2048]{1,0:T(1,128)} %bitcast.1, s32[1,128]{1,0:T(1,128)} %rank.1), custom_call_target="tpu_custom_call" | custom-call | flops 67108864 | bytes 1048576 | tf_op jit(solution)/shard_map/pallas_call | solution.py:80
  1.6 3.1 %collective-permute-start = (bf16[128,640]{1,0:T(8,128)(2,1)S(1)}, bf16[128,640]{1,0:T(8,128)(2,1)S(1)}, u32[]{:S(2)}, u32[]{:S(2)}) collective-permute-start(bf16[128,640]{1,0:T(8,128)(2,1)S(1)} %get-tuple-element.30.refs_1_), channel_id=1, source_target_pairs={{0,4},{2,6},{4,8},{6,10},{8,12},{10,14},{12,0},{14,2},{1,5},{3,7},... | collective-permute-start | bytes 491528 | tf_op jit(solution)/shard_map/ppermute | solution.py:246
  4.7 1.6 %collective-permute-start.1 = (bf16[128,640]{1,0:T(8,128)(2,1)S(1)}, bf16[128,640]{1,0:T(8,128)(2,1)S(1)}, u32[]{:S(2)}, u32[]{:S(2)}) collective-permute-start(bf16[128,640]{1,0:T(8,128)(2,1)S(1)} %get-tuple-element.31.refs_2_), channel_id=1, source_target_pairs={{0,4},{2,6},{4,8},{6,10},{8,12},{10,14},{12,0},{14,2},{1,5},{3,7},... | collective-permute-start | bytes 491528 | tf_op jit(solution)/shard_map/ppermute | solution.py:246
  6.3 1.6 %collective-permute-start.2 = (bf16[128,768]{1,0:T(8,128)(2,1)S(1)}, bf16[128,768]{1,0:T(8,128)(2,1)S(1)}, u32[]{:S(2)}, u32[]{:S(2)}) collective-permute-start(bf16[128,768]{1,0:T(8,128)(2,1)S(1)} %get-tuple-element.32.refs_3_), channel_id=1, source_target_pairs={{0,4},{2,6},{4,8},{6,10},{8,12},{10,14},{12,0},{14,2},{1,5},{3,7},... | collective-permute-start | bytes 589832 | tf_op jit(solution)/shard_map/ppermute | solution.py:246
  7.8 2.7 %shard_map.56 = (f32[384,128]{1,0:T(8,128)S(1)}, f32[384,128]{1,0:T(8,128)S(1)}, bf16[384,2048]{1,0:T(8,128)(2,1)S(1)}, bf16[384,2048]{1,0:T(8,128)(2,1)S(1)}) custom-call(bf16[768,2048]{1,0:T(8,128)(2,1)} %refs_0_.1, bf16[128,640]{1,0:T(8,128)(2,1)S(1)} %get-tuple-element.30.refs_1_, bf16[128,640]{1,0:T(8,128)(2,1)S(1)} %get-tuple-element.31.refs_2_, ...), custom_call_target="tpu_custom_call" | custom-call | flops 402653184 | bytes 393216 | tf_op jit(solution)/shard_map/pallas_call | solution.py:181
  10.5 1.2 %collective-permute-done.refs_2_ = bf16[128,640]{1,0:T(8,128)(2,1)S(1)} collective-permute-done((bf16[128,640]{1,0:T(8,128)(2,1)S(1)}, bf16[128,640]{1,0:T(8,128)(2,1)S(1)}, u32[]{:S(2)}, u32[]{:S(2)}) %collective-permute-start) | collective-permute-done | bytes 163872 | tf_op jit(solution)/shard_map/ppermute | solution.py:246
  11.8 1.8 %collective-permute-start.3 = (bf16[128,640]{1,0:T(8,128)(2,1)S(1)}, bf16[128,640]{1,0:T(8,128)(2,1)S(1)}, u32[]{:S(2)}, u32[]{:S(2)}) collective-permute-start(bf16[128,640]{1,0:T(8,128)(2,1)S(1)} %broadcast_select_fusion.2), channel_id=1, source_target_pairs={{0,2},{2,0},{4,6},{6,4},{8,10},{10,8},{12,14},{14,12},{1,3},{3,1},... | collective-permute-start | bytes 491528 | tf_op jit(solution)/shard_map/ppermute | solution.py:246
  13.6 1.7 %collective-permute-done.1.refs_3_ = bf16[128,640]{1,0:T(8,128)(2,1)S(1)} collective-permute-done((bf16[128,640]{1,0:T(8,128)(2,1)S(1)}, bf16[128,640]{1,0:T(8,128)(2,1)S(1)}, u32[]{:S(2)}, u32[]{:S(2)}) %collective-permute-start.1) | collective-permute-done | bytes 163872 | tf_op jit(solution)/shard_map/ppermute | solution.py:246
  15.3 1.8 %collective-permute-start.7 = (bf16[128,640]{1,0:T(8,128)(2,1)S(1)}, bf16[128,640]{1,0:T(8,128)(2,1)S(1)}, u32[]{:S(2)}, u32[]{:S(2)}) collective-permute-start(bf16[128,640]{1,0:T(8,128)(2,1)S(1)} %broadcast_select_fusion.1), channel_id=1, source_target_pairs={{0,2},{2,0},{4,6},{6,4},{8,10},{10,8},{12,14},{14,12},{1,3},{3,1},... | collective-permute-start | bytes 491528 | tf_op jit(solution)/shard_map/ppermute | solution.py:246
  17.1 0.8 %collective-permute-done.3.refs_3_ = bf16[128,640]{1,0:T(8,128)(2,1)S(1)} collective-permute-done((bf16[128,640]{1,0:T(8,128)(2,1)S(1)}, bf16[128,640]{1,0:T(8,128)(2,1)S(1)}, u32[]{:S(2)}, u32[]{:S(2)}) %collective-permute-start.3) | collective-permute-done | bytes 163872 | tf_op jit(solution)/shard_map/ppermute | solution.py:246
  17.9 0.8 %collective-permute-start.4 = (bf16[128,640]{1,0:T(8,128)(2,1)S(1)}, bf16[128,640]{1,0:T(8,128)(2,1)S(1)}, u32[]{:S(2)}, u32[]{:S(2)}) collective-permute-start(bf16[128,640]{1,0:T(8,128)(2,1)S(1)} %collective-permute-done.3.refs_3_), channel_id=1, source_target_pairs={{0,4},{2,6},{4,8},{6,10},{8,12},{10,14},{12,0},{14,2},{1,5},{3,7},... | collective-permute-start | bytes 491528 | tf_op jit(solution)/shard_map/ppermute | solution.py:246
  18.7 1.6 %collective-permute-start.6 = (bf16[128,768]{1,0:T(8,128)(2,1)S(1)}, bf16[128,768]{1,0:T(8,128)(2,1)S(1)}, u32[]{:S(2)}, u32[]{:S(2)}) collective-permute-start(bf16[128,768]{1,0:T(8,128)(2,1)S(1)} %broadcast_select_fusion), channel_id=1, source_target_pairs={{0,2},{2,4},{4,6},{6,8},{8,10},{10,12},{12,14},{14,0},{1,3},{3,5},... | collective-permute-start | bytes 589832 | tf_op jit(solution)/shard_map/ppermute | solution.py:246
  20.3 1.5 %collective-permute-start.5 = (bf16[128,768]{1,0:T(8,128)(2,1)S(1)}, bf16[128,768]{1,0:T(8,128)(2,1)S(1)}, u32[]{:S(2)}, u32[]{:S(2)}) collective-permute-start(bf16[128,768]{1,0:T(8,128)(2,1)S(1)} %collective-permute-done.2.refs_4_), channel_id=1, source_target_pairs={{0,2},{2,0},{4,6},{6,4},{8,10},{10,8},{12,14},{14,12},{1,3},{3,1},... | collective-permute-start | bytes 589832 | tf_op jit(solution)/shard_map/ppermute | solution.py:246
  21.8 1.6 %collective-permute-start.9 = (bf16[128,640]{1,0:T(8,128)(2,1)S(1)}, bf16[128,640]{1,0:T(8,128)(2,1)S(1)}, u32[]{:S(2)}, u32[]{:S(2)}) collective-permute-start(bf16[128,640]{1,0:T(8,128)(2,1)S(1)} %collective-permute-done.7.refs_2_), channel_id=1, source_target_pairs={{0,4},{2,6},{4,8},{6,10},{8,12},{10,14},{12,0},{14,2},{1,5},{3,7},... | collective-permute-start | bytes 491528 | tf_op jit(solution)/shard_map/ppermute | solution.py:246
  24.0 1.0 %shard_map.57 = (f32[384,128]{1,0:T(8,128)S(1)}, f32[384,128]{1,0:T(8,128)S(1)}) custom-call(bf16[384,2048]{1,0:T(8,128)(2,1)S(1)} %get-tuple-element.33.refs_0_.refs_1_, bf16[384,2048]{1,0:T(8,128)(2,1)S(1)} %get-tuple-element.34.refs_1_.refs_2_, bf16[128,640]{1,0:T(8,128)(2,1)S(1)} %collective-permute-done.refs_2_, ...), custom_call_target="tpu_custom_call" | custom-call | flops 402653184 | bytes 393216 | tf_op jit(solution)/shard_map/pallas_call | solution.py:181
  25.0 1.5 %collective-permute-done.4.refs_4_ = bf16[128,640]{1,0:T(8,128)(2,1)S(1)} collective-permute-done((bf16[128,640]{1,0:T(8,128)(2,1)S(1)}, bf16[128,640]{1,0:T(8,128)(2,1)S(1)}, u32[]{:S(2)}, u32[]{:S(2)}) %collective-permute-start.4) | collective-permute-done | bytes 163872 | tf_op jit(solution)/shard_map/ppermute | solution.py:246
  26.5 0.5 %shard_map.58 = (f32[384,128]{1,0:T(8,128)S(1)}, f32[384,128]{1,0:T(8,128)S(1)}, f32[384,128]{1,0:T(8,128)S(1)}, f32[384,128]{1,0:T(8,128)S(1)}, s32[8,128]{1,0:T(8,128)S(1)}) custom-call(s32[1]{0:T(128)S(6)} %copy.8.refs_0_, bf16[384,2048]{1,0:T(8,128)(2,1)S(1)} %get-tuple-element.33.refs_0_.refs_1_, ...), custom_call_target="tpu_custom_call" | custom-call | flops 251658240 | bytes 786432 | tf_op jit(solution)/shard_map/pallas_call | solution.py:181
  27.0 0.4 %shard_map.59 = (f32[384,128]{1,0:T(8,128)S(1)}, f32[384,128]{1,0:T(8,128)S(1)}, f32[384,128]{1,0:T(8,128)S(1)}, f32[384,128]{1,0:T(8,128)S(1)}) custom-call(bf16[384,2048]{1,0:T(8,128)(2,1)S(1)} %get-tuple-element.33.refs_0_.refs_1_, bf16[384,2048]{1,0:T(8,128)(2,1)S(1)} %get-tuple-element.34.refs_1_.refs_2_, ...), custom_call_target="tpu_custom_call" | custom-call | flops 125829120 | bytes 786432 | tf_op jit(solution)/shard_map/pallas_call | solution.py:181
  27.4 3.6 %collective-permute-done.6.refs_3_ = bf16[128,768]{1,0:T(8,128)(2,1)S(1)} collective-permute-done((bf16[128,768]{1,0:T(8,128)(2,1)S(1)}, bf16[128,768]{1,0:T(8,128)(2,1)S(1)}, u32[]{:S(2)}, u32[]{:S(2)}) %collective-permute-start.6) | collective-permute-done | bytes 196640 | tf_op jit(solution)/shard_map/ppermute | solution.py:246
  31.1 0.5 %shard_map.60 = (f32[384,128]{1,0:T(8,128)S(1)}, f32[384,128]{1,0:T(8,128)S(1)}, f32[384,128]{1,0:T(8,128)S(1)}, f32[384,128]{1,0:T(8,128)S(1)}) custom-call(bf16[384,2048]{1,0:T(8,128)(2,1)S(1)} %get-tuple-element.33.refs_0_.refs_1_, bf16[384,2048]{1,0:T(8,128)(2,1)S(1)} %get-tuple-element.34.refs_1_.refs_2_, ...), custom_call_target="tpu_custom_call" | custom-call | flops 301989888 | bytes 786432 | tf_op jit(solution)/shard_map/pallas_call | solution.py:181
  32.0 0.6 %collective-permute-start.10 = (f32[384,128]{1,0:T(8,128)S(1)}, f32[384,128]{1,0:T(8,128)S(1)}, u32[]{:S(2)}, u32[]{:S(2)}) collective-permute-start(f32[384,128]{1,0:T(8,128)S(1)} %shard_map.62), channel_id=1, source_target_pairs={{0,1},{1,0},{2,3},{3,2},{4,5},{5,4},{6,7},{7,6},{8,9},{9,8},{10,11... | collective-permute-start | bytes 589832 | tf_op jit(solution)/shard_map/ppermute | solution.py:246
  32.5 0.8 %shard_map.63.refs_4_ = f32[384,512]{1,0:T(8,128)} custom-call(s32[8,128]{1,0:T(8,128)S(1)} %get-tuple-element.39.limit, f32[384,128]{1,0:T(8,128)S(1)} %get-tuple-element.37.refs_0_, f32[384,128]{1,0:T(8,128)S(1)} %collective-permute-done.11.refs_1_, f32[384,128]{1,0:T(8,128)S(1)} %get-tuple-element.35.refs_2_, f32[384,128]{1,0:T(8,128)S(1)} %collective-permute-done.12.refs_3_), custom_call_target="tpu_custom_call" | custom-call | flops 98304 | bytes 1179648 | tf_op jit(solution)/shard_map/pallas_call | solution.py:216
  33.3 0.3 shard_map.61.refs_2_
  33.7 0.8 %shard_map.64 = f32[384,512]{1,0:T(8,128)} custom-call(s32[8,128]{1,0:T(8,128)S(1)} %get-tuple-element.39.limit, f32[384,128]{1,0:T(8,128)S(1)} %get-tuple-element.49.refs_0_, f32[384,128]{1,0:T(8,128)S(1)} %collective-permute-done.8.refs_1_, f32[384,128]{1,0:T(8,128)S(1)} %shard_map.61.refs_2_, ...), custom_call_target="tpu_custom_call", output_to_operand_aliasing={{}: (5, {})} | custom-call | flops 98304 | bytes 1179648 | tf_op jit(solution)/shard_map/pallas_call | solution.py:216
  (15 shorter events, 0.5 us)
Async XLA Ops:
  1.6 10.1 %collective-permute-start = (bf16[128,640]{1,0:T(8,128)(2,1)S(1)}, bf16[128,640]{1,0:T(8,128)(2,1)S(1)}, u32[]{:S(2)}, u32[]{:S(2)}) collective-permute-start(bf16[128,640]{1,0:T(8,128)(2,1)S(1)} %get-tuple-element.30.refs_1_), channel_id=1, source_target_pairs={{0,4},{2,6},{4,8},{6,10},{8,12},{10,14},{12,0},{14,2},{1,5},{3,7},... | collective-permute-start | bytes 491528 | tf_op jit(solution)/shard_map/ppermute | solution.py:246
  4.7 10.6 %collective-permute-start.1 = (bf16[128,640]{1,0:T(8,128)(2,1)S(1)}, bf16[128,640]{1,0:T(8,128)(2,1)S(1)}, u32[]{:S(2)}, u32[]{:S(2)}) collective-permute-start(bf16[128,640]{1,0:T(8,128)(2,1)S(1)} %get-tuple-element.31.refs_2_), channel_id=1, source_target_pairs={{0,4},{2,6},{4,8},{6,10},{8,12},{10,14},{12,0},{14,2},{1,5},{3,7},... | collective-permute-start | bytes 491528 | tf_op jit(solution)/shard_map/ppermute | solution.py:246
  6.3 12.4 %collective-permute-start.2 = (bf16[128,768]{1,0:T(8,128)(2,1)S(1)}, bf16[128,768]{1,0:T(8,128)(2,1)S(1)}, u32[]{:S(2)}, u32[]{:S(2)}) collective-permute-start(bf16[128,768]{1,0:T(8,128)(2,1)S(1)} %get-tuple-element.32.refs_3_), channel_id=1, source_target_pairs={{0,4},{2,6},{4,8},{6,10},{8,12},{10,14},{12,0},{14,2},{1,5},{3,7},... | collective-permute-start | bytes 589832 | tf_op jit(solution)/shard_map/ppermute | solution.py:246
  11.8 6.1 %collective-permute-start.3 = (bf16[128,640]{1,0:T(8,128)(2,1)S(1)}, bf16[128,640]{1,0:T(8,128)(2,1)S(1)}, u32[]{:S(2)}, u32[]{:S(2)}) collective-permute-start(bf16[128,640]{1,0:T(8,128)(2,1)S(1)} %broadcast_select_fusion.2), channel_id=1, source_target_pairs={{0,2},{2,0},{4,6},{6,4},{8,10},{10,8},{12,14},{14,12},{1,3},{3,1},... | collective-permute-start | bytes 491528 | tf_op jit(solution)/shard_map/ppermute | solution.py:246
  15.3 6.5 %collective-permute-start.7 = (bf16[128,640]{1,0:T(8,128)(2,1)S(1)}, bf16[128,640]{1,0:T(8,128)(2,1)S(1)}, u32[]{:S(2)}, u32[]{:S(2)}) collective-permute-start(bf16[128,640]{1,0:T(8,128)(2,1)S(1)} %broadcast_select_fusion.1), channel_id=1, source_target_pairs={{0,2},{2,0},{4,6},{6,4},{8,10},{10,8},{12,14},{14,12},{1,3},{3,1},... | collective-permute-start | bytes 491528 | tf_op jit(solution)/shard_map/ppermute | solution.py:246
  17.9 8.6 %collective-permute-start.4 = (bf16[128,640]{1,0:T(8,128)(2,1)S(1)}, bf16[128,640]{1,0:T(8,128)(2,1)S(1)}, u32[]{:S(2)}, u32[]{:S(2)}) collective-permute-start(bf16[128,640]{1,0:T(8,128)(2,1)S(1)} %collective-permute-done.3.refs_3_), channel_id=1, source_target_pairs={{0,4},{2,6},{4,8},{6,10},{8,12},{10,14},{12,0},{14,2},{1,5},{3,7},... | collective-permute-start | bytes 491528 | tf_op jit(solution)/shard_map/ppermute | solution.py:246
  18.7 12.3 %collective-permute-start.6 = (bf16[128,768]{1,0:T(8,128)(2,1)S(1)}, bf16[128,768]{1,0:T(8,128)(2,1)S(1)}, u32[]{:S(2)}, u32[]{:S(2)}) collective-permute-start(bf16[128,768]{1,0:T(8,128)(2,1)S(1)} %broadcast_select_fusion), channel_id=1, source_target_pairs={{0,2},{2,4},{4,6},{6,8},{8,10},{10,12},{12,14},{14,0},{1,3},{3,5},... | collective-permute-start | bytes 589832 | tf_op jit(solution)/shard_map/ppermute | solution.py:246
  20.3 10.7 %collective-permute-start.5 = (bf16[128,768]{1,0:T(8,128)(2,1)S(1)}, bf16[128,768]{1,0:T(8,128)(2,1)S(1)}, u32[]{:S(2)}, u32[]{:S(2)}) collective-permute-start(bf16[128,768]{1,0:T(8,128)(2,1)S(1)} %collective-permute-done.2.refs_4_), channel_id=1, source_target_pairs={{0,2},{2,0},{4,6},{6,4},{8,10},{10,8},{12,14},{14,12},{1,3},{3,1},... | collective-permute-start | bytes 589832 | tf_op jit(solution)/shard_map/ppermute | solution.py:246
  21.8 9.9 %collective-permute-start.9 = (bf16[128,640]{1,0:T(8,128)(2,1)S(1)}, bf16[128,640]{1,0:T(8,128)(2,1)S(1)}, u32[]{:S(2)}, u32[]{:S(2)}) collective-permute-start(bf16[128,640]{1,0:T(8,128)(2,1)S(1)} %collective-permute-done.7.refs_2_), channel_id=1, source_target_pairs={{0,4},{2,6},{4,8},{6,10},{8,12},{10,14},{12,0},{14,2},{1,5},{3,7},... | collective-permute-start | bytes 491528 | tf_op jit(solution)/shard_map/ppermute | solution.py:246
  23.4 9.2 %collective-permute-start.11 = (f32[384,128]{1,0:T(8,128)S(1)}, f32[384,128]{1,0:T(8,128)S(1)}, u32[]{:S(2)}, u32[]{:S(2)}) collective-permute-start(f32[384,128]{1,0:T(8,128)S(1)} %get-tuple-element.53), channel_id=1, source_target_pairs={{0,1},{1,0},{2,3},{3,2},{4,5},{5,4},{6,7},{7,6},{8,9},{9,8},{10,11... | collective-permute-start | bytes 589832 | tf_op jit(solution)/shard_map/ppermute | solution.py:246
  26.5 6.0 %collective-permute-start.12 = (f32[384,128]{1,0:T(8,128)S(1)}, f32[384,128]{1,0:T(8,128)S(1)}, u32[]{:S(2)}, u32[]{:S(2)}) collective-permute-start(f32[384,128]{1,0:T(8,128)S(1)} %get-tuple-element.54), channel_id=1, source_target_pairs={{0,1},{1,0},{2,3},{3,2},{4,5},{5,4},{6,7},{7,6},{8,9},{9,8},{10,11... | collective-permute-start | bytes 589832 | tf_op jit(solution)/shard_map/ppermute | solution.py:246
  31.6 2.1 %collective-permute-start.8 = (f32[384,128]{1,0:T(8,128)S(1)}, f32[384,128]{1,0:T(8,128)S(1)}, u32[]{:S(2)}, u32[]{:S(2)}) collective-permute-start(f32[384,128]{1,0:T(8,128)S(1)} %get-tuple-element.50), channel_id=1, source_target_pairs={{0,1},{1,0},{2,3},{3,2},{4,5},{5,4},{6,7},{7,6},{8,9},{9,8},{10,11... | collective-permute-start | bytes 589832 | tf_op jit(solution)/shard_map/ppermute | solution.py:246
  32.0 1.7 %collective-permute-start.10 = (f32[384,128]{1,0:T(8,128)S(1)}, f32[384,128]{1,0:T(8,128)S(1)}, u32[]{:S(2)}, u32[]{:S(2)}) collective-permute-start(f32[384,128]{1,0:T(8,128)S(1)} %shard_map.62), channel_id=1, source_target_pairs={{0,1},{1,0},{2,3},{3,2},{4,5},{5,4},{6,7},{7,6},{8,9},{9,8},{10,11... | collective-permute-start | bytes 589832 | tf_op jit(solution)/shard_map/ppermute | solution.py:246

commit v18 on v17

--- a/solution.py
+++ b/solution.py
@@ -9,12 +9,13 @@
 
 STEPS = 4
 KINDS = "UUT"
-PARTS = (5, 5, 6)
+PARTS = (4, 6, 6)
 CHAIN = ("b0", "o1", "b2", "t1")
 ORDER = ("B0", "B1", "B2", "C0", "C1", "E0", "E1", "R2", "C2")
 TIES = {"C2": "C0"}
 EARLY = "C0"
 OUT = "none"
+WEIGHT = 2
 CHUNKS = len(PARTS)
 VMEM_BYTES = 16 * 1024 * 1024
 
@@ -145,7 +146,7 @@
             outs[len(sides) * i + at_side][...] = sums[i]
 
 
-def more_scores(stores, pieces, carries, valid=None, sides=(0, 1)):
+def more_scores(stores, pieces, carries, valid=None, sides=(0, 1), weight=1):
     operands, placed = [], []
 
     def place(block):
@@ -185,7 +186,7 @@
         out_specs=[whole_spec()] * (count + len(more)),
         scratch_shapes=[pltpu.SemaphoreType.DMA((2,))] if loading else [],
         compiler_params=params(),
-        cost_estimate=cost(flops, 4 * half * columns * count),
+        cost_estimate=cost(weight * flops, weight * 4 * half * columns * count),
     )(*first, *operands)
     totals = [tuple(outs[i:i + len(sides)]) for i in range(0, count, len(sides))]
     if valid is not None:
@@ -311,9 +312,11 @@
             pieces.append((n, [(part, *blocks[part]) for part in parts]))
             todo -= {n} if 0 in parts else set()
         if one is None:
-            one, three, limit = more_scores(stores, pieces, [one, three], limited)
+            one, three, limit = more_scores(
+                stores, pieces, [one, three], limited, weight=WEIGHT
+            )
         elif one_pair is None:
-            one, three = more_scores(stores, pieces, [one, three])
+            one, three = more_scores(stores, pieces, [one, three], weight=WEIGHT)
         else:
             pieces = [(n, [(0, *blocks) for _, *blocks in targets]) for n, targets in pieces]
             [[theirs]] = more_scores(stores, pieces, [three], sides=(0,))

time: 34.6 us -> 33.6 us (0.971)
  starting transfers between devices: 15.9 us -> 14.1 us
  Pallas kernels: 8.89 us -> 9.51 us
    ppermute x13, starting transfers between devices: 15.9 us -> 14.1 us  [send(): return lax.ppermute(block, axis, route)]
    pallas_call x7, Pallas kernels: 5.69 us -> 6.33 us  [more_scores(): pl.pallas_call(functools.partial(scores_kernel, tuple(placed), fresh, loa...]
  transfers between devices with their start and end apart: 13 -> 13, of which waited for: 5 -> 5; matrix products, arithmetic and copies ran while one was open for 0% -> 0% of each run, Pallas kernels for 19% -> 21%
where the time goes in v18:
time: 33.6 us; the launch traced here: 33.4 us
  starting transfers between devices  14.1 us (42%)
  Pallas kernels  9.51 us (28%)
  waiting for transfers between devices  8.92 us (27%)
  between operations  0.79 us (2%)
    ppermute x13, starting transfers between devices, send(): return lax.ppermute(block, axis, route)  14.1 us
    ppermute x13, waiting for transfers between devices, send(): return lax.ppermute(block, axis, route)  8.92 us
    pallas_call x7, Pallas kernels, more_scores(): pl.pallas_call(functools.partial(scores_kernel, tuple(placed), fresh, loa...  6.33 us
    pallas_call x2, Pallas kernels, finish(): pl.pallas_call(functools.partial(finish_kernel, places), out_shape=pltpu....  1.6 us
    pallas_call x1, Pallas kernels, prepare(): pl.pallas_call(prepare_kernel, out_shape=shapes, in_specs=[far_spec()] *...  1.58 us
  transfers between devices with their start and end apart: 13, of which 5 were waited for; matrix products, arithmetic and copies ran while one was open for 0% of the time, Pallas kernels for 21%

profile of v18, /device:TPU:0, one launch (start us, length us, event | category | flops | bytes accessed | tf_op | source)
XLA Modules:
  0.0 33.4 jit_solution(16022326831288704134)
XLA Ops:
  0.0 1.6 %shard_map.55 = (bf16[128,512]{1,0:T(8,128)(2,1)S(1)}, bf16[128,768]{1,0:T(8,128)(2,1)S(1)}, bf16[128,768]{1,0:T(8,128)(2,1)S(1)}) custom-call(bf16[128,2048]{1,0:T(8,128)(2,1)} %queries.1, f32[1,2048]{1,0:T(1,128)} %bitcast.1, s32[1,128]{1,0:T(1,128)} %rank.1), custom_call_target="tpu_custom_call" | custom-call | flops 67108864 | bytes 1048576 | tf_op jit(solution)/shard_map/pallas_call | solution.py:81
  1.6 3.1 %collective-permute-start = (bf16[128,512]{1,0:T(8,128)(2,1)S(1)}, bf16[128,512]{1,0:T(8,128)(2,1)S(1)}, u32[]{:S(2)}, u32[]{:S(2)}) collective-permute-start(bf16[128,512]{1,0:T(8,128)(2,1)S(1)} %get-tuple-element.30.refs_1_), channel_id=1, source_target_pairs={{0,4},{2,6},{4,8},{6,10},{8,12},{10,14},{12,0},{14,2},{1,5},{3,7},... | collective-permute-start | bytes 393224 | tf_op jit(solution)/shard_map/ppermute | solution.py:247
  4.7 1.6 %collective-permute-start.1 = (bf16[128,768]{1,0:T(8,128)(2,1)S(1)}, bf16[128,768]{1,0:T(8,128)(2,1)S(1)}, u32[]{:S(2)}, u32[]{:S(2)}) collective-permute-start(bf16[128,768]{1,0:T(8,128)(2,1)S(1)} %get-tuple-element.31.refs_2_), channel_id=1, source_target_pairs={{0,4},{2,6},{4,8},{6,10},{8,12},{10,14},{12,0},{14,2},{1,5},{3,7},... | collective-permute-start | bytes 589832 | tf_op jit(solution)/shard_map/ppermute | solution.py:247
  6.2 1.6 %collective-permute-start.2 = (bf16[128,768]{1,0:T(8,128)(2,1)S(1)}, bf16[128,768]{1,0:T(8,128)(2,1)S(1)}, u32[]{:S(2)}, u32[]{:S(2)}) collective-permute-start(bf16[128,768]{1,0:T(8,128)(2,1)S(1)} %get-tuple-element.32.refs_3_), channel_id=1, source_target_pairs={{0,4},{2,6},{4,8},{6,10},{8,12},{10,14},{12,0},{14,2},{1,5},{3,7},... | collective-permute-start | bytes 589832 | tf_op jit(solution)/shard_map/ppermute | solution.py:247
  7.8 3.3 %shard_map.56 = (f32[384,128]{1,0:T(8,128)S(1)}, f32[384,128]{1,0:T(8,128)S(1)}, bf16[384,2048]{1,0:T(8,128)(2,1)S(1)}, bf16[384,2048]{1,0:T(8,128)(2,1)S(1)}) custom-call(bf16[768,2048]{1,0:T(8,128)(2,1)} %refs_0_.1, bf16[128,512]{1,0:T(8,128)(2,1)S(1)} %get-tuple-element.30.refs_1_, bf16[128,768]{1,0:T(8,128)(2,1)S(1)} %get-tuple-element.31.refs_2_, ...), custom_call_target="tpu_custom_call" | custom-call | flops 402653184 | bytes 393216 | tf_op jit(solution)/shard_map/pallas_call | solution.py:182
  11.2 1.6 %collective-permute-start.3 = (bf16[128,512]{1,0:T(8,128)(2,1)S(1)}, bf16[128,512]{1,0:T(8,128)(2,1)S(1)}, u32[]{:S(2)}, u32[]{:S(2)}) collective-permute-start(bf16[128,512]{1,0:T(8,128)(2,1)S(1)} %broadcast_select_fusion.2), channel_id=1, source_target_pairs={{0,2},{2,0},{4,6},{6,4},{8,10},{10,8},{12,14},{14,12},{1,3},{3,1},... | collective-permute-start | bytes 393224 | tf_op jit(solution)/shard_map/ppermute | solution.py:247
  12.8 2.4 %collective-permute-done.1.refs_3_ = bf16[128,768]{1,0:T(8,128)(2,1)S(1)} collective-permute-done((bf16[128,768]{1,0:T(8,128)(2,1)S(1)}, bf16[128,768]{1,0:T(8,128)(2,1)S(1)}, u32[]{:S(2)}, u32[]{:S(2)}) %collective-permute-start.1) | collective-permute-done | bytes 196640 | tf_op jit(solution)/shard_map/ppermute | solution.py:247
  15.3 1.8 %collective-permute-start.7 = (bf16[128,768]{1,0:T(8,128)(2,1)S(1)}, bf16[128,768]{1,0:T(8,128)(2,1)S(1)}, u32[]{:S(2)}, u32[]{:S(2)}) collective-permute-start(bf16[128,768]{1,0:T(8,128)(2,1)S(1)} %broadcast_select_fusion), channel_id=1, source_target_pairs={{0,2},{2,0},{4,6},{6,4},{8,10},{10,8},{12,14},{14,12},{1,3},{3,1},... | collective-permute-start | bytes 589832 | tf_op jit(solution)/shard_map/ppermute | solution.py:247
  17.1 1.6 %collective-permute-done.2.refs_4_ = bf16[128,768]{1,0:T(8,128)(2,1)S(1)} collective-permute-done((bf16[128,768]{1,0:T(8,128)(2,1)S(1)}, bf16[128,768]{1,0:T(8,128)(2,1)S(1)}, u32[]{:S(2)}, u32[]{:S(2)}) %collective-permute-start.2) | collective-permute-done | bytes 196640 | tf_op jit(solution)/shard_map/ppermute | solution.py:247
  18.6 1.5 %collective-permute-start.6 = (bf16[128,768]{1,0:T(8,128)(2,1)S(1)}, bf16[128,768]{1,0:T(8,128)(2,1)S(1)}, u32[]{:S(2)}, u32[]{:S(2)}) collective-permute-start(bf16[128,768]{1,0:T(8,128)(2,1)S(1)} %broadcast_select_fusion.1), channel_id=1, source_target_pairs={{0,2},{2,4},{4,6},{6,8},{8,10},{10,12},{12,14},{14,0},{1,3},{3,5},... | collective-permute-start | bytes 589832 | tf_op jit(solution)/shard_map/ppermute | solution.py:247
  20.2 0.3 collective-permute-start.5
  20.5 0.6 %collective-permute-done.7.refs_2_ = bf16[128,768]{1,0:T(8,128)(2,1)S(1)} collective-permute-done((bf16[128,768]{1,0:T(8,128)(2,1)S(1)}, bf16[128,768]{1,0:T(8,128)(2,1)S(1)}, u32[]{:S(2)}, u32[]{:S(2)}) %collective-permute-start.7) | collective-permute-done | bytes 196640 | tf_op jit(solution)/shard_map/ppermute | solution.py:247
  21.1 1.4 %collective-permute-start.9 = (bf16[128,768]{1,0:T(8,128)(2,1)S(1)}, bf16[128,768]{1,0:T(8,128)(2,1)S(1)}, u32[]{:S(2)}, u32[]{:S(2)}) collective-permute-start(bf16[128,768]{1,0:T(8,128)(2,1)S(1)} %collective-permute-done.7.refs_2_), channel_id=1, source_target_pairs={{0,4},{2,6},{4,8},{6,10},{8,12},{10,14},{12,0},{14,2},{1,5},{3,7},... | collective-permute-start | bytes 589832 | tf_op jit(solution)/shard_map/ppermute | solution.py:247
  23.2 1.0 %shard_map.57 = (f32[384,128]{1,0:T(8,128)S(1)}, f32[384,128]{1,0:T(8,128)S(1)}) custom-call(bf16[384,2048]{1,0:T(8,128)(2,1)S(1)} %get-tuple-element.33.refs_0_.refs_1_, bf16[384,2048]{1,0:T(8,128)(2,1)S(1)} %get-tuple-element.34.refs_1_.refs_2_, bf16[128,512]{1,0:T(8,128)(2,1)S(1)} %collective-permute-done.refs_2_, ...), custom_call_target="tpu_custom_call" | custom-call | flops 402653184 | bytes 393216 | tf_op jit(solution)/shard_map/pallas_call | solution.py:182
  24.2 0.6 %collective-permute-start.12 = (f32[384,128]{1,0:T(8,128)S(1)}, f32[384,128]{1,0:T(8,128)S(1)}, u32[]{:S(2)}, u32[]{:S(2)}) collective-permute-start(f32[384,128]{1,0:T(8,128)S(1)} %get-tuple-element.54), channel_id=1, source_target_pairs={{0,1},{1,0},{2,3},{3,2},{4,5},{5,4},{6,7},{7,6},{8,9},{9,8},{10,11... | collective-permute-start | bytes 589832 | tf_op jit(solution)/shard_map/ppermute | solution.py:247
  24.7 0.4 %shard_map.58 = (f32[384,128]{1,0:T(8,128)S(1)}, f32[384,128]{1,0:T(8,128)S(1)}, f32[384,128]{1,0:T(8,128)S(1)}, f32[384,128]{1,0:T(8,128)S(1)}, s32[8,128]{1,0:T(8,128)S(1)}) custom-call(s32[1]{0:T(128)S(6)} %copy.8.refs_0_, bf16[384,2048]{1,0:T(8,128)(2,1)S(1)} %get-tuple-element.33.refs_0_.refs_1_, ...), custom_call_target="tpu_custom_call" | custom-call | flops 402653184 | bytes 1572864 | tf_op jit(solution)/shard_map/pallas_call | solution.py:182
  25.1 0.5 %shard_map.59 = (f32[384,128]{1,0:T(8,128)S(1)}, f32[384,128]{1,0:T(8,128)S(1)}, f32[384,128]{1,0:T(8,128)S(1)}, f32[384,128]{1,0:T(8,128)S(1)}) custom-call(bf16[384,2048]{1,0:T(8,128)(2,1)S(1)} %get-tuple-element.33.refs_0_.refs_1_, bf16[384,2048]{1,0:T(8,128)(2,1)S(1)} %get-tuple-element.34.refs_1_.refs_2_, ...), custom_call_target="tpu_custom_call" | custom-call | flops 301989888 | bytes 1572864 | tf_op jit(solution)/shard_map/pallas_call | solution.py:182
  25.6 3.7 %collective-permute-done.6.refs_3_ = bf16[128,768]{1,0:T(8,128)(2,1)S(1)} collective-permute-done((bf16[128,768]{1,0:T(8,128)(2,1)S(1)}, bf16[128,768]{1,0:T(8,128)(2,1)S(1)}, u32[]{:S(2)}, u32[]{:S(2)}) %collective-permute-start.6) | collective-permute-done | bytes 196640 | tf_op jit(solution)/shard_map/ppermute | solution.py:247
  29.3 0.6 %collective-permute-done.5.refs_2_ = bf16[128,768]{1,0:T(8,128)(2,1)S(1)} collective-permute-done((bf16[128,768]{1,0:T(8,128)(2,1)S(1)}, bf16[128,768]{1,0:T(8,128)(2,1)S(1)}, u32[]{:S(2)}, u32[]{:S(2)}) %collective-permute-start.5) | collective-permute-done | bytes 196640 | tf_op jit(solution)/shard_map/ppermute | solution.py:247
  30.0 0.5 %shard_map.60 = (f32[384,128]{1,0:T(8,128)S(1)}, f32[384,128]{1,0:T(8,128)S(1)}, f32[384,128]{1,0:T(8,128)S(1)}, f32[384,128]{1,0:T(8,128)S(1)}) custom-call(bf16[384,2048]{1,0:T(8,128)(2,1)S(1)} %get-tuple-element.33.refs_0_.refs_1_, bf16[384,2048]{1,0:T(8,128)(2,1)S(1)} %get-tuple-element.34.refs_1_.refs_2_, ...), custom_call_target="tpu_custom_call" | custom-call | flops 603979776 | bytes 1572864 | tf_op jit(solution)/shard_map/pallas_call | solution.py:182
  30.6 0.3 shard_map.62
  30.9 0.5 %collective-permute-start.10 = (f32[384,128]{1,0:T(8,128)S(1)}, f32[384,128]{1,0:T(8,128)S(1)}, u32[]{:S(2)}, u32[]{:S(2)}) collective-permute-start(f32[384,128]{1,0:T(8,128)S(1)} %shard_map.62), channel_id=1, source_target_pairs={{0,1},{1,0},{2,3},{3,2},{4,5},{5,4},{6,7},{7,6},{8,9},{9,8},{10,11... | collective-permute-start | bytes 589832 | tf_op jit(solution)/shard_map/ppermute | solution.py:247
  31.5 0.8 %shard_map.63.refs_4_ = f32[384,512]{1,0:T(8,128)} custom-call(s32[8,128]{1,0:T(8,128)S(1)} %get-tuple-element.39.limit, f32[384,128]{1,0:T(8,128)S(1)} %get-tuple-element.37.refs_0_, f32[384,128]{1,0:T(8,128)S(1)} %collective-permute-done.11.refs_1_, f32[384,128]{1,0:T(8,128)S(1)} %get-tuple-element.35.refs_2_, f32[384,128]{1,0:T(8,128)S(1)} %collective-permute-done.12.refs_3_), custom_call_target="tpu_custom_call" | custom-call | flops 98304 | bytes 1179648 | tf_op jit(solution)/shard_map/pallas_call | solution.py:217
  32.6 0.8 %shard_map.64 = f32[384,512]{1,0:T(8,128)} custom-call(s32[8,128]{1,0:T(8,128)S(1)} %get-tuple-element.39.limit, f32[384,128]{1,0:T(8,128)S(1)} %get-tuple-element.49.refs_0_, f32[384,128]{1,0:T(8,128)S(1)} %collective-permute-done.8.refs_1_, f32[384,128]{1,0:T(8,128)S(1)} %shard_map.61.refs_2_, ...), custom_call_target="tpu_custom_call", output_to_operand_aliasing={{}: (5, {})} | custom-call | flops 98304 | bytes 1179648 | tf_op jit(solution)/shard_map/pallas_call | solution.py:217
  (15 shorter events, 0.5 us)
Async XLA Ops:
  1.6 9.6 %collective-permute-start = (bf16[128,512]{1,0:T(8,128)(2,1)S(1)}, bf16[128,512]{1,0:T(8,128)(2,1)S(1)}, u32[]{:S(2)}, u32[]{:S(2)}) collective-permute-start(bf16[128,512]{1,0:T(8,128)(2,1)S(1)} %get-tuple-element.30.refs_1_), channel_id=1, source_target_pairs={{0,4},{2,6},{4,8},{6,10},{8,12},{10,14},{12,0},{14,2},{1,5},{3,7},... | collective-permute-start | bytes 393224 | tf_op jit(solution)/shard_map/ppermute | solution.py:247
  4.7 10.6 %collective-permute-start.1 = (bf16[128,768]{1,0:T(8,128)(2,1)S(1)}, bf16[128,768]{1,0:T(8,128)(2,1)S(1)}, u32[]{:S(2)}, u32[]{:S(2)}) collective-permute-start(bf16[128,768]{1,0:T(8,128)(2,1)S(1)} %get-tuple-element.31.refs_2_), channel_id=1, source_target_pairs={{0,4},{2,6},{4,8},{6,10},{8,12},{10,14},{12,0},{14,2},{1,5},{3,7},... | collective-permute-start | bytes 589832 | tf_op jit(solution)/shard_map/ppermute | solution.py:247
  6.2 12.4 %collective-permute-start.2 = (bf16[128,768]{1,0:T(8,128)(2,1)S(1)}, bf16[128,768]{1,0:T(8,128)(2,1)S(1)}, u32[]{:S(2)}, u32[]{:S(2)}) collective-permute-start(bf16[128,768]{1,0:T(8,128)(2,1)S(1)} %get-tuple-element.32.refs_3_), channel_id=1, source_target_pairs={{0,4},{2,6},{4,8},{6,10},{8,12},{10,14},{12,0},{14,2},{1,5},{3,7},... | collective-permute-start | bytes 589832 | tf_op jit(solution)/shard_map/ppermute | solution.py:247
  11.2 5.9 %collective-permute-start.3 = (bf16[128,512]{1,0:T(8,128)(2,1)S(1)}, bf16[128,512]{1,0:T(8,128)(2,1)S(1)}, u32[]{:S(2)}, u32[]{:S(2)}) collective-permute-start(bf16[128,512]{1,0:T(8,128)(2,1)S(1)} %broadcast_select_fusion.2), channel_id=1, source_target_pairs={{0,2},{2,0},{4,6},{6,4},{8,10},{10,8},{12,14},{14,12},{1,3},{3,1},... | collective-permute-start | bytes 393224 | tf_op jit(solution)/shard_map/ppermute | solution.py:247
  15.3 5.9 %collective-permute-start.7 = (bf16[128,768]{1,0:T(8,128)(2,1)S(1)}, bf16[128,768]{1,0:T(8,128)(2,1)S(1)}, u32[]{:S(2)}, u32[]{:S(2)}) collective-permute-start(bf16[128,768]{1,0:T(8,128)(2,1)S(1)} %broadcast_select_fusion), channel_id=1, source_target_pairs={{0,2},{2,0},{4,6},{6,4},{8,10},{10,8},{12,14},{14,12},{1,3},{3,1},... | collective-permute-start | bytes 589832 | tf_op jit(solution)/shard_map/ppermute | solution.py:247
  17.1 7.1 %collective-permute-start.4 = (bf16[128,512]{1,0:T(8,128)(2,1)S(1)}, bf16[128,512]{1,0:T(8,128)(2,1)S(1)}, u32[]{:S(2)}, u32[]{:S(2)}) collective-permute-start(bf16[128,512]{1,0:T(8,128)(2,1)S(1)} %collective-permute-done.3.refs_3_), channel_id=1, source_target_pairs={{0,4},{2,6},{4,8},{6,10},{8,12},{10,14},{12,0},{14,2},{1,5},{3,7},... | collective-permute-start | bytes 393224 | tf_op jit(solution)/shard_map/ppermute | solution.py:247
  18.6 10.7 %collective-permute-start.6 = (bf16[128,768]{1,0:T(8,128)(2,1)S(1)}, bf16[128,768]{1,0:T(8,128)(2,1)S(1)}, u32[]{:S(2)}, u32[]{:S(2)}) collective-permute-start(bf16[128,768]{1,0:T(8,128)(2,1)S(1)} %broadcast_select_fusion.1), channel_id=1, source_target_pairs={{0,2},{2,4},{4,6},{6,8},{8,10},{10,12},{12,14},{14,0},{1,3},{3,5},... | collective-permute-start | bytes 589832 | tf_op jit(solution)/shard_map/ppermute | solution.py:247
  20.2 9.8 %collective-permute-start.5 = (bf16[128,768]{1,0:T(8,128)(2,1)S(1)}, bf16[128,768]{1,0:T(8,128)(2,1)S(1)}, u32[]{:S(2)}, u32[]{:S(2)}) collective-permute-start(bf16[128,768]{1,0:T(8,128)(2,1)S(1)} %collective-permute-done.2.refs_4_), channel_id=1, source_target_pairs={{0,2},{2,0},{4,6},{6,4},{8,10},{10,8},{12,14},{14,12},{1,3},{3,1},... | collective-permute-start | bytes 589832 | tf_op jit(solution)/shard_map/ppermute | solution.py:247
  21.1 9.5 %collective-permute-start.9 = (bf16[128,768]{1,0:T(8,128)(2,1)S(1)}, bf16[128,768]{1,0:T(8,128)(2,1)S(1)}, u32[]{:S(2)}, u32[]{:S(2)}) collective-permute-start(bf16[128,768]{1,0:T(8,128)(2,1)S(1)} %collective-permute-done.7.refs_2_), channel_id=1, source_target_pairs={{0,4},{2,6},{4,8},{6,10},{8,12},{10,14},{12,0},{14,2},{1,5},{3,7},... | collective-permute-start | bytes 589832 | tf_op jit(solution)/shard_map/ppermute | solution.py:247
  22.5 8.9 %collective-permute-start.11 = (f32[384,128]{1,0:T(8,128)S(1)}, f32[384,128]{1,0:T(8,128)S(1)}, u32[]{:S(2)}, u32[]{:S(2)}) collective-permute-start(f32[384,128]{1,0:T(8,128)S(1)} %get-tuple-element.53), channel_id=1, source_target_pairs={{0,1},{1,0},{2,3},{3,2},{4,5},{5,4},{6,7},{7,6},{8,9},{9,8},{10,11... | collective-permute-start | bytes 589832 | tf_op jit(solution)/shard_map/ppermute | solution.py:247
  24.2 7.3 %collective-permute-start.12 = (f32[384,128]{1,0:T(8,128)S(1)}, f32[384,128]{1,0:T(8,128)S(1)}, u32[]{:S(2)}, u32[]{:S(2)}) collective-permute-start(f32[384,128]{1,0:T(8,128)S(1)} %get-tuple-element.54), channel_id=1, source_target_pairs={{0,1},{1,0},{2,3},{3,2},{4,5},{5,4},{6,7},{7,6},{8,9},{9,8},{10,11... | collective-permute-start | bytes 589832 | tf_op jit(solution)/shard_map/ppermute | solution.py:247
  30.5 2.1 %collective-permute-start.8 = (f32[384,128]{1,0:T(8,128)S(1)}, f32[384,128]{1,0:T(8,128)S(1)}, u32[]{:S(2)}, u32[]{:S(2)}) collective-permute-start(f32[384,128]{1,0:T(8,128)S(1)} %get-tuple-element.50), channel_id=1, source_target_pairs={{0,1},{1,0},{2,3},{3,2},{4,5},{5,4},{6,7},{7,6},{8,9},{9,8},{10,11... | collective-permute-start | bytes 589832 | tf_op jit(solution)/shard_map/ppermute | solution.py:247
  30.9 1.7 %collective-permute-start.10 = (f32[384,128]{1,0:T(8,128)S(1)}, f32[384,128]{1,0:T(8,128)S(1)}, u32[]{:S(2)}, u32[]{:S(2)}) collective-permute-start(f32[384,128]{1,0:T(8,128)S(1)} %shard_map.62), channel_id=1, source_target_pairs={{0,1},{1,0},{2,3},{3,2},{4,5},{5,4},{6,7},{7,6},{8,9},{9,8},{10,11... | collective-permute-start | bytes 589832 | tf_op jit(solution)/shard_map/ppermute | solution.py:247

commit v19 on v18

--- a/solution.py
+++ b/solution.py
@@ -8,13 +8,12 @@
 from jax.sharding import PartitionSpec as P
 
 STEPS = 4
-KINDS = "UUT"
+KINDS = "UTU"
 PARTS = (4, 6, 6)
-CHAIN = ("b0", "o1", "b2", "t1")
-ORDER = ("B0", "B1", "B2", "C0", "C1", "E0", "E1", "R2", "C2")
-TIES = {"C2": "C0"}
+CHAIN = ("b0", "o2", "b1", "t2")
+ORDER = ("B0", "B2", "B1", "C0", "C2", "E0", "E2", "R1", "C1")
+TIES = {"C1": "C0"}
 EARLY = "C0"
-OUT = "none"
 WEIGHT = 2
 CHUNKS = len(PARTS)
 VMEM_BYTES = 16 * 1024 * 1024
@@ -299,34 +298,32 @@
     [two] = more_scores(stores, [(n, [(0, two_back[n])]) for n in range(CHUNKS)], [None])
     two_pair = exchanged(two)
     limited = after(valid_rows, two[1])
-    one = three = one_pair = None
-    todo, out = set(range(CHUNKS)), None
-    for group in CHAIN:
+    one = three = None
+    def pieces_of(group):
         pieces = []
-        if group == OUT:
-            out = finish(limit, [own_pair, two_pair], (0, 2), STEPS)
-            one = after(one[0], out), one[1]
         for item in group.split():
             n, parts = int(item[1:]), {"b": (0, 1), "o": (0,), "t": (1,)}[item[0]]
             blocks = one_back[n], three_back[n]
             pieces.append((n, [(part, *blocks[part]) for part in parts]))
-            todo -= {n} if 0 in parts else set()
+        return pieces
+
+    for group in CHAIN[:-2]:
         if one is None:
             one, three, limit = more_scores(
-                stores, pieces, [one, three], limited, weight=WEIGHT
+                stores, pieces_of(group), [one, three], limited, weight=WEIGHT
             )
-        elif one_pair is None:
-            one, three = more_scores(stores, pieces, [one, three], weight=WEIGHT)
         else:
-            pieces = [(n, [(0, *blocks) for _, *blocks in targets]) for n, targets in pieces]
-            [[theirs]] = more_scores(stores, pieces, [three], sides=(0,))
-            [[ours]] = more_scores(stores, pieces, [three], sides=(1,))
-            three = theirs, ours
-        if one_pair is None and not todo:
-            one_pair = exchanged(one)
-    if out is None:
-        out = finish(limit, [own_pair, two_pair], (0, 2), STEPS)
-    return finish(limit, [one_pair, exchanged(three)], (1, 3), STEPS, out)
+            one, three = more_scores(stores, pieces_of(group), [one, three], weight=WEIGHT)
+    out = finish(limit, [own_pair], (0,), STEPS)
+    one = after(one[0], out), one[1]
+    late, last = pieces_of(CHAIN[-2]), pieces_of(CHAIN[-1])
+    [one_theirs], [three_theirs] = more_scores(stores, late, [one, three], sides=(0,))
+    one_came = send(one_theirs, over_dim, "dim")
+    only = [(n, [(0, *blocks) for _, *blocks in targets]) for n, targets in last]
+    [[three_theirs]] = more_scores(stores, only, [(three_theirs, None)], sides=(0,))
+    three_came = send(three_theirs, over_dim, "dim")
+    [one_ours], [three_ours] = more_scores(stores, late + last, [one, three], sides=(1,))
+    return finish(limit, [(one_ours, one_came), two_pair, (three_ours, three_came)], (1, 2, 3), STEPS, out)
 
 
 def solution(mesh):

time: 33.6 us -> 37.8 us (1.12)
  Pallas kernels: 9.51 us -> 13.1 us
  waiting for transfers between devices: 8.92 us -> 5.45 us
  other arithmetic: 0.06 us -> 2.83 us
  local copies, waits for them, and re-layouts: 0 us -> 1.1 us
    ppermute x13, waiting for transfers between devices: 8.92 us -> 5.45 us  [send(): return lax.ppermute(block, axis, route)]
    select_n x3, other arithmetic: 0.06 us -> 2.83 us  [by_parity(): return jnp.where(odd, at_odd, at_even)]
    pallas_call x7, Pallas kernels: 6.33 us -> 8.37 us  [more_scores(): pl.pallas_call(functools.partial(scores_kernel, tuple(placed), fresh, loa...]
    unnamed x0 -> x4, local copies, waits for them, and re-layouts: none -> 1.1 us
    pallas_call x2, Pallas kernels: 1.6 us -> 2.51 us  [finish(): pl.pallas_call(functools.partial(finish_kernel, places), out_shape=pltpu....]
    pallas_call x1, Pallas kernels: 1.58 us -> 2.25 us  [prepare(): pl.pallas_call(prepare_kernel, out_shape=shapes, in_specs=[far_spec()] *...]
  transfers between devices with their start and end apart: 13 -> 13, of which waited for: 5 -> 3; matrix products, arithmetic and copies ran while one was open for 0% -> 8% of each run, Pallas kernels for 21% -> 27%
where the time goes in v19:
time: 37.8 us; the launch traced here: 37.6 us
  starting transfers between devices  14.2 us (38%)
  Pallas kernels  13.1 us (35%)
  waiting for transfers between devices  5.45 us (14%)
  other arithmetic  2.83 us (7%)
  local copies, waits for them, and re-layouts  1.1 us (3%)
  between operations  0.8 us (2%)
    ppermute x13, starting transfers between devices, send(): return lax.ppermute(block, axis, route)  14.2 us
    pallas_call x7, Pallas kernels, more_scores(): pl.pallas_call(functools.partial(scores_kernel, tuple(placed), fresh, loa...  8.37 us
    ppermute x13, waiting for transfers between devices, send(): return lax.ppermute(block, axis, route)  5.45 us
    select_n x3, other arithmetic, by_parity(): return jnp.where(odd, at_odd, at_even)  2.83 us
    pallas_call x2, Pallas kernels, finish(): pl.pallas_call(functools.partial(finish_kernel, places), out_shape=pltpu....  2.51 us
    pallas_call x1, Pallas kernels, prepare(): pl.pallas_call(prepare_kernel, out_shape=shapes, in_specs=[far_spec()] *...  2.25 us
    unnamed x4, local copies, waits for them, and re-layouts  1.1 us
  transfers between devices with their start and end apart: 13, of which 3 were waited for; matrix products, arithmetic and copies ran while one was open for 8% of the time, Pallas kernels for 27%

profile of v19, /device:TPU:0, one launch (start us, length us, event | category | flops | bytes accessed | tf_op | source)
XLA Modules:
  0.0 37.6 jit_solution(15763696601804368609)
XLA Ops:
  0.0 2.2 %shard_map.55 = (bf16[128,512]{1,0:T(8,128)(2,1)}, bf16[128,768]{1,0:T(8,128)(2,1)}, bf16[128,768]{1,0:T(8,128)(2,1)}) custom-call(bf16[128,2048]{1,0:T(8,128)(2,1)} %queries.1, f32[1,2048]{1,0:T(1,128)} %bitcast.1, s32[1,128]{1,0:T(1,128)} %rank.1), custom_call_target="tpu_custom_call" | custom-call | flops 67108864 | bytes 1048576 | tf_op jit(solution)/shard_map/pallas_call | solution.py:80
  2.3 3.1 %collective-permute-start = (bf16[128,512]{1,0:T(8,128)(2,1)}, bf16[128,512]{1,0:T(8,128)(2,1)}, u32[]{:S(2)}, u32[]{:S(2)}) collective-permute-start(bf16[128,512]{1,0:T(8,128)(2,1)} %get-tuple-element.31.refs_1_), channel_id=1, source_target_pairs={{0,4},{2,6},{4,8},{6,10},{8,12},{10,14},{12,0},{14,2},{1,5},{3,7},... | collective-permute-start | bytes 393224 | tf_op jit(solution)/shard_map/ppermute | solution.py:246
  5.3 1.6 %collective-permute-start.2 = (bf16[128,768]{1,0:T(8,128)(2,1)}, bf16[128,768]{1,0:T(8,128)(2,1)S(1)}, u32[]{:S(2)}, u32[]{:S(2)}) collective-permute-start(bf16[128,768]{1,0:T(8,128)(2,1)} %get-tuple-element.33.refs_3_), channel_id=1, source_target_pairs={{0,4},{2,6},{4,8},{6,10},{8,12},{10,14},{12,0},{14,2},{1,5},{3,7},... | collective-permute-start | bytes 589832 | tf_op jit(solution)/shard_map/ppermute | solution.py:246
  6.9 1.6 %collective-permute-start.1 = (bf16[128,768]{1,0:T(8,128)(2,1)}, bf16[128,768]{1,0:T(8,128)(2,1)S(1)}, u32[]{:S(2)}, u32[]{:S(2)}) collective-permute-start(bf16[128,768]{1,0:T(8,128)(2,1)} %get-tuple-element.32.refs_2_), channel_id=1, source_target_pairs={{0,4},{2,6},{4,8},{6,10},{8,12},{10,14},{12,0},{14,2},{1,5},{3,7},... | collective-permute-start | bytes 589832 | tf_op jit(solution)/shard_map/ppermute | solution.py:246
  8.5 4.4 %shard_map.56 = (f32[384,128]{1,0:T(8,128)}, f32[384,128]{1,0:T(8,128)S(1)}, bf16[384,2048]{1,0:T(8,128)(2,1)S(1)}, bf16[384,2048]{1,0:T(8,128)(2,1)S(1)}) custom-call(bf16[768,2048]{1,0:T(8,128)(2,1)} %refs_0_.1, bf16[128,512]{1,0:T(8,128)(2,1)} %get-tuple-element.31.refs_1_, bf16[128,768]{1,0:T(8,128)(2,1)} %get-tuple-element.32.refs_2_, ...), custom_call_target="tpu_custom_call" | custom-call | flops 402653184 | bytes 393216 | tf_op jit(solution)/shard_map/pallas_call | solution.py:181
  12.9 0.7 %copy-done = f32[384,128]{1,0:T(8,128)} copy-done((f32[384,128]{1,0:T(8,128)}, f32[384,128]{1,0:T(8,128)S(1)}, u32[]{:S(2)}) %copy-start) | copy-done | bytes 196632
  13.6 0.9 %broadcast_select_fusion.2 = bf16[128,512]{1,0:T(8,128)(2,1)S(1)} fusion(bf16[128,512]{1,0:T(8,128)(2,1)} %collective-permute-done.refs_2_, bf16[128,512]{1,0:T(8,128)(2,1)} %get-tuple-element.31.refs_1_, pred[]{:T(512)S(6)} %eq.3), kind=kLoop, calls=%fused_computation.2 | loop fusion | flops 65536 | bytes 393217 | tf_op jit(solution)/shard_map/jit(_where)/select_n | solution.py:253
  14.5 1.6 %collective-permute-start.3 = (bf16[128,512]{1,0:T(8,128)(2,1)S(1)}, bf16[128,512]{1,0:T(8,128)(2,1)S(1)}, u32[]{:S(2)}, u32[]{:S(2)}) collective-permute-start(bf16[128,512]{1,0:T(8,128)(2,1)S(1)} %broadcast_select_fusion.2), channel_id=1, source_target_pairs={{0,2},{2,0},{4,6},{6,4},{8,10},{10,8},{12,14},{14,12},{1,3},{3,1},... | collective-permute-start | bytes 393224 | tf_op jit(solution)/shard_map/ppermute | solution.py:246
  16.1 0.9 %broadcast_select_fusion = bf16[128,768]{1,0:T(8,128)(2,1)S(1)} fusion(bf16[128,768]{1,0:T(8,128)(2,1)S(1)} %collective-permute-done.2.refs_4_, bf16[128,768]{1,0:T(8,128)(2,1)} %get-tuple-element.33.refs_3_, pred[]{:T(512)S(6)} %eq.3), kind=kLoop, calls=%fused_computation | loop fusion | flops 98304 | bytes 589825 | tf_op jit(solution)/shard_map/jit(_where)/select_n | solution.py:253
  17.1 0.9 %collective-permute-start.7 = (bf16[128,768]{1,0:T(8,128)(2,1)S(1)}, bf16[128,768]{1,0:T(8,128)(2,1)S(1)}, u32[]{:S(2)}, u32[]{:S(2)}) collective-permute-start(bf16[128,768]{1,0:T(8,128)(2,1)S(1)} %broadcast_select_fusion), channel_id=1, source_target_pairs={{0,2},{2,0},{4,6},{6,4},{8,10},{10,8},{12,14},{14,12},{1,3},{3,1},... | collective-permute-start | bytes 589832 | tf_op jit(solution)/shard_map/ppermute | solution.py:246
  17.9 3.0 %collective-permute-done.3.refs_3_ = bf16[128,512]{1,0:T(8,128)(2,1)S(1)} collective-permute-done((bf16[128,512]{1,0:T(8,128)(2,1)S(1)}, bf16[128,512]{1,0:T(8,128)(2,1)S(1)}, u32[]{:S(2)}, u32[]{:S(2)}) %collective-permute-start.3) | collective-permute-done | bytes 131104 | tf_op jit(solution)/shard_map/ppermute | solution.py:246
  21.0 1.0 %broadcast_select_fusion.1 = bf16[128,768]{1,0:T(8,128)(2,1)S(1)} fusion(bf16[128,768]{1,0:T(8,128)(2,1)S(1)} %collective-permute-done.1.refs_3_, bf16[128,768]{1,0:T(8,128)(2,1)} %get-tuple-element.32.refs_2_, pred[]{:T(512)S(6)} %eq.3), kind=kLoop, calls=%fused_computation.1 | loop fusion | flops 98304 | bytes 589825 | tf_op jit(solution)/shard_map/jit(_where)/select_n | solution.py:253
  21.9 0.8 %collective-permute-start.6 = (bf16[128,768]{1,0:T(8,128)(2,1)S(1)}, bf16[128,768]{1,0:T(8,128)(2,1)S(1)}, u32[]{:S(2)}, u32[]{:S(2)}) collective-permute-start(bf16[128,768]{1,0:T(8,128)(2,1)S(1)} %broadcast_select_fusion.1), channel_id=1, source_target_pairs={{0,2},{2,4},{4,6},{6,8},{8,10},{10,12},{12,14},{14,0},{1,3},{3,5},... | collective-permute-start | bytes 589832 | tf_op jit(solution)/shard_map/ppermute | solution.py:246
  22.7 2.5 %collective-permute-start.5 = (bf16[128,768]{1,0:T(8,128)(2,1)S(1)}, bf16[128,768]{1,0:T(8,128)(2,1)S(1)}, u32[]{:S(2)}, u32[]{:S(2)}) collective-permute-start(bf16[128,768]{1,0:T(8,128)(2,1)S(1)} %collective-permute-done.1.refs_3_), channel_id=1, source_target_pairs={{0,2},{2,0},{4,6},{6,4},{8,10},{10,8},{12,14},{14,12},{1,3},{3,1},... | collective-permute-start | bytes 589832 | tf_op jit(solution)/shard_map/ppermute | solution.py:246
  25.2 1.6 %collective-permute-start.8 = (bf16[128,768]{1,0:T(8,128)(2,1)S(1)}, bf16[128,768]{1,0:T(8,128)(2,1)S(1)}, u32[]{:S(2)}, u32[]{:S(2)}) collective-permute-start(bf16[128,768]{1,0:T(8,128)(2,1)S(1)} %collective-permute-done.7.refs_2_), channel_id=1, source_target_pairs={{0,4},{2,6},{4,8},{6,10},{8,12},{10,14},{12,0},{14,2},{1,5},{3,7},... | collective-permute-start | bytes 589832 | tf_op jit(solution)/shard_map/ppermute | solution.py:246
  27.4 1.9 %shard_map.57 = (f32[384,128]{1,0:T(8,128)S(1)}, f32[384,128]{1,0:T(8,128)S(1)}) custom-call(bf16[384,2048]{1,0:T(8,128)(2,1)S(1)} %get-tuple-element.34.refs_0_.refs_1_, bf16[384,2048]{1,0:T(8,128)(2,1)S(1)} %get-tuple-element.35.refs_1_.refs_2_, bf16[128,512]{1,0:T(8,128)(2,1)} %collective-permute-done.refs_2_, ...), custom_call_target="tpu_custom_call" | custom-call | flops 402653184 | bytes 393216 | tf_op jit(solution)/shard_map/pallas_call | solution.py:181
  29.8 0.4 %copy-done.1 = f32[384,128]{1,0:T(8,128)S(1)} copy-done((f32[384,128]{1,0:T(8,128)S(1)}, f32[384,128]{1,0:T(8,128)}, u32[]{:S(2)}) %copy-start.1) | copy-done | bytes 196632
  30.2 1.6 %shard_map.61.refs_6_ = f32[384,512]{1,0:T(8,128)} custom-call(s32[8,128]{1,0:T(8,128)S(1)} %get-tuple-element.40.limit, f32[384,128]{1,0:T(8,128)S(1)} %copy-done.1, f32[384,128]{1,0:T(8,128)} %collective-permute-done.9.refs_1_), custom_call_target="tpu_custom_call" | custom-call | flops 49152 | bytes 589824 | tf_op jit(solution)/shard_map/pallas_call | solution.py:216
  31.9 0.5 %shard_map.59 = (f32[384,128]{1,0:T(8,128)S(1)}, f32[384,128]{1,0:T(8,128)S(1)}, f32[384,128]{1,0:T(8,128)S(1)}, f32[384,128]{1,0:T(8,128)S(1)}) custom-call(bf16[384,2048]{1,0:T(8,128)(2,1)S(1)} %get-tuple-element.34.refs_0_.refs_1_, bf16[384,2048]{1,0:T(8,128)(2,1)S(1)} %get-tuple-element.35.refs_1_.refs_2_, ...), custom_call_target="tpu_custom_call" | custom-call | flops 301989888 | bytes 1572864 | tf_op jit(solution)/shard_map/pallas_call | solution.py:181
  32.4 1.9 %collective-permute-done.6.refs_3_ = bf16[128,768]{1,0:T(8,128)(2,1)S(1)} collective-permute-done((bf16[128,768]{1,0:T(8,128)(2,1)S(1)}, bf16[128,768]{1,0:T(8,128)(2,1)S(1)}, u32[]{:S(2)}, u32[]{:S(2)}) %collective-permute-start.6) | collective-permute-done | bytes 196640 | tf_op jit(solution)/shard_map/ppermute | solution.py:246
  35.1 0.6 %collective-permute-start.12 = (f32[384,128]{1,0:T(8,128)S(1)}, f32[384,128]{1,0:T(8,128)S(1)}, u32[]{:S(2)}, u32[]{:S(2)}) collective-permute-start(f32[384,128]{1,0:T(8,128)S(1)} %shard_map.63), channel_id=1, source_target_pairs={{0,1},{1,0},{2,3},{3,2},{4,5},{5,4},{6,7},{7,6},{8,9},{9,8},{10,11... | collective-permute-start | bytes 589832 | tf_op jit(solution)/shard_map/ppermute | solution.py:246
  35.6 0.5 %shard_map.60 = (f32[384,128]{1,0:T(8,128)S(1)}, f32[384,128]{1,0:T(8,128)S(1)}) custom-call(bf16[384,2048]{1,0:T(8,128)(2,1)S(1)} %get-tuple-element.34.refs_0_.refs_1_, bf16[384,2048]{1,0:T(8,128)(2,1)S(1)} %get-tuple-element.35.refs_1_.refs_2_, bf16[128,768]{1,0:T(8,128)(2,1)S(1)} %collective-permute-done.5.refs_2_, ...), custom_call_target="tpu_custom_call" | custom-call | flops 452984832 | bytes 393216 | tf_op jit(solution)/shard_map/pallas_call | solution.py:181
  36.2 0.5 %collective-permute-done.12.refs_5_ = f32[384,128]{1,0:T(8,128)S(1)} collective-permute-done((f32[384,128]{1,0:T(8,128)S(1)}, f32[384,128]{1,0:T(8,128)S(1)}, u32[]{:S(2)}, u32[]{:S(2)}) %collective-permute-start.12) | collective-permute-done | bytes 196640 | tf_op jit(solution)/shard_map/ppermute | solution.py:246
  36.7 0.9 %shard_map.64 = f32[384,512]{1,0:T(8,128)} custom-call(s32[8,128]{1,0:T(8,128)S(1)} %get-tuple-element.40.limit, f32[384,128]{1,0:T(8,128)S(1)} %get-tuple-element.48.refs_0_, f32[384,128]{1,0:T(8,128)S(1)} %collective-permute-done.10.refs_1_, f32[384,128]{1,0:T(8,128)S(1)} %get-tuple-element.36.refs_2_, ...), custom_call_target="tpu_custom_call", output_to_operand_aliasing={{}: (7, {})} | custom-call | flops 147456 | bytes 1769472 | tf_op jit(solution)/shard_map/pallas_call | solution.py:216
  (19 shorter events, 1.4 us)
Async XLA Ops:
  2.3 11.4 %collective-permute-start = (bf16[128,512]{1,0:T(8,128)(2,1)}, bf16[128,512]{1,0:T(8,128)(2,1)}, u32[]{:S(2)}, u32[]{:S(2)}) collective-permute-start(bf16[128,512]{1,0:T(8,128)(2,1)} %get-tuple-element.31.refs_1_), channel_id=1, source_target_pairs={{0,4},{2,6},{4,8},{6,10},{8,12},{10,14},{12,0},{14,2},{1,5},{3,7},... | collective-permute-start | bytes 393224 | tf_op jit(solution)/shard_map/ppermute | solution.py:246
  5.3 10.8 %collective-permute-start.2 = (bf16[128,768]{1,0:T(8,128)(2,1)}, bf16[128,768]{1,0:T(8,128)(2,1)S(1)}, u32[]{:S(2)}, u32[]{:S(2)}) collective-permute-start(bf16[128,768]{1,0:T(8,128)(2,1)} %get-tuple-element.33.refs_3_), channel_id=1, source_target_pairs={{0,4},{2,6},{4,8},{6,10},{8,12},{10,14},{12,0},{14,2},{1,5},{3,7},... | collective-permute-start | bytes 589832 | tf_op jit(solution)/shard_map/ppermute | solution.py:246
  6.9 14.1 %collective-permute-start.1 = (bf16[128,768]{1,0:T(8,128)(2,1)}, bf16[128,768]{1,0:T(8,128)(2,1)S(1)}, u32[]{:S(2)}, u32[]{:S(2)}) collective-permute-start(bf16[128,768]{1,0:T(8,128)(2,1)} %get-tuple-element.32.refs_2_), channel_id=1, source_target_pairs={{0,4},{2,6},{4,8},{6,10},{8,12},{10,14},{12,0},{14,2},{1,5},{3,7},... | collective-permute-start | bytes 589832 | tf_op jit(solution)/shard_map/ppermute | solution.py:246
  12.9 0.7 %copy-start = (f32[384,128]{1,0:T(8,128)}, f32[384,128]{1,0:T(8,128)S(1)}, u32[]{:S(2)}) copy-start(f32[384,128]{1,0:T(8,128)S(1)} %get-tuple-element.38.refs_0_) | copy-start | bytes 589828
  13.6 16.2 %collective-permute-start.9 = (f32[384,128]{1,0:T(8,128)}, f32[384,128]{1,0:T(8,128)}, u32[]{:S(2)}, u32[]{:S(2)}) collective-permute-start(f32[384,128]{1,0:T(8,128)} %get-tuple-element.50), channel_id=1, source_target_pairs={{0,1},{1,0},{2,3},{3,2},{4,5},{5,4},{6,7},{7,6},{8,9},{9,8},{10,11... | collective-permute-start | bytes 589832 | tf_op jit(solution)/shard_map/ppermute | solution.py:246
  14.5 6.4 %collective-permute-start.3 = (bf16[128,512]{1,0:T(8,128)(2,1)S(1)}, bf16[128,512]{1,0:T(8,128)(2,1)S(1)}, u32[]{:S(2)}, u32[]{:S(2)}) collective-permute-start(bf16[128,512]{1,0:T(8,128)(2,1)S(1)} %broadcast_select_fusion.2), channel_id=1, source_target_pairs={{0,2},{2,0},{4,6},{6,4},{8,10},{10,8},{12,14},{14,12},{1,3},{3,1},... | collective-permute-start | bytes 393224 | tf_op jit(solution)/shard_map/ppermute | solution.py:246
  17.1 8.1 %collective-permute-start.7 = (bf16[128,768]{1,0:T(8,128)(2,1)S(1)}, bf16[128,768]{1,0:T(8,128)(2,1)S(1)}, u32[]{:S(2)}, u32[]{:S(2)}) collective-permute-start(bf16[128,768]{1,0:T(8,128)(2,1)S(1)} %broadcast_select_fusion), channel_id=1, source_target_pairs={{0,2},{2,0},{4,6},{6,4},{8,10},{10,8},{12,14},{14,12},{1,3},{3,1},... | collective-permute-start | bytes 589832 | tf_op jit(solution)/shard_map/ppermute | solution.py:246
  20.9 8.4 %collective-permute-start.4 = (bf16[128,512]{1,0:T(8,128)(2,1)S(1)}, bf16[128,512]{1,0:T(8,128)(2,1)S(1)}, u32[]{:S(2)}, u32[]{:S(2)}) collective-permute-start(bf16[128,512]{1,0:T(8,128)(2,1)S(1)} %collective-permute-done.3.refs_3_), channel_id=1, source_target_pairs={{0,4},{2,6},{4,8},{6,10},{8,12},{10,14},{12,0},{14,2},{1,5},{3,7},... | collective-permute-start | bytes 393224 | tf_op jit(solution)/shard_map/ppermute | solution.py:246
  21.9 12.3 %collective-permute-start.6 = (bf16[128,768]{1,0:T(8,128)(2,1)S(1)}, bf16[128,768]{1,0:T(8,128)(2,1)S(1)}, u32[]{:S(2)}, u32[]{:S(2)}) collective-permute-start(bf16[128,768]{1,0:T(8,128)(2,1)S(1)} %broadcast_select_fusion.1), channel_id=1, source_target_pairs={{0,2},{2,4},{4,6},{6,8},{8,10},{10,12},{12,14},{14,0},{1,3},{3,5},... | collective-permute-start | bytes 589832 | tf_op jit(solution)/shard_map/ppermute | solution.py:246
  22.7 11.6 %collective-permute-start.5 = (bf16[128,768]{1,0:T(8,128)(2,1)S(1)}, bf16[128,768]{1,0:T(8,128)(2,1)S(1)}, u32[]{:S(2)}, u32[]{:S(2)}) collective-permute-start(bf16[128,768]{1,0:T(8,128)(2,1)S(1)} %collective-permute-done.1.refs_3_), channel_id=1, source_target_pairs={{0,2},{2,0},{4,6},{6,4},{8,10},{10,8},{12,14},{14,12},{1,3},{3,1},... | collective-permute-start | bytes 589832 | tf_op jit(solution)/shard_map/ppermute | solution.py:246
  25.2 9.6 %collective-permute-start.8 = (bf16[128,768]{1,0:T(8,128)(2,1)S(1)}, bf16[128,768]{1,0:T(8,128)(2,1)S(1)}, u32[]{:S(2)}, u32[]{:S(2)}) collective-permute-start(bf16[128,768]{1,0:T(8,128)(2,1)S(1)} %collective-permute-done.7.refs_2_), channel_id=1, source_target_pairs={{0,4},{2,6},{4,8},{6,10},{8,12},{10,14},{12,0},{14,2},{1,5},{3,7},... | collective-permute-start | bytes 589832 | tf_op jit(solution)/shard_map/ppermute | solution.py:246
  29.3 0.9 %copy-start.1 = (f32[384,128]{1,0:T(8,128)S(1)}, f32[384,128]{1,0:T(8,128)}, u32[]{:S(2)}) copy-start(f32[384,128]{1,0:T(8,128)} %copy-done) | copy-start | bytes 589828
  29.3 6.8 %collective-permute-start.11 = (f32[384,128]{1,0:T(8,128)S(1)}, f32[384,128]{1,0:T(8,128)S(1)}, u32[]{:S(2)}, u32[]{:S(2)}) collective-permute-start(f32[384,128]{1,0:T(8,128)S(1)} %get-tuple-element.54), channel_id=1, source_target_pairs={{0,1},{1,0},{2,3},{3,2},{4,5},{5,4},{6,7},{7,6},{8,9},{9,8},{10,11... | collective-permute-start | bytes 589832 | tf_op jit(solution)/shard_map/ppermute | solution.py:246
  34.7 1.5 %collective-permute-start.10 = (f32[384,128]{1,0:T(8,128)S(1)}, f32[384,128]{1,0:T(8,128)S(1)}, u32[]{:S(2)}, u32[]{:S(2)}) collective-permute-start(f32[384,128]{1,0:T(8,128)S(1)} %get-tuple-element.53), channel_id=1, source_target_pairs={{0,1},{1,0},{2,3},{3,2},{4,5},{5,4},{6,7},{7,6},{8,9},{9,8},{10,11... | collective-permute-start | bytes 589832 | tf_op jit(solution)/shard_map/ppermute | solution.py:246
  35.1 1.6 %collective-permute-start.12 = (f32[384,128]{1,0:T(8,128)S(1)}, f32[384,128]{1,0:T(8,128)S(1)}, u32[]{:S(2)}, u32[]{:S(2)}) collective-permute-start(f32[384,128]{1,0:T(8,128)S(1)} %shard_map.63), channel_id=1, source_target_pairs={{0,1},{1,0},{2,3},{3,2},{4,5},{5,4},{6,7},{7,6},{8,9},{9,8},{10,11... | collective-permute-start | bytes 589832 | tf_op jit(solution)/shard_map/ppermute | solution.py:246

commit v20 on v19

--- a/solution.py
+++ b/solution.py
@@ -8,11 +8,11 @@
 from jax.sharding import PartitionSpec as P
 
 STEPS = 4
-KINDS = "UTU"
+KINDS = "UUT"
 PARTS = (4, 6, 6)
-CHAIN = ("b0", "o2", "b1", "t2")
-ORDER = ("B0", "B2", "B1", "C0", "C2", "E0", "E2", "R1", "C1")
-TIES = {"C1": "C0"}
+CHAIN = ("b0", "o1", "b2", "t1")
+ORDER = ("B0", "B1", "B2", "C0", "C1", "E0", "E1", "R2", "C2")
+TIES = {"C2": "C0"}
 EARLY = "C0"
 WEIGHT = 2
 CHUNKS = len(PARTS)
@@ -314,16 +314,16 @@
             )
         else:
             one, three = more_scores(stores, pieces_of(group), [one, three], weight=WEIGHT)
-    out = finish(limit, [own_pair], (0,), STEPS)
-    one = after(one[0], out), one[1]
     late, last = pieces_of(CHAIN[-2]), pieces_of(CHAIN[-1])
     [one_theirs], [three_theirs] = more_scores(stores, late, [one, three], sides=(0,))
     one_came = send(one_theirs, over_dim, "dim")
     only = [(n, [(0, *blocks) for _, *blocks in targets]) for n, targets in last]
     [[three_theirs]] = more_scores(stores, only, [(three_theirs, None)], sides=(0,))
     three_came = send(three_theirs, over_dim, "dim")
-    [one_ours], [three_ours] = more_scores(stores, late + last, [one, three], sides=(1,))
-    return finish(limit, [(one_ours, one_came), two_pair, (three_ours, three_came)], (1, 2, 3), STEPS, out)
+    [one_ours], [three_ours] = more_scores(stores, late, [one, three], sides=(1,))
+    [[three_ours]] = more_scores(stores, only, [(None, three_ours)], sides=(1,))
+    pairs = [own_pair, (one_ours, one_came), two_pair, (three_ours, three_came)]
+    return finish(limit, pairs, (0, 1, 2, 3), STEPS)
 
 
 def solution(mesh):

time: 37.8 us -> 33.5 us (0.89)
  Pallas kernels: 13.1 us -> 9.07 us
  waiting for transfers between devices: 5.45 us -> 9.27 us
  other arithmetic: 2.83 us -> 0.06 us
  local copies, waits for them, and re-layouts: 1.1 us -> 0 us
    ppermute x13, waiting for transfers between devices: 5.45 us -> 9.27 us  [send(): return lax.ppermute(block, axis, route)]
    select_n x3, other arithmetic: 2.83 us -> 0.06 us  [by_parity(): return jnp.where(odd, at_odd, at_even)]
    pallas_call x7 -> x8, Pallas kernels: 8.37 us -> 6.55 us  [more_scores(): pl.pallas_call(functools.partial(scores_kernel, tuple(placed), fresh, loa...]
    pallas_call x2 -> x1, Pallas kernels: 2.51 us -> 0.95 us  [finish(): pl.pallas_call(functools.partial(finish_kernel, places), out_shape=pltpu....]
    unnamed x4 -> x0, local copies, waits for them, and re-layouts: 1.1 us -> none
    pallas_call x1, Pallas kernels: 2.25 us -> 1.58 us  [prepare(): pl.pallas_call(prepare_kernel, out_shape=shapes, in_specs=[far_spec()] *...]
  transfers between devices with their start and end apart: 13 -> 13, of which waited for: 3 -> 6; matrix products, arithmetic and copies ran while one was open for 8% -> 0% of each run, Pallas kernels for 27% -> 20%
where the time goes in v20:
time: 33.5 us; the launch traced here: 33.3 us
  starting transfers between devices  14.1 us (42%)
  waiting for transfers between devices  9.27 us (28%)
  Pallas kernels  9.07 us (27%)
  between operations  0.8 us (2%)
    ppermute x13, starting transfers between devices, send(): return lax.ppermute(block, axis, route)  14.1 us
    ppermute x13, waiting for transfers between devices, send(): return lax.ppermute(block, axis, route)  9.27 us
    pallas_call x8, Pallas kernels, more_scores(): pl.pallas_call(functools.partial(scores_kernel, tuple(placed), fresh, loa...  6.55 us
    pallas_call x1, Pallas kernels, prepare(): pl.pallas_call(prepare_kernel, out_shape=shapes, in_specs=[far_spec()] *...  1.58 us
    pallas_call x1, Pallas kernels, finish(): pl.pallas_call(functools.partial(finish_kernel, places), out_shape=pltpu....  0.95 us
  transfers between devices with their start and end apart: 13, of which 6 were waited for; matrix products, arithmetic and copies ran while one was open for 0% of the time, Pallas kernels for 20%

profile of v20, /device:TPU:0, one launch (start us, length us, event | category | flops | bytes accessed | tf_op | source)
XLA Modules:
  0.0 33.3 jit_solution(4278623807653992038)
XLA Ops:
  0.0 1.6 %shard_map.55 = (bf16[128,512]{1,0:T(8,128)(2,1)S(1)}, bf16[128,768]{1,0:T(8,128)(2,1)S(1)}, bf16[128,768]{1,0:T(8,128)(2,1)S(1)}) custom-call(bf16[128,2048]{1,0:T(8,128)(2,1)} %queries.1, f32[1,2048]{1,0:T(1,128)} %bitcast.1, s32[1,128]{1,0:T(1,128)} %rank.1), custom_call_target="tpu_custom_call" | custom-call | flops 67108864 | bytes 1048576 | tf_op jit(solution)/shard_map/pallas_call | solution.py:80
  1.6 3.1 %collective-permute-start = (bf16[128,512]{1,0:T(8,128)(2,1)S(1)}, bf16[128,512]{1,0:T(8,128)(2,1)S(1)}, u32[]{:S(2)}, u32[]{:S(2)}) collective-permute-start(bf16[128,512]{1,0:T(8,128)(2,1)S(1)} %get-tuple-element.30.refs_1_), channel_id=1, source_target_pairs={{0,4},{2,6},{4,8},{6,10},{8,12},{10,14},{12,0},{14,2},{1,5},{3,7},... | collective-permute-start | bytes 393224 | tf_op jit(solution)/shard_map/ppermute | solution.py:246
  4.7 1.6 %collective-permute-start.1 = (bf16[128,768]{1,0:T(8,128)(2,1)S(1)}, bf16[128,768]{1,0:T(8,128)(2,1)S(1)}, u32[]{:S(2)}, u32[]{:S(2)}) collective-permute-start(bf16[128,768]{1,0:T(8,128)(2,1)S(1)} %get-tuple-element.31.refs_2_), channel_id=1, source_target_pairs={{0,4},{2,6},{4,8},{6,10},{8,12},{10,14},{12,0},{14,2},{1,5},{3,7},... | collective-permute-start | bytes 589832 | tf_op jit(solution)/shard_map/ppermute | solution.py:246
  6.2 1.6 %collective-permute-start.2 = (bf16[128,768]{1,0:T(8,128)(2,1)S(1)}, bf16[128,768]{1,0:T(8,128)(2,1)S(1)}, u32[]{:S(2)}, u32[]{:S(2)}) collective-permute-start(bf16[128,768]{1,0:T(8,128)(2,1)S(1)} %get-tuple-element.32.refs_3_), channel_id=1, source_target_pairs={{0,4},{2,6},{4,8},{6,10},{8,12},{10,14},{12,0},{14,2},{1,5},{3,7},... | collective-permute-start | bytes 589832 | tf_op jit(solution)/shard_map/ppermute | solution.py:246
  7.8 3.3 %shard_map.56 = (f32[384,128]{1,0:T(8,128)S(1)}, f32[384,128]{1,0:T(8,128)S(1)}, bf16[384,2048]{1,0:T(8,128)(2,1)S(1)}, bf16[384,2048]{1,0:T(8,128)(2,1)S(1)}) custom-call(bf16[768,2048]{1,0:T(8,128)(2,1)} %refs_0_.1, bf16[128,512]{1,0:T(8,128)(2,1)S(1)} %get-tuple-element.30.refs_1_, bf16[128,768]{1,0:T(8,128)(2,1)S(1)} %get-tuple-element.31.refs_2_, ...), custom_call_target="tpu_custom_call" | custom-call | flops 402653184 | bytes 393216 | tf_op jit(solution)/shard_map/pallas_call | solution.py:181
  11.2 1.6 %collective-permute-start.3 = (bf16[128,512]{1,0:T(8,128)(2,1)S(1)}, bf16[128,512]{1,0:T(8,128)(2,1)S(1)}, u32[]{:S(2)}, u32[]{:S(2)}) collective-permute-start(bf16[128,512]{1,0:T(8,128)(2,1)S(1)} %broadcast_select_fusion.2), channel_id=1, source_target_pairs={{0,2},{2,0},{4,6},{6,4},{8,10},{10,8},{12,14},{14,12},{1,3},{3,1},... | collective-permute-start | bytes 393224 | tf_op jit(solution)/shard_map/ppermute | solution.py:246
  12.8 2.4 %collective-permute-done.1.refs_3_ = bf16[128,768]{1,0:T(8,128)(2,1)S(1)} collective-permute-done((bf16[128,768]{1,0:T(8,128)(2,1)S(1)}, bf16[128,768]{1,0:T(8,128)(2,1)S(1)}, u32[]{:S(2)}, u32[]{:S(2)}) %collective-permute-start.1) | collective-permute-done | bytes 196640 | tf_op jit(solution)/shard_map/ppermute | solution.py:246
  15.3 1.8 %collective-permute-start.8 = (bf16[128,768]{1,0:T(8,128)(2,1)S(1)}, bf16[128,768]{1,0:T(8,128)(2,1)S(1)}, u32[]{:S(2)}, u32[]{:S(2)}) collective-permute-start(bf16[128,768]{1,0:T(8,128)(2,1)S(1)} %broadcast_select_fusion), channel_id=1, source_target_pairs={{0,2},{2,0},{4,6},{6,4},{8,10},{10,8},{12,14},{14,12},{1,3},{3,1},... | collective-permute-start | bytes 589832 | tf_op jit(solution)/shard_map/ppermute | solution.py:246
  17.1 1.6 %collective-permute-done.2.refs_4_ = bf16[128,768]{1,0:T(8,128)(2,1)S(1)} collective-permute-done((bf16[128,768]{1,0:T(8,128)(2,1)S(1)}, bf16[128,768]{1,0:T(8,128)(2,1)S(1)}, u32[]{:S(2)}, u32[]{:S(2)}) %collective-permute-start.2) | collective-permute-done | bytes 196640 | tf_op jit(solution)/shard_map/ppermute | solution.py:246
  18.6 1.5 %collective-permute-start.7 = (bf16[128,768]{1,0:T(8,128)(2,1)S(1)}, bf16[128,768]{1,0:T(8,128)(2,1)S(1)}, u32[]{:S(2)}, u32[]{:S(2)}) collective-permute-start(bf16[128,768]{1,0:T(8,128)(2,1)S(1)} %broadcast_select_fusion.1), channel_id=1, source_target_pairs={{0,2},{2,4},{4,6},{6,8},{8,10},{10,12},{12,14},{14,0},{1,3},{3,5},... | collective-permute-start | bytes 589832 | tf_op jit(solution)/shard_map/ppermute | solution.py:246
  20.2 0.3 collective-permute-start.6
  20.5 0.6 %collective-permute-done.8.refs_2_ = bf16[128,768]{1,0:T(8,128)(2,1)S(1)} collective-permute-done((bf16[128,768]{1,0:T(8,128)(2,1)S(1)}, bf16[128,768]{1,0:T(8,128)(2,1)S(1)}, u32[]{:S(2)}, u32[]{:S(2)}) %collective-permute-start.8) | collective-permute-done | bytes 196640 | tf_op jit(solution)/shard_map/ppermute | solution.py:246
  21.1 1.4 %collective-permute-start.11 = (bf16[128,768]{1,0:T(8,128)(2,1)S(1)}, bf16[128,768]{1,0:T(8,128)(2,1)S(1)}, u32[]{:S(2)}, u32[]{:S(2)}) collective-permute-start(bf16[128,768]{1,0:T(8,128)(2,1)S(1)} %collective-permute-done.8.refs_2_), channel_id=1, source_target_pairs={{0,4},{2,6},{4,8},{6,10},{8,12},{10,14},{12,0},{14,2},{1,5},{3,7},... | collective-permute-start | bytes 589832 | tf_op jit(solution)/shard_map/ppermute | solution.py:246
  23.2 1.0 %shard_map.57 = (f32[384,128]{1,0:T(8,128)S(1)}, f32[384,128]{1,0:T(8,128)S(1)}) custom-call(bf16[384,2048]{1,0:T(8,128)(2,1)S(1)} %get-tuple-element.33.refs_0_.refs_1_, bf16[384,2048]{1,0:T(8,128)(2,1)S(1)} %get-tuple-element.34.refs_1_.refs_2_, bf16[128,512]{1,0:T(8,128)(2,1)S(1)} %collective-permute-done.refs_2_, ...), custom_call_target="tpu_custom_call" | custom-call | flops 402653184 | bytes 393216 | tf_op jit(solution)/shard_map/pallas_call | solution.py:181
  24.2 0.6 %collective-permute-start.10 = (f32[384,128]{1,0:T(8,128)S(1)}, f32[384,128]{1,0:T(8,128)S(1)}, u32[]{:S(2)}, u32[]{:S(2)}) collective-permute-start(f32[384,128]{1,0:T(8,128)S(1)} %get-tuple-element.52), channel_id=1, source_target_pairs={{0,1},{1,0},{2,3},{3,2},{4,5},{5,4},{6,7},{7,6},{8,9},{9,8},{10,11... | collective-permute-start | bytes 589832 | tf_op jit(solution)/shard_map/ppermute | solution.py:246
  24.7 0.4 %shard_map.58 = (f32[384,128]{1,0:T(8,128)S(1)}, f32[384,128]{1,0:T(8,128)S(1)}, f32[384,128]{1,0:T(8,128)S(1)}, f32[384,128]{1,0:T(8,128)S(1)}, s32[8,128]{1,0:T(8,128)S(1)}) custom-call(s32[1]{0:T(128)S(6)} %copy.6.refs_0_, bf16[384,2048]{1,0:T(8,128)(2,1)S(1)} %get-tuple-element.33.refs_0_.refs_1_, ...), custom_call_target="tpu_custom_call" | custom-call | flops 402653184 | bytes 1572864 | tf_op jit(solution)/shard_map/pallas_call | solution.py:181
  25.1 0.5 %shard_map.59 = (f32[384,128]{1,0:T(8,128)S(1)}, f32[384,128]{1,0:T(8,128)S(1)}, f32[384,128]{1,0:T(8,128)S(1)}, f32[384,128]{1,0:T(8,128)S(1)}) custom-call(bf16[384,2048]{1,0:T(8,128)(2,1)S(1)} %get-tuple-element.33.refs_0_.refs_1_, bf16[384,2048]{1,0:T(8,128)(2,1)S(1)} %get-tuple-element.34.refs_1_.refs_2_, ...), custom_call_target="tpu_custom_call" | custom-call | flops 301989888 | bytes 1572864 | tf_op jit(solution)/shard_map/pallas_call | solution.py:181
  25.6 3.7 %collective-permute-done.7.refs_3_ = bf16[128,768]{1,0:T(8,128)(2,1)S(1)} collective-permute-done((bf16[128,768]{1,0:T(8,128)(2,1)S(1)}, bf16[128,768]{1,0:T(8,128)(2,1)S(1)}, u32[]{:S(2)}, u32[]{:S(2)}) %collective-permute-start.7) | collective-permute-done | bytes 196640 | tf_op jit(solution)/shard_map/ppermute | solution.py:246
  29.3 0.6 %collective-permute-done.6.refs_2_ = bf16[128,768]{1,0:T(8,128)(2,1)S(1)} collective-permute-done((bf16[128,768]{1,0:T(8,128)(2,1)S(1)}, bf16[128,768]{1,0:T(8,128)(2,1)S(1)}, u32[]{:S(2)}, u32[]{:S(2)}) %collective-permute-start.6) | collective-permute-done | bytes 196640 | tf_op jit(solution)/shard_map/ppermute | solution.py:246
  30.0 0.4 %shard_map.61 = (f32[384,128]{1,0:T(8,128)S(1)}, f32[384,128]{1,0:T(8,128)S(1)}) custom-call(bf16[384,2048]{1,0:T(8,128)(2,1)S(1)} %get-tuple-element.33.refs_0_.refs_1_, bf16[384,2048]{1,0:T(8,128)(2,1)S(1)} %get-tuple-element.34.refs_1_.refs_2_, bf16[128,768]{1,0:T(8,128)(2,1)S(1)} %collective-permute-done.6.refs_2_, ...), custom_call_target="tpu_custom_call" | custom-call | flops 301989888 | bytes 393216 | tf_op jit(solution)/shard_map/pallas_call | solution.py:181
  30.8 0.5 %collective-permute-start.12 = (f32[384,128]{1,0:T(8,128)S(1)}, f32[384,128]{1,0:T(8,128)S(1)}, u32[]{:S(2)}, u32[]{:S(2)}) collective-permute-start(f32[384,128]{1,0:T(8,128)S(1)} %shard_map.63), channel_id=1, source_target_pairs={{0,1},{1,0},{2,3},{3,2},{4,5},{5,4},{6,7},{7,6},{8,9},{9,8},{10,11... | collective-permute-start | bytes 589832 | tf_op jit(solution)/shard_map/ppermute | solution.py:246
  31.3 0.4 %shard_map.60 = (f32[384,128]{1,0:T(8,128)S(1)}, f32[384,128]{1,0:T(8,128)S(1)}) custom-call(bf16[384,2048]{1,0:T(8,128)(2,1)S(1)} %get-tuple-element.33.refs_0_.refs_1_, bf16[384,2048]{1,0:T(8,128)(2,1)S(1)} %get-tuple-element.34.refs_1_.refs_2_, bf16[128,768]{1,0:T(8,128)(2,1)S(1)} %collective-permute-done.6.refs_2_, ...), custom_call_target="tpu_custom_call" | custom-call | flops 301989888 | bytes 393216 | tf_op jit(solution)/shard_map/pallas_call | solution.py:181
  32.0 0.4 %collective-permute-done.12.refs_7_ = f32[384,128]{1,0:T(8,128)S(1)} collective-permute-done((f32[384,128]{1,0:T(8,128)S(1)}, f32[384,128]{1,0:T(8,128)S(1)}, u32[]{:S(2)}, u32[]{:S(2)}) %collective-permute-start.12) | collective-permute-done | bytes 196640 | tf_op jit(solution)/shard_map/ppermute | solution.py:246
  32.4 0.9 %shard_map.64 = f32[384,512]{1,0:T(8,128)} custom-call(s32[8,128]{1,0:T(8,128)S(1)} %get-tuple-element.39.limit, f32[384,128]{1,0:T(8,128)S(1)} %get-tuple-element.37.refs_0_, f32[384,128]{1,0:T(8,128)S(1)} %collective-permute-done.5.refs_1_, f32[384,128]{1,0:T(8,128)S(1)} %get-tuple-element.48.refs_2_, f32[384,128]{1,0:T(8,128)S(1)} %collective-permute-done.9.refs_3_, ...), custom_call_target="tpu_custom_call" | custom-call | flops 196608 | bytes 2359296 | tf_op jit(solution)/shard_map/pallas_call | solution.py:216
  (15 shorter events, 0.8 us)
Async XLA Ops:
  1.6 9.6 %collective-permute-start = (bf16[128,512]{1,0:T(8,128)(2,1)S(1)}, bf16[128,512]{1,0:T(8,128)(2,1)S(1)}, u32[]{:S(2)}, u32[]{:S(2)}) collective-permute-start(bf16[128,512]{1,0:T(8,128)(2,1)S(1)} %get-tuple-element.30.refs_1_), channel_id=1, source_target_pairs={{0,4},{2,6},{4,8},{6,10},{8,12},{10,14},{12,0},{14,2},{1,5},{3,7},... | collective-permute-start | bytes 393224 | tf_op jit(solution)/shard_map/ppermute | solution.py:246
  4.7 10.6 %collective-permute-start.1 = (bf16[128,768]{1,0:T(8,128)(2,1)S(1)}, bf16[128,768]{1,0:T(8,128)(2,1)S(1)}, u32[]{:S(2)}, u32[]{:S(2)}) collective-permute-start(bf16[128,768]{1,0:T(8,128)(2,1)S(1)} %get-tuple-element.31.refs_2_), channel_id=1, source_target_pairs={{0,4},{2,6},{4,8},{6,10},{8,12},{10,14},{12,0},{14,2},{1,5},{3,7},... | collective-permute-start | bytes 589832 | tf_op jit(solution)/shard_map/ppermute | solution.py:246
  6.2 12.4 %collective-permute-start.2 = (bf16[128,768]{1,0:T(8,128)(2,1)S(1)}, bf16[128,768]{1,0:T(8,128)(2,1)S(1)}, u32[]{:S(2)}, u32[]{:S(2)}) collective-permute-start(bf16[128,768]{1,0:T(8,128)(2,1)S(1)} %get-tuple-element.32.refs_3_), channel_id=1, source_target_pairs={{0,4},{2,6},{4,8},{6,10},{8,12},{10,14},{12,0},{14,2},{1,5},{3,7},... | collective-permute-start | bytes 589832 | tf_op jit(solution)/shard_map/ppermute | solution.py:246
  11.2 5.9 %collective-permute-start.3 = (bf16[128,512]{1,0:T(8,128)(2,1)S(1)}, bf16[128,512]{1,0:T(8,128)(2,1)S(1)}, u32[]{:S(2)}, u32[]{:S(2)}) collective-permute-start(bf16[128,512]{1,0:T(8,128)(2,1)S(1)} %broadcast_select_fusion.2), channel_id=1, source_target_pairs={{0,2},{2,0},{4,6},{6,4},{8,10},{10,8},{12,14},{14,12},{1,3},{3,1},... | collective-permute-start | bytes 393224 | tf_op jit(solution)/shard_map/ppermute | solution.py:246
  15.3 5.9 %collective-permute-start.8 = (bf16[128,768]{1,0:T(8,128)(2,1)S(1)}, bf16[128,768]{1,0:T(8,128)(2,1)S(1)}, u32[]{:S(2)}, u32[]{:S(2)}) collective-permute-start(bf16[128,768]{1,0:T(8,128)(2,1)S(1)} %broadcast_select_fusion), channel_id=1, source_target_pairs={{0,2},{2,0},{4,6},{6,4},{8,10},{10,8},{12,14},{14,12},{1,3},{3,1},... | collective-permute-start | bytes 589832 | tf_op jit(solution)/shard_map/ppermute | solution.py:246
  17.1 7.1 %collective-permute-start.4 = (bf16[128,512]{1,0:T(8,128)(2,1)S(1)}, bf16[128,512]{1,0:T(8,128)(2,1)S(1)}, u32[]{:S(2)}, u32[]{:S(2)}) collective-permute-start(bf16[128,512]{1,0:T(8,128)(2,1)S(1)} %collective-permute-done.3.refs_3_), channel_id=1, source_target_pairs={{0,4},{2,6},{4,8},{6,10},{8,12},{10,14},{12,0},{14,2},{1,5},{3,7},... | collective-permute-start | bytes 393224 | tf_op jit(solution)/shard_map/ppermute | solution.py:246
  18.6 10.7 %collective-permute-start.7 = (bf16[128,768]{1,0:T(8,128)(2,1)S(1)}, bf16[128,768]{1,0:T(8,128)(2,1)S(1)}, u32[]{:S(2)}, u32[]{:S(2)}) collective-permute-start(bf16[128,768]{1,0:T(8,128)(2,1)S(1)} %broadcast_select_fusion.1), channel_id=1, source_target_pairs={{0,2},{2,4},{4,6},{6,8},{8,10},{10,12},{12,14},{14,0},{1,3},{3,5},... | collective-permute-start | bytes 589832 | tf_op jit(solution)/shard_map/ppermute | solution.py:246
  20.2 9.8 %collective-permute-start.6 = (bf16[128,768]{1,0:T(8,128)(2,1)S(1)}, bf16[128,768]{1,0:T(8,128)(2,1)S(1)}, u32[]{:S(2)}, u32[]{:S(2)}) collective-permute-start(bf16[128,768]{1,0:T(8,128)(2,1)S(1)} %collective-permute-done.2.refs_4_), channel_id=1, source_target_pairs={{0,2},{2,0},{4,6},{6,4},{8,10},{10,8},{12,14},{14,12},{1,3},{3,1},... | collective-permute-start | bytes 589832 | tf_op jit(solution)/shard_map/ppermute | solution.py:246
  21.1 9.3 %collective-permute-start.11 = (bf16[128,768]{1,0:T(8,128)(2,1)S(1)}, bf16[128,768]{1,0:T(8,128)(2,1)S(1)}, u32[]{:S(2)}, u32[]{:S(2)}) collective-permute-start(bf16[128,768]{1,0:T(8,128)(2,1)S(1)} %collective-permute-done.8.refs_2_), channel_id=1, source_target_pairs={{0,4},{2,6},{4,8},{6,10},{8,12},{10,14},{12,0},{14,2},{1,5},{3,7},... | collective-permute-start | bytes 589832 | tf_op jit(solution)/shard_map/ppermute | solution.py:246
  22.5 9.5 %collective-permute-start.5 = (f32[384,128]{1,0:T(8,128)S(1)}, f32[384,128]{1,0:T(8,128)S(1)}, u32[]{:S(2)}, u32[]{:S(2)}) collective-permute-start(f32[384,128]{1,0:T(8,128)S(1)} %get-tuple-element.40), channel_id=1, source_target_pairs={{0,1},{1,0},{2,3},{3,2},{4,5},{5,4},{6,7},{7,6},{8,9},{9,8},{10,11... | collective-permute-start | bytes 589832 | tf_op jit(solution)/shard_map/ppermute | solution.py:246
  24.2 7.9 %collective-permute-start.10 = (f32[384,128]{1,0:T(8,128)S(1)}, f32[384,128]{1,0:T(8,128)S(1)}, u32[]{:S(2)}, u32[]{:S(2)}) collective-permute-start(f32[384,128]{1,0:T(8,128)S(1)} %get-tuple-element.52), channel_id=1, source_target_pairs={{0,1},{1,0},{2,3},{3,2},{4,5},{5,4},{6,7},{7,6},{8,9},{9,8},{10,11... | collective-permute-start | bytes 589832 | tf_op jit(solution)/shard_map/ppermute | solution.py:246
  30.4 1.7 %collective-permute-start.9 = (f32[384,128]{1,0:T(8,128)S(1)}, f32[384,128]{1,0:T(8,128)S(1)}, u32[]{:S(2)}, u32[]{:S(2)}) collective-permute-start(f32[384,128]{1,0:T(8,128)S(1)} %get-tuple-element.51), channel_id=1, source_target_pairs={{0,1},{1,0},{2,3},{3,2},{4,5},{5,4},{6,7},{7,6},{8,9},{9,8},{10,11... | collective-permute-start | bytes 589832 | tf_op jit(solution)/shard_map/ppermute | solution.py:246
  30.8 1.6 %collective-permute-start.12 = (f32[384,128]{1,0:T(8,128)S(1)}, f32[384,128]{1,0:T(8,128)S(1)}, u32[]{:S(2)}, u32[]{:S(2)}) collective-permute-start(f32[384,128]{1,0:T(8,128)S(1)} %shard_map.63), channel_id=1, source_target_pairs={{0,1},{1,0},{2,3},{3,2},{4,5},{5,4},{6,7},{7,6},{8,9},{9,8},{10,11... | collective-permute-start | bytes 589832 | tf_op jit(solution)/shard_map/ppermute | solution.py:246

commit v21 on v18

--- a/solution.py
+++ b/solution.py
@@ -51,47 +51,86 @@
     )
 
 
-def prepare_kernel(queries, precond, rank, *refs):
-    chunks, (held, scale, places, arrived) = refs[:CHUNKS], refs[CHUNKS:]
+def ordered_chunk(raw, scale, rank, cut):
+    rows = raw.shape[0]
+    positions = lax.broadcasted_iota(jnp.int32, (rows, rows), 0)
+    placing = (positions == rank[...]).astype(jnp.bfloat16)
+    pre = (raw[:, cut].astype(jnp.float32) * scale[:, cut]).astype(jnp.bfloat16)
+    return jnp.dot(placing, pre, preferred_element_type=jnp.float32).astype(jnp.bfloat16)
+
+
+def prepare_first_kernel(queries, precond, rank, chunk, raw, scale, places, arrived):
+    depth = queries.shape[1]
+    cut, rest = slice(0, chunk.shape[1]), slice(chunk.shape[1], depth)
+    loads = [
+        pltpu.make_async_copy(rank, places, arrived.at[0]),
+        pltpu.make_async_copy(precond, scale, arrived.at[1]),
+        pltpu.make_async_copy(queries.at[:, cut], raw.at[:, cut], arrived.at[2]),
+        pltpu.make_async_copy(queries.at[:, rest], raw.at[:, rest], arrived.at[3]),
+    ]
+    for load in loads:
+        load.start()
+    for load in loads[:3]:
+        load.wait()
+    chunk[...] = ordered_chunk(raw, scale, places, cut)
+    loads[3].wait()
+
+
+def prepare_rest_kernel(cuts, raw, scale, places, *chunks):
+    for cut, chunk in zip(cuts, chunks):
+        chunk[...] = ordered_chunk(raw, scale, places, cut)
+
+
+def prepare(queries, precond, rank):
     rows, depth = queries.shape
     cuts = cuts_of(depth)
-    loads = [pltpu.make_async_copy(rank, places, arrived.at[CHUNKS])]
-    loads.append(pltpu.make_async_copy(precond, scale, arrived.at[CHUNKS + 1]))
-    for n, cut in enumerate(cuts):
-        loads.append(pltpu.make_async_copy(queries.at[:, cut], held.at[:, cut], arrived.at[n]))
+    shapes = [
+        jax.ShapeDtypeStruct((rows, cut.stop - cut.start), jnp.bfloat16) for cut in cuts
+    ]
+    held = [jax.ShapeDtypeStruct(x.shape, x.dtype) for x in (queries, precond, rank)]
+    chunk, *held = pl.pallas_call(
+        prepare_first_kernel,
+        out_shape=[shapes[0], *held],
+        in_specs=[far_spec()] * 3,
+        out_specs=[whole_spec()] * 4,
+        scratch_shapes=[pltpu.SemaphoreType.DMA((4,))],
+        compiler_params=params(),
+        cost_estimate=cost(2 * rows * rows * cuts[0].stop, 2 * rows * depth),
+    )(in_hbm(queries), in_hbm(precond), in_hbm(rank))
+    rest = pl.pallas_call(
+        functools.partial(prepare_rest_kernel, cuts[1:]),
+        out_shape=shapes[1:],
+        in_specs=[whole_spec()] * 3,
+        out_specs=[whole_spec()] * (CHUNKS - 1),
+        compiler_params=params(),
+        cost_estimate=cost(2 * rows * rows * depth, 2 * rows * depth),
+    )(*held)
+    return [chunk, *rest]
+
+
+def load_kernel(store, other, mine, arrived):
+    half = other.shape[0]
+    me = lax.axis_index("dim")
+    loads = []
+    for n, (where, to) in enumerate(((1 - me, other), (me, mine))):
+        place = pl.ds(pl.multiple_of(where * half, half), half)
+        loads.append(pltpu.make_async_copy(store.at[place], to, arrived.at[n]))
+        loads[n].start()
     for load in loads:
-        load.start()
-    loads[0].wait()
-    loads[1].wait()
-    positions = lax.broadcasted_iota(jnp.int32, (rows, rows), 0)
-    placing = (positions == places[...]).astype(jnp.bfloat16)
-    for n, cut in enumerate(cuts):
-        loads[2 + n].wait()
-        pre = (held[:, cut].astype(jnp.float32) * scale[:, cut]).astype(jnp.bfloat16)
-        chunks[n][...] = jnp.dot(placing, pre, preferred_element_type=jnp.float32).astype(
-            jnp.bfloat16
-        )
-
-
-def prepare(queries, precond, rank):
-    rows, depth = queries.shape
-    shapes = [
-        jax.ShapeDtypeStruct((rows, cut.stop - cut.start), jnp.bfloat16) for cut in cuts_of(depth)
-    ]
+        load.wait()
+
+
+def loaded(store):
+    half = jax.ShapeDtypeStruct((store.shape[0] // 2, store.shape[1]), store.dtype)
     return pl.pallas_call(
-        prepare_kernel,
-        out_shape=shapes,
-        in_specs=[far_spec()] * 3,
-        out_specs=[whole_spec()] * CHUNKS,
-        scratch_shapes=[
-            pltpu.VMEM((rows, depth), jnp.bfloat16),
-            pltpu.VMEM((1, depth), jnp.float32),
-            pltpu.VMEM((1, rows), jnp.int32),
-            pltpu.SemaphoreType.DMA((CHUNKS + 2,)),
-        ],
-        compiler_params=params(),
-        cost_estimate=cost(2 * rows * rows * depth, 4 * rows * depth),
-    )(in_hbm(queries), in_hbm(precond), in_hbm(rank))
+        load_kernel,
+        out_shape=[half] * 2,
+        in_specs=[far_spec()],
+        out_specs=[whole_spec()] * 2,
+        scratch_shapes=[pltpu.SemaphoreType.DMA((2,))],
+        compiler_params=params(),
+        cost_estimate=cost(0, 2 * store.size),
+    )(in_hbm(store))
 
 
 def scores_kernel(pieces, fresh, loading, counted, sides, *refs):
@@ -254,12 +293,11 @@
         return jnp.where(odd, at_odd, at_even)
 
     own = prepare(queries, precond[None, :], query_rank)
-    first, stores = more_scores(store, [(n, [(0, own[n])]) for n in range(CHUNKS)], [None])
-    own_pair = exchanged(first)
+    stores = tuple(loaded(store))
     moved = {}
 
     def tied(name, block):
-        earlier = [first[1]] if name == EARLY else []
+        earlier = [stores[1]] if name == EARLY else []
         return after(block, *earlier, *(moved[key] for key in TIES.get(name, "").split()))
 
     def move(name, block, route):
@@ -296,8 +334,10 @@
             direct = moved[f"R{n}"]
             one_back[n], three_back[n] = (swapped, direct), (direct, swapped)
 
-    [two] = more_scores(stores, [(n, [(0, two_back[n])]) for n in range(CHUNKS)], [None])
-    two_pair = exchanged(two)
+    first, two = more_scores(
+        stores, [(n, [(0, own[n]), (1, two_back[n])]) for n in range(CHUNKS)], [None, None]
+    )
+    own_pair, two_pair = exchanged(first), exchanged(two)
     limited = after(valid_rows, two[1])
     one = three = one_pair = None
     todo, out = set(range(CHUNKS)), None

time: 33.6 us -> 34.5 us (1.027)
  waiting for transfers between devices: 8.92 us -> 5.84 us
  other arithmetic: 0.06 us -> 1.9 us
  starting transfers between devices: 14.1 us -> 15.1 us
  Pallas kernels: 9.51 us -> 10.4 us
    ppermute x13, waiting for transfers between devices: 8.92 us -> 5.84 us  [send(): return lax.ppermute(block, axis, route)]
    pallas_call x1 -> x3, Pallas kernels: 1.58 us -> 4.64 us  [the longest x1 1.9 us: loaded(): pl.pallas_call(load_kernel, out_shape=[half] * 2, in_specs=[far_spec()],...]
    pallas_call x7 -> x6, Pallas kernels: 6.33 us -> 4.19 us  [more_scores(): pl.pallas_call(functools.partial(scores_kernel, tuple(placed), fresh, loa...]
    select_n x3, other arithmetic: 0.06 us -> 1.9 us  [by_parity(): return jnp.where(odd, at_odd, at_even)]
    ppermute x13, starting transfers between devices: 14.1 us -> 15.1 us  [send(): return lax.ppermute(block, axis, route)]
  transfers between devices with their start and end apart: 13 -> 13, of which waited for: 5 -> 5; matrix products, arithmetic and copies ran while one was open for 0% -> 6% of each run, Pallas kernels for 21% -> 23%
where the time goes in v21:
time: 34.5 us; the launch traced here: 34.1 us
  starting transfers between devices  15.1 us (44%)
  Pallas kernels  10.4 us (30%)
  waiting for transfers between devices  5.84 us (17%)
  other arithmetic  1.9 us (6%)
  between operations  0.79 us (2%)
    ppermute x13, starting transfers between devices, send(): return lax.ppermute(block, axis, route)  15.1 us
    ppermute x13, waiting for transfers between devices, send(): return lax.ppermute(block, axis, route)  5.84 us
    pallas_call x6, Pallas kernels, more_scores(): pl.pallas_call(functools.partial(scores_kernel, tuple(placed), fresh, loa...  4.19 us
    select_n x3, other arithmetic, by_parity(): return jnp.where(odd, at_odd, at_even)  1.9 us
    pallas_call x1, Pallas kernels, loaded(): pl.pallas_call(load_kernel, out_shape=[half] * 2, in_specs=[far_spec()],...  1.9 us
    pallas_call x1, Pallas kernels, prepare(): pl.pallas_call(prepare_first_kernel, out_shape=[shapes[0], *held], in_spe...  1.8 us
    pallas_call x2, Pallas kernels, finish(): pl.pallas_call(functools.partial(finish_kernel, places), out_shape=pltpu....  1.6 us
    pallas_call x1, Pallas kernels, prepare(): pl.pallas_call(functools.partial(prepare_rest_kernel, cuts[1:]), out_shap...  0.94 us
  transfers between devices with their start and end apart: 13, of which 5 were waited for; matrix products, arithmetic and copies ran while one was open for 6% of the time, Pallas kernels for 23%

profile of v21, /device:TPU:0, one launch (start us, length us, event | category | flops | bytes accessed | tf_op | source)
XLA Modules:
  0.0 34.1 jit_solution(16692969318406428859)
XLA Ops:
  0.0 1.8 %shard_map.56 = (bf16[128,512]{1,0:T(8,128)(2,1)}, bf16[128,2048]{1,0:T(8,128)(2,1)S(1)}, f32[1,2048]{1,0:T(1,128)S(1)}, s32[1,128]{1,0:T(1,128)S(1)}) custom-call(bf16[128,2048]{1,0:T(8,128)(2,1)} %queries.1, f32[1,2048]{1,0:T(1,128)} %bitcast.1, s32[1,128]{1,0:T(1,128)} %rank.1), custom_call_target="tpu_custom_call" | custom-call | flops 16777216 | bytes 524288 | tf_op jit(solution)/shard_map/pallas_call | solution.py:91
  1.8 3.1 %collective-permute-start = (bf16[128,512]{1,0:T(8,128)(2,1)}, bf16[128,512]{1,0:T(8,128)(2,1)}, u32[]{:S(2)}, u32[]{:S(2)}) collective-permute-start(bf16[128,512]{1,0:T(8,128)(2,1)} %get-tuple-element.35.refs_2_), channel_id=1, source_target_pairs={{0,4},{2,6},{4,8},{6,10},{8,12},{10,14},{12,0},{14,2},{1,5},{3,7},... | collective-permute-start | bytes 393224 | tf_op jit(solution)/shard_map/ppermute | solution.py:286
  4.9 0.9 %shard_map.57 = (bf16[128,768]{1,0:T(8,128)(2,1)S(1)}, bf16[128,768]{1,0:T(8,128)(2,1)}) custom-call(bf16[128,2048]{1,0:T(8,128)(2,1)S(1)} %get-tuple-element.36.raw, f32[1,2048]{1,0:T(1,128)S(1)} %get-tuple-element.37.scale, s32[1,128]{1,0:T(1,128)S(1)} %get-tuple-element.38.places), custom_call_target="tpu_custom_call" | custom-call | flops 67108864 | bytes 524288 | tf_op jit(solution)/shard_map/pallas_call | solution.py:100
  5.8 1.6 %collective-permute-start.1 = (bf16[128,768]{1,0:T(8,128)(2,1)S(1)}, bf16[128,768]{1,0:T(8,128)(2,1)}, u32[]{:S(2)}, u32[]{:S(2)}) collective-permute-start(bf16[128,768]{1,0:T(8,128)(2,1)S(1)} %get-tuple-element.39.refs_4_), channel_id=1, source_target_pairs={{0,4},{2,6},{4,8},{6,10},{8,12},{10,14},{12,0},{14,2},{1,5},{3,7},... | collective-permute-start | bytes 589832 | tf_op jit(solution)/shard_map/ppermute | solution.py:286
  7.4 1.6 %collective-permute-start.2 = (bf16[128,768]{1,0:T(8,128)(2,1)}, bf16[128,768]{1,0:T(8,128)(2,1)S(1)}, u32[]{:S(2)}, u32[]{:S(2)}) collective-permute-start(bf16[128,768]{1,0:T(8,128)(2,1)} %get-tuple-element.40.refs_6_), channel_id=1, source_target_pairs={{0,4},{2,6},{4,8},{6,10},{8,12},{10,14},{12,0},{14,2},{1,5},{3,7},... | collective-permute-start | bytes 589832 | tf_op jit(solution)/shard_map/ppermute | solution.py:286
  9.0 1.9 %shard_map.55 = (bf16[384,2048]{1,0:T(8,128)(2,1)S(1)}, bf16[384,2048]{1,0:T(8,128)(2,1)S(1)}) custom-call(bf16[768,2048]{1,0:T(8,128)(2,1)} %store.1), custom_call_target="tpu_custom_call" | custom-call | bytes 3145728 | tf_op jit(solution)/shard_map/pallas_call | solution.py:125
  10.9 0.7 %collective-permute-done.refs_3_ = bf16[128,512]{1,0:T(8,128)(2,1)} collective-permute-done((bf16[128,512]{1,0:T(8,128)(2,1)}, bf16[128,512]{1,0:T(8,128)(2,1)}, u32[]{:S(2)}, u32[]{:S(2)}) %collective-permute-start) | collective-permute-done | bytes 131104 | tf_op jit(solution)/shard_map/ppermute | solution.py:286
  11.6 0.9 %broadcast_select_fusion.2 = bf16[128,512]{1,0:T(8,128)(2,1)S(1)} fusion(bf16[128,512]{1,0:T(8,128)(2,1)} %collective-permute-done.refs_3_, bf16[128,512]{1,0:T(8,128)(2,1)} %get-tuple-element.35.refs_2_, pred[]{:T(512)S(6)} %eq.3), kind=kLoop, calls=%fused_computation.2 | loop fusion | flops 65536 | bytes 393217 | tf_op jit(solution)/shard_map/jit(_where)/select_n | solution.py:293
  12.5 1.6 %collective-permute-start.3 = (bf16[128,512]{1,0:T(8,128)(2,1)S(1)}, bf16[128,512]{1,0:T(8,128)(2,1)S(1)}, u32[]{:S(2)}, u32[]{:S(2)}) collective-permute-start(bf16[128,512]{1,0:T(8,128)(2,1)S(1)} %broadcast_select_fusion.2), channel_id=1, source_target_pairs={{0,2},{2,0},{4,6},{6,4},{8,10},{10,8},{12,14},{14,12},{1,3},{3,1},... | collective-permute-start | bytes 393224 | tf_op jit(solution)/shard_map/ppermute | solution.py:286
  14.1 1.7 %collective-permute-done.1.refs_5_ = bf16[128,768]{1,0:T(8,128)(2,1)} collective-permute-done((bf16[128,768]{1,0:T(8,128)(2,1)S(1)}, bf16[128,768]{1,0:T(8,128)(2,1)}, u32[]{:S(2)}, u32[]{:S(2)}) %collective-permute-start.1) | collective-permute-done | bytes 196640 | tf_op jit(solution)/shard_map/ppermute | solution.py:286
  15.8 2.5 %collective-permute-start.7 = (bf16[128,768]{1,0:T(8,128)(2,1)S(1)}, bf16[128,768]{1,0:T(8,128)(2,1)S(1)}, u32[]{:S(2)}, u32[]{:S(2)}) collective-permute-start(bf16[128,768]{1,0:T(8,128)(2,1)S(1)} %broadcast_select_fusion), channel_id=1, source_target_pairs={{0,2},{2,0},{4,6},{6,4},{8,10},{10,8},{12,14},{14,12},{1,3},{3,1},... | collective-permute-start | bytes 589832 | tf_op jit(solution)/shard_map/ppermute | solution.py:286
  18.3 0.7 %collective-permute-done.2.refs_7_ = bf16[128,768]{1,0:T(8,128)(2,1)S(1)} collective-permute-done((bf16[128,768]{1,0:T(8,128)(2,1)}, bf16[128,768]{1,0:T(8,128)(2,1)S(1)}, u32[]{:S(2)}, u32[]{:S(2)}) %collective-permute-start.2) | collective-permute-done | bytes 196640 | tf_op jit(solution)/shard_map/ppermute | solution.py:286
  19.1 0.9 %broadcast_select_fusion.1 = bf16[128,768]{1,0:T(8,128)(2,1)S(1)} fusion(bf16[128,768]{1,0:T(8,128)(2,1)S(1)} %collective-permute-done.2.refs_7_, bf16[128,768]{1,0:T(8,128)(2,1)} %get-tuple-element.40.refs_6_, pred[]{:T(512)S(6)} %eq.3), kind=kLoop, calls=%fused_computation.1 | loop fusion | flops 98304 | bytes 589825 | tf_op jit(solution)/shard_map/jit(_where)/select_n | solution.py:293
  20.0 0.6 %collective-permute-start.6 = (bf16[128,768]{1,0:T(8,128)(2,1)S(1)}, bf16[128,768]{1,0:T(8,128)(2,1)S(1)}, u32[]{:S(2)}, u32[]{:S(2)}) collective-permute-start(bf16[128,768]{1,0:T(8,128)(2,1)S(1)} %broadcast_select_fusion.1), channel_id=1, source_target_pairs={{0,2},{2,4},{4,6},{6,8},{8,10},{10,12},{12,14},{14,0},{1,3},{3,5},... | collective-permute-start | bytes 589832 | tf_op jit(solution)/shard_map/ppermute | solution.py:286
  20.6 1.4 %collective-permute-start.5 = (bf16[128,768]{1,0:T(8,128)(2,1)S(1)}, bf16[128,768]{1,0:T(8,128)(2,1)S(1)}, u32[]{:S(2)}, u32[]{:S(2)}) collective-permute-start(bf16[128,768]{1,0:T(8,128)(2,1)S(1)} %collective-permute-done.2.refs_7_), channel_id=1, source_target_pairs={{0,2},{2,0},{4,6},{6,4},{8,10},{10,8},{12,14},{14,12},{1,3},{3,1},... | collective-permute-start | bytes 589832 | tf_op jit(solution)/shard_map/ppermute | solution.py:286
  23.1 1.6 %collective-permute-start.9 = (bf16[128,768]{1,0:T(8,128)(2,1)S(1)}, bf16[128,768]{1,0:T(8,128)(2,1)S(1)}, u32[]{:S(2)}, u32[]{:S(2)}) collective-permute-start(bf16[128,768]{1,0:T(8,128)(2,1)S(1)} %collective-permute-done.7.refs_2_), channel_id=1, source_target_pairs={{0,4},{2,6},{4,8},{6,10},{8,12},{10,14},{12,0},{14,2},{1,5},{3,7},... | collective-permute-start | bytes 589832 | tf_op jit(solution)/shard_map/ppermute | solution.py:286
  24.7 2.2 %shard_map.58 = (f32[384,128]{1,0:T(8,128)S(1)}, f32[384,128]{1,0:T(8,128)S(1)}, f32[384,128]{1,0:T(8,128)S(1)}, f32[384,128]{1,0:T(8,128)S(1)}) custom-call(bf16[384,2048]{1,0:T(8,128)(2,1)S(1)} %get-tuple-element.33.refs_0_.refs_1_, bf16[384,2048]{1,0:T(8,128)(2,1)S(1)} %get-tuple-element.34.refs_1_.refs_2_, bf16[128,512]{1,0:T(8,128)(2,1)} %get-tuple-element.35.refs_2_, ...), custom_call_target="tpu_custom_call" | custom-call | flops 805306368 | bytes 786432 | tf_op jit(solution)/shard_map/pallas_call | solution.py:221
  26.9 0.5 %collective-permute-start.12 = (f32[384,128]{1,0:T(8,128)S(1)}, f32[384,128]{1,0:T(8,128)S(1)}, u32[]{:S(2)}, u32[]{:S(2)}) collective-permute-start(f32[384,128]{1,0:T(8,128)S(1)} %get-tuple-element.60), channel_id=1, source_target_pairs={{0,1},{1,0},{2,3},{3,2},{4,5},{5,4},{6,7},{7,6},{8,9},{9,8},{10,11... | collective-permute-start | bytes 589832 | tf_op jit(solution)/shard_map/ppermute | solution.py:286
  27.8 0.5 %shard_map.60 = (f32[384,128]{1,0:T(8,128)S(1)}, f32[384,128]{1,0:T(8,128)S(1)}, f32[384,128]{1,0:T(8,128)S(1)}, f32[384,128]{1,0:T(8,128)S(1)}) custom-call(bf16[384,2048]{1,0:T(8,128)(2,1)S(1)} %get-tuple-element.33.refs_0_.refs_1_, bf16[384,2048]{1,0:T(8,128)(2,1)S(1)} %get-tuple-element.34.refs_1_.refs_2_, ...), custom_call_target="tpu_custom_call" | custom-call | flops 301989888 | bytes 1572864 | tf_op jit(solution)/shard_map/pallas_call | solution.py:221
  28.3 2.3 %collective-permute-done.6.refs_3_ = bf16[128,768]{1,0:T(8,128)(2,1)S(1)} collective-permute-done((bf16[128,768]{1,0:T(8,128)(2,1)S(1)}, bf16[128,768]{1,0:T(8,128)(2,1)S(1)}, u32[]{:S(2)}, u32[]{:S(2)}) %collective-permute-start.6) | collective-permute-done | bytes 196640 | tf_op jit(solution)/shard_map/ppermute | solution.py:286
  30.6 0.5 %shard_map.61 = (f32[384,128]{1,0:T(8,128)S(1)}, f32[384,128]{1,0:T(8,128)S(1)}, f32[384,128]{1,0:T(8,128)S(1)}, f32[384,128]{1,0:T(8,128)S(1)}) custom-call(bf16[384,2048]{1,0:T(8,128)(2,1)S(1)} %get-tuple-element.33.refs_0_.refs_1_, bf16[384,2048]{1,0:T(8,128)(2,1)S(1)} %get-tuple-element.34.refs_1_.refs_2_, ...), custom_call_target="tpu_custom_call" | custom-call | flops 603979776 | bytes 1572864 | tf_op jit(solution)/shard_map/pallas_call | solution.py:221
  31.6 0.6 %collective-permute-start.10 = (f32[384,128]{1,0:T(8,128)S(1)}, f32[384,128]{1,0:T(8,128)S(1)}, u32[]{:S(2)}, u32[]{:S(2)}) collective-permute-start(f32[384,128]{1,0:T(8,128)S(1)} %shard_map.63), channel_id=1, source_target_pairs={{0,1},{1,0},{2,3},{3,2},{4,5},{5,4},{6,7},{7,6},{8,9},{9,8},{10,11... | collective-permute-start | bytes 589832 | tf_op jit(solution)/shard_map/ppermute | solution.py:286
  32.1 0.8 %shard_map.64.refs_4_ = f32[384,512]{1,0:T(8,128)} custom-call(s32[8,128]{1,0:T(8,128)S(1)} %get-tuple-element.44.limit, f32[384,128]{1,0:T(8,128)S(1)} %get-tuple-element.58.refs_0_, f32[384,128]{1,0:T(8,128)S(1)} %collective-permute-done.11.refs_1_, f32[384,128]{1,0:T(8,128)S(1)} %get-tuple-element.41.refs_2_, f32[384,128]{1,0:T(8,128)S(1)} %collective-permute-done.12.refs_3_), custom_call_target="tpu_custom_call" | custom-call | flops 98304 | bytes 1179648 | tf_op jit(solution)/shard_map/pallas_call | solution.py:256
  33.3 0.8 %shard_map.65 = f32[384,512]{1,0:T(8,128)} custom-call(s32[8,128]{1,0:T(8,128)S(1)} %get-tuple-element.44.limit, f32[384,128]{1,0:T(8,128)S(1)} %get-tuple-element.54.refs_0_, f32[384,128]{1,0:T(8,128)S(1)} %collective-permute-done.8.refs_1_, f32[384,128]{1,0:T(8,128)S(1)} %shard_map.62.refs_2_, ...), custom_call_target="tpu_custom_call", output_to_operand_aliasing={{}: (5, {})} | custom-call | flops 98304 | bytes 1179648 | tf_op jit(solution)/shard_map/pallas_call | solution.py:256
  (16 shorter events, 1.6 us)
Async XLA Ops:
  1.8 9.7 %collective-permute-start = (bf16[128,512]{1,0:T(8,128)(2,1)}, bf16[128,512]{1,0:T(8,128)(2,1)}, u32[]{:S(2)}, u32[]{:S(2)}) collective-permute-start(bf16[128,512]{1,0:T(8,128)(2,1)} %get-tuple-element.35.refs_2_), channel_id=1, source_target_pairs={{0,4},{2,6},{4,8},{6,10},{8,12},{10,14},{12,0},{14,2},{1,5},{3,7},... | collective-permute-start | bytes 393224 | tf_op jit(solution)/shard_map/ppermute | solution.py:286
  5.8 9.9 %collective-permute-start.1 = (bf16[128,768]{1,0:T(8,128)(2,1)S(1)}, bf16[128,768]{1,0:T(8,128)(2,1)}, u32[]{:S(2)}, u32[]{:S(2)}) collective-permute-start(bf16[128,768]{1,0:T(8,128)(2,1)S(1)} %get-tuple-element.39.refs_4_), channel_id=1, source_target_pairs={{0,4},{2,6},{4,8},{6,10},{8,12},{10,14},{12,0},{14,2},{1,5},{3,7},... | collective-permute-start | bytes 589832 | tf_op jit(solution)/shard_map/ppermute | solution.py:286
  7.4 11.6 %collective-permute-start.2 = (bf16[128,768]{1,0:T(8,128)(2,1)}, bf16[128,768]{1,0:T(8,128)(2,1)S(1)}, u32[]{:S(2)}, u32[]{:S(2)}) collective-permute-start(bf16[128,768]{1,0:T(8,128)(2,1)} %get-tuple-element.40.refs_6_), channel_id=1, source_target_pairs={{0,4},{2,6},{4,8},{6,10},{8,12},{10,14},{12,0},{14,2},{1,5},{3,7},... | collective-permute-start | bytes 589832 | tf_op jit(solution)/shard_map/ppermute | solution.py:286
  12.5 5.8 %collective-permute-start.3 = (bf16[128,512]{1,0:T(8,128)(2,1)S(1)}, bf16[128,512]{1,0:T(8,128)(2,1)S(1)}, u32[]{:S(2)}, u32[]{:S(2)}) collective-permute-start(bf16[128,512]{1,0:T(8,128)(2,1)S(1)} %broadcast_select_fusion.2), channel_id=1, source_target_pairs={{0,2},{2,0},{4,6},{6,4},{8,10},{10,8},{12,14},{14,12},{1,3},{3,1},... | collective-permute-start | bytes 393224 | tf_op jit(solution)/shard_map/ppermute | solution.py:286
  15.8 7.3 %collective-permute-start.7 = (bf16[128,768]{1,0:T(8,128)(2,1)S(1)}, bf16[128,768]{1,0:T(8,128)(2,1)S(1)}, u32[]{:S(2)}, u32[]{:S(2)}) collective-permute-start(bf16[128,768]{1,0:T(8,128)(2,1)S(1)} %broadcast_select_fusion), channel_id=1, source_target_pairs={{0,2},{2,0},{4,6},{6,4},{8,10},{10,8},{12,14},{14,12},{1,3},{3,1},... | collective-permute-start | bytes 589832 | tf_op jit(solution)/shard_map/ppermute | solution.py:286
  18.3 8.6 %collective-permute-start.4 = (bf16[128,512]{1,0:T(8,128)(2,1)S(1)}, bf16[128,512]{1,0:T(8,128)(2,1)S(1)}, u32[]{:S(2)}, u32[]{:S(2)}) collective-permute-start(bf16[128,512]{1,0:T(8,128)(2,1)S(1)} %collective-permute-done.3.refs_3_), channel_id=1, source_target_pairs={{0,4},{2,6},{4,8},{6,10},{8,12},{10,14},{12,0},{14,2},{1,5},{3,7},... | collective-permute-start | bytes 393224 | tf_op jit(solution)/shard_map/ppermute | solution.py:286
  20.0 10.6 %collective-permute-start.6 = (bf16[128,768]{1,0:T(8,128)(2,1)S(1)}, bf16[128,768]{1,0:T(8,128)(2,1)S(1)}, u32[]{:S(2)}, u32[]{:S(2)}) collective-permute-start(bf16[128,768]{1,0:T(8,128)(2,1)S(1)} %broadcast_select_fusion.1), channel_id=1, source_target_pairs={{0,2},{2,4},{4,6},{6,8},{8,10},{10,12},{12,14},{14,0},{1,3},{3,5},... | collective-permute-start | bytes 589832 | tf_op jit(solution)/shard_map/ppermute | solution.py:286
  20.6 10.0 %collective-permute-start.5 = (bf16[128,768]{1,0:T(8,128)(2,1)S(1)}, bf16[128,768]{1,0:T(8,128)(2,1)S(1)}, u32[]{:S(2)}, u32[]{:S(2)}) collective-permute-start(bf16[128,768]{1,0:T(8,128)(2,1)S(1)} %collective-permute-done.2.refs_7_), channel_id=1, source_target_pairs={{0,2},{2,0},{4,6},{6,4},{8,10},{10,8},{12,14},{14,12},{1,3},{3,1},... | collective-permute-start | bytes 589832 | tf_op jit(solution)/shard_map/ppermute | solution.py:286
  23.1 8.2 %collective-permute-start.9 = (bf16[128,768]{1,0:T(8,128)(2,1)S(1)}, bf16[128,768]{1,0:T(8,128)(2,1)S(1)}, u32[]{:S(2)}, u32[]{:S(2)}) collective-permute-start(bf16[128,768]{1,0:T(8,128)(2,1)S(1)} %collective-permute-done.7.refs_2_), channel_id=1, source_target_pairs={{0,4},{2,6},{4,8},{6,10},{8,12},{10,14},{12,0},{14,2},{1,5},{3,7},... | collective-permute-start | bytes 589832 | tf_op jit(solution)/shard_map/ppermute | solution.py:286
  26.8 5.3 %collective-permute-start.11 = (f32[384,128]{1,0:T(8,128)S(1)}, f32[384,128]{1,0:T(8,128)S(1)}, u32[]{:S(2)}, u32[]{:S(2)}) collective-permute-start(f32[384,128]{1,0:T(8,128)S(1)} %get-tuple-element.59), channel_id=1, source_target_pairs={{0,1},{1,0},{2,3},{3,2},{4,5},{5,4},{6,7},{7,6},{8,9},{9,8},{10,11... | collective-permute-start | bytes 589832 | tf_op jit(solution)/shard_map/ppermute | solution.py:286
  26.9 5.2 %collective-permute-start.12 = (f32[384,128]{1,0:T(8,128)S(1)}, f32[384,128]{1,0:T(8,128)S(1)}, u32[]{:S(2)}, u32[]{:S(2)}) collective-permute-start(f32[384,128]{1,0:T(8,128)S(1)} %get-tuple-element.60), channel_id=1, source_target_pairs={{0,1},{1,0},{2,3},{3,2},{4,5},{5,4},{6,7},{7,6},{8,9},{9,8},{10,11... | collective-permute-start | bytes 589832 | tf_op jit(solution)/shard_map/ppermute | solution.py:286
  31.1 2.1 %collective-permute-start.8 = (f32[384,128]{1,0:T(8,128)S(1)}, f32[384,128]{1,0:T(8,128)S(1)}, u32[]{:S(2)}, u32[]{:S(2)}) collective-permute-start(f32[384,128]{1,0:T(8,128)S(1)} %get-tuple-element.55), channel_id=1, source_target_pairs={{0,1},{1,0},{2,3},{3,2},{4,5},{5,4},{6,7},{7,6},{8,9},{9,8},{10,11... | collective-permute-start | bytes 589832 | tf_op jit(solution)/shard_map/ppermute | solution.py:286
  31.6 1.7 %collective-permute-start.10 = (f32[384,128]{1,0:T(8,128)S(1)}, f32[384,128]{1,0:T(8,128)S(1)}, u32[]{:S(2)}, u32[]{:S(2)}) collective-permute-start(f32[384,128]{1,0:T(8,128)S(1)} %shard_map.63), channel_id=1, source_target_pairs={{0,1},{1,0},{2,3},{3,2},{4,5},{5,4},{6,7},{7,6},{8,9},{9,8},{10,11... | collective-permute-start | bytes 589832 | tf_op jit(solution)/shard_map/ppermute | solution.py:286

commit v22 on v18

--- a/solution.py
+++ b/solution.py
@@ -14,7 +14,6 @@
 ORDER = ("B0", "B1", "B2", "C0", "C1", "E0", "E1", "R2", "C2")
 TIES = {"C2": "C0"}
 EARLY = "C0"
-OUT = "none"
 WEIGHT = 2
 CHUNKS = len(PARTS)
 VMEM_BYTES = 16 * 1024 * 1024
@@ -52,7 +51,7 @@
 
 
 def prepare_kernel(queries, precond, rank, *refs):
-    chunks, (held, scale, places, arrived) = refs[:CHUNKS], refs[CHUNKS:]
+    chunks, (own, held, scale, places, arrived) = refs[:CHUNKS], refs[CHUNKS:]
     rows, depth = queries.shape
     cuts = cuts_of(depth)
     loads = [pltpu.make_async_copy(rank, places, arrived.at[CHUNKS])]
@@ -68,9 +67,9 @@
     for n, cut in enumerate(cuts):
         loads[2 + n].wait()
         pre = (held[:, cut].astype(jnp.float32) * scale[:, cut]).astype(jnp.bfloat16)
-        chunks[n][...] = jnp.dot(placing, pre, preferred_element_type=jnp.float32).astype(
-            jnp.bfloat16
-        )
+        ordered = jnp.dot(placing, pre, preferred_element_type=jnp.float32).astype(jnp.bfloat16)
+        chunks[n][...] = ordered
+        own[:, cut] = ordered
 
 
 def prepare(queries, precond, rank):
@@ -80,9 +79,9 @@
     ]
     return pl.pallas_call(
         prepare_kernel,
-        out_shape=shapes,
+        out_shape=shapes + [jax.ShapeDtypeStruct((rows, depth), jnp.bfloat16)],
         in_specs=[far_spec()] * 3,
-        out_specs=[whole_spec()] * CHUNKS,
+        out_specs=[whole_spec()] * (CHUNKS + 1),
         scratch_shapes=[
             pltpu.VMEM((rows, depth), jnp.bfloat16),
             pltpu.VMEM((1, depth), jnp.float32),
@@ -117,7 +116,7 @@
     count_out = len(sides) * count
     outs = refs[-count_out:]
     carried = refs[-count_out - len(sides) * (count - sum(fresh)):-count_out]
-    cuts = cuts_of(other.shape[1])
+    cuts = cuts_of(other.shape[1]) + [slice(0, other.shape[1])]
     stacks = []
     for n, targets in pieces:
         values = []
@@ -253,8 +252,8 @@
     def by_parity(at_even, at_odd):
         return jnp.where(odd, at_odd, at_even)
 
-    own = prepare(queries, precond[None, :], query_rank)
-    first, stores = more_scores(store, [(n, [(0, own[n])]) for n in range(CHUNKS)], [None])
+    *own, undivided = prepare(queries, precond[None, :], query_rank)
+    first, stores = more_scores(store, [(CHUNKS, [(0, undivided)])], [None])
     own_pair = exchanged(first)
     moved = {}
 
@@ -300,12 +299,9 @@
     two_pair = exchanged(two)
     limited = after(valid_rows, two[1])
     one = three = one_pair = None
-    todo, out = set(range(CHUNKS)), None
+    todo = set(range(CHUNKS))
     for group in CHAIN:
         pieces = []
-        if group == OUT:
-            out = finish(limit, [own_pair, two_pair], (0, 2), STEPS)
-            one = after(one[0], out), one[1]
         for item in group.split():
             n, parts = int(item[1:]), {"b": (0, 1), "o": (0,), "t": (1,)}[item[0]]
             blocks = one_back[n], three_back[n]
@@ -324,8 +320,7 @@
             three = theirs, ours
         if one_pair is None and not todo:
             one_pair = exchanged(one)
-    if out is None:
-        out = finish(limit, [own_pair, two_pair], (0, 2), STEPS)
+    out = finish(limit, [own_pair, two_pair], (0, 2), STEPS)
     return finish(limit, [one_pair, exchanged(three)], (1, 3), STEPS, out)
 
 

time: 33.6 us -> 33.6 us (level)
  no operation moved by 1% of the time
where the time goes in v22:
time: 33.6 us; the launch traced here: 33.4 us
  starting transfers between devices  14.1 us (42%)
  Pallas kernels  9.51 us (28%)
  waiting for transfers between devices  8.92 us (27%)
  between operations  0.79 us (2%)
    ppermute x13, starting transfers between devices, send(): return lax.ppermute(block, axis, route)  14.1 us
    ppermute x13, waiting for transfers between devices, send(): return lax.ppermute(block, axis, route)  8.92 us
    pallas_call x7, Pallas kernels, more_scores(): pl.pallas_call(functools.partial(scores_kernel, tuple(placed), fresh, loa...  6.33 us
    pallas_call x2, Pallas kernels, finish(): pl.pallas_call(functools.partial(finish_kernel, places), out_shape=pltpu....  1.6 us
    pallas_call x1, Pallas kernels, prepare(): pl.pallas_call(prepare_kernel, out_shape=shapes + [jax.ShapeDtypeStruct((...  1.58 us
  transfers between devices with their start and end apart: 13, of which 5 were waited for; matrix products, arithmetic and copies ran while one was open for 0% of the time, Pallas kernels for 21%

profile of v22, /device:TPU:0, one launch (start us, length us, event | category | flops | bytes accessed | tf_op | source)
XLA Modules:
  0.0 33.4 jit_solution(3254411655337363322)
XLA Ops:
  0.0 1.6 %shard_map.55 = (bf16[128,512]{1,0:T(8,128)(2,1)S(1)}, bf16[128,768]{1,0:T(8,128)(2,1)S(1)}, bf16[128,768]{1,0:T(8,128)(2,1)S(1)}, bf16[128,2048]{1,0:T(8,128)(2,1)S(1)}) custom-call(bf16[128,2048]{1,0:T(8,128)(2,1)} %queries.1, f32[1,2048]{1,0:T(1,128)} %bitcast.1, s32[1,128]{1,0:T(1,128)} %rank.1), custom_call_target="tpu_custom_call" | custom-call | flops 67108864 | bytes 1048576 | tf_op jit(solution)/shard_map/pallas_call | solution.py:80
  1.6 3.1 %collective-permute-start = (bf16[128,512]{1,0:T(8,128)(2,1)S(1)}, bf16[128,512]{1,0:T(8,128)(2,1)S(1)}, u32[]{:S(2)}, u32[]{:S(2)}) collective-permute-start(bf16[128,512]{1,0:T(8,128)(2,1)S(1)} %get-tuple-element.34), channel_id=1, source_target_pairs={{0,4},{2,6},{4,8},{6,10},{8,12},{10,14},{12,0},{14,2},{1,5},{3,7},... | collective-permute-start | bytes 393224 | tf_op jit(solution)/shard_map/ppermute | solution.py:246
  4.7 1.6 %collective-permute-start.1 = (bf16[128,768]{1,0:T(8,128)(2,1)S(1)}, bf16[128,768]{1,0:T(8,128)(2,1)S(1)}, u32[]{:S(2)}, u32[]{:S(2)}) collective-permute-start(bf16[128,768]{1,0:T(8,128)(2,1)S(1)} %get-tuple-element.35), channel_id=1, source_target_pairs={{0,4},{2,6},{4,8},{6,10},{8,12},{10,14},{12,0},{14,2},{1,5},{3,7},... | collective-permute-start | bytes 589832 | tf_op jit(solution)/shard_map/ppermute | solution.py:246
  6.2 1.6 %collective-permute-start.2 = (bf16[128,768]{1,0:T(8,128)(2,1)S(1)}, bf16[128,768]{1,0:T(8,128)(2,1)S(1)}, u32[]{:S(2)}, u32[]{:S(2)}) collective-permute-start(bf16[128,768]{1,0:T(8,128)(2,1)S(1)} %get-tuple-element.36), channel_id=1, source_target_pairs={{0,4},{2,6},{4,8},{6,10},{8,12},{10,14},{12,0},{14,2},{1,5},{3,7},... | collective-permute-start | bytes 589832 | tf_op jit(solution)/shard_map/ppermute | solution.py:246
  7.8 3.3 %shard_map.56 = (f32[384,128]{1,0:T(8,128)S(1)}, f32[384,128]{1,0:T(8,128)S(1)}, bf16[384,2048]{1,0:T(8,128)(2,1)S(1)}, bf16[384,2048]{1,0:T(8,128)(2,1)S(1)}) custom-call(bf16[768,2048]{1,0:T(8,128)(2,1)} %refs_0_.1, bf16[128,2048]{1,0:T(8,128)(2,1)S(1)} %get-tuple-element.31.refs_1_), custom_call_target="tpu_custom_call" | custom-call | flops 402653184 | bytes 393216 | tf_op jit(solution)/shard_map/pallas_call | solution.py:181
  11.2 1.6 %collective-permute-start.3 = (bf16[128,512]{1,0:T(8,128)(2,1)S(1)}, bf16[128,512]{1,0:T(8,128)(2,1)S(1)}, u32[]{:S(2)}, u32[]{:S(2)}) collective-permute-start(bf16[128,512]{1,0:T(8,128)(2,1)S(1)} %broadcast_select_fusion.2), channel_id=1, source_target_pairs={{0,2},{2,0},{4,6},{6,4},{8,10},{10,8},{12,14},{14,12},{1,3},{3,1},... | collective-permute-start | bytes 393224 | tf_op jit(solution)/shard_map/ppermute | solution.py:246
  12.8 2.4 %collective-permute-done.1.refs_3_ = bf16[128,768]{1,0:T(8,128)(2,1)S(1)} collective-permute-done((bf16[128,768]{1,0:T(8,128)(2,1)S(1)}, bf16[128,768]{1,0:T(8,128)(2,1)S(1)}, u32[]{:S(2)}, u32[]{:S(2)}) %collective-permute-start.1) | collective-permute-done | bytes 196640 | tf_op jit(solution)/shard_map/ppermute | solution.py:246
  15.3 1.8 %collective-permute-start.7 = (bf16[128,768]{1,0:T(8,128)(2,1)S(1)}, bf16[128,768]{1,0:T(8,128)(2,1)S(1)}, u32[]{:S(2)}, u32[]{:S(2)}) collective-permute-start(bf16[128,768]{1,0:T(8,128)(2,1)S(1)} %broadcast_select_fusion), channel_id=1, source_target_pairs={{0,2},{2,0},{4,6},{6,4},{8,10},{10,8},{12,14},{14,12},{1,3},{3,1},... | collective-permute-start | bytes 589832 | tf_op jit(solution)/shard_map/ppermute | solution.py:246
  17.1 1.6 %collective-permute-done.2.refs_4_ = bf16[128,768]{1,0:T(8,128)(2,1)S(1)} collective-permute-done((bf16[128,768]{1,0:T(8,128)(2,1)S(1)}, bf16[128,768]{1,0:T(8,128)(2,1)S(1)}, u32[]{:S(2)}, u32[]{:S(2)}) %collective-permute-start.2) | collective-permute-done | bytes 196640 | tf_op jit(solution)/shard_map/ppermute | solution.py:246
  18.6 1.5 %collective-permute-start.6 = (bf16[128,768]{1,0:T(8,128)(2,1)S(1)}, bf16[128,768]{1,0:T(8,128)(2,1)S(1)}, u32[]{:S(2)}, u32[]{:S(2)}) collective-permute-start(bf16[128,768]{1,0:T(8,128)(2,1)S(1)} %broadcast_select_fusion.1), channel_id=1, source_target_pairs={{0,2},{2,4},{4,6},{6,8},{8,10},{10,12},{12,14},{14,0},{1,3},{3,5},... | collective-permute-start | bytes 589832 | tf_op jit(solution)/shard_map/ppermute | solution.py:246
  20.2 0.3 collective-permute-start.5
  20.5 0.6 %collective-permute-done.7.refs_2_ = bf16[128,768]{1,0:T(8,128)(2,1)S(1)} collective-permute-done((bf16[128,768]{1,0:T(8,128)(2,1)S(1)}, bf16[128,768]{1,0:T(8,128)(2,1)S(1)}, u32[]{:S(2)}, u32[]{:S(2)}) %collective-permute-start.7) | collective-permute-done | bytes 196640 | tf_op jit(solution)/shard_map/ppermute | solution.py:246
  21.1 1.4 %collective-permute-start.9 = (bf16[128,768]{1,0:T(8,128)(2,1)S(1)}, bf16[128,768]{1,0:T(8,128)(2,1)S(1)}, u32[]{:S(2)}, u32[]{:S(2)}) collective-permute-start(bf16[128,768]{1,0:T(8,128)(2,1)S(1)} %collective-permute-done.7.refs_2_), channel_id=1, source_target_pairs={{0,4},{2,6},{4,8},{6,10},{8,12},{10,14},{12,0},{14,2},{1,5},{3,7},... | collective-permute-start | bytes 589832 | tf_op jit(solution)/shard_map/ppermute | solution.py:246
  23.2 1.0 %shard_map.57 = (f32[384,128]{1,0:T(8,128)S(1)}, f32[384,128]{1,0:T(8,128)S(1)}) custom-call(bf16[384,2048]{1,0:T(8,128)(2,1)S(1)} %get-tuple-element.32.refs_0_.refs_1_, bf16[384,2048]{1,0:T(8,128)(2,1)S(1)} %get-tuple-element.33.refs_1_.refs_2_, bf16[128,512]{1,0:T(8,128)(2,1)S(1)} %collective-permute-done.refs_2_, ...), custom_call_target="tpu_custom_call" | custom-call | flops 402653184 | bytes 393216 | tf_op jit(solution)/shard_map/pallas_call | solution.py:181
  24.2 0.6 %collective-permute-start.12 = (f32[384,128]{1,0:T(8,128)S(1)}, f32[384,128]{1,0:T(8,128)S(1)}, u32[]{:S(2)}, u32[]{:S(2)}) collective-permute-start(f32[384,128]{1,0:T(8,128)S(1)} %get-tuple-element.56), channel_id=1, source_target_pairs={{0,1},{1,0},{2,3},{3,2},{4,5},{5,4},{6,7},{7,6},{8,9},{9,8},{10,11... | collective-permute-start | bytes 589832 | tf_op jit(solution)/shard_map/ppermute | solution.py:246
  24.7 0.4 %shard_map.58 = (f32[384,128]{1,0:T(8,128)S(1)}, f32[384,128]{1,0:T(8,128)S(1)}, f32[384,128]{1,0:T(8,128)S(1)}, f32[384,128]{1,0:T(8,128)S(1)}, s32[8,128]{1,0:T(8,128)S(1)}) custom-call(s32[1]{0:T(128)S(6)} %copy.8.refs_0_, bf16[384,2048]{1,0:T(8,128)(2,1)S(1)} %get-tuple-element.32.refs_0_.refs_1_, ...), custom_call_target="tpu_custom_call" | custom-call | flops 402653184 | bytes 1572864 | tf_op jit(solution)/shard_map/pallas_call | solution.py:181
  25.1 0.5 %shard_map.59 = (f32[384,128]{1,0:T(8,128)S(1)}, f32[384,128]{1,0:T(8,128)S(1)}, f32[384,128]{1,0:T(8,128)S(1)}, f32[384,128]{1,0:T(8,128)S(1)}) custom-call(bf16[384,2048]{1,0:T(8,128)(2,1)S(1)} %get-tuple-element.32.refs_0_.refs_1_, bf16[384,2048]{1,0:T(8,128)(2,1)S(1)} %get-tuple-element.33.refs_1_.refs_2_, ...), custom_call_target="tpu_custom_call" | custom-call | flops 301989888 | bytes 1572864 | tf_op jit(solution)/shard_map/pallas_call | solution.py:181
  25.6 3.7 %collective-permute-done.6.refs_3_ = bf16[128,768]{1,0:T(8,128)(2,1)S(1)} collective-permute-done((bf16[128,768]{1,0:T(8,128)(2,1)S(1)}, bf16[128,768]{1,0:T(8,128)(2,1)S(1)}, u32[]{:S(2)}, u32[]{:S(2)}) %collective-permute-start.6) | collective-permute-done | bytes 196640 | tf_op jit(solution)/shard_map/ppermute | solution.py:246
  29.3 0.6 %collective-permute-done.5.refs_2_ = bf16[128,768]{1,0:T(8,128)(2,1)S(1)} collective-permute-done((bf16[128,768]{1,0:T(8,128)(2,1)S(1)}, bf16[128,768]{1,0:T(8,128)(2,1)S(1)}, u32[]{:S(2)}, u32[]{:S(2)}) %collective-permute-start.5) | collective-permute-done | bytes 196640 | tf_op jit(solution)/shard_map/ppermute | solution.py:246
  30.0 0.5 %shard_map.60 = (f32[384,128]{1,0:T(8,128)S(1)}, f32[384,128]{1,0:T(8,128)S(1)}, f32[384,128]{1,0:T(8,128)S(1)}, f32[384,128]{1,0:T(8,128)S(1)}) custom-call(bf16[384,2048]{1,0:T(8,128)(2,1)S(1)} %get-tuple-element.32.refs_0_.refs_1_, bf16[384,2048]{1,0:T(8,128)(2,1)S(1)} %get-tuple-element.33.refs_1_.refs_2_, ...), custom_call_target="tpu_custom_call" | custom-call | flops 603979776 | bytes 1572864 | tf_op jit(solution)/shard_map/pallas_call | solution.py:181
  30.6 0.3 shard_map.62
  30.9 0.5 %collective-permute-start.10 = (f32[384,128]{1,0:T(8,128)S(1)}, f32[384,128]{1,0:T(8,128)S(1)}, u32[]{:S(2)}, u32[]{:S(2)}) collective-permute-start(f32[384,128]{1,0:T(8,128)S(1)} %shard_map.62), channel_id=1, source_target_pairs={{0,1},{1,0},{2,3},{3,2},{4,5},{5,4},{6,7},{7,6},{8,9},{9,8},{10,11... | collective-permute-start | bytes 589832 | tf_op jit(solution)/shard_map/ppermute | solution.py:246
  31.5 0.8 %shard_map.63.refs_4_ = f32[384,512]{1,0:T(8,128)} custom-call(s32[8,128]{1,0:T(8,128)S(1)} %get-tuple-element.41.limit, f32[384,128]{1,0:T(8,128)S(1)} %get-tuple-element.39.refs_0_, f32[384,128]{1,0:T(8,128)S(1)} %collective-permute-done.11.refs_1_, f32[384,128]{1,0:T(8,128)S(1)} %get-tuple-element.37.refs_2_, f32[384,128]{1,0:T(8,128)S(1)} %collective-permute-done.12.refs_3_), custom_call_target="tpu_custom_call" | custom-call | flops 98304 | bytes 1179648 | tf_op jit(solution)/shard_map/pallas_call | solution.py:216
  32.6 0.8 %shard_map.64 = f32[384,512]{1,0:T(8,128)} custom-call(s32[8,128]{1,0:T(8,128)S(1)} %get-tuple-element.41.limit, f32[384,128]{1,0:T(8,128)S(1)} %get-tuple-element.51.refs_0_, f32[384,128]{1,0:T(8,128)S(1)} %collective-permute-done.8.refs_1_, f32[384,128]{1,0:T(8,128)S(1)} %shard_map.61.refs_2_, ...), custom_call_target="tpu_custom_call", output_to_operand_aliasing={{}: (5, {})} | custom-call | flops 98304 | bytes 1179648 | tf_op jit(solution)/shard_map/pallas_call | solution.py:216
  (15 shorter events, 0.5 us)
Async XLA Ops:
  1.6 9.6 %collective-permute-start = (bf16[128,512]{1,0:T(8,128)(2,1)S(1)}, bf16[128,512]{1,0:T(8,128)(2,1)S(1)}, u32[]{:S(2)}, u32[]{:S(2)}) collective-permute-start(bf16[128,512]{1,0:T(8,128)(2,1)S(1)} %get-tuple-element.34), channel_id=1, source_target_pairs={{0,4},{2,6},{4,8},{6,10},{8,12},{10,14},{12,0},{14,2},{1,5},{3,7},... | collective-permute-start | bytes 393224 | tf_op jit(solution)/shard_map/ppermute | solution.py:246
  4.7 10.6 %collective-permute-start.1 = (bf16[128,768]{1,0:T(8,128)(2,1)S(1)}, bf16[128,768]{1,0:T(8,128)(2,1)S(1)}, u32[]{:S(2)}, u32[]{:S(2)}) collective-permute-start(bf16[128,768]{1,0:T(8,128)(2,1)S(1)} %get-tuple-element.35), channel_id=1, source_target_pairs={{0,4},{2,6},{4,8},{6,10},{8,12},{10,14},{12,0},{14,2},{1,5},{3,7},... | collective-permute-start | bytes 589832 | tf_op jit(solution)/shard_map/ppermute | solution.py:246
  6.2 12.4 %collective-permute-start.2 = (bf16[128,768]{1,0:T(8,128)(2,1)S(1)}, bf16[128,768]{1,0:T(8,128)(2,1)S(1)}, u32[]{:S(2)}, u32[]{:S(2)}) collective-permute-start(bf16[128,768]{1,0:T(8,128)(2,1)S(1)} %get-tuple-element.36), channel_id=1, source_target_pairs={{0,4},{2,6},{4,8},{6,10},{8,12},{10,14},{12,0},{14,2},{1,5},{3,7},... | collective-permute-start | bytes 589832 | tf_op jit(solution)/shard_map/ppermute | solution.py:246
  11.2 5.9 %collective-permute-start.3 = (bf16[128,512]{1,0:T(8,128)(2,1)S(1)}, bf16[128,512]{1,0:T(8,128)(2,1)S(1)}, u32[]{:S(2)}, u32[]{:S(2)}) collective-permute-start(bf16[128,512]{1,0:T(8,128)(2,1)S(1)} %broadcast_select_fusion.2), channel_id=1, source_target_pairs={{0,2},{2,0},{4,6},{6,4},{8,10},{10,8},{12,14},{14,12},{1,3},{3,1},... | collective-permute-start | bytes 393224 | tf_op jit(solution)/shard_map/ppermute | solution.py:246
  15.3 5.9 %collective-permute-start.7 = (bf16[128,768]{1,0:T(8,128)(2,1)S(1)}, bf16[128,768]{1,0:T(8,128)(2,1)S(1)}, u32[]{:S(2)}, u32[]{:S(2)}) collective-permute-start(bf16[128,768]{1,0:T(8,128)(2,1)S(1)} %broadcast_select_fusion), channel_id=1, source_target_pairs={{0,2},{2,0},{4,6},{6,4},{8,10},{10,8},{12,14},{14,12},{1,3},{3,1},... | collective-permute-start | bytes 589832 | tf_op jit(solution)/shard_map/ppermute | solution.py:246
  17.1 7.1 %collective-permute-start.4 = (bf16[128,512]{1,0:T(8,128)(2,1)S(1)}, bf16[128,512]{1,0:T(8,128)(2,1)S(1)}, u32[]{:S(2)}, u32[]{:S(2)}) collective-permute-start(bf16[128,512]{1,0:T(8,128)(2,1)S(1)} %collective-permute-done.3.refs_3_), channel_id=1, source_target_pairs={{0,4},{2,6},{4,8},{6,10},{8,12},{10,14},{12,0},{14,2},{1,5},{3,7},... | collective-permute-start | bytes 393224 | tf_op jit(solution)/shard_map/ppermute | solution.py:246
  18.6 10.7 %collective-permute-start.6 = (bf16[128,768]{1,0:T(8,128)(2,1)S(1)}, bf16[128,768]{1,0:T(8,128)(2,1)S(1)}, u32[]{:S(2)}, u32[]{:S(2)}) collective-permute-start(bf16[128,768]{1,0:T(8,128)(2,1)S(1)} %broadcast_select_fusion.1), channel_id=1, source_target_pairs={{0,2},{2,4},{4,6},{6,8},{8,10},{10,12},{12,14},{14,0},{1,3},{3,5},... | collective-permute-start | bytes 589832 | tf_op jit(solution)/shard_map/ppermute | solution.py:246
  20.2 9.8 %collective-permute-start.5 = (bf16[128,768]{1,0:T(8,128)(2,1)S(1)}, bf16[128,768]{1,0:T(8,128)(2,1)S(1)}, u32[]{:S(2)}, u32[]{:S(2)}) collective-permute-start(bf16[128,768]{1,0:T(8,128)(2,1)S(1)} %collective-permute-done.2.refs_4_), channel_id=1, source_target_pairs={{0,2},{2,0},{4,6},{6,4},{8,10},{10,8},{12,14},{14,12},{1,3},{3,1},... | collective-permute-start | bytes 589832 | tf_op jit(solution)/shard_map/ppermute | solution.py:246
  21.1 9.5 %collective-permute-start.9 = (bf16[128,768]{1,0:T(8,128)(2,1)S(1)}, bf16[128,768]{1,0:T(8,128)(2,1)S(1)}, u32[]{:S(2)}, u32[]{:S(2)}) collective-permute-start(bf16[128,768]{1,0:T(8,128)(2,1)S(1)} %collective-permute-done.7.refs_2_), channel_id=1, source_target_pairs={{0,4},{2,6},{4,8},{6,10},{8,12},{10,14},{12,0},{14,2},{1,5},{3,7},... | collective-permute-start | bytes 589832 | tf_op jit(solution)/shard_map/ppermute | solution.py:246
  22.5 8.9 %collective-permute-start.11 = (f32[384,128]{1,0:T(8,128)S(1)}, f32[384,128]{1,0:T(8,128)S(1)}, u32[]{:S(2)}, u32[]{:S(2)}) collective-permute-start(f32[384,128]{1,0:T(8,128)S(1)} %get-tuple-element.55), channel_id=1, source_target_pairs={{0,1},{1,0},{2,3},{3,2},{4,5},{5,4},{6,7},{7,6},{8,9},{9,8},{10,11... | collective-permute-start | bytes 589832 | tf_op jit(solution)/shard_map/ppermute | solution.py:246
  24.2 7.3 %collective-permute-start.12 = (f32[384,128]{1,0:T(8,128)S(1)}, f32[384,128]{1,0:T(8,128)S(1)}, u32[]{:S(2)}, u32[]{:S(2)}) collective-permute-start(f32[384,128]{1,0:T(8,128)S(1)} %get-tuple-element.56), channel_id=1, source_target_pairs={{0,1},{1,0},{2,3},{3,2},{4,5},{5,4},{6,7},{7,6},{8,9},{9,8},{10,11... | collective-permute-start | bytes 589832 | tf_op jit(solution)/shard_map/ppermute | solution.py:246
  30.5 2.1 %collective-permute-start.8 = (f32[384,128]{1,0:T(8,128)S(1)}, f32[384,128]{1,0:T(8,128)S(1)}, u32[]{:S(2)}, u32[]{:S(2)}) collective-permute-start(f32[384,128]{1,0:T(8,128)S(1)} %get-tuple-element.52), channel_id=1, source_target_pairs={{0,1},{1,0},{2,3},{3,2},{4,5},{5,4},{6,7},{7,6},{8,9},{9,8},{10,11... | collective-permute-start | bytes 589832 | tf_op jit(solution)/shard_map/ppermute | solution.py:246
  30.9 1.7 %collective-permute-start.10 = (f32[384,128]{1,0:T(8,128)S(1)}, f32[384,128]{1,0:T(8,128)S(1)}, u32[]{:S(2)}, u32[]{:S(2)}) collective-permute-start(f32[384,128]{1,0:T(8,128)S(1)} %shard_map.62), channel_id=1, source_target_pairs={{0,1},{1,0},{2,3},{3,2},{4,5},{5,4},{6,7},{7,6},{8,9},{9,8},{10,11... | collective-permute-start | bytes 589832 | tf_op jit(solution)/shard_map/ppermute | solution.py:246

commit v23 on v22

--- a/solution.py
+++ b/solution.py
@@ -9,12 +9,12 @@
 
 STEPS = 4
 KINDS = "UUT"
-PARTS = (4, 6, 6)
+PARTS = (4, 7, 5)
 CHAIN = ("b0", "o1", "b2", "t1")
 ORDER = ("B0", "B1", "B2", "C0", "C1", "E0", "E1", "R2", "C2")
 TIES = {"C2": "C0"}
 EARLY = "C0"
-WEIGHT = 2
+WEIGHT = 3
 CHUNKS = len(PARTS)
 VMEM_BYTES = 16 * 1024 * 1024
 

time: 33.6 us -> 34 us (1.012)
  starting transfers between devices: 14.1 us -> 14.7 us
    ppermute x13, starting transfers between devices: 14.1 us -> 14.7 us  [send(): return lax.ppermute(block, axis, route)]
  transfers between devices with their start and end apart: 13 -> 13, of which waited for: 5 -> 6; matrix products, arithmetic and copies ran while one was open for 0% -> 0% of each run, Pallas kernels for 21% -> 22%
where the time goes in v23:
time: 34 us; the launch traced here: 33.8 us
  starting transfers between devices  14.7 us (43%)
  Pallas kernels  9.69 us (28%)
  waiting for transfers between devices  8.59 us (25%)
  between operations  0.8 us (2%)
    ppermute x13, starting transfers between devices, send(): return lax.ppermute(block, axis, route)  14.7 us
    ppermute x13, waiting for transfers between devices, send(): return lax.ppermute(block, axis, route)  8.59 us
    pallas_call x7, Pallas kernels, more_scores(): pl.pallas_call(functools.partial(scores_kernel, tuple(placed), fresh, loa...  6.52 us
    pallas_call x2, Pallas kernels, finish(): pl.pallas_call(functools.partial(finish_kernel, places), out_shape=pltpu....  1.6 us
    pallas_call x1, Pallas kernels, prepare(): pl.pallas_call(prepare_kernel, out_shape=shapes + [jax.ShapeDtypeStruct((...  1.57 us
  transfers between devices with their start and end apart: 13, of which 6 were waited for; matrix products, arithmetic and copies ran while one was open for 0% of the time, Pallas kernels for 22%

profile of v23, /device:TPU:0, one launch (start us, length us, event | category | flops | bytes accessed | tf_op | source)
XLA Modules:
  0.0 33.8 jit_solution(8803368767632144015)
XLA Ops:
  0.0 1.6 %shard_map.55 = (bf16[128,512]{1,0:T(8,128)(2,1)S(1)}, bf16[128,896]{1,0:T(8,128)(2,1)S(1)}, bf16[128,640]{1,0:T(8,128)(2,1)S(1)}, bf16[128,2048]{1,0:T(8,128)(2,1)S(1)}) custom-call(bf16[128,2048]{1,0:T(8,128)(2,1)} %queries.1, f32[1,2048]{1,0:T(1,128)} %bitcast.1, s32[1,128]{1,0:T(1,128)} %rank.1), custom_call_target="tpu_custom_call" | custom-call | flops 67108864 | bytes 1048576 | tf_op jit(solution)/shard_map/pallas_call | solution.py:80
  1.6 3.1 %collective-permute-start = (bf16[128,512]{1,0:T(8,128)(2,1)S(1)}, bf16[128,512]{1,0:T(8,128)(2,1)S(1)}, u32[]{:S(2)}, u32[]{:S(2)}) collective-permute-start(bf16[128,512]{1,0:T(8,128)(2,1)S(1)} %get-tuple-element.34), channel_id=1, source_target_pairs={{0,4},{2,6},{4,8},{6,10},{8,12},{10,14},{12,0},{14,2},{1,5},{3,7},... | collective-permute-start | bytes 393224 | tf_op jit(solution)/shard_map/ppermute | solution.py:246
  4.7 1.6 %collective-permute-start.1 = (bf16[128,896]{1,0:T(8,128)(2,1)S(1)}, bf16[128,896]{1,0:T(8,128)(2,1)S(1)}, u32[]{:S(2)}, u32[]{:S(2)}) collective-permute-start(bf16[128,896]{1,0:T(8,128)(2,1)S(1)} %get-tuple-element.35), channel_id=1, source_target_pairs={{0,4},{2,6},{4,8},{6,10},{8,12},{10,14},{12,0},{14,2},{1,5},{3,7},... | collective-permute-start | bytes 688136 | tf_op jit(solution)/shard_map/ppermute | solution.py:246
  6.2 1.6 %collective-permute-start.2 = (bf16[128,640]{1,0:T(8,128)(2,1)S(1)}, bf16[128,640]{1,0:T(8,128)(2,1)S(1)}, u32[]{:S(2)}, u32[]{:S(2)}) collective-permute-start(bf16[128,640]{1,0:T(8,128)(2,1)S(1)} %get-tuple-element.36), channel_id=1, source_target_pairs={{0,4},{2,6},{4,8},{6,10},{8,12},{10,14},{12,0},{14,2},{1,5},{3,7},... | collective-permute-start | bytes 491528 | tf_op jit(solution)/shard_map/ppermute | solution.py:246
  7.8 3.3 %shard_map.56 = (f32[384,128]{1,0:T(8,128)S(1)}, f32[384,128]{1,0:T(8,128)S(1)}, bf16[384,2048]{1,0:T(8,128)(2,1)S(1)}, bf16[384,2048]{1,0:T(8,128)(2,1)S(1)}) custom-call(bf16[768,2048]{1,0:T(8,128)(2,1)} %refs_0_.1, bf16[128,2048]{1,0:T(8,128)(2,1)S(1)} %get-tuple-element.31.refs_1_), custom_call_target="tpu_custom_call" | custom-call | flops 402653184 | bytes 393216 | tf_op jit(solution)/shard_map/pallas_call | solution.py:181
  11.2 1.6 %collective-permute-start.3 = (bf16[128,512]{1,0:T(8,128)(2,1)S(1)}, bf16[128,512]{1,0:T(8,128)(2,1)S(1)}, u32[]{:S(2)}, u32[]{:S(2)}) collective-permute-start(bf16[128,512]{1,0:T(8,128)(2,1)S(1)} %broadcast_select_fusion.2), channel_id=1, source_target_pairs={{0,2},{2,0},{4,6},{6,4},{8,10},{10,8},{12,14},{14,12},{1,3},{3,1},... | collective-permute-start | bytes 393224 | tf_op jit(solution)/shard_map/ppermute | solution.py:246
  12.8 3.1 %collective-permute-done.1.refs_3_ = bf16[128,896]{1,0:T(8,128)(2,1)S(1)} collective-permute-done((bf16[128,896]{1,0:T(8,128)(2,1)S(1)}, bf16[128,896]{1,0:T(8,128)(2,1)S(1)}, u32[]{:S(2)}, u32[]{:S(2)}) %collective-permute-start.1) | collective-permute-done | bytes 229408 | tf_op jit(solution)/shard_map/ppermute | solution.py:246
  16.0 1.8 %collective-permute-start.7 = (bf16[128,896]{1,0:T(8,128)(2,1)S(1)}, bf16[128,896]{1,0:T(8,128)(2,1)S(1)}, u32[]{:S(2)}, u32[]{:S(2)}) collective-permute-start(bf16[128,896]{1,0:T(8,128)(2,1)S(1)} %broadcast_select_fusion), channel_id=1, source_target_pairs={{0,2},{2,0},{4,6},{6,4},{8,10},{10,8},{12,14},{14,12},{1,3},{3,1},... | collective-permute-start | bytes 688136 | tf_op jit(solution)/shard_map/ppermute | solution.py:246
  17.8 0.8 %collective-permute-done.2.refs_4_ = bf16[128,640]{1,0:T(8,128)(2,1)S(1)} collective-permute-done((bf16[128,640]{1,0:T(8,128)(2,1)S(1)}, bf16[128,640]{1,0:T(8,128)(2,1)S(1)}, u32[]{:S(2)}, u32[]{:S(2)}) %collective-permute-start.2) | collective-permute-done | bytes 163872 | tf_op jit(solution)/shard_map/ppermute | solution.py:246
  18.6 1.5 %collective-permute-start.6 = (bf16[128,640]{1,0:T(8,128)(2,1)S(1)}, bf16[128,640]{1,0:T(8,128)(2,1)S(1)}, u32[]{:S(2)}, u32[]{:S(2)}) collective-permute-start(bf16[128,640]{1,0:T(8,128)(2,1)S(1)} %broadcast_select_fusion.1), channel_id=1, source_target_pairs={{0,2},{2,4},{4,6},{6,8},{8,10},{10,12},{12,14},{14,0},{1,3},{3,5},... | collective-permute-start | bytes 491528 | tf_op jit(solution)/shard_map/ppermute | solution.py:246
  20.2 0.5 %collective-permute-start.5 = (bf16[128,640]{1,0:T(8,128)(2,1)S(1)}, bf16[128,640]{1,0:T(8,128)(2,1)S(1)}, u32[]{:S(2)}, u32[]{:S(2)}) collective-permute-start(bf16[128,640]{1,0:T(8,128)(2,1)S(1)} %collective-permute-done.2.refs_4_), channel_id=1, source_target_pairs={{0,2},{2,0},{4,6},{6,4},{8,10},{10,8},{12,14},{14,12},{1,3},{3,1},... | collective-permute-start | bytes 491528 | tf_op jit(solution)/shard_map/ppermute | solution.py:246
  20.7 2.7 %collective-permute-done.7.refs_2_ = bf16[128,896]{1,0:T(8,128)(2,1)S(1)} collective-permute-done((bf16[128,896]{1,0:T(8,128)(2,1)S(1)}, bf16[128,896]{1,0:T(8,128)(2,1)S(1)}, u32[]{:S(2)}, u32[]{:S(2)}) %collective-permute-start.7) | collective-permute-done | bytes 229408 | tf_op jit(solution)/shard_map/ppermute | solution.py:246
  23.3 2.3 %collective-permute-start.9 = (bf16[128,896]{1,0:T(8,128)(2,1)S(1)}, bf16[128,896]{1,0:T(8,128)(2,1)S(1)}, u32[]{:S(2)}, u32[]{:S(2)}) collective-permute-start(bf16[128,896]{1,0:T(8,128)(2,1)S(1)} %collective-permute-done.7.refs_2_), channel_id=1, source_target_pairs={{0,4},{2,6},{4,8},{6,10},{8,12},{10,14},{12,0},{14,2},{1,5},{3,7},... | collective-permute-start | bytes 688136 | tf_op jit(solution)/shard_map/ppermute | solution.py:246
  26.3 1.0 %shard_map.57 = (f32[384,128]{1,0:T(8,128)S(1)}, f32[384,128]{1,0:T(8,128)S(1)}) custom-call(bf16[384,2048]{1,0:T(8,128)(2,1)S(1)} %get-tuple-element.32.refs_0_.refs_1_, bf16[384,2048]{1,0:T(8,128)(2,1)S(1)} %get-tuple-element.33.refs_1_.refs_2_, bf16[128,512]{1,0:T(8,128)(2,1)S(1)} %collective-permute-done.refs_2_, ...), custom_call_target="tpu_custom_call" | custom-call | flops 402653184 | bytes 393216 | tf_op jit(solution)/shard_map/pallas_call | solution.py:181
  27.3 0.6 %collective-permute-start.12 = (f32[384,128]{1,0:T(8,128)S(1)}, f32[384,128]{1,0:T(8,128)S(1)}, u32[]{:S(2)}, u32[]{:S(2)}) collective-permute-start(f32[384,128]{1,0:T(8,128)S(1)} %get-tuple-element.56), channel_id=1, source_target_pairs={{0,1},{1,0},{2,3},{3,2},{4,5},{5,4},{6,7},{7,6},{8,9},{9,8},{10,11... | collective-permute-start | bytes 589832 | tf_op jit(solution)/shard_map/ppermute | solution.py:246
  27.8 0.4 %shard_map.58 = (f32[384,128]{1,0:T(8,128)S(1)}, f32[384,128]{1,0:T(8,128)S(1)}, f32[384,128]{1,0:T(8,128)S(1)}, f32[384,128]{1,0:T(8,128)S(1)}, s32[8,128]{1,0:T(8,128)S(1)}) custom-call(s32[1]{0:T(128)S(6)} %copy.8.refs_0_, bf16[384,2048]{1,0:T(8,128)(2,1)S(1)} %get-tuple-element.32.refs_0_.refs_1_, ...), custom_call_target="tpu_custom_call" | custom-call | flops 603979776 | bytes 2359296 | tf_op jit(solution)/shard_map/pallas_call | solution.py:181
  28.3 0.5 %shard_map.59 = (f32[384,128]{1,0:T(8,128)S(1)}, f32[384,128]{1,0:T(8,128)S(1)}, f32[384,128]{1,0:T(8,128)S(1)}, f32[384,128]{1,0:T(8,128)S(1)}) custom-call(bf16[384,2048]{1,0:T(8,128)(2,1)S(1)} %get-tuple-element.32.refs_0_.refs_1_, bf16[384,2048]{1,0:T(8,128)(2,1)S(1)} %get-tuple-element.33.refs_1_.refs_2_, ...), custom_call_target="tpu_custom_call" | custom-call | flops 528482304 | bytes 2359296 | tf_op jit(solution)/shard_map/pallas_call | solution.py:181
  28.8 0.2 collective-permute-done.5.refs_2_
  29.1 0.5 %shard_map.60 = (f32[384,128]{1,0:T(8,128)S(1)}, f32[384,128]{1,0:T(8,128)S(1)}, f32[384,128]{1,0:T(8,128)S(1)}, f32[384,128]{1,0:T(8,128)S(1)}) custom-call(bf16[384,2048]{1,0:T(8,128)(2,1)S(1)} %get-tuple-element.32.refs_0_.refs_1_, bf16[384,2048]{1,0:T(8,128)(2,1)S(1)} %get-tuple-element.33.refs_1_.refs_2_, ...), custom_call_target="tpu_custom_call" | custom-call | flops 754974720 | bytes 2359296 | tf_op jit(solution)/shard_map/pallas_call | solution.py:181
  29.7 1.5 %collective-permute-done.9.refs_2_ = bf16[128,896]{1,0:T(8,128)(2,1)S(1)} collective-permute-done((bf16[128,896]{1,0:T(8,128)(2,1)S(1)}, bf16[128,896]{1,0:T(8,128)(2,1)S(1)}, u32[]{:S(2)}, u32[]{:S(2)}) %collective-permute-start.9) | collective-permute-done | bytes 229408 | tf_op jit(solution)/shard_map/ppermute | solution.py:246
  31.2 0.4 %shard_map.62 = f32[384,128]{1,0:T(8,128)S(1)} custom-call(bf16[384,2048]{1,0:T(8,128)(2,1)S(1)} %get-tuple-element.32.refs_0_.refs_1_, bf16[384,2048]{1,0:T(8,128)(2,1)S(1)} %get-tuple-element.33.refs_1_.refs_2_, bf16[128,896]{1,0:T(8,128)(2,1)S(1)} %collective-permute-done.9.refs_2_, f32[384,128]{1,0:T(8,128)S(1)} %get-tuple-element.54.refs_3_), custom_call_target="tpu_custom_call" | custom-call | flops 176160768 | bytes 196608 | tf_op jit(solution)/shard_map/pallas_call | solution.py:181
  31.6 0.8 %shard_map.63.refs_4_ = f32[384,512]{1,0:T(8,128)} custom-call(s32[8,128]{1,0:T(8,128)S(1)} %get-tuple-element.41.limit, f32[384,128]{1,0:T(8,128)S(1)} %get-tuple-element.39.refs_0_, f32[384,128]{1,0:T(8,128)S(1)} %collective-permute-done.11.refs_1_, f32[384,128]{1,0:T(8,128)S(1)} %get-tuple-element.37.refs_2_, f32[384,128]{1,0:T(8,128)S(1)} %collective-permute-done.12.refs_3_), custom_call_target="tpu_custom_call" | custom-call | flops 98304 | bytes 1179648 | tf_op jit(solution)/shard_map/pallas_call | solution.py:216
  32.4 0.4 %shard_map.61.refs_2_ = f32[384,128]{1,0:T(8,128)S(1)} custom-call(bf16[384,2048]{1,0:T(8,128)(2,1)S(1)} %get-tuple-element.32.refs_0_.refs_1_, bf16[384,2048]{1,0:T(8,128)(2,1)S(1)} %get-tuple-element.33.refs_1_.refs_2_, bf16[128,896]{1,0:T(8,128)(2,1)S(1)} %collective-permute-done.9.refs_2_, f32[384,128]{1,0:T(8,128)S(1)} %get-tuple-element.53.refs_3_), custom_call_target="tpu_custom_call" | custom-call | flops 176160768 | bytes 196608 | tf_op jit(solution)/shard_map/pallas_call | solution.py:181
  33.0 0.8 %shard_map.64 = f32[384,512]{1,0:T(8,128)} custom-call(s32[8,128]{1,0:T(8,128)S(1)} %get-tuple-element.41.limit, f32[384,128]{1,0:T(8,128)S(1)} %get-tuple-element.51.refs_0_, f32[384,128]{1,0:T(8,128)S(1)} %collective-permute-done.8.refs_1_, f32[384,128]{1,0:T(8,128)S(1)} %shard_map.61.refs_2_, ...), custom_call_target="tpu_custom_call", output_to_operand_aliasing={{}: (5, {})} | custom-call | flops 98304 | bytes 1179648 | tf_op jit(solution)/shard_map/pallas_call | solution.py:216
  (15 shorter events, 0.5 us)
Async XLA Ops:
  1.6 9.6 %collective-permute-start = (bf16[128,512]{1,0:T(8,128)(2,1)S(1)}, bf16[128,512]{1,0:T(8,128)(2,1)S(1)}, u32[]{:S(2)}, u32[]{:S(2)}) collective-permute-start(bf16[128,512]{1,0:T(8,128)(2,1)S(1)} %get-tuple-element.34), channel_id=1, source_target_pairs={{0,4},{2,6},{4,8},{6,10},{8,12},{10,14},{12,0},{14,2},{1,5},{3,7},... | collective-permute-start | bytes 393224 | tf_op jit(solution)/shard_map/ppermute | solution.py:246
  4.7 11.3 %collective-permute-start.1 = (bf16[128,896]{1,0:T(8,128)(2,1)S(1)}, bf16[128,896]{1,0:T(8,128)(2,1)S(1)}, u32[]{:S(2)}, u32[]{:S(2)}) collective-permute-start(bf16[128,896]{1,0:T(8,128)(2,1)S(1)} %get-tuple-element.35), channel_id=1, source_target_pairs={{0,4},{2,6},{4,8},{6,10},{8,12},{10,14},{12,0},{14,2},{1,5},{3,7},... | collective-permute-start | bytes 688136 | tf_op jit(solution)/shard_map/ppermute | solution.py:246
  6.2 12.4 %collective-permute-start.2 = (bf16[128,640]{1,0:T(8,128)(2,1)S(1)}, bf16[128,640]{1,0:T(8,128)(2,1)S(1)}, u32[]{:S(2)}, u32[]{:S(2)}) collective-permute-start(bf16[128,640]{1,0:T(8,128)(2,1)S(1)} %get-tuple-element.36), channel_id=1, source_target_pairs={{0,4},{2,6},{4,8},{6,10},{8,12},{10,14},{12,0},{14,2},{1,5},{3,7},... | collective-permute-start | bytes 491528 | tf_op jit(solution)/shard_map/ppermute | solution.py:246
  11.2 6.6 %collective-permute-start.3 = (bf16[128,512]{1,0:T(8,128)(2,1)S(1)}, bf16[128,512]{1,0:T(8,128)(2,1)S(1)}, u32[]{:S(2)}, u32[]{:S(2)}) collective-permute-start(bf16[128,512]{1,0:T(8,128)(2,1)S(1)} %broadcast_select_fusion.2), channel_id=1, source_target_pairs={{0,2},{2,0},{4,6},{6,4},{8,10},{10,8},{12,14},{14,12},{1,3},{3,1},... | collective-permute-start | bytes 393224 | tf_op jit(solution)/shard_map/ppermute | solution.py:246
  16.0 7.4 %collective-permute-start.7 = (bf16[128,896]{1,0:T(8,128)(2,1)S(1)}, bf16[128,896]{1,0:T(8,128)(2,1)S(1)}, u32[]{:S(2)}, u32[]{:S(2)}) collective-permute-start(bf16[128,896]{1,0:T(8,128)(2,1)S(1)} %broadcast_select_fusion), channel_id=1, source_target_pairs={{0,2},{2,0},{4,6},{6,4},{8,10},{10,8},{12,14},{14,12},{1,3},{3,1},... | collective-permute-start | bytes 688136 | tf_op jit(solution)/shard_map/ppermute | solution.py:246
  17.8 9.5 %collective-permute-start.4 = (bf16[128,512]{1,0:T(8,128)(2,1)S(1)}, bf16[128,512]{1,0:T(8,128)(2,1)S(1)}, u32[]{:S(2)}, u32[]{:S(2)}) collective-permute-start(bf16[128,512]{1,0:T(8,128)(2,1)S(1)} %collective-permute-done.3.refs_3_), channel_id=1, source_target_pairs={{0,4},{2,6},{4,8},{6,10},{8,12},{10,14},{12,0},{14,2},{1,5},{3,7},... | collective-permute-start | bytes 393224 | tf_op jit(solution)/shard_map/ppermute | solution.py:246
  18.6 10.2 %collective-permute-start.6 = (bf16[128,640]{1,0:T(8,128)(2,1)S(1)}, bf16[128,640]{1,0:T(8,128)(2,1)S(1)}, u32[]{:S(2)}, u32[]{:S(2)}) collective-permute-start(bf16[128,640]{1,0:T(8,128)(2,1)S(1)} %broadcast_select_fusion.1), channel_id=1, source_target_pairs={{0,2},{2,4},{4,6},{6,8},{8,10},{10,12},{12,14},{14,0},{1,3},{3,5},... | collective-permute-start | bytes 491528 | tf_op jit(solution)/shard_map/ppermute | solution.py:246
  20.2 8.9 %collective-permute-start.5 = (bf16[128,640]{1,0:T(8,128)(2,1)S(1)}, bf16[128,640]{1,0:T(8,128)(2,1)S(1)}, u32[]{:S(2)}, u32[]{:S(2)}) collective-permute-start(bf16[128,640]{1,0:T(8,128)(2,1)S(1)} %collective-permute-done.2.refs_4_), channel_id=1, source_target_pairs={{0,2},{2,0},{4,6},{6,4},{8,10},{10,8},{12,14},{14,12},{1,3},{3,1},... | collective-permute-start | bytes 491528 | tf_op jit(solution)/shard_map/ppermute | solution.py:246
  23.3 7.8 %collective-permute-start.9 = (bf16[128,896]{1,0:T(8,128)(2,1)S(1)}, bf16[128,896]{1,0:T(8,128)(2,1)S(1)}, u32[]{:S(2)}, u32[]{:S(2)}) collective-permute-start(bf16[128,896]{1,0:T(8,128)(2,1)S(1)} %collective-permute-done.7.refs_2_), channel_id=1, source_target_pairs={{0,4},{2,6},{4,8},{6,10},{8,12},{10,14},{12,0},{14,2},{1,5},{3,7},... | collective-permute-start | bytes 688136 | tf_op jit(solution)/shard_map/ppermute | solution.py:246
  25.6 6.0 %collective-permute-start.11 = (f32[384,128]{1,0:T(8,128)S(1)}, f32[384,128]{1,0:T(8,128)S(1)}, u32[]{:S(2)}, u32[]{:S(2)}) collective-permute-start(f32[384,128]{1,0:T(8,128)S(1)} %get-tuple-element.55), channel_id=1, source_target_pairs={{0,1},{1,0},{2,3},{3,2},{4,5},{5,4},{6,7},{7,6},{8,9},{9,8},{10,11... | collective-permute-start | bytes 589832 | tf_op jit(solution)/shard_map/ppermute | solution.py:246
  27.3 4.3 %collective-permute-start.12 = (f32[384,128]{1,0:T(8,128)S(1)}, f32[384,128]{1,0:T(8,128)S(1)}, u32[]{:S(2)}, u32[]{:S(2)}) collective-permute-start(f32[384,128]{1,0:T(8,128)S(1)} %get-tuple-element.56), channel_id=1, source_target_pairs={{0,1},{1,0},{2,3},{3,2},{4,5},{5,4},{6,7},{7,6},{8,9},{9,8},{10,11... | collective-permute-start | bytes 589832 | tf_op jit(solution)/shard_map/ppermute | solution.py:246
  29.6 3.2 %collective-permute-start.8 = (f32[384,128]{1,0:T(8,128)S(1)}, f32[384,128]{1,0:T(8,128)S(1)}, u32[]{:S(2)}, u32[]{:S(2)}) collective-permute-start(f32[384,128]{1,0:T(8,128)S(1)} %get-tuple-element.52), channel_id=1, source_target_pairs={{0,1},{1,0},{2,3},{3,2},{4,5},{5,4},{6,7},{7,6},{8,9},{9,8},{10,11... | collective-permute-start | bytes 589832 | tf_op jit(solution)/shard_map/ppermute | solution.py:246
  31.5 1.5 %collective-permute-start.10 = (f32[384,128]{1,0:T(8,128)S(1)}, f32[384,128]{1,0:T(8,128)S(1)}, u32[]{:S(2)}, u32[]{:S(2)}) collective-permute-start(f32[384,128]{1,0:T(8,128)S(1)} %shard_map.62), channel_id=1, source_target_pairs={{0,1},{1,0},{2,3},{3,2},{4,5},{5,4},{6,7},{7,6},{8,9},{9,8},{10,11... | collective-permute-start | bytes 589832 | tf_op jit(solution)/shard_map/ppermute | solution.py:246

commit v24 on v22

--- a/solution.py
+++ b/solution.py
@@ -12,7 +12,7 @@
 PARTS = (4, 6, 6)
 CHAIN = ("b0", "o1", "b2", "t1")
 ORDER = ("B0", "B1", "B2", "C0", "C1", "E0", "E1", "R2", "C2")
-TIES = {"C2": "C0"}
+TIES = {"C2": "C0", "R2": "C0"}
 EARLY = "C0"
 WEIGHT = 2
 CHUNKS = len(PARTS)

time: 33.6 us -> 34.2 us (1.018)
  waiting for transfers between devices: 8.92 us -> 10.1 us
  starting transfers between devices: 14.1 us -> 13.6 us
    ppermute x13, waiting for transfers between devices: 8.92 us -> 10.1 us  [send(): return lax.ppermute(block, axis, route)]
    ppermute x13, starting transfers between devices: 14.1 us -> 13.6 us  [send(): return lax.ppermute(block, axis, route)]
  transfers between devices with their start and end apart: 13 -> 13, of which waited for: 5 -> 6; matrix products, arithmetic and copies ran while one was open for 0% -> 0% of each run, Pallas kernels for 21% -> 21%
where the time goes in v24:
time: 34.2 us; the launch traced here: 34 us
  starting transfers between devices  13.6 us (40%)
  waiting for transfers between devices  10.1 us (30%)
  Pallas kernels  9.49 us (28%)
  between operations  0.78 us (2%)
    ppermute x13, starting transfers between devices, send(): return lax.ppermute(block, axis, route)  13.6 us
    ppermute x13, waiting for transfers between devices, send(): return lax.ppermute(block, axis, route)  10.1 us
    pallas_call x7, Pallas kernels, more_scores(): pl.pallas_call(functools.partial(scores_kernel, tuple(placed), fresh, loa...  6.31 us
    pallas_call x2, Pallas kernels, finish(): pl.pallas_call(functools.partial(finish_kernel, places), out_shape=pltpu....  1.6 us
    pallas_call x1, Pallas kernels, prepare(): pl.pallas_call(prepare_kernel, out_shape=shapes + [jax.ShapeDtypeStruct((...  1.58 us
  transfers between devices with their start and end apart: 13, of which 6 were waited for; matrix products, arithmetic and copies ran while one was open for 0% of the time, Pallas kernels for 21%

profile of v24, /device:TPU:0, one launch (start us, length us, event | category | flops | bytes accessed | tf_op | source)
XLA Modules:
  0.0 34.0 jit_solution(13691801940375627033)
XLA Ops:
  0.0 1.6 %shard_map.55 = (bf16[128,512]{1,0:T(8,128)(2,1)S(1)}, bf16[128,768]{1,0:T(8,128)(2,1)S(1)}, bf16[128,768]{1,0:T(8,128)(2,1)S(1)}, bf16[128,2048]{1,0:T(8,128)(2,1)S(1)}) custom-call(bf16[128,2048]{1,0:T(8,128)(2,1)} %queries.1, f32[1,2048]{1,0:T(1,128)} %bitcast.1, s32[1,128]{1,0:T(1,128)} %rank.1), custom_call_target="tpu_custom_call" | custom-call | flops 67108864 | bytes 1048576 | tf_op jit(solution)/shard_map/pallas_call | solution.py:80
  1.6 3.1 %collective-permute-start = (bf16[128,512]{1,0:T(8,128)(2,1)S(1)}, bf16[128,512]{1,0:T(8,128)(2,1)S(1)}, u32[]{:S(2)}, u32[]{:S(2)}) collective-permute-start(bf16[128,512]{1,0:T(8,128)(2,1)S(1)} %get-tuple-element.35), channel_id=1, source_target_pairs={{0,4},{2,6},{4,8},{6,10},{8,12},{10,14},{12,0},{14,2},{1,5},{3,7},... | collective-permute-start | bytes 393224 | tf_op jit(solution)/shard_map/ppermute | solution.py:246
  4.7 1.6 %collective-permute-start.1 = (bf16[128,768]{1,0:T(8,128)(2,1)S(1)}, bf16[128,768]{1,0:T(8,128)(2,1)S(1)}, u32[]{:S(2)}, u32[]{:S(2)}) collective-permute-start(bf16[128,768]{1,0:T(8,128)(2,1)S(1)} %get-tuple-element.36), channel_id=1, source_target_pairs={{0,4},{2,6},{4,8},{6,10},{8,12},{10,14},{12,0},{14,2},{1,5},{3,7},... | collective-permute-start | bytes 589832 | tf_op jit(solution)/shard_map/ppermute | solution.py:246
  6.2 1.6 %collective-permute-start.2 = (bf16[128,768]{1,0:T(8,128)(2,1)S(1)}, bf16[128,768]{1,0:T(8,128)(2,1)S(1)}, u32[]{:S(2)}, u32[]{:S(2)}) collective-permute-start(bf16[128,768]{1,0:T(8,128)(2,1)S(1)} %get-tuple-element.37), channel_id=1, source_target_pairs={{0,4},{2,6},{4,8},{6,10},{8,12},{10,14},{12,0},{14,2},{1,5},{3,7},... | collective-permute-start | bytes 589832 | tf_op jit(solution)/shard_map/ppermute | solution.py:246
  7.8 3.3 %shard_map.56 = (f32[384,128]{1,0:T(8,128)S(1)}, f32[384,128]{1,0:T(8,128)S(1)}, bf16[384,2048]{1,0:T(8,128)(2,1)S(1)}, bf16[384,2048]{1,0:T(8,128)(2,1)S(1)}) custom-call(bf16[768,2048]{1,0:T(8,128)(2,1)} %refs_0_.1, bf16[128,2048]{1,0:T(8,128)(2,1)S(1)} %get-tuple-element.32.refs_1_), custom_call_target="tpu_custom_call" | custom-call | flops 402653184 | bytes 393216 | tf_op jit(solution)/shard_map/pallas_call | solution.py:181
  11.2 1.6 %collective-permute-start.3 = (bf16[128,512]{1,0:T(8,128)(2,1)S(1)}, bf16[128,512]{1,0:T(8,128)(2,1)S(1)}, u32[]{:S(2)}, u32[]{:S(2)}) collective-permute-start(bf16[128,512]{1,0:T(8,128)(2,1)S(1)} %broadcast_select_fusion.2), channel_id=1, source_target_pairs={{0,2},{2,0},{4,6},{6,4},{8,10},{10,8},{12,14},{14,12},{1,3},{3,1},... | collective-permute-start | bytes 393224 | tf_op jit(solution)/shard_map/ppermute | solution.py:246
  12.8 2.4 %collective-permute-done.1.refs_3_ = bf16[128,768]{1,0:T(8,128)(2,1)S(1)} collective-permute-done((bf16[128,768]{1,0:T(8,128)(2,1)S(1)}, bf16[128,768]{1,0:T(8,128)(2,1)S(1)}, u32[]{:S(2)}, u32[]{:S(2)}) %collective-permute-start.1) | collective-permute-done | bytes 196640 | tf_op jit(solution)/shard_map/ppermute | solution.py:246
  15.3 1.8 %collective-permute-start.7 = (bf16[128,768]{1,0:T(8,128)(2,1)S(1)}, bf16[128,768]{1,0:T(8,128)(2,1)S(1)}, u32[]{:S(2)}, u32[]{:S(2)}) collective-permute-start(bf16[128,768]{1,0:T(8,128)(2,1)S(1)} %broadcast_select_fusion), channel_id=1, source_target_pairs={{0,2},{2,0},{4,6},{6,4},{8,10},{10,8},{12,14},{14,12},{1,3},{3,1},... | collective-permute-start | bytes 589832 | tf_op jit(solution)/shard_map/ppermute | solution.py:246
  17.1 1.6 %collective-permute-done.2.refs_4_ = bf16[128,768]{1,0:T(8,128)(2,1)S(1)} collective-permute-done((bf16[128,768]{1,0:T(8,128)(2,1)S(1)}, bf16[128,768]{1,0:T(8,128)(2,1)S(1)}, u32[]{:S(2)}, u32[]{:S(2)}) %collective-permute-start.2) | collective-permute-done | bytes 196640 | tf_op jit(solution)/shard_map/ppermute | solution.py:246
  18.6 1.6 %collective-permute-start.5 = (bf16[128,768]{1,0:T(8,128)(2,1)S(1)}, bf16[128,768]{1,0:T(8,128)(2,1)S(1)}, u32[]{:S(2)}, u32[]{:S(2)}) collective-permute-start(bf16[128,768]{1,0:T(8,128)(2,1)S(1)} %collective-permute-done.2.refs_4_), channel_id=1, source_target_pairs={{0,2},{2,0},{4,6},{6,4},{8,10},{10,8},{12,14},{14,12},{1,3},{3,1},... | collective-permute-start | bytes 589832 | tf_op jit(solution)/shard_map/ppermute | solution.py:246
  20.2 0.5 %collective-permute-start.6 = (bf16[128,768]{1,0:T(8,128)(2,1)S(1)}, bf16[128,768]{1,0:T(8,128)(2,1)S(1)}, u32[]{:S(2)}, u32[]{:S(2)}) collective-permute-start(bf16[128,768]{1,0:T(8,128)(2,1)S(1)} %broadcast_select_fusion.1), channel_id=1, source_target_pairs={{0,2},{2,4},{4,6},{6,8},{8,10},{10,12},{12,14},{14,0},{1,3},{3,5},... | collective-permute-start | bytes 589832 | tf_op jit(solution)/shard_map/ppermute | solution.py:246
  20.7 0.6 %collective-permute-done.7.refs_2_ = bf16[128,768]{1,0:T(8,128)(2,1)S(1)} collective-permute-done((bf16[128,768]{1,0:T(8,128)(2,1)S(1)}, bf16[128,768]{1,0:T(8,128)(2,1)S(1)}, u32[]{:S(2)}, u32[]{:S(2)}) %collective-permute-start.7) | collective-permute-done | bytes 196640 | tf_op jit(solution)/shard_map/ppermute | solution.py:246
  21.3 0.7 %collective-permute-start.9 = (bf16[128,768]{1,0:T(8,128)(2,1)S(1)}, bf16[128,768]{1,0:T(8,128)(2,1)S(1)}, u32[]{:S(2)}, u32[]{:S(2)}) collective-permute-start(bf16[128,768]{1,0:T(8,128)(2,1)S(1)} %collective-permute-done.7.refs_2_), channel_id=1, source_target_pairs={{0,4},{2,6},{4,8},{6,10},{8,12},{10,14},{12,0},{14,2},{1,5},{3,7},... | collective-permute-start | bytes 589832 | tf_op jit(solution)/shard_map/ppermute | solution.py:246
  22.7 1.0 %shard_map.57 = (f32[384,128]{1,0:T(8,128)S(1)}, f32[384,128]{1,0:T(8,128)S(1)}) custom-call(bf16[384,2048]{1,0:T(8,128)(2,1)S(1)} %get-tuple-element.33.refs_0_.refs_1_, bf16[384,2048]{1,0:T(8,128)(2,1)S(1)} %get-tuple-element.34.refs_1_.refs_2_, bf16[128,512]{1,0:T(8,128)(2,1)S(1)} %collective-permute-done.refs_2_, ...), custom_call_target="tpu_custom_call" | custom-call | flops 402653184 | bytes 393216 | tf_op jit(solution)/shard_map/pallas_call | solution.py:181
  23.8 0.4 %collective-permute-start.12 = (f32[384,128]{1,0:T(8,128)S(1)}, f32[384,128]{1,0:T(8,128)S(1)}, u32[]{:S(2)}, u32[]{:S(2)}) collective-permute-start(f32[384,128]{1,0:T(8,128)S(1)} %get-tuple-element.58), channel_id=1, source_target_pairs={{0,1},{1,0},{2,3},{3,2},{4,5},{5,4},{6,7},{7,6},{8,9},{9,8},{10,11... | collective-permute-start | bytes 589832 | tf_op jit(solution)/shard_map/ppermute | solution.py:246
  24.3 0.4 %shard_map.58 = (f32[384,128]{1,0:T(8,128)S(1)}, f32[384,128]{1,0:T(8,128)S(1)}, f32[384,128]{1,0:T(8,128)S(1)}, f32[384,128]{1,0:T(8,128)S(1)}, s32[8,128]{1,0:T(8,128)S(1)}) custom-call(s32[1]{0:T(128)S(6)} %copy.8.refs_0_, bf16[384,2048]{1,0:T(8,128)(2,1)S(1)} %get-tuple-element.33.refs_0_.refs_1_, ...), custom_call_target="tpu_custom_call" | custom-call | flops 402653184 | bytes 1572864 | tf_op jit(solution)/shard_map/pallas_call | solution.py:181
  24.7 0.5 %shard_map.59 = (f32[384,128]{1,0:T(8,128)S(1)}, f32[384,128]{1,0:T(8,128)S(1)}, f32[384,128]{1,0:T(8,128)S(1)}, f32[384,128]{1,0:T(8,128)S(1)}) custom-call(bf16[384,2048]{1,0:T(8,128)(2,1)S(1)} %get-tuple-element.33.refs_0_.refs_1_, bf16[384,2048]{1,0:T(8,128)(2,1)S(1)} %get-tuple-element.34.refs_1_.refs_2_, ...), custom_call_target="tpu_custom_call" | custom-call | flops 301989888 | bytes 1572864 | tf_op jit(solution)/shard_map/pallas_call | solution.py:181
  25.2 2.9 %collective-permute-done.5.refs_2_ = bf16[128,768]{1,0:T(8,128)(2,1)S(1)} collective-permute-done((bf16[128,768]{1,0:T(8,128)(2,1)S(1)}, bf16[128,768]{1,0:T(8,128)(2,1)S(1)}, u32[]{:S(2)}, u32[]{:S(2)}) %collective-permute-start.5) | collective-permute-done | bytes 196640 | tf_op jit(solution)/shard_map/ppermute | solution.py:246
  28.1 2.6 %collective-permute-done.6.refs_3_ = bf16[128,768]{1,0:T(8,128)(2,1)S(1)} collective-permute-done((bf16[128,768]{1,0:T(8,128)(2,1)S(1)}, bf16[128,768]{1,0:T(8,128)(2,1)S(1)}, u32[]{:S(2)}, u32[]{:S(2)}) %collective-permute-start.6) | collective-permute-done | bytes 196640 | tf_op jit(solution)/shard_map/ppermute | solution.py:246
  30.6 0.5 %shard_map.60 = (f32[384,128]{1,0:T(8,128)S(1)}, f32[384,128]{1,0:T(8,128)S(1)}, f32[384,128]{1,0:T(8,128)S(1)}, f32[384,128]{1,0:T(8,128)S(1)}) custom-call(bf16[384,2048]{1,0:T(8,128)(2,1)S(1)} %get-tuple-element.33.refs_0_.refs_1_, bf16[384,2048]{1,0:T(8,128)(2,1)S(1)} %get-tuple-element.34.refs_1_.refs_2_, ...), custom_call_target="tpu_custom_call" | custom-call | flops 603979776 | bytes 1572864 | tf_op jit(solution)/shard_map/pallas_call | solution.py:181
  31.2 0.3 shard_map.62
  31.5 0.6 %collective-permute-start.10 = (f32[384,128]{1,0:T(8,128)S(1)}, f32[384,128]{1,0:T(8,128)S(1)}, u32[]{:S(2)}, u32[]{:S(2)}) collective-permute-start(f32[384,128]{1,0:T(8,128)S(1)} %shard_map.62), channel_id=1, source_target_pairs={{0,1},{1,0},{2,3},{3,2},{4,5},{5,4},{6,7},{7,6},{8,9},{9,8},{10,11... | collective-permute-start | bytes 589832 | tf_op jit(solution)/shard_map/ppermute | solution.py:246
  32.1 0.8 %shard_map.63.refs_4_ = f32[384,512]{1,0:T(8,128)} custom-call(s32[8,128]{1,0:T(8,128)S(1)} %get-tuple-element.42.limit, f32[384,128]{1,0:T(8,128)S(1)} %get-tuple-element.40.refs_0_, f32[384,128]{1,0:T(8,128)S(1)} %collective-permute-done.11.refs_1_, f32[384,128]{1,0:T(8,128)S(1)} %get-tuple-element.38.refs_2_, f32[384,128]{1,0:T(8,128)S(1)} %collective-permute-done.12.refs_3_), custom_call_target="tpu_custom_call" | custom-call | flops 98304 | bytes 1179648 | tf_op jit(solution)/shard_map/pallas_call | solution.py:216
  33.2 0.8 %shard_map.64 = f32[384,512]{1,0:T(8,128)} custom-call(s32[8,128]{1,0:T(8,128)S(1)} %get-tuple-element.42.limit, f32[384,128]{1,0:T(8,128)S(1)} %get-tuple-element.53.refs_0_, f32[384,128]{1,0:T(8,128)S(1)} %collective-permute-done.8.refs_1_, f32[384,128]{1,0:T(8,128)S(1)} %shard_map.61.refs_2_, ...), custom_call_target="tpu_custom_call", output_to_operand_aliasing={{}: (5, {})} | custom-call | flops 98304 | bytes 1179648 | tf_op jit(solution)/shard_map/pallas_call | solution.py:216
  (15 shorter events, 0.6 us)
Async XLA Ops:
  1.6 9.6 %collective-permute-start = (bf16[128,512]{1,0:T(8,128)(2,1)S(1)}, bf16[128,512]{1,0:T(8,128)(2,1)S(1)}, u32[]{:S(2)}, u32[]{:S(2)}) collective-permute-start(bf16[128,512]{1,0:T(8,128)(2,1)S(1)} %get-tuple-element.35), channel_id=1, source_target_pairs={{0,4},{2,6},{4,8},{6,10},{8,12},{10,14},{12,0},{14,2},{1,5},{3,7},... | collective-permute-start | bytes 393224 | tf_op jit(solution)/shard_map/ppermute | solution.py:246
  4.7 10.6 %collective-permute-start.1 = (bf16[128,768]{1,0:T(8,128)(2,1)S(1)}, bf16[128,768]{1,0:T(8,128)(2,1)S(1)}, u32[]{:S(2)}, u32[]{:S(2)}) collective-permute-start(bf16[128,768]{1,0:T(8,128)(2,1)S(1)} %get-tuple-element.36), channel_id=1, source_target_pairs={{0,4},{2,6},{4,8},{6,10},{8,12},{10,14},{12,0},{14,2},{1,5},{3,7},... | collective-permute-start | bytes 589832 | tf_op jit(solution)/shard_map/ppermute | solution.py:246
  6.2 12.4 %collective-permute-start.2 = (bf16[128,768]{1,0:T(8,128)(2,1)S(1)}, bf16[128,768]{1,0:T(8,128)(2,1)S(1)}, u32[]{:S(2)}, u32[]{:S(2)}) collective-permute-start(bf16[128,768]{1,0:T(8,128)(2,1)S(1)} %get-tuple-element.37), channel_id=1, source_target_pairs={{0,4},{2,6},{4,8},{6,10},{8,12},{10,14},{12,0},{14,2},{1,5},{3,7},... | collective-permute-start | bytes 589832 | tf_op jit(solution)/shard_map/ppermute | solution.py:246
  11.2 5.9 %collective-permute-start.3 = (bf16[128,512]{1,0:T(8,128)(2,1)S(1)}, bf16[128,512]{1,0:T(8,128)(2,1)S(1)}, u32[]{:S(2)}, u32[]{:S(2)}) collective-permute-start(bf16[128,512]{1,0:T(8,128)(2,1)S(1)} %broadcast_select_fusion.2), channel_id=1, source_target_pairs={{0,2},{2,0},{4,6},{6,4},{8,10},{10,8},{12,14},{14,12},{1,3},{3,1},... | collective-permute-start | bytes 393224 | tf_op jit(solution)/shard_map/ppermute | solution.py:246
  15.3 6.1 %collective-permute-start.7 = (bf16[128,768]{1,0:T(8,128)(2,1)S(1)}, bf16[128,768]{1,0:T(8,128)(2,1)S(1)}, u32[]{:S(2)}, u32[]{:S(2)}) collective-permute-start(bf16[128,768]{1,0:T(8,128)(2,1)S(1)} %broadcast_select_fusion), channel_id=1, source_target_pairs={{0,2},{2,0},{4,6},{6,4},{8,10},{10,8},{12,14},{14,12},{1,3},{3,1},... | collective-permute-start | bytes 589832 | tf_op jit(solution)/shard_map/ppermute | solution.py:246
  17.1 6.8 %collective-permute-start.4 = (bf16[128,512]{1,0:T(8,128)(2,1)S(1)}, bf16[128,512]{1,0:T(8,128)(2,1)S(1)}, u32[]{:S(2)}, u32[]{:S(2)}) collective-permute-start(bf16[128,512]{1,0:T(8,128)(2,1)S(1)} %collective-permute-done.3.refs_3_), channel_id=1, source_target_pairs={{0,4},{2,6},{4,8},{6,10},{8,12},{10,14},{12,0},{14,2},{1,5},{3,7},... | collective-permute-start | bytes 393224 | tf_op jit(solution)/shard_map/ppermute | solution.py:246
  18.6 9.4 %collective-permute-start.5 = (bf16[128,768]{1,0:T(8,128)(2,1)S(1)}, bf16[128,768]{1,0:T(8,128)(2,1)S(1)}, u32[]{:S(2)}, u32[]{:S(2)}) collective-permute-start(bf16[128,768]{1,0:T(8,128)(2,1)S(1)} %collective-permute-done.2.refs_4_), channel_id=1, source_target_pairs={{0,2},{2,0},{4,6},{6,4},{8,10},{10,8},{12,14},{14,12},{1,3},{3,1},... | collective-permute-start | bytes 589832 | tf_op jit(solution)/shard_map/ppermute | solution.py:246
  20.2 10.4 %collective-permute-start.6 = (bf16[128,768]{1,0:T(8,128)(2,1)S(1)}, bf16[128,768]{1,0:T(8,128)(2,1)S(1)}, u32[]{:S(2)}, u32[]{:S(2)}) collective-permute-start(bf16[128,768]{1,0:T(8,128)(2,1)S(1)} %broadcast_select_fusion.1), channel_id=1, source_target_pairs={{0,2},{2,4},{4,6},{6,8},{8,10},{10,12},{12,14},{14,0},{1,3},{3,5},... | collective-permute-start | bytes 589832 | tf_op jit(solution)/shard_map/ppermute | solution.py:246
  21.3 9.9 %collective-permute-start.9 = (bf16[128,768]{1,0:T(8,128)(2,1)S(1)}, bf16[128,768]{1,0:T(8,128)(2,1)S(1)}, u32[]{:S(2)}, u32[]{:S(2)}) collective-permute-start(bf16[128,768]{1,0:T(8,128)(2,1)S(1)} %collective-permute-done.7.refs_2_), channel_id=1, source_target_pairs={{0,4},{2,6},{4,8},{6,10},{8,12},{10,14},{12,0},{14,2},{1,5},{3,7},... | collective-permute-start | bytes 589832 | tf_op jit(solution)/shard_map/ppermute | solution.py:246
  22.1 10.0 %collective-permute-start.11 = (f32[384,128]{1,0:T(8,128)S(1)}, f32[384,128]{1,0:T(8,128)S(1)}, u32[]{:S(2)}, u32[]{:S(2)}) collective-permute-start(f32[384,128]{1,0:T(8,128)S(1)} %get-tuple-element.57), channel_id=1, source_target_pairs={{0,1},{1,0},{2,3},{3,2},{4,5},{5,4},{6,7},{7,6},{8,9},{9,8},{10,11... | collective-permute-start | bytes 589832 | tf_op jit(solution)/shard_map/ppermute | solution.py:246
  23.8 8.3 %collective-permute-start.12 = (f32[384,128]{1,0:T(8,128)S(1)}, f32[384,128]{1,0:T(8,128)S(1)}, u32[]{:S(2)}, u32[]{:S(2)}) collective-permute-start(f32[384,128]{1,0:T(8,128)S(1)} %get-tuple-element.58), channel_id=1, source_target_pairs={{0,1},{1,0},{2,3},{3,2},{4,5},{5,4},{6,7},{7,6},{8,9},{9,8},{10,11... | collective-permute-start | bytes 589832 | tf_op jit(solution)/shard_map/ppermute | solution.py:246
  31.1 2.1 %collective-permute-start.8 = (f32[384,128]{1,0:T(8,128)S(1)}, f32[384,128]{1,0:T(8,128)S(1)}, u32[]{:S(2)}, u32[]{:S(2)}) collective-permute-start(f32[384,128]{1,0:T(8,128)S(1)} %get-tuple-element.54), channel_id=1, source_target_pairs={{0,1},{1,0},{2,3},{3,2},{4,5},{5,4},{6,7},{7,6},{8,9},{9,8},{10,11... | collective-permute-start | bytes 589832 | tf_op jit(solution)/shard_map/ppermute | solution.py:246
  31.5 1.7 %collective-permute-start.10 = (f32[384,128]{1,0:T(8,128)S(1)}, f32[384,128]{1,0:T(8,128)S(1)}, u32[]{:S(2)}, u32[]{:S(2)}) collective-permute-start(f32[384,128]{1,0:T(8,128)S(1)} %shard_map.62), channel_id=1, source_target_pairs={{0,1},{1,0},{2,3},{3,2},{4,5},{5,4},{6,7},{7,6},{8,9},{9,8},{10,11... | collective-permute-start | bytes 589832 | tf_op jit(solution)/shard_map/ppermute | solution.py:246

commit v25 on v22

--- a/solution.py
+++ b/solution.py
@@ -13,7 +13,7 @@
 CHAIN = ("b0", "o1", "b2", "t1")
 ORDER = ("B0", "B1", "B2", "C0", "C1", "E0", "E1", "R2", "C2")
 TIES = {"C2": "C0"}
-EARLY = "C0"
+EARLY = "none"
 WEIGHT = 2
 CHUNKS = len(PARTS)
 VMEM_BYTES = 16 * 1024 * 1024

time: 33.6 us -> 33.6 us (level)
  transfers between devices with their start and end apart: 13 -> 13, of which waited for: 5 -> 6; matrix products, arithmetic and copies ran while one was open for 0% -> 0% of each run, Pallas kernels for 21% -> 21%
where the time goes in v25:
time: 33.6 us; the launch traced here: 33.4 us
  starting transfers between devices  14.4 us (43%)
  Pallas kernels  9.51 us (28%)
  waiting for transfers between devices  8.62 us (26%)
  between operations  0.78 us (2%)
    ppermute x13, starting transfers between devices, send(): return lax.ppermute(block, axis, route)  14.4 us
    ppermute x13, waiting for transfers between devices, send(): return lax.ppermute(block, axis, route)  8.62 us
    pallas_call x7, Pallas kernels, more_scores(): pl.pallas_call(functools.partial(scores_kernel, tuple(placed), fresh, loa...  6.33 us
    pallas_call x2, Pallas kernels, finish(): pl.pallas_call(functools.partial(finish_kernel, places), out_shape=pltpu....  1.6 us
    pallas_call x1, Pallas kernels, prepare(): pl.pallas_call(prepare_kernel, out_shape=shapes + [jax.ShapeDtypeStruct((...  1.58 us
  transfers between devices with their start and end apart: 13, of which 6 were waited for; matrix products, arithmetic and copies ran while one was open for 0% of the time, Pallas kernels for 21%

profile of v25, /device:TPU:0, one launch (start us, length us, event | category | flops | bytes accessed | tf_op | source)
XLA Modules:
  0.0 33.4 jit_solution(6861683390593809611)
XLA Ops:
  0.0 1.6 %shard_map.55 = (bf16[128,512]{1,0:T(8,128)(2,1)S(1)}, bf16[128,768]{1,0:T(8,128)(2,1)S(1)}, bf16[128,768]{1,0:T(8,128)(2,1)S(1)}, bf16[128,2048]{1,0:T(8,128)(2,1)S(1)}) custom-call(bf16[128,2048]{1,0:T(8,128)(2,1)} %queries.1, f32[1,2048]{1,0:T(1,128)} %bitcast.1, s32[1,128]{1,0:T(1,128)} %rank.1), custom_call_target="tpu_custom_call" | custom-call | flops 67108864 | bytes 1048576 | tf_op jit(solution)/shard_map/pallas_call | solution.py:80
  1.6 3.1 %collective-permute-start = (bf16[128,512]{1,0:T(8,128)(2,1)S(1)}, bf16[128,512]{1,0:T(8,128)(2,1)S(1)}, u32[]{:S(2)}, u32[]{:S(2)}) collective-permute-start(bf16[128,512]{1,0:T(8,128)(2,1)S(1)} %get-tuple-element.33), channel_id=1, source_target_pairs={{0,4},{2,6},{4,8},{6,10},{8,12},{10,14},{12,0},{14,2},{1,5},{3,7},... | collective-permute-start | bytes 393224 | tf_op jit(solution)/shard_map/ppermute | solution.py:246
  4.7 1.6 %collective-permute-start.1 = (bf16[128,768]{1,0:T(8,128)(2,1)S(1)}, bf16[128,768]{1,0:T(8,128)(2,1)S(1)}, u32[]{:S(2)}, u32[]{:S(2)}) collective-permute-start(bf16[128,768]{1,0:T(8,128)(2,1)S(1)} %get-tuple-element.34), channel_id=1, source_target_pairs={{0,4},{2,6},{4,8},{6,10},{8,12},{10,14},{12,0},{14,2},{1,5},{3,7},... | collective-permute-start | bytes 589832 | tf_op jit(solution)/shard_map/ppermute | solution.py:246
  6.2 1.6 %collective-permute-start.2 = (bf16[128,768]{1,0:T(8,128)(2,1)S(1)}, bf16[128,768]{1,0:T(8,128)(2,1)S(1)}, u32[]{:S(2)}, u32[]{:S(2)}) collective-permute-start(bf16[128,768]{1,0:T(8,128)(2,1)S(1)} %get-tuple-element.35), channel_id=1, source_target_pairs={{0,4},{2,6},{4,8},{6,10},{8,12},{10,14},{12,0},{14,2},{1,5},{3,7},... | collective-permute-start | bytes 589832 | tf_op jit(solution)/shard_map/ppermute | solution.py:246
  7.8 3.2 %collective-permute-done.refs_2_ = bf16[128,512]{1,0:T(8,128)(2,1)S(1)} collective-permute-done((bf16[128,512]{1,0:T(8,128)(2,1)S(1)}, bf16[128,512]{1,0:T(8,128)(2,1)S(1)}, u32[]{:S(2)}, u32[]{:S(2)}) %collective-permute-start) | collective-permute-done | bytes 131104 | tf_op jit(solution)/shard_map/ppermute | solution.py:246
  11.0 1.8 %collective-permute-start.3 = (bf16[128,512]{1,0:T(8,128)(2,1)S(1)}, bf16[128,512]{1,0:T(8,128)(2,1)S(1)}, u32[]{:S(2)}, u32[]{:S(2)}) collective-permute-start(bf16[128,512]{1,0:T(8,128)(2,1)S(1)} %broadcast_select_fusion.2), channel_id=1, source_target_pairs={{0,2},{2,0},{4,6},{6,4},{8,10},{10,8},{12,14},{14,12},{1,3},{3,1},... | collective-permute-start | bytes 393224 | tf_op jit(solution)/shard_map/ppermute | solution.py:246
  12.8 2.4 %collective-permute-done.1.refs_3_ = bf16[128,768]{1,0:T(8,128)(2,1)S(1)} collective-permute-done((bf16[128,768]{1,0:T(8,128)(2,1)S(1)}, bf16[128,768]{1,0:T(8,128)(2,1)S(1)}, u32[]{:S(2)}, u32[]{:S(2)}) %collective-permute-start.1) | collective-permute-done | bytes 196640 | tf_op jit(solution)/shard_map/ppermute | solution.py:246
  15.3 1.8 %collective-permute-start.7 = (bf16[128,768]{1,0:T(8,128)(2,1)S(1)}, bf16[128,768]{1,0:T(8,128)(2,1)S(1)}, u32[]{:S(2)}, u32[]{:S(2)}) collective-permute-start(bf16[128,768]{1,0:T(8,128)(2,1)S(1)} %broadcast_select_fusion), channel_id=1, source_target_pairs={{0,2},{2,0},{4,6},{6,4},{8,10},{10,8},{12,14},{14,12},{1,3},{3,1},... | collective-permute-start | bytes 589832 | tf_op jit(solution)/shard_map/ppermute | solution.py:246
  17.1 1.6 %collective-permute-done.2.refs_4_ = bf16[128,768]{1,0:T(8,128)(2,1)S(1)} collective-permute-done((bf16[128,768]{1,0:T(8,128)(2,1)S(1)}, bf16[128,768]{1,0:T(8,128)(2,1)S(1)}, u32[]{:S(2)}, u32[]{:S(2)}) %collective-permute-start.2) | collective-permute-done | bytes 196640 | tf_op jit(solution)/shard_map/ppermute | solution.py:246
  18.6 1.7 %collective-permute-start.6 = (bf16[128,768]{1,0:T(8,128)(2,1)S(1)}, bf16[128,768]{1,0:T(8,128)(2,1)S(1)}, u32[]{:S(2)}, u32[]{:S(2)}) collective-permute-start(bf16[128,768]{1,0:T(8,128)(2,1)S(1)} %broadcast_select_fusion.1), channel_id=1, source_target_pairs={{0,2},{2,4},{4,6},{6,8},{8,10},{10,12},{12,14},{14,0},{1,3},{3,5},... | collective-permute-start | bytes 589832 | tf_op jit(solution)/shard_map/ppermute | solution.py:246
  20.5 0.6 %collective-permute-done.7.refs_2_ = bf16[128,768]{1,0:T(8,128)(2,1)S(1)} collective-permute-done((bf16[128,768]{1,0:T(8,128)(2,1)S(1)}, bf16[128,768]{1,0:T(8,128)(2,1)S(1)}, u32[]{:S(2)}, u32[]{:S(2)}) %collective-permute-start.7) | collective-permute-done | bytes 196640 | tf_op jit(solution)/shard_map/ppermute | solution.py:246
  21.1 1.5 %collective-permute-start.9 = (bf16[128,768]{1,0:T(8,128)(2,1)S(1)}, bf16[128,768]{1,0:T(8,128)(2,1)S(1)}, u32[]{:S(2)}, u32[]{:S(2)}) collective-permute-start(bf16[128,768]{1,0:T(8,128)(2,1)S(1)} %collective-permute-done.7.refs_2_), channel_id=1, source_target_pairs={{0,4},{2,6},{4,8},{6,10},{8,12},{10,14},{12,0},{14,2},{1,5},{3,7},... | collective-permute-start | bytes 589832 | tf_op jit(solution)/shard_map/ppermute | solution.py:246
  22.6 3.3 %shard_map.56 = (f32[384,128]{1,0:T(8,128)S(1)}, f32[384,128]{1,0:T(8,128)S(1)}, bf16[384,2048]{1,0:T(8,128)(2,1)S(1)}, bf16[384,2048]{1,0:T(8,128)(2,1)S(1)}) custom-call(bf16[768,2048]{1,0:T(8,128)(2,1)} %refs_0_.1, bf16[128,2048]{1,0:T(8,128)(2,1)S(1)} %get-tuple-element.30.refs_1_), custom_call_target="tpu_custom_call" | custom-call | flops 402653184 | bytes 393216 | tf_op jit(solution)/shard_map/pallas_call | solution.py:181
  26.7 1.0 %shard_map.57 = (f32[384,128]{1,0:T(8,128)S(1)}, f32[384,128]{1,0:T(8,128)S(1)}) custom-call(bf16[384,2048]{1,0:T(8,128)(2,1)S(1)} %get-tuple-element.31.refs_0_.refs_1_, bf16[384,2048]{1,0:T(8,128)(2,1)S(1)} %get-tuple-element.32.refs_1_.refs_2_, bf16[128,512]{1,0:T(8,128)(2,1)S(1)} %collective-permute-done.refs_2_, ...), custom_call_target="tpu_custom_call" | custom-call | flops 402653184 | bytes 393216 | tf_op jit(solution)/shard_map/pallas_call | solution.py:181
  27.7 0.6 %collective-permute-start.12 = (f32[384,128]{1,0:T(8,128)S(1)}, f32[384,128]{1,0:T(8,128)S(1)}, u32[]{:S(2)}, u32[]{:S(2)}) collective-permute-start(f32[384,128]{1,0:T(8,128)S(1)} %get-tuple-element.54), channel_id=1, source_target_pairs={{0,1},{1,0},{2,3},{3,2},{4,5},{5,4},{6,7},{7,6},{8,9},{9,8},{10,11... | collective-permute-start | bytes 589832 | tf_op jit(solution)/shard_map/ppermute | solution.py:246
  28.2 0.4 %shard_map.58 = (f32[384,128]{1,0:T(8,128)S(1)}, f32[384,128]{1,0:T(8,128)S(1)}, f32[384,128]{1,0:T(8,128)S(1)}, f32[384,128]{1,0:T(8,128)S(1)}, s32[8,128]{1,0:T(8,128)S(1)}) custom-call(s32[1]{0:T(128)S(6)} %copy.8.refs_0_, bf16[384,2048]{1,0:T(8,128)(2,1)S(1)} %get-tuple-element.31.refs_0_.refs_1_, ...), custom_call_target="tpu_custom_call" | custom-call | flops 402653184 | bytes 1572864 | tf_op jit(solution)/shard_map/pallas_call | solution.py:181
  28.6 0.5 %shard_map.59 = (f32[384,128]{1,0:T(8,128)S(1)}, f32[384,128]{1,0:T(8,128)S(1)}, f32[384,128]{1,0:T(8,128)S(1)}, f32[384,128]{1,0:T(8,128)S(1)}) custom-call(bf16[384,2048]{1,0:T(8,128)(2,1)S(1)} %get-tuple-element.31.refs_0_.refs_1_, bf16[384,2048]{1,0:T(8,128)(2,1)S(1)} %get-tuple-element.32.refs_1_.refs_2_, ...), custom_call_target="tpu_custom_call" | custom-call | flops 301989888 | bytes 1572864 | tf_op jit(solution)/shard_map/pallas_call | solution.py:181
  29.3 0.6 %collective-permute-done.5.refs_2_ = bf16[128,768]{1,0:T(8,128)(2,1)S(1)} collective-permute-done((bf16[128,768]{1,0:T(8,128)(2,1)S(1)}, bf16[128,768]{1,0:T(8,128)(2,1)S(1)}, u32[]{:S(2)}, u32[]{:S(2)}) %collective-permute-start.5) | collective-permute-done | bytes 196640 | tf_op jit(solution)/shard_map/ppermute | solution.py:246
  30.0 0.5 %shard_map.60 = (f32[384,128]{1,0:T(8,128)S(1)}, f32[384,128]{1,0:T(8,128)S(1)}, f32[384,128]{1,0:T(8,128)S(1)}, f32[384,128]{1,0:T(8,128)S(1)}) custom-call(bf16[384,2048]{1,0:T(8,128)(2,1)S(1)} %get-tuple-element.31.refs_0_.refs_1_, bf16[384,2048]{1,0:T(8,128)(2,1)S(1)} %get-tuple-element.32.refs_1_.refs_2_, ...), custom_call_target="tpu_custom_call" | custom-call | flops 603979776 | bytes 1572864 | tf_op jit(solution)/shard_map/pallas_call | solution.py:181
  30.6 0.3 shard_map.62
  30.9 0.5 %collective-permute-start.10 = (f32[384,128]{1,0:T(8,128)S(1)}, f32[384,128]{1,0:T(8,128)S(1)}, u32[]{:S(2)}, u32[]{:S(2)}) collective-permute-start(f32[384,128]{1,0:T(8,128)S(1)} %shard_map.62), channel_id=1, source_target_pairs={{0,1},{1,0},{2,3},{3,2},{4,5},{5,4},{6,7},{7,6},{8,9},{9,8},{10,11... | collective-permute-start | bytes 589832 | tf_op jit(solution)/shard_map/ppermute | solution.py:246
  31.5 0.8 %shard_map.63.refs_4_ = f32[384,512]{1,0:T(8,128)} custom-call(s32[8,128]{1,0:T(8,128)S(1)} %get-tuple-element.38.limit, f32[384,128]{1,0:T(8,128)S(1)} %get-tuple-element.52.refs_0_, f32[384,128]{1,0:T(8,128)S(1)} %collective-permute-done.11.refs_1_, f32[384,128]{1,0:T(8,128)S(1)} %get-tuple-element.36.refs_2_, f32[384,128]{1,0:T(8,128)S(1)} %collective-permute-done.12.refs_3_), custom_call_target="tpu_custom_call" | custom-call | flops 98304 | bytes 1179648 | tf_op jit(solution)/shard_map/pallas_call | solution.py:216
  32.3 0.3 shard_map.61.refs_2_
  32.6 0.8 %shard_map.64 = f32[384,512]{1,0:T(8,128)} custom-call(s32[8,128]{1,0:T(8,128)S(1)} %get-tuple-element.38.limit, f32[384,128]{1,0:T(8,128)S(1)} %get-tuple-element.48.refs_0_, f32[384,128]{1,0:T(8,128)S(1)} %collective-permute-done.8.refs_1_, f32[384,128]{1,0:T(8,128)S(1)} %shard_map.61.refs_2_, ...), custom_call_target="tpu_custom_call", output_to_operand_aliasing={{}: (5, {})} | custom-call | flops 98304 | bytes 1179648 | tf_op jit(solution)/shard_map/pallas_call | solution.py:216
  (15 shorter events, 0.6 us)
Async XLA Ops:
  1.6 9.4 %collective-permute-start = (bf16[128,512]{1,0:T(8,128)(2,1)S(1)}, bf16[128,512]{1,0:T(8,128)(2,1)S(1)}, u32[]{:S(2)}, u32[]{:S(2)}) collective-permute-start(bf16[128,512]{1,0:T(8,128)(2,1)S(1)} %get-tuple-element.33), channel_id=1, source_target_pairs={{0,4},{2,6},{4,8},{6,10},{8,12},{10,14},{12,0},{14,2},{1,5},{3,7},... | collective-permute-start | bytes 393224 | tf_op jit(solution)/shard_map/ppermute | solution.py:246
  4.7 10.6 %collective-permute-start.1 = (bf16[128,768]{1,0:T(8,128)(2,1)S(1)}, bf16[128,768]{1,0:T(8,128)(2,1)S(1)}, u32[]{:S(2)}, u32[]{:S(2)}) collective-permute-start(bf16[128,768]{1,0:T(8,128)(2,1)S(1)} %get-tuple-element.34), channel_id=1, source_target_pairs={{0,4},{2,6},{4,8},{6,10},{8,12},{10,14},{12,0},{14,2},{1,5},{3,7},... | collective-permute-start | bytes 589832 | tf_op jit(solution)/shard_map/ppermute | solution.py:246
  6.2 12.4 %collective-permute-start.2 = (bf16[128,768]{1,0:T(8,128)(2,1)S(1)}, bf16[128,768]{1,0:T(8,128)(2,1)S(1)}, u32[]{:S(2)}, u32[]{:S(2)}) collective-permute-start(bf16[128,768]{1,0:T(8,128)(2,1)S(1)} %get-tuple-element.35), channel_id=1, source_target_pairs={{0,4},{2,6},{4,8},{6,10},{8,12},{10,14},{12,0},{14,2},{1,5},{3,7},... | collective-permute-start | bytes 589832 | tf_op jit(solution)/shard_map/ppermute | solution.py:246
  11.0 6.0 %collective-permute-start.3 = (bf16[128,512]{1,0:T(8,128)(2,1)S(1)}, bf16[128,512]{1,0:T(8,128)(2,1)S(1)}, u32[]{:S(2)}, u32[]{:S(2)}) collective-permute-start(bf16[128,512]{1,0:T(8,128)(2,1)S(1)} %broadcast_select_fusion.2), channel_id=1, source_target_pairs={{0,2},{2,0},{4,6},{6,4},{8,10},{10,8},{12,14},{14,12},{1,3},{3,1},... | collective-permute-start | bytes 393224 | tf_op jit(solution)/shard_map/ppermute | solution.py:246
  15.3 5.9 %collective-permute-start.7 = (bf16[128,768]{1,0:T(8,128)(2,1)S(1)}, bf16[128,768]{1,0:T(8,128)(2,1)S(1)}, u32[]{:S(2)}, u32[]{:S(2)}) collective-permute-start(bf16[128,768]{1,0:T(8,128)(2,1)S(1)} %broadcast_select_fusion), channel_id=1, source_target_pairs={{0,2},{2,0},{4,6},{6,4},{8,10},{10,8},{12,14},{14,12},{1,3},{3,1},... | collective-permute-start | bytes 589832 | tf_op jit(solution)/shard_map/ppermute | solution.py:246
  17.1 10.6 %collective-permute-start.4 = (bf16[128,512]{1,0:T(8,128)(2,1)S(1)}, bf16[128,512]{1,0:T(8,128)(2,1)S(1)}, u32[]{:S(2)}, u32[]{:S(2)}) collective-permute-start(bf16[128,512]{1,0:T(8,128)(2,1)S(1)} %collective-permute-done.3.refs_3_), channel_id=1, source_target_pairs={{0,4},{2,6},{4,8},{6,10},{8,12},{10,14},{12,0},{14,2},{1,5},{3,7},... | collective-permute-start | bytes 393224 | tf_op jit(solution)/shard_map/ppermute | solution.py:246
  18.6 10.7 %collective-permute-start.6 = (bf16[128,768]{1,0:T(8,128)(2,1)S(1)}, bf16[128,768]{1,0:T(8,128)(2,1)S(1)}, u32[]{:S(2)}, u32[]{:S(2)}) collective-permute-start(bf16[128,768]{1,0:T(8,128)(2,1)S(1)} %broadcast_select_fusion.1), channel_id=1, source_target_pairs={{0,2},{2,4},{4,6},{6,8},{8,10},{10,12},{12,14},{14,0},{1,3},{3,5},... | collective-permute-start | bytes 589832 | tf_op jit(solution)/shard_map/ppermute | solution.py:246
  20.3 9.7 %collective-permute-start.5 = (bf16[128,768]{1,0:T(8,128)(2,1)S(1)}, bf16[128,768]{1,0:T(8,128)(2,1)S(1)}, u32[]{:S(2)}, u32[]{:S(2)}) collective-permute-start(bf16[128,768]{1,0:T(8,128)(2,1)S(1)} %collective-permute-done.2.refs_4_), channel_id=1, source_target_pairs={{0,2},{2,0},{4,6},{6,4},{8,10},{10,8},{12,14},{14,12},{1,3},{3,1},... | collective-permute-start | bytes 589832 | tf_op jit(solution)/shard_map/ppermute | solution.py:246
  21.1 9.5 %collective-permute-start.9 = (bf16[128,768]{1,0:T(8,128)(2,1)S(1)}, bf16[128,768]{1,0:T(8,128)(2,1)S(1)}, u32[]{:S(2)}, u32[]{:S(2)}) collective-permute-start(bf16[128,768]{1,0:T(8,128)(2,1)S(1)} %collective-permute-done.7.refs_2_), channel_id=1, source_target_pairs={{0,4},{2,6},{4,8},{6,10},{8,12},{10,14},{12,0},{14,2},{1,5},{3,7},... | collective-permute-start | bytes 589832 | tf_op jit(solution)/shard_map/ppermute | solution.py:246
  26.0 5.5 %collective-permute-start.11 = (f32[384,128]{1,0:T(8,128)S(1)}, f32[384,128]{1,0:T(8,128)S(1)}, u32[]{:S(2)}, u32[]{:S(2)}) collective-permute-start(f32[384,128]{1,0:T(8,128)S(1)} %get-tuple-element.53), channel_id=1, source_target_pairs={{0,1},{1,0},{2,3},{3,2},{4,5},{5,4},{6,7},{7,6},{8,9},{9,8},{10,11... | collective-permute-start | bytes 589832 | tf_op jit(solution)/shard_map/ppermute | solution.py:246
  27.7 3.8 %collective-permute-start.12 = (f32[384,128]{1,0:T(8,128)S(1)}, f32[384,128]{1,0:T(8,128)S(1)}, u32[]{:S(2)}, u32[]{:S(2)}) collective-permute-start(f32[384,128]{1,0:T(8,128)S(1)} %get-tuple-element.54), channel_id=1, source_target_pairs={{0,1},{1,0},{2,3},{3,2},{4,5},{5,4},{6,7},{7,6},{8,9},{9,8},{10,11... | collective-permute-start | bytes 589832 | tf_op jit(solution)/shard_map/ppermute | solution.py:246
  30.5 2.1 %collective-permute-start.8 = (f32[384,128]{1,0:T(8,128)S(1)}, f32[384,128]{1,0:T(8,128)S(1)}, u32[]{:S(2)}, u32[]{:S(2)}) collective-permute-start(f32[384,128]{1,0:T(8,128)S(1)} %get-tuple-element.49), channel_id=1, source_target_pairs={{0,1},{1,0},{2,3},{3,2},{4,5},{5,4},{6,7},{7,6},{8,9},{9,8},{10,11... | collective-permute-start | bytes 589832 | tf_op jit(solution)/shard_map/ppermute | solution.py:246
  30.9 1.7 %collective-permute-start.10 = (f32[384,128]{1,0:T(8,128)S(1)}, f32[384,128]{1,0:T(8,128)S(1)}, u32[]{:S(2)}, u32[]{:S(2)}) collective-permute-start(f32[384,128]{1,0:T(8,128)S(1)} %shard_map.62), channel_id=1, source_target_pairs={{0,1},{1,0},{2,3},{3,2},{4,5},{5,4},{6,7},{7,6},{8,9},{9,8},{10,11... | collective-permute-start | bytes 589832 | tf_op jit(solution)/shard_map/ppermute | solution.py:246

commit v26 on v22

--- a/solution.py
+++ b/solution.py
@@ -58,12 +58,12 @@
     loads.append(pltpu.make_async_copy(precond, scale, arrived.at[CHUNKS + 1]))
     for n, cut in enumerate(cuts):
         loads.append(pltpu.make_async_copy(queries.at[:, cut], held.at[:, cut], arrived.at[n]))
-    for load in loads:
+    for load in loads[2:] + loads[:2]:
         load.start()
     loads[0].wait()
-    loads[1].wait()
     positions = lax.broadcasted_iota(jnp.int32, (rows, rows), 0)
     placing = (positions == places[...]).astype(jnp.bfloat16)
+    loads[1].wait()
     for n, cut in enumerate(cuts):
         loads[2 + n].wait()
         pre = (held[:, cut].astype(jnp.float32) * scale[:, cut]).astype(jnp.bfloat16)

time: 33.6 us -> 33.6 us (level)
  no operation moved by 1% of the time
where the time goes in v26:
time: 33.6 us; the launch traced here: 33.4 us
  starting transfers between devices  14.1 us (42%)
  Pallas kernels  9.54 us (28%)
  waiting for transfers between devices  8.94 us (27%)
  between operations  0.79 us (2%)
    ppermute x13, starting transfers between devices, send(): return lax.ppermute(block, axis, route)  14.1 us
    ppermute x13, waiting for transfers between devices, send(): return lax.ppermute(block, axis, route)  8.94 us
    pallas_call x7, Pallas kernels, more_scores(): pl.pallas_call(functools.partial(scores_kernel, tuple(placed), fresh, loa...  6.32 us
    pallas_call x1, Pallas kernels, prepare(): pl.pallas_call(prepare_kernel, out_shape=shapes + [jax.ShapeDtypeStruct((...  1.62 us
    pallas_call x2, Pallas kernels, finish(): pl.pallas_call(functools.partial(finish_kernel, places), out_shape=pltpu....  1.6 us
  transfers between devices with their start and end apart: 13, of which 5 were waited for; matrix products, arithmetic and copies ran while one was open for 0% of the time, Pallas kernels for 21%

profile of v26, /device:TPU:0, one launch (start us, length us, event | category | flops | bytes accessed | tf_op | source)
XLA Modules:
  0.0 33.4 jit_solution(1137789068242320346)
XLA Ops:
  0.0 1.6 %shard_map.55 = (bf16[128,512]{1,0:T(8,128)(2,1)S(1)}, bf16[128,768]{1,0:T(8,128)(2,1)S(1)}, bf16[128,768]{1,0:T(8,128)(2,1)S(1)}, bf16[128,2048]{1,0:T(8,128)(2,1)S(1)}) custom-call(bf16[128,2048]{1,0:T(8,128)(2,1)} %queries.1, f32[1,2048]{1,0:T(1,128)} %bitcast.1, s32[1,128]{1,0:T(1,128)} %rank.1), custom_call_target="tpu_custom_call" | custom-call | flops 67108864 | bytes 1048576 | tf_op jit(solution)/shard_map/pallas_call | solution.py:80
  1.6 3.1 %collective-permute-start = (bf16[128,512]{1,0:T(8,128)(2,1)S(1)}, bf16[128,512]{1,0:T(8,128)(2,1)S(1)}, u32[]{:S(2)}, u32[]{:S(2)}) collective-permute-start(bf16[128,512]{1,0:T(8,128)(2,1)S(1)} %get-tuple-element.34), channel_id=1, source_target_pairs={{0,4},{2,6},{4,8},{6,10},{8,12},{10,14},{12,0},{14,2},{1,5},{3,7},... | collective-permute-start | bytes 393224 | tf_op jit(solution)/shard_map/ppermute | solution.py:246
  4.7 1.6 %collective-permute-start.1 = (bf16[128,768]{1,0:T(8,128)(2,1)S(1)}, bf16[128,768]{1,0:T(8,128)(2,1)S(1)}, u32[]{:S(2)}, u32[]{:S(2)}) collective-permute-start(bf16[128,768]{1,0:T(8,128)(2,1)S(1)} %get-tuple-element.35), channel_id=1, source_target_pairs={{0,4},{2,6},{4,8},{6,10},{8,12},{10,14},{12,0},{14,2},{1,5},{3,7},... | collective-permute-start | bytes 589832 | tf_op jit(solution)/shard_map/ppermute | solution.py:246
  6.3 1.6 %collective-permute-start.2 = (bf16[128,768]{1,0:T(8,128)(2,1)S(1)}, bf16[128,768]{1,0:T(8,128)(2,1)S(1)}, u32[]{:S(2)}, u32[]{:S(2)}) collective-permute-start(bf16[128,768]{1,0:T(8,128)(2,1)S(1)} %get-tuple-element.36), channel_id=1, source_target_pairs={{0,4},{2,6},{4,8},{6,10},{8,12},{10,14},{12,0},{14,2},{1,5},{3,7},... | collective-permute-start | bytes 589832 | tf_op jit(solution)/shard_map/ppermute | solution.py:246
  7.9 3.3 %shard_map.56 = (f32[384,128]{1,0:T(8,128)S(1)}, f32[384,128]{1,0:T(8,128)S(1)}, bf16[384,2048]{1,0:T(8,128)(2,1)S(1)}, bf16[384,2048]{1,0:T(8,128)(2,1)S(1)}) custom-call(bf16[768,2048]{1,0:T(8,128)(2,1)} %refs_0_.1, bf16[128,2048]{1,0:T(8,128)(2,1)S(1)} %get-tuple-element.31.refs_1_), custom_call_target="tpu_custom_call" | custom-call | flops 402653184 | bytes 393216 | tf_op jit(solution)/shard_map/pallas_call | solution.py:181
  11.2 1.6 %collective-permute-start.3 = (bf16[128,512]{1,0:T(8,128)(2,1)S(1)}, bf16[128,512]{1,0:T(8,128)(2,1)S(1)}, u32[]{:S(2)}, u32[]{:S(2)}) collective-permute-start(bf16[128,512]{1,0:T(8,128)(2,1)S(1)} %broadcast_select_fusion.2), channel_id=1, source_target_pairs={{0,2},{2,0},{4,6},{6,4},{8,10},{10,8},{12,14},{14,12},{1,3},{3,1},... | collective-permute-start | bytes 393224 | tf_op jit(solution)/shard_map/ppermute | solution.py:246
  12.9 2.4 %collective-permute-done.1.refs_3_ = bf16[128,768]{1,0:T(8,128)(2,1)S(1)} collective-permute-done((bf16[128,768]{1,0:T(8,128)(2,1)S(1)}, bf16[128,768]{1,0:T(8,128)(2,1)S(1)}, u32[]{:S(2)}, u32[]{:S(2)}) %collective-permute-start.1) | collective-permute-done | bytes 196640 | tf_op jit(solution)/shard_map/ppermute | solution.py:246
  15.3 1.8 %collective-permute-start.7 = (bf16[128,768]{1,0:T(8,128)(2,1)S(1)}, bf16[128,768]{1,0:T(8,128)(2,1)S(1)}, u32[]{:S(2)}, u32[]{:S(2)}) collective-permute-start(bf16[128,768]{1,0:T(8,128)(2,1)S(1)} %broadcast_select_fusion), channel_id=1, source_target_pairs={{0,2},{2,0},{4,6},{6,4},{8,10},{10,8},{12,14},{14,12},{1,3},{3,1},... | collective-permute-start | bytes 589832 | tf_op jit(solution)/shard_map/ppermute | solution.py:246
  17.1 1.5 %collective-permute-done.2.refs_4_ = bf16[128,768]{1,0:T(8,128)(2,1)S(1)} collective-permute-done((bf16[128,768]{1,0:T(8,128)(2,1)S(1)}, bf16[128,768]{1,0:T(8,128)(2,1)S(1)}, u32[]{:S(2)}, u32[]{:S(2)}) %collective-permute-start.2) | collective-permute-done | bytes 196640 | tf_op jit(solution)/shard_map/ppermute | solution.py:246
  18.7 1.5 %collective-permute-start.6 = (bf16[128,768]{1,0:T(8,128)(2,1)S(1)}, bf16[128,768]{1,0:T(8,128)(2,1)S(1)}, u32[]{:S(2)}, u32[]{:S(2)}) collective-permute-start(bf16[128,768]{1,0:T(8,128)(2,1)S(1)} %broadcast_select_fusion.1), channel_id=1, source_target_pairs={{0,2},{2,4},{4,6},{6,8},{8,10},{10,12},{12,14},{14,0},{1,3},{3,5},... | collective-permute-start | bytes 589832 | tf_op jit(solution)/shard_map/ppermute | solution.py:246
  20.2 0.3 collective-permute-start.5
  20.5 0.6 %collective-permute-done.7.refs_2_ = bf16[128,768]{1,0:T(8,128)(2,1)S(1)} collective-permute-done((bf16[128,768]{1,0:T(8,128)(2,1)S(1)}, bf16[128,768]{1,0:T(8,128)(2,1)S(1)}, u32[]{:S(2)}, u32[]{:S(2)}) %collective-permute-start.7) | collective-permute-done | bytes 196640 | tf_op jit(solution)/shard_map/ppermute | solution.py:246
  21.2 1.4 %collective-permute-start.9 = (bf16[128,768]{1,0:T(8,128)(2,1)S(1)}, bf16[128,768]{1,0:T(8,128)(2,1)S(1)}, u32[]{:S(2)}, u32[]{:S(2)}) collective-permute-start(bf16[128,768]{1,0:T(8,128)(2,1)S(1)} %collective-permute-done.7.refs_2_), channel_id=1, source_target_pairs={{0,4},{2,6},{4,8},{6,10},{8,12},{10,14},{12,0},{14,2},{1,5},{3,7},... | collective-permute-start | bytes 589832 | tf_op jit(solution)/shard_map/ppermute | solution.py:246
  23.2 1.0 %shard_map.57 = (f32[384,128]{1,0:T(8,128)S(1)}, f32[384,128]{1,0:T(8,128)S(1)}) custom-call(bf16[384,2048]{1,0:T(8,128)(2,1)S(1)} %get-tuple-element.32.refs_0_.refs_1_, bf16[384,2048]{1,0:T(8,128)(2,1)S(1)} %get-tuple-element.33.refs_1_.refs_2_, bf16[128,512]{1,0:T(8,128)(2,1)S(1)} %collective-permute-done.refs_2_, ...), custom_call_target="tpu_custom_call" | custom-call | flops 402653184 | bytes 393216 | tf_op jit(solution)/shard_map/pallas_call | solution.py:181
  24.2 0.6 %collective-permute-start.12 = (f32[384,128]{1,0:T(8,128)S(1)}, f32[384,128]{1,0:T(8,128)S(1)}, u32[]{:S(2)}, u32[]{:S(2)}) collective-permute-start(f32[384,128]{1,0:T(8,128)S(1)} %get-tuple-element.56), channel_id=1, source_target_pairs={{0,1},{1,0},{2,3},{3,2},{4,5},{5,4},{6,7},{7,6},{8,9},{9,8},{10,11... | collective-permute-start | bytes 589832 | tf_op jit(solution)/shard_map/ppermute | solution.py:246
  24.8 0.4 %shard_map.58 = (f32[384,128]{1,0:T(8,128)S(1)}, f32[384,128]{1,0:T(8,128)S(1)}, f32[384,128]{1,0:T(8,128)S(1)}, f32[384,128]{1,0:T(8,128)S(1)}, s32[8,128]{1,0:T(8,128)S(1)}) custom-call(s32[1]{0:T(128)S(6)} %copy.8.refs_0_, bf16[384,2048]{1,0:T(8,128)(2,1)S(1)} %get-tuple-element.32.refs_0_.refs_1_, ...), custom_call_target="tpu_custom_call" | custom-call | flops 402653184 | bytes 1572864 | tf_op jit(solution)/shard_map/pallas_call | solution.py:181
  25.2 0.5 %shard_map.59 = (f32[384,128]{1,0:T(8,128)S(1)}, f32[384,128]{1,0:T(8,128)S(1)}, f32[384,128]{1,0:T(8,128)S(1)}, f32[384,128]{1,0:T(8,128)S(1)}) custom-call(bf16[384,2048]{1,0:T(8,128)(2,1)S(1)} %get-tuple-element.32.refs_0_.refs_1_, bf16[384,2048]{1,0:T(8,128)(2,1)S(1)} %get-tuple-element.33.refs_1_.refs_2_, ...), custom_call_target="tpu_custom_call" | custom-call | flops 301989888 | bytes 1572864 | tf_op jit(solution)/shard_map/pallas_call | solution.py:181
  25.6 3.8 %collective-permute-done.6.refs_3_ = bf16[128,768]{1,0:T(8,128)(2,1)S(1)} collective-permute-done((bf16[128,768]{1,0:T(8,128)(2,1)S(1)}, bf16[128,768]{1,0:T(8,128)(2,1)S(1)}, u32[]{:S(2)}, u32[]{:S(2)}) %collective-permute-start.6) | collective-permute-done | bytes 196640 | tf_op jit(solution)/shard_map/ppermute | solution.py:246
  29.4 0.6 %collective-permute-done.5.refs_2_ = bf16[128,768]{1,0:T(8,128)(2,1)S(1)} collective-permute-done((bf16[128,768]{1,0:T(8,128)(2,1)S(1)}, bf16[128,768]{1,0:T(8,128)(2,1)S(1)}, u32[]{:S(2)}, u32[]{:S(2)}) %collective-permute-start.5) | collective-permute-done | bytes 196640 | tf_op jit(solution)/shard_map/ppermute | solution.py:246
  30.0 0.5 %shard_map.60 = (f32[384,128]{1,0:T(8,128)S(1)}, f32[384,128]{1,0:T(8,128)S(1)}, f32[384,128]{1,0:T(8,128)S(1)}, f32[384,128]{1,0:T(8,128)S(1)}) custom-call(bf16[384,2048]{1,0:T(8,128)(2,1)S(1)} %get-tuple-element.32.refs_0_.refs_1_, bf16[384,2048]{1,0:T(8,128)(2,1)S(1)} %get-tuple-element.33.refs_1_.refs_2_, ...), custom_call_target="tpu_custom_call" | custom-call | flops 603979776 | bytes 1572864 | tf_op jit(solution)/shard_map/pallas_call | solution.py:181
  30.6 0.3 shard_map.62
  30.9 0.5 %collective-permute-start.10 = (f32[384,128]{1,0:T(8,128)S(1)}, f32[384,128]{1,0:T(8,128)S(1)}, u32[]{:S(2)}, u32[]{:S(2)}) collective-permute-start(f32[384,128]{1,0:T(8,128)S(1)} %shard_map.62), channel_id=1, source_target_pairs={{0,1},{1,0},{2,3},{3,2},{4,5},{5,4},{6,7},{7,6},{8,9},{9,8},{10,11... | collective-permute-start | bytes 589832 | tf_op jit(solution)/shard_map/ppermute | solution.py:246
  31.5 0.8 %shard_map.63.refs_4_ = f32[384,512]{1,0:T(8,128)} custom-call(s32[8,128]{1,0:T(8,128)S(1)} %get-tuple-element.41.limit, f32[384,128]{1,0:T(8,128)S(1)} %get-tuple-element.39.refs_0_, f32[384,128]{1,0:T(8,128)S(1)} %collective-permute-done.11.refs_1_, f32[384,128]{1,0:T(8,128)S(1)} %get-tuple-element.37.refs_2_, f32[384,128]{1,0:T(8,128)S(1)} %collective-permute-done.12.refs_3_), custom_call_target="tpu_custom_call" | custom-call | flops 98304 | bytes 1179648 | tf_op jit(solution)/shard_map/pallas_call | solution.py:216
  32.6 0.8 %shard_map.64 = f32[384,512]{1,0:T(8,128)} custom-call(s32[8,128]{1,0:T(8,128)S(1)} %get-tuple-element.41.limit, f32[384,128]{1,0:T(8,128)S(1)} %get-tuple-element.51.refs_0_, f32[384,128]{1,0:T(8,128)S(1)} %collective-permute-done.8.refs_1_, f32[384,128]{1,0:T(8,128)S(1)} %shard_map.61.refs_2_, ...), custom_call_target="tpu_custom_call", output_to_operand_aliasing={{}: (5, {})} | custom-call | flops 98304 | bytes 1179648 | tf_op jit(solution)/shard_map/pallas_call | solution.py:216
  (15 shorter events, 0.5 us)
Async XLA Ops:
  1.6 9.6 %collective-permute-start = (bf16[128,512]{1,0:T(8,128)(2,1)S(1)}, bf16[128,512]{1,0:T(8,128)(2,1)S(1)}, u32[]{:S(2)}, u32[]{:S(2)}) collective-permute-start(bf16[128,512]{1,0:T(8,128)(2,1)S(1)} %get-tuple-element.34), channel_id=1, source_target_pairs={{0,4},{2,6},{4,8},{6,10},{8,12},{10,14},{12,0},{14,2},{1,5},{3,7},... | collective-permute-start | bytes 393224 | tf_op jit(solution)/shard_map/ppermute | solution.py:246
  4.7 10.6 %collective-permute-start.1 = (bf16[128,768]{1,0:T(8,128)(2,1)S(1)}, bf16[128,768]{1,0:T(8,128)(2,1)S(1)}, u32[]{:S(2)}, u32[]{:S(2)}) collective-permute-start(bf16[128,768]{1,0:T(8,128)(2,1)S(1)} %get-tuple-element.35), channel_id=1, source_target_pairs={{0,4},{2,6},{4,8},{6,10},{8,12},{10,14},{12,0},{14,2},{1,5},{3,7},... | collective-permute-start | bytes 589832 | tf_op jit(solution)/shard_map/ppermute | solution.py:246
  6.3 12.4 %collective-permute-start.2 = (bf16[128,768]{1,0:T(8,128)(2,1)S(1)}, bf16[128,768]{1,0:T(8,128)(2,1)S(1)}, u32[]{:S(2)}, u32[]{:S(2)}) collective-permute-start(bf16[128,768]{1,0:T(8,128)(2,1)S(1)} %get-tuple-element.36), channel_id=1, source_target_pairs={{0,4},{2,6},{4,8},{6,10},{8,12},{10,14},{12,0},{14,2},{1,5},{3,7},... | collective-permute-start | bytes 589832 | tf_op jit(solution)/shard_map/ppermute | solution.py:246
  11.2 5.9 %collective-permute-start.3 = (bf16[128,512]{1,0:T(8,128)(2,1)S(1)}, bf16[128,512]{1,0:T(8,128)(2,1)S(1)}, u32[]{:S(2)}, u32[]{:S(2)}) collective-permute-start(bf16[128,512]{1,0:T(8,128)(2,1)S(1)} %broadcast_select_fusion.2), channel_id=1, source_target_pairs={{0,2},{2,0},{4,6},{6,4},{8,10},{10,8},{12,14},{14,12},{1,3},{3,1},... | collective-permute-start | bytes 393224 | tf_op jit(solution)/shard_map/ppermute | solution.py:246
  15.3 5.9 %collective-permute-start.7 = (bf16[128,768]{1,0:T(8,128)(2,1)S(1)}, bf16[128,768]{1,0:T(8,128)(2,1)S(1)}, u32[]{:S(2)}, u32[]{:S(2)}) collective-permute-start(bf16[128,768]{1,0:T(8,128)(2,1)S(1)} %broadcast_select_fusion), channel_id=1, source_target_pairs={{0,2},{2,0},{4,6},{6,4},{8,10},{10,8},{12,14},{14,12},{1,3},{3,1},... | collective-permute-start | bytes 589832 | tf_op jit(solution)/shard_map/ppermute | solution.py:246
  17.1 7.1 %collective-permute-start.4 = (bf16[128,512]{1,0:T(8,128)(2,1)S(1)}, bf16[128,512]{1,0:T(8,128)(2,1)S(1)}, u32[]{:S(2)}, u32[]{:S(2)}) collective-permute-start(bf16[128,512]{1,0:T(8,128)(2,1)S(1)} %collective-permute-done.3.refs_3_), channel_id=1, source_target_pairs={{0,4},{2,6},{4,8},{6,10},{8,12},{10,14},{12,0},{14,2},{1,5},{3,7},... | collective-permute-start | bytes 393224 | tf_op jit(solution)/shard_map/ppermute | solution.py:246
  18.7 10.7 %collective-permute-start.6 = (bf16[128,768]{1,0:T(8,128)(2,1)S(1)}, bf16[128,768]{1,0:T(8,128)(2,1)S(1)}, u32[]{:S(2)}, u32[]{:S(2)}) collective-permute-start(bf16[128,768]{1,0:T(8,128)(2,1)S(1)} %broadcast_select_fusion.1), channel_id=1, source_target_pairs={{0,2},{2,4},{4,6},{6,8},{8,10},{10,12},{12,14},{14,0},{1,3},{3,5},... | collective-permute-start | bytes 589832 | tf_op jit(solution)/shard_map/ppermute | solution.py:246
  20.2 9.8 %collective-permute-start.5 = (bf16[128,768]{1,0:T(8,128)(2,1)S(1)}, bf16[128,768]{1,0:T(8,128)(2,1)S(1)}, u32[]{:S(2)}, u32[]{:S(2)}) collective-permute-start(bf16[128,768]{1,0:T(8,128)(2,1)S(1)} %collective-permute-done.2.refs_4_), channel_id=1, source_target_pairs={{0,2},{2,0},{4,6},{6,4},{8,10},{10,8},{12,14},{14,12},{1,3},{3,1},... | collective-permute-start | bytes 589832 | tf_op jit(solution)/shard_map/ppermute | solution.py:246
  21.2 9.4 %collective-permute-start.9 = (bf16[128,768]{1,0:T(8,128)(2,1)S(1)}, bf16[128,768]{1,0:T(8,128)(2,1)S(1)}, u32[]{:S(2)}, u32[]{:S(2)}) collective-permute-start(bf16[128,768]{1,0:T(8,128)(2,1)S(1)} %collective-permute-done.7.refs_2_), channel_id=1, source_target_pairs={{0,4},{2,6},{4,8},{6,10},{8,12},{10,14},{12,0},{14,2},{1,5},{3,7},... | collective-permute-start | bytes 589832 | tf_op jit(solution)/shard_map/ppermute | solution.py:246
  22.6 8.9 %collective-permute-start.11 = (f32[384,128]{1,0:T(8,128)S(1)}, f32[384,128]{1,0:T(8,128)S(1)}, u32[]{:S(2)}, u32[]{:S(2)}) collective-permute-start(f32[384,128]{1,0:T(8,128)S(1)} %get-tuple-element.55), channel_id=1, source_target_pairs={{0,1},{1,0},{2,3},{3,2},{4,5},{5,4},{6,7},{7,6},{8,9},{9,8},{10,11... | collective-permute-start | bytes 589832 | tf_op jit(solution)/shard_map/ppermute | solution.py:246
  24.2 7.3 %collective-permute-start.12 = (f32[384,128]{1,0:T(8,128)S(1)}, f32[384,128]{1,0:T(8,128)S(1)}, u32[]{:S(2)}, u32[]{:S(2)}) collective-permute-start(f32[384,128]{1,0:T(8,128)S(1)} %get-tuple-element.56), channel_id=1, source_target_pairs={{0,1},{1,0},{2,3},{3,2},{4,5},{5,4},{6,7},{7,6},{8,9},{9,8},{10,11... | collective-permute-start | bytes 589832 | tf_op jit(solution)/shard_map/ppermute | solution.py:246
  30.5 2.1 %collective-permute-start.8 = (f32[384,128]{1,0:T(8,128)S(1)}, f32[384,128]{1,0:T(8,128)S(1)}, u32[]{:S(2)}, u32[]{:S(2)}) collective-permute-start(f32[384,128]{1,0:T(8,128)S(1)} %get-tuple-element.52), channel_id=1, source_target_pairs={{0,1},{1,0},{2,3},{3,2},{4,5},{5,4},{6,7},{7,6},{8,9},{9,8},{10,11... | collective-permute-start | bytes 589832 | tf_op jit(solution)/shard_map/ppermute | solution.py:246
  30.9 1.7 %collective-permute-start.10 = (f32[384,128]{1,0:T(8,128)S(1)}, f32[384,128]{1,0:T(8,128)S(1)}, u32[]{:S(2)}, u32[]{:S(2)}) collective-permute-start(f32[384,128]{1,0:T(8,128)S(1)} %shard_map.62), channel_id=1, source_target_pairs={{0,1},{1,0},{2,3},{3,2},{4,5},{5,4},{6,7},{7,6},{8,9},{9,8},{10,11... | collective-permute-start | bytes 589832 | tf_op jit(solution)/shard_map/ppermute | solution.py:246

commit v27 on v22

--- a/solution.py
+++ b/solution.py
@@ -201,10 +201,15 @@
     stores = []
     for n, place in enumerate(places):
         cut = slice(n * columns, (n + 1) * columns)
-        summed[:, cut] = jnp.where(inside, refs[2 * n][...] + refs[2 * n + 1][...], 0.0)
-        to = out.at[:, place * columns:(place + 1) * columns]
-        stores.append(pltpu.make_async_copy(summed.at[:, cut], to, left.at[n]))
-        stores[n].start()
+        for part in range(2):
+            rows = slice(part * half // 2, (part + 1) * half // 2)
+            total = refs[2 * n][rows, :] + refs[2 * n + 1][rows, :]
+            summed[rows, cut] = jnp.where(inside[rows, :], total, 0.0)
+            to = out.at[rows, place * columns:(place + 1) * columns]
+            stores.append(
+                pltpu.make_async_copy(summed.at[rows, cut], to, left.at[2 * n + part])
+            )
+            stores[-1].start()
     for store in stores:
         store.wait()
 
@@ -221,7 +226,7 @@
         out_specs=far_spec(),
         scratch_shapes=[
             pltpu.VMEM((half, columns * len(places)), jnp.float32),
-            pltpu.SemaphoreType.DMA((len(places),)),
+            pltpu.SemaphoreType.DMA((2 * len(places),)),
         ],
         input_output_aliases={1 + len(operands): 0} if given else {},
         compiler_params=params(),

time: 33.6 us -> 33.6 us (level)
  no operation moved by 1% of the time
where the time goes in v27:
time: 33.6 us; the launch traced here: 33.4 us
  starting transfers between devices  14.1 us (42%)
  Pallas kernels  9.51 us (28%)
  waiting for transfers between devices  8.92 us (27%)
  between operations  0.79 us (2%)
    ppermute x13, starting transfers between devices, send(): return lax.ppermute(block, axis, route)  14.1 us
    ppermute x13, waiting for transfers between devices, send(): return lax.ppermute(block, axis, route)  8.92 us
    pallas_call x7, Pallas kernels, more_scores(): pl.pallas_call(functools.partial(scores_kernel, tuple(placed), fresh, loa...  6.34 us
    pallas_call x2, Pallas kernels, finish(): pl.pallas_call(functools.partial(finish_kernel, places), out_shape=pltpu....  1.59 us
    pallas_call x1, Pallas kernels, prepare(): pl.pallas_call(prepare_kernel, out_shape=shapes + [jax.ShapeDtypeStruct((...  1.58 us
  transfers between devices with their start and end apart: 13, of which 5 were waited for; matrix products, arithmetic and copies ran while one was open for 0% of the time, Pallas kernels for 21%

profile of v27, /device:TPU:0, one launch (start us, length us, event | category | flops | bytes accessed | tf_op | source)
XLA Modules:
  0.0 33.4 jit_solution(7361993900025398050)
XLA Ops:
  0.0 1.6 %shard_map.55 = (bf16[128,512]{1,0:T(8,128)(2,1)S(1)}, bf16[128,768]{1,0:T(8,128)(2,1)S(1)}, bf16[128,768]{1,0:T(8,128)(2,1)S(1)}, bf16[128,2048]{1,0:T(8,128)(2,1)S(1)}) custom-call(bf16[128,2048]{1,0:T(8,128)(2,1)} %queries.1, f32[1,2048]{1,0:T(1,128)} %bitcast.1, s32[1,128]{1,0:T(1,128)} %rank.1), custom_call_target="tpu_custom_call" | custom-call | flops 67108864 | bytes 1048576 | tf_op jit(solution)/shard_map/pallas_call | solution.py:80
  1.6 3.1 %collective-permute-start = (bf16[128,512]{1,0:T(8,128)(2,1)S(1)}, bf16[128,512]{1,0:T(8,128)(2,1)S(1)}, u32[]{:S(2)}, u32[]{:S(2)}) collective-permute-start(bf16[128,512]{1,0:T(8,128)(2,1)S(1)} %get-tuple-element.34), channel_id=1, source_target_pairs={{0,4},{2,6},{4,8},{6,10},{8,12},{10,14},{12,0},{14,2},{1,5},{3,7},... | collective-permute-start | bytes 393224 | tf_op jit(solution)/shard_map/ppermute | solution.py:251
  4.7 1.6 %collective-permute-start.1 = (bf16[128,768]{1,0:T(8,128)(2,1)S(1)}, bf16[128,768]{1,0:T(8,128)(2,1)S(1)}, u32[]{:S(2)}, u32[]{:S(2)}) collective-permute-start(bf16[128,768]{1,0:T(8,128)(2,1)S(1)} %get-tuple-element.35), channel_id=1, source_target_pairs={{0,4},{2,6},{4,8},{6,10},{8,12},{10,14},{12,0},{14,2},{1,5},{3,7},... | collective-permute-start | bytes 589832 | tf_op jit(solution)/shard_map/ppermute | solution.py:251
  6.2 1.6 %collective-permute-start.2 = (bf16[128,768]{1,0:T(8,128)(2,1)S(1)}, bf16[128,768]{1,0:T(8,128)(2,1)S(1)}, u32[]{:S(2)}, u32[]{:S(2)}) collective-permute-start(bf16[128,768]{1,0:T(8,128)(2,1)S(1)} %get-tuple-element.36), channel_id=1, source_target_pairs={{0,4},{2,6},{4,8},{6,10},{8,12},{10,14},{12,0},{14,2},{1,5},{3,7},... | collective-permute-start | bytes 589832 | tf_op jit(solution)/shard_map/ppermute | solution.py:251
  7.8 3.3 %shard_map.56 = (f32[384,128]{1,0:T(8,128)S(1)}, f32[384,128]{1,0:T(8,128)S(1)}, bf16[384,2048]{1,0:T(8,128)(2,1)S(1)}, bf16[384,2048]{1,0:T(8,128)(2,1)S(1)}) custom-call(bf16[768,2048]{1,0:T(8,128)(2,1)} %refs_0_.1, bf16[128,2048]{1,0:T(8,128)(2,1)S(1)} %get-tuple-element.31.refs_1_), custom_call_target="tpu_custom_call" | custom-call | flops 402653184 | bytes 393216 | tf_op jit(solution)/shard_map/pallas_call | solution.py:181
  11.2 1.6 %collective-permute-start.3 = (bf16[128,512]{1,0:T(8,128)(2,1)S(1)}, bf16[128,512]{1,0:T(8,128)(2,1)S(1)}, u32[]{:S(2)}, u32[]{:S(2)}) collective-permute-start(bf16[128,512]{1,0:T(8,128)(2,1)S(1)} %broadcast_select_fusion.2), channel_id=1, source_target_pairs={{0,2},{2,0},{4,6},{6,4},{8,10},{10,8},{12,14},{14,12},{1,3},{3,1},... | collective-permute-start | bytes 393224 | tf_op jit(solution)/shard_map/ppermute | solution.py:251
  12.8 2.4 %collective-permute-done.1.refs_3_ = bf16[128,768]{1,0:T(8,128)(2,1)S(1)} collective-permute-done((bf16[128,768]{1,0:T(8,128)(2,1)S(1)}, bf16[128,768]{1,0:T(8,128)(2,1)S(1)}, u32[]{:S(2)}, u32[]{:S(2)}) %collective-permute-start.1) | collective-permute-done | bytes 196640 | tf_op jit(solution)/shard_map/ppermute | solution.py:251
  15.3 1.8 %collective-permute-start.7 = (bf16[128,768]{1,0:T(8,128)(2,1)S(1)}, bf16[128,768]{1,0:T(8,128)(2,1)S(1)}, u32[]{:S(2)}, u32[]{:S(2)}) collective-permute-start(bf16[128,768]{1,0:T(8,128)(2,1)S(1)} %broadcast_select_fusion), channel_id=1, source_target_pairs={{0,2},{2,0},{4,6},{6,4},{8,10},{10,8},{12,14},{14,12},{1,3},{3,1},... | collective-permute-start | bytes 589832 | tf_op jit(solution)/shard_map/ppermute | solution.py:251
  17.1 1.6 %collective-permute-done.2.refs_4_ = bf16[128,768]{1,0:T(8,128)(2,1)S(1)} collective-permute-done((bf16[128,768]{1,0:T(8,128)(2,1)S(1)}, bf16[128,768]{1,0:T(8,128)(2,1)S(1)}, u32[]{:S(2)}, u32[]{:S(2)}) %collective-permute-start.2) | collective-permute-done | bytes 196640 | tf_op jit(solution)/shard_map/ppermute | solution.py:251
  18.6 1.5 %collective-permute-start.6 = (bf16[128,768]{1,0:T(8,128)(2,1)S(1)}, bf16[128,768]{1,0:T(8,128)(2,1)S(1)}, u32[]{:S(2)}, u32[]{:S(2)}) collective-permute-start(bf16[128,768]{1,0:T(8,128)(2,1)S(1)} %broadcast_select_fusion.1), channel_id=1, source_target_pairs={{0,2},{2,4},{4,6},{6,8},{8,10},{10,12},{12,14},{14,0},{1,3},{3,5},... | collective-permute-start | bytes 589832 | tf_op jit(solution)/shard_map/ppermute | solution.py:251
  20.2 0.3 collective-permute-start.5
  20.5 0.6 %collective-permute-done.7.refs_2_ = bf16[128,768]{1,0:T(8,128)(2,1)S(1)} collective-permute-done((bf16[128,768]{1,0:T(8,128)(2,1)S(1)}, bf16[128,768]{1,0:T(8,128)(2,1)S(1)}, u32[]{:S(2)}, u32[]{:S(2)}) %collective-permute-start.7) | collective-permute-done | bytes 196640 | tf_op jit(solution)/shard_map/ppermute | solution.py:251
  21.1 1.4 %collective-permute-start.9 = (bf16[128,768]{1,0:T(8,128)(2,1)S(1)}, bf16[128,768]{1,0:T(8,128)(2,1)S(1)}, u32[]{:S(2)}, u32[]{:S(2)}) collective-permute-start(bf16[128,768]{1,0:T(8,128)(2,1)S(1)} %collective-permute-done.7.refs_2_), channel_id=1, source_target_pairs={{0,4},{2,6},{4,8},{6,10},{8,12},{10,14},{12,0},{14,2},{1,5},{3,7},... | collective-permute-start | bytes 589832 | tf_op jit(solution)/shard_map/ppermute | solution.py:251
  23.2 1.0 %shard_map.57 = (f32[384,128]{1,0:T(8,128)S(1)}, f32[384,128]{1,0:T(8,128)S(1)}) custom-call(bf16[384,2048]{1,0:T(8,128)(2,1)S(1)} %get-tuple-element.32.refs_0_.refs_1_, bf16[384,2048]{1,0:T(8,128)(2,1)S(1)} %get-tuple-element.33.refs_1_.refs_2_, bf16[128,512]{1,0:T(8,128)(2,1)S(1)} %collective-permute-done.refs_2_, ...), custom_call_target="tpu_custom_call" | custom-call | flops 402653184 | bytes 393216 | tf_op jit(solution)/shard_map/pallas_call | solution.py:181
  24.2 0.6 %collective-permute-start.12 = (f32[384,128]{1,0:T(8,128)S(1)}, f32[384,128]{1,0:T(8,128)S(1)}, u32[]{:S(2)}, u32[]{:S(2)}) collective-permute-start(f32[384,128]{1,0:T(8,128)S(1)} %get-tuple-element.56), channel_id=1, source_target_pairs={{0,1},{1,0},{2,3},{3,2},{4,5},{5,4},{6,7},{7,6},{8,9},{9,8},{10,11... | collective-permute-start | bytes 589832 | tf_op jit(solution)/shard_map/ppermute | solution.py:251
  24.7 0.4 %shard_map.58 = (f32[384,128]{1,0:T(8,128)S(1)}, f32[384,128]{1,0:T(8,128)S(1)}, f32[384,128]{1,0:T(8,128)S(1)}, f32[384,128]{1,0:T(8,128)S(1)}, s32[8,128]{1,0:T(8,128)S(1)}) custom-call(s32[1]{0:T(128)S(6)} %copy.8.refs_0_, bf16[384,2048]{1,0:T(8,128)(2,1)S(1)} %get-tuple-element.32.refs_0_.refs_1_, ...), custom_call_target="tpu_custom_call" | custom-call | flops 402653184 | bytes 1572864 | tf_op jit(solution)/shard_map/pallas_call | solution.py:181
  25.1 0.5 %shard_map.59 = (f32[384,128]{1,0:T(8,128)S(1)}, f32[384,128]{1,0:T(8,128)S(1)}, f32[384,128]{1,0:T(8,128)S(1)}, f32[384,128]{1,0:T(8,128)S(1)}) custom-call(bf16[384,2048]{1,0:T(8,128)(2,1)S(1)} %get-tuple-element.32.refs_0_.refs_1_, bf16[384,2048]{1,0:T(8,128)(2,1)S(1)} %get-tuple-element.33.refs_1_.refs_2_, ...), custom_call_target="tpu_custom_call" | custom-call | flops 301989888 | bytes 1572864 | tf_op jit(solution)/shard_map/pallas_call | solution.py:181
  25.6 3.7 %collective-permute-done.6.refs_3_ = bf16[128,768]{1,0:T(8,128)(2,1)S(1)} collective-permute-done((bf16[128,768]{1,0:T(8,128)(2,1)S(1)}, bf16[128,768]{1,0:T(8,128)(2,1)S(1)}, u32[]{:S(2)}, u32[]{:S(2)}) %collective-permute-start.6) | collective-permute-done | bytes 196640 | tf_op jit(solution)/shard_map/ppermute | solution.py:251
  29.3 0.6 %collective-permute-done.5.refs_2_ = bf16[128,768]{1,0:T(8,128)(2,1)S(1)} collective-permute-done((bf16[128,768]{1,0:T(8,128)(2,1)S(1)}, bf16[128,768]{1,0:T(8,128)(2,1)S(1)}, u32[]{:S(2)}, u32[]{:S(2)}) %collective-permute-start.5) | collective-permute-done | bytes 196640 | tf_op jit(solution)/shard_map/ppermute | solution.py:251
  30.0 0.5 %shard_map.60 = (f32[384,128]{1,0:T(8,128)S(1)}, f32[384,128]{1,0:T(8,128)S(1)}, f32[384,128]{1,0:T(8,128)S(1)}, f32[384,128]{1,0:T(8,128)S(1)}) custom-call(bf16[384,2048]{1,0:T(8,128)(2,1)S(1)} %get-tuple-element.32.refs_0_.refs_1_, bf16[384,2048]{1,0:T(8,128)(2,1)S(1)} %get-tuple-element.33.refs_1_.refs_2_, ...), custom_call_target="tpu_custom_call" | custom-call | flops 603979776 | bytes 1572864 | tf_op jit(solution)/shard_map/pallas_call | solution.py:181
  30.6 0.3 shard_map.62
  30.9 0.5 %collective-permute-start.10 = (f32[384,128]{1,0:T(8,128)S(1)}, f32[384,128]{1,0:T(8,128)S(1)}, u32[]{:S(2)}, u32[]{:S(2)}) collective-permute-start(f32[384,128]{1,0:T(8,128)S(1)} %shard_map.62), channel_id=1, source_target_pairs={{0,1},{1,0},{2,3},{3,2},{4,5},{5,4},{6,7},{7,6},{8,9},{9,8},{10,11... | collective-permute-start | bytes 589832 | tf_op jit(solution)/shard_map/ppermute | solution.py:251
  31.5 0.8 %shard_map.63.refs_4_ = f32[384,512]{1,0:T(8,128)} custom-call(s32[8,128]{1,0:T(8,128)S(1)} %get-tuple-element.41.limit, f32[384,128]{1,0:T(8,128)S(1)} %get-tuple-element.39.refs_0_, f32[384,128]{1,0:T(8,128)S(1)} %collective-permute-done.11.refs_1_, f32[384,128]{1,0:T(8,128)S(1)} %get-tuple-element.37.refs_2_, f32[384,128]{1,0:T(8,128)S(1)} %collective-permute-done.12.refs_3_), custom_call_target="tpu_custom_call" | custom-call | flops 98304 | bytes 1179648 | tf_op jit(solution)/shard_map/pallas_call | solution.py:221
  32.6 0.8 %shard_map.64 = f32[384,512]{1,0:T(8,128)} custom-call(s32[8,128]{1,0:T(8,128)S(1)} %get-tuple-element.41.limit, f32[384,128]{1,0:T(8,128)S(1)} %get-tuple-element.51.refs_0_, f32[384,128]{1,0:T(8,128)S(1)} %collective-permute-done.8.refs_1_, f32[384,128]{1,0:T(8,128)S(1)} %shard_map.61.refs_2_, ...), custom_call_target="tpu_custom_call", output_to_operand_aliasing={{}: (5, {})} | custom-call | flops 98304 | bytes 1179648 | tf_op jit(solution)/shard_map/pallas_call | solution.py:221
  (15 shorter events, 0.5 us)
Async XLA Ops:
  1.6 9.6 %collective-permute-start = (bf16[128,512]{1,0:T(8,128)(2,1)S(1)}, bf16[128,512]{1,0:T(8,128)(2,1)S(1)}, u32[]{:S(2)}, u32[]{:S(2)}) collective-permute-start(bf16[128,512]{1,0:T(8,128)(2,1)S(1)} %get-tuple-element.34), channel_id=1, source_target_pairs={{0,4},{2,6},{4,8},{6,10},{8,12},{10,14},{12,0},{14,2},{1,5},{3,7},... | collective-permute-start | bytes 393224 | tf_op jit(solution)/shard_map/ppermute | solution.py:251
  4.7 10.6 %collective-permute-start.1 = (bf16[128,768]{1,0:T(8,128)(2,1)S(1)}, bf16[128,768]{1,0:T(8,128)(2,1)S(1)}, u32[]{:S(2)}, u32[]{:S(2)}) collective-permute-start(bf16[128,768]{1,0:T(8,128)(2,1)S(1)} %get-tuple-element.35), channel_id=1, source_target_pairs={{0,4},{2,6},{4,8},{6,10},{8,12},{10,14},{12,0},{14,2},{1,5},{3,7},... | collective-permute-start | bytes 589832 | tf_op jit(solution)/shard_map/ppermute | solution.py:251
  6.2 12.4 %collective-permute-start.2 = (bf16[128,768]{1,0:T(8,128)(2,1)S(1)}, bf16[128,768]{1,0:T(8,128)(2,1)S(1)}, u32[]{:S(2)}, u32[]{:S(2)}) collective-permute-start(bf16[128,768]{1,0:T(8,128)(2,1)S(1)} %get-tuple-element.36), channel_id=1, source_target_pairs={{0,4},{2,6},{4,8},{6,10},{8,12},{10,14},{12,0},{14,2},{1,5},{3,7},... | collective-permute-start | bytes 589832 | tf_op jit(solution)/shard_map/ppermute | solution.py:251
  11.2 5.9 %collective-permute-start.3 = (bf16[128,512]{1,0:T(8,128)(2,1)S(1)}, bf16[128,512]{1,0:T(8,128)(2,1)S(1)}, u32[]{:S(2)}, u32[]{:S(2)}) collective-permute-start(bf16[128,512]{1,0:T(8,128)(2,1)S(1)} %broadcast_select_fusion.2), channel_id=1, source_target_pairs={{0,2},{2,0},{4,6},{6,4},{8,10},{10,8},{12,14},{14,12},{1,3},{3,1},... | collective-permute-start | bytes 393224 | tf_op jit(solution)/shard_map/ppermute | solution.py:251
  15.3 5.9 %collective-permute-start.7 = (bf16[128,768]{1,0:T(8,128)(2,1)S(1)}, bf16[128,768]{1,0:T(8,128)(2,1)S(1)}, u32[]{:S(2)}, u32[]{:S(2)}) collective-permute-start(bf16[128,768]{1,0:T(8,128)(2,1)S(1)} %broadcast_select_fusion), channel_id=1, source_target_pairs={{0,2},{2,0},{4,6},{6,4},{8,10},{10,8},{12,14},{14,12},{1,3},{3,1},... | collective-permute-start | bytes 589832 | tf_op jit(solution)/shard_map/ppermute | solution.py:251
  17.1 7.1 %collective-permute-start.4 = (bf16[128,512]{1,0:T(8,128)(2,1)S(1)}, bf16[128,512]{1,0:T(8,128)(2,1)S(1)}, u32[]{:S(2)}, u32[]{:S(2)}) collective-permute-start(bf16[128,512]{1,0:T(8,128)(2,1)S(1)} %collective-permute-done.3.refs_3_), channel_id=1, source_target_pairs={{0,4},{2,6},{4,8},{6,10},{8,12},{10,14},{12,0},{14,2},{1,5},{3,7},... | collective-permute-start | bytes 393224 | tf_op jit(solution)/shard_map/ppermute | solution.py:251
  18.6 10.7 %collective-permute-start.6 = (bf16[128,768]{1,0:T(8,128)(2,1)S(1)}, bf16[128,768]{1,0:T(8,128)(2,1)S(1)}, u32[]{:S(2)}, u32[]{:S(2)}) collective-permute-start(bf16[128,768]{1,0:T(8,128)(2,1)S(1)} %broadcast_select_fusion.1), channel_id=1, source_target_pairs={{0,2},{2,4},{4,6},{6,8},{8,10},{10,12},{12,14},{14,0},{1,3},{3,5},... | collective-permute-start | bytes 589832 | tf_op jit(solution)/shard_map/ppermute | solution.py:251
  20.2 9.8 %collective-permute-start.5 = (bf16[128,768]{1,0:T(8,128)(2,1)S(1)}, bf16[128,768]{1,0:T(8,128)(2,1)S(1)}, u32[]{:S(2)}, u32[]{:S(2)}) collective-permute-start(bf16[128,768]{1,0:T(8,128)(2,1)S(1)} %collective-permute-done.2.refs_4_), channel_id=1, source_target_pairs={{0,2},{2,0},{4,6},{6,4},{8,10},{10,8},{12,14},{14,12},{1,3},{3,1},... | collective-permute-start | bytes 589832 | tf_op jit(solution)/shard_map/ppermute | solution.py:251
  21.1 9.5 %collective-permute-start.9 = (bf16[128,768]{1,0:T(8,128)(2,1)S(1)}, bf16[128,768]{1,0:T(8,128)(2,1)S(1)}, u32[]{:S(2)}, u32[]{:S(2)}) collective-permute-start(bf16[128,768]{1,0:T(8,128)(2,1)S(1)} %collective-permute-done.7.refs_2_), channel_id=1, source_target_pairs={{0,4},{2,6},{4,8},{6,10},{8,12},{10,14},{12,0},{14,2},{1,5},{3,7},... | collective-permute-start | bytes 589832 | tf_op jit(solution)/shard_map/ppermute | solution.py:251
  22.5 8.9 %collective-permute-start.11 = (f32[384,128]{1,0:T(8,128)S(1)}, f32[384,128]{1,0:T(8,128)S(1)}, u32[]{:S(2)}, u32[]{:S(2)}) collective-permute-start(f32[384,128]{1,0:T(8,128)S(1)} %get-tuple-element.55), channel_id=1, source_target_pairs={{0,1},{1,0},{2,3},{3,2},{4,5},{5,4},{6,7},{7,6},{8,9},{9,8},{10,11... | collective-permute-start | bytes 589832 | tf_op jit(solution)/shard_map/ppermute | solution.py:251
  24.2 7.3 %collective-permute-start.12 = (f32[384,128]{1,0:T(8,128)S(1)}, f32[384,128]{1,0:T(8,128)S(1)}, u32[]{:S(2)}, u32[]{:S(2)}) collective-permute-start(f32[384,128]{1,0:T(8,128)S(1)} %get-tuple-element.56), channel_id=1, source_target_pairs={{0,1},{1,0},{2,3},{3,2},{4,5},{5,4},{6,7},{7,6},{8,9},{9,8},{10,11... | collective-permute-start | bytes 589832 | tf_op jit(solution)/shard_map/ppermute | solution.py:251
  30.5 2.1 %collective-permute-start.8 = (f32[384,128]{1,0:T(8,128)S(1)}, f32[384,128]{1,0:T(8,128)S(1)}, u32[]{:S(2)}, u32[]{:S(2)}) collective-permute-start(f32[384,128]{1,0:T(8,128)S(1)} %get-tuple-element.52), channel_id=1, source_target_pairs={{0,1},{1,0},{2,3},{3,2},{4,5},{5,4},{6,7},{7,6},{8,9},{9,8},{10,11... | collective-permute-start | bytes 589832 | tf_op jit(solution)/shard_map/ppermute | solution.py:251
  30.9 1.7 %collective-permute-start.10 = (f32[384,128]{1,0:T(8,128)S(1)}, f32[384,128]{1,0:T(8,128)S(1)}, u32[]{:S(2)}, u32[]{:S(2)}) collective-permute-start(f32[384,128]{1,0:T(8,128)S(1)} %shard_map.62), channel_id=1, source_target_pairs={{0,1},{1,0},{2,3},{3,2},{4,5},{5,4},{6,7},{7,6},{8,9},{9,8},{10,11... | collective-permute-start | bytes 589832 | tf_op jit(solution)/shard_map/ppermute | solution.py:251

commit v28 on v20

--- a/solution.py
+++ b/solution.py
@@ -14,6 +14,7 @@
 ORDER = ("B0", "B1", "B2", "C0", "C1", "E0", "E1", "R2", "C2")
 TIES = {"C2": "C0"}
 EARLY = "C0"
+OUT = False
 WEIGHT = 2
 CHUNKS = len(PARTS)
 VMEM_BYTES = 16 * 1024 * 1024
@@ -314,6 +315,9 @@
             )
         else:
             one, three = more_scores(stores, pieces_of(group), [one, three], weight=WEIGHT)
+    out = finish(limit, [own_pair, two_pair], (0, 2), STEPS)
+    if OUT:
+        one = after(one[0], out), one[1]
     late, last = pieces_of(CHAIN[-2]), pieces_of(CHAIN[-1])
     [one_theirs], [three_theirs] = more_scores(stores, late, [one, three], sides=(0,))
     one_came = send(one_theirs, over_dim, "dim")
@@ -322,8 +326,7 @@
     three_came = send(three_theirs, over_dim, "dim")
     [one_ours], [three_ours] = more_scores(stores, late, [one, three], sides=(1,))
     [[three_ours]] = more_scores(stores, only, [(None, three_ours)], sides=(1,))
-    pairs = [own_pair, (one_ours, one_came), two_pair, (three_ours, three_came)]
-    return finish(limit, pairs, (0, 1, 2, 3), STEPS)
+    return finish(limit, [(one_ours, one_came), (three_ours, three_came)], (1, 3), STEPS, out)
 
 
 def solution(mesh):

time: 33.5 us -> 33.8 us (level)
  Pallas kernels: 9.07 us -> 9.75 us
  waiting for transfers between devices: 9.27 us -> 8.93 us
    pallas_call x1 -> x2, Pallas kernels: 0.95 us -> 1.61 us  [finish(): pl.pallas_call(functools.partial(finish_kernel, places), out_shape=pltpu....]
    ppermute x13, waiting for transfers between devices: 9.27 us -> 8.93 us  [send(): return lax.ppermute(block, axis, route)]
  transfers between devices with their start and end apart: 13 -> 13, of which waited for: 6 -> 5; matrix products, arithmetic and copies ran while one was open for 0% -> 0% of each run, Pallas kernels for 20% -> 22%
where the time goes in v28:
time: 33.8 us; the launch traced here: 33.7 us
  starting transfers between devices  14.1 us (42%)
  Pallas kernels  9.75 us (29%)
  waiting for transfers between devices  8.93 us (26%)
  between operations  0.8 us (2%)
    ppermute x13, starting transfers between devices, send(): return lax.ppermute(block, axis, route)  14.1 us
    ppermute x13, waiting for transfers between devices, send(): return lax.ppermute(block, axis, route)  8.93 us
    pallas_call x8, Pallas kernels, more_scores(): pl.pallas_call(functools.partial(scores_kernel, tuple(placed), fresh, loa...  6.56 us
    pallas_call x2, Pallas kernels, finish(): pl.pallas_call(functools.partial(finish_kernel, places), out_shape=pltpu....  1.61 us
    pallas_call x1, Pallas kernels, prepare(): pl.pallas_call(prepare_kernel, out_shape=shapes, in_specs=[far_spec()] *...  1.58 us
  transfers between devices with their start and end apart: 13, of which 5 were waited for; matrix products, arithmetic and copies ran while one was open for 0% of the time, Pallas kernels for 22%

profile of v28, /device:TPU:0, one launch (start us, length us, event | category | flops | bytes accessed | tf_op | source)
XLA Modules:
  0.0 33.7 jit_solution(6502003918476208403)
XLA Ops:
  0.0 1.6 %shard_map.55 = (bf16[128,512]{1,0:T(8,128)(2,1)S(1)}, bf16[128,768]{1,0:T(8,128)(2,1)S(1)}, bf16[128,768]{1,0:T(8,128)(2,1)S(1)}) custom-call(bf16[128,2048]{1,0:T(8,128)(2,1)} %queries.1, f32[1,2048]{1,0:T(1,128)} %bitcast.1, s32[1,128]{1,0:T(1,128)} %rank.1), custom_call_target="tpu_custom_call" | custom-call | flops 67108864 | bytes 1048576 | tf_op jit(solution)/shard_map/pallas_call | solution.py:81
  1.6 3.1 %collective-permute-start = (bf16[128,512]{1,0:T(8,128)(2,1)S(1)}, bf16[128,512]{1,0:T(8,128)(2,1)S(1)}, u32[]{:S(2)}, u32[]{:S(2)}) collective-permute-start(bf16[128,512]{1,0:T(8,128)(2,1)S(1)} %get-tuple-element.30.refs_1_), channel_id=1, source_target_pairs={{0,4},{2,6},{4,8},{6,10},{8,12},{10,14},{12,0},{14,2},{1,5},{3,7},... | collective-permute-start | bytes 393224 | tf_op jit(solution)/shard_map/ppermute | solution.py:247
  4.7 1.6 %collective-permute-start.1 = (bf16[128,768]{1,0:T(8,128)(2,1)S(1)}, bf16[128,768]{1,0:T(8,128)(2,1)S(1)}, u32[]{:S(2)}, u32[]{:S(2)}) collective-permute-start(bf16[128,768]{1,0:T(8,128)(2,1)S(1)} %get-tuple-element.31.refs_2_), channel_id=1, source_target_pairs={{0,4},{2,6},{4,8},{6,10},{8,12},{10,14},{12,0},{14,2},{1,5},{3,7},... | collective-permute-start | bytes 589832 | tf_op jit(solution)/shard_map/ppermute | solution.py:247
  6.2 1.6 %collective-permute-start.2 = (bf16[128,768]{1,0:T(8,128)(2,1)S(1)}, bf16[128,768]{1,0:T(8,128)(2,1)S(1)}, u32[]{:S(2)}, u32[]{:S(2)}) collective-permute-start(bf16[128,768]{1,0:T(8,128)(2,1)S(1)} %get-tuple-element.32.refs_3_), channel_id=1, source_target_pairs={{0,4},{2,6},{4,8},{6,10},{8,12},{10,14},{12,0},{14,2},{1,5},{3,7},... | collective-permute-start | bytes 589832 | tf_op jit(solution)/shard_map/ppermute | solution.py:247
  7.8 3.3 %shard_map.56 = (f32[384,128]{1,0:T(8,128)S(1)}, f32[384,128]{1,0:T(8,128)S(1)}, bf16[384,2048]{1,0:T(8,128)(2,1)S(1)}, bf16[384,2048]{1,0:T(8,128)(2,1)S(1)}) custom-call(bf16[768,2048]{1,0:T(8,128)(2,1)} %refs_0_.1, bf16[128,512]{1,0:T(8,128)(2,1)S(1)} %get-tuple-element.30.refs_1_, bf16[128,768]{1,0:T(8,128)(2,1)S(1)} %get-tuple-element.31.refs_2_, ...), custom_call_target="tpu_custom_call" | custom-call | flops 402653184 | bytes 393216 | tf_op jit(solution)/shard_map/pallas_call | solution.py:182
  11.2 1.6 %collective-permute-start.3 = (bf16[128,512]{1,0:T(8,128)(2,1)S(1)}, bf16[128,512]{1,0:T(8,128)(2,1)S(1)}, u32[]{:S(2)}, u32[]{:S(2)}) collective-permute-start(bf16[128,512]{1,0:T(8,128)(2,1)S(1)} %broadcast_select_fusion.2), channel_id=1, source_target_pairs={{0,2},{2,0},{4,6},{6,4},{8,10},{10,8},{12,14},{14,12},{1,3},{3,1},... | collective-permute-start | bytes 393224 | tf_op jit(solution)/shard_map/ppermute | solution.py:247
  12.8 2.4 %collective-permute-done.1.refs_3_ = bf16[128,768]{1,0:T(8,128)(2,1)S(1)} collective-permute-done((bf16[128,768]{1,0:T(8,128)(2,1)S(1)}, bf16[128,768]{1,0:T(8,128)(2,1)S(1)}, u32[]{:S(2)}, u32[]{:S(2)}) %collective-permute-start.1) | collective-permute-done | bytes 196640 | tf_op jit(solution)/shard_map/ppermute | solution.py:247
  15.3 1.8 %collective-permute-start.7 = (bf16[128,768]{1,0:T(8,128)(2,1)S(1)}, bf16[128,768]{1,0:T(8,128)(2,1)S(1)}, u32[]{:S(2)}, u32[]{:S(2)}) collective-permute-start(bf16[128,768]{1,0:T(8,128)(2,1)S(1)} %broadcast_select_fusion), channel_id=1, source_target_pairs={{0,2},{2,0},{4,6},{6,4},{8,10},{10,8},{12,14},{14,12},{1,3},{3,1},... | collective-permute-start | bytes 589832 | tf_op jit(solution)/shard_map/ppermute | solution.py:247
  17.1 1.6 %collective-permute-done.2.refs_4_ = bf16[128,768]{1,0:T(8,128)(2,1)S(1)} collective-permute-done((bf16[128,768]{1,0:T(8,128)(2,1)S(1)}, bf16[128,768]{1,0:T(8,128)(2,1)S(1)}, u32[]{:S(2)}, u32[]{:S(2)}) %collective-permute-start.2) | collective-permute-done | bytes 196640 | tf_op jit(solution)/shard_map/ppermute | solution.py:247
  18.6 1.5 %collective-permute-start.6 = (bf16[128,768]{1,0:T(8,128)(2,1)S(1)}, bf16[128,768]{1,0:T(8,128)(2,1)S(1)}, u32[]{:S(2)}, u32[]{:S(2)}) collective-permute-start(bf16[128,768]{1,0:T(8,128)(2,1)S(1)} %broadcast_select_fusion.1), channel_id=1, source_target_pairs={{0,2},{2,4},{4,6},{6,8},{8,10},{10,12},{12,14},{14,0},{1,3},{3,5},... | collective-permute-start | bytes 589832 | tf_op jit(solution)/shard_map/ppermute | solution.py:247
  20.2 0.3 collective-permute-start.5
  20.5 0.6 %collective-permute-done.7.refs_2_ = bf16[128,768]{1,0:T(8,128)(2,1)S(1)} collective-permute-done((bf16[128,768]{1,0:T(8,128)(2,1)S(1)}, bf16[128,768]{1,0:T(8,128)(2,1)S(1)}, u32[]{:S(2)}, u32[]{:S(2)}) %collective-permute-start.7) | collective-permute-done | bytes 196640 | tf_op jit(solution)/shard_map/ppermute | solution.py:247
  21.1 1.4 %collective-permute-start.9 = (bf16[128,768]{1,0:T(8,128)(2,1)S(1)}, bf16[128,768]{1,0:T(8,128)(2,1)S(1)}, u32[]{:S(2)}, u32[]{:S(2)}) collective-permute-start(bf16[128,768]{1,0:T(8,128)(2,1)S(1)} %collective-permute-done.7.refs_2_), channel_id=1, source_target_pairs={{0,4},{2,6},{4,8},{6,10},{8,12},{10,14},{12,0},{14,2},{1,5},{3,7},... | collective-permute-start | bytes 589832 | tf_op jit(solution)/shard_map/ppermute | solution.py:247
  23.2 1.0 %shard_map.57 = (f32[384,128]{1,0:T(8,128)S(1)}, f32[384,128]{1,0:T(8,128)S(1)}) custom-call(bf16[384,2048]{1,0:T(8,128)(2,1)S(1)} %get-tuple-element.33.refs_0_.refs_1_, bf16[384,2048]{1,0:T(8,128)(2,1)S(1)} %get-tuple-element.34.refs_1_.refs_2_, bf16[128,512]{1,0:T(8,128)(2,1)S(1)} %collective-permute-done.refs_2_, ...), custom_call_target="tpu_custom_call" | custom-call | flops 402653184 | bytes 393216 | tf_op jit(solution)/shard_map/pallas_call | solution.py:182
  24.2 0.6 %collective-permute-start.12 = (f32[384,128]{1,0:T(8,128)S(1)}, f32[384,128]{1,0:T(8,128)S(1)}, u32[]{:S(2)}, u32[]{:S(2)}) collective-permute-start(f32[384,128]{1,0:T(8,128)S(1)} %get-tuple-element.54), channel_id=1, source_target_pairs={{0,1},{1,0},{2,3},{3,2},{4,5},{5,4},{6,7},{7,6},{8,9},{9,8},{10,11... | collective-permute-start | bytes 589832 | tf_op jit(solution)/shard_map/ppermute | solution.py:247
  24.7 0.4 %shard_map.58 = (f32[384,128]{1,0:T(8,128)S(1)}, f32[384,128]{1,0:T(8,128)S(1)}, f32[384,128]{1,0:T(8,128)S(1)}, f32[384,128]{1,0:T(8,128)S(1)}, s32[8,128]{1,0:T(8,128)S(1)}) custom-call(s32[1]{0:T(128)S(6)} %copy.8.refs_0_, bf16[384,2048]{1,0:T(8,128)(2,1)S(1)} %get-tuple-element.33.refs_0_.refs_1_, ...), custom_call_target="tpu_custom_call" | custom-call | flops 402653184 | bytes 1572864 | tf_op jit(solution)/shard_map/pallas_call | solution.py:182
  25.1 0.5 %shard_map.59 = (f32[384,128]{1,0:T(8,128)S(1)}, f32[384,128]{1,0:T(8,128)S(1)}, f32[384,128]{1,0:T(8,128)S(1)}, f32[384,128]{1,0:T(8,128)S(1)}) custom-call(bf16[384,2048]{1,0:T(8,128)(2,1)S(1)} %get-tuple-element.33.refs_0_.refs_1_, bf16[384,2048]{1,0:T(8,128)(2,1)S(1)} %get-tuple-element.34.refs_1_.refs_2_, ...), custom_call_target="tpu_custom_call" | custom-call | flops 301989888 | bytes 1572864 | tf_op jit(solution)/shard_map/pallas_call | solution.py:182
  25.6 3.7 %collective-permute-done.6.refs_3_ = bf16[128,768]{1,0:T(8,128)(2,1)S(1)} collective-permute-done((bf16[128,768]{1,0:T(8,128)(2,1)S(1)}, bf16[128,768]{1,0:T(8,128)(2,1)S(1)}, u32[]{:S(2)}, u32[]{:S(2)}) %collective-permute-start.6) | collective-permute-done | bytes 196640 | tf_op jit(solution)/shard_map/ppermute | solution.py:247
  29.3 0.6 %collective-permute-done.5.refs_2_ = bf16[128,768]{1,0:T(8,128)(2,1)S(1)} collective-permute-done((bf16[128,768]{1,0:T(8,128)(2,1)S(1)}, bf16[128,768]{1,0:T(8,128)(2,1)S(1)}, u32[]{:S(2)}, u32[]{:S(2)}) %collective-permute-start.5) | collective-permute-done | bytes 196640 | tf_op jit(solution)/shard_map/ppermute | solution.py:247
  30.0 0.4 %shard_map.61 = (f32[384,128]{1,0:T(8,128)S(1)}, f32[384,128]{1,0:T(8,128)S(1)}) custom-call(bf16[384,2048]{1,0:T(8,128)(2,1)S(1)} %get-tuple-element.33.refs_0_.refs_1_, bf16[384,2048]{1,0:T(8,128)(2,1)S(1)} %get-tuple-element.34.refs_1_.refs_2_, bf16[128,768]{1,0:T(8,128)(2,1)S(1)} %collective-permute-done.5.refs_2_, ...), custom_call_target="tpu_custom_call" | custom-call | flops 301989888 | bytes 393216 | tf_op jit(solution)/shard_map/pallas_call | solution.py:182
  30.8 0.6 %collective-permute-start.10 = (f32[384,128]{1,0:T(8,128)S(1)}, f32[384,128]{1,0:T(8,128)S(1)}, u32[]{:S(2)}, u32[]{:S(2)}) collective-permute-start(f32[384,128]{1,0:T(8,128)S(1)} %shard_map.63), channel_id=1, source_target_pairs={{0,1},{1,0},{2,3},{3,2},{4,5},{5,4},{6,7},{7,6},{8,9},{9,8},{10,11... | collective-permute-start | bytes 589832 | tf_op jit(solution)/shard_map/ppermute | solution.py:247
  31.3 0.8 %shard_map.64.refs_4_ = f32[384,512]{1,0:T(8,128)} custom-call(s32[8,128]{1,0:T(8,128)S(1)} %get-tuple-element.39.limit, f32[384,128]{1,0:T(8,128)S(1)} %get-tuple-element.37.refs_0_, f32[384,128]{1,0:T(8,128)S(1)} %collective-permute-done.11.refs_1_, f32[384,128]{1,0:T(8,128)S(1)} %get-tuple-element.35.refs_2_, f32[384,128]{1,0:T(8,128)S(1)} %collective-permute-done.12.refs_3_), custom_call_target="tpu_custom_call" | custom-call | flops 98304 | bytes 1179648 | tf_op jit(solution)/shard_map/pallas_call | solution.py:217
  32.1 0.4 %shard_map.60 = (f32[384,128]{1,0:T(8,128)S(1)}, f32[384,128]{1,0:T(8,128)S(1)}) custom-call(bf16[384,2048]{1,0:T(8,128)(2,1)S(1)} %get-tuple-element.33.refs_0_.refs_1_, bf16[384,2048]{1,0:T(8,128)(2,1)S(1)} %get-tuple-element.34.refs_1_.refs_2_, bf16[128,768]{1,0:T(8,128)(2,1)S(1)} %collective-permute-done.5.refs_2_, ...), custom_call_target="tpu_custom_call" | custom-call | flops 301989888 | bytes 393216 | tf_op jit(solution)/shard_map/pallas_call | solution.py:182
  32.9 0.8 %shard_map.65 = f32[384,512]{1,0:T(8,128)} custom-call(s32[8,128]{1,0:T(8,128)S(1)} %get-tuple-element.39.limit, f32[384,128]{1,0:T(8,128)S(1)} %get-tuple-element.47.refs_0_, f32[384,128]{1,0:T(8,128)S(1)} %collective-permute-done.8.refs_1_, f32[384,128]{1,0:T(8,128)S(1)} %shard_map.62.refs_2_, ...), custom_call_target="tpu_custom_call", output_to_operand_aliasing={{}: (5, {})} | custom-call | flops 98304 | bytes 1179648 | tf_op jit(solution)/shard_map/pallas_call | solution.py:217
  (16 shorter events, 0.8 us)
Async XLA Ops:
  1.6 9.6 %collective-permute-start = (bf16[128,512]{1,0:T(8,128)(2,1)S(1)}, bf16[128,512]{1,0:T(8,128)(2,1)S(1)}, u32[]{:S(2)}, u32[]{:S(2)}) collective-permute-start(bf16[128,512]{1,0:T(8,128)(2,1)S(1)} %get-tuple-element.30.refs_1_), channel_id=1, source_target_pairs={{0,4},{2,6},{4,8},{6,10},{8,12},{10,14},{12,0},{14,2},{1,5},{3,7},... | collective-permute-start | bytes 393224 | tf_op jit(solution)/shard_map/ppermute | solution.py:247
  4.7 10.6 %collective-permute-start.1 = (bf16[128,768]{1,0:T(8,128)(2,1)S(1)}, bf16[128,768]{1,0:T(8,128)(2,1)S(1)}, u32[]{:S(2)}, u32[]{:S(2)}) collective-permute-start(bf16[128,768]{1,0:T(8,128)(2,1)S(1)} %get-tuple-element.31.refs_2_), channel_id=1, source_target_pairs={{0,4},{2,6},{4,8},{6,10},{8,12},{10,14},{12,0},{14,2},{1,5},{3,7},... | collective-permute-start | bytes 589832 | tf_op jit(solution)/shard_map/ppermute | solution.py:247
  6.2 12.4 %collective-permute-start.2 = (bf16[128,768]{1,0:T(8,128)(2,1)S(1)}, bf16[128,768]{1,0:T(8,128)(2,1)S(1)}, u32[]{:S(2)}, u32[]{:S(2)}) collective-permute-start(bf16[128,768]{1,0:T(8,128)(2,1)S(1)} %get-tuple-element.32.refs_3_), channel_id=1, source_target_pairs={{0,4},{2,6},{4,8},{6,10},{8,12},{10,14},{12,0},{14,2},{1,5},{3,7},... | collective-permute-start | bytes 589832 | tf_op jit(solution)/shard_map/ppermute | solution.py:247
  11.2 5.9 %collective-permute-start.3 = (bf16[128,512]{1,0:T(8,128)(2,1)S(1)}, bf16[128,512]{1,0:T(8,128)(2,1)S(1)}, u32[]{:S(2)}, u32[]{:S(2)}) collective-permute-start(bf16[128,512]{1,0:T(8,128)(2,1)S(1)} %broadcast_select_fusion.2), channel_id=1, source_target_pairs={{0,2},{2,0},{4,6},{6,4},{8,10},{10,8},{12,14},{14,12},{1,3},{3,1},... | collective-permute-start | bytes 393224 | tf_op jit(solution)/shard_map/ppermute | solution.py:247
  15.3 5.9 %collective-permute-start.7 = (bf16[128,768]{1,0:T(8,128)(2,1)S(1)}, bf16[128,768]{1,0:T(8,128)(2,1)S(1)}, u32[]{:S(2)}, u32[]{:S(2)}) collective-permute-start(bf16[128,768]{1,0:T(8,128)(2,1)S(1)} %broadcast_select_fusion), channel_id=1, source_target_pairs={{0,2},{2,0},{4,6},{6,4},{8,10},{10,8},{12,14},{14,12},{1,3},{3,1},... | collective-permute-start | bytes 589832 | tf_op jit(solution)/shard_map/ppermute | solution.py:247
  17.1 7.1 %collective-permute-start.4 = (bf16[128,512]{1,0:T(8,128)(2,1)S(1)}, bf16[128,512]{1,0:T(8,128)(2,1)S(1)}, u32[]{:S(2)}, u32[]{:S(2)}) collective-permute-start(bf16[128,512]{1,0:T(8,128)(2,1)S(1)} %collective-permute-done.3.refs_3_), channel_id=1, source_target_pairs={{0,4},{2,6},{4,8},{6,10},{8,12},{10,14},{12,0},{14,2},{1,5},{3,7},... | collective-permute-start | bytes 393224 | tf_op jit(solution)/shard_map/ppermute | solution.py:247
  18.6 10.7 %collective-permute-start.6 = (bf16[128,768]{1,0:T(8,128)(2,1)S(1)}, bf16[128,768]{1,0:T(8,128)(2,1)S(1)}, u32[]{:S(2)}, u32[]{:S(2)}) collective-permute-start(bf16[128,768]{1,0:T(8,128)(2,1)S(1)} %broadcast_select_fusion.1), channel_id=1, source_target_pairs={{0,2},{2,4},{4,6},{6,8},{8,10},{10,12},{12,14},{14,0},{1,3},{3,5},... | collective-permute-start | bytes 589832 | tf_op jit(solution)/shard_map/ppermute | solution.py:247
  20.2 9.8 %collective-permute-start.5 = (bf16[128,768]{1,0:T(8,128)(2,1)S(1)}, bf16[128,768]{1,0:T(8,128)(2,1)S(1)}, u32[]{:S(2)}, u32[]{:S(2)}) collective-permute-start(bf16[128,768]{1,0:T(8,128)(2,1)S(1)} %collective-permute-done.2.refs_4_), channel_id=1, source_target_pairs={{0,2},{2,0},{4,6},{6,4},{8,10},{10,8},{12,14},{14,12},{1,3},{3,1},... | collective-permute-start | bytes 589832 | tf_op jit(solution)/shard_map/ppermute | solution.py:247
  21.1 9.3 %collective-permute-start.9 = (bf16[128,768]{1,0:T(8,128)(2,1)S(1)}, bf16[128,768]{1,0:T(8,128)(2,1)S(1)}, u32[]{:S(2)}, u32[]{:S(2)}) collective-permute-start(bf16[128,768]{1,0:T(8,128)(2,1)S(1)} %collective-permute-done.7.refs_2_), channel_id=1, source_target_pairs={{0,4},{2,6},{4,8},{6,10},{8,12},{10,14},{12,0},{14,2},{1,5},{3,7},... | collective-permute-start | bytes 589832 | tf_op jit(solution)/shard_map/ppermute | solution.py:247
  22.5 8.8 %collective-permute-start.11 = (f32[384,128]{1,0:T(8,128)S(1)}, f32[384,128]{1,0:T(8,128)S(1)}, u32[]{:S(2)}, u32[]{:S(2)}) collective-permute-start(f32[384,128]{1,0:T(8,128)S(1)} %get-tuple-element.53), channel_id=1, source_target_pairs={{0,1},{1,0},{2,3},{3,2},{4,5},{5,4},{6,7},{7,6},{8,9},{9,8},{10,11... | collective-permute-start | bytes 589832 | tf_op jit(solution)/shard_map/ppermute | solution.py:247
  24.2 7.2 %collective-permute-start.12 = (f32[384,128]{1,0:T(8,128)S(1)}, f32[384,128]{1,0:T(8,128)S(1)}, u32[]{:S(2)}, u32[]{:S(2)}) collective-permute-start(f32[384,128]{1,0:T(8,128)S(1)} %get-tuple-element.54), channel_id=1, source_target_pairs={{0,1},{1,0},{2,3},{3,2},{4,5},{5,4},{6,7},{7,6},{8,9},{9,8},{10,11... | collective-permute-start | bytes 589832 | tf_op jit(solution)/shard_map/ppermute | solution.py:247
  30.4 2.5 %collective-permute-start.8 = (f32[384,128]{1,0:T(8,128)S(1)}, f32[384,128]{1,0:T(8,128)S(1)}, u32[]{:S(2)}, u32[]{:S(2)}) collective-permute-start(f32[384,128]{1,0:T(8,128)S(1)} %get-tuple-element.50), channel_id=1, source_target_pairs={{0,1},{1,0},{2,3},{3,2},{4,5},{5,4},{6,7},{7,6},{8,9},{9,8},{10,11... | collective-permute-start | bytes 589832 | tf_op jit(solution)/shard_map/ppermute | solution.py:247
  30.8 2.1 %collective-permute-start.10 = (f32[384,128]{1,0:T(8,128)S(1)}, f32[384,128]{1,0:T(8,128)S(1)}, u32[]{:S(2)}, u32[]{:S(2)}) collective-permute-start(f32[384,128]{1,0:T(8,128)S(1)} %shard_map.63), channel_id=1, source_target_pairs={{0,1},{1,0},{2,3},{3,2},{4,5},{5,4},{6,7},{7,6},{8,9},{9,8},{10,11... | collective-permute-start | bytes 589832 | tf_op jit(solution)/shard_map/ppermute | solution.py:247
